TPU v7x, 32 devices: a whole 2x2x4 slice. The times are simulated.
32 devices in a mesh: scen: 2 (over x), row: 8 (over z, y), col: 2 (over core).
Axes of the slice: x: 2, y: 2, z: 4, core: 2. Of those that a mesh axis runs over, the one named last changes fastest.
Arguments:
- slip_deficit: float32 [4096, 512], P(('row', 'col'), 'scen'), parts along dimension 1, may hold values from -6 to 6
- state_var: float32 [4096, 512], P(('row', 'col'), 'scen'), parts along dimension 1, may hold values from -0.5 to 0.5
- tau_load: float32 [4096, 512], P(('row', 'col'), 'scen'), parts along dimension 1, may hold values from -4 to 4
- sigma_base: float32 [4096], P(('row', 'col')), may hold values from 1 to 3
- a_coef: float32 [4096], P(('row', 'col')), may hold values from 0.5 to 1
- b_coef: float32 [4096], P(('row', 'col')), may hold values from 0.5 to 1
- v_basis: bfloat16 [16, 16, 32, 256], P('row', 'col'), may hold values from -0.375 to 0.375
- u_basis: bfloat16 [2, 16, 16, 32, 256], P(None, 'row', 'col'), may hold values from -0.25 to 0.25
- dense_blocks: bfloat16 [2, 16, 4, 256, 256], P(None, 'row', 'col'), may hold values from -0.25 to 0.25
- block_ranks: int32 [16, 16], P('row', 'col'), may hold values from 0 to 32, as said below
- near_index: int32 [16, 4], P('row', 'col'), may hold values from 0 to 15, as said below
Outputs:
- mean_rate: float32 [4096, 512], P(('row', 'col'), 'scen'), parts along dimension 1
- mean_change: float32 [4096, 512], P(('row', 'col'), 'scen'), parts along dimension 1
There are 2 independent parts, one for each index of `scen`. A program takes and returns all parts, laid end to end along the dimension named above; an argument that names none is the same for every part. Nothing has to cross between parts.
Inputs may be any that keep to these rules, and one draw needn't show every extreme that they name: `near_index`: row p names 4 different column blocks; entries j * 2 to (j + 1) * 2 - 1 lie in column tile j, from j * 8 to (j + 1) * 8 - 1; the column block that holds element block p is among them. `block_ranks`: 0 exactly on the blocks that near_index names for that row; every other block has a rank of 8 or more.
All inputs are finite; a program needn't handle non-finite values.
Results may differ from a plain program's by a relative error of at most 0.0041.
Values may be sent and summed in bfloat16 or wider, within the bound.
No kernel may reach another device: no remote copies, remote signals or barrier semaphores. Data moves between devices by JAX's collectives and lax.ppermute only.
A program may use at most 128 MiB of HBM per device.

v0:
```python
import jax
import jax.numpy as jnp
from jax import lax
from jax.sharding import PartitionSpec as P

NEWTON = 2


damping = 0.5
sigma_floor = 0.5
section_step = 0.1


def inverse_sinh(value):
    magnitude = jnp.abs(value)
    result = jnp.log(magnitude + jnp.sqrt(magnitude * magnitude + 1.0))
    return jnp.where(value < 0.0, -result, result)


def far_field(blocks, v_part, u_part, rank_part):
    projected = jnp.einsum("pqkb,qbe->pqke", v_part, blocks, preferred_element_type=jnp.float32)
    rank_count = v_part.shape[2]
    inside = lax.broadcasted_iota(jnp.int32, (1, 1, rank_count), 2) < rank_part[:, :, None]
    projected = jnp.where(inside[:, :, :, None], projected, 0.0).astype(jnp.bfloat16)
    return jnp.einsum("cpqkb,pqke->cpbe", u_part, projected, preferred_element_type=jnp.float32)


def near_field(picked, dense_blocks):
    return jnp.einsum("cpsab,psbe->cpae", dense_blocks, picked, preferred_element_type=jnp.float32)


def friction(shear, normal, state, tau_load, sigma_base, a_coef, b_coef):
    a_wide = a_coef[:, None]
    b_wide = b_coef[:, None]
    tau = tau_load + shear
    sigma = jnp.maximum(sigma_base[:, None] + normal, sigma_floor)
    weight = jnp.exp(-state / a_wide)
    first = tau / (sigma * a_wide)
    second = inverse_sinh(tau / (2.0 * damping * weight))
    slope = jnp.where(jnp.abs(first) < jnp.abs(second), first, second)
    for newton_step in range(NEWTON):
        excess = sigma * a_wide * slope + 2.0 * damping * weight * jnp.sinh(slope) - tau
        deriv = sigma * a_wide + 2.0 * damping * weight * jnp.cosh(slope)
        slope = slope - excess / deriv
    rate = 2.0 * weight * jnp.sinh(slope)
    change = b_wide * (jnp.exp(-state / b_wide) - jnp.abs(rate))
    return (rate, change)


def body(
    slip_deficit,
    state_var,
    tau_load,
    sigma_base,
    a_coef,
    b_coef,
    v_basis,
    u_basis,
    dense_blocks,
    block_ranks,
    near_index,
):
    block_size = slip_deficit.shape[0]
    members = slip_deficit.shape[1]
    tile_count = lax.axis_size("row")
    near_local = near_index - lax.axis_index("col") * tile_count
    row_blocks = near_index.shape[0]
    slot_count = near_index.shape[1]
    held = row_blocks * slot_count
    flat_near = near_local.reshape(held)

    def lattice(field_half):
        whole = lax.all_gather(field_half, "row", axis=0, tiled=True)
        blocks = whole.reshape(tile_count, block_size, members)
        picked = blocks[flat_near].reshape(row_blocks, slot_count, block_size, members)
        partial_value = far_field(blocks, v_basis, u_basis, block_ranks) + near_field(
            picked, dense_blocks
        )
        summed = lax.psum_scatter(partial_value, "col", scatter_dimension=1, tiled=True)
        return (summed[0, 0], summed[1, 0])

    slip_half = slip_deficit.astype(jnp.bfloat16)
    stress_one, normal_one = lattice(slip_half)
    rate_one, change_one = friction(
        stress_one, normal_one, state_var, tau_load, sigma_base, a_coef, b_coef
    )
    rate_half = rate_one.astype(jnp.bfloat16)
    stress_add, normal_add = lattice(rate_half)
    stress_two = stress_one + section_step * stress_add
    normal_two = normal_one + section_step * normal_add
    state_two = state_var + section_step * change_one
    rate_two, change_two = friction(
        stress_two, normal_two, state_two, tau_load, sigma_base, a_coef, b_coef
    )
    return ((rate_one + rate_two) * 0.5, (change_one + change_two) * 0.5)


def solution(mesh):
    placed = (
        P(("row", "col"), "scen"),
        P(("row", "col"), "scen"),
        P(("row", "col"), "scen"),
        P(("row", "col")),
        P(("row", "col")),
        P(("row", "col")),
        P("row", "col", None, None),
        P(None, "row", "col", None, None),
        P(None, "row", "col", None, None),
        P("row", "col"),
        P("row", "col"),
    )
    return jax.shard_map(
        body,
        mesh=mesh,
        in_specs=placed,
        out_specs=(P(("row", "col"), "scen"), P(("row", "col"), "scen")),
        check_vma=False,
    )
```

profile of v0, /device:TPU:0, one launch (start us, length us, event | category | flops | bytes accessed | tf_op | source)
XLA Modules:
  0.0 150.1 jit_solution(18124892261071501017)
XLA Ops:
  7.2 0.0 copy-start
  7.2 0.0 all-gather.3.cloned.1.call-start
  7.2 1.7 %convert_element_type.12 = bf16[256,256]{1,0:T(8,128)(2,1)} convert(f32[256,256]{1,0:T(8,128)} %param.11) | non-fusion elementwise | flops 65536 | bytes 393216 | tf_op jit(solution)/shard_map/convert_element_type | solution.py:82
  8.9 0.0 all-gather.3.cloned.1.call-update
  8.9 0.0 reduce-scatter.5.cloned.1.call-start
  9.0 0.0 copy-start.8
  9.0 0.7 copy-done.8
  9.7 0.1 reshape.59
  9.8 0.7 copy-done.7
  10.5 0.1 iota_compare_fusion
  10.5 43.1 %all-gather.3.cloned.1.call-done = bf16[2048,256]{1,0:T(8,128)(2,1)} async-done(((bf16[256,256]{1,0:T(8,128)(2,1)}), bf16[2048,256]{1,0:T(8,128)(2,1)}) %all-gather.3.cloned.1.call-update) | async-done | bytes 1048592 | tf_op jit(solution)/shard_map/all_gather | solution.py:73
  53.6 1.8 %gather_fusion = bf16[4,256,256]{2,1,0:T(8,128)(2,1)S(1)} fusion(bf16[8,256,256]{2,1,0:T(8,128)(2,1)} %bitcast.134, s32[1024]{0:T(1024)S(1)} %pad_clamp_fusion), kind=kCustom, calls=%fused_computation | custom fusion | bytes 1048592 | tf_op jit(solution)/shard_map/gather | solution.py:75
  55.4 0.0 copy-done
  55.4 0.0 copy-start.9
  55.4 0.0 copy-start.10
  55.4 0.5 convolution_bitcast_fusion.3
  56.0 0.5 copy-done.9
  56.5 0.1 copy-done.10
  56.5 2.9 %fusion.1 = f32[2,2,256,256]{2,3,0,1:T(8,128)} fusion(f32[2,256,2,256]{3,1,2,0:T(8,128)S(1)} %convolution_bitcast_fusion.3, bf16[8,256,256,1]{2,1,0,3:T(8,128)(2,1)} %bitcast.135, bf16[2,8,32,256]{3,2,1,0:T(8,128)(2,1)S(1)} %copy-done.10, bf16[2,2,8,32,256]{4,3,2,1,0:T(8,128)(2,1)S(1)} %copy-done.9, pred[2,8,32]{2,1,0:T(8,128)(4,1)S(1)} %iota_compare_fusion), kind=kOutput, calls=%fused_computation.7 | convolution fusion | flops 201850880 | bytes 3932672 | tf_op jit(solution)/shard_map/cpqkb,pqke->cpbe/dot_general | solution.py:25
  59.4 0.0 reduce-scatter.5.cloned.1.call-update
  59.4 0.0 copy-start.3
  59.4 0.0 all-gather.5.cloned.1.call-start
  59.5 0.9 copy-done.2
  60.3 0.1 copy.49
  60.5 0.0 copy-done.3
  60.5 0.0 copy-start.5
  60.5 0.1 copy.44
  60.6 0.0 copy-start.4
  60.7 6.2 %reduce-scatter.5.cloned.1.call-done = f32[2,1,256,256]{2,3,0,1:T(8,128)} async-done(((f32[2,2,256,256]{2,3,0,1:T(8,128)}), f32[2,1,256,256]{2,3,0,1:T(8,128)}) %reduce-scatter.5.cloned.1.call-update) | async-done | bytes 524304 | tf_op jit(solution)/shard_map/reduce_scatter | solution.py:79
  66.9 0.0 copy-done.5
  66.9 2.8 %fusion.60 = (bf16[256,256]{0,1:T(8,128)(2,1)}, f32[256,256]{0,1:T(8,128)S(1)}) fusion(f32[2,1,256,256]{2,3,0,1:T(8,128)} %reduce-scatter.5.cloned.1.call-done, f32[256]{0:T(256)S(1)} %copy-done.4, f32[256,256]{0,1:T(8,128)S(1)} %copy.49, f32[2,1,256,256]{2,3,1,0:T(8,128)} %bitcast.132, f32[256]{0:T(256)S(1)} %copy-done.5, f32[256,256]{0,1:T(8,128)S(1)} %copy.44), kind=kLoop, calls=%fused_computation.97 | loop fusion | flops 4587520 | bytes 1443840 | tf_op jit(solution)/shard_map/convert_element_type | solution.py:87
  69.7 0.0 all-gather.5.cloned.1.call-update
  69.7 0.0 all-reduce.3.cloned.1.call-start
  69.7 40.8 %all-gather.5.cloned.1.call-done = bf16[2048,256]{0,1:T(8,128)(2,1)} async-done(((bf16[256,256]{0,1:T(8,128)(2,1)}), bf16[2048,256]{0,1:T(8,128)(2,1)}) %all-gather.5.cloned.1.call-update) | async-done | bytes 1048592 | tf_op jit(solution)/shard_map/all_gather | solution.py:73
  110.6 1.5 copy.74
  112.0 0.6 gather_fusion.1
  112.6 1.5 %convolution_bitcast_fusion.2 = f32[2,256,2,256]{3,1,2,0:T(8,128)} fusion(bf16[2,2,256,256,1]{3,2,1,4,0:T(8,128)(2,1)S(1)} %bitcast.130, bf16[2,2,2,256,256]{4,3,2,1,0:T(8,128)(2,1)S(1)} %copy-done), kind=kOutput, calls=%fused_computation.4 | convolution fusion | flops 268435456 | bytes 2621440 | tf_op jit(solution)/shard_map/cpsab,psbe->cpae/dot_general | solution.py:29
  114.1 3.1 %fusion.3 = f32[2,2,256,256]{2,3,0,1:T(8,128)} fusion(f32[2,256,2,256]{3,1,2,0:T(8,128)} %convolution_bitcast_fusion.2, bf16[8,256,256,1]{2,1,0,3:T(8,128)(2,1)S(1)} %bitcast.129, bf16[2,8,32,256]{3,2,1,0:T(8,128)(2,1)} %param.17, bf16[2,2,8,32,256]{4,3,2,1,0:T(8,128)(2,1)} %param.18, pred[2,8,32]{2,1,0:T(8,128)(4,1)S(1)} %iota_compare_fusion), kind=kOutput, calls=%fused_computation.9 | convolution fusion | flops 201850880 | bytes 3932672 | tf_op jit(solution)/shard_map/cpqkb,pqke->cpbe/dot_general | solution.py:25
  117.3 2.3 %copy.56 = f32[2,2,256,256]{2,3,1,0:T(8,128)} copy(f32[2,2,256,256]{2,3,0,1:T(8,128)} %fusion.3) | data formatting | bytes 2097152 | tf_op jit(solution)/shard_map/add | solution.py:76
  119.6 0.0 all-reduce.3.cloned.1.call-update
  119.6 0.0 copy-start.11
  119.6 0.7 copy-done.11
  120.3 0.6 dynamic-slice
  120.9 17.3 %all-reduce.3.cloned.1.call-done = f32[2,2,256,256]{2,3,1,0:T(8,128)} async-done(((f32[2,2,256,256]{2,3,1,0:T(8,128)}), f32[2,2,256,256]{2,3,1,0:T(8,128)}) %all-reduce.3.cloned.1.call-update) | async-done | bytes 1048592
  138.2 0.7 copy-done.6
  138.9 3.0 %add_multiply_fusion = (f32[256,256]{0,1:T(8,128)S(1)}, f32[256,256]{0,1:T(8,128)S(1)}) fusion(f32[256,256]{0,1:T(8,128)S(1)} %copy.44, f32[256]{0:T(256)S(1)} %copy-done.6, f32[256,256]{0,1:T(8,128)S(1)} %get-tuple-element.11, f32[2,2,256,256]{2,3,1,0:T(8,128)} %all-reduce.3.cloned.1.call-done, u32[]{:T(128)S(6)} %convert.2, u32[]{:T(128)} %bitcast.46, ...), kind=kLoop, calls=%fused_computation.72 | loop fusion | flops 5636096 | bytes 2362376 | tf_op jit(solution)/shard_map/mul | solution.py:95
  141.9 0.8 copy.58
  142.8 0.8 copy.59
  (10 shorter events, 0.1 us)
Async XLA Ops:
  7.2 48.2 %copy-start = (bf16[2,2,2,256,256]{4,3,2,1,0:T(8,128)(2,1)S(1)}, bf16[2,2,2,256,256]{4,3,2,1,0:T(8,128)(2,1)}, u32[]{:S(2)}) copy-start(bf16[2,2,2,256,256]{4,3,2,1,0:T(8,128)(2,1)} %param.19) | copy-start | bytes 3145732
  7.2 46.4 %all-gather.3.cloned.1.call-start = ((), (), s32[]{:S(2)}) async-start(), calls=%async_computation.1 | async-start | bytes 1179648 | tf_op jit(solution)/shard_map/all_gather | solution.py:73
  8.9 57.9 %reduce-scatter.5.cloned.1.call-start = ((), (), s32[]{:S(2)}) async-start(), calls=%async_computation.2 | async-start | bytes 1572864 | tf_op jit(solution)/shard_map/reduce_scatter | solution.py:79
  9.0 0.7 copy-start.8
  9.8 0.7 copy-start.7
  55.4 1.0 copy-start.9
  55.4 1.1 copy-start.10
  59.4 0.9 copy-start.2
  59.4 1.1 copy-start.3
  59.4 51.1 %all-gather.5.cloned.1.call-start = ((), (), s32[]{:S(2)}) async-start(), calls=%async_computation.3 | async-start | bytes 1179648 | tf_op jit(solution)/shard_map/all_gather | solution.py:73
  60.5 6.4 %copy-start.5 = (f32[256]{0:T(256)S(1)}, f32[256]{0:T(256)}, u32[]{:S(2)}) copy-start(f32[256]{0:T(256)} %param.15) | copy-start | bytes 3076
  60.6 6.2 %copy-start.4 = (f32[256]{0:T(256)S(1)}, f32[256]{0:T(256)}, u32[]{:S(2)}) copy-start(f32[256]{0:T(256)} %param.14) | copy-start | bytes 3076
  69.7 68.5 %all-reduce.3.cloned.1.call-start = ((), (), s32[]{:S(2)}) async-start(), calls=%async_computation.4 | async-start | bytes 2097152
  119.5 18.7 %copy-start.1 = (f32[2,1,256,256]{2,3,0,1:T(8,128)S(1)}, f32[2,1,256,256]{2,3,0,1:T(8,128)}, u32[]{:S(2)}) copy-start(f32[2,1,256,256]{2,3,0,1:T(8,128)} %reduce-scatter.5.cloned.1.call-done) | copy-start | bytes 1572868
  119.6 0.7 copy-start.11
  138.2 0.7 copy-start.6
Sparse Core Ops, SparseCore 0:
  10.7 42.8 all-gather.2
  59.5 7.2 reduce-scatter.4
  69.8 40.6 all-gather.4
  119.7 18.4 all-reduce.2
where the time goes:
time: 151 us; the launch traced here: 150 us
  waiting for transfers between devices  107 us (71%)
  between operations  13.9 us (9%)
  local copies, waits for them, and re-layouts  12.9 us (9%)
  matrix products  8.03 us (5%)
  other arithmetic  7.58 us (5%)
    all_gather x2, waiting for transfers between devices, lattice(): whole = lax.all_gather(field_half, 'row', axis=0, tiled=True)  83.9 us
    unnamed x5, waiting for transfers between devices  17.4 us
    unnamed x29, local copies, waits for them, and re-layouts  6.7 us
    reduce_scatter x1, waiting for transfers between devices, lattice(): lax.psum_scatter(partial_value, 'col', scatter_dimension=1, tiled=True)  6.23 us
    dot_general x2, matrix products, far_field(): jnp.einsum('cpqkb,pqke->cpbe', u_part, projected, preferred_element_type=...  5.98 us
  transfers between devices with their start and end apart: 4, of which 4 were waited for; matrix products, arithmetic and copies ran while one was open for 1% of the time, Pallas kernels for 0%

commit v1 on v0

v1 whole, which is shorter than its diff:
```python
import functools

import jax
import jax.numpy as jnp
from jax import lax
from jax.experimental import pallas as pl
from jax.experimental.pallas import tpu as pltpu
from jax.sharding import PartitionSpec as P

NEWTON = 2
RING_LIMIT = 16

damping = 0.5
sigma_floor = 0.5
section_step = 0.1


def ring_rows(count):
    return list(range(0, count, 2)) + list(range(1, count, 2))[::-1]


def ring_gather(block, count):
    me = lax.axis_index("row")
    if count > RING_LIMIT:
        whole = lax.all_gather(block, "row", axis=0)
        return [(jnp.int32(r), [whole[r]]) for r in range(count)]
    ring = ring_rows(count)
    place = [ring.index(r) for r in range(count)]
    up = [(ring[i], ring[(i + 1) % count]) for i in range(count)]
    down = [(ring[(i + 1) % count], ring[i]) for i in range(count)]
    table = jnp.array(ring, jnp.int32)
    my_place = jnp.array(place, jnp.int32)[me]

    def row_at(shift):
        return table[(my_place + shift) % count]

    found = [(row_at(0), [block])]
    from_left = from_right = block
    steps = (count - 1) // 2
    for step in range(1, steps + 1):
        from_left = lax.ppermute(from_left, "row", up)
        from_right = lax.ppermute(from_right, "row", down)
        found.append((row_at(-step), [from_left]))
        found.append((row_at(step), [from_right]))
    if count % 2 == 0:
        half = block.shape[0] // 2
        if steps == 0:
            found.append((row_at(1), [lax.ppermute(block, "row", up)]))
        else:
            top = lax.ppermute(from_left[:half], "row", up)
            low = lax.ppermute(from_right[half:], "row", down)
            found.append((row_at(steps + 1), [top, low]))
    return found


def lattice_kernel(pieces, order_ref, rank_ref, near_ref, pick_ref, *refs):
    total = sum(pieces)
    blocks = refs[:total]
    v_ref, u_ref, d_ref, out_ref, x_all, v_mine, u_mine, d_mine, proj, x_sem, w_sem = refs[total:]
    count, size = x_all.shape[0], x_all.shape[1]
    rank_count = v_mine.shape[1]
    slots = d_mine.shape[1]
    row = pick_ref[0]
    copies = []
    at = 0
    for place, parts in enumerate(pieces):
        tall = size // parts
        for part in range(parts):
            copies.append(
                pltpu.make_async_copy(
                    blocks[at], x_all.at[order_ref[place], pl.ds(part * tall, tall)], x_sem.at[at]
                )
            )
            at += 1
    weights = [
        pltpu.make_async_copy(v_ref.at[row], v_mine, w_sem.at[0]),
        pltpu.make_async_copy(d_ref.at[:, row], d_mine, w_sem.at[1]),
        pltpu.make_async_copy(u_ref.at[:, row], u_mine, w_sem.at[2]),
    ]
    for copy in copies + weights:
        copy.start()
    for copy in copies:
        copy.wait()
    weights[0].wait()
    for q in range(count):
        part = jnp.dot(v_mine[q], x_all[q], preferred_element_type=jnp.float32)
        inside = lax.broadcasted_iota(jnp.int32, part.shape, 0) < rank_ref[row, q]
        proj[pl.ds(q * rank_count, rank_count), :] = jnp.where(inside, part, 0.0).astype(proj.dtype)
    weights[1].wait()
    weights[2].wait()
    picked = [x_all[near_ref[row, s]] for s in range(slots)]
    for kind in range(u_mine.shape[0]):
        u_flat = u_mine[kind].reshape(count * rank_count, size)
        sums = lax.dot_general(
            u_flat, proj[...], (((0,), (0,)), ((), ())), preferred_element_type=jnp.float32
        )
        for s in range(slots):
            sums += jnp.dot(d_mine[kind, s], picked[s], preferred_element_type=jnp.float32)
        out_ref[kind] = sums.astype(out_ref.dtype)


def lattice_row(found, order, ranks, near, row, v_basis, u_basis, dense_blocks, kind):
    pieces = tuple(len(parts) for _, parts in found)
    blocks = [part for _, parts in found for part in parts]
    kinds, _, count, rank_count, size = u_basis.shape
    slots = dense_blocks.shape[2]
    members = blocks[0].shape[1]
    half = blocks[0].dtype
    smem = pl.BlockSpec(memory_space=pltpu.SMEM)
    far = pl.BlockSpec(memory_space=pl.ANY)
    return pl.pallas_call(
        functools.partial(lattice_kernel, pieces),
        out_shape=jax.ShapeDtypeStruct((kinds, size, members), kind),
        in_specs=[smem] * 4 + [far] * (len(blocks) + 3),
        out_specs=pl.BlockSpec(memory_space=pltpu.VMEM),
        scratch_shapes=[
            pltpu.VMEM((count, size, members), half),
            pltpu.VMEM((count, rank_count, size), half),
            pltpu.VMEM((kinds, count, rank_count, size), half),
            pltpu.VMEM((kinds, slots, size, size), half),
            pltpu.VMEM((count * rank_count, members), half),
            pltpu.SemaphoreType.DMA((len(blocks),)),
            pltpu.SemaphoreType.DMA((3,)),
        ],
        compiler_params=pltpu.CompilerParams(vmem_limit_bytes=40 * 1024 * 1024),
        cost_estimate=pl.CostEstimate(
            flops=2 * size * members * (count * rank_count * 3 + kinds * slots * size),
            bytes_accessed=4 * 1024 * 1024,
            transcendentals=0,
        ),
    )(order, ranks, near, row, *blocks, v_basis, u_basis, dense_blocks)


def inverse_sinh(value):
    magnitude = jnp.abs(value)
    result = jnp.log(magnitude + jnp.sqrt(magnitude * magnitude + 1.0))
    return jnp.where(value < 0.0, -result, result)


def sinh_cosh(value):
    grown = jnp.exp(value)
    shrunk = 1.0 / grown
    square = value * value
    small = value * (
        1.0 + square * (1 / 6 + square * (1 / 120 + square * (1 / 5040 + square * (1 / 362880))))
    )
    sinh = jnp.where(square < 1.0, small, 0.5 * (grown - shrunk))
    return sinh, 0.5 * (grown + shrunk)


def friction(shear, normal, state, tau_load, sigma_base, a_wide, b_wide):
    tau = tau_load + shear
    sigma = jnp.maximum(sigma_base + normal, sigma_floor)
    weight = jnp.exp(-state / a_wide)
    stiff = sigma * a_wide
    first = tau / stiff
    second = inverse_sinh(tau / (2.0 * damping * weight))
    slope = jnp.where(jnp.abs(first) < jnp.abs(second), first, second)
    for newton_step in range(NEWTON):
        sinh, cosh = sinh_cosh(slope)
        excess = stiff * slope + 2.0 * damping * weight * sinh - tau
        deriv = stiff + 2.0 * damping * weight * cosh
        slope = slope - excess / deriv
    rate = 2.0 * weight * sinh_cosh(slope)[0]
    change = b_wide * (jnp.exp(-state / b_wide) - jnp.abs(rate))
    return (rate, change)


def section_one_kernel(own, other, state, tau, coef, stress, normal, rate, change, rate_half):
    size, members = state.shape
    step = min(size, 64)

    @pl.loop(0, size // step)
    def _(index):
        rows = pl.ds(pl.multiple_of(index * step, step), step)
        shear = own[0, rows, :] + other[0, rows, :].astype(jnp.float32)
        press = own[1, rows, :] + other[1, rows, :].astype(jnp.float32)
        stress[rows, :] = shear
        normal[rows, :] = press
        first, second = friction(
            shear, press, state[rows, :], tau[rows, :], coef[rows, 0:1], coef[rows, 1:2], coef[rows, 2:3]
        )
        rate[rows, :] = first
        change[rows, :] = second
        rate_half[rows, :] = first.astype(rate_half.dtype)


def section_two_kernel(own, other, state, tau, coef, stress, normal, rate, change, mean_rate, mean_change):
    size, members = state.shape
    step = min(size, 64)

    @pl.loop(0, size // step)
    def _(index):
        rows = pl.ds(pl.multiple_of(index * step, step), step)
        shear = stress[rows, :] + section_step * (own[0, rows, :] + other[0, rows, :].astype(jnp.float32))
        press = normal[rows, :] + section_step * (own[1, rows, :] + other[1, rows, :].astype(jnp.float32))
        first, second = friction(
            shear,
            press,
            state[rows, :] + section_step * change[rows, :],
            tau[rows, :],
            coef[rows, 0:1],
            coef[rows, 1:2],
            coef[rows, 2:3],
        )
        mean_rate[rows, :] = (rate[rows, :] + first) * 0.5
        mean_change[rows, :] = (change[rows, :] + second) * 0.5


def section(kernel, outs, *args):
    vmem = pl.BlockSpec(memory_space=pltpu.VMEM)
    return pl.pallas_call(
        kernel,
        out_shape=outs,
        in_specs=[vmem] * len(args),
        out_specs=tuple([vmem] * len(outs)),
        compiler_params=pltpu.CompilerParams(vmem_limit_bytes=24 * 1024 * 1024),
        cost_estimate=pl.CostEstimate(
            flops=200 * outs[0].size, bytes_accessed=8 * 4 * outs[0].size, transcendentals=12 * outs[0].size
        ),
    )(*args)


def body(
    slip_deficit,
    state_var,
    tau_load,
    sigma_base,
    a_coef,
    b_coef,
    v_basis,
    u_basis,
    dense_blocks,
    block_ranks,
    near_index,
):
    count = lax.axis_size("row")
    col = lax.axis_index("col")
    near = near_index - col * count
    coef = jnp.stack([sigma_base, a_coef, b_coef], axis=1)
    mine, twin = col.reshape(1), (1 - col).reshape(1)
    swap = [(0, 1), (1, 0)]

    def lattice(field_half):
        found = ring_gather(field_half, count)
        order = jnp.stack([row for row, _ in found])

        def one(row, kind):
            return lattice_row(
                found, order, block_ranks, near, row, v_basis, u_basis, dense_blocks, kind
            )

        other = lax.ppermute(one(twin, jnp.bfloat16), "col", swap)
        return one(mine, jnp.float32), other

    full = jax.ShapeDtypeStruct(slip_deficit.shape, jnp.float32)
    narrow = jax.ShapeDtypeStruct(slip_deficit.shape, jnp.bfloat16)
    own, other = lattice(slip_deficit.astype(jnp.bfloat16))
    stress, normal, rate, change, rate_half = section(
        section_one_kernel, (full, full, full, full, narrow), own, other, state_var, tau_load, coef
    )
    own, other = lattice(rate_half)
    return section(
        section_two_kernel,
        (full, full),
        own,
        other,
        state_var,
        tau_load,
        coef,
        stress,
        normal,
        rate,
        change,
    )


def solution(mesh):
    placed = (
        P(("row", "col"), "scen"),
        P(("row", "col"), "scen"),
        P(("row", "col"), "scen"),
        P(("row", "col")),
        P(("row", "col")),
        P(("row", "col")),
        P("row", "col", None, None),
        P(None, "row", "col", None, None),
        P(None, "row", "col", None, None),
        P("row", "col"),
        P("row", "col"),
    )
    return jax.shard_map(
        body,
        mesh=mesh,
        in_specs=placed,
        out_specs=(P(("row", "col"), "scen"), P(("row", "col"), "scen")),
        check_vma=False,
    )
```

time: 151 us -> 75.5 us (0.50)
  waiting for transfers between devices: 107 us -> 23.6 us
  starting transfers between devices: 0.16 us -> 17.8 us
  Pallas kernels: 0 us -> 15.4 us
  matrix products: 8.03 us -> 0 us
  other arithmetic: 7.58 us -> 1.03 us
  between operations: 13.9 us -> 7.47 us
  local copies, waits for them, and re-layouts: 12.9 us -> 9.69 us
    all_gather x2 -> x0, waiting for transfers between devices: 83.9 us -> none  [lattice(): whole = lax.all_gather(field_half, 'row', axis=0, tiled=True)]
    ppermute x0 -> x18, waiting for transfers between devices: none -> 23.6 us  [the longest x6 19.8 us: ring_gather(): from_right = lax.ppermute(from_right, 'row', down)]
    ppermute x0 -> x18, starting transfers between devices: none -> 17.8 us  [the longest x6 11.5 us: ring_gather(): from_right = lax.ppermute(from_right, 'row', down)]
    unnamed x5 -> x0, waiting for transfers between devices: 17.4 us -> none
    pallas_call x0 -> x6, Pallas kernels: none -> 15.4 us  [the longest x4 11.8 us: lattice_row(): pl.pallas_call(functools.partial(lattice_kernel, pieces), out_shape=jax.S...]
    dot_general x4 -> x0, matrix products: 8.03 us -> none  [the longest x2 5.98 us: far_field(): jnp.einsum('cpqkb,pqke->cpbe', u_part, projected, preferred_element_type=...]
    reduce_scatter x1 -> x0, waiting for transfers between devices: 6.23 us -> none  [lattice(): lax.psum_scatter(partial_value, 'col', scatter_dimension=1, tiled=True)]
    another operation x0 -> x2, local copies, waits for them, and re-layouts: none -> 5.21 us  [the longest x1 5.07 us: lattice(): order = jnp.stack([row for row, _ in found])]
  transfers between devices with their start and end apart: 4 -> 18, of which waited for: 4 -> 8; matrix products, arithmetic and copies ran while one was open for 1% -> 9% of each run, Pallas kernels for 0% -> 8%
where the time goes in v1:
time: 75.5 us; the launch traced here: 75 us
  waiting for transfers between devices  23.6 us (31%)
  starting transfers between devices  17.8 us (24%)
  Pallas kernels  15.4 us (20%)
  local copies, waits for them, and re-layouts  9.69 us (13%)
  between operations  7.47 us (10%)
  other arithmetic  1.03 us (1%)
    ppermute x6, waiting for transfers between devices, ring_gather(): from_right = lax.ppermute(from_right, 'row', down)  19.8 us
    pallas_call x4, Pallas kernels, lattice_row(): pl.pallas_call(functools.partial(lattice_kernel, pieces), out_shape=jax.S...  11.8 us
    ppermute x6, starting transfers between devices, ring_gather(): from_right = lax.ppermute(from_right, 'row', down)  11.5 us
    another operation x1, local copies, waits for them, and re-layouts, lattice(): order = jnp.stack([row for row, _ in found])  5.07 us
    pallas_call x2, Pallas kernels, section(): pl.pallas_call(kernel, out_shape=outs, in_specs=[vmem] * len(args), out_s...  3.57 us
    ppermute x2, starting transfers between devices, ring_gather(): low = lax.ppermute(from_right[half:], 'row', down)  3.55 us
    unnamed x26, local copies, waits for them, and re-layouts  3.2 us
    ppermute x2, waiting for transfers between devices, ring_gather(): low = lax.ppermute(from_right[half:], 'row', down)  2.18 us
  transfers between devices with their start and end apart: 18, of which 8 were waited for; matrix products, arithmetic and copies ran while one was open for 9% of the time, Pallas kernels for 8%

profile of v1, /device:TPU:0, one launch (start us, length us, event | category | flops | bytes accessed | tf_op | source)
XLA Modules:
  0.0 75.0 jit_solution(11388300620320480116)
XLA Ops:
  0.6 1.0 %convert_element_type.3.refs_0_ = bf16[256,256]{1,0:T(8,128)(2,1)S(1)} convert(f32[256,256]{1,0:T(8,128)} %param.15) | non-fusion elementwise | flops 65536 | bytes 393216 | tf_op jit(solution)/shard_map/convert_element_type | solution.py:258
  1.7 3.0 %collective-permute-start.1 = (bf16[256,256]{1,0:T(8,128)(2,1)S(1)}, bf16[256,256]{1,0:T(8,128)(2,1)S(1)}, u32[]{:S(2)}, u32[]{:S(2)}) collective-permute-start(bf16[256,256]{1,0:T(8,128)(2,1)S(1)} %convert_element_type.3.refs_0_), channel_id=1, source_target_pairs={{4,0},{8,4},{12,8},{14,12},{10,14},{6,10},{2,6},{0,2},{5,1},{9,5},... | collective-permute-start | bytes 393224 | tf_op jit(solution)/shard_map/ppermute | solution.py:42
  4.7 0.1 collective-permute-start
  4.8 3.4 %collective-permute-done.1.refs_2_ = bf16[256,256]{1,0:T(8,128)(2,1)S(1)} collective-permute-done((bf16[256,256]{1,0:T(8,128)(2,1)S(1)}, bf16[256,256]{1,0:T(8,128)(2,1)S(1)}, u32[]{:S(2)}, u32[]{:S(2)}) %collective-permute-start.1) | collective-permute-done | bytes 131104 | tf_op jit(solution)/shard_map/ppermute | solution.py:42
  8.2 1.7 %collective-permute-start.3 = (bf16[256,256]{1,0:T(8,128)(2,1)S(1)}, bf16[256,256]{1,0:T(8,128)(2,1)S(1)}, u32[]{:S(2)}, u32[]{:S(2)}) collective-permute-start(bf16[256,256]{1,0:T(8,128)(2,1)S(1)} %collective-permute-done.1.refs_2_), channel_id=1, source_target_pairs={{4,0},{8,4},{12,8},{14,12},{10,14},{6,10},{2,6},{0,2},{5,1},{9,5},... | collective-permute-start | bytes 393224 | tf_op jit(solution)/shard_map/ppermute | solution.py:42
  9.9 0.3 collective-permute-start.2
  10.3 2.9 %collective-permute-done.3.refs_4_ = bf16[256,256]{1,0:T(8,128)(2,1)S(1)} collective-permute-done((bf16[256,256]{1,0:T(8,128)(2,1)S(1)}, bf16[256,256]{1,0:T(8,128)(2,1)S(1)}, u32[]{:S(2)}, u32[]{:S(2)}) %collective-permute-start.3) | collective-permute-done | bytes 131104 | tf_op jit(solution)/shard_map/ppermute | solution.py:42
  13.2 1.7 %collective-permute-start.5 = (bf16[256,256]{1,0:T(8,128)(2,1)S(1)}, bf16[256,256]{1,0:T(8,128)(2,1)S(1)}, u32[]{:S(2)}, u32[]{:S(2)}) collective-permute-start(bf16[256,256]{1,0:T(8,128)(2,1)S(1)} %collective-permute-done.3.refs_4_), channel_id=1, source_target_pairs={{4,0},{8,4},{12,8},{14,12},{10,14},{6,10},{2,6},{0,2},{5,1},{9,5},... | collective-permute-start | bytes 393224 | tf_op jit(solution)/shard_map/ppermute | solution.py:42
  14.9 0.0 collective-permute-done.2.refs_3_
  14.9 0.3 collective-permute-start.4
  15.2 3.4 %collective-permute-done.5.refs_6_ = bf16[256,256]{1,0:T(8,128)(2,1)S(1)} collective-permute-done((bf16[256,256]{1,0:T(8,128)(2,1)S(1)}, bf16[256,256]{1,0:T(8,128)(2,1)S(1)}, u32[]{:S(2)}, u32[]{:S(2)}) %collective-permute-start.5) | collective-permute-done | bytes 131104 | tf_op jit(solution)/shard_map/ppermute | solution.py:42
  18.6 2.0 %collective-permute-start.7 = (bf16[128,256]{1,0:T(8,128)(2,1)S(1)}, bf16[128,256]{1,0:T(8,128)(2,1)S(1)}, u32[]{:S(2)}, u32[]{:S(2)}) collective-permute-start(bf16[128,256]{1,0:T(8,128)(2,1)S(1)} %slice.17), channel_id=1, source_target_pairs={{4,0},{8,4},{12,8},{14,12},{10,14},{6,10},{2,6},{0,2},{5,1},{9,5},... | collective-permute-start | bytes 196616 | tf_op jit(solution)/shard_map/ppermute | solution.py:51
  20.6 0.3 collective-permute-start.6
  20.9 0.6 dynamic_slice.54
  28.1 0.0 copy-start.7
  28.1 0.6 copy-done.7
  28.7 0.7 fusion
  29.4 5.1 %stack.18.order_ref = s32[8]{0:T(128)S(1)} concatenate(s32[1]{0:T(128)} %get-tuple-element.18, s32[1]{0:T(128)} %get-tuple-element.17, s32[1]{0:T(128)} %get-tuple-element.16, s32[1]{0:T(128)} %get-tuple-element.15, s32[1]{0:T(128)} %get-tuple-element.14, s32[1]{0:T(128)} %get-tuple-element.13, s32[1]{0:T(128)} %get-tuple-element.19, s32[1]{0:T(128)} %get-tuple-element.12), dimensions={0} | concatenate | bytes 64 | tf_op jit(solution)/shard_map/stack | solution.py:246
  34.5 0.0 collective-permute-done.7.refs_8_
  34.5 0.6 copy-done.6
  35.2 1.2 %copy-done = bf16[2,2,2,256,256]{4,3,2,1,0:T(8,128)(2,1)S(1)} copy-done((bf16[2,2,2,256,256]{4,3,2,1,0:T(8,128)(2,1)S(1)}, bf16[2,2,2,256,256]{4,3,2,1,0:T(8,128)(2,1)}, u32[]{:S(2)}) %copy-start) | copy-done | bytes 1048600
  36.4 3.0 %shard_map.159 = bf16[2,256,256]{2,1,0:T(8,128)(2,1)S(1)} custom-call(s32[8]{0:T(128)S(1)} %stack.18.order_ref, s32[2,8]{1,0:T(2,128)S(1)} %copy-done.6, s32[2,2]{1,0:T(2,128)S(1)} %broadcast_subtract_fusion.near_ref, s32[1]{0:T(128)} %bitcast.2.pick_ref, bf16[256,256]{1,0:T(8,128)(2,1)S(1)} %convert_element_type.3.refs_0_, ...), custom_call_target="tpu_custom_call" | custom-call | flops 234881024 | bytes 4194304 | tf_op jit(solution)/shard_map/pallas_call | solution.py:111
  39.4 0.1 collective-permute-start.8
  39.4 0.0 copy-start.8
  39.5 0.7 copy-done.8
  40.1 0.1 copy.20.coef
  40.3 0.0 copy-start.4
  40.3 0.0 copy-start.5
  40.3 3.0 %shard_map.158.own = f32[2,256,256]{2,1,0:T(8,128)S(1)} custom-call(s32[8]{0:T(128)S(1)} %stack.18.order_ref, s32[2,8]{1,0:T(2,128)S(1)} %copy-done.6, s32[2,2]{1,0:T(2,128)S(1)} %broadcast_subtract_fusion.near_ref, s32[1]{0:T(128)} %bitcast.1.pick_ref, bf16[256,256]{1,0:T(8,128)(2,1)S(1)} %convert_element_type.3.refs_0_, ...), custom_call_target="tpu_custom_call" | custom-call | flops 234881024 | bytes 4194304 | tf_op jit(solution)/shard_map/pallas_call | solution.py:111
  43.3 0.0 collective-permute-done.8.other
  43.3 1.4 %shard_map.160 = (f32[256,256]{1,0:T(8,128)S(1)}, f32[256,256]{1,0:T(8,128)S(1)}, f32[256,256]{1,0:T(8,128)S(1)}, f32[256,256]{1,0:T(8,128)S(1)}, bf16[256,256]{1,0:T(8,128)(2,1)S(1)}) custom-call(f32[2,256,256]{2,1,0:T(8,128)S(1)} %shard_map.158.own, bf16[2,256,256]{2,1,0:T(8,128)(2,1)S(1)} %collective-permute-done.8.other, f32[256,256]{1,0:T(8,128)S(1)} %copy-done.4, ...), custom_call_target="tpu_custom_call" | custom-call | flops 13107200 | bytes 2097152 | tf_op jit(solution)/shard_map/pallas_call | solution.py:212
  44.7 1.8 %collective-permute-start.10 = (bf16[256,256]{1,0:T(8,128)(2,1)S(1)}, bf16[256,256]{1,0:T(8,128)(2,1)S(1)}, u32[]{:S(2)}, u32[]{:S(2)}) collective-permute-start(bf16[256,256]{1,0:T(8,128)(2,1)S(1)} %get-tuple-element.7.refs_0_), channel_id=1, source_target_pairs={{4,0},{8,4},{12,8},{14,12},{10,14},{6,10},{2,6},{0,2},{5,1},{9,5},... | collective-permute-start | bytes 393224 | tf_op jit(solution)/shard_map/ppermute | solution.py:42
  46.5 0.3 collective-permute-start.9
  46.8 3.9 %collective-permute-done.10.refs_2_ = bf16[256,256]{1,0:T(8,128)(2,1)S(1)} collective-permute-done((bf16[256,256]{1,0:T(8,128)(2,1)S(1)}, bf16[256,256]{1,0:T(8,128)(2,1)S(1)}, u32[]{:S(2)}, u32[]{:S(2)}) %collective-permute-start.10) | collective-permute-done | bytes 131104 | tf_op jit(solution)/shard_map/ppermute | solution.py:42
  50.7 1.7 %collective-permute-start.12 = (bf16[256,256]{1,0:T(8,128)(2,1)S(1)}, bf16[256,256]{1,0:T(8,128)(2,1)S(1)}, u32[]{:S(2)}, u32[]{:S(2)}) collective-permute-start(bf16[256,256]{1,0:T(8,128)(2,1)S(1)} %collective-permute-done.10.refs_2_), channel_id=1, source_target_pairs={{4,0},{8,4},{12,8},{14,12},{10,14},{6,10},{2,6},{0,2},{5,1},{9,5},... | collective-permute-start | bytes 393224 | tf_op jit(solution)/shard_map/ppermute | solution.py:42
  52.4 0.3 collective-permute-start.11
  52.8 3.2 %collective-permute-done.12.refs_4_ = bf16[256,256]{1,0:T(8,128)(2,1)S(1)} collective-permute-done((bf16[256,256]{1,0:T(8,128)(2,1)S(1)}, bf16[256,256]{1,0:T(8,128)(2,1)S(1)}, u32[]{:S(2)}, u32[]{:S(2)}) %collective-permute-start.12) | collective-permute-done | bytes 131104 | tf_op jit(solution)/shard_map/ppermute | solution.py:42
  55.9 1.6 %collective-permute-start.14 = (bf16[256,256]{1,0:T(8,128)(2,1)S(1)}, bf16[256,256]{1,0:T(8,128)(2,1)S(1)}, u32[]{:S(2)}, u32[]{:S(2)}) collective-permute-start(bf16[256,256]{1,0:T(8,128)(2,1)S(1)} %collective-permute-done.12.refs_4_), channel_id=1, source_target_pairs={{4,0},{8,4},{12,8},{14,12},{10,14},{6,10},{2,6},{0,2},{5,1},{9,5},... | collective-permute-start | bytes 393224 | tf_op jit(solution)/shard_map/ppermute | solution.py:42
  57.5 0.4 collective-permute-start.13
  58.0 2.9 %collective-permute-done.14.refs_6_ = bf16[256,256]{1,0:T(8,128)(2,1)S(1)} collective-permute-done((bf16[256,256]{1,0:T(8,128)(2,1)S(1)}, bf16[256,256]{1,0:T(8,128)(2,1)S(1)}, u32[]{:S(2)}, u32[]{:S(2)}) %collective-permute-start.14) | collective-permute-done | bytes 131104 | tf_op jit(solution)/shard_map/ppermute | solution.py:42
  60.9 1.6 %collective-permute-start.16 = (bf16[128,256]{1,0:T(8,128)(2,1)S(1)}, bf16[128,256]{1,0:T(8,128)(2,1)S(1)}, u32[]{:S(2)}, u32[]{:S(2)}) collective-permute-start(bf16[128,256]{1,0:T(8,128)(2,1)S(1)} %slice.19), channel_id=1, source_target_pairs={{4,0},{8,4},{12,8},{14,12},{10,14},{6,10},{2,6},{0,2},{5,1},{9,5},... | collective-permute-start | bytes 196616 | tf_op jit(solution)/shard_map/ppermute | solution.py:51
  62.5 0.5 collective-permute-start.15
  63.0 2.2 %collective-permute-done.16.refs_8_ = bf16[128,256]{1,0:T(8,128)(2,1)S(1)} collective-permute-done((bf16[128,256]{1,0:T(8,128)(2,1)S(1)}, bf16[128,256]{1,0:T(8,128)(2,1)S(1)}, u32[]{:S(2)}, u32[]{:S(2)}) %collective-permute-start.16) | collective-permute-done | bytes 65568 | tf_op jit(solution)/shard_map/ppermute | solution.py:51
  65.2 1.7 %collective-permute-done.15.refs_7_ = bf16[128,256]{1,0:T(8,128)(2,1)S(1)} collective-permute-done((bf16[128,256]{1,0:T(8,128)(2,1)S(1)}, bf16[128,256]{1,0:T(8,128)(2,1)S(1)}, u32[]{:S(2)}, u32[]{:S(2)}) %collective-permute-start.15) | collective-permute-done | bytes 65568 | tf_op jit(solution)/shard_map/ppermute | solution.py:50
  66.8 3.0 %shard_map.162 = bf16[2,256,256]{2,1,0:T(8,128)(2,1)S(1)} custom-call(s32[8]{0:T(128)S(1)} %stack.18.order_ref, s32[2,8]{1,0:T(2,128)S(1)} %copy-done.6, s32[2,2]{1,0:T(2,128)S(1)} %broadcast_subtract_fusion.near_ref, s32[1]{0:T(128)} %bitcast.2.pick_ref, bf16[256,256]{1,0:T(8,128)(2,1)S(1)} %get-tuple-element.7.refs_0_, ...), custom_call_target="tpu_custom_call" | custom-call | flops 234881024 | bytes 4194304 | tf_op jit(solution)/shard_map/pallas_call | solution.py:111
  69.8 0.1 collective-permute-start.17
  69.9 3.0 %shard_map.161.own = f32[2,256,256]{2,1,0:T(8,128)S(1)} custom-call(s32[8]{0:T(128)S(1)} %stack.18.order_ref, s32[2,8]{1,0:T(2,128)S(1)} %copy-done.6, s32[2,2]{1,0:T(2,128)S(1)} %broadcast_subtract_fusion.near_ref, s32[1]{0:T(128)} %bitcast.1.pick_ref, bf16[256,256]{1,0:T(8,128)(2,1)S(1)} %get-tuple-element.7.refs_0_, ...), custom_call_target="tpu_custom_call" | custom-call | flops 234881024 | bytes 4194304 | tf_op jit(solution)/shard_map/pallas_call | solution.py:111
  72.8 2.2 %shard_map.163 = (f32[256,256]{1,0:T(8,128)}, f32[256,256]{1,0:T(8,128)}) custom-call(f32[2,256,256]{2,1,0:T(8,128)S(1)} %shard_map.161.own, bf16[2,256,256]{2,1,0:T(8,128)(2,1)S(1)} %collective-permute-done.17.other, f32[256,256]{1,0:T(8,128)S(1)} %copy-done.4, f32[256,256]{1,0:T(8,128)S(1)} %copy-done.5, f32[256,3]{1,0:T(8,128)S(1)} %copy.20.coef, ...), custom_call_target="tpu_custom_call" | custom-call | flops 13107200 | bytes 2097152 | tf_op jit(solution)/shard_map/pallas_call | solution.py:212
  (31 shorter events, 0.1 us)
Async XLA Ops:
  0.6 33.9 %copy-start.2 = (bf16[2,2,8,32,256]{4,3,2,1,0:T(8,128)(2,1)S(1)}, bf16[2,2,8,32,256]{4,3,2,1,0:T(8,128)(2,1)}, u32[]{:S(2)}) copy-start(bf16[2,2,8,32,256]{4,3,2,1,0:T(8,128)(2,1)} %refs_10_.7) | copy-start | bytes 1572868
  1.7 6.6 %collective-permute-start.1 = (bf16[256,256]{1,0:T(8,128)(2,1)S(1)}, bf16[256,256]{1,0:T(8,128)(2,1)S(1)}, u32[]{:S(2)}, u32[]{:S(2)}) collective-permute-start(bf16[256,256]{1,0:T(8,128)(2,1)S(1)} %convert_element_type.3.refs_0_), channel_id=1, source_target_pairs={{4,0},{8,4},{12,8},{14,12},{10,14},{6,10},{2,6},{0,2},{5,1},{9,5},... | collective-permute-start | bytes 393224 | tf_op jit(solution)/shard_map/ppermute | solution.py:42
  4.7 5.2 %collective-permute-start = (bf16[256,256]{1,0:T(8,128)(2,1)S(1)}, bf16[256,256]{1,0:T(8,128)(2,1)S(1)}, u32[]{:S(2)}, u32[]{:S(2)}) collective-permute-start(bf16[256,256]{1,0:T(8,128)(2,1)S(1)} %convert_element_type.3.refs_0_), channel_id=1, source_target_pairs={{0,4},{4,8},{8,12},{12,14},{14,10},{10,6},{6,2},{2,0},{1,5},{5,9},... | collective-permute-start | bytes 393224 | tf_op jit(solution)/shard_map/ppermute | solution.py:41
  8.2 5.0 %collective-permute-start.3 = (bf16[256,256]{1,0:T(8,128)(2,1)S(1)}, bf16[256,256]{1,0:T(8,128)(2,1)S(1)}, u32[]{:S(2)}, u32[]{:S(2)}) collective-permute-start(bf16[256,256]{1,0:T(8,128)(2,1)S(1)} %collective-permute-done.1.refs_2_), channel_id=1, source_target_pairs={{4,0},{8,4},{12,8},{14,12},{10,14},{6,10},{2,6},{0,2},{5,1},{9,5},... | collective-permute-start | bytes 393224 | tf_op jit(solution)/shard_map/ppermute | solution.py:42
  9.9 5.0 %collective-permute-start.2 = (bf16[256,256]{1,0:T(8,128)(2,1)S(1)}, bf16[256,256]{1,0:T(8,128)(2,1)S(1)}, u32[]{:S(2)}, u32[]{:S(2)}) collective-permute-start(bf16[256,256]{1,0:T(8,128)(2,1)S(1)} %collective-permute-done.refs_1_), channel_id=1, source_target_pairs={{0,4},{4,8},{8,12},{12,14},{14,10},{10,6},{6,2},{2,0},{1,5},{5,9},... | collective-permute-start | bytes 393224 | tf_op jit(solution)/shard_map/ppermute | solution.py:41
  13.2 5.4 %collective-permute-start.5 = (bf16[256,256]{1,0:T(8,128)(2,1)S(1)}, bf16[256,256]{1,0:T(8,128)(2,1)S(1)}, u32[]{:S(2)}, u32[]{:S(2)}) collective-permute-start(bf16[256,256]{1,0:T(8,128)(2,1)S(1)} %collective-permute-done.3.refs_4_), channel_id=1, source_target_pairs={{4,0},{8,4},{12,8},{14,12},{10,14},{6,10},{2,6},{0,2},{5,1},{9,5},... | collective-permute-start | bytes 393224 | tf_op jit(solution)/shard_map/ppermute | solution.py:42
  14.9 5.7 %collective-permute-start.4 = (bf16[256,256]{1,0:T(8,128)(2,1)S(1)}, bf16[256,256]{1,0:T(8,128)(2,1)S(1)}, u32[]{:S(2)}, u32[]{:S(2)}) collective-permute-start(bf16[256,256]{1,0:T(8,128)(2,1)S(1)} %collective-permute-done.2.refs_3_), channel_id=1, source_target_pairs={{0,4},{4,8},{8,12},{12,14},{14,10},{10,6},{6,2},{2,0},{1,5},{5,9},... | collective-permute-start | bytes 393224 | tf_op jit(solution)/shard_map/ppermute | solution.py:41
  15.2 5.6 %copy-start.11 = (s32[2,2]{1,0:T(2,128)S(1)}, s32[2,2]{1,0:T(2,128)}, u32[]{:S(2)}) copy-start(s32[2,2]{1,0:T(2,128)} %param.25) | copy-start | bytes 52
  15.2 5.6 %copy-start.12 = (s32[8]{0:T(128)S(1)}, s32[8]{0:T(128)}, u32[]{:S(2)}) copy-start(s32[8]{0:T(128)} %constant.101.clone) | copy-start | bytes 100
  15.2 19.3 %copy-start.3 = (bf16[2,8,32,256]{3,2,1,0:T(8,128)(2,1)S(1)}, bf16[2,8,32,256]{3,2,1,0:T(8,128)(2,1)}, u32[]{:S(2)}) copy-start(bf16[2,8,32,256]{3,2,1,0:T(8,128)(2,1)} %refs_9_.7) | copy-start | bytes 786436
  18.6 15.9 %collective-permute-start.7 = (bf16[128,256]{1,0:T(8,128)(2,1)S(1)}, bf16[128,256]{1,0:T(8,128)(2,1)S(1)}, u32[]{:S(2)}, u32[]{:S(2)}) collective-permute-start(bf16[128,256]{1,0:T(8,128)(2,1)S(1)} %slice.17), channel_id=1, source_target_pairs={{4,0},{8,4},{12,8},{14,12},{10,14},{6,10},{2,6},{0,2},{5,1},{9,5},... | collective-permute-start | bytes 196616 | tf_op jit(solution)/shard_map/ppermute | solution.py:51
  20.6 13.9 %collective-permute-start.6 = (bf16[128,256]{1,0:T(8,128)(2,1)S(1)}, bf16[128,256]{1,0:T(8,128)(2,1)S(1)}, u32[]{:S(2)}, u32[]{:S(2)}) collective-permute-start(bf16[128,256]{1,0:T(8,128)(2,1)S(1)} %slice.16), channel_id=1, source_target_pairs={{0,4},{4,8},{8,12},{12,14},{14,10},{10,6},{6,2},{2,0},{1,5},{5,9},... | collective-permute-start | bytes 196616 | tf_op jit(solution)/shard_map/ppermute | solution.py:50
  28.1 0.7 copy-start.7
  34.5 0.7 copy-start.6
  35.2 1.2 %copy-start = (bf16[2,2,2,256,256]{4,3,2,1,0:T(8,128)(2,1)S(1)}, bf16[2,2,2,256,256]{4,3,2,1,0:T(8,128)(2,1)}, u32[]{:S(2)}) copy-start(bf16[2,2,2,256,256]{4,3,2,1,0:T(8,128)(2,1)} %refs_11_.7) | copy-start | bytes 3145732
  36.4 3.1 %copy-start.9 = (f32[256]{0:T(256)S(1)}, f32[256]{0:T(256)}, u32[]{:S(2)}) copy-start(f32[256]{0:T(256)} %param.19) | copy-start | bytes 3076
  36.4 3.1 %copy-start.10 = (f32[256]{0:T(256)S(1)}, f32[256]{0:T(256)}, u32[]{:S(2)}) copy-start(f32[256]{0:T(256)} %param.18) | copy-start | bytes 3076
  36.4 3.9 %copy-start.1 = (bf16[2,2,2,256,256]{4,3,2,1,0:T(8,128)(2,1)S(1)}, bf16[2,2,2,256,256]{4,3,2,1,0:T(8,128)(2,1)}, u32[]{:S(2)}) copy-start(bf16[2,2,2,256,256]{4,3,2,1,0:T(8,128)(2,1)} %refs_11_.7) | copy-start | bytes 3145732
  39.4 3.9 %collective-permute-start.8 = (bf16[2,256,256]{2,1,0:T(8,128)(2,1)S(1)}, bf16[2,256,256]{2,1,0:T(8,128)(2,1)S(1)}, u32[]{:S(2)}, u32[]{:S(2)}) collective-permute-start(bf16[2,256,256]{2,1,0:T(8,128)(2,1)S(1)} %shard_map.159), channel_id=1, source_target_pairs={{0,1},{1,0},{2,3},{3,2},{4,5},{5,4},{6,7},{7,6},{8,9},{9,8},{10,11... | collective-permute-start | bytes 786440 | tf_op jit(solution)/shard_map/ppermute | solution.py:253
  39.4 0.7 copy-start.8
  40.3 3.0 %copy-start.4 = (f32[256,256]{1,0:T(8,128)S(1)}, f32[256,256]{1,0:T(8,128)}, u32[]{:S(2)}) copy-start(f32[256,256]{1,0:T(8,128)} %state.3) | copy-start | bytes 786436
  40.3 3.0 %copy-start.5 = (f32[256,256]{1,0:T(8,128)S(1)}, f32[256,256]{1,0:T(8,128)}, u32[]{:S(2)}) copy-start(f32[256,256]{1,0:T(8,128)} %tau.3) | copy-start | bytes 786436
  44.7 6.0 %collective-permute-start.10 = (bf16[256,256]{1,0:T(8,128)(2,1)S(1)}, bf16[256,256]{1,0:T(8,128)(2,1)S(1)}, u32[]{:S(2)}, u32[]{:S(2)}) collective-permute-start(bf16[256,256]{1,0:T(8,128)(2,1)S(1)} %get-tuple-element.7.refs_0_), channel_id=1, source_target_pairs={{4,0},{8,4},{12,8},{14,12},{10,14},{6,10},{2,6},{0,2},{5,1},{9,5},... | collective-permute-start | bytes 393224 | tf_op jit(solution)/shard_map/ppermute | solution.py:42
  46.5 5.9 %collective-permute-start.9 = (bf16[256,256]{1,0:T(8,128)(2,1)S(1)}, bf16[256,256]{1,0:T(8,128)(2,1)S(1)}, u32[]{:S(2)}, u32[]{:S(2)}) collective-permute-start(bf16[256,256]{1,0:T(8,128)(2,1)S(1)} %get-tuple-element.7.refs_0_), channel_id=1, source_target_pairs={{0,4},{4,8},{8,12},{12,14},{14,10},{10,6},{6,2},{2,0},{1,5},{5,9},... | collective-permute-start | bytes 393224 | tf_op jit(solution)/shard_map/ppermute | solution.py:41
  50.7 5.2 %collective-permute-start.12 = (bf16[256,256]{1,0:T(8,128)(2,1)S(1)}, bf16[256,256]{1,0:T(8,128)(2,1)S(1)}, u32[]{:S(2)}, u32[]{:S(2)}) collective-permute-start(bf16[256,256]{1,0:T(8,128)(2,1)S(1)} %collective-permute-done.10.refs_2_), channel_id=1, source_target_pairs={{4,0},{8,4},{12,8},{14,12},{10,14},{6,10},{2,6},{0,2},{5,1},{9,5},... | collective-permute-start | bytes 393224 | tf_op jit(solution)/shard_map/ppermute | solution.py:42
  52.4 5.1 %collective-permute-start.11 = (bf16[256,256]{1,0:T(8,128)(2,1)S(1)}, bf16[256,256]{1,0:T(8,128)(2,1)S(1)}, u32[]{:S(2)}, u32[]{:S(2)}) collective-permute-start(bf16[256,256]{1,0:T(8,128)(2,1)S(1)} %collective-permute-done.9.refs_1_), channel_id=1, source_target_pairs={{0,4},{4,8},{8,12},{12,14},{14,10},{10,6},{6,2},{2,0},{1,5},{5,9},... | collective-permute-start | bytes 393224 | tf_op jit(solution)/shard_map/ppermute | solution.py:41
  55.9 5.0 %collective-permute-start.14 = (bf16[256,256]{1,0:T(8,128)(2,1)S(1)}, bf16[256,256]{1,0:T(8,128)(2,1)S(1)}, u32[]{:S(2)}, u32[]{:S(2)}) collective-permute-start(bf16[256,256]{1,0:T(8,128)(2,1)S(1)} %collective-permute-done.12.refs_4_), channel_id=1, source_target_pairs={{4,0},{8,4},{12,8},{14,12},{10,14},{6,10},{2,6},{0,2},{5,1},{9,5},... | collective-permute-start | bytes 393224 | tf_op jit(solution)/shard_map/ppermute | solution.py:42
  57.5 5.0 %collective-permute-start.13 = (bf16[256,256]{1,0:T(8,128)(2,1)S(1)}, bf16[256,256]{1,0:T(8,128)(2,1)S(1)}, u32[]{:S(2)}, u32[]{:S(2)}) collective-permute-start(bf16[256,256]{1,0:T(8,128)(2,1)S(1)} %collective-permute-done.11.refs_3_), channel_id=1, source_target_pairs={{0,4},{4,8},{8,12},{12,14},{14,10},{10,6},{6,2},{2,0},{1,5},{5,9},... | collective-permute-start | bytes 393224 | tf_op jit(solution)/shard_map/ppermute | solution.py:41
  60.9 4.3 %collective-permute-start.16 = (bf16[128,256]{1,0:T(8,128)(2,1)S(1)}, bf16[128,256]{1,0:T(8,128)(2,1)S(1)}, u32[]{:S(2)}, u32[]{:S(2)}) collective-permute-start(bf16[128,256]{1,0:T(8,128)(2,1)S(1)} %slice.19), channel_id=1, source_target_pairs={{4,0},{8,4},{12,8},{14,12},{10,14},{6,10},{2,6},{0,2},{5,1},{9,5},... | collective-permute-start | bytes 196616 | tf_op jit(solution)/shard_map/ppermute | solution.py:51
  62.5 4.3 %collective-permute-start.15 = (bf16[128,256]{1,0:T(8,128)(2,1)S(1)}, bf16[128,256]{1,0:T(8,128)(2,1)S(1)}, u32[]{:S(2)}, u32[]{:S(2)}) collective-permute-start(bf16[128,256]{1,0:T(8,128)(2,1)S(1)} %slice.18), channel_id=1, source_target_pairs={{0,4},{4,8},{8,12},{12,14},{14,10},{10,6},{6,2},{2,0},{1,5},{5,9},... | collective-permute-start | bytes 196616 | tf_op jit(solution)/shard_map/ppermute | solution.py:50
  69.8 3.0 %collective-permute-start.17 = (bf16[2,256,256]{2,1,0:T(8,128)(2,1)S(1)}, bf16[2,256,256]{2,1,0:T(8,128)(2,1)S(1)}, u32[]{:S(2)}, u32[]{:S(2)}) collective-permute-start(bf16[2,256,256]{2,1,0:T(8,128)(2,1)S(1)} %shard_map.162), channel_id=1, source_target_pairs={{0,1},{1,0},{2,3},{3,2},{4,5},{5,4},{6,7},{7,6},{8,9},{9,8},{10,11... | collective-permute-start | bytes 786440 | tf_op jit(solution)/shard_map/ppermute | solution.py:253

commit v2 on v1

v2 whole, which is shorter than its diff:
```python
import functools

import jax
import jax.numpy as jnp
from jax import lax
from jax.experimental import pallas as pl
from jax.experimental.pallas import tpu as pltpu
from jax.sharding import PartitionSpec as P

NEWTON = 2
RING_LIMIT = 16

damping = 0.5
sigma_floor = 0.5
section_step = 0.1


def ring_rows(count):
    return list(range(0, count, 2)) + list(range(1, count, 2))[::-1]


def row_met(turn, row, col, count):
    place = jnp.where(row % 2 == 0, row // 2, count - 1 - row // 2)
    place = lax.rem(place + turn * (2 * col - 1) + count, count)
    return jnp.where(place < count // 2, 2 * place, 2 * (count - 1 - place) + 1)


def ring_gather(block, count, cols):
    ring = ring_rows(count)
    hops = [(ring[i], ring[(i + 1) % count]) for i in range(count)]

    def way(turn):
        return [
            ((a, b) if (c + turn) % 2 == 0 else (b, a), c) for c in range(cols) for a, b in hops
        ]

    ahead, back = ([(a * cols + c, b * cols + c) for (a, b), c in way(turn)] for turn in (0, 1))
    first = second = block
    found = [block]
    for _ in range((count - 1) // 2):
        first = lax.ppermute(first, ("row", "col"), ahead)
        second = lax.ppermute(second, ("row", "col"), back)
        found += [first, second]
    half = block.shape[0] // 2
    top = lax.ppermute(first[:half], ("row", "col"), ahead)
    low = lax.ppermute(second[half:], ("row", "col"), back)
    return found, [top, low]


def arrivals(count):
    return [0] + [sign * step for step in range(1, (count - 1) // 2 + 1) for sign in (1, -1)]


def near_kernel(count, turns, ring, row_ref, col_ref, rank_ref, near_ref, v_ref, d_ref, *refs):
    blocks = refs[: len(turns)]
    proj_ref, sums_ref, picked = refs[len(turns) :]
    rank_count = v_ref.shape[2]
    row, col = row_ref[0], col_ref[0]
    rows, slots = near_ref.shape
    met = [row_met(turn, row, col, count) if ring else turn for turn in turns]
    proj_ref[...] = jnp.zeros_like(proj_ref)
    picked[...] = jnp.zeros_like(picked)
    for q, block in zip(met, blocks):
        for p in range(rows):
            part = jnp.dot(v_ref[p, q], block[...], preferred_element_type=jnp.float32)
            inside = lax.broadcasted_iota(jnp.int32, part.shape, 0) < rank_ref[p, q]
            at = pl.ds(pl.multiple_of(q * rank_count, rank_count), rank_count)
            proj_ref[p, at, :] = jnp.where(inside, part, 0.0).astype(proj_ref.dtype)
            for s in range(slots):

                @pl.when(near_ref[p, s] - col * count == q)
                def _():
                    picked[p * slots + s] = block[...]

    for p in range(rows):
        for kind in range(d_ref.shape[0]):
            total = jnp.dot(d_ref[kind, p, 0], picked[p * slots], preferred_element_type=jnp.float32)
            for s in range(1, slots):
                total += jnp.dot(
                    d_ref[kind, p, s], picked[p * slots + s], preferred_element_type=jnp.float32
                )
            sums_ref[p, kind] = total


def finish_kernel(
    count, turn, ring, swap, row_ref, col_ref, rank_ref, near_ref, v_ref, u_ref, d_ref, proj_ref, sums_ref, *refs
):
    parts = refs[:-2]
    out_ref, proj = refs[-2:]
    rank_count = v_ref.shape[2]
    row, col = row_ref[0], col_ref[0]
    slots = near_ref.shape[1]
    p = 1 - col if swap else col
    q = row_met(turn, row, col, count) if ring else turn
    tall = v_ref.shape[3] // len(parts)

    def times(weights):
        pieces = [
            jnp.dot(weights[:, i * tall : (i + 1) * tall], part[...], preferred_element_type=jnp.float32)
            for i, part in enumerate(parts)
        ]
        return sum(pieces[1:], pieces[0])

    proj[...] = proj_ref[p]
    last = times(v_ref[p, q])
    inside = lax.broadcasted_iota(jnp.int32, last.shape, 0) < rank_ref[p, q]
    at = pl.ds(pl.multiple_of(q * rank_count, rank_count), rank_count)
    proj[at, :] = jnp.where(inside, last, 0.0).astype(proj.dtype)
    for kind in range(u_ref.shape[0]):
        total = sums_ref[p, kind] + jnp.dot(
            u_ref[kind, p], proj[...], preferred_element_type=jnp.float32
        )
        out_ref[kind] = total.astype(out_ref.dtype)
    for s in range(slots):

        @pl.when(near_ref[p, s] - col * count == q)
        def _():
            for kind in range(u_ref.shape[0]):
                total = out_ref[kind].astype(jnp.float32) + times(d_ref[kind, p, s])
                out_ref[kind] = total.astype(out_ref.dtype)


def on_core(kernel, outs, scalars, arrays, scratch, flops):
    smem, vmem = pl.BlockSpec(memory_space=pltpu.SMEM), pl.BlockSpec(memory_space=pltpu.VMEM)
    return pl.pallas_call(
        kernel,
        out_shape=outs,
        in_specs=[smem] * len(scalars) + [vmem] * len(arrays),
        out_specs=jax.tree.map(lambda _: vmem, outs),
        scratch_shapes=scratch,
        compiler_params=pltpu.CompilerParams(vmem_limit_bytes=32 * 1024 * 1024),
        cost_estimate=pl.CostEstimate(
            flops=flops, bytes_accessed=sum(a.size * a.dtype.itemsize for a in arrays), transcendentals=0
        ),
    )(*scalars, *arrays)


def inverse_sinh(value):
    magnitude = jnp.abs(value)
    result = jnp.log(magnitude + jnp.sqrt(magnitude * magnitude + 1.0))
    return jnp.where(value < 0.0, -result, result)


def sinh_cosh(value):
    grown = jnp.exp(value)
    shrunk = 1.0 / grown
    square = value * value
    small = value * (
        1.0 + square * (1 / 6 + square * (1 / 120 + square * (1 / 5040 + square * (1 / 362880))))
    )
    sinh = jnp.where(square < 1.0, small, 0.5 * (grown - shrunk))
    return sinh, 0.5 * (grown + shrunk)


def friction(shear, normal, state, tau_load, sigma_base, a_wide, b_wide):
    tau = tau_load + shear
    sigma = jnp.maximum(sigma_base + normal, sigma_floor)
    weight = jnp.exp(-state / a_wide)
    stiff = sigma * a_wide
    first = tau / stiff
    second = inverse_sinh(tau / (2.0 * damping * weight))
    slope = jnp.where(jnp.abs(first) < jnp.abs(second), first, second)
    for newton_step in range(NEWTON):
        sinh, cosh = sinh_cosh(slope)
        excess = stiff * slope + 2.0 * damping * weight * sinh - tau
        deriv = stiff + 2.0 * damping * weight * cosh
        slope = slope - excess / deriv
    rate = 2.0 * weight * sinh_cosh(slope)[0]
    change = b_wide * (jnp.exp(-state / b_wide) - jnp.abs(rate))
    return (rate, change)


def section_one_kernel(own, other, state, tau, coef, stress, normal, rate, change, rate_half):
    size, members = state.shape
    step = min(size, 64)

    @pl.loop(0, size // step)
    def _(index):
        rows = pl.ds(pl.multiple_of(index * step, step), step)
        shear = own[0, rows, :] + other[0, rows, :].astype(jnp.float32)
        press = own[1, rows, :] + other[1, rows, :].astype(jnp.float32)
        stress[rows, :] = shear
        normal[rows, :] = press
        first, second = friction(
            shear, press, state[rows, :], tau[rows, :], coef[rows, 0:1], coef[rows, 1:2], coef[rows, 2:3]
        )
        rate[rows, :] = first
        change[rows, :] = second
        rate_half[rows, :] = first.astype(rate_half.dtype)


def section_two_kernel(own, other, state, tau, coef, stress, normal, rate, change, mean_rate, mean_change):
    size, members = state.shape
    step = min(size, 64)

    @pl.loop(0, size // step)
    def _(index):
        rows = pl.ds(pl.multiple_of(index * step, step), step)
        shear = stress[rows, :] + section_step * (own[0, rows, :] + other[0, rows, :].astype(jnp.float32))
        press = normal[rows, :] + section_step * (own[1, rows, :] + other[1, rows, :].astype(jnp.float32))
        first, second = friction(
            shear,
            press,
            state[rows, :] + section_step * change[rows, :],
            tau[rows, :],
            coef[rows, 0:1],
            coef[rows, 1:2],
            coef[rows, 2:3],
        )
        mean_rate[rows, :] = (rate[rows, :] + first) * 0.5
        mean_change[rows, :] = (change[rows, :] + second) * 0.5


def section(kernel, outs, *args):
    vmem = pl.BlockSpec(memory_space=pltpu.VMEM)
    return pl.pallas_call(
        kernel,
        out_shape=outs,
        in_specs=[vmem] * len(args),
        out_specs=tuple([vmem] * len(outs)),
        compiler_params=pltpu.CompilerParams(vmem_limit_bytes=24 * 1024 * 1024),
        cost_estimate=pl.CostEstimate(
            flops=200 * outs[0].size, bytes_accessed=8 * 4 * outs[0].size, transcendentals=12 * outs[0].size
        ),
    )(*args)


def body(
    slip_deficit,
    state_var,
    tau_load,
    sigma_base,
    a_coef,
    b_coef,
    v_basis,
    u_basis,
    dense_blocks,
    block_ranks,
    near_index,
):
    count, cols = lax.axis_size("row"), lax.axis_size("col")
    size, members = slip_deficit.shape
    kinds, rows, _, rank_count, _ = u_basis.shape
    slots = near_index.shape[1]
    ring = cols == 2 and count % 2 == 0 and 4 <= count <= RING_LIMIT
    coef = jnp.stack([sigma_base, a_coef, b_coef], axis=1)
    u_turned = jnp.swapaxes(u_basis.reshape(kinds, rows, count * rank_count, size), 2, 3)
    scalars = (
        lax.axis_index("row").reshape(1),
        lax.axis_index("col").reshape(1),
        block_ranks,
        near_index,
    )
    swap = [(0, 1), (1, 0)]
    narrow = jnp.bfloat16

    def lattice(field_half):
        if ring:
            found, last = ring_gather(field_half, count, cols)
            turns, turn = arrivals(count), count // 2
        else:
            whole = lax.all_gather(field_half, "row", axis=0)
            found, last = [whole[r] for r in range(count - 1)], [whole[count - 1]]
            turns, turn = list(range(count - 1)), count - 1
        proj, sums = on_core(
            functools.partial(near_kernel, count, turns, ring),
            (
                jax.ShapeDtypeStruct((rows, count * rank_count, members), narrow),
                jax.ShapeDtypeStruct((rows, kinds, size, members), jnp.float32),
            ),
            scalars,
            (v_basis, dense_blocks, *found),
            [pltpu.VMEM((rows * slots, size, members), narrow)],
            2 * rows * size * members * (count * rank_count + kinds * slots * size),
        )

        def finish(twin, kind):
            return on_core(
                functools.partial(finish_kernel, count, turn, ring, twin),
                jax.ShapeDtypeStruct((kinds, size, members), kind),
                scalars,
                (v_basis, u_turned, dense_blocks, proj, sums, *last),
                [pltpu.VMEM((count * rank_count, members), narrow)],
                2 * kinds * size * members * count * rank_count,
            )

        other = lax.ppermute(finish(True, narrow), "col", swap)
        return finish(False, jnp.float32), other

    full = jax.ShapeDtypeStruct(slip_deficit.shape, jnp.float32)
    half = jax.ShapeDtypeStruct(slip_deficit.shape, narrow)
    own, other = lattice(slip_deficit.astype(narrow))
    stress, normal, rate, change, rate_half = section(
        section_one_kernel, (full, full, full, full, half), own, other, state_var, tau_load, coef
    )
    own, other = lattice(rate_half)
    return section(
        section_two_kernel,
        (full, full),
        own,
        other,
        state_var,
        tau_load,
        coef,
        stress,
        normal,
        rate,
        change,
    )


def solution(mesh):
    placed = (
        P(("row", "col"), "scen"),
        P(("row", "col"), "scen"),
        P(("row", "col"), "scen"),
        P(("row", "col")),
        P(("row", "col")),
        P(("row", "col")),
        P("row", "col", None, None),
        P(None, "row", "col", None, None),
        P(None, "row", "col", None, None),
        P("row", "col"),
        P("row", "col"),
    )
    return jax.shard_map(
        body,
        mesh=mesh,
        in_specs=placed,
        out_specs=(P(("row", "col"), "scen"), P(("row", "col"), "scen")),
        check_vma=False,
    )
```

time: 75.5 us -> 66.4 us (0.88)
  between operations: 7.47 us -> 0.89 us
  waiting for transfers between devices: 23.6 us -> 22.2 us
  local copies, waits for them, and re-layouts: 9.69 us -> 8.93 us
    another operation x1 -> x0, local copies, waits for them, and re-layouts: 5.07 us -> none  [lattice(): order = jnp.stack([row for row, _ in found])]
    unnamed x26 -> x34, local copies, waits for them, and re-layouts: 3.2 us -> 6.24 us
    ppermute x18, waiting for transfers between devices: 23.6 us -> 22.2 us  [the longest x6 19.6 us: ring_gather(): first = lax.ppermute(first, ('row', 'col'), ahead)]
    reshape x0 -> x1, local copies, waits for them, and re-layouts: none -> 1.29 us  [body(): u_basis.reshape(kinds, rows, count * rank_count, size)]
    dynamic_slice x2 -> x0, local copies, waits for them, and re-layouts: 1.25 us -> none  [the longest x1 0.67 us: row_at(): return table[(my_place + shift) % count]]
    slice x4, local copies, waits for them, and re-layouts: 0.02 us -> 1.26 us  [the longest x2 0.64 us: ring_gather(): low = lax.ppermute(second[half:], ('row', 'col'), back)]
    pallas_call x2, Pallas kernels: 3.57 us -> 4.52 us  [section(): pl.pallas_call(kernel, out_shape=outs, in_specs=[vmem] * len(args), out_s...]
    pallas_call x4 -> x6, Pallas kernels: 11.8 us -> 11.3 us  [on_core(): pl.pallas_call(kernel, out_shape=outs, in_specs=[smem] * len(scalars) + [...]
  transfers between devices with their start and end apart: 18 -> 18, of which waited for: 8 -> 10; matrix products, arithmetic and copies ran while one was open for 9% -> 4% of each run, Pallas kernels for 8% -> 13%
where the time goes in v2:
time: 66.4 us; the launch traced here: 66.3 us
  waiting for transfers between devices  22.2 us (33%)
  starting transfers between devices  17.4 us (26%)
  Pallas kernels  15.8 us (24%)
  local copies, waits for them, and re-layouts  8.93 us (13%)
  other arithmetic  1.06 us (2%)
  between operations  0.89 us (1%)
    ppermute x6, waiting for transfers between devices, ring_gather(): first = lax.ppermute(first, ('row', 'col'), ahead)  19.6 us
    pallas_call x6, Pallas kernels, on_core(): pl.pallas_call(kernel, out_shape=outs, in_specs=[smem] * len(scalars) + [...  11.3 us
    ppermute x6, starting transfers between devices, ring_gather(): first = lax.ppermute(first, ('row', 'col'), ahead)  8.6 us
    unnamed x34, local copies, waits for them, and re-layouts  6.24 us
    ppermute x6, starting transfers between devices, ring_gather(): second = lax.ppermute(second, ('row', 'col'), back)  5.43 us
    pallas_call x2, Pallas kernels, section(): pl.pallas_call(kernel, out_shape=outs, in_specs=[vmem] * len(args), out_s...  4.52 us
    ppermute x6, waiting for transfers between devices, ring_gather(): second = lax.ppermute(second, ('row', 'col'), back)  1.97 us
    ppermute x2, starting transfers between devices, ring_gather(): low = lax.ppermute(second[half:], ('row', 'col'), back)  1.89 us
  transfers between devices with their start and end apart: 18, of which 10 were waited for; matrix products, arithmetic and copies ran while one was open for 4% of the time, Pallas kernels for 13%

profile of v2, /device:TPU:0, one launch (start us, length us, event | category | flops | bytes accessed | tf_op | source)
XLA Modules:
  0.0 66.3 jit_solution(13046855865982946763)
XLA Ops:
  0.6 1.1 %convert_element_type.3.refs_0_ = bf16[256,256]{1,0:T(8,128)(2,1)S(1)} convert(f32[256,256]{1,0:T(8,128)} %param.11) | non-fusion elementwise | flops 65536 | bytes 393216 | tf_op jit(solution)/shard_map/convert_element_type | solution.py:292
  1.7 3.1 %collective-permute-start = (bf16[256,256]{1,0:T(8,128)(2,1)S(1)}, bf16[256,256]{1,0:T(8,128)(2,1)S(1)}, u32[]{:S(2)}, u32[]{:S(2)}) collective-permute-start(bf16[256,256]{1,0:T(8,128)(2,1)S(1)} %convert_element_type.3.refs_0_), channel_id=1, source_target_pairs={{0,4},{4,8},{8,12},{12,14},{14,10},{10,6},{6,2},{2,0},{5,1},{9,5},... | collective-permute-start | bytes 393224 | tf_op jit(solution)/shard_map/ppermute | solution.py:41
  4.8 3.7 %collective-permute-done.refs_1_ = bf16[256,256]{1,0:T(8,128)(2,1)S(1)} collective-permute-done((bf16[256,256]{1,0:T(8,128)(2,1)S(1)}, bf16[256,256]{1,0:T(8,128)(2,1)S(1)}, u32[]{:S(2)}, u32[]{:S(2)}) %collective-permute-start) | collective-permute-done | bytes 131104 | tf_op jit(solution)/shard_map/ppermute | solution.py:41
  8.5 1.6 %collective-permute-start.2 = (bf16[256,256]{1,0:T(8,128)(2,1)S(1)}, bf16[256,256]{1,0:T(8,128)(2,1)S(1)}, u32[]{:S(2)}, u32[]{:S(2)}) collective-permute-start(bf16[256,256]{1,0:T(8,128)(2,1)S(1)} %collective-permute-done.refs_1_), channel_id=1, source_target_pairs={{0,4},{4,8},{8,12},{12,14},{14,10},{10,6},{6,2},{2,0},{5,1},{9,5},... | collective-permute-start | bytes 393224 | tf_op jit(solution)/shard_map/ppermute | solution.py:41
  10.1 0.9 %collective-permute-start.3 = (bf16[256,256]{1,0:T(8,128)(2,1)S(1)}, bf16[256,256]{1,0:T(8,128)(2,1)S(1)}, u32[]{:S(2)}, u32[]{:S(2)}) collective-permute-start(bf16[256,256]{1,0:T(8,128)(2,1)S(1)} %collective-permute-done.1.refs_2_), channel_id=1, source_target_pairs={{4,0},{8,4},{12,8},{14,12},{10,14},{6,10},{2,6},{0,2},{1,5},{5,9},... | collective-permute-start | bytes 393224 | tf_op jit(solution)/shard_map/ppermute | solution.py:42
  11.0 3.7 %collective-permute-done.2.refs_3_ = bf16[256,256]{1,0:T(8,128)(2,1)S(1)} collective-permute-done((bf16[256,256]{1,0:T(8,128)(2,1)S(1)}, bf16[256,256]{1,0:T(8,128)(2,1)S(1)}, u32[]{:S(2)}, u32[]{:S(2)}) %collective-permute-start.2) | collective-permute-done | bytes 131104 | tf_op jit(solution)/shard_map/ppermute | solution.py:41
  14.7 0.3 collective-permute-start.4
  15.0 0.6 copy-done.8
  15.7 0.7 %collective-permute-done.3.refs_4_ = bf16[256,256]{1,0:T(8,128)(2,1)S(1)} collective-permute-done((bf16[256,256]{1,0:T(8,128)(2,1)S(1)}, bf16[256,256]{1,0:T(8,128)(2,1)S(1)}, u32[]{:S(2)}, u32[]{:S(2)}) %collective-permute-start.3) | collective-permute-done | bytes 131104 | tf_op jit(solution)/shard_map/ppermute | solution.py:42
  16.4 1.0 %collective-permute-start.5 = (bf16[256,256]{1,0:T(8,128)(2,1)S(1)}, bf16[256,256]{1,0:T(8,128)(2,1)S(1)}, u32[]{:S(2)}, u32[]{:S(2)}) collective-permute-start(bf16[256,256]{1,0:T(8,128)(2,1)S(1)} %collective-permute-done.3.refs_4_), channel_id=1, source_target_pairs={{4,0},{8,4},{12,8},{14,12},{10,14},{6,10},{2,6},{0,2},{1,5},{5,9},... | collective-permute-start | bytes 393224 | tf_op jit(solution)/shard_map/ppermute | solution.py:42
  17.4 0.6 copy-done.10
  18.0 1.7 %collective-permute-done.4.refs_5_ = bf16[256,256]{1,0:T(8,128)(2,1)S(1)} collective-permute-done((bf16[256,256]{1,0:T(8,128)(2,1)S(1)}, bf16[256,256]{1,0:T(8,128)(2,1)S(1)}, u32[]{:S(2)}, u32[]{:S(2)}) %collective-permute-start.4) | collective-permute-done | bytes 131104 | tf_op jit(solution)/shard_map/ppermute | solution.py:41
  19.7 0.6 slice.16
  20.3 0.3 collective-permute-start.6
  20.6 1.3 %collective-permute-done.5.refs_6_ = bf16[256,256]{1,0:T(8,128)(2,1)S(1)} collective-permute-done((bf16[256,256]{1,0:T(8,128)(2,1)S(1)}, bf16[256,256]{1,0:T(8,128)(2,1)S(1)}, u32[]{:S(2)}, u32[]{:S(2)}) %collective-permute-start.5) | collective-permute-done | bytes 131104 | tf_op jit(solution)/shard_map/ppermute | solution.py:42
  21.9 0.6 slice.17
  22.6 0.8 %collective-permute-start.7 = (bf16[128,256]{1,0:T(8,128)(2,1)}, bf16[128,256]{1,0:T(8,128)(2,1)}, u32[]{:S(2)}, u32[]{:S(2)}) collective-permute-start(bf16[128,256]{1,0:T(8,128)(2,1)} %slice.17), channel_id=1, source_target_pairs={{4,0},{8,4},{12,8},{14,12},{10,14},{6,10},{2,6},{0,2},{1,5},{5,9},... | collective-permute-start | bytes 196616 | tf_op jit(solution)/shard_map/ppermute | solution.py:46
  23.4 1.3 %copy.18 = bf16[2,2,256,256]{2,3,1,0:T(8,128)(2,1)S(1)} copy(bf16[2,2,256,256]{3,2,1,0:T(8,128)(2,1)} %bitcast.11) | data formatting | bytes 1048576 | tf_op jit(solution)/shard_map/reshape | solution.py:247
  24.7 0.6 copy-done.12
  25.4 0.9 %copy-done.5 = bf16[256,256]{1,0:T(8,128)(2,1)S(1)} copy-done((bf16[256,256]{1,0:T(8,128)(2,1)S(1)}, bf16[256,256]{1,0:T(8,128)(2,1)}, u32[]{:S(2)}) %copy-start.5) | copy-done | bytes 131096
  26.3 0.9 %copy-done.7 = bf16[256,256]{1,0:T(8,128)(2,1)S(1)} copy-done((bf16[256,256]{1,0:T(8,128)(2,1)S(1)}, bf16[256,256]{1,0:T(8,128)(2,1)}, u32[]{:S(2)}) %copy-start.7) | copy-done | bytes 131096
  27.2 0.9 %copy-done.9 = bf16[256,256]{1,0:T(8,128)(2,1)S(1)} copy-done((bf16[256,256]{1,0:T(8,128)(2,1)S(1)}, bf16[256,256]{1,0:T(8,128)(2,1)}, u32[]{:S(2)}) %copy-start.9) | copy-done | bytes 131096
  28.1 0.9 %copy-done.11 = bf16[256,256]{1,0:T(8,128)(2,1)S(1)} copy-done((bf16[256,256]{1,0:T(8,128)(2,1)S(1)}, bf16[256,256]{1,0:T(8,128)(2,1)}, u32[]{:S(2)}) %copy-start.11) | copy-done | bytes 131096
  29.0 3.2 %shard_map.122 = (bf16[2,256,256]{2,1,0:T(8,128)(2,1)S(1)}, f32[2,2,256,256]{3,2,1,0:T(8,128)S(1)}) custom-call(s32[1]{0:T(128)} %bitcast.row_ref, s32[1]{0:T(128)} %bitcast.1.col_ref, s32[2,8]{1,0:T(2,128)S(1)} %copy-done.12, s32[2,2]{1,0:T(2,128)S(1)} %copy-done.13, bf16[2,8,32,256]{3,2,1,0:T(8,128)(2,1)S(1)} %copy-done.1, ...), custom_call_target="tpu_custom_call" | custom-call | flops 335544320 | bytes 2228224 | tf_op jit(solution)/shard_map/pallas_call | solution.py:125
  32.2 1.5 %shard_map.124 = bf16[2,256,256]{2,1,0:T(8,128)(2,1)S(1)} custom-call(s32[1]{0:T(128)} %bitcast.row_ref, s32[1]{0:T(128)} %bitcast.1.col_ref, s32[2,8]{1,0:T(2,128)S(1)} %copy-done.12, s32[2,2]{1,0:T(2,128)S(1)} %copy-done.13, bf16[2,8,32,256]{3,2,1,0:T(8,128)(2,1)S(1)} %copy-done.1, bf16[2,2,256,256]{3,2,1,0:T(8,128)(2,1)S(1)} %bitcast.7, ...), custom_call_target="tpu_custom_call" | custom-call | flops 67108864 | bytes 3276800 | tf_op jit(solution)/shard_map/pallas_call | solution.py:125
  33.7 0.1 collective-permute-start.8
  33.8 0.7 copy-done.14
  34.5 0.1 copy.19.coef
  34.7 1.3 %shard_map.123.own = f32[2,256,256]{2,1,0:T(8,128)S(1)} custom-call(s32[1]{0:T(128)} %bitcast.row_ref, s32[1]{0:T(128)} %bitcast.1.col_ref, s32[2,8]{1,0:T(2,128)S(1)} %copy-done.12, s32[2,2]{1,0:T(2,128)S(1)} %copy-done.13, bf16[2,8,32,256]{3,2,1,0:T(8,128)(2,1)S(1)} %copy-done.1, bf16[2,2,256,256]{3,2,1,0:T(8,128)(2,1)S(1)} %bitcast.8, ...), custom_call_target="tpu_custom_call" | custom-call | flops 67108864 | bytes 3276800 | tf_op jit(solution)/shard_map/pallas_call | solution.py:125
  36.0 2.3 %shard_map.125 = (f32[256,256]{1,0:T(8,128)S(1)}, f32[256,256]{1,0:T(8,128)S(1)}, f32[256,256]{1,0:T(8,128)S(1)}, f32[256,256]{1,0:T(8,128)S(1)}, bf16[256,256]{1,0:T(8,128)(2,1)S(1)}) custom-call(f32[2,256,256]{2,1,0:T(8,128)S(1)} %shard_map.123.own, bf16[2,256,256]{2,1,0:T(8,128)(2,1)} %collective-permute-done.8.other, f32[256,256]{1,0:T(8,128)S(1)} %copy-done.2, ...), custom_call_target="tpu_custom_call" | custom-call | flops 13107200 | bytes 2097152 | tf_op jit(solution)/shard_map/pallas_call | solution.py:216
  38.3 1.0 %collective-permute-start.9 = (bf16[256,256]{1,0:T(8,128)(2,1)S(1)}, bf16[256,256]{1,0:T(8,128)(2,1)S(1)}, u32[]{:S(2)}, u32[]{:S(2)}) collective-permute-start(bf16[256,256]{1,0:T(8,128)(2,1)S(1)} %get-tuple-element.13.refs_0_), channel_id=1, source_target_pairs={{0,4},{4,8},{8,12},{12,14},{14,10},{10,6},{6,2},{2,0},{5,1},{9,5},... | collective-permute-start | bytes 393224 | tf_op jit(solution)/shard_map/ppermute | solution.py:41
  39.3 1.2 %collective-permute-start.10 = (bf16[256,256]{1,0:T(8,128)(2,1)S(1)}, bf16[256,256]{1,0:T(8,128)(2,1)S(1)}, u32[]{:S(2)}, u32[]{:S(2)}) collective-permute-start(bf16[256,256]{1,0:T(8,128)(2,1)S(1)} %get-tuple-element.13.refs_0_), channel_id=1, source_target_pairs={{4,0},{8,4},{12,8},{14,12},{10,14},{6,10},{2,6},{0,2},{1,5},{5,9},... | collective-permute-start | bytes 393224 | tf_op jit(solution)/shard_map/ppermute | solution.py:42
  40.6 3.0 %collective-permute-done.9.refs_1_ = bf16[256,256]{1,0:T(8,128)(2,1)S(1)} collective-permute-done((bf16[256,256]{1,0:T(8,128)(2,1)S(1)}, bf16[256,256]{1,0:T(8,128)(2,1)S(1)}, u32[]{:S(2)}, u32[]{:S(2)}) %collective-permute-start.9) | collective-permute-done | bytes 131104 | tf_op jit(solution)/shard_map/ppermute | solution.py:41
  43.5 1.5 %collective-permute-start.11 = (bf16[256,256]{1,0:T(8,128)(2,1)S(1)}, bf16[256,256]{1,0:T(8,128)(2,1)S(1)}, u32[]{:S(2)}, u32[]{:S(2)}) collective-permute-start(bf16[256,256]{1,0:T(8,128)(2,1)S(1)} %collective-permute-done.9.refs_1_), channel_id=1, source_target_pairs={{0,4},{4,8},{8,12},{12,14},{14,10},{10,6},{6,2},{2,0},{5,1},{9,5},... | collective-permute-start | bytes 393224 | tf_op jit(solution)/shard_map/ppermute | solution.py:41
  45.1 1.3 %collective-permute-start.12 = (bf16[256,256]{1,0:T(8,128)(2,1)S(1)}, bf16[256,256]{1,0:T(8,128)(2,1)S(1)}, u32[]{:S(2)}, u32[]{:S(2)}) collective-permute-start(bf16[256,256]{1,0:T(8,128)(2,1)S(1)} %collective-permute-done.10.refs_2_), channel_id=1, source_target_pairs={{4,0},{8,4},{12,8},{14,12},{10,14},{6,10},{2,6},{0,2},{1,5},{5,9},... | collective-permute-start | bytes 393224 | tf_op jit(solution)/shard_map/ppermute | solution.py:42
  46.4 3.9 %collective-permute-done.11.refs_3_ = bf16[256,256]{1,0:T(8,128)(2,1)S(1)} collective-permute-done((bf16[256,256]{1,0:T(8,128)(2,1)S(1)}, bf16[256,256]{1,0:T(8,128)(2,1)S(1)}, u32[]{:S(2)}, u32[]{:S(2)}) %collective-permute-start.11) | collective-permute-done | bytes 131104 | tf_op jit(solution)/shard_map/ppermute | solution.py:41
  50.3 1.1 %collective-permute-start.13 = (bf16[256,256]{1,0:T(8,128)(2,1)S(1)}, bf16[256,256]{1,0:T(8,128)(2,1)S(1)}, u32[]{:S(2)}, u32[]{:S(2)}) collective-permute-start(bf16[256,256]{1,0:T(8,128)(2,1)S(1)} %collective-permute-done.11.refs_3_), channel_id=1, source_target_pairs={{0,4},{4,8},{8,12},{12,14},{14,10},{10,6},{6,2},{2,0},{5,1},{9,5},... | collective-permute-start | bytes 393224 | tf_op jit(solution)/shard_map/ppermute | solution.py:41
  51.4 0.9 %collective-permute-start.14 = (bf16[256,256]{1,0:T(8,128)(2,1)S(1)}, bf16[256,256]{1,0:T(8,128)(2,1)S(1)}, u32[]{:S(2)}, u32[]{:S(2)}) collective-permute-start(bf16[256,256]{1,0:T(8,128)(2,1)S(1)} %collective-permute-done.12.refs_4_), channel_id=1, source_target_pairs={{4,0},{8,4},{12,8},{14,12},{10,14},{6,10},{2,6},{0,2},{1,5},{5,9},... | collective-permute-start | bytes 393224 | tf_op jit(solution)/shard_map/ppermute | solution.py:42
  52.4 3.6 %collective-permute-done.13.refs_5_ = bf16[256,256]{1,0:T(8,128)(2,1)S(1)} collective-permute-done((bf16[256,256]{1,0:T(8,128)(2,1)S(1)}, bf16[256,256]{1,0:T(8,128)(2,1)S(1)}, u32[]{:S(2)}, u32[]{:S(2)}) %collective-permute-start.13) | collective-permute-done | bytes 131104 | tf_op jit(solution)/shard_map/ppermute | solution.py:41
  55.9 1.0 %collective-permute-start.15 = (bf16[128,256]{1,0:T(8,128)(2,1)S(1)}, bf16[128,256]{1,0:T(8,128)(2,1)S(1)}, u32[]{:S(2)}, u32[]{:S(2)}) collective-permute-start(bf16[128,256]{1,0:T(8,128)(2,1)S(1)} %slice.18), channel_id=1, source_target_pairs={{0,4},{4,8},{8,12},{12,14},{14,10},{10,6},{6,2},{2,0},{5,1},{9,5},... | collective-permute-start | bytes 196616 | tf_op jit(solution)/shard_map/ppermute | solution.py:45
  57.0 1.1 %collective-permute-start.16 = (bf16[128,256]{1,0:T(8,128)(2,1)S(1)}, bf16[128,256]{1,0:T(8,128)(2,1)S(1)}, u32[]{:S(2)}, u32[]{:S(2)}) collective-permute-start(bf16[128,256]{1,0:T(8,128)(2,1)S(1)} %slice.19), channel_id=1, source_target_pairs={{4,0},{8,4},{12,8},{14,12},{10,14},{6,10},{2,6},{0,2},{1,5},{5,9},... | collective-permute-start | bytes 196616 | tf_op jit(solution)/shard_map/ppermute | solution.py:46
  58.0 3.2 %shard_map.126 = (bf16[2,256,256]{2,1,0:T(8,128)(2,1)S(1)}, f32[2,2,256,256]{3,2,1,0:T(8,128)S(1)}) custom-call(s32[1]{0:T(128)} %bitcast.row_ref, s32[1]{0:T(128)} %bitcast.1.col_ref, s32[2,8]{1,0:T(2,128)S(1)} %copy-done.12, s32[2,2]{1,0:T(2,128)S(1)} %copy-done.13, bf16[2,8,32,256]{3,2,1,0:T(8,128)(2,1)S(1)} %copy-done.1, ...), custom_call_target="tpu_custom_call" | custom-call | flops 335544320 | bytes 2228224 | tf_op jit(solution)/shard_map/pallas_call | solution.py:125
  61.2 0.1 collective-permute-done.16.refs_1_
  61.3 1.2 %shard_map.128 = bf16[2,256,256]{2,1,0:T(8,128)(2,1)S(1)} custom-call(s32[1]{0:T(128)} %bitcast.row_ref, s32[1]{0:T(128)} %bitcast.1.col_ref, s32[2,8]{1,0:T(2,128)S(1)} %copy-done.12, s32[2,2]{1,0:T(2,128)S(1)} %copy-done.13, bf16[2,8,32,256]{3,2,1,0:T(8,128)(2,1)S(1)} %copy-done.1, bf16[2,2,256,256]{3,2,1,0:T(8,128)(2,1)S(1)} %bitcast.9, ...), custom_call_target="tpu_custom_call" | custom-call | flops 67108864 | bytes 3276800 | tf_op jit(solution)/shard_map/pallas_call | solution.py:125
  62.5 0.1 collective-permute-start.17
  62.6 0.9 %shard_map.127.own = f32[2,256,256]{2,1,0:T(8,128)S(1)} custom-call(s32[1]{0:T(128)} %bitcast.row_ref, s32[1]{0:T(128)} %bitcast.1.col_ref, s32[2,8]{1,0:T(2,128)S(1)} %copy-done.12, s32[2,2]{1,0:T(2,128)S(1)} %copy-done.13, bf16[2,8,32,256]{3,2,1,0:T(8,128)(2,1)S(1)} %copy-done.1, bf16[2,2,256,256]{3,2,1,0:T(8,128)(2,1)S(1)} %bitcast.10, ...), custom_call_target="tpu_custom_call" | custom-call | flops 67108864 | bytes 3276800 | tf_op jit(solution)/shard_map/pallas_call | solution.py:125
  63.5 0.6 collective-permute-done.17.other
  64.1 2.2 %shard_map.129 = (f32[256,256]{1,0:T(8,128)}, f32[256,256]{1,0:T(8,128)}) custom-call(f32[2,256,256]{2,1,0:T(8,128)S(1)} %shard_map.127.own, bf16[2,256,256]{2,1,0:T(8,128)(2,1)S(1)} %collective-permute-done.17.other, f32[256,256]{1,0:T(8,128)S(1)} %copy-done.2, f32[256,256]{1,0:T(8,128)S(1)} %copy-done.3, f32[256,3]{1,0:T(8,128)S(1)} %copy.19.coef, ...), custom_call_target="tpu_custom_call" | custom-call | flops 13107200 | bytes 2097152 | tf_op jit(solution)/shard_map/pallas_call | solution.py:216
  (38 shorter events, 0.1 us)
Async XLA Ops:
  0.6 24.1 %copy-start = (bf16[2,2,2,256,256]{4,3,2,1,0:T(8,128)(2,1)S(1)}, bf16[2,2,2,256,256]{4,3,2,1,0:T(8,128)(2,1)}, u32[]{:S(2)}) copy-start(bf16[2,2,2,256,256]{4,3,2,1,0:T(8,128)(2,1)} %d_ref.11) | copy-start | bytes 3145732
  1.7 6.8 %collective-permute-start = (bf16[256,256]{1,0:T(8,128)(2,1)S(1)}, bf16[256,256]{1,0:T(8,128)(2,1)S(1)}, u32[]{:S(2)}, u32[]{:S(2)}) collective-permute-start(bf16[256,256]{1,0:T(8,128)(2,1)S(1)} %convert_element_type.3.refs_0_), channel_id=1, source_target_pairs={{0,4},{4,8},{8,12},{12,14},{14,10},{10,6},{6,2},{2,0},{5,1},{9,5},... | collective-permute-start | bytes 393224 | tf_op jit(solution)/shard_map/ppermute | solution.py:41
  4.8 5.3 %collective-permute-start.1 = (bf16[256,256]{1,0:T(8,128)(2,1)S(1)}, bf16[256,256]{1,0:T(8,128)(2,1)S(1)}, u32[]{:S(2)}, u32[]{:S(2)}) collective-permute-start(bf16[256,256]{1,0:T(8,128)(2,1)S(1)} %convert_element_type.3.refs_0_), channel_id=1, source_target_pairs={{4,0},{8,4},{12,8},{14,12},{10,14},{6,10},{2,6},{0,2},{1,5},{5,9},... | collective-permute-start | bytes 393224 | tf_op jit(solution)/shard_map/ppermute | solution.py:42
  8.5 14.0 %copy-start.4 = (bf16[256,256]{1,0:T(8,128)(2,1)}, bf16[256,256]{1,0:T(8,128)(2,1)S(1)}, u32[]{:S(2)}) copy-start(bf16[256,256]{1,0:T(8,128)(2,1)S(1)} %collective-permute-done.refs_1_) | copy-start | bytes 393220
  8.5 6.2 %collective-permute-start.2 = (bf16[256,256]{1,0:T(8,128)(2,1)S(1)}, bf16[256,256]{1,0:T(8,128)(2,1)S(1)}, u32[]{:S(2)}, u32[]{:S(2)}) collective-permute-start(bf16[256,256]{1,0:T(8,128)(2,1)S(1)} %collective-permute-done.refs_1_), channel_id=1, source_target_pairs={{0,4},{4,8},{8,12},{12,14},{14,10},{10,6},{6,2},{2,0},{5,1},{9,5},... | collective-permute-start | bytes 393224 | tf_op jit(solution)/shard_map/ppermute | solution.py:41
  10.1 12.5 %copy-start.6 = (bf16[256,256]{1,0:T(8,128)(2,1)}, bf16[256,256]{1,0:T(8,128)(2,1)S(1)}, u32[]{:S(2)}) copy-start(bf16[256,256]{1,0:T(8,128)(2,1)S(1)} %collective-permute-done.1.refs_2_) | copy-start | bytes 393220
  10.1 6.3 %collective-permute-start.3 = (bf16[256,256]{1,0:T(8,128)(2,1)S(1)}, bf16[256,256]{1,0:T(8,128)(2,1)S(1)}, u32[]{:S(2)}, u32[]{:S(2)}) collective-permute-start(bf16[256,256]{1,0:T(8,128)(2,1)S(1)} %collective-permute-done.1.refs_2_), channel_id=1, source_target_pairs={{4,0},{8,4},{12,8},{14,12},{10,14},{6,10},{2,6},{0,2},{1,5},{5,9},... | collective-permute-start | bytes 393224 | tf_op jit(solution)/shard_map/ppermute | solution.py:42
  14.7 5.0 %collective-permute-start.4 = (bf16[256,256]{1,0:T(8,128)(2,1)S(1)}, bf16[256,256]{1,0:T(8,128)(2,1)S(1)}, u32[]{:S(2)}, u32[]{:S(2)}) collective-permute-start(bf16[256,256]{1,0:T(8,128)(2,1)S(1)} %collective-permute-done.2.refs_3_), channel_id=1, source_target_pairs={{0,4},{4,8},{8,12},{12,14},{14,10},{10,6},{6,2},{2,0},{5,1},{9,5},... | collective-permute-start | bytes 393224 | tf_op jit(solution)/shard_map/ppermute | solution.py:41
  15.0 0.6 copy-start.8
  16.4 5.6 %collective-permute-start.5 = (bf16[256,256]{1,0:T(8,128)(2,1)S(1)}, bf16[256,256]{1,0:T(8,128)(2,1)S(1)}, u32[]{:S(2)}, u32[]{:S(2)}) collective-permute-start(bf16[256,256]{1,0:T(8,128)(2,1)S(1)} %collective-permute-done.3.refs_4_), channel_id=1, source_target_pairs={{4,0},{8,4},{12,8},{14,12},{10,14},{6,10},{2,6},{0,2},{1,5},{5,9},... | collective-permute-start | bytes 393224 | tf_op jit(solution)/shard_map/ppermute | solution.py:42
  17.4 0.6 copy-start.10
  20.3 11.8 %collective-permute-start.6 = (bf16[128,256]{1,0:T(8,128)(2,1)}, bf16[128,256]{1,0:T(8,128)(2,1)}, u32[]{:S(2)}, u32[]{:S(2)}) collective-permute-start(bf16[128,256]{1,0:T(8,128)(2,1)} %slice.16), channel_id=1, source_target_pairs={{0,4},{4,8},{8,12},{12,14},{14,10},{10,6},{6,2},{2,0},{5,1},{9,5},... | collective-permute-start | bytes 196616 | tf_op jit(solution)/shard_map/ppermute | solution.py:45
  22.6 9.6 %collective-permute-start.7 = (bf16[128,256]{1,0:T(8,128)(2,1)}, bf16[128,256]{1,0:T(8,128)(2,1)}, u32[]{:S(2)}, u32[]{:S(2)}) collective-permute-start(bf16[128,256]{1,0:T(8,128)(2,1)} %slice.17), channel_id=1, source_target_pairs={{4,0},{8,4},{12,8},{14,12},{10,14},{6,10},{2,6},{0,2},{1,5},{5,9},... | collective-permute-start | bytes 196616 | tf_op jit(solution)/shard_map/ppermute | solution.py:46
  23.4 1.3 %copy-start.1 = (bf16[2,8,32,256]{3,2,1,0:T(8,128)(2,1)S(1)}, bf16[2,8,32,256]{3,2,1,0:T(8,128)(2,1)}, u32[]{:S(2)}) copy-start(bf16[2,8,32,256]{3,2,1,0:T(8,128)(2,1)} %v_ref.11) | copy-start | bytes 786436
  23.4 1.3 %copy-start.13 = (s32[2,2]{1,0:T(2,128)S(1)}, s32[2,2]{1,0:T(2,128)}, u32[]{:S(2)}) copy-start(s32[2,2]{1,0:T(2,128)} %near_ref.11) | copy-start | bytes 52
  24.7 0.7 %copy-start.12 = (s32[2,8]{1,0:T(2,128)S(1)}, s32[2,8]{1,0:T(2,128)}, u32[]{:S(2)}) copy-start(s32[2,8]{1,0:T(2,128)} %rank_ref.11) | copy-start | bytes 196
  25.4 0.9 %copy-start.5 = (bf16[256,256]{1,0:T(8,128)(2,1)S(1)}, bf16[256,256]{1,0:T(8,128)(2,1)}, u32[]{:S(2)}) copy-start(bf16[256,256]{1,0:T(8,128)(2,1)} %copy-done.4) | copy-start | bytes 393220
  26.3 0.9 %copy-start.7 = (bf16[256,256]{1,0:T(8,128)(2,1)S(1)}, bf16[256,256]{1,0:T(8,128)(2,1)}, u32[]{:S(2)}) copy-start(bf16[256,256]{1,0:T(8,128)(2,1)} %copy-done.6) | copy-start | bytes 393220
  27.2 0.9 %copy-start.9 = (bf16[256,256]{1,0:T(8,128)(2,1)S(1)}, bf16[256,256]{1,0:T(8,128)(2,1)}, u32[]{:S(2)}) copy-start(bf16[256,256]{1,0:T(8,128)(2,1)} %copy-done.8) | copy-start | bytes 393220
  28.1 0.9 %copy-start.11 = (bf16[256,256]{1,0:T(8,128)(2,1)S(1)}, bf16[256,256]{1,0:T(8,128)(2,1)}, u32[]{:S(2)}) copy-start(bf16[256,256]{1,0:T(8,128)(2,1)} %copy-done.10) | copy-start | bytes 393220
  32.2 1.7 %copy-start.15 = (f32[256]{0:T(256)S(1)}, f32[256]{0:T(256)}, u32[]{:S(2)}) copy-start(f32[256]{0:T(256)} %param.15) | copy-start | bytes 3076
  32.2 1.7 %copy-start.16 = (f32[256]{0:T(256)S(1)}, f32[256]{0:T(256)}, u32[]{:S(2)}) copy-start(f32[256]{0:T(256)} %param.14) | copy-start | bytes 3076
  33.7 2.3 %collective-permute-start.8 = (bf16[2,256,256]{2,1,0:T(8,128)(2,1)S(1)}, bf16[2,256,256]{2,1,0:T(8,128)(2,1)}, u32[]{:S(2)}, u32[]{:S(2)}) collective-permute-start(bf16[2,256,256]{2,1,0:T(8,128)(2,1)S(1)} %shard_map.124), channel_id=1, source_target_pairs={{0,1},{1,0},{2,3},{3,2},{4,5},{5,4},{6,7},{7,6},{8,9},{9,8},{10,11... | collective-permute-start | bytes 786440 | tf_op jit(solution)/shard_map/ppermute | solution.py:287
  33.8 0.7 %copy-start.14 = (f32[256]{0:T(256)S(1)}, f32[256]{0:T(256)}, u32[]{:S(2)}) copy-start(f32[256]{0:T(256)} %param.16) | copy-start | bytes 3076
  34.7 1.4 %copy-start.2 = (f32[256,256]{1,0:T(8,128)S(1)}, f32[256,256]{1,0:T(8,128)}, u32[]{:S(2)}) copy-start(f32[256,256]{1,0:T(8,128)} %state.3) | copy-start | bytes 786436
  34.7 1.4 %copy-start.3 = (f32[256,256]{1,0:T(8,128)S(1)}, f32[256,256]{1,0:T(8,128)}, u32[]{:S(2)}) copy-start(f32[256,256]{1,0:T(8,128)} %tau.3) | copy-start | bytes 786436
  38.3 5.2 %collective-permute-start.9 = (bf16[256,256]{1,0:T(8,128)(2,1)S(1)}, bf16[256,256]{1,0:T(8,128)(2,1)S(1)}, u32[]{:S(2)}, u32[]{:S(2)}) collective-permute-start(bf16[256,256]{1,0:T(8,128)(2,1)S(1)} %get-tuple-element.13.refs_0_), channel_id=1, source_target_pairs={{0,4},{4,8},{8,12},{12,14},{14,10},{10,6},{6,2},{2,0},{5,1},{9,5},... | collective-permute-start | bytes 393224 | tf_op jit(solution)/shard_map/ppermute | solution.py:41
  39.3 5.7 %collective-permute-start.10 = (bf16[256,256]{1,0:T(8,128)(2,1)S(1)}, bf16[256,256]{1,0:T(8,128)(2,1)S(1)}, u32[]{:S(2)}, u32[]{:S(2)}) collective-permute-start(bf16[256,256]{1,0:T(8,128)(2,1)S(1)} %get-tuple-element.13.refs_0_), channel_id=1, source_target_pairs={{4,0},{8,4},{12,8},{14,12},{10,14},{6,10},{2,6},{0,2},{1,5},{5,9},... | collective-permute-start | bytes 393224 | tf_op jit(solution)/shard_map/ppermute | solution.py:42
  43.5 6.8 %collective-permute-start.11 = (bf16[256,256]{1,0:T(8,128)(2,1)S(1)}, bf16[256,256]{1,0:T(8,128)(2,1)S(1)}, u32[]{:S(2)}, u32[]{:S(2)}) collective-permute-start(bf16[256,256]{1,0:T(8,128)(2,1)S(1)} %collective-permute-done.9.refs_1_), channel_id=1, source_target_pairs={{0,4},{4,8},{8,12},{12,14},{14,10},{10,6},{6,2},{2,0},{5,1},{9,5},... | collective-permute-start | bytes 393224 | tf_op jit(solution)/shard_map/ppermute | solution.py:41
  45.1 6.3 %collective-permute-start.12 = (bf16[256,256]{1,0:T(8,128)(2,1)S(1)}, bf16[256,256]{1,0:T(8,128)(2,1)S(1)}, u32[]{:S(2)}, u32[]{:S(2)}) collective-permute-start(bf16[256,256]{1,0:T(8,128)(2,1)S(1)} %collective-permute-done.10.refs_2_), channel_id=1, source_target_pairs={{4,0},{8,4},{12,8},{14,12},{10,14},{6,10},{2,6},{0,2},{1,5},{5,9},... | collective-permute-start | bytes 393224 | tf_op jit(solution)/shard_map/ppermute | solution.py:42
  50.3 5.6 %collective-permute-start.13 = (bf16[256,256]{1,0:T(8,128)(2,1)S(1)}, bf16[256,256]{1,0:T(8,128)(2,1)S(1)}, u32[]{:S(2)}, u32[]{:S(2)}) collective-permute-start(bf16[256,256]{1,0:T(8,128)(2,1)S(1)} %collective-permute-done.11.refs_3_), channel_id=1, source_target_pairs={{0,4},{4,8},{8,12},{12,14},{14,10},{10,6},{6,2},{2,0},{5,1},{9,5},... | collective-permute-start | bytes 393224 | tf_op jit(solution)/shard_map/ppermute | solution.py:41
  51.4 5.6 %collective-permute-start.14 = (bf16[256,256]{1,0:T(8,128)(2,1)S(1)}, bf16[256,256]{1,0:T(8,128)(2,1)S(1)}, u32[]{:S(2)}, u32[]{:S(2)}) collective-permute-start(bf16[256,256]{1,0:T(8,128)(2,1)S(1)} %collective-permute-done.12.refs_4_), channel_id=1, source_target_pairs={{4,0},{8,4},{12,8},{14,12},{10,14},{6,10},{2,6},{0,2},{1,5},{5,9},... | collective-permute-start | bytes 393224 | tf_op jit(solution)/shard_map/ppermute | solution.py:42
  55.9 5.3 %collective-permute-start.15 = (bf16[128,256]{1,0:T(8,128)(2,1)S(1)}, bf16[128,256]{1,0:T(8,128)(2,1)S(1)}, u32[]{:S(2)}, u32[]{:S(2)}) collective-permute-start(bf16[128,256]{1,0:T(8,128)(2,1)S(1)} %slice.18), channel_id=1, source_target_pairs={{0,4},{4,8},{8,12},{12,14},{14,10},{10,6},{6,2},{2,0},{5,1},{9,5},... | collective-permute-start | bytes 196616 | tf_op jit(solution)/shard_map/ppermute | solution.py:45
  57.0 4.3 %collective-permute-start.16 = (bf16[128,256]{1,0:T(8,128)(2,1)S(1)}, bf16[128,256]{1,0:T(8,128)(2,1)S(1)}, u32[]{:S(2)}, u32[]{:S(2)}) collective-permute-start(bf16[128,256]{1,0:T(8,128)(2,1)S(1)} %slice.19), channel_id=1, source_target_pairs={{4,0},{8,4},{12,8},{14,12},{10,14},{6,10},{2,6},{0,2},{1,5},{5,9},... | collective-permute-start | bytes 196616 | tf_op jit(solution)/shard_map/ppermute | solution.py:46
  62.5 1.6 %collective-permute-start.17 = (bf16[2,256,256]{2,1,0:T(8,128)(2,1)S(1)}, bf16[2,256,256]{2,1,0:T(8,128)(2,1)S(1)}, u32[]{:S(2)}, u32[]{:S(2)}) collective-permute-start(bf16[2,256,256]{2,1,0:T(8,128)(2,1)S(1)} %shard_map.128), channel_id=1, source_target_pairs={{0,1},{1,0},{2,3},{3,2},{4,5},{5,4},{6,7},{7,6},{8,9},{9,8},{10,11... | collective-permute-start | bytes 786440 | tf_op jit(solution)/shard_map/ppermute | solution.py:287

commit v3 on v0

v3 whole, which is shorter than its diff:
```python
import functools

import jax
import jax.numpy as jnp
from jax import lax
from jax.experimental import pallas as pl
from jax.experimental.pallas import tpu as pltpu
from jax.sharding import PartitionSpec as P

NEWTON = 2
DIRECT_LIMIT = 16
LATE = 4

damping = 0.5
sigma_floor = 0.5
section_step = 0.1


def arrivals(count, direct):
    if not direct:
        return list(range(count))
    length = count // 2
    shifts = list(range(length - 1, 0, -1))
    early = [(0, 0), (0, 1)] + [(shift, 0) for shift in shifts[:-1]]
    late = [(shift, 0) for shift in shifts[-1:]] + [(shift, 1) for shift in shifts[-1:]]
    return early + late + [(shift, 1) for shift in shifts[:-1]]


def row_met(spot, row, count):
    if not isinstance(spot, tuple):
        return spot
    shift, other = spot
    z, y = row // 2, row % 2
    return lax.rem(z - shift + count // 2, count // 2) * 2 + (1 - y if other else y)


def gather_direct(block, count):
    length = count // 2

    def along(shift, other, data):
        hops = [
            (z * 2 + y, (z + shift) % length * 2 + (1 - y if other else y))
            for z in range(length)
            for y in range(2)
        ]
        return lax.ppermute(data, "row", hops)

    shifts = list(range(length - 1, 0, -1))
    far, last = {}, []
    across = along(0, 1, block)
    for shift in shifts[:-1]:
        far[shift] = along(shift, 0, block)
    if shifts:
        held = block
        if far:
            held, _ = lax.optimization_barrier((block, far[shifts[0]]))
        last = [along(shifts[-1], 0, held), along(shifts[-1], 1, held)]
    passed = [along(0, 1, far[shift]) for shift in shifts[:-1]]
    return [block, across, *far.values(), *last, *passed]


def narrow_kernel(wide_ref, narrow_ref):
    narrow_ref[...] = wide_ref[...].astype(narrow_ref.dtype)


def prepare_kernel(
    spots, row_ref, rank_ref, v_ref, u_ref, sigma_ref, a_ref, b_ref, state_ref, v_out, u_out, coef_out, weight_out, decay_out
):
    kinds, rows, count, rank_count, size = u_ref.shape
    row = row_ref[0]
    met = [row_met(spot, row, count) for spot in spots]
    for at, q in enumerate(met):
        for p in range(rows):
            inside = lax.broadcasted_iota(jnp.int32, (rank_count, size), 0) < rank_ref[p, q]
            v_out[at, p] = jnp.where(inside, v_ref[p, q].astype(jnp.float32), 0.0).astype(v_out.dtype)
    for p in range(rows):
        for kind in range(kinds):
            for first in range(0, count, 4):
                group = [u_ref[kind, p, q] for q in met[first : first + 4]]
                turned = jnp.concatenate(group, axis=0).astype(jnp.float32).T
                u_out[p, kind * size : (kind + 1) * size, first * rank_count : (first + len(group)) * rank_count] = (
                    turned.astype(u_out.dtype)
                )
    lanes = coef_out.shape[2]
    for at, ref in enumerate((sigma_ref, a_ref, b_ref)):
        coef_out[at] = jnp.broadcast_to(ref[...], (lanes, size)).T
    for first in range(0, state_ref.shape[1], lanes):
        part = slice(first, first + lanes)
        state = state_ref[:, part]
        weight_out[:, part] = jnp.exp(-state / coef_out[1])
        decay_out[:, part] = jnp.exp(-state / coef_out[2])


def sums_kernel(spots, first, pick, before, row_ref, col_ref, near_ref, v_ref, u_ref, d_ref, *refs):
    blocks = refs[: len(spots)]
    refs = refs[len(spots) :]
    if before:
        sums_ref, refs = refs[0], refs[1:]
    out_ref, x_all, proj, total = refs
    count, rows, rank_count, size = v_ref.shape
    kinds, slots = d_ref.shape[0], near_ref.shape[1]
    row, col = row_ref[0], col_ref[0]
    met = [row_met(spot, row, count) for spot in spots]
    chosen = list(range(rows)) if pick is None else [col if pick == 0 else 1 - col]
    for at, block in enumerate(blocks):
        x_all[at] = block[...]
    for at, block in enumerate(blocks):
        if pick is None:
            weights = v_ref[first + at].reshape(rows * rank_count, size)
        else:
            weights = v_ref[first + at, chosen[0]]
        part = jnp.dot(weights, block[...], preferred_element_type=jnp.float32).astype(proj.dtype)
        for place in range(len(chosen)):
            proj[place, at * rank_count : (at + 1) * rank_count, :] = part[
                place * rank_count : (place + 1) * rank_count
            ]
    lanes = slice(first * rank_count, (first + len(blocks)) * rank_count)
    for place, p in enumerate(chosen):
        gained = jnp.dot(u_ref[p, :, lanes], proj[place], preferred_element_type=jnp.float32)
        for kind in range(kinds):
            piece = gained[kind * size : (kind + 1) * size]
            total[place, kind] = sums_ref[p, kind] + piece if before else piece
    for place, p in enumerate(chosen):
        for s in range(slots):
            near = near_ref[p, s] - col * count
            at = sum(jnp.where(near == q, i, 0) for i, q in enumerate(met))
            hit = sum(jnp.where(near == q, 1, 0) for q in met)

            @pl.when(hit > 0)
            def _():
                block = x_all[at]
                for kind in range(kinds):
                    total[place, kind] += jnp.dot(
                        d_ref[kind, p, s], block, preferred_element_type=jnp.float32
                    )
    for place in range(len(chosen)):
        for kind in range(kinds):
            if pick is None:
                out_ref[place, kind] = total[place, kind]
            else:
                out_ref[kind] = total[place, kind].astype(out_ref.dtype)


def inverse_sinh(value):
    magnitude = jnp.abs(value)
    result = jnp.log(magnitude + jnp.sqrt(magnitude * magnitude + 1.0))
    return jnp.where(value < 0.0, -result, result)


def sinh_cosh(value):
    grown = jnp.exp(value)
    shrunk = jnp.exp(-value)
    square = value * value
    small = value * (
        1.0 + square * (1 / 6 + square * (1 / 120 + square * (1 / 5040 + square * (1 / 362880))))
    )
    sinh = jnp.where(square < 1.0, small, 0.5 * (grown - shrunk))
    return sinh, 0.5 * (grown + shrunk)


def friction(shear, normal, weight, decay, tau_load, sigma_base, a_wide, b_wide):
    tau = tau_load + shear
    sigma = jnp.maximum(sigma_base + normal, sigma_floor)
    stiff = sigma * a_wide
    first = tau / stiff
    second = inverse_sinh(tau / (2.0 * damping * weight))
    slope = jnp.where(jnp.abs(first) < jnp.abs(second), first, second)
    for newton_step in range(NEWTON):
        sinh, cosh = sinh_cosh(slope)
        excess = stiff * slope + 2.0 * damping * weight * sinh - tau
        deriv = stiff + 2.0 * damping * weight * cosh
        slope = slope - excess / deriv
    rate = 2.0 * weight * sinh_cosh(slope)[0]
    change = b_wide * (decay - jnp.abs(rate))
    return (rate, change)


def over_pieces(size, members, lanes, work):
    step = min(size, 16)

    @pl.loop(0, size // step)
    def _(index):
        rows = pl.ds(pl.multiple_of(index * step, step), step)
        for first in range(0, members, lanes):
            work(rows, slice(first, first + lanes))


def section_one_kernel(own, other, weight, decay, tau, coef, stress, normal, rate, change, rate_half):
    size, members = tau.shape

    def work(rows, part):
        shear = own[0, rows, part] + other[0, rows, part].astype(jnp.float32)
        press = own[1, rows, part] + other[1, rows, part].astype(jnp.float32)
        stress[rows, part] = shear
        normal[rows, part] = press
        first, second = friction(
            shear,
            press,
            weight[rows, part],
            decay[rows, part],
            tau[rows, part],
            coef[0, rows, :],
            coef[1, rows, :],
            coef[2, rows, :],
        )
        rate[rows, part] = first
        change[rows, part] = second
        rate_half[rows, part] = first.astype(rate_half.dtype)

    over_pieces(size, members, coef.shape[2], work)


def section_two_kernel(
    own, other, state, tau, coef, stress, normal, rate, change, mean_rate, mean_change
):
    size, members = tau.shape

    def work(rows, part):
        shear = own[0, rows, part] + other[0, rows, part].astype(jnp.float32)
        press = own[1, rows, part] + other[1, rows, part].astype(jnp.float32)
        sigma, a_wide, b_wide = coef[0, rows, :], coef[1, rows, :], coef[2, rows, :]
        later = state[rows, part] + section_step * change[rows, part]
        first, second = friction(
            stress[rows, part] + section_step * shear,
            normal[rows, part] + section_step * press,
            jnp.exp(-later / a_wide),
            jnp.exp(-later / b_wide),
            tau[rows, part],
            sigma,
            a_wide,
            b_wide,
        )
        mean_rate[rows, part] = (rate[rows, part] + first) * 0.5
        mean_change[rows, part] = (change[rows, part] + second) * 0.5

    over_pieces(size, members, coef.shape[2], work)


def on_core(kernel, outs, scalars, arrays, scratch=(), flops=0, room=16):
    smem, vmem = pl.BlockSpec(memory_space=pltpu.SMEM), pl.BlockSpec(memory_space=pltpu.VMEM)
    return pl.pallas_call(
        kernel,
        out_shape=outs,
        in_specs=[smem] * len(scalars) + [vmem] * len(arrays),
        out_specs=jax.tree.map(lambda _: vmem, outs),
        scratch_shapes=list(scratch),
        compiler_params=pltpu.CompilerParams(vmem_limit_bytes=room * 1024 * 1024),
        cost_estimate=pl.CostEstimate(
            flops=flops, bytes_accessed=sum(a.size * a.dtype.itemsize for a in arrays), transcendentals=0
        ),
    )(*scalars, *arrays)


def body(
    slip_deficit,
    state_var,
    tau_load,
    sigma_base,
    a_coef,
    b_coef,
    v_basis,
    u_basis,
    dense_blocks,
    block_ranks,
    near_index,
):
    count = lax.axis_size("row")
    size, members = slip_deficit.shape
    kinds, rows, _, rank_count, _ = u_basis.shape
    direct = count % 2 == 0 and count <= DIRECT_LIMIT
    spots = arrivals(count, direct)
    early = max(count - LATE, 0)
    room = 16 if direct else 40
    lanes = min(members, 128)
    narrow, wide = jnp.bfloat16, jnp.float32
    row, col = lax.axis_index("row").reshape(1), lax.axis_index("col").reshape(1)
    swap = [(0, 1), (1, 0)]

    def shaped(*shape, kind=wide):
        return jax.ShapeDtypeStruct(shape, kind)

    full = shaped(size, members)
    v_met, u_met, coef, weight, decay = on_core(
        functools.partial(prepare_kernel, spots),
        (
            shaped(count, rows, rank_count, size, kind=narrow),
            shaped(rows, kinds * size, count * rank_count, kind=narrow),
            shaped(3, size, lanes),
            full,
            full,
        ),
        (row, block_ranks),
        (
            v_basis,
            u_basis,
            sigma_base.reshape(1, size),
            a_coef.reshape(1, size),
            b_coef.reshape(1, size),
            state_var,
        ),
        room=room,
    )

    def add(blocks, first, pick, before, kind):
        held = rows if pick is None else 1
        lead = (rows, kinds) if pick is None else (kinds,)
        return on_core(
            functools.partial(
                sums_kernel, spots[first : first + len(blocks)], first, pick, before is not None
            ),
            shaped(*lead, size, members, kind=kind),
            (row, col, near_index),
            (v_met, u_met, dense_blocks, *blocks, *(() if before is None else (before,))),
            (
                pltpu.VMEM((len(blocks), size, members), narrow),
                pltpu.VMEM((held, len(blocks) * rank_count, members), narrow),
                pltpu.VMEM((held, kinds, size, members), wide),
            ),
            2 * held * size * members * rank_count * len(blocks) * 3,
            room,
        )

    def lattice(field_half):
        if direct:
            blocks = gather_direct(field_half, count)
        else:
            whole = lax.all_gather(field_half, "row", axis=0)
            blocks = [whole[r] for r in range(count)]
        sums = add(blocks[:early], 0, None, None, wide) if early else None
        other = lax.ppermute(add(blocks[early:], early, 1, sums, narrow), "col", swap)
        return add(blocks[early:], early, 0, sums, wide), other

    slip_half = on_core(narrow_kernel, shaped(size, members, kind=narrow), (), (slip_deficit,))
    own, other = lattice(slip_half)
    stress, normal, rate, change, rate_half = on_core(
        section_one_kernel,
        (full, full, full, full, shaped(size, members, kind=narrow)),
        (),
        (own, other, weight, decay, tau_load, coef),
        flops=200 * size * members,
    )
    own, other = lattice(rate_half)
    return on_core(
        section_two_kernel,
        (full, full),
        (),
        (own, other, state_var, tau_load, coef, stress, normal, rate, change),
        flops=200 * size * members,
    )


def solution(mesh):
    placed = (
        P(("row", "col"), "scen"),
        P(("row", "col"), "scen"),
        P(("row", "col"), "scen"),
        P(("row", "col")),
        P(("row", "col")),
        P(("row", "col")),
        P("row", "col", None, None),
        P(None, "row", "col", None, None),
        P(None, "row", "col", None, None),
        P("row", "col"),
        P("row", "col"),
    )
    return jax.shard_map(
        body,
        mesh=mesh,
        in_specs=placed,
        out_specs=(P(("row", "col"), "scen"), P(("row", "col"), "scen")),
        check_vma=False,
    )
```

time: 151 us -> 62.5 us (0.41)
  waiting for transfers between devices: 107 us -> 23.2 us
  starting transfers between devices: 0.16 us -> 18.5 us
  Pallas kernels: 0 us -> 13.2 us
  between operations: 13.9 us -> 0.82 us
  matrix products: 8.03 us -> 0 us
  other arithmetic: 7.58 us -> 0 us
  local copies, waits for them, and re-layouts: 12.9 us -> 6.43 us
    all_gather x2 -> x0, waiting for transfers between devices: 83.9 us -> none  [lattice(): whole = lax.all_gather(field_half, 'row', axis=0, tiled=True)]
    ppermute x0 -> x16, waiting for transfers between devices: none -> 23.2 us  [the longest x14 22.6 us: along(): return lax.ppermute(data, 'row', hops)]
    ppermute x0 -> x16, starting transfers between devices: none -> 18.5 us  [the longest x14 18.3 us: along(): return lax.ppermute(data, 'row', hops)]
    unnamed x5 -> x0, waiting for transfers between devices: 17.4 us -> none
    pallas_call x0 -> x10, Pallas kernels: none -> 13.2 us  [on_core(): pl.pallas_call(kernel, out_shape=outs, in_specs=[smem] * len(scalars) + [...]
    dot_general x4 -> x0, matrix products: 8.03 us -> none  [the longest x2 5.98 us: far_field(): jnp.einsum('cpqkb,pqke->cpbe', u_part, projected, preferred_element_type=...]
    reduce_scatter x1 -> x0, waiting for transfers between devices: 6.23 us -> none  [lattice(): lax.psum_scatter(partial_value, 'col', scatter_dimension=1, tiled=True)]
    convert_element_type x2 -> x0, other arithmetic: 4.48 us -> none  [the longest x1 2.79 us: body(): rate_half = rate_one.astype(jnp.bfloat16)]
  transfers between devices with their start and end apart: 4 -> 16, of which waited for: 4 -> 9; matrix products, arithmetic and copies ran while one was open for 1% -> 0% of each run, Pallas kernels for 0% -> 11%
where the time goes in v3:
time: 62.5 us; the launch traced here: 62.1 us
  waiting for transfers between devices  23.2 us (37%)
  starting transfers between devices  18.5 us (30%)
  Pallas kernels  13.2 us (21%)
  local copies, waits for them, and re-layouts  6.43 us (10%)
  between operations  0.82 us (1%)
    ppermute x14, waiting for transfers between devices, along(): return lax.ppermute(data, 'row', hops)  22.6 us
    ppermute x14, starting transfers between devices, along(): return lax.ppermute(data, 'row', hops)  18.3 us
    pallas_call x10, Pallas kernels, on_core(): pl.pallas_call(kernel, out_shape=outs, in_specs=[smem] * len(scalars) + [...  13.2 us
    unnamed x22, local copies, waits for them, and re-layouts  6.43 us
  transfers between devices with their start and end apart: 16, of which 9 were waited for; matrix products, arithmetic and copies ran while one was open for 0% of the time, Pallas kernels for 11%

profile of v3, /device:TPU:0, one launch (start us, length us, event | category | flops | bytes accessed | tf_op | source)
XLA Modules:
  0.0 62.1 jit_solution(16572395375125323830)
XLA Ops:
  0.7 1.0 %copy-done.4 = f32[256,256]{1,0:T(8,128)S(1)} copy-done((f32[256,256]{1,0:T(8,128)S(1)}, f32[256,256]{1,0:T(8,128)}, u32[]{:S(2)}) %copy-start.4) | copy-done | bytes 262168
  1.7 5.1 %collective-permute-start = (bf16[256,256]{1,0:T(8,128)(2,1)S(1)}, bf16[256,256]{1,0:T(8,128)(2,1)S(1)}, u32[]{:S(2)}, u32[]{:S(2)}) collective-permute-start(bf16[256,256]{1,0:T(8,128)(2,1)S(1)} %shard_map.123.refs_0_), channel_id=1, source_target_pairs={{0,12},{2,14},{4,0},{6,2},{8,4},{10,6},{12,8},{14,10},{1,13},{3,15... | collective-permute-start | bytes 393224 | tf_op jit(solution)/shard_map/ppermute | solution.py:46
  6.8 0.0 collective-permute-start.4
  6.8 1.5 %collective-permute-start.6 = (bf16[256,256]{1,0:T(8,128)(2,1)S(1)}, bf16[256,256]{1,0:T(8,128)(2,1)S(1)}, u32[]{:S(2)}, u32[]{:S(2)}) collective-permute-start(bf16[256,256]{1,0:T(8,128)(2,1)S(1)} %shard_map.123.refs_0_), channel_id=1, source_target_pairs={{0,2},{2,0},{4,6},{6,4},{8,10},{10,8},{12,14},{14,12},{1,3},{3,1},... | collective-permute-start | bytes 393224 | tf_op jit(solution)/shard_map/ppermute | solution.py:46
  8.3 2.4 %collective-permute-done.refs_2_ = bf16[256,256]{1,0:T(8,128)(2,1)S(1)} collective-permute-done((bf16[256,256]{1,0:T(8,128)(2,1)S(1)}, bf16[256,256]{1,0:T(8,128)(2,1)S(1)}, u32[]{:S(2)}, u32[]{:S(2)}) %collective-permute-start) | collective-permute-done | bytes 131104 | tf_op jit(solution)/shard_map/ppermute | solution.py:46
  10.7 4.5 %collective-permute-done.4.refs_3_ = bf16[256,256]{1,0:T(8,128)(2,1)S(1)} collective-permute-done((bf16[256,256]{1,0:T(8,128)(2,1)S(1)}, bf16[256,256]{1,0:T(8,128)(2,1)S(1)}, u32[]{:S(2)}, u32[]{:S(2)}) %collective-permute-start.4) | collective-permute-done | bytes 131104 | tf_op jit(solution)/shard_map/ppermute | solution.py:46
  15.2 1.5 %collective-permute-start.5 = (bf16[256,256]{1,0:T(8,128)(2,1)S(1)}, bf16[256,256]{1,0:T(8,128)(2,1)S(1)}, u32[]{:S(2)}, u32[]{:S(2)}) collective-permute-start(bf16[256,256]{1,0:T(8,128)(2,1)S(1)} %collective-permute-done.4.refs_3_), channel_id=1, source_target_pairs={{0,2},{2,0},{4,6},{6,4},{8,10},{10,8},{12,14},{14,12},{1,3},{3,1},... | collective-permute-start | bytes 393224 | tf_op jit(solution)/shard_map/ppermute | solution.py:46
  16.7 0.7 %collective-permute-start.2 = (bf16[256,256]{1,0:T(8,128)(2,1)S(1)}, bf16[256,256]{1,0:T(8,128)(2,1)S(1)}, u32[]{:S(2)}, u32[]{:S(2)}) collective-permute-start(bf16[256,256]{1,0:T(8,128)(2,1)S(1)} %shard_map.123.refs_0_), channel_id=1, source_target_pairs={{0,6},{2,4},{4,10},{6,8},{8,14},{10,12},{12,2},{14,0},{1,7},{3,5},... | collective-permute-start | bytes 393224 | tf_op jit(solution)/shard_map/ppermute | solution.py:46
  17.4 0.5 collective-permute-start.1
  17.9 1.5 %collective-permute-start.3 = (bf16[256,256]{1,0:T(8,128)(2,1)S(1)}, bf16[256,256]{1,0:T(8,128)(2,1)S(1)}, u32[]{:S(2)}, u32[]{:S(2)}) collective-permute-start(bf16[256,256]{1,0:T(8,128)(2,1)S(1)} %collective-permute-done.refs_2_), channel_id=1, source_target_pairs={{0,2},{2,0},{4,6},{6,4},{8,10},{10,8},{12,14},{14,12},{1,3},{3,1},... | collective-permute-start | bytes 393224 | tf_op jit(solution)/shard_map/ppermute | solution.py:46
  19.4 1.0 %copy-done.3 = bf16[2,2,8,32,256]{4,3,2,1,0:T(8,128)(2,1)S(1)} copy-done((bf16[2,2,8,32,256]{4,3,2,1,0:T(8,128)(2,1)S(1)}, bf16[2,2,8,32,256]{4,3,2,1,0:T(8,128)(2,1)}, u32[]{:S(2)}) %copy-start.3) | copy-done | bytes 524312
  20.5 0.9 %copy-done.5 = bf16[2,8,32,256]{3,2,1,0:T(8,128)(2,1)S(1)} copy-done((bf16[2,8,32,256]{3,2,1,0:T(8,128)(2,1)S(1)}, bf16[2,8,32,256]{3,2,1,0:T(8,128)(2,1)}, u32[]{:S(2)}) %copy-start.5) | copy-done | bytes 262168
  21.4 0.7 %copy-done.7 = s32[2,8]{1,0:T(2,128)S(1)} copy-done((s32[2,8]{1,0:T(2,128)S(1)}, s32[2,8]{1,0:T(2,128)}, u32[]{:S(2)}) %copy-start.7) | copy-done | bytes 88
  22.1 0.7 %copy-done.8 = f32[256]{0:T(256)S(1)} copy-done((f32[256]{0:T(256)S(1)}, f32[256]{0:T(256)}, u32[]{:S(2)}) %copy-start.8) | copy-done | bytes 1048
  22.8 0.7 %copy-done.9 = f32[256]{0:T(256)S(1)} copy-done((f32[256]{0:T(256)S(1)}, f32[256]{0:T(256)}, u32[]{:S(2)}) %copy-start.9) | copy-done | bytes 1048
  23.4 0.7 %copy-done.10 = f32[256]{0:T(256)S(1)} copy-done((f32[256]{0:T(256)S(1)}, f32[256]{0:T(256)}, u32[]{:S(2)}) %copy-start.10) | copy-done | bytes 1048
  24.1 1.0 %shard_map.122 = (bf16[8,2,32,256]{3,2,1,0:T(8,128)(2,1)S(1)}, bf16[2,512,256]{2,1,0:T(8,128)(2,1)S(1)}, f32[3,256,128]{2,1,0:T(8,128)S(1)}, f32[256,256]{1,0:T(8,128)S(1)}, f32[256,256]{1,0:T(8,128)S(1)}) custom-call(s32[1]{0:T(128)} %bitcast.row_ref, s32[2,8]{1,0:T(2,128)S(1)} %copy-done.7, bf16[2,8,32,256]{3,2,1,0:T(8,128)(2,1)S(1)} %copy-done.5, ...), custom_call_target="tpu_custom_call" | custom-call | bytes 1051648 | tf_op jit(solution)/shard_map/pallas_call | solution.py:241
  25.1 0.0 copy-start.6
  25.1 0.7 %copy-done.6 = s32[2,2]{1,0:T(2,128)S(1)} copy-done((s32[2,2]{1,0:T(2,128)S(1)}, s32[2,2]{1,0:T(2,128)}, u32[]{:S(2)}) %copy-start.6) | copy-done | bytes 40
  25.8 1.8 %shard_map.124.refs_4_ = f32[2,2,256,256]{3,2,1,0:T(8,128)S(1)} custom-call(s32[1]{0:T(128)} %bitcast.row_ref, s32[1]{0:T(128)} %bitcast.1.col_ref, s32[2,2]{1,0:T(2,128)S(1)} %copy-done.6, bf16[8,2,32,256]{3,2,1,0:T(8,128)(2,1)S(1)} %get-tuple-element.14.v_ref, bf16[2,512,256]{2,1,0:T(8,128)(2,1)S(1)} %get-tuple-element.15.u_ref, ...), custom_call_target="tpu_custom_call" | custom-call | flops 100663296 | bytes 2359296 | tf_op jit(solution)/shard_map/pallas_call | solution.py:241
  27.6 0.0 collective-permute-done.2.refs_1_
  27.6 0.0 collective-permute-done.1.refs_0_
  27.6 1.0 %shard_map.126 = bf16[2,256,256]{2,1,0:T(8,128)(2,1)S(1)} custom-call(s32[1]{0:T(128)} %bitcast.row_ref, s32[1]{0:T(128)} %bitcast.1.col_ref, s32[2,2]{1,0:T(2,128)S(1)} %copy-done.6, bf16[8,2,32,256]{3,2,1,0:T(8,128)(2,1)S(1)} %get-tuple-element.14.v_ref, bf16[2,512,256]{2,1,0:T(8,128)(2,1)S(1)} %get-tuple-element.15.u_ref, ...), custom_call_target="tpu_custom_call" | custom-call | flops 50331648 | bytes 3407872 | tf_op jit(solution)/shard_map/pallas_call | solution.py:241
  28.6 0.0 copy-start.1
  28.6 0.1 collective-permute-start.7
  28.7 1.2 %shard_map.125.own = f32[2,256,256]{2,1,0:T(8,128)S(1)} custom-call(s32[1]{0:T(128)} %bitcast.row_ref, s32[1]{0:T(128)} %bitcast.1.col_ref, s32[2,2]{1,0:T(2,128)S(1)} %copy-done.6, bf16[8,2,32,256]{3,2,1,0:T(8,128)(2,1)S(1)} %get-tuple-element.14.v_ref, bf16[2,512,256]{2,1,0:T(8,128)(2,1)S(1)} %get-tuple-element.15.u_ref, ...), custom_call_target="tpu_custom_call" | custom-call | flops 50331648 | bytes 3407872 | tf_op jit(solution)/shard_map/pallas_call | solution.py:241
  30.0 0.3 collective-permute-done.7.other
  30.3 1.5 %shard_map.127 = (f32[256,256]{1,0:T(8,128)S(1)}, f32[256,256]{1,0:T(8,128)S(1)}, f32[256,256]{1,0:T(8,128)S(1)}, f32[256,256]{1,0:T(8,128)S(1)}, bf16[256,256]{1,0:T(8,128)(2,1)S(1)}) custom-call(f32[2,256,256]{2,1,0:T(8,128)S(1)} %shard_map.125.own, bf16[2,256,256]{2,1,0:T(8,128)(2,1)S(1)} %collective-permute-done.7.other, ...), custom_call_target="tpu_custom_call" | custom-call | flops 13107200 | bytes 1966080 | tf_op jit(solution)/shard_map/pallas_call | solution.py:241
  31.8 3.6 %collective-permute-start.8 = (bf16[256,256]{1,0:T(8,128)(2,1)S(1)}, bf16[256,256]{1,0:T(8,128)(2,1)S(1)}, u32[]{:S(2)}, u32[]{:S(2)}) collective-permute-start(bf16[256,256]{1,0:T(8,128)(2,1)S(1)} %get-tuple-element.21.refs_0_), channel_id=1, source_target_pairs={{0,12},{2,14},{4,0},{6,2},{8,4},{10,6},{12,8},{14,10},{1,13},{3,15... | collective-permute-start | bytes 393224 | tf_op jit(solution)/shard_map/ppermute | solution.py:46
  35.4 1.6 %collective-permute-start.12 = (bf16[256,256]{1,0:T(8,128)(2,1)S(1)}, bf16[256,256]{1,0:T(8,128)(2,1)S(1)}, u32[]{:S(2)}, u32[]{:S(2)}) collective-permute-start(bf16[256,256]{1,0:T(8,128)(2,1)S(1)} %get-tuple-element.21.refs_0_), channel_id=1, source_target_pairs={{0,8},{2,10},{4,12},{6,14},{8,0},{10,2},{12,4},{14,6},{1,9},{3,11}... | collective-permute-start | bytes 393224 | tf_op jit(solution)/shard_map/ppermute | solution.py:46
  37.0 0.3 collective-permute-start.14
  37.2 2.1 %collective-permute-done.8.refs_2_ = bf16[256,256]{1,0:T(8,128)(2,1)S(1)} collective-permute-done((bf16[256,256]{1,0:T(8,128)(2,1)S(1)}, bf16[256,256]{1,0:T(8,128)(2,1)S(1)}, u32[]{:S(2)}, u32[]{:S(2)}) %collective-permute-start.8) | collective-permute-done | bytes 131104 | tf_op jit(solution)/shard_map/ppermute | solution.py:46
  39.4 6.8 %collective-permute-done.12.refs_3_ = bf16[256,256]{1,0:T(8,128)(2,1)S(1)} collective-permute-done((bf16[256,256]{1,0:T(8,128)(2,1)S(1)}, bf16[256,256]{1,0:T(8,128)(2,1)S(1)}, u32[]{:S(2)}, u32[]{:S(2)}) %collective-permute-start.12) | collective-permute-done | bytes 131104 | tf_op jit(solution)/shard_map/ppermute | solution.py:46
  46.2 0.3 collective-permute-start.13
  46.5 0.6 collective-permute-start.10
  47.1 0.7 %collective-permute-start.9 = (bf16[256,256]{1,0:T(8,128)(2,1)S(1)}, bf16[256,256]{1,0:T(8,128)(2,1)S(1)}, u32[]{:S(2)}, u32[]{:S(2)}) collective-permute-start(bf16[256,256]{1,0:T(8,128)(2,1)S(1)} %get-tuple-element.21.refs_0_), channel_id=1, source_target_pairs={{0,4},{2,6},{4,8},{6,10},{8,12},{10,14},{12,0},{14,2},{1,5},{3,7},... | collective-permute-start | bytes 393224 | tf_op jit(solution)/shard_map/ppermute | solution.py:46
  47.7 0.5 collective-permute-start.11
  48.2 0.0 collective-permute-done.14.refs_1_
  48.2 1.8 %shard_map.128.refs_4_ = f32[2,2,256,256]{3,2,1,0:T(8,128)S(1)} custom-call(s32[1]{0:T(128)} %bitcast.row_ref, s32[1]{0:T(128)} %bitcast.1.col_ref, s32[2,2]{1,0:T(2,128)S(1)} %copy-done.6, bf16[8,2,32,256]{3,2,1,0:T(8,128)(2,1)S(1)} %get-tuple-element.14.v_ref, bf16[2,512,256]{2,1,0:T(8,128)(2,1)S(1)} %get-tuple-element.15.u_ref, ...), custom_call_target="tpu_custom_call" | custom-call | flops 100663296 | bytes 2359296 | tf_op jit(solution)/shard_map/pallas_call | solution.py:241
  50.0 5.1 %collective-permute-done.13.refs_3_ = bf16[256,256]{1,0:T(8,128)(2,1)S(1)} collective-permute-done((bf16[256,256]{1,0:T(8,128)(2,1)S(1)}, bf16[256,256]{1,0:T(8,128)(2,1)S(1)}, u32[]{:S(2)}, u32[]{:S(2)}) %collective-permute-start.13) | collective-permute-done | bytes 131104 | tf_op jit(solution)/shard_map/ppermute | solution.py:46
  55.1 0.1 collective-permute-done.10.refs_1_
  55.2 1.6 %collective-permute-done.9.refs_0_ = bf16[256,256]{1,0:T(8,128)(2,1)S(1)} collective-permute-done((bf16[256,256]{1,0:T(8,128)(2,1)S(1)}, bf16[256,256]{1,0:T(8,128)(2,1)S(1)}, u32[]{:S(2)}, u32[]{:S(2)}) %collective-permute-start.9) | collective-permute-done | bytes 131104 | tf_op jit(solution)/shard_map/ppermute | solution.py:46
  56.8 0.0 collective-permute-done.11.refs_2_
  56.8 1.0 %shard_map.130 = bf16[2,256,256]{2,1,0:T(8,128)(2,1)S(1)} custom-call(s32[1]{0:T(128)} %bitcast.row_ref, s32[1]{0:T(128)} %bitcast.1.col_ref, s32[2,2]{1,0:T(2,128)S(1)} %copy-done.6, bf16[8,2,32,256]{3,2,1,0:T(8,128)(2,1)S(1)} %get-tuple-element.14.v_ref, bf16[2,512,256]{2,1,0:T(8,128)(2,1)S(1)} %get-tuple-element.15.u_ref, ...), custom_call_target="tpu_custom_call" | custom-call | flops 50331648 | bytes 3407872 | tf_op jit(solution)/shard_map/pallas_call | solution.py:241
  57.8 0.1 collective-permute-start.15
  57.9 1.2 %shard_map.129.own = f32[2,256,256]{2,1,0:T(8,128)S(1)} custom-call(s32[1]{0:T(128)} %bitcast.row_ref, s32[1]{0:T(128)} %bitcast.1.col_ref, s32[2,2]{1,0:T(2,128)S(1)} %copy-done.6, bf16[8,2,32,256]{3,2,1,0:T(8,128)(2,1)S(1)} %get-tuple-element.14.v_ref, bf16[2,512,256]{2,1,0:T(8,128)(2,1)S(1)} %get-tuple-element.15.u_ref, ...), custom_call_target="tpu_custom_call" | custom-call | flops 50331648 | bytes 3407872 | tf_op jit(solution)/shard_map/pallas_call | solution.py:241
  59.2 0.3 collective-permute-done.15.other
  59.4 2.7 %shard_map.131 = (f32[256,256]{1,0:T(8,128)}, f32[256,256]{1,0:T(8,128)}) custom-call(f32[2,256,256]{2,1,0:T(8,128)S(1)} %shard_map.129.own, bf16[2,256,256]{2,1,0:T(8,128)(2,1)S(1)} %collective-permute-done.15.other, f32[256,256]{1,0:T(8,128)S(1)} %copy-done.2, f32[256,256]{1,0:T(8,128)S(1)} %copy-done.1, f32[3,256,128]{2,1,0:T(8,128)S(1)} %get-tuple-element.19.coef, ...), custom_call_target="tpu_custom_call" | custom-call | flops 13107200 | bytes 2752512 | tf_op jit(solution)/shard_map/pallas_call | solution.py:241
  (16 shorter events, 0.0 us)
Async XLA Ops:
  0.6 18.8 %copy-start.2 = (f32[256,256]{1,0:T(8,128)S(1)}, f32[256,256]{1,0:T(8,128)}, u32[]{:S(2)}) copy-start(f32[256,256]{1,0:T(8,128)} %state.1) | copy-start | bytes 786436
  0.6 24.5 %copy-start = (bf16[2,2,2,256,256]{4,3,2,1,0:T(8,128)(2,1)S(1)}, bf16[2,2,2,256,256]{4,3,2,1,0:T(8,128)(2,1)}, u32[]{:S(2)}) copy-start(bf16[2,2,2,256,256]{4,3,2,1,0:T(8,128)(2,1)} %d_ref.11) | copy-start | bytes 3145732
  0.6 1.1 %copy-start.4 = (f32[256,256]{1,0:T(8,128)S(1)}, f32[256,256]{1,0:T(8,128)}, u32[]{:S(2)}) copy-start(f32[256,256]{1,0:T(8,128)} %wide_ref.1) | copy-start | bytes 786436
  1.7 9.0 %collective-permute-start = (bf16[256,256]{1,0:T(8,128)(2,1)S(1)}, bf16[256,256]{1,0:T(8,128)(2,1)S(1)}, u32[]{:S(2)}, u32[]{:S(2)}) collective-permute-start(bf16[256,256]{1,0:T(8,128)(2,1)S(1)} %shard_map.123.refs_0_), channel_id=1, source_target_pairs={{0,12},{2,14},{4,0},{6,2},{8,4},{10,6},{12,8},{14,10},{1,13},{3,15... | collective-permute-start | bytes 393224 | tf_op jit(solution)/shard_map/ppermute | solution.py:46
  6.8 8.4 %collective-permute-start.4 = (bf16[256,256]{1,0:T(8,128)(2,1)S(1)}, bf16[256,256]{1,0:T(8,128)(2,1)S(1)}, u32[]{:S(2)}, u32[]{:S(2)}) collective-permute-start(bf16[256,256]{1,0:T(8,128)(2,1)S(1)} %shard_map.123.refs_0_), channel_id=1, source_target_pairs={{0,8},{2,10},{4,12},{6,14},{8,0},{10,2},{12,4},{14,6},{1,9},{3,11}... | collective-permute-start | bytes 393224 | tf_op jit(solution)/shard_map/ppermute | solution.py:46
  6.8 18.3 %collective-permute-start.6 = (bf16[256,256]{1,0:T(8,128)(2,1)S(1)}, bf16[256,256]{1,0:T(8,128)(2,1)S(1)}, u32[]{:S(2)}, u32[]{:S(2)}) collective-permute-start(bf16[256,256]{1,0:T(8,128)(2,1)S(1)} %shard_map.123.refs_0_), channel_id=1, source_target_pairs={{0,2},{2,0},{4,6},{6,4},{8,10},{10,8},{12,14},{14,12},{1,3},{3,1},... | collective-permute-start | bytes 393224 | tf_op jit(solution)/shard_map/ppermute | solution.py:46
  15.2 12.4 %collective-permute-start.5 = (bf16[256,256]{1,0:T(8,128)(2,1)S(1)}, bf16[256,256]{1,0:T(8,128)(2,1)S(1)}, u32[]{:S(2)}, u32[]{:S(2)}) collective-permute-start(bf16[256,256]{1,0:T(8,128)(2,1)S(1)} %collective-permute-done.4.refs_3_), channel_id=1, source_target_pairs={{0,2},{2,0},{4,6},{6,4},{8,10},{10,8},{12,14},{14,12},{1,3},{3,1},... | collective-permute-start | bytes 393224 | tf_op jit(solution)/shard_map/ppermute | solution.py:46
  16.7 10.9 %collective-permute-start.2 = (bf16[256,256]{1,0:T(8,128)(2,1)S(1)}, bf16[256,256]{1,0:T(8,128)(2,1)S(1)}, u32[]{:S(2)}, u32[]{:S(2)}) collective-permute-start(bf16[256,256]{1,0:T(8,128)(2,1)S(1)} %shard_map.123.refs_0_), channel_id=1, source_target_pairs={{0,6},{2,4},{4,10},{6,8},{8,14},{10,12},{12,2},{14,0},{1,7},{3,5},... | collective-permute-start | bytes 393224 | tf_op jit(solution)/shard_map/ppermute | solution.py:46
  17.4 10.2 %collective-permute-start.1 = (bf16[256,256]{1,0:T(8,128)(2,1)S(1)}, bf16[256,256]{1,0:T(8,128)(2,1)S(1)}, u32[]{:S(2)}, u32[]{:S(2)}) collective-permute-start(bf16[256,256]{1,0:T(8,128)(2,1)S(1)} %shard_map.123.refs_0_), channel_id=1, source_target_pairs={{0,4},{2,6},{4,8},{6,10},{8,12},{10,14},{12,0},{14,2},{1,5},{3,7},... | collective-permute-start | bytes 393224 | tf_op jit(solution)/shard_map/ppermute | solution.py:46
  17.9 9.7 %collective-permute-start.3 = (bf16[256,256]{1,0:T(8,128)(2,1)S(1)}, bf16[256,256]{1,0:T(8,128)(2,1)S(1)}, u32[]{:S(2)}, u32[]{:S(2)}) collective-permute-start(bf16[256,256]{1,0:T(8,128)(2,1)S(1)} %collective-permute-done.refs_2_), channel_id=1, source_target_pairs={{0,2},{2,0},{4,6},{6,4},{8,10},{10,8},{12,14},{14,12},{1,3},{3,1},... | collective-permute-start | bytes 393224 | tf_op jit(solution)/shard_map/ppermute | solution.py:46
  19.4 1.0 %copy-start.3 = (bf16[2,2,8,32,256]{4,3,2,1,0:T(8,128)(2,1)S(1)}, bf16[2,2,8,32,256]{4,3,2,1,0:T(8,128)(2,1)}, u32[]{:S(2)}) copy-start(bf16[2,2,8,32,256]{4,3,2,1,0:T(8,128)(2,1)} %u_ref.1) | copy-start | bytes 1572868
  20.5 0.9 %copy-start.5 = (bf16[2,8,32,256]{3,2,1,0:T(8,128)(2,1)S(1)}, bf16[2,8,32,256]{3,2,1,0:T(8,128)(2,1)}, u32[]{:S(2)}) copy-start(bf16[2,8,32,256]{3,2,1,0:T(8,128)(2,1)} %v_ref.1) | copy-start | bytes 786436
  21.4 0.7 %copy-start.7 = (s32[2,8]{1,0:T(2,128)S(1)}, s32[2,8]{1,0:T(2,128)}, u32[]{:S(2)}) copy-start(s32[2,8]{1,0:T(2,128)} %rank_ref.1) | copy-start | bytes 196
  22.1 0.7 %copy-start.8 = (f32[256]{0:T(256)S(1)}, f32[256]{0:T(256)}, u32[]{:S(2)}) copy-start(f32[256]{0:T(256)} %param.14) | copy-start | bytes 3076
  22.8 0.7 %copy-start.9 = (f32[256]{0:T(256)S(1)}, f32[256]{0:T(256)}, u32[]{:S(2)}) copy-start(f32[256]{0:T(256)} %param.15) | copy-start | bytes 3076
  23.4 0.7 %copy-start.10 = (f32[256]{0:T(256)S(1)}, f32[256]{0:T(256)}, u32[]{:S(2)}) copy-start(f32[256]{0:T(256)} %param.16) | copy-start | bytes 3076
  25.1 0.7 %copy-start.6 = (s32[2,2]{1,0:T(2,128)S(1)}, s32[2,2]{1,0:T(2,128)}, u32[]{:S(2)}) copy-start(s32[2,2]{1,0:T(2,128)} %near_ref.11) | copy-start | bytes 52
  28.6 1.6 %copy-start.1 = (f32[256,256]{1,0:T(8,128)S(1)}, f32[256,256]{1,0:T(8,128)}, u32[]{:S(2)}) copy-start(f32[256,256]{1,0:T(8,128)} %tau.3) | copy-start | bytes 786436
  28.6 1.6 %collective-permute-start.7 = (bf16[2,256,256]{2,1,0:T(8,128)(2,1)S(1)}, bf16[2,256,256]{2,1,0:T(8,128)(2,1)S(1)}, u32[]{:S(2)}, u32[]{:S(2)}) collective-permute-start(bf16[2,256,256]{2,1,0:T(8,128)(2,1)S(1)} %shard_map.126), channel_id=1, source_target_pairs={{0,1},{1,0},{2,3},{3,2},{4,5},{5,4},{6,7},{7,6},{8,9},{9,8},{10,11... | collective-permute-start | bytes 786440 | tf_op jit(solution)/shard_map/ppermute | solution.py:330
  31.8 7.6 %collective-permute-start.8 = (bf16[256,256]{1,0:T(8,128)(2,1)S(1)}, bf16[256,256]{1,0:T(8,128)(2,1)S(1)}, u32[]{:S(2)}, u32[]{:S(2)}) collective-permute-start(bf16[256,256]{1,0:T(8,128)(2,1)S(1)} %get-tuple-element.21.refs_0_), channel_id=1, source_target_pairs={{0,12},{2,14},{4,0},{6,2},{8,4},{10,6},{12,8},{14,10},{1,13},{3,15... | collective-permute-start | bytes 393224 | tf_op jit(solution)/shard_map/ppermute | solution.py:46
  35.4 10.8 %collective-permute-start.12 = (bf16[256,256]{1,0:T(8,128)(2,1)S(1)}, bf16[256,256]{1,0:T(8,128)(2,1)S(1)}, u32[]{:S(2)}, u32[]{:S(2)}) collective-permute-start(bf16[256,256]{1,0:T(8,128)(2,1)S(1)} %get-tuple-element.21.refs_0_), channel_id=1, source_target_pairs={{0,8},{2,10},{4,12},{6,14},{8,0},{10,2},{12,4},{14,6},{1,9},{3,11}... | collective-permute-start | bytes 393224 | tf_op jit(solution)/shard_map/ppermute | solution.py:46
  37.0 11.3 %collective-permute-start.14 = (bf16[256,256]{1,0:T(8,128)(2,1)S(1)}, bf16[256,256]{1,0:T(8,128)(2,1)S(1)}, u32[]{:S(2)}, u32[]{:S(2)}) collective-permute-start(bf16[256,256]{1,0:T(8,128)(2,1)S(1)} %get-tuple-element.21.refs_0_), channel_id=1, source_target_pairs={{0,2},{2,0},{4,6},{6,4},{8,10},{10,8},{12,14},{14,12},{1,3},{3,1},... | collective-permute-start | bytes 393224 | tf_op jit(solution)/shard_map/ppermute | solution.py:46
  46.2 9.0 %collective-permute-start.13 = (bf16[256,256]{1,0:T(8,128)(2,1)S(1)}, bf16[256,256]{1,0:T(8,128)(2,1)S(1)}, u32[]{:S(2)}, u32[]{:S(2)}) collective-permute-start(bf16[256,256]{1,0:T(8,128)(2,1)S(1)} %collective-permute-done.12.refs_3_), channel_id=1, source_target_pairs={{0,2},{2,0},{4,6},{6,4},{8,10},{10,8},{12,14},{14,12},{1,3},{3,1},... | collective-permute-start | bytes 393224 | tf_op jit(solution)/shard_map/ppermute | solution.py:46
  46.5 8.7 %collective-permute-start.10 = (bf16[256,256]{1,0:T(8,128)(2,1)S(1)}, bf16[256,256]{1,0:T(8,128)(2,1)S(1)}, u32[]{:S(2)}, u32[]{:S(2)}) collective-permute-start(bf16[256,256]{1,0:T(8,128)(2,1)S(1)} %get-tuple-element.21.refs_0_), channel_id=1, source_target_pairs={{0,6},{2,4},{4,10},{6,8},{8,14},{10,12},{12,2},{14,0},{1,7},{3,5},... | collective-permute-start | bytes 393224 | tf_op jit(solution)/shard_map/ppermute | solution.py:46
  47.1 9.8 %collective-permute-start.9 = (bf16[256,256]{1,0:T(8,128)(2,1)S(1)}, bf16[256,256]{1,0:T(8,128)(2,1)S(1)}, u32[]{:S(2)}, u32[]{:S(2)}) collective-permute-start(bf16[256,256]{1,0:T(8,128)(2,1)S(1)} %get-tuple-element.21.refs_0_), channel_id=1, source_target_pairs={{0,4},{2,6},{4,8},{6,10},{8,12},{10,14},{12,0},{14,2},{1,5},{3,7},... | collective-permute-start | bytes 393224 | tf_op jit(solution)/shard_map/ppermute | solution.py:46
  47.7 9.1 %collective-permute-start.11 = (bf16[256,256]{1,0:T(8,128)(2,1)S(1)}, bf16[256,256]{1,0:T(8,128)(2,1)S(1)}, u32[]{:S(2)}, u32[]{:S(2)}) collective-permute-start(bf16[256,256]{1,0:T(8,128)(2,1)S(1)} %collective-permute-done.8.refs_2_), channel_id=1, source_target_pairs={{0,2},{2,0},{4,6},{6,4},{8,10},{10,8},{12,14},{14,12},{1,3},{3,1},... | collective-permute-start | bytes 393224 | tf_op jit(solution)/shard_map/ppermute | solution.py:46
  57.8 1.6 %collective-permute-start.15 = (bf16[2,256,256]{2,1,0:T(8,128)(2,1)S(1)}, bf16[2,256,256]{2,1,0:T(8,128)(2,1)S(1)}, u32[]{:S(2)}, u32[]{:S(2)}) collective-permute-start(bf16[2,256,256]{2,1,0:T(8,128)(2,1)S(1)} %shard_map.130), channel_id=1, source_target_pairs={{0,1},{1,0},{2,3},{3,2},{4,5},{5,4},{6,7},{7,6},{8,9},{9,8},{10,11... | collective-permute-start | bytes 786440 | tf_op jit(solution)/shard_map/ppermute | solution.py:330

commit v4 on v3

--- a/solution.py
+++ b/solution.py
@@ -51,21 +51,42 @@
     for shift in shifts[:-1]:
         far[shift] = along(shift, 0, block)
     if shifts:
-        held = block
-        if far:
-            held, _ = lax.optimization_barrier((block, far[shifts[0]]))
-        last = [along(shifts[-1], 0, held), along(shifts[-1], 1, held)]
+        last = [along(shifts[-1], 0, block), along(shifts[-1], 1, block)]
     passed = [along(0, 1, far[shift]) for shift in shifts[:-1]]
     return [block, across, *far.values(), *last, *passed]
 
 
-def narrow_kernel(wide_ref, narrow_ref):
-    narrow_ref[...] = wide_ref[...].astype(narrow_ref.dtype)
-
-
-def prepare_kernel(
-    spots, row_ref, rank_ref, v_ref, u_ref, sigma_ref, a_ref, b_ref, state_ref, v_out, u_out, coef_out, weight_out, decay_out
-):
+PIECES = 4
+
+
+def row_pieces(size):
+    tall = size // PIECES
+    return [pl.ds(at * tall, tall) for at in range(PIECES)]
+
+
+def narrow_kernel(wide_ref, narrow_ref, held, sem):
+    copies = [
+        pltpu.make_async_copy(wide_ref.at[part], held.at[part], sem.at[at])
+        for at, part in enumerate(row_pieces(held.shape[0]))
+    ]
+    for copy in copies:
+        copy.start()
+    for copy, part in zip(copies, row_pieces(held.shape[0])):
+        copy.wait()
+        narrow_ref[part, :] = held[part, :].astype(narrow_ref.dtype)
+
+
+def prepare_kernel(spots, row_ref, *refs):
+    far, (v_out, u_out, coef_out, weight_out, decay_out), near, sem = refs[:7], refs[7:12], refs[12:19], refs[19]
+    copies = [
+        pltpu.make_async_copy(source, held, sem.at[at])
+        for at, (source, held) in enumerate(zip(far, near))
+    ]
+    for copy in copies:
+        copy.start()
+    for copy in copies:
+        copy.wait()
+    rank_ref, v_ref, u_ref, sigma_ref, a_ref, b_ref, state_ref = near
     kinds, rows, count, rank_count, size = u_ref.shape
     row = row_ref[0]
     met = [row_met(spot, row, count) for spot in spots]
@@ -175,12 +196,12 @@
     return (rate, change)
 
 
-def over_pieces(size, members, lanes, work):
-    step = min(size, 16)
-
-    @pl.loop(0, size // step)
+def over_pieces(begin, tall, members, lanes, work):
+    step = min(tall, 16)
+
+    @pl.loop(0, tall // step)
     def _(index):
-        rows = pl.ds(pl.multiple_of(index * step, step), step)
+        rows = pl.ds(pl.multiple_of(begin + index * step, step), step)
         for first in range(0, members, lanes):
             work(rows, slice(first, first + lanes))
 
@@ -207,11 +228,11 @@
         change[rows, part] = second
         rate_half[rows, part] = first.astype(rate_half.dtype)
 
-    over_pieces(size, members, coef.shape[2], work)
+    over_pieces(0, size, members, coef.shape[2], work)
 
 
 def section_two_kernel(
-    own, other, state, tau, coef, stress, normal, rate, change, mean_rate, mean_change
+    own, other, state, tau, coef, stress, normal, rate, change, rate_out, change_out, mean_rate, mean_change, sem
 ):
     size, members = tau.shape
 
@@ -233,16 +254,25 @@
         mean_rate[rows, part] = (rate[rows, part] + first) * 0.5
         mean_change[rows, part] = (change[rows, part] + second) * 0.5
 
-    over_pieces(size, members, coef.shape[2], work)
-
-
-def on_core(kernel, outs, scalars, arrays, scratch=(), flops=0, room=16):
+    copies = []
+    for at, part in enumerate(row_pieces(size)):
+        over_pieces(part.start, part.size, members, coef.shape[2], work)
+        for kind, (held, out) in enumerate(((mean_rate, rate_out), (mean_change, change_out))):
+            copies.append(pltpu.make_async_copy(held.at[part], out.at[part], sem.at[kind, at]))
+            copies[-1].start()
+    for copy in copies:
+        copy.wait()
+
+
+def on_core(kernel, outs, scalars, arrays, scratch=(), flops=0, room=16, far=(), out_far=False):
     smem, vmem = pl.BlockSpec(memory_space=pltpu.SMEM), pl.BlockSpec(memory_space=pltpu.VMEM)
+    hbm = pl.BlockSpec(memory_space=pl.ANY)
+    arrays = (*(pltpu.with_memory_space_constraint(a, pltpu.HBM) for a in far), *arrays)
     return pl.pallas_call(
         kernel,
         out_shape=outs,
-        in_specs=[smem] * len(scalars) + [vmem] * len(arrays),
-        out_specs=jax.tree.map(lambda _: vmem, outs),
+        in_specs=[smem] * len(scalars) + [hbm] * len(far) + [vmem] * (len(arrays) - len(far)),
+        out_specs=jax.tree.map(lambda _: hbm if out_far else vmem, outs),
         scratch_shapes=list(scratch),
         compiler_params=pltpu.CompilerParams(vmem_limit_bytes=room * 1024 * 1024),
         cost_estimate=pl.CostEstimate(
@@ -289,8 +319,19 @@
             full,
             full,
         ),
-        (row, block_ranks),
+        (row,),
+        (),
         (
+            pltpu.SMEM(block_ranks.shape, jnp.int32),
+            pltpu.VMEM(v_basis.shape, narrow),
+            pltpu.VMEM(u_basis.shape, narrow),
+            *[pltpu.VMEM((1, size), wide)] * 3,
+            pltpu.VMEM((size, members), wide),
+            pltpu.SemaphoreType.DMA((7,)),
+        ),
+        room=room,
+        far=(
+            block_ranks,
             v_basis,
             u_basis,
             sigma_base.reshape(1, size),
@@ -298,7 +339,6 @@
             b_coef.reshape(1, size),
             state_var,
         ),
-        room=room,
     )
 
     def add(blocks, first, pick, before, kind):
@@ -330,7 +370,14 @@
         other = lax.ppermute(add(blocks[early:], early, 1, sums, narrow), "col", swap)
         return add(blocks[early:], early, 0, sums, wide), other
 
-    slip_half = on_core(narrow_kernel, shaped(size, members, kind=narrow), (), (slip_deficit,))
+    slip_half = on_core(
+        narrow_kernel,
+        shaped(size, members, kind=narrow),
+        (),
+        (),
+        (pltpu.VMEM((size, members), wide), pltpu.SemaphoreType.DMA((PIECES,))),
+        far=(slip_deficit,),
+    )
     own, other = lattice(slip_half)
     stress, normal, rate, change, rate_half = on_core(
         section_one_kernel,
@@ -345,7 +392,13 @@
         (full, full),
         (),
         (own, other, state_var, tau_load, coef, stress, normal, rate, change),
+        (
+            pltpu.VMEM((size, members), wide),
+            pltpu.VMEM((size, members), wide),
+            pltpu.SemaphoreType.DMA((2, PIECES)),
+        ),
         flops=200 * size * members,
+        out_far=True,
     )
 
 

time: 62.5 us -> 52.7 us (0.84)
  waiting for transfers between devices: 23.2 us -> 13 us
  local copies, waits for them, and re-layouts: 6.43 us -> 0.68 us
  starting transfers between devices: 18.5 us -> 23.2 us
  Pallas kernels: 13.2 us -> 14.9 us
    ppermute x14, waiting for transfers between devices: 22.6 us -> 12.5 us  [along(): return lax.ppermute(data, 'row', hops)]
    unnamed x22 -> x8, local copies, waits for them, and re-layouts: 6.43 us -> 0.68 us
    ppermute x14, starting transfers between devices: 18.3 us -> 23.1 us  [along(): return lax.ppermute(data, 'row', hops)]
    pallas_call x10, Pallas kernels: 13.2 us -> 14.9 us  [on_core(): pl.pallas_call(kernel, out_shape=outs, in_specs=[smem] * len(scalars) + [...]
  transfers between devices with their start and end apart: 16 -> 16, of which waited for: 9 -> 10; matrix products, arithmetic and copies ran while one was open for 0% -> 0% of each run, Pallas kernels for 11% -> 14%
where the time goes in v4:
time: 52.7 us; the launch traced here: 52.6 us
  starting transfers between devices  23.2 us (44%)
  Pallas kernels  14.9 us (28%)
  waiting for transfers between devices  13 us (25%)
  between operations  0.8 us (2%)
  local copies, waits for them, and re-layouts  0.68 us (1%)
    ppermute x14, starting transfers between devices, along(): return lax.ppermute(data, 'row', hops)  23.1 us
    pallas_call x10, Pallas kernels, on_core(): pl.pallas_call(kernel, out_shape=outs, in_specs=[smem] * len(scalars) + [...  14.9 us
    ppermute x14, waiting for transfers between devices, along(): return lax.ppermute(data, 'row', hops)  12.5 us
  transfers between devices with their start and end apart: 16, of which 10 were waited for; matrix products, arithmetic and copies ran while one was open for 0% of the time, Pallas kernels for 14%

profile of v4, /device:TPU:0, one launch (start us, length us, event | category | flops | bytes accessed | tf_op | source)
XLA Modules:
  0.0 52.6 jit_solution(5829429688109743404)
XLA Ops:
  0.6 0.0 copy-start
  0.6 1.1 %shard_map.123.refs_0_ = bf16[256,256]{1,0:T(8,128)(2,1)S(1)} custom-call(f32[256,256]{1,0:T(8,128)} %wide_ref.1), custom_call_target="tpu_custom_call" | custom-call | bytes 262144 | tf_op jit(solution)/shard_map/pallas_call | solution.py:271
  1.7 4.1 %collective-permute-start.4 = (bf16[256,256]{1,0:T(8,128)(2,1)S(1)}, bf16[256,256]{1,0:T(8,128)(2,1)S(1)}, u32[]{:S(2)}, u32[]{:S(2)}) collective-permute-start(bf16[256,256]{1,0:T(8,128)(2,1)S(1)} %shard_map.123.refs_0_), channel_id=1, source_target_pairs={{0,8},{2,10},{4,12},{6,14},{8,0},{10,2},{12,4},{14,6},{1,9},{3,11}... | collective-permute-start | bytes 393224 | tf_op jit(solution)/shard_map/ppermute | solution.py:46
  5.8 1.3 %collective-permute-start.2 = (bf16[256,256]{1,0:T(8,128)(2,1)S(1)}, bf16[256,256]{1,0:T(8,128)(2,1)S(1)}, u32[]{:S(2)}, u32[]{:S(2)}) collective-permute-start(bf16[256,256]{1,0:T(8,128)(2,1)S(1)} %shard_map.123.refs_0_), channel_id=1, source_target_pairs={{0,12},{2,14},{4,0},{6,2},{8,4},{10,6},{12,8},{14,10},{1,13},{3,15... | collective-permute-start | bytes 393224 | tf_op jit(solution)/shard_map/ppermute | solution.py:46
  7.2 1.5 %collective-permute-start.6 = (bf16[256,256]{1,0:T(8,128)(2,1)S(1)}, bf16[256,256]{1,0:T(8,128)(2,1)S(1)}, u32[]{:S(2)}, u32[]{:S(2)}) collective-permute-start(bf16[256,256]{1,0:T(8,128)(2,1)S(1)} %shard_map.123.refs_0_), channel_id=1, source_target_pairs={{0,2},{2,0},{4,6},{6,4},{8,10},{10,8},{12,14},{14,12},{1,3},{3,1},... | collective-permute-start | bytes 393224 | tf_op jit(solution)/shard_map/ppermute | solution.py:46
  8.7 0.6 %collective-permute-start.1 = (bf16[256,256]{1,0:T(8,128)(2,1)S(1)}, bf16[256,256]{1,0:T(8,128)(2,1)S(1)}, u32[]{:S(2)}, u32[]{:S(2)}) collective-permute-start(bf16[256,256]{1,0:T(8,128)(2,1)S(1)} %shard_map.123.refs_0_), channel_id=1, source_target_pairs={{0,6},{2,4},{4,10},{6,8},{8,14},{10,12},{12,2},{14,0},{1,7},{3,5},... | collective-permute-start | bytes 393224 | tf_op jit(solution)/shard_map/ppermute | solution.py:46
  9.3 1.6 %collective-permute-start = (bf16[256,256]{1,0:T(8,128)(2,1)S(1)}, bf16[256,256]{1,0:T(8,128)(2,1)S(1)}, u32[]{:S(2)}, u32[]{:S(2)}) collective-permute-start(bf16[256,256]{1,0:T(8,128)(2,1)S(1)} %shard_map.123.refs_0_), channel_id=1, source_target_pairs={{0,4},{2,6},{4,8},{6,10},{8,12},{10,14},{12,0},{14,2},{1,5},{3,7},... | collective-permute-start | bytes 393224 | tf_op jit(solution)/shard_map/ppermute | solution.py:46
  10.9 2.9 %collective-permute-done.4.refs_3_ = bf16[256,256]{1,0:T(8,128)(2,1)S(1)} collective-permute-done((bf16[256,256]{1,0:T(8,128)(2,1)S(1)}, bf16[256,256]{1,0:T(8,128)(2,1)S(1)}, u32[]{:S(2)}, u32[]{:S(2)}) %collective-permute-start.4) | collective-permute-done | bytes 131104 | tf_op jit(solution)/shard_map/ppermute | solution.py:46
  13.8 2.2 %collective-permute-start.5 = (bf16[256,256]{1,0:T(8,128)(2,1)S(1)}, bf16[256,256]{1,0:T(8,128)(2,1)S(1)}, u32[]{:S(2)}, u32[]{:S(2)}) collective-permute-start(bf16[256,256]{1,0:T(8,128)(2,1)S(1)} %collective-permute-done.4.refs_3_), channel_id=1, source_target_pairs={{0,2},{2,0},{4,6},{6,4},{8,10},{10,8},{12,14},{14,12},{1,3},{3,1},... | collective-permute-start | bytes 393224 | tf_op jit(solution)/shard_map/ppermute | solution.py:46
  15.9 0.0 collective-permute-done.2.refs_2_
  15.9 0.0 collective-permute-start.3
  16.0 1.7 %shard_map.122 = (bf16[8,2,32,256]{3,2,1,0:T(8,128)(2,1)S(1)}, bf16[2,512,256]{2,1,0:T(8,128)(2,1)S(1)}, f32[3,256,128]{2,1,0:T(8,128)S(1)}, f32[256,256]{1,0:T(8,128)S(1)}, f32[256,256]{1,0:T(8,128)S(1)}) custom-call(s32[1]{0:T(128)} %bitcast.row_ref, s32[2,8]{1,0:T(2,128)} %refs_0_.1, bf16[2,8,32,256]{3,2,1,0:T(8,128)(2,1)} %refs_1_.1, ...), custom_call_target="tpu_custom_call" | custom-call | bytes 1051712 | tf_op jit(solution)/shard_map/pallas_call | solution.py:271
  17.7 0.0 collective-permute-done.6.refs_1_
  17.7 0.0 copy-start.3
  17.7 0.0 copy-done
  17.7 0.7 %copy-done.3 = s32[2,2]{1,0:T(2,128)S(1)} copy-done((s32[2,2]{1,0:T(2,128)S(1)}, s32[2,2]{1,0:T(2,128)}, u32[]{:S(2)}) %copy-start.3) | copy-done | bytes 40
  18.4 1.6 %shard_map.124.refs_4_ = f32[2,2,256,256]{3,2,1,0:T(8,128)S(1)} custom-call(s32[1]{0:T(128)} %bitcast.row_ref, s32[1]{0:T(128)} %bitcast.1.col_ref, s32[2,2]{1,0:T(2,128)S(1)} %copy-done.3, bf16[8,2,32,256]{3,2,1,0:T(8,128)(2,1)S(1)} %get-tuple-element.12.v_ref, bf16[2,512,256]{2,1,0:T(8,128)(2,1)S(1)} %get-tuple-element.13.u_ref, ...), custom_call_target="tpu_custom_call" | custom-call | flops 100663296 | bytes 2359296 | tf_op jit(solution)/shard_map/pallas_call | solution.py:271
  19.9 0.0 collective-permute-done.1.refs_1_
  19.9 0.0 collective-permute-done.refs_0_
  19.9 0.5 collective-permute-done.5.refs_3_
  20.4 1.4 %collective-permute-done.3.refs_2_ = bf16[256,256]{1,0:T(8,128)(2,1)S(1)} collective-permute-done((bf16[256,256]{1,0:T(8,128)(2,1)S(1)}, bf16[256,256]{1,0:T(8,128)(2,1)S(1)}, u32[]{:S(2)}, u32[]{:S(2)}) %collective-permute-start.3) | collective-permute-done | bytes 131104 | tf_op jit(solution)/shard_map/ppermute | solution.py:46
  21.8 1.2 %shard_map.126 = bf16[2,256,256]{2,1,0:T(8,128)(2,1)S(1)} custom-call(s32[1]{0:T(128)} %bitcast.row_ref, s32[1]{0:T(128)} %bitcast.1.col_ref, s32[2,2]{1,0:T(2,128)S(1)} %copy-done.3, bf16[8,2,32,256]{3,2,1,0:T(8,128)(2,1)S(1)} %get-tuple-element.12.v_ref, bf16[2,512,256]{2,1,0:T(8,128)(2,1)S(1)} %get-tuple-element.13.u_ref, ...), custom_call_target="tpu_custom_call" | custom-call | flops 50331648 | bytes 3407872 | tf_op jit(solution)/shard_map/pallas_call | solution.py:271
  23.1 0.0 copy-start.1
  23.1 0.1 collective-permute-start.7
  23.2 1.2 %shard_map.125.own = f32[2,256,256]{2,1,0:T(8,128)S(1)} custom-call(s32[1]{0:T(128)} %bitcast.row_ref, s32[1]{0:T(128)} %bitcast.1.col_ref, s32[2,2]{1,0:T(2,128)S(1)} %copy-done.3, bf16[8,2,32,256]{3,2,1,0:T(8,128)(2,1)S(1)} %get-tuple-element.12.v_ref, bf16[2,512,256]{2,1,0:T(8,128)(2,1)S(1)} %get-tuple-element.13.u_ref, ...), custom_call_target="tpu_custom_call" | custom-call | flops 50331648 | bytes 3407872 | tf_op jit(solution)/shard_map/pallas_call | solution.py:271
  24.4 0.3 collective-permute-done.7.other
  24.7 1.5 %shard_map.127 = (f32[256,256]{1,0:T(8,128)S(1)}, f32[256,256]{1,0:T(8,128)S(1)}, f32[256,256]{1,0:T(8,128)S(1)}, f32[256,256]{1,0:T(8,128)S(1)}, bf16[256,256]{1,0:T(8,128)(2,1)S(1)}) custom-call(f32[2,256,256]{2,1,0:T(8,128)S(1)} %shard_map.125.own, bf16[2,256,256]{2,1,0:T(8,128)(2,1)S(1)} %collective-permute-done.7.other, ...), custom_call_target="tpu_custom_call" | custom-call | flops 13107200 | bytes 1966080 | tf_op jit(solution)/shard_map/pallas_call | solution.py:271
  26.2 3.9 %collective-permute-start.12 = (bf16[256,256]{1,0:T(8,128)(2,1)S(1)}, bf16[256,256]{1,0:T(8,128)(2,1)S(1)}, u32[]{:S(2)}, u32[]{:S(2)}) collective-permute-start(bf16[256,256]{1,0:T(8,128)(2,1)S(1)} %get-tuple-element.17.refs_0_), channel_id=1, source_target_pairs={{0,8},{2,10},{4,12},{6,14},{8,0},{10,2},{12,4},{14,6},{1,9},{3,11}... | collective-permute-start | bytes 393224 | tf_op jit(solution)/shard_map/ppermute | solution.py:46
  30.1 3.6 %collective-permute-start.10 = (bf16[256,256]{1,0:T(8,128)(2,1)S(1)}, bf16[256,256]{1,0:T(8,128)(2,1)S(1)}, u32[]{:S(2)}, u32[]{:S(2)}) collective-permute-start(bf16[256,256]{1,0:T(8,128)(2,1)S(1)} %get-tuple-element.17.refs_0_), channel_id=1, source_target_pairs={{0,12},{2,14},{4,0},{6,2},{8,4},{10,6},{12,8},{14,10},{1,13},{3,15... | collective-permute-start | bytes 393224 | tf_op jit(solution)/shard_map/ppermute | solution.py:46
  33.7 1.0 %collective-permute-start.14 = (bf16[256,256]{1,0:T(8,128)(2,1)S(1)}, bf16[256,256]{1,0:T(8,128)(2,1)S(1)}, u32[]{:S(2)}, u32[]{:S(2)}) collective-permute-start(bf16[256,256]{1,0:T(8,128)(2,1)S(1)} %get-tuple-element.17.refs_0_), channel_id=1, source_target_pairs={{0,2},{2,0},{4,6},{6,4},{8,10},{10,8},{12,14},{14,12},{1,3},{3,1},... | collective-permute-start | bytes 393224 | tf_op jit(solution)/shard_map/ppermute | solution.py:46
  34.7 0.0 collective-permute-start.9
  34.7 0.5 %collective-permute-start.8 = (bf16[256,256]{1,0:T(8,128)(2,1)S(1)}, bf16[256,256]{1,0:T(8,128)(2,1)S(1)}, u32[]{:S(2)}, u32[]{:S(2)}) collective-permute-start(bf16[256,256]{1,0:T(8,128)(2,1)S(1)} %get-tuple-element.17.refs_0_), channel_id=1, source_target_pairs={{0,4},{2,6},{4,8},{6,10},{8,12},{10,14},{12,0},{14,2},{1,5},{3,7},... | collective-permute-start | bytes 393224 | tf_op jit(solution)/shard_map/ppermute | solution.py:46
  35.2 0.0 collective-permute-done.12.refs_3_
  35.2 1.7 %collective-permute-start.13 = (bf16[256,256]{1,0:T(8,128)(2,1)S(1)}, bf16[256,256]{1,0:T(8,128)(2,1)S(1)}, u32[]{:S(2)}, u32[]{:S(2)}) collective-permute-start(bf16[256,256]{1,0:T(8,128)(2,1)S(1)} %collective-permute-done.12.refs_3_), channel_id=1, source_target_pairs={{0,2},{2,0},{4,6},{6,4},{8,10},{10,8},{12,14},{14,12},{1,3},{3,1},... | collective-permute-start | bytes 393224 | tf_op jit(solution)/shard_map/ppermute | solution.py:46
  37.0 0.6 %collective-permute-done.10.refs_2_ = bf16[256,256]{1,0:T(8,128)(2,1)S(1)} collective-permute-done((bf16[256,256]{1,0:T(8,128)(2,1)S(1)}, bf16[256,256]{1,0:T(8,128)(2,1)S(1)}, u32[]{:S(2)}, u32[]{:S(2)}) %collective-permute-start.10) | collective-permute-done | bytes 131104 | tf_op jit(solution)/shard_map/ppermute | solution.py:46
  37.6 1.0 %collective-permute-start.11 = (bf16[256,256]{1,0:T(8,128)(2,1)S(1)}, bf16[256,256]{1,0:T(8,128)(2,1)S(1)}, u32[]{:S(2)}, u32[]{:S(2)}) collective-permute-start(bf16[256,256]{1,0:T(8,128)(2,1)S(1)} %collective-permute-done.10.refs_2_), channel_id=1, source_target_pairs={{0,2},{2,0},{4,6},{6,4},{8,10},{10,8},{12,14},{14,12},{1,3},{3,1},... | collective-permute-start | bytes 393224 | tf_op jit(solution)/shard_map/ppermute | solution.py:46
  38.6 2.0 %collective-permute-done.14.refs_1_ = bf16[256,256]{1,0:T(8,128)(2,1)S(1)} collective-permute-done((bf16[256,256]{1,0:T(8,128)(2,1)S(1)}, bf16[256,256]{1,0:T(8,128)(2,1)S(1)}, u32[]{:S(2)}, u32[]{:S(2)}) %collective-permute-start.14) | collective-permute-done | bytes 131104 | tf_op jit(solution)/shard_map/ppermute | solution.py:46
  40.6 1.6 %shard_map.128.refs_4_ = f32[2,2,256,256]{3,2,1,0:T(8,128)S(1)} custom-call(s32[1]{0:T(128)} %bitcast.row_ref, s32[1]{0:T(128)} %bitcast.1.col_ref, s32[2,2]{1,0:T(2,128)S(1)} %copy-done.3, bf16[8,2,32,256]{3,2,1,0:T(8,128)(2,1)S(1)} %get-tuple-element.12.v_ref, bf16[2,512,256]{2,1,0:T(8,128)(2,1)S(1)} %get-tuple-element.13.u_ref, ...), custom_call_target="tpu_custom_call" | custom-call | flops 100663296 | bytes 2359296 | tf_op jit(solution)/shard_map/pallas_call | solution.py:271
  42.1 2.0 %collective-permute-done.9.refs_1_ = bf16[256,256]{1,0:T(8,128)(2,1)S(1)} collective-permute-done((bf16[256,256]{1,0:T(8,128)(2,1)S(1)}, bf16[256,256]{1,0:T(8,128)(2,1)S(1)}, u32[]{:S(2)}, u32[]{:S(2)}) %collective-permute-start.9) | collective-permute-done | bytes 131104 | tf_op jit(solution)/shard_map/ppermute | solution.py:46
  44.1 1.7 %collective-permute-done.8.refs_0_ = bf16[256,256]{1,0:T(8,128)(2,1)S(1)} collective-permute-done((bf16[256,256]{1,0:T(8,128)(2,1)S(1)}, bf16[256,256]{1,0:T(8,128)(2,1)S(1)}, u32[]{:S(2)}, u32[]{:S(2)}) %collective-permute-start.8) | collective-permute-done | bytes 131104 | tf_op jit(solution)/shard_map/ppermute | solution.py:46
  45.8 0.0 collective-permute-done.13.refs_3_
  45.8 1.4 %collective-permute-done.11.refs_2_ = bf16[256,256]{1,0:T(8,128)(2,1)S(1)} collective-permute-done((bf16[256,256]{1,0:T(8,128)(2,1)S(1)}, bf16[256,256]{1,0:T(8,128)(2,1)S(1)}, u32[]{:S(2)}, u32[]{:S(2)}) %collective-permute-start.11) | collective-permute-done | bytes 131104 | tf_op jit(solution)/shard_map/ppermute | solution.py:46
  47.2 1.2 %shard_map.130 = bf16[2,256,256]{2,1,0:T(8,128)(2,1)S(1)} custom-call(s32[1]{0:T(128)} %bitcast.row_ref, s32[1]{0:T(128)} %bitcast.1.col_ref, s32[2,2]{1,0:T(2,128)S(1)} %copy-done.3, bf16[8,2,32,256]{3,2,1,0:T(8,128)(2,1)S(1)} %get-tuple-element.12.v_ref, bf16[2,512,256]{2,1,0:T(8,128)(2,1)S(1)} %get-tuple-element.13.u_ref, ...), custom_call_target="tpu_custom_call" | custom-call | flops 50331648 | bytes 3407872 | tf_op jit(solution)/shard_map/pallas_call | solution.py:271
  48.4 0.0 copy-start.2
  48.5 0.1 collective-permute-start.15
  48.5 1.2 %shard_map.129.own = f32[2,256,256]{2,1,0:T(8,128)S(1)} custom-call(s32[1]{0:T(128)} %bitcast.row_ref, s32[1]{0:T(128)} %bitcast.1.col_ref, s32[2,2]{1,0:T(2,128)S(1)} %copy-done.3, bf16[8,2,32,256]{3,2,1,0:T(8,128)(2,1)S(1)} %get-tuple-element.12.v_ref, bf16[2,512,256]{2,1,0:T(8,128)(2,1)S(1)} %get-tuple-element.13.u_ref, ...), custom_call_target="tpu_custom_call" | custom-call | flops 50331648 | bytes 3407872 | tf_op jit(solution)/shard_map/pallas_call | solution.py:271
  49.8 0.3 collective-permute-done.15.other
  50.1 2.6 %shard_map.131 = (f32[256,256]{1,0:T(8,128)}, f32[256,256]{1,0:T(8,128)}) custom-call(f32[2,256,256]{2,1,0:T(8,128)S(1)} %shard_map.129.own, bf16[2,256,256]{2,1,0:T(8,128)(2,1)S(1)} %collective-permute-done.15.other, f32[256,256]{1,0:T(8,128)S(1)} %copy-done.2, f32[256,256]{1,0:T(8,128)S(1)} %copy-done.1, f32[3,256,128]{2,1,0:T(8,128)S(1)} %get-tuple-element.16.coef, ...), custom_call_target="tpu_custom_call" | custom-call | flops 13107200 | bytes 2752512 | tf_op jit(solution)/shard_map/pallas_call | solution.py:271
  (2 shorter events, 0.0 us)
Async XLA Ops:
  0.6 17.1 %copy-start = (bf16[2,2,2,256,256]{4,3,2,1,0:T(8,128)(2,1)S(1)}, bf16[2,2,2,256,256]{4,3,2,1,0:T(8,128)(2,1)}, u32[]{:S(2)}) copy-start(bf16[2,2,2,256,256]{4,3,2,1,0:T(8,128)(2,1)} %d_ref.11) | copy-start | bytes 3145732
  1.7 12.1 %collective-permute-start.4 = (bf16[256,256]{1,0:T(8,128)(2,1)S(1)}, bf16[256,256]{1,0:T(8,128)(2,1)S(1)}, u32[]{:S(2)}, u32[]{:S(2)}) collective-permute-start(bf16[256,256]{1,0:T(8,128)(2,1)S(1)} %shard_map.123.refs_0_), channel_id=1, source_target_pairs={{0,8},{2,10},{4,12},{6,14},{8,0},{10,2},{12,4},{14,6},{1,9},{3,11}... | collective-permute-start | bytes 393224 | tf_op jit(solution)/shard_map/ppermute | solution.py:46
  5.8 10.1 %collective-permute-start.2 = (bf16[256,256]{1,0:T(8,128)(2,1)S(1)}, bf16[256,256]{1,0:T(8,128)(2,1)S(1)}, u32[]{:S(2)}, u32[]{:S(2)}) collective-permute-start(bf16[256,256]{1,0:T(8,128)(2,1)S(1)} %shard_map.123.refs_0_), channel_id=1, source_target_pairs={{0,12},{2,14},{4,0},{6,2},{8,4},{10,6},{12,8},{14,10},{1,13},{3,15... | collective-permute-start | bytes 393224 | tf_op jit(solution)/shard_map/ppermute | solution.py:46
  7.2 10.5 %collective-permute-start.6 = (bf16[256,256]{1,0:T(8,128)(2,1)S(1)}, bf16[256,256]{1,0:T(8,128)(2,1)S(1)}, u32[]{:S(2)}, u32[]{:S(2)}) collective-permute-start(bf16[256,256]{1,0:T(8,128)(2,1)S(1)} %shard_map.123.refs_0_), channel_id=1, source_target_pairs={{0,2},{2,0},{4,6},{6,4},{8,10},{10,8},{12,14},{14,12},{1,3},{3,1},... | collective-permute-start | bytes 393224 | tf_op jit(solution)/shard_map/ppermute | solution.py:46
  8.7 11.2 %collective-permute-start.1 = (bf16[256,256]{1,0:T(8,128)(2,1)S(1)}, bf16[256,256]{1,0:T(8,128)(2,1)S(1)}, u32[]{:S(2)}, u32[]{:S(2)}) collective-permute-start(bf16[256,256]{1,0:T(8,128)(2,1)S(1)} %shard_map.123.refs_0_), channel_id=1, source_target_pairs={{0,6},{2,4},{4,10},{6,8},{8,14},{10,12},{12,2},{14,0},{1,7},{3,5},... | collective-permute-start | bytes 393224 | tf_op jit(solution)/shard_map/ppermute | solution.py:46
  9.3 10.6 %collective-permute-start = (bf16[256,256]{1,0:T(8,128)(2,1)S(1)}, bf16[256,256]{1,0:T(8,128)(2,1)S(1)}, u32[]{:S(2)}, u32[]{:S(2)}) collective-permute-start(bf16[256,256]{1,0:T(8,128)(2,1)S(1)} %shard_map.123.refs_0_), channel_id=1, source_target_pairs={{0,4},{2,6},{4,8},{6,10},{8,12},{10,14},{12,0},{14,2},{1,5},{3,7},... | collective-permute-start | bytes 393224 | tf_op jit(solution)/shard_map/ppermute | solution.py:46
  13.8 6.7 %collective-permute-start.5 = (bf16[256,256]{1,0:T(8,128)(2,1)S(1)}, bf16[256,256]{1,0:T(8,128)(2,1)S(1)}, u32[]{:S(2)}, u32[]{:S(2)}) collective-permute-start(bf16[256,256]{1,0:T(8,128)(2,1)S(1)} %collective-permute-done.4.refs_3_), channel_id=1, source_target_pairs={{0,2},{2,0},{4,6},{6,4},{8,10},{10,8},{12,14},{14,12},{1,3},{3,1},... | collective-permute-start | bytes 393224 | tf_op jit(solution)/shard_map/ppermute | solution.py:46
  15.9 5.9 %collective-permute-start.3 = (bf16[256,256]{1,0:T(8,128)(2,1)S(1)}, bf16[256,256]{1,0:T(8,128)(2,1)S(1)}, u32[]{:S(2)}, u32[]{:S(2)}) collective-permute-start(bf16[256,256]{1,0:T(8,128)(2,1)S(1)} %collective-permute-done.2.refs_2_), channel_id=1, source_target_pairs={{0,2},{2,0},{4,6},{6,4},{8,10},{10,8},{12,14},{14,12},{1,3},{3,1},... | collective-permute-start | bytes 393224 | tf_op jit(solution)/shard_map/ppermute | solution.py:46
  17.7 0.7 %copy-start.3 = (s32[2,2]{1,0:T(2,128)S(1)}, s32[2,2]{1,0:T(2,128)}, u32[]{:S(2)}) copy-start(s32[2,2]{1,0:T(2,128)} %near_ref.11) | copy-start | bytes 52
  23.1 1.6 %copy-start.1 = (f32[256,256]{1,0:T(8,128)S(1)}, f32[256,256]{1,0:T(8,128)}, u32[]{:S(2)}) copy-start(f32[256,256]{1,0:T(8,128)} %tau.3) | copy-start | bytes 786436
  23.1 1.6 %collective-permute-start.7 = (bf16[2,256,256]{2,1,0:T(8,128)(2,1)S(1)}, bf16[2,256,256]{2,1,0:T(8,128)(2,1)S(1)}, u32[]{:S(2)}, u32[]{:S(2)}) collective-permute-start(bf16[2,256,256]{2,1,0:T(8,128)(2,1)S(1)} %shard_map.126), channel_id=1, source_target_pairs={{0,1},{1,0},{2,3},{3,2},{4,5},{5,4},{6,7},{7,6},{8,9},{9,8},{10,11... | collective-permute-start | bytes 786440 | tf_op jit(solution)/shard_map/ppermute | solution.py:370
  26.2 9.0 %collective-permute-start.12 = (bf16[256,256]{1,0:T(8,128)(2,1)S(1)}, bf16[256,256]{1,0:T(8,128)(2,1)S(1)}, u32[]{:S(2)}, u32[]{:S(2)}) collective-permute-start(bf16[256,256]{1,0:T(8,128)(2,1)S(1)} %get-tuple-element.17.refs_0_), channel_id=1, source_target_pairs={{0,8},{2,10},{4,12},{6,14},{8,0},{10,2},{12,4},{14,6},{1,9},{3,11}... | collective-permute-start | bytes 393224 | tf_op jit(solution)/shard_map/ppermute | solution.py:46
  30.1 7.5 %collective-permute-start.10 = (bf16[256,256]{1,0:T(8,128)(2,1)S(1)}, bf16[256,256]{1,0:T(8,128)(2,1)S(1)}, u32[]{:S(2)}, u32[]{:S(2)}) collective-permute-start(bf16[256,256]{1,0:T(8,128)(2,1)S(1)} %get-tuple-element.17.refs_0_), channel_id=1, source_target_pairs={{0,12},{2,14},{4,0},{6,2},{8,4},{10,6},{12,8},{14,10},{1,13},{3,15... | collective-permute-start | bytes 393224 | tf_op jit(solution)/shard_map/ppermute | solution.py:46
  33.7 6.9 %collective-permute-start.14 = (bf16[256,256]{1,0:T(8,128)(2,1)S(1)}, bf16[256,256]{1,0:T(8,128)(2,1)S(1)}, u32[]{:S(2)}, u32[]{:S(2)}) collective-permute-start(bf16[256,256]{1,0:T(8,128)(2,1)S(1)} %get-tuple-element.17.refs_0_), channel_id=1, source_target_pairs={{0,2},{2,0},{4,6},{6,4},{8,10},{10,8},{12,14},{14,12},{1,3},{3,1},... | collective-permute-start | bytes 393224 | tf_op jit(solution)/shard_map/ppermute | solution.py:46
  34.7 9.5 %collective-permute-start.9 = (bf16[256,256]{1,0:T(8,128)(2,1)S(1)}, bf16[256,256]{1,0:T(8,128)(2,1)S(1)}, u32[]{:S(2)}, u32[]{:S(2)}) collective-permute-start(bf16[256,256]{1,0:T(8,128)(2,1)S(1)} %get-tuple-element.17.refs_0_), channel_id=1, source_target_pairs={{0,6},{2,4},{4,10},{6,8},{8,14},{10,12},{12,2},{14,0},{1,7},{3,5},... | collective-permute-start | bytes 393224 | tf_op jit(solution)/shard_map/ppermute | solution.py:46
  34.7 11.2 %collective-permute-start.8 = (bf16[256,256]{1,0:T(8,128)(2,1)S(1)}, bf16[256,256]{1,0:T(8,128)(2,1)S(1)}, u32[]{:S(2)}, u32[]{:S(2)}) collective-permute-start(bf16[256,256]{1,0:T(8,128)(2,1)S(1)} %get-tuple-element.17.refs_0_), channel_id=1, source_target_pairs={{0,4},{2,6},{4,8},{6,10},{8,12},{10,14},{12,0},{14,2},{1,5},{3,7},... | collective-permute-start | bytes 393224 | tf_op jit(solution)/shard_map/ppermute | solution.py:46
  35.2 10.6 %collective-permute-start.13 = (bf16[256,256]{1,0:T(8,128)(2,1)S(1)}, bf16[256,256]{1,0:T(8,128)(2,1)S(1)}, u32[]{:S(2)}, u32[]{:S(2)}) collective-permute-start(bf16[256,256]{1,0:T(8,128)(2,1)S(1)} %collective-permute-done.12.refs_3_), channel_id=1, source_target_pairs={{0,2},{2,0},{4,6},{6,4},{8,10},{10,8},{12,14},{14,12},{1,3},{3,1},... | collective-permute-start | bytes 393224 | tf_op jit(solution)/shard_map/ppermute | solution.py:46
  37.6 9.6 %collective-permute-start.11 = (bf16[256,256]{1,0:T(8,128)(2,1)S(1)}, bf16[256,256]{1,0:T(8,128)(2,1)S(1)}, u32[]{:S(2)}, u32[]{:S(2)}) collective-permute-start(bf16[256,256]{1,0:T(8,128)(2,1)S(1)} %collective-permute-done.10.refs_2_), channel_id=1, source_target_pairs={{0,2},{2,0},{4,6},{6,4},{8,10},{10,8},{12,14},{14,12},{1,3},{3,1},... | collective-permute-start | bytes 393224 | tf_op jit(solution)/shard_map/ppermute | solution.py:46
  48.4 1.6 %copy-start.2 = (f32[256,256]{1,0:T(8,128)S(1)}, f32[256,256]{1,0:T(8,128)}, u32[]{:S(2)}) copy-start(f32[256,256]{1,0:T(8,128)} %state.1) | copy-start | bytes 786436
  48.5 1.6 %collective-permute-start.15 = (bf16[2,256,256]{2,1,0:T(8,128)(2,1)S(1)}, bf16[2,256,256]{2,1,0:T(8,128)(2,1)S(1)}, u32[]{:S(2)}, u32[]{:S(2)}) collective-permute-start(bf16[2,256,256]{2,1,0:T(8,128)(2,1)S(1)} %shard_map.130), channel_id=1, source_target_pairs={{0,1},{1,0},{2,3},{3,2},{4,5},{5,4},{6,7},{7,6},{8,9},{9,8},{10,11... | collective-permute-start | bytes 786440 | tf_op jit(solution)/shard_map/ppermute | solution.py:370

commit v5 on v4

--- a/solution.py
+++ b/solution.py
@@ -9,7 +9,8 @@
 
 NEWTON = 2
 DIRECT_LIMIT = 16
-LATE = 4
+LATE = 3
+TILE = 128
 
 damping = 0.5
 sigma_floor = 0.5
@@ -21,9 +22,12 @@
         return list(range(count))
     length = count // 2
     shifts = list(range(length - 1, 0, -1))
-    early = [(0, 0), (0, 1)] + [(shift, 0) for shift in shifts[:-1]]
-    late = [(shift, 0) for shift in shifts[-1:]] + [(shift, 1) for shift in shifts[-1:]]
-    return early + late + [(shift, 1) for shift in shifts[:-1]]
+    return [(0, 0), (0, 1)] + [(shift, 0) for shift in shifts] + [(shift, 1) for shift in shifts[::-1]]
+
+
+def columns(first, last, early, rank_count):
+    gap = -early * rank_count % TILE if first >= early else 0
+    return slice(first * rank_count + gap, last * rank_count + gap)
 
 
 def row_met(spot, row, count):
@@ -46,14 +50,16 @@
         return lax.ppermute(data, "row", hops)
 
     shifts = list(range(length - 1, 0, -1))
-    far, last = {}, []
+    far = [along(shift, 0, block) for shift in shifts[:-1]]
     across = along(0, 1, block)
-    for shift in shifts[:-1]:
-        far[shift] = along(shift, 0, block)
+    passed = [along(0, 1, data) for data in far]
+    near = []
     if shifts:
-        last = [along(shifts[-1], 0, block), along(shifts[-1], 1, block)]
-    passed = [along(0, 1, far[shift]) for shift in shifts[:-1]]
-    return [block, across, *far.values(), *last, *passed]
+        after = lax.optimization_barrier((block, across))[0]
+        near = [along(shifts[-1], 0, after)]
+        after = lax.optimization_barrier((block, far[0]))[0] if far else block
+        passed.append(along(shifts[-1], 1, after))
+    return [block, across, *far, *near, *passed[::-1]]
 
 
 PIECES = 4
@@ -76,7 +82,7 @@
         narrow_ref[part, :] = held[part, :].astype(narrow_ref.dtype)
 
 
-def prepare_kernel(spots, row_ref, *refs):
+def prepare_kernel(spots, early, row_ref, *refs):
     far, (v_out, u_out, coef_out, weight_out, decay_out), near, sem = refs[:7], refs[7:12], refs[12:19], refs[19]
     copies = [
         pltpu.make_async_copy(source, held, sem.at[at])
@@ -96,11 +102,17 @@
             v_out[at, p] = jnp.where(inside, v_ref[p, q].astype(jnp.float32), 0.0).astype(v_out.dtype)
     for p in range(rows):
         for kind in range(kinds):
-            for first in range(0, count, 4):
-                group = [u_ref[kind, p, q] for q in met[first : first + 4]]
+            for first, last in ((0, early), (early, count)):
+                group = [u_ref[kind, p, q] for q in met[first:last]]
+                if not group:
+                    continue
+                spare = -len(group) * rank_count % TILE
+                if spare:
+                    group.append(jnp.zeros((spare, size), u_ref.dtype))
                 turned = jnp.concatenate(group, axis=0).astype(jnp.float32).T
-                u_out[p, kind * size : (kind + 1) * size, first * rank_count : (first + len(group)) * rank_count] = (
-                    turned.astype(u_out.dtype)
+                start = columns(first, last, early, rank_count).start
+                u_out[p, kind * size : (kind + 1) * size, start : start + turned.shape[1]] = turned.astype(
+                    u_out.dtype
                 )
     lanes = coef_out.shape[2]
     for at, ref in enumerate((sigma_ref, a_ref, b_ref)):
@@ -112,7 +124,7 @@
         decay_out[:, part] = jnp.exp(-state / coef_out[2])
 
 
-def sums_kernel(spots, first, pick, before, row_ref, col_ref, near_ref, v_ref, u_ref, d_ref, *refs):
+def sums_kernel(spots, first, early, pick, before, row_ref, col_ref, near_ref, v_ref, u_ref, d_ref, *refs):
     blocks = refs[: len(spots)]
     refs = refs[len(spots) :]
     if before:
@@ -135,7 +147,7 @@
             proj[place, at * rank_count : (at + 1) * rank_count, :] = part[
                 place * rank_count : (place + 1) * rank_count
             ]
-    lanes = slice(first * rank_count, (first + len(blocks)) * rank_count)
+    lanes = columns(first, first + len(blocks), early, rank_count)
     for place, p in enumerate(chosen):
         gained = jnp.dot(u_ref[p, :, lanes], proj[place], preferred_element_type=jnp.float32)
         for kind in range(kinds):
@@ -300,6 +312,7 @@
     direct = count % 2 == 0 and count <= DIRECT_LIMIT
     spots = arrivals(count, direct)
     early = max(count - LATE, 0)
+    width = -(-columns(early, count, early, rank_count).stop // TILE) * TILE
     room = 16 if direct else 40
     lanes = min(members, 128)
     narrow, wide = jnp.bfloat16, jnp.float32
@@ -311,10 +324,10 @@
 
     full = shaped(size, members)
     v_met, u_met, coef, weight, decay = on_core(
-        functools.partial(prepare_kernel, spots),
+        functools.partial(prepare_kernel, spots, early),
         (
             shaped(count, rows, rank_count, size, kind=narrow),
-            shaped(rows, kinds * size, count * rank_count, kind=narrow),
+            shaped(rows, kinds * size, width, kind=narrow),
             shaped(3, size, lanes),
             full,
             full,
@@ -346,7 +359,7 @@
         lead = (rows, kinds) if pick is None else (kinds,)
         return on_core(
             functools.partial(
-                sums_kernel, spots[first : first + len(blocks)], first, pick, before is not None
+                sums_kernel, spots[first : first + len(blocks)], first, early, pick, before is not None
             ),
             shaped(*lead, size, members, kind=kind),
             (row, col, near_index),

time: 52.7 us -> 63.2 us (1.20)
  waiting for transfers between devices: 13 us -> 31.8 us
  starting transfers between devices: 23.2 us -> 14.6 us
    ppermute x14, waiting for transfers between devices: 12.5 us -> 31.2 us  [along(): return lax.ppermute(data, 'row', hops)]
    ppermute x14, starting transfers between devices: 23.1 us -> 14.5 us  [along(): return lax.ppermute(data, 'row', hops)]
  transfers between devices with their start and end apart: 16 -> 16, of which waited for: 10 -> 11; matrix products, arithmetic and copies ran while one was open for 0% -> 0% of each run, Pallas kernels for 14% -> 12%
where the time goes in v5:
time: 63.2 us; the launch traced here: 62.9 us
  waiting for transfers between devices  31.8 us (50%)
  Pallas kernels  15 us (24%)
  starting transfers between devices  14.6 us (23%)
  between operations  0.78 us (1%)
  local copies, waits for them, and re-layouts  0.68 us (1%)
    ppermute x14, waiting for transfers between devices, along(): return lax.ppermute(data, 'row', hops)  31.2 us
    pallas_call x10, Pallas kernels, on_core(): pl.pallas_call(kernel, out_shape=outs, in_specs=[smem] * len(scalars) + [...  15 us
    ppermute x14, starting transfers between devices, along(): return lax.ppermute(data, 'row', hops)  14.5 us
  transfers between devices with their start and end apart: 16, of which 11 were waited for; matrix products, arithmetic and copies ran while one was open for 0% of the time, Pallas kernels for 12%

profile of v5, /device:TPU:0, one launch (start us, length us, event | category | flops | bytes accessed | tf_op | source)
XLA Modules:
  0.0 62.9 jit_solution(17907016572609590848)
XLA Ops:
  0.6 0.0 copy-start
  0.6 1.1 %shard_map.123.refs_0_ = bf16[256,256]{1,0:T(8,128)(2,1)S(1)} custom-call(f32[256,256]{1,0:T(8,128)} %wide_ref.1), custom_call_target="tpu_custom_call" | custom-call | bytes 262144 | tf_op jit(solution)/shard_map/pallas_call | solution.py:283
  1.7 3.0 %collective-permute-start.5 = (bf16[256,256]{1,0:T(8,128)(2,1)S(1)}, bf16[256,256]{1,0:T(8,128)(2,1)S(1)}, u32[]{:S(2)}, u32[]{:S(2)}) collective-permute-start(bf16[256,256]{1,0:T(8,128)(2,1)S(1)} %shard_map.123.refs_0_), channel_id=1, source_target_pairs={{0,2},{2,0},{4,6},{6,4},{8,10},{10,8},{12,14},{14,12},{1,3},{3,1},... | collective-permute-start | bytes 393224 | tf_op jit(solution)/shard_map/ppermute | solution.py:50
  4.7 3.6 %collective-permute-start = (bf16[256,256]{1,0:T(8,128)(2,1)S(1)}, bf16[256,256]{1,0:T(8,128)(2,1)S(1)}, u32[]{:S(2)}, u32[]{:S(2)}) collective-permute-start(bf16[256,256]{1,0:T(8,128)(2,1)S(1)} %shard_map.123.refs_0_), channel_id=1, source_target_pairs={{0,12},{2,14},{4,0},{6,2},{8,4},{10,6},{12,8},{14,10},{1,13},{3,15... | collective-permute-start | bytes 393224 | tf_op jit(solution)/shard_map/ppermute | solution.py:50
  8.3 0.0 collective-permute-start.2
  8.3 0.0 collective-permute-done.5.refs_1_
  8.3 1.7 %collective-permute-start.6 = (bf16[256,256]{1,0:T(8,128)(2,1)S(1)}, bf16[256,256]{1,0:T(8,128)(2,1)S(1)}, u32[]{:S(2)}, u32[]{:S(2)}) collective-permute-start(bf16[256,256]{1,0:T(8,128)(2,1)S(1)} %shard_map.123.refs_0_), channel_id=1, source_target_pairs={{0,4},{2,6},{4,8},{6,10},{8,12},{10,14},{12,0},{14,2},{1,5},{3,7},... | collective-permute-start | bytes 393224 | tf_op jit(solution)/shard_map/ppermute | solution.py:50
  10.0 2.2 %collective-permute-done.refs_2_ = bf16[256,256]{1,0:T(8,128)(2,1)S(1)} collective-permute-done((bf16[256,256]{1,0:T(8,128)(2,1)S(1)}, bf16[256,256]{1,0:T(8,128)(2,1)S(1)}, u32[]{:S(2)}, u32[]{:S(2)}) %collective-permute-start) | collective-permute-done | bytes 131104 | tf_op jit(solution)/shard_map/ppermute | solution.py:50
  12.3 6.9 %collective-permute-done.2.refs_3_ = bf16[256,256]{1,0:T(8,128)(2,1)S(1)} collective-permute-done((bf16[256,256]{1,0:T(8,128)(2,1)S(1)}, bf16[256,256]{1,0:T(8,128)(2,1)S(1)}, u32[]{:S(2)}, u32[]{:S(2)}) %collective-permute-start.2) | collective-permute-done | bytes 131104 | tf_op jit(solution)/shard_map/ppermute | solution.py:50
  19.1 0.5 collective-permute-start.3
  19.7 0.0 collective-permute-start.1
  19.7 1.5 %collective-permute-start.4 = (bf16[256,256]{1,0:T(8,128)(2,1)S(1)}, bf16[256,256]{1,0:T(8,128)(2,1)S(1)}, u32[]{:S(2)}, u32[]{:S(2)}) collective-permute-start(bf16[256,256]{1,0:T(8,128)(2,1)S(1)} %collective-permute-done.refs_2_), channel_id=1, source_target_pairs={{0,2},{2,0},{4,6},{6,4},{8,10},{10,8},{12,14},{14,12},{1,3},{3,1},... | collective-permute-start | bytes 393224 | tf_op jit(solution)/shard_map/ppermute | solution.py:50
  21.2 1.7 %shard_map.122 = (bf16[8,2,32,256]{3,2,1,0:T(8,128)(2,1)S(1)}, bf16[2,512,384]{2,1,0:T(8,128)(2,1)S(1)}, f32[3,256,128]{2,1,0:T(8,128)S(1)}, f32[256,256]{1,0:T(8,128)S(1)}, f32[256,256]{1,0:T(8,128)S(1)}) custom-call(s32[1]{0:T(128)} %bitcast.row_ref, s32[2,8]{1,0:T(2,128)} %refs_0_.1, bf16[2,8,32,256]{3,2,1,0:T(8,128)(2,1)} %refs_1_.1, ...), custom_call_target="tpu_custom_call" | custom-call | bytes 1051712 | tf_op jit(solution)/shard_map/pallas_call | solution.py:283
  22.9 0.0 collective-permute-done.6.refs_4_
  22.9 0.0 copy-start.3
  23.0 0.7 %copy-done.3 = s32[2,2]{1,0:T(2,128)S(1)} copy-done((s32[2,2]{1,0:T(2,128)S(1)}, s32[2,2]{1,0:T(2,128)}, u32[]{:S(2)}) %copy-start.3) | copy-done | bytes 40
  23.6 1.8 %shard_map.124.refs_3_ = f32[2,2,256,256]{3,2,1,0:T(8,128)S(1)} custom-call(s32[1]{0:T(128)} %bitcast.row_ref, s32[1]{0:T(128)} %bitcast.1.col_ref, s32[2,2]{1,0:T(2,128)S(1)} %copy-done.3, bf16[8,2,32,256]{3,2,1,0:T(8,128)(2,1)S(1)} %get-tuple-element.16.v_ref, bf16[2,512,384]{2,1,0:T(8,128)(2,1)S(1)} %get-tuple-element.17.u_ref, ...), custom_call_target="tpu_custom_call" | custom-call | flops 125829120 | bytes 2752512 | tf_op jit(solution)/shard_map/pallas_call | solution.py:283
  25.5 2.5 %collective-permute-done.3.refs_1_ = bf16[256,256]{1,0:T(8,128)(2,1)S(1)} collective-permute-done((bf16[256,256]{1,0:T(8,128)(2,1)S(1)}, bf16[256,256]{1,0:T(8,128)(2,1)S(1)}, u32[]{:S(2)}, u32[]{:S(2)}) %collective-permute-start.3) | collective-permute-done | bytes 131104 | tf_op jit(solution)/shard_map/ppermute | solution.py:50
  28.0 0.0 collective-permute-done.1.refs_0_
  28.0 1.4 %collective-permute-done.4.refs_2_ = bf16[256,256]{1,0:T(8,128)(2,1)S(1)} collective-permute-done((bf16[256,256]{1,0:T(8,128)(2,1)S(1)}, bf16[256,256]{1,0:T(8,128)(2,1)S(1)}, u32[]{:S(2)}, u32[]{:S(2)}) %collective-permute-start.4) | collective-permute-done | bytes 131104 | tf_op jit(solution)/shard_map/ppermute | solution.py:50
  29.4 1.0 %shard_map.126 = bf16[2,256,256]{2,1,0:T(8,128)(2,1)S(1)} custom-call(s32[1]{0:T(128)} %bitcast.row_ref, s32[1]{0:T(128)} %bitcast.1.col_ref, s32[2,2]{1,0:T(2,128)S(1)} %copy-done.3, bf16[8,2,32,256]{3,2,1,0:T(8,128)(2,1)S(1)} %get-tuple-element.16.v_ref, bf16[2,512,384]{2,1,0:T(8,128)(2,1)S(1)} %get-tuple-element.17.u_ref, ...), custom_call_target="tpu_custom_call" | custom-call | flops 37748736 | bytes 3538944 | tf_op jit(solution)/shard_map/pallas_call | solution.py:283
  30.4 0.0 copy-start.1
  30.4 0.1 collective-permute-start.7
  30.5 1.2 %shard_map.125.own = f32[2,256,256]{2,1,0:T(8,128)S(1)} custom-call(s32[1]{0:T(128)} %bitcast.row_ref, s32[1]{0:T(128)} %bitcast.1.col_ref, s32[2,2]{1,0:T(2,128)S(1)} %copy-done.3, bf16[8,2,32,256]{3,2,1,0:T(8,128)(2,1)S(1)} %get-tuple-element.16.v_ref, bf16[2,512,384]{2,1,0:T(8,128)(2,1)S(1)} %get-tuple-element.17.u_ref, ...), custom_call_target="tpu_custom_call" | custom-call | flops 37748736 | bytes 3538944 | tf_op jit(solution)/shard_map/pallas_call | solution.py:283
  31.7 0.3 collective-permute-done.7.other
  32.0 1.5 %shard_map.127 = (f32[256,256]{1,0:T(8,128)S(1)}, f32[256,256]{1,0:T(8,128)S(1)}, f32[256,256]{1,0:T(8,128)S(1)}, f32[256,256]{1,0:T(8,128)S(1)}, bf16[256,256]{1,0:T(8,128)(2,1)S(1)}) custom-call(f32[2,256,256]{2,1,0:T(8,128)S(1)} %shard_map.125.own, bf16[2,256,256]{2,1,0:T(8,128)(2,1)S(1)} %collective-permute-done.7.other, ...), custom_call_target="tpu_custom_call" | custom-call | flops 13107200 | bytes 1966080 | tf_op jit(solution)/shard_map/pallas_call | solution.py:283
  33.6 0.6 collective-permute-start.13
  34.1 1.5 %collective-permute-start.8 = (bf16[256,256]{1,0:T(8,128)(2,1)S(1)}, bf16[256,256]{1,0:T(8,128)(2,1)S(1)}, u32[]{:S(2)}, u32[]{:S(2)}) collective-permute-start(bf16[256,256]{1,0:T(8,128)(2,1)S(1)} %get-tuple-element.25.refs_0_), channel_id=1, source_target_pairs={{0,12},{2,14},{4,0},{6,2},{8,4},{10,6},{12,8},{14,10},{1,13},{3,15... | collective-permute-start | bytes 393224 | tf_op jit(solution)/shard_map/ppermute | solution.py:50
  35.6 0.0 collective-permute-start.10
  35.6 3.6 %collective-permute-done.13.refs_1_ = bf16[256,256]{1,0:T(8,128)(2,1)S(1)} collective-permute-done((bf16[256,256]{1,0:T(8,128)(2,1)S(1)}, bf16[256,256]{1,0:T(8,128)(2,1)S(1)}, u32[]{:S(2)}, u32[]{:S(2)}) %collective-permute-start.13) | collective-permute-done | bytes 131104 | tf_op jit(solution)/shard_map/ppermute | solution.py:50
  39.2 0.0 collective-permute-start.14
  39.2 0.7 %collective-permute-done.8.refs_2_ = bf16[256,256]{1,0:T(8,128)(2,1)S(1)} collective-permute-done((bf16[256,256]{1,0:T(8,128)(2,1)S(1)}, bf16[256,256]{1,0:T(8,128)(2,1)S(1)}, u32[]{:S(2)}, u32[]{:S(2)}) %collective-permute-start.8) | collective-permute-done | bytes 131104 | tf_op jit(solution)/shard_map/ppermute | solution.py:50
  39.9 7.2 %collective-permute-done.10.refs_3_ = bf16[256,256]{1,0:T(8,128)(2,1)S(1)} collective-permute-done((bf16[256,256]{1,0:T(8,128)(2,1)S(1)}, bf16[256,256]{1,0:T(8,128)(2,1)S(1)}, u32[]{:S(2)}, u32[]{:S(2)}) %collective-permute-start.10) | collective-permute-done | bytes 131104 | tf_op jit(solution)/shard_map/ppermute | solution.py:50
  47.1 1.1 %collective-permute-start.11 = (bf16[256,256]{1,0:T(8,128)(2,1)S(1)}, bf16[256,256]{1,0:T(8,128)(2,1)S(1)}, u32[]{:S(2)}, u32[]{:S(2)}) collective-permute-start(bf16[256,256]{1,0:T(8,128)(2,1)S(1)} %collective-permute-done.10.refs_3_), channel_id=1, source_target_pairs={{0,2},{2,0},{4,6},{6,4},{8,10},{10,8},{12,14},{14,12},{1,3},{3,1},... | collective-permute-start | bytes 393224 | tf_op jit(solution)/shard_map/ppermute | solution.py:50
  48.2 0.0 collective-permute-start.9
  48.2 0.9 %collective-permute-start.12 = (bf16[256,256]{1,0:T(8,128)(2,1)S(1)}, bf16[256,256]{1,0:T(8,128)(2,1)S(1)}, u32[]{:S(2)}, u32[]{:S(2)}) collective-permute-start(bf16[256,256]{1,0:T(8,128)(2,1)S(1)} %collective-permute-done.8.refs_2_), channel_id=1, source_target_pairs={{0,2},{2,0},{4,6},{6,4},{8,10},{10,8},{12,14},{14,12},{1,3},{3,1},... | collective-permute-start | bytes 393224 | tf_op jit(solution)/shard_map/ppermute | solution.py:50
  49.1 0.0 collective-permute-done.14.refs_4_
  49.1 1.8 %shard_map.128.refs_3_ = f32[2,2,256,256]{3,2,1,0:T(8,128)S(1)} custom-call(s32[1]{0:T(128)} %bitcast.row_ref, s32[1]{0:T(128)} %bitcast.1.col_ref, s32[2,2]{1,0:T(2,128)S(1)} %copy-done.3, bf16[8,2,32,256]{3,2,1,0:T(8,128)(2,1)S(1)} %get-tuple-element.16.v_ref, bf16[2,512,384]{2,1,0:T(8,128)(2,1)S(1)} %get-tuple-element.17.u_ref, ...), custom_call_target="tpu_custom_call" | custom-call | flops 125829120 | bytes 2752512 | tf_op jit(solution)/shard_map/pallas_call | solution.py:283
  51.0 5.2 %collective-permute-done.11.refs_1_ = bf16[256,256]{1,0:T(8,128)(2,1)S(1)} collective-permute-done((bf16[256,256]{1,0:T(8,128)(2,1)S(1)}, bf16[256,256]{1,0:T(8,128)(2,1)S(1)}, u32[]{:S(2)}, u32[]{:S(2)}) %collective-permute-start.11) | collective-permute-done | bytes 131104 | tf_op jit(solution)/shard_map/ppermute | solution.py:50
  56.2 0.0 collective-permute-done.9.refs_0_
  56.2 1.4 %collective-permute-done.12.refs_2_ = bf16[256,256]{1,0:T(8,128)(2,1)S(1)} collective-permute-done((bf16[256,256]{1,0:T(8,128)(2,1)S(1)}, bf16[256,256]{1,0:T(8,128)(2,1)S(1)}, u32[]{:S(2)}, u32[]{:S(2)}) %collective-permute-start.12) | collective-permute-done | bytes 131104 | tf_op jit(solution)/shard_map/ppermute | solution.py:50
  57.6 1.0 %shard_map.130 = bf16[2,256,256]{2,1,0:T(8,128)(2,1)S(1)} custom-call(s32[1]{0:T(128)} %bitcast.row_ref, s32[1]{0:T(128)} %bitcast.1.col_ref, s32[2,2]{1,0:T(2,128)S(1)} %copy-done.3, bf16[8,2,32,256]{3,2,1,0:T(8,128)(2,1)S(1)} %get-tuple-element.16.v_ref, bf16[2,512,384]{2,1,0:T(8,128)(2,1)S(1)} %get-tuple-element.17.u_ref, ...), custom_call_target="tpu_custom_call" | custom-call | flops 37748736 | bytes 3538944 | tf_op jit(solution)/shard_map/pallas_call | solution.py:283
  58.7 0.0 copy-start.2
  58.7 0.1 collective-permute-start.15
  58.8 1.2 %shard_map.129.own = f32[2,256,256]{2,1,0:T(8,128)S(1)} custom-call(s32[1]{0:T(128)} %bitcast.row_ref, s32[1]{0:T(128)} %bitcast.1.col_ref, s32[2,2]{1,0:T(2,128)S(1)} %copy-done.3, bf16[8,2,32,256]{3,2,1,0:T(8,128)(2,1)S(1)} %get-tuple-element.16.v_ref, bf16[2,512,384]{2,1,0:T(8,128)(2,1)S(1)} %get-tuple-element.17.u_ref, ...), custom_call_target="tpu_custom_call" | custom-call | flops 37748736 | bytes 3538944 | tf_op jit(solution)/shard_map/pallas_call | solution.py:283
  60.0 0.3 collective-permute-done.15.other
  60.3 0.0 copy-done.2
  60.3 2.6 %shard_map.131 = (f32[256,256]{1,0:T(8,128)}, f32[256,256]{1,0:T(8,128)}) custom-call(f32[2,256,256]{2,1,0:T(8,128)S(1)} %shard_map.129.own, bf16[2,256,256]{2,1,0:T(8,128)(2,1)S(1)} %collective-permute-done.15.other, f32[256,256]{1,0:T(8,128)S(1)} %copy-done.2, f32[256,256]{1,0:T(8,128)S(1)} %copy-done.1, f32[3,256,128]{2,1,0:T(8,128)S(1)} %get-tuple-element.22.coef, ...), custom_call_target="tpu_custom_call" | custom-call | flops 13107200 | bytes 2752512 | tf_op jit(solution)/shard_map/pallas_call | solution.py:283
  (2 shorter events, 0.0 us)
Async XLA Ops:
  0.6 22.3 %copy-start = (bf16[2,2,2,256,256]{4,3,2,1,0:T(8,128)(2,1)S(1)}, bf16[2,2,2,256,256]{4,3,2,1,0:T(8,128)(2,1)}, u32[]{:S(2)}) copy-start(bf16[2,2,2,256,256]{4,3,2,1,0:T(8,128)(2,1)} %d_ref.11) | copy-start | bytes 3145732
  1.7 6.6 %collective-permute-start.5 = (bf16[256,256]{1,0:T(8,128)(2,1)S(1)}, bf16[256,256]{1,0:T(8,128)(2,1)S(1)}, u32[]{:S(2)}, u32[]{:S(2)}) collective-permute-start(bf16[256,256]{1,0:T(8,128)(2,1)S(1)} %shard_map.123.refs_0_), channel_id=1, source_target_pairs={{0,2},{2,0},{4,6},{6,4},{8,10},{10,8},{12,14},{14,12},{1,3},{3,1},... | collective-permute-start | bytes 393224 | tf_op jit(solution)/shard_map/ppermute | solution.py:50
  4.7 7.5 %collective-permute-start = (bf16[256,256]{1,0:T(8,128)(2,1)S(1)}, bf16[256,256]{1,0:T(8,128)(2,1)S(1)}, u32[]{:S(2)}, u32[]{:S(2)}) collective-permute-start(bf16[256,256]{1,0:T(8,128)(2,1)S(1)} %shard_map.123.refs_0_), channel_id=1, source_target_pairs={{0,12},{2,14},{4,0},{6,2},{8,4},{10,6},{12,8},{14,10},{1,13},{3,15... | collective-permute-start | bytes 393224 | tf_op jit(solution)/shard_map/ppermute | solution.py:50
  8.3 10.8 %collective-permute-start.2 = (bf16[256,256]{1,0:T(8,128)(2,1)S(1)}, bf16[256,256]{1,0:T(8,128)(2,1)S(1)}, u32[]{:S(2)}, u32[]{:S(2)}) collective-permute-start(bf16[256,256]{1,0:T(8,128)(2,1)S(1)} %shard_map.123.refs_0_), channel_id=1, source_target_pairs={{0,8},{2,10},{4,12},{6,14},{8,0},{10,2},{12,4},{14,6},{1,9},{3,11}... | collective-permute-start | bytes 393224 | tf_op jit(solution)/shard_map/ppermute | solution.py:50
  8.3 14.6 %collective-permute-start.6 = (bf16[256,256]{1,0:T(8,128)(2,1)S(1)}, bf16[256,256]{1,0:T(8,128)(2,1)S(1)}, u32[]{:S(2)}, u32[]{:S(2)}) collective-permute-start(bf16[256,256]{1,0:T(8,128)(2,1)S(1)} %shard_map.123.refs_0_), channel_id=1, source_target_pairs={{0,4},{2,6},{4,8},{6,10},{8,12},{10,14},{12,0},{14,2},{1,5},{3,7},... | collective-permute-start | bytes 393224 | tf_op jit(solution)/shard_map/ppermute | solution.py:50
  19.1 8.9 %collective-permute-start.3 = (bf16[256,256]{1,0:T(8,128)(2,1)S(1)}, bf16[256,256]{1,0:T(8,128)(2,1)S(1)}, u32[]{:S(2)}, u32[]{:S(2)}) collective-permute-start(bf16[256,256]{1,0:T(8,128)(2,1)S(1)} %collective-permute-done.2.refs_3_), channel_id=1, source_target_pairs={{0,2},{2,0},{4,6},{6,4},{8,10},{10,8},{12,14},{14,12},{1,3},{3,1},... | collective-permute-start | bytes 393224 | tf_op jit(solution)/shard_map/ppermute | solution.py:50
  19.7 8.3 %collective-permute-start.1 = (bf16[256,256]{1,0:T(8,128)(2,1)S(1)}, bf16[256,256]{1,0:T(8,128)(2,1)S(1)}, u32[]{:S(2)}, u32[]{:S(2)}) collective-permute-start(bf16[256,256]{1,0:T(8,128)(2,1)S(1)} %shard_map.123.refs_0_), channel_id=1, source_target_pairs={{0,6},{2,4},{4,10},{6,8},{8,14},{10,12},{12,2},{14,0},{1,7},{3,5},... | collective-permute-start | bytes 393224 | tf_op jit(solution)/shard_map/ppermute | solution.py:50
  19.7 9.7 %collective-permute-start.4 = (bf16[256,256]{1,0:T(8,128)(2,1)S(1)}, bf16[256,256]{1,0:T(8,128)(2,1)S(1)}, u32[]{:S(2)}, u32[]{:S(2)}) collective-permute-start(bf16[256,256]{1,0:T(8,128)(2,1)S(1)} %collective-permute-done.refs_2_), channel_id=1, source_target_pairs={{0,2},{2,0},{4,6},{6,4},{8,10},{10,8},{12,14},{14,12},{1,3},{3,1},... | collective-permute-start | bytes 393224 | tf_op jit(solution)/shard_map/ppermute | solution.py:50
  22.9 0.7 %copy-start.3 = (s32[2,2]{1,0:T(2,128)S(1)}, s32[2,2]{1,0:T(2,128)}, u32[]{:S(2)}) copy-start(s32[2,2]{1,0:T(2,128)} %near_ref.11) | copy-start | bytes 52
  30.4 1.6 %copy-start.1 = (f32[256,256]{1,0:T(8,128)S(1)}, f32[256,256]{1,0:T(8,128)}, u32[]{:S(2)}) copy-start(f32[256,256]{1,0:T(8,128)} %tau.3) | copy-start | bytes 786436
  30.4 1.6 %collective-permute-start.7 = (bf16[2,256,256]{2,1,0:T(8,128)(2,1)S(1)}, bf16[2,256,256]{2,1,0:T(8,128)(2,1)S(1)}, u32[]{:S(2)}, u32[]{:S(2)}) collective-permute-start(bf16[2,256,256]{2,1,0:T(8,128)(2,1)S(1)} %shard_map.126), channel_id=1, source_target_pairs={{0,1},{1,0},{2,3},{3,2},{4,5},{5,4},{6,7},{7,6},{8,9},{9,8},{10,11... | collective-permute-start | bytes 786440 | tf_op jit(solution)/shard_map/ppermute | solution.py:383
  33.6 5.7 %collective-permute-start.13 = (bf16[256,256]{1,0:T(8,128)(2,1)S(1)}, bf16[256,256]{1,0:T(8,128)(2,1)S(1)}, u32[]{:S(2)}, u32[]{:S(2)}) collective-permute-start(bf16[256,256]{1,0:T(8,128)(2,1)S(1)} %get-tuple-element.25.refs_0_), channel_id=1, source_target_pairs={{0,2},{2,0},{4,6},{6,4},{8,10},{10,8},{12,14},{14,12},{1,3},{3,1},... | collective-permute-start | bytes 393224 | tf_op jit(solution)/shard_map/ppermute | solution.py:50
  34.1 5.8 %collective-permute-start.8 = (bf16[256,256]{1,0:T(8,128)(2,1)S(1)}, bf16[256,256]{1,0:T(8,128)(2,1)S(1)}, u32[]{:S(2)}, u32[]{:S(2)}) collective-permute-start(bf16[256,256]{1,0:T(8,128)(2,1)S(1)} %get-tuple-element.25.refs_0_), channel_id=1, source_target_pairs={{0,12},{2,14},{4,0},{6,2},{8,4},{10,6},{12,8},{14,10},{1,13},{3,15... | collective-permute-start | bytes 393224 | tf_op jit(solution)/shard_map/ppermute | solution.py:50
  35.6 11.5 %collective-permute-start.10 = (bf16[256,256]{1,0:T(8,128)(2,1)S(1)}, bf16[256,256]{1,0:T(8,128)(2,1)S(1)}, u32[]{:S(2)}, u32[]{:S(2)}) collective-permute-start(bf16[256,256]{1,0:T(8,128)(2,1)S(1)} %get-tuple-element.25.refs_0_), channel_id=1, source_target_pairs={{0,8},{2,10},{4,12},{6,14},{8,0},{10,2},{12,4},{14,6},{1,9},{3,11}... | collective-permute-start | bytes 393224 | tf_op jit(solution)/shard_map/ppermute | solution.py:50
  39.2 9.9 %collective-permute-start.14 = (bf16[256,256]{1,0:T(8,128)(2,1)S(1)}, bf16[256,256]{1,0:T(8,128)(2,1)S(1)}, u32[]{:S(2)}, u32[]{:S(2)}) collective-permute-start(bf16[256,256]{1,0:T(8,128)(2,1)S(1)} %get-tuple-element.25.refs_0_), channel_id=1, source_target_pairs={{0,4},{2,6},{4,8},{6,10},{8,12},{10,14},{12,0},{14,2},{1,5},{3,7},... | collective-permute-start | bytes 393224 | tf_op jit(solution)/shard_map/ppermute | solution.py:50
  47.1 9.1 %collective-permute-start.11 = (bf16[256,256]{1,0:T(8,128)(2,1)S(1)}, bf16[256,256]{1,0:T(8,128)(2,1)S(1)}, u32[]{:S(2)}, u32[]{:S(2)}) collective-permute-start(bf16[256,256]{1,0:T(8,128)(2,1)S(1)} %collective-permute-done.10.refs_3_), channel_id=1, source_target_pairs={{0,2},{2,0},{4,6},{6,4},{8,10},{10,8},{12,14},{14,12},{1,3},{3,1},... | collective-permute-start | bytes 393224 | tf_op jit(solution)/shard_map/ppermute | solution.py:50
  48.2 8.0 %collective-permute-start.9 = (bf16[256,256]{1,0:T(8,128)(2,1)S(1)}, bf16[256,256]{1,0:T(8,128)(2,1)S(1)}, u32[]{:S(2)}, u32[]{:S(2)}) collective-permute-start(bf16[256,256]{1,0:T(8,128)(2,1)S(1)} %get-tuple-element.25.refs_0_), channel_id=1, source_target_pairs={{0,6},{2,4},{4,10},{6,8},{8,14},{10,12},{12,2},{14,0},{1,7},{3,5},... | collective-permute-start | bytes 393224 | tf_op jit(solution)/shard_map/ppermute | solution.py:50
  48.2 9.4 %collective-permute-start.12 = (bf16[256,256]{1,0:T(8,128)(2,1)S(1)}, bf16[256,256]{1,0:T(8,128)(2,1)S(1)}, u32[]{:S(2)}, u32[]{:S(2)}) collective-permute-start(bf16[256,256]{1,0:T(8,128)(2,1)S(1)} %collective-permute-done.8.refs_2_), channel_id=1, source_target_pairs={{0,2},{2,0},{4,6},{6,4},{8,10},{10,8},{12,14},{14,12},{1,3},{3,1},... | collective-permute-start | bytes 393224 | tf_op jit(solution)/shard_map/ppermute | solution.py:50
  58.7 1.6 %copy-start.2 = (f32[256,256]{1,0:T(8,128)S(1)}, f32[256,256]{1,0:T(8,128)}, u32[]{:S(2)}) copy-start(f32[256,256]{1,0:T(8,128)} %state.1) | copy-start | bytes 786436
  58.7 1.6 %collective-permute-start.15 = (bf16[2,256,256]{2,1,0:T(8,128)(2,1)S(1)}, bf16[2,256,256]{2,1,0:T(8,128)(2,1)S(1)}, u32[]{:S(2)}, u32[]{:S(2)}) collective-permute-start(bf16[2,256,256]{2,1,0:T(8,128)(2,1)S(1)} %shard_map.130), channel_id=1, source_target_pairs={{0,1},{1,0},{2,3},{3,2},{4,5},{5,4},{6,7},{7,6},{8,9},{9,8},{10,11... | collective-permute-start | bytes 786440 | tf_op jit(solution)/shard_map/ppermute | solution.py:383

commit v6 on v4

--- a/solution.py
+++ b/solution.py
@@ -9,7 +9,7 @@
 
 NEWTON = 2
 DIRECT_LIMIT = 16
-LATE = 4
+TILE = 128
 
 damping = 0.5
 sigma_floor = 0.5
@@ -18,12 +18,15 @@
 
 def arrivals(count, direct):
     if not direct:
-        return list(range(count))
+        cuts = [0, max(count - 4, 1), max(count - 2, 1), count]
+        groups = [list(range(first, last)) for first, last in zip(cuts, cuts[1:])]
+        return [group for group in groups if group]
     length = count // 2
-    shifts = list(range(length - 1, 0, -1))
-    early = [(0, 0), (0, 1)] + [(shift, 0) for shift in shifts[:-1]]
-    late = [(shift, 0) for shift in shifts[-1:]] + [(shift, 1) for shift in shifts[-1:]]
-    return early + late + [(shift, 1) for shift in shifts[:-1]]
+    split = length // 2
+    whole = [shift for shift in range(1, length) if shift != split]
+    first = [(0, 0), (0, 1)] + [(shift, 0) for shift in whole]
+    passed = [(shift, 1) for shift in whole]
+    return [group for group in (first, passed, [(split, 0), (split, 1)]) if group]
 
 
 def row_met(spot, row, count):
@@ -34,8 +37,9 @@
     return lax.rem(z - shift + count // 2, count // 2) * 2 + (1 - y if other else y)
 
 
-def gather_direct(block, count):
+def gather_direct(block, top, low, count):
     length = count // 2
+    split = length // 2
 
     def along(shift, other, data):
         hops = [
@@ -45,15 +49,15 @@
         ]
         return lax.ppermute(data, "row", hops)
 
-    shifts = list(range(length - 1, 0, -1))
-    far, last = {}, []
+    whole = [along(shift, 0, block) for shift in range(1, length) if shift != split]
+    split_top = along(split, 0, top)
     across = along(0, 1, block)
-    for shift in shifts[:-1]:
-        far[shift] = along(shift, 0, block)
-    if shifts:
-        last = [along(shifts[-1], 0, block), along(shifts[-1], 1, block)]
-    passed = [along(0, 1, far[shift]) for shift in shifts[:-1]]
-    return [block, across, *far.values(), *last, *passed]
+    split_low, split_far = along(split, 0, low), along(split, 1, low)
+    passed = [along(0, 1, data) for data in whole]
+    far_top = along(0, 1, split_top)
+    groups = [[(block,), (across,)] + [(data,) for data in whole]]
+    groups += [[(data,) for data in passed]] if passed else []
+    return groups + [[(split_top, split_low), (far_top, split_far)]]
 
 
 PIECES = 4
@@ -64,7 +68,21 @@
     return [pl.ds(at * tall, tall) for at in range(PIECES)]
 
 
-def narrow_kernel(wide_ref, narrow_ref, held, sem):
+def store_half(outs, rows, part, value):
+    whole, top, low = outs
+    whole[rows, part] = value
+    half = top.shape[0]
+
+    @pl.when(rows.start < half)
+    def _():
+        top[rows, part] = value
+
+    @pl.when(rows.start >= half)
+    def _():
+        low[pl.ds(pl.multiple_of(rows.start - half, 16), rows.size), part] = value
+
+
+def narrow_kernel(wide_ref, whole, top, low, held, sem):
     copies = [
         pltpu.make_async_copy(wide_ref.at[part], held.at[part], sem.at[at])
         for at, part in enumerate(row_pieces(held.shape[0]))
@@ -73,10 +91,10 @@
         copy.start()
     for copy, part in zip(copies, row_pieces(held.shape[0])):
         copy.wait()
-        narrow_ref[part, :] = held[part, :].astype(narrow_ref.dtype)
-
-
-def prepare_kernel(spots, row_ref, *refs):
+        store_half((whole, top, low), part, slice(None), held[part, :].astype(whole.dtype))
+
+
+def prepare_kernel(groups, row_ref, *refs):
     far, (v_out, u_out, coef_out, weight_out, decay_out), near, sem = refs[:7], refs[7:12], refs[12:19], refs[19]
     copies = [
         pltpu.make_async_copy(source, held, sem.at[at])
@@ -89,19 +107,23 @@
     rank_ref, v_ref, u_ref, sigma_ref, a_ref, b_ref, state_ref = near
     kinds, rows, count, rank_count, size = u_ref.shape
     row = row_ref[0]
-    met = [row_met(spot, row, count) for spot in spots]
+    met = [row_met(spot, row, count) for group in groups for spot in group]
     for at, q in enumerate(met):
         for p in range(rows):
             inside = lax.broadcasted_iota(jnp.int32, (rank_count, size), 0) < rank_ref[p, q]
             v_out[at, p] = jnp.where(inside, v_ref[p, q].astype(jnp.float32), 0.0).astype(v_out.dtype)
     for p in range(rows):
         for kind in range(kinds):
-            for first in range(0, count, 4):
-                group = [u_ref[kind, p, q] for q in met[first : first + 4]]
+            first = start = 0
+            for spots in groups:
+                group = [u_ref[kind, p, q] for q in met[first : first + len(spots)]]
+                spare = -len(group) * rank_count % TILE
+                if spare:
+                    group.append(jnp.zeros((spare, size), u_ref.dtype))
                 turned = jnp.concatenate(group, axis=0).astype(jnp.float32).T
-                u_out[p, kind * size : (kind + 1) * size, first * rank_count : (first + len(group)) * rank_count] = (
-                    turned.astype(u_out.dtype)
-                )
+                stop = start + turned.shape[1]
+                u_out[p, kind * size : (kind + 1) * size, start:stop] = turned.astype(u_out.dtype)
+                first, start = first + len(spots), stop
     lanes = coef_out.shape[2]
     for at, ref in enumerate((sigma_ref, a_ref, b_ref)):
         coef_out[at] = jnp.broadcast_to(ref[...], (lanes, size)).T
@@ -112,9 +134,9 @@
         decay_out[:, part] = jnp.exp(-state / coef_out[2])
 
 
-def sums_kernel(spots, first, pick, before, row_ref, col_ref, near_ref, v_ref, u_ref, d_ref, *refs):
-    blocks = refs[: len(spots)]
-    refs = refs[len(spots) :]
+def sums_kernel(spots, pieces, first, start, pick, before, row_ref, col_ref, near_ref, v_ref, u_ref, d_ref, *refs):
+    blocks = [refs[sum(pieces[:at]) : sum(pieces[: at + 1])] for at in range(len(pieces))]
+    refs = refs[sum(pieces) :]
     if before:
         sums_ref, refs = refs[0], refs[1:]
     out_ref, x_all, proj, total = refs
@@ -123,19 +145,21 @@
     row, col = row_ref[0], col_ref[0]
     met = [row_met(spot, row, count) for spot in spots]
     chosen = list(range(rows)) if pick is None else [col if pick == 0 else 1 - col]
-    for at, block in enumerate(blocks):
-        x_all[at] = block[...]
-    for at, block in enumerate(blocks):
+    for at, parts in enumerate(blocks):
+        tall = size // len(parts)
+        for place, part in enumerate(parts):
+            x_all[at, place * tall : (place + 1) * tall, :] = part[...]
+    for at in range(len(blocks)):
         if pick is None:
             weights = v_ref[first + at].reshape(rows * rank_count, size)
         else:
             weights = v_ref[first + at, chosen[0]]
-        part = jnp.dot(weights, block[...], preferred_element_type=jnp.float32).astype(proj.dtype)
+        part = jnp.dot(weights, x_all[at], preferred_element_type=jnp.float32).astype(proj.dtype)
         for place in range(len(chosen)):
             proj[place, at * rank_count : (at + 1) * rank_count, :] = part[
                 place * rank_count : (place + 1) * rank_count
             ]
-    lanes = slice(first * rank_count, (first + len(blocks)) * rank_count)
+    lanes = slice(start, start + len(blocks) * rank_count)
     for place, p in enumerate(chosen):
         gained = jnp.dot(u_ref[p, :, lanes], proj[place], preferred_element_type=jnp.float32)
         for kind in range(kinds):
@@ -206,7 +230,7 @@
             work(rows, slice(first, first + lanes))
 
 
-def section_one_kernel(own, other, weight, decay, tau, coef, stress, normal, rate, change, rate_half):
+def section_one_kernel(own, other, weight, decay, tau, coef, stress, normal, rate, change, *rate_half):
     size, members = tau.shape
 
     def work(rows, part):
@@ -226,7 +250,7 @@
         )
         rate[rows, part] = first
         change[rows, part] = second
-        rate_half[rows, part] = first.astype(rate_half.dtype)
+        store_half(rate_half, rows, part, first.astype(rate_half[0].dtype))
 
     over_pieces(0, size, members, coef.shape[2], work)
 
@@ -297,9 +321,11 @@
     count = lax.axis_size("row")
     size, members = slip_deficit.shape
     kinds, rows, _, rank_count, _ = u_basis.shape
-    direct = count % 2 == 0 and count <= DIRECT_LIMIT
-    spots = arrivals(count, direct)
-    early = max(count - LATE, 0)
+    direct = count % 2 == 0 and 4 <= count <= DIRECT_LIMIT
+    groups = arrivals(count, direct)
+    firsts = [sum(len(group) for group in groups[:at]) for at in range(len(groups))]
+    tiles = [-(-len(group) * rank_count // TILE) * TILE for group in groups]
+    starts = [sum(tiles[:at]) for at in range(len(groups))]
     room = 16 if direct else 40
     lanes = min(members, 128)
     narrow, wide = jnp.bfloat16, jnp.float32
@@ -311,10 +337,10 @@
 
     full = shaped(size, members)
     v_met, u_met, coef, weight, decay = on_core(
-        functools.partial(prepare_kernel, spots),
+        functools.partial(prepare_kernel, groups),
         (
             shaped(count, rows, rank_count, size, kind=narrow),
-            shaped(rows, kinds * size, count * rank_count, kind=narrow),
+            shaped(rows, kinds * size, sum(tiles), kind=narrow),
             shaped(3, size, lanes),
             full,
             full,
@@ -341,16 +367,23 @@
         ),
     )
 
-    def add(blocks, first, pick, before, kind):
+    def add(blocks, at, pick, before, kind):
         held = rows if pick is None else 1
         lead = (rows, kinds) if pick is None else (kinds,)
+        pieces = tuple(len(parts) for parts in blocks)
         return on_core(
             functools.partial(
-                sums_kernel, spots[first : first + len(blocks)], first, pick, before is not None
+                sums_kernel, groups[at], pieces, firsts[at], starts[at], pick, before is not None
             ),
             shaped(*lead, size, members, kind=kind),
             (row, col, near_index),
-            (v_met, u_met, dense_blocks, *blocks, *(() if before is None else (before,))),
+            (
+                v_met,
+                u_met,
+                dense_blocks,
+                *[part for parts in blocks for part in parts],
+                *(() if before is None else (before,)),
+            ),
             (
                 pltpu.VMEM((len(blocks), size, members), narrow),
                 pltpu.VMEM((held, len(blocks) * rank_count, members), narrow),
@@ -360,33 +393,40 @@
             room,
         )
 
-    def lattice(field_half):
+    def lattice(block, top, low):
         if direct:
-            blocks = gather_direct(field_half, count)
+            found = gather_direct(block, top, low, count)
         else:
-            whole = lax.all_gather(field_half, "row", axis=0)
-            blocks = [whole[r] for r in range(count)]
-        sums = add(blocks[:early], 0, None, None, wide) if early else None
-        other = lax.ppermute(add(blocks[early:], early, 1, sums, narrow), "col", swap)
-        return add(blocks[early:], early, 0, sums, wide), other
-
+            whole = lax.all_gather(block, "row", axis=0)
+            found = [[(whole[r],) for r in group] for group in groups]
+        sums = None
+        for at in range(len(groups) - 1):
+            sums = add(found[at], at, None, sums, wide)
+        other = lax.ppermute(add(found[-1], len(groups) - 1, 1, sums, narrow), "col", swap)
+        return add(found[-1], len(groups) - 1, 0, sums, wide), other
+
+    halves = (
+        shaped(size, members, kind=narrow),
+        shaped(size // 2, members, kind=narrow),
+        shaped(size // 2, members, kind=narrow),
+    )
     slip_half = on_core(
         narrow_kernel,
-        shaped(size, members, kind=narrow),
+        halves,
         (),
         (),
         (pltpu.VMEM((size, members), wide), pltpu.SemaphoreType.DMA((PIECES,))),
         far=(slip_deficit,),
     )
-    own, other = lattice(slip_half)
-    stress, normal, rate, change, rate_half = on_core(
+    own, other = lattice(*slip_half)
+    stress, normal, rate, change, *rate_half = on_core(
         section_one_kernel,
-        (full, full, full, full, shaped(size, members, kind=narrow)),
+        (full, full, full, full, *halves),
         (),
         (own, other, weight, decay, tau_load, coef),
         flops=200 * size * members,
     )
-    own, other = lattice(rate_half)
+    own, other = lattice(*rate_half)
     return on_core(
         section_two_kernel,
         (full, full),

time: 52.7 us -> 64.1 us (1.22)
  the two profiles are of different devices: /device:TPU:0 before, /device:TPU:9 now
where the time goes in v6:
time: 64.1 us; the launch traced here: 63.9 us
  starting transfers between devices  32.8 us (51%)
  Pallas kernels  18.3 us (29%)
  waiting for transfers between devices  11.3 us (18%)
  between operations  0.86 us (1%)
  local copies, waits for them, and re-layouts  0.68 us (1%)
    ppermute x18, starting transfers between devices, along(): return lax.ppermute(data, 'row', hops)  22.3 us
    pallas_call x12, Pallas kernels, on_core(): pl.pallas_call(kernel, out_shape=outs, in_specs=[smem] * len(scalars) + [...  18.3 us
    ppermute x18, waiting for transfers between devices, along(): return lax.ppermute(data, 'row', hops)  10.9 us
    ppermute x2, starting transfers between devices, lattice(): lax.ppermute(add(found[-1], len(groups) - 1, 1, sums, narrow), 'col', swap)  10.5 us
  transfers between devices with their start and end apart: 20, of which 8 were waited for; matrix products, arithmetic and copies ran while one was open for 0% of the time, Pallas kernels for 15%

profile of v6, /device:TPU:9, one launch (start us, length us, event | category | flops | bytes accessed | tf_op | source)
XLA Modules:
  0.0 63.9 jit_solution(13913129548380372655)
XLA Ops:
  0.6 1.1 %shard_map.123 = (bf16[256,256]{1,0:T(8,128)(2,1)S(1)}, bf16[128,256]{1,0:T(8,128)(2,1)S(1)}, bf16[128,256]{1,0:T(8,128)(2,1)S(1)}) custom-call(f32[256,256]{1,0:T(8,128)} %wide_ref.1), custom_call_target="tpu_custom_call" | custom-call | bytes 262144 | tf_op jit(solution)/shard_map/pallas_call | solution.py:295
  1.7 1.3 %collective-permute-start.4 = (bf16[256,256]{1,0:T(8,128)(2,1)S(1)}, bf16[256,256]{1,0:T(8,128)(2,1)S(1)}, u32[]{:S(2)}, u32[]{:S(2)}) collective-permute-start(bf16[256,256]{1,0:T(8,128)(2,1)S(1)} %get-tuple-element.21.refs_0_), channel_id=1, source_target_pairs={{0,4},{2,6},{4,8},{6,10},{8,12},{10,14},{12,0},{14,2},{1,5},{3,7},... | collective-permute-start | bytes 393224 | tf_op jit(solution)/shard_map/ppermute | solution.py:50
  3.1 0.2 collective-permute-start.6
  3.2 1.2 %collective-permute-start.8 = (bf16[256,256]{1,0:T(8,128)(2,1)S(1)}, bf16[256,256]{1,0:T(8,128)(2,1)S(1)}, u32[]{:S(2)}, u32[]{:S(2)}) collective-permute-start(bf16[256,256]{1,0:T(8,128)(2,1)S(1)} %get-tuple-element.21.refs_0_), channel_id=1, source_target_pairs={{0,2},{2,0},{4,6},{6,4},{8,10},{10,8},{12,14},{14,12},{1,3},{3,1},... | collective-permute-start | bytes 393224 | tf_op jit(solution)/shard_map/ppermute | solution.py:50
  4.5 1.7 %collective-permute-done.4.refs_2_ = bf16[256,256]{1,0:T(8,128)(2,1)S(1)} collective-permute-done((bf16[256,256]{1,0:T(8,128)(2,1)S(1)}, bf16[256,256]{1,0:T(8,128)(2,1)S(1)}, u32[]{:S(2)}, u32[]{:S(2)}) %collective-permute-start.4) | collective-permute-done | bytes 131104 | tf_op jit(solution)/shard_map/ppermute | solution.py:50
  6.1 1.2 %collective-permute-start.5 = (bf16[256,256]{1,0:T(8,128)(2,1)S(1)}, bf16[256,256]{1,0:T(8,128)(2,1)S(1)}, u32[]{:S(2)}, u32[]{:S(2)}) collective-permute-start(bf16[256,256]{1,0:T(8,128)(2,1)S(1)} %collective-permute-done.4.refs_2_), channel_id=1, source_target_pairs={{0,2},{2,0},{4,6},{6,4},{8,10},{10,8},{12,14},{14,12},{1,3},{3,1},... | collective-permute-start | bytes 393224 | tf_op jit(solution)/shard_map/ppermute | solution.py:50
  7.4 3.5 %collective-permute-done.6.refs_3_ = bf16[256,256]{1,0:T(8,128)(2,1)S(1)} collective-permute-done((bf16[256,256]{1,0:T(8,128)(2,1)S(1)}, bf16[256,256]{1,0:T(8,128)(2,1)S(1)}, u32[]{:S(2)}, u32[]{:S(2)}) %collective-permute-start.6) | collective-permute-done | bytes 131104 | tf_op jit(solution)/shard_map/ppermute | solution.py:50
  10.8 1.2 %collective-permute-start.7 = (bf16[256,256]{1,0:T(8,128)(2,1)S(1)}, bf16[256,256]{1,0:T(8,128)(2,1)S(1)}, u32[]{:S(2)}, u32[]{:S(2)}) collective-permute-start(bf16[256,256]{1,0:T(8,128)(2,1)S(1)} %collective-permute-done.6.refs_3_), channel_id=1, source_target_pairs={{0,2},{2,0},{4,6},{6,4},{8,10},{10,8},{12,14},{14,12},{1,3},{3,1},... | collective-permute-start | bytes 393224 | tf_op jit(solution)/shard_map/ppermute | solution.py:50
  12.1 0.6 collective-permute-start
  12.7 1.8 %collective-permute-start.1 = (bf16[128,256]{1,0:T(8,128)(2,1)S(1)}, bf16[128,256]{1,0:T(8,128)(2,1)S(1)}, u32[]{:S(2)}, u32[]{:S(2)}) collective-permute-start(bf16[128,256]{1,0:T(8,128)(2,1)S(1)} %get-tuple-element.20), channel_id=1, source_target_pairs={{0,8},{2,10},{4,12},{6,14},{8,0},{10,2},{12,4},{14,6},{1,9},{3,11}... | collective-permute-start | bytes 196616 | tf_op jit(solution)/shard_map/ppermute | solution.py:50
  14.4 1.7 %collective-permute-done.refs_0_ = bf16[128,256]{1,0:T(8,128)(2,1)S(1)} collective-permute-done((bf16[128,256]{1,0:T(8,128)(2,1)S(1)}, bf16[128,256]{1,0:T(8,128)(2,1)S(1)}, u32[]{:S(2)}, u32[]{:S(2)}) %collective-permute-start) | collective-permute-done | bytes 65568 | tf_op jit(solution)/shard_map/ppermute | solution.py:50
  16.2 1.0 %collective-permute-start.3 = (bf16[128,256]{1,0:T(8,128)(2,1)S(1)}, bf16[128,256]{1,0:T(8,128)(2,1)S(1)}, u32[]{:S(2)}, u32[]{:S(2)}) collective-permute-start(bf16[128,256]{1,0:T(8,128)(2,1)S(1)} %get-tuple-element.20), channel_id=1, source_target_pairs={{0,10},{2,8},{4,14},{6,12},{8,2},{10,0},{12,6},{14,4},{1,11},{3,9}... | collective-permute-start | bytes 196616 | tf_op jit(solution)/shard_map/ppermute | solution.py:50
  17.2 1.0 %collective-permute-start.2 = (bf16[128,256]{1,0:T(8,128)(2,1)S(1)}, bf16[128,256]{1,0:T(8,128)(2,1)S(1)}, u32[]{:S(2)}, u32[]{:S(2)}) collective-permute-start(bf16[128,256]{1,0:T(8,128)(2,1)S(1)} %collective-permute-done.refs_0_), channel_id=1, source_target_pairs={{0,2},{2,0},{4,6},{6,4},{8,10},{10,8},{12,14},{14,12},{1,3},{3,1},... | collective-permute-start | bytes 196616 | tf_op jit(solution)/shard_map/ppermute | solution.py:50
  18.2 1.7 %shard_map.122 = (bf16[8,2,32,256]{3,2,1,0:T(8,128)(2,1)S(1)}, bf16[2,512,384]{2,1,0:T(8,128)(2,1)S(1)}, f32[3,256,128]{2,1,0:T(8,128)S(1)}, f32[256,256]{1,0:T(8,128)S(1)}, f32[256,256]{1,0:T(8,128)S(1)}) custom-call(s32[1]{0:T(128)} %bitcast.row_ref, s32[2,8]{1,0:T(2,128)} %refs_0_.1, bf16[2,8,32,256]{3,2,1,0:T(8,128)(2,1)} %refs_1_.1, ...), custom_call_target="tpu_custom_call" | custom-call | bytes 1051712 | tf_op jit(solution)/shard_map/pallas_call | solution.py:295
  19.9 0.0 copy-start.3
  20.0 0.7 %copy-done.3 = s32[2,2]{1,0:T(2,128)S(1)} copy-done((s32[2,2]{1,0:T(2,128)S(1)}, s32[2,2]{1,0:T(2,128)}, u32[]{:S(2)}) %copy-start.3) | copy-done | bytes 40
  20.6 1.8 %shard_map.124.refs_2_ = f32[2,2,256,256]{3,2,1,0:T(8,128)S(1)} custom-call(s32[1]{0:T(128)} %bitcast.row_ref, s32[1]{0:T(128)} %bitcast.1.col_ref, s32[2,2]{1,0:T(2,128)S(1)} %copy-done.3, bf16[8,2,32,256]{3,2,1,0:T(8,128)(2,1)S(1)} %get-tuple-element.17.v_ref, bf16[2,512,384]{2,1,0:T(8,128)(2,1)S(1)} %get-tuple-element.18.u_ref, ...), custom_call_target="tpu_custom_call" | custom-call | flops 100663296 | bytes 2621440 | tf_op jit(solution)/shard_map/pallas_call | solution.py:295
  22.4 0.0 collective-permute-done.7.refs_1_
  22.4 1.3 %shard_map.125.refs_4_ = f32[2,2,256,256]{3,2,1,0:T(8,128)S(1)} custom-call(s32[1]{0:T(128)} %bitcast.row_ref, s32[1]{0:T(128)} %bitcast.1.col_ref, s32[2,2]{1,0:T(2,128)S(1)} %copy-done.3, bf16[8,2,32,256]{3,2,1,0:T(8,128)(2,1)S(1)} %get-tuple-element.17.v_ref, bf16[2,512,384]{2,1,0:T(8,128)(2,1)S(1)} %get-tuple-element.18.u_ref, ...), custom_call_target="tpu_custom_call" | custom-call | flops 50331648 | bytes 3407872 | tf_op jit(solution)/shard_map/pallas_call | solution.py:295
  23.8 0.0 collective-permute-done.3.refs_3_
  23.8 0.0 collective-permute-done.2.refs_2_
  23.8 0.9 %shard_map.127 = bf16[2,256,256]{2,1,0:T(8,128)(2,1)S(1)} custom-call(s32[1]{0:T(128)} %bitcast.row_ref, s32[1]{0:T(128)} %bitcast.1.col_ref, s32[2,2]{1,0:T(2,128)S(1)} %copy-done.3, bf16[8,2,32,256]{3,2,1,0:T(8,128)(2,1)S(1)} %get-tuple-element.17.v_ref, bf16[2,512,384]{2,1,0:T(8,128)(2,1)S(1)} %get-tuple-element.18.u_ref, ...), custom_call_target="tpu_custom_call" | custom-call | flops 25165824 | bytes 3407872 | tf_op jit(solution)/shard_map/pallas_call | solution.py:295
  24.7 0.0 copy-start.1
  24.7 6.1 %collective-permute-start.9 = (bf16[2,256,256]{2,1,0:T(8,128)(2,1)S(1)}, bf16[2,256,256]{2,1,0:T(8,128)(2,1)S(1)}, u32[]{:S(2)}, u32[]{:S(2)}) collective-permute-start(bf16[2,256,256]{2,1,0:T(8,128)(2,1)S(1)} %shard_map.127), channel_id=1, source_target_pairs={{0,1},{1,0},{2,3},{3,2},{4,5},{5,4},{6,7},{7,6},{8,9},{9,8},{10,11... | collective-permute-start | bytes 786440 | tf_op jit(solution)/shard_map/ppermute | solution.py:405
  30.8 0.9 %shard_map.126.own = f32[2,256,256]{2,1,0:T(8,128)S(1)} custom-call(s32[1]{0:T(128)} %bitcast.row_ref, s32[1]{0:T(128)} %bitcast.1.col_ref, s32[2,2]{1,0:T(2,128)S(1)} %copy-done.3, bf16[8,2,32,256]{3,2,1,0:T(8,128)(2,1)S(1)} %get-tuple-element.17.v_ref, bf16[2,512,384]{2,1,0:T(8,128)(2,1)S(1)} %get-tuple-element.18.u_ref, ...), custom_call_target="tpu_custom_call" | custom-call | flops 25165824 | bytes 3407872 | tf_op jit(solution)/shard_map/pallas_call | solution.py:295
  31.8 0.2 collective-permute-done.9.other
  32.0 3.0 %shard_map.128 = (f32[256,256]{1,0:T(8,128)S(1)}, f32[256,256]{1,0:T(8,128)S(1)}, f32[256,256]{1,0:T(8,128)S(1)}, f32[256,256]{1,0:T(8,128)S(1)}, bf16[256,256]{...) custom-call(f32[2,256,256]{2,1,0:T(8,128)S(1)} %shard_map.126.own, ...), custom_call_target="tpu_custom_call" | custom-call | flops 13107200 | bytes 1966080 | tf_op jit(solution)/shard_map/pallas_call | solution.py:295
  35.0 0.1 collective-permute-start.14
  35.1 1.5 %collective-permute-start.16 = (bf16[256,256]{1,0:T(8,128)(2,1)S(1)}, bf16[256,256]{1,0:T(8,128)(2,1)S(1)}, u32[]{:S(2)}, u32[]{:S(2)}) collective-permute-start(bf16[256,256]{1,0:T(8,128)(2,1)S(1)} %get-tuple-element.27.refs_0_), channel_id=1, source_target_pairs={{0,12},{2,14},{4,0},{6,2},{8,4},{10,6},{12,8},{14,10},{1,13},{3,15... | collective-permute-start | bytes 393224 | tf_op jit(solution)/shard_map/ppermute | solution.py:50
  36.5 1.4 %collective-permute-start.18 = (bf16[256,256]{1,0:T(8,128)(2,1)S(1)}, bf16[256,256]{1,0:T(8,128)(2,1)S(1)}, u32[]{:S(2)}, u32[]{:S(2)}) collective-permute-start(bf16[256,256]{1,0:T(8,128)(2,1)S(1)} %get-tuple-element.27.refs_0_), channel_id=1, source_target_pairs={{0,2},{2,0},{4,6},{6,4},{8,10},{10,8},{12,14},{14,12},{1,3},{3,1},... | collective-permute-start | bytes 393224 | tf_op jit(solution)/shard_map/ppermute | solution.py:50
  37.9 1.8 %collective-permute-done.14.refs_2_ = bf16[256,256]{1,0:T(8,128)(2,1)S(1)} collective-permute-done((bf16[256,256]{1,0:T(8,128)(2,1)S(1)}, bf16[256,256]{1,0:T(8,128)(2,1)S(1)}, u32[]{:S(2)}, u32[]{:S(2)}) %collective-permute-start.14) | collective-permute-done | bytes 131104 | tf_op jit(solution)/shard_map/ppermute | solution.py:50
  39.8 1.5 %collective-permute-start.15 = (bf16[256,256]{1,0:T(8,128)(2,1)S(1)}, bf16[256,256]{1,0:T(8,128)(2,1)S(1)}, u32[]{:S(2)}, u32[]{:S(2)}) collective-permute-start(bf16[256,256]{1,0:T(8,128)(2,1)S(1)} %collective-permute-done.14.refs_2_), channel_id=1, source_target_pairs={{0,2},{2,0},{4,6},{6,4},{8,10},{10,8},{12,14},{14,12},{1,3},{3,1},... | collective-permute-start | bytes 393224 | tf_op jit(solution)/shard_map/ppermute | solution.py:50
  41.2 0.5 collective-permute-done.16.refs_3_
  41.7 0.7 %collective-permute-start.17 = (bf16[256,256]{1,0:T(8,128)(2,1)S(1)}, bf16[256,256]{1,0:T(8,128)(2,1)S(1)}, u32[]{:S(2)}, u32[]{:S(2)}) collective-permute-start(bf16[256,256]{1,0:T(8,128)(2,1)S(1)} %collective-permute-done.16.refs_3_), channel_id=1, source_target_pairs={{0,2},{2,0},{4,6},{6,4},{8,10},{10,8},{12,14},{14,12},{1,3},{3,1},... | collective-permute-start | bytes 393224 | tf_op jit(solution)/shard_map/ppermute | solution.py:50
  42.4 3.7 %collective-permute-start.10 = (bf16[128,256]{1,0:T(8,128)(2,1)S(1)}, bf16[128,256]{1,0:T(8,128)(2,1)S(1)}, u32[]{:S(2)}, u32[]{:S(2)}) collective-permute-start(bf16[128,256]{1,0:T(8,128)(2,1)S(1)} %get-tuple-element.25), channel_id=1, source_target_pairs={{0,8},{2,10},{4,12},{6,14},{8,0},{10,2},{12,4},{14,6},{1,9},{3,11}... | collective-permute-start | bytes 196616 | tf_op jit(solution)/shard_map/ppermute | solution.py:50
  46.1 0.0 collective-permute-start.11
  46.2 1.7 %collective-permute-done.10.refs_0_ = bf16[128,256]{1,0:T(8,128)(2,1)S(1)} collective-permute-done((bf16[128,256]{1,0:T(8,128)(2,1)S(1)}, bf16[128,256]{1,0:T(8,128)(2,1)S(1)}, u32[]{:S(2)}, u32[]{:S(2)}) %collective-permute-start.10) | collective-permute-done | bytes 65568 | tf_op jit(solution)/shard_map/ppermute | solution.py:50
  47.8 3.1 %collective-permute-start.13 = (bf16[128,256]{1,0:T(8,128)(2,1)S(1)}, bf16[128,256]{1,0:T(8,128)(2,1)S(1)}, u32[]{:S(2)}, u32[]{:S(2)}) collective-permute-start(bf16[128,256]{1,0:T(8,128)(2,1)S(1)} %get-tuple-element.26), channel_id=1, source_target_pairs={{0,10},{2,8},{4,14},{6,12},{8,2},{10,0},{12,6},{14,4},{1,11},{3,9}... | collective-permute-start | bytes 196616 | tf_op jit(solution)/shard_map/ppermute | solution.py:50
  50.9 0.0 collective-permute-done.18.refs_1_
  50.9 0.8 %collective-permute-start.12 = (bf16[128,256]{1,0:T(8,128)(2,1)S(1)}, bf16[128,256]{1,0:T(8,128)(2,1)S(1)}, u32[]{:S(2)}, u32[]{:S(2)}) collective-permute-start(bf16[128,256]{1,0:T(8,128)(2,1)S(1)} %collective-permute-done.10.refs_0_), channel_id=1, source_target_pairs={{0,2},{2,0},{4,6},{6,4},{8,10},{10,8},{12,14},{14,12},{1,3},{3,1},... | collective-permute-start | bytes 196616 | tf_op jit(solution)/shard_map/ppermute | solution.py:50
  51.7 1.8 %shard_map.129.refs_2_ = f32[2,2,256,256]{3,2,1,0:T(8,128)S(1)} custom-call(s32[1]{0:T(128)} %bitcast.row_ref, s32[1]{0:T(128)} %bitcast.1.col_ref, s32[2,2]{1,0:T(2,128)S(1)} %copy-done.3, bf16[8,2,32,256]{3,2,1,0:T(8,128)(2,1)S(1)} %get-tuple-element.17.v_ref, bf16[2,512,384]{2,1,0:T(8,128)(2,1)S(1)} %get-tuple-element.18.u_ref, ...), custom_call_target="tpu_custom_call" | custom-call | flops 100663296 | bytes 2621440 | tf_op jit(solution)/shard_map/pallas_call | solution.py:295
  53.5 1.3 %shard_map.130.refs_4_ = f32[2,2,256,256]{3,2,1,0:T(8,128)S(1)} custom-call(s32[1]{0:T(128)} %bitcast.row_ref, s32[1]{0:T(128)} %bitcast.1.col_ref, s32[2,2]{1,0:T(2,128)S(1)} %copy-done.3, bf16[8,2,32,256]{3,2,1,0:T(8,128)(2,1)S(1)} %get-tuple-element.17.v_ref, bf16[2,512,384]{2,1,0:T(8,128)(2,1)S(1)} %get-tuple-element.18.u_ref, ...), custom_call_target="tpu_custom_call" | custom-call | flops 50331648 | bytes 3407872 | tf_op jit(solution)/shard_map/pallas_call | solution.py:295
  54.8 0.9 %shard_map.132 = bf16[2,256,256]{2,1,0:T(8,128)(2,1)S(1)} custom-call(s32[1]{0:T(128)} %bitcast.row_ref, s32[1]{0:T(128)} %bitcast.1.col_ref, s32[2,2]{1,0:T(2,128)S(1)} %copy-done.3, bf16[8,2,32,256]{3,2,1,0:T(8,128)(2,1)S(1)} %get-tuple-element.17.v_ref, bf16[2,512,384]{2,1,0:T(8,128)(2,1)S(1)} %get-tuple-element.18.u_ref, ...), custom_call_target="tpu_custom_call" | custom-call | flops 25165824 | bytes 3407872 | tf_op jit(solution)/shard_map/pallas_call | solution.py:295
  55.8 0.0 copy-start.2
  55.8 4.4 %collective-permute-start.19 = (bf16[2,256,256]{2,1,0:T(8,128)(2,1)S(1)}, bf16[2,256,256]{2,1,0:T(8,128)(2,1)S(1)}, u32[]{:S(2)}, u32[]{:S(2)}) collective-permute-start(bf16[2,256,256]{2,1,0:T(8,128)(2,1)S(1)} %shard_map.132), channel_id=1, source_target_pairs={{0,1},{1,0},{2,3},{3,2},{4,5},{5,4},{6,7},{7,6},{8,9},{9,8},{10,11... | collective-permute-start | bytes 786440 | tf_op jit(solution)/shard_map/ppermute | solution.py:405
  60.2 0.9 %shard_map.131.own = f32[2,256,256]{2,1,0:T(8,128)S(1)} custom-call(s32[1]{0:T(128)} %bitcast.row_ref, s32[1]{0:T(128)} %bitcast.1.col_ref, s32[2,2]{1,0:T(2,128)S(1)} %copy-done.3, bf16[8,2,32,256]{3,2,1,0:T(8,128)(2,1)S(1)} %get-tuple-element.17.v_ref, bf16[2,512,384]{2,1,0:T(8,128)(2,1)S(1)} %get-tuple-element.18.u_ref, ...), custom_call_target="tpu_custom_call" | custom-call | flops 25165824 | bytes 3407872 | tf_op jit(solution)/shard_map/pallas_call | solution.py:295
  61.1 0.2 collective-permute-done.19.other
  61.4 2.6 %shard_map.133 = (f32[256,256]{1,0:T(8,128)}, f32[256,256]{1,0:T(8,128)}) custom-call(f32[2,256,256]{2,1,0:T(8,128)S(1)} %shard_map.131.own, bf16[2,256,256]{2,1,0:T(8,128)(2,1)S(1)} %collective-permute-done.19.other, f32[256,256]{1,0:T(8,128)S(1)} %copy-done.2, f32[256,256]{1,0:T(8,128)S(1)} %copy-done.1, f32[3,256,128]{2,1,0:T(8,128)S(1)} %get-tuple-element.24.coef, ...), custom_call_target="tpu_custom_call" | custom-call | flops 13107200 | bytes 2752512 | tf_op jit(solution)/shard_map/pallas_call | solution.py:295
  (12 shorter events, 0.0 us)
Async XLA Ops:
  0.6 19.3 %copy-start = (bf16[2,2,2,256,256]{4,3,2,1,0:T(8,128)(2,1)S(1)}, bf16[2,2,2,256,256]{4,3,2,1,0:T(8,128)(2,1)}, u32[]{:S(2)}) copy-start(bf16[2,2,2,256,256]{4,3,2,1,0:T(8,128)(2,1)} %d_ref.15) | copy-start | bytes 3145732
  1.7 4.4 %collective-permute-start.4 = (bf16[256,256]{1,0:T(8,128)(2,1)S(1)}, bf16[256,256]{1,0:T(8,128)(2,1)S(1)}, u32[]{:S(2)}, u32[]{:S(2)}) collective-permute-start(bf16[256,256]{1,0:T(8,128)(2,1)S(1)} %get-tuple-element.21.refs_0_), channel_id=1, source_target_pairs={{0,4},{2,6},{4,8},{6,10},{8,12},{10,14},{12,0},{14,2},{1,5},{3,7},... | collective-permute-start | bytes 393224 | tf_op jit(solution)/shard_map/ppermute | solution.py:50
  3.1 7.8 %collective-permute-start.6 = (bf16[256,256]{1,0:T(8,128)(2,1)S(1)}, bf16[256,256]{1,0:T(8,128)(2,1)S(1)}, u32[]{:S(2)}, u32[]{:S(2)}) collective-permute-start(bf16[256,256]{1,0:T(8,128)(2,1)S(1)} %get-tuple-element.21.refs_0_), channel_id=1, source_target_pairs={{0,12},{2,14},{4,0},{6,2},{8,4},{10,6},{12,8},{14,10},{1,13},{3,15... | collective-permute-start | bytes 393224 | tf_op jit(solution)/shard_map/ppermute | solution.py:50
  3.2 14.0 %collective-permute-start.8 = (bf16[256,256]{1,0:T(8,128)(2,1)S(1)}, bf16[256,256]{1,0:T(8,128)(2,1)S(1)}, u32[]{:S(2)}, u32[]{:S(2)}) collective-permute-start(bf16[256,256]{1,0:T(8,128)(2,1)S(1)} %get-tuple-element.21.refs_0_), channel_id=1, source_target_pairs={{0,2},{2,0},{4,6},{6,4},{8,10},{10,8},{12,14},{14,12},{1,3},{3,1},... | collective-permute-start | bytes 393224 | tf_op jit(solution)/shard_map/ppermute | solution.py:50
  6.1 16.3 %collective-permute-start.5 = (bf16[256,256]{1,0:T(8,128)(2,1)S(1)}, bf16[256,256]{1,0:T(8,128)(2,1)S(1)}, u32[]{:S(2)}, u32[]{:S(2)}) collective-permute-start(bf16[256,256]{1,0:T(8,128)(2,1)S(1)} %collective-permute-done.4.refs_2_), channel_id=1, source_target_pairs={{0,2},{2,0},{4,6},{6,4},{8,10},{10,8},{12,14},{14,12},{1,3},{3,1},... | collective-permute-start | bytes 393224 | tf_op jit(solution)/shard_map/ppermute | solution.py:50
  10.8 11.6 %collective-permute-start.7 = (bf16[256,256]{1,0:T(8,128)(2,1)S(1)}, bf16[256,256]{1,0:T(8,128)(2,1)S(1)}, u32[]{:S(2)}, u32[]{:S(2)}) collective-permute-start(bf16[256,256]{1,0:T(8,128)(2,1)S(1)} %collective-permute-done.6.refs_3_), channel_id=1, source_target_pairs={{0,2},{2,0},{4,6},{6,4},{8,10},{10,8},{12,14},{14,12},{1,3},{3,1},... | collective-permute-start | bytes 393224 | tf_op jit(solution)/shard_map/ppermute | solution.py:50
  12.1 4.1 %collective-permute-start = (bf16[128,256]{1,0:T(8,128)(2,1)S(1)}, bf16[128,256]{1,0:T(8,128)(2,1)S(1)}, u32[]{:S(2)}, u32[]{:S(2)}) collective-permute-start(bf16[128,256]{1,0:T(8,128)(2,1)S(1)} %get-tuple-element.19), channel_id=1, source_target_pairs={{0,8},{2,10},{4,12},{6,14},{8,0},{10,2},{12,4},{14,6},{1,9},{3,11}... | collective-permute-start | bytes 196616 | tf_op jit(solution)/shard_map/ppermute | solution.py:50
  12.7 11.1 %collective-permute-start.1 = (bf16[128,256]{1,0:T(8,128)(2,1)S(1)}, bf16[128,256]{1,0:T(8,128)(2,1)S(1)}, u32[]{:S(2)}, u32[]{:S(2)}) collective-permute-start(bf16[128,256]{1,0:T(8,128)(2,1)S(1)} %get-tuple-element.20), channel_id=1, source_target_pairs={{0,8},{2,10},{4,12},{6,14},{8,0},{10,2},{12,4},{14,6},{1,9},{3,11}... | collective-permute-start | bytes 196616 | tf_op jit(solution)/shard_map/ppermute | solution.py:50
  16.2 7.6 %collective-permute-start.3 = (bf16[128,256]{1,0:T(8,128)(2,1)S(1)}, bf16[128,256]{1,0:T(8,128)(2,1)S(1)}, u32[]{:S(2)}, u32[]{:S(2)}) collective-permute-start(bf16[128,256]{1,0:T(8,128)(2,1)S(1)} %get-tuple-element.20), channel_id=1, source_target_pairs={{0,10},{2,8},{4,14},{6,12},{8,2},{10,0},{12,6},{14,4},{1,11},{3,9}... | collective-permute-start | bytes 196616 | tf_op jit(solution)/shard_map/ppermute | solution.py:50
  17.2 6.6 %collective-permute-start.2 = (bf16[128,256]{1,0:T(8,128)(2,1)S(1)}, bf16[128,256]{1,0:T(8,128)(2,1)S(1)}, u32[]{:S(2)}, u32[]{:S(2)}) collective-permute-start(bf16[128,256]{1,0:T(8,128)(2,1)S(1)} %collective-permute-done.refs_0_), channel_id=1, source_target_pairs={{0,2},{2,0},{4,6},{6,4},{8,10},{10,8},{12,14},{14,12},{1,3},{3,1},... | collective-permute-start | bytes 196616 | tf_op jit(solution)/shard_map/ppermute | solution.py:50
  19.9 0.7 %copy-start.3 = (s32[2,2]{1,0:T(2,128)S(1)}, s32[2,2]{1,0:T(2,128)}, u32[]{:S(2)}) copy-start(s32[2,2]{1,0:T(2,128)} %near_ref.15) | copy-start | bytes 52
  24.7 7.3 %copy-start.1 = (f32[256,256]{1,0:T(8,128)S(1)}, f32[256,256]{1,0:T(8,128)}, u32[]{:S(2)}) copy-start(f32[256,256]{1,0:T(8,128)} %tau.3) | copy-start | bytes 786436
  24.7 7.2 %collective-permute-start.9 = (bf16[2,256,256]{2,1,0:T(8,128)(2,1)S(1)}, bf16[2,256,256]{2,1,0:T(8,128)(2,1)S(1)}, u32[]{:S(2)}, u32[]{:S(2)}) collective-permute-start(bf16[2,256,256]{2,1,0:T(8,128)(2,1)S(1)} %shard_map.127), channel_id=1, source_target_pairs={{0,1},{1,0},{2,3},{3,2},{4,5},{5,4},{6,7},{7,6},{8,9},{9,8},{10,11... | collective-permute-start | bytes 786440 | tf_op jit(solution)/shard_map/ppermute | solution.py:405
  35.0 4.8 %collective-permute-start.14 = (bf16[256,256]{1,0:T(8,128)(2,1)S(1)}, bf16[256,256]{1,0:T(8,128)(2,1)S(1)}, u32[]{:S(2)}, u32[]{:S(2)}) collective-permute-start(bf16[256,256]{1,0:T(8,128)(2,1)S(1)} %get-tuple-element.27.refs_0_), channel_id=1, source_target_pairs={{0,4},{2,6},{4,8},{6,10},{8,12},{10,14},{12,0},{14,2},{1,5},{3,7},... | collective-permute-start | bytes 393224 | tf_op jit(solution)/shard_map/ppermute | solution.py:50
  35.1 6.7 %collective-permute-start.16 = (bf16[256,256]{1,0:T(8,128)(2,1)S(1)}, bf16[256,256]{1,0:T(8,128)(2,1)S(1)}, u32[]{:S(2)}, u32[]{:S(2)}) collective-permute-start(bf16[256,256]{1,0:T(8,128)(2,1)S(1)} %get-tuple-element.27.refs_0_), channel_id=1, source_target_pairs={{0,12},{2,14},{4,0},{6,2},{8,4},{10,6},{12,8},{14,10},{1,13},{3,15... | collective-permute-start | bytes 393224 | tf_op jit(solution)/shard_map/ppermute | solution.py:50
  36.5 14.4 %collective-permute-start.18 = (bf16[256,256]{1,0:T(8,128)(2,1)S(1)}, bf16[256,256]{1,0:T(8,128)(2,1)S(1)}, u32[]{:S(2)}, u32[]{:S(2)}) collective-permute-start(bf16[256,256]{1,0:T(8,128)(2,1)S(1)} %get-tuple-element.27.refs_0_), channel_id=1, source_target_pairs={{0,2},{2,0},{4,6},{6,4},{8,10},{10,8},{12,14},{14,12},{1,3},{3,1},... | collective-permute-start | bytes 393224 | tf_op jit(solution)/shard_map/ppermute | solution.py:50
  39.8 13.7 %collective-permute-start.15 = (bf16[256,256]{1,0:T(8,128)(2,1)S(1)}, bf16[256,256]{1,0:T(8,128)(2,1)S(1)}, u32[]{:S(2)}, u32[]{:S(2)}) collective-permute-start(bf16[256,256]{1,0:T(8,128)(2,1)S(1)} %collective-permute-done.14.refs_2_), channel_id=1, source_target_pairs={{0,2},{2,0},{4,6},{6,4},{8,10},{10,8},{12,14},{14,12},{1,3},{3,1},... | collective-permute-start | bytes 393224 | tf_op jit(solution)/shard_map/ppermute | solution.py:50
  41.7 11.7 %collective-permute-start.17 = (bf16[256,256]{1,0:T(8,128)(2,1)S(1)}, bf16[256,256]{1,0:T(8,128)(2,1)S(1)}, u32[]{:S(2)}, u32[]{:S(2)}) collective-permute-start(bf16[256,256]{1,0:T(8,128)(2,1)S(1)} %collective-permute-done.16.refs_3_), channel_id=1, source_target_pairs={{0,2},{2,0},{4,6},{6,4},{8,10},{10,8},{12,14},{14,12},{1,3},{3,1},... | collective-permute-start | bytes 393224 | tf_op jit(solution)/shard_map/ppermute | solution.py:50
  42.4 5.4 %collective-permute-start.10 = (bf16[128,256]{1,0:T(8,128)(2,1)S(1)}, bf16[128,256]{1,0:T(8,128)(2,1)S(1)}, u32[]{:S(2)}, u32[]{:S(2)}) collective-permute-start(bf16[128,256]{1,0:T(8,128)(2,1)S(1)} %get-tuple-element.25), channel_id=1, source_target_pairs={{0,8},{2,10},{4,12},{6,14},{8,0},{10,2},{12,4},{14,6},{1,9},{3,11}... | collective-permute-start | bytes 196616 | tf_op jit(solution)/shard_map/ppermute | solution.py:50
  46.1 8.7 %collective-permute-start.11 = (bf16[128,256]{1,0:T(8,128)(2,1)S(1)}, bf16[128,256]{1,0:T(8,128)(2,1)S(1)}, u32[]{:S(2)}, u32[]{:S(2)}) collective-permute-start(bf16[128,256]{1,0:T(8,128)(2,1)S(1)} %get-tuple-element.26), channel_id=1, source_target_pairs={{0,8},{2,10},{4,12},{6,14},{8,0},{10,2},{12,4},{14,6},{1,9},{3,11}... | collective-permute-start | bytes 196616 | tf_op jit(solution)/shard_map/ppermute | solution.py:50
  47.8 7.0 %collective-permute-start.13 = (bf16[128,256]{1,0:T(8,128)(2,1)S(1)}, bf16[128,256]{1,0:T(8,128)(2,1)S(1)}, u32[]{:S(2)}, u32[]{:S(2)}) collective-permute-start(bf16[128,256]{1,0:T(8,128)(2,1)S(1)} %get-tuple-element.26), channel_id=1, source_target_pairs={{0,10},{2,8},{4,14},{6,12},{8,2},{10,0},{12,6},{14,4},{1,11},{3,9}... | collective-permute-start | bytes 196616 | tf_op jit(solution)/shard_map/ppermute | solution.py:50
  50.9 3.9 %collective-permute-start.12 = (bf16[128,256]{1,0:T(8,128)(2,1)S(1)}, bf16[128,256]{1,0:T(8,128)(2,1)S(1)}, u32[]{:S(2)}, u32[]{:S(2)}) collective-permute-start(bf16[128,256]{1,0:T(8,128)(2,1)S(1)} %collective-permute-done.10.refs_0_), channel_id=1, source_target_pairs={{0,2},{2,0},{4,6},{6,4},{8,10},{10,8},{12,14},{14,12},{1,3},{3,1},... | collective-permute-start | bytes 196616 | tf_op jit(solution)/shard_map/ppermute | solution.py:50
  55.8 5.6 %copy-start.2 = (f32[256,256]{1,0:T(8,128)S(1)}, f32[256,256]{1,0:T(8,128)}, u32[]{:S(2)}) copy-start(f32[256,256]{1,0:T(8,128)} %state.1) | copy-start | bytes 786436
  55.8 5.6 %collective-permute-start.19 = (bf16[2,256,256]{2,1,0:T(8,128)(2,1)S(1)}, bf16[2,256,256]{2,1,0:T(8,128)(2,1)S(1)}, u32[]{:S(2)}, u32[]{:S(2)}) collective-permute-start(bf16[2,256,256]{2,1,0:T(8,128)(2,1)S(1)} %shard_map.132), channel_id=1, source_target_pairs={{0,1},{1,0},{2,3},{3,2},{4,5},{5,4},{6,7},{7,6},{8,9},{9,8},{10,11... | collective-permute-start | bytes 786440 | tf_op jit(solution)/shard_map/ppermute | solution.py:405

commit v7 on v4

--- a/solution.py
+++ b/solution.py
@@ -8,7 +8,7 @@
 from jax.sharding import PartitionSpec as P
 
 NEWTON = 2
-DIRECT_LIMIT = 16
+DIRECT_COUNTS = (4, 8)
 LATE = 4
 
 damping = 0.5
@@ -19,41 +19,24 @@
 def arrivals(count, direct):
     if not direct:
         return list(range(count))
-    length = count // 2
-    shifts = list(range(length - 1, 0, -1))
-    early = [(0, 0), (0, 1)] + [(shift, 0) for shift in shifts[:-1]]
-    late = [(shift, 0) for shift in shifts[-1:]] + [(shift, 1) for shift in shifts[-1:]]
-    return early + late + [(shift, 1) for shift in shifts[:-1]]
-
-
-def row_met(spot, row, count):
-    if not isinstance(spot, tuple):
-        return spot
-    shift, other = spot
-    z, y = row // 2, row % 2
-    return lax.rem(z - shift + count // 2, count // 2) * 2 + (1 - y if other else y)
+    return [0, 1, 4, 2, 3, 5, 6, 7] if count == 8 else [0, 1, 2, 3]
+
+
+def row_met(spot, row, direct):
+    return jnp.bitwise_xor(row, spot) if direct else spot
 
 
 def gather_direct(block, count):
-    length = count // 2
-
-    def along(shift, other, data):
-        hops = [
-            (z * 2 + y, (z + shift) % length * 2 + (1 - y if other else y))
-            for z in range(length)
-            for y in range(2)
-        ]
-        return lax.ppermute(data, "row", hops)
-
-    shifts = list(range(length - 1, 0, -1))
-    far, last = {}, []
-    across = along(0, 1, block)
-    for shift in shifts[:-1]:
-        far[shift] = along(shift, 0, block)
-    if shifts:
-        last = [along(shifts[-1], 0, block), along(shifts[-1], 1, block)]
-    passed = [along(0, 1, far[shift]) for shift in shifts[:-1]]
-    return [block, across, *far.values(), *last, *passed]
+    def swapped(mask, data):
+        return lax.ppermute(data, "row", [(row, row ^ mask) for row in range(count)])
+
+    found = {0: block}
+    for mask in (4, 1, 2, 3) if count == 8 else (1, 2, 3):
+        found[mask] = swapped(mask, block)
+    if count == 8:
+        for mask in (1, 2, 3):
+            found[4 + mask] = swapped(mask, found[4])
+    return [found[mask] for mask in arrivals(count, True)]
 
 
 PIECES = 4
@@ -76,7 +59,7 @@
         narrow_ref[part, :] = held[part, :].astype(narrow_ref.dtype)
 
 
-def prepare_kernel(spots, row_ref, *refs):
+def prepare_kernel(spots, direct, row_ref, *refs):
     far, (v_out, u_out, coef_out, weight_out, decay_out), near, sem = refs[:7], refs[7:12], refs[12:19], refs[19]
     copies = [
         pltpu.make_async_copy(source, held, sem.at[at])
@@ -89,7 +72,7 @@
     rank_ref, v_ref, u_ref, sigma_ref, a_ref, b_ref, state_ref = near
     kinds, rows, count, rank_count, size = u_ref.shape
     row = row_ref[0]
-    met = [row_met(spot, row, count) for spot in spots]
+    met = [row_met(spot, row, direct) for spot in spots]
     for at, q in enumerate(met):
         for p in range(rows):
             inside = lax.broadcasted_iota(jnp.int32, (rank_count, size), 0) < rank_ref[p, q]
@@ -112,7 +95,7 @@
         decay_out[:, part] = jnp.exp(-state / coef_out[2])
 
 
-def sums_kernel(spots, first, pick, before, row_ref, col_ref, near_ref, v_ref, u_ref, d_ref, *refs):
+def sums_kernel(spots, direct, first, pick, before, row_ref, col_ref, near_ref, v_ref, u_ref, d_ref, *refs):
     blocks = refs[: len(spots)]
     refs = refs[len(spots) :]
     if before:
@@ -121,7 +104,7 @@
     count, rows, rank_count, size = v_ref.shape
     kinds, slots = d_ref.shape[0], near_ref.shape[1]
     row, col = row_ref[0], col_ref[0]
-    met = [row_met(spot, row, count) for spot in spots]
+    met = [row_met(spot, row, direct) for spot in spots]
     chosen = list(range(rows)) if pick is None else [col if pick == 0 else 1 - col]
     for at, block in enumerate(blocks):
         x_all[at] = block[...]
@@ -297,7 +280,7 @@
     count = lax.axis_size("row")
     size, members = slip_deficit.shape
     kinds, rows, _, rank_count, _ = u_basis.shape
-    direct = count % 2 == 0 and count <= DIRECT_LIMIT
+    direct = count in DIRECT_COUNTS
     spots = arrivals(count, direct)
     early = max(count - LATE, 0)
     room = 16 if direct else 40
@@ -311,7 +294,7 @@
 
     full = shaped(size, members)
     v_met, u_met, coef, weight, decay = on_core(
-        functools.partial(prepare_kernel, spots),
+        functools.partial(prepare_kernel, spots, direct),
         (
             shaped(count, rows, rank_count, size, kind=narrow),
             shaped(rows, kinds * size, count * rank_count, kind=narrow),
@@ -346,7 +329,7 @@
         lead = (rows, kinds) if pick is None else (kinds,)
         return on_core(
             functools.partial(
-                sums_kernel, spots[first : first + len(blocks)], first, pick, before is not None
+                sums_kernel, spots[first : first + len(blocks)], direct, first, pick, before is not None
             ),
             shaped(*lead, size, members, kind=kind),
             (row, col, near_index),

time: 52.7 us -> 49.7 us (0.943)
  starting transfers between devices: 23.2 us -> 20.1 us
    ppermute x14, starting transfers between devices: 23.1 us -> 20 us  [swapped(): lax.ppermute(data, 'row', [(row, row ^ mask) for row in range(count)])]
    ppermute x14, waiting for transfers between devices: 12.5 us -> 11.7 us  [swapped(): lax.ppermute(data, 'row', [(row, row ^ mask) for row in range(count)])]
  transfers between devices with their start and end apart: 16 -> 16, of which waited for: 10 -> 9; matrix products, arithmetic and copies ran while one was open for 0% -> 0% of each run, Pallas kernels for 14% -> 16%
where the time goes in v7:
time: 49.7 us; the launch traced here: 49.2 us
  starting transfers between devices  20.1 us (40%)
  Pallas kernels  14.9 us (30%)
  waiting for transfers between devices  12.7 us (26%)
  between operations  0.8 us (2%)
  local copies, waits for them, and re-layouts  0.68 us (1%)
    ppermute x14, starting transfers between devices, swapped(): lax.ppermute(data, 'row', [(row, row ^ mask) for row in range(count)])  20 us
    pallas_call x10, Pallas kernels, on_core(): pl.pallas_call(kernel, out_shape=outs, in_specs=[smem] * len(scalars) + [...  14.9 us
    ppermute x14, waiting for transfers between devices, swapped(): lax.ppermute(data, 'row', [(row, row ^ mask) for row in range(count)])  11.7 us
    ppermute x2, waiting for transfers between devices, lattice(): lax.ppermute(add(blocks[early:], early, 1, sums, narrow), 'col', swap)  1.01 us
  transfers between devices with their start and end apart: 16, of which 9 were waited for; matrix products, arithmetic and copies ran while one was open for 0% of the time, Pallas kernels for 16%

profile of v7, /device:TPU:0, one launch (start us, length us, event | category | flops | bytes accessed | tf_op | source)
XLA Modules:
  0.0 49.2 jit_solution(9826882015868205376)
XLA Ops:
  0.6 0.0 copy-start
  0.6 1.1 %shard_map.123.refs_0_ = bf16[256,256]{1,0:T(8,128)(2,1)S(1)} custom-call(f32[256,256]{1,0:T(8,128)} %wide_ref.1), custom_call_target="tpu_custom_call" | custom-call | bytes 262144 | tf_op jit(solution)/shard_map/pallas_call | solution.py:254
  1.7 4.1 %collective-permute-start.1 = (bf16[256,256]{1,0:T(8,128)(2,1)S(1)}, bf16[256,256]{1,0:T(8,128)(2,1)S(1)}, u32[]{:S(2)}, u32[]{:S(2)}) collective-permute-start(bf16[256,256]{1,0:T(8,128)(2,1)S(1)} %shard_map.123.refs_0_), channel_id=1, source_target_pairs={{0,8},{2,10},{4,12},{6,14},{8,0},{10,2},{12,4},{14,6},{1,9},{3,11}... | collective-permute-start | bytes 393224 | tf_op jit(solution)/shard_map/ppermute | solution.py:31
  5.8 1.6 %collective-permute-start.6 = (bf16[256,256]{1,0:T(8,128)(2,1)S(1)}, bf16[256,256]{1,0:T(8,128)(2,1)S(1)}, u32[]{:S(2)}, u32[]{:S(2)}) collective-permute-start(bf16[256,256]{1,0:T(8,128)(2,1)S(1)} %shard_map.123.refs_0_), channel_id=1, source_target_pairs={{0,4},{2,6},{4,0},{6,2},{8,12},{10,14},{12,8},{14,10},{1,5},{3,7},... | collective-permute-start | bytes 393224 | tf_op jit(solution)/shard_map/ppermute | solution.py:31
  7.4 1.5 %collective-permute-start.5 = (bf16[256,256]{1,0:T(8,128)(2,1)S(1)}, bf16[256,256]{1,0:T(8,128)(2,1)S(1)}, u32[]{:S(2)}, u32[]{:S(2)}) collective-permute-start(bf16[256,256]{1,0:T(8,128)(2,1)S(1)} %shard_map.123.refs_0_), channel_id=1, source_target_pairs={{0,2},{2,0},{4,6},{6,4},{8,10},{10,8},{12,14},{14,12},{1,3},{3,1},... | collective-permute-start | bytes 393224 | tf_op jit(solution)/shard_map/ppermute | solution.py:31
  8.9 0.4 collective-permute-start
  9.3 2.9 %collective-permute-done.1.refs_2_ = bf16[256,256]{1,0:T(8,128)(2,1)S(1)} collective-permute-done((bf16[256,256]{1,0:T(8,128)(2,1)S(1)}, bf16[256,256]{1,0:T(8,128)(2,1)S(1)}, u32[]{:S(2)}, u32[]{:S(2)}) %collective-permute-start.1) | collective-permute-done | bytes 131104 | tf_op jit(solution)/shard_map/ppermute | solution.py:31
  12.2 1.6 %collective-permute-start.4 = (bf16[256,256]{1,0:T(8,128)(2,1)S(1)}, bf16[256,256]{1,0:T(8,128)(2,1)S(1)}, u32[]{:S(2)}, u32[]{:S(2)}) collective-permute-start(bf16[256,256]{1,0:T(8,128)(2,1)S(1)} %collective-permute-done.1.refs_2_), channel_id=1, source_target_pairs={{0,6},{2,4},{4,2},{6,0},{8,14},{10,12},{12,10},{14,8},{1,7},{3,5},... | collective-permute-start | bytes 393224 | tf_op jit(solution)/shard_map/ppermute | solution.py:31
  13.8 1.4 %collective-permute-start.3 = (bf16[256,256]{1,0:T(8,128)(2,1)S(1)}, bf16[256,256]{1,0:T(8,128)(2,1)S(1)}, u32[]{:S(2)}, u32[]{:S(2)}) collective-permute-start(bf16[256,256]{1,0:T(8,128)(2,1)S(1)} %collective-permute-done.1.refs_2_), channel_id=1, source_target_pairs={{0,4},{2,6},{4,0},{6,2},{8,12},{10,14},{12,8},{14,10},{1,5},{3,7},... | collective-permute-start | bytes 393224 | tf_op jit(solution)/shard_map/ppermute | solution.py:31
  15.2 0.0 collective-permute-done.6.refs_3_
  15.3 0.5 collective-permute-start.2
  15.7 1.7 %shard_map.122 = (bf16[8,2,32,256]{3,2,1,0:T(8,128)(2,1)S(1)}, bf16[2,512,256]{2,1,0:T(8,128)(2,1)S(1)}, f32[3,256,128]{2,1,0:T(8,128)S(1)}, f32[256,256]{1,0:T(8,128)S(1)}, f32[256,256]{1,0:T(8,128)S(1)}) custom-call(s32[1]{0:T(128)} %bitcast.row_ref, s32[2,8]{1,0:T(2,128)} %refs_0_.1, bf16[2,8,32,256]{3,2,1,0:T(8,128)(2,1)} %refs_1_.1, ...), custom_call_target="tpu_custom_call" | custom-call | bytes 1051712 | tf_op jit(solution)/shard_map/pallas_call | solution.py:254
  17.4 0.0 collective-permute-done.5.refs_1_
  17.4 0.0 copy-start.3
  17.4 0.7 %copy-done.3 = s32[2,2]{1,0:T(2,128)S(1)} copy-done((s32[2,2]{1,0:T(2,128)S(1)}, s32[2,2]{1,0:T(2,128)}, u32[]{:S(2)}) %copy-start.3) | copy-done | bytes 40
  18.1 2.0 %shard_map.124.refs_4_ = f32[2,2,256,256]{3,2,1,0:T(8,128)S(1)} custom-call(s32[1]{0:T(128)} %bitcast.row_ref, s32[1]{0:T(128)} %bitcast.1.col_ref, s32[2,2]{1,0:T(2,128)S(1)} %copy-done.3, bf16[8,2,32,256]{3,2,1,0:T(8,128)(2,1)S(1)} %get-tuple-element.12.v_ref, bf16[2,512,256]{2,1,0:T(8,128)(2,1)S(1)} %get-tuple-element.13.u_ref, ...), custom_call_target="tpu_custom_call" | custom-call | flops 100663296 | bytes 2359296 | tf_op jit(solution)/shard_map/pallas_call | solution.py:254
  20.1 0.0 collective-permute-done.refs_0_
  20.1 0.0 collective-permute-done.4.refs_3_
  20.1 0.7 %collective-permute-done.3.refs_2_ = bf16[256,256]{1,0:T(8,128)(2,1)S(1)} collective-permute-done((bf16[256,256]{1,0:T(8,128)(2,1)S(1)}, bf16[256,256]{1,0:T(8,128)(2,1)S(1)}, u32[]{:S(2)}, u32[]{:S(2)}) %collective-permute-start.3) | collective-permute-done | bytes 131104 | tf_op jit(solution)/shard_map/ppermute | solution.py:31
  20.9 1.0 %collective-permute-done.2.refs_1_ = bf16[256,256]{1,0:T(8,128)(2,1)S(1)} collective-permute-done((bf16[256,256]{1,0:T(8,128)(2,1)S(1)}, bf16[256,256]{1,0:T(8,128)(2,1)S(1)}, u32[]{:S(2)}, u32[]{:S(2)}) %collective-permute-start.2) | collective-permute-done | bytes 131104 | tf_op jit(solution)/shard_map/ppermute | solution.py:31
  21.9 1.0 %shard_map.126 = bf16[2,256,256]{2,1,0:T(8,128)(2,1)S(1)} custom-call(s32[1]{0:T(128)} %bitcast.row_ref, s32[1]{0:T(128)} %bitcast.1.col_ref, s32[2,2]{1,0:T(2,128)S(1)} %copy-done.3, bf16[8,2,32,256]{3,2,1,0:T(8,128)(2,1)S(1)} %get-tuple-element.12.v_ref, bf16[2,512,256]{2,1,0:T(8,128)(2,1)S(1)} %get-tuple-element.13.u_ref, ...), custom_call_target="tpu_custom_call" | custom-call | flops 50331648 | bytes 3407872 | tf_op jit(solution)/shard_map/pallas_call | solution.py:254
  22.9 0.0 copy-start.1
  22.9 0.1 collective-permute-start.7
  23.0 1.0 %shard_map.125.own = f32[2,256,256]{2,1,0:T(8,128)S(1)} custom-call(s32[1]{0:T(128)} %bitcast.row_ref, s32[1]{0:T(128)} %bitcast.1.col_ref, s32[2,2]{1,0:T(2,128)S(1)} %copy-done.3, bf16[8,2,32,256]{3,2,1,0:T(8,128)(2,1)S(1)} %get-tuple-element.12.v_ref, bf16[2,512,256]{2,1,0:T(8,128)(2,1)S(1)} %get-tuple-element.13.u_ref, ...), custom_call_target="tpu_custom_call" | custom-call | flops 50331648 | bytes 3407872 | tf_op jit(solution)/shard_map/pallas_call | solution.py:254
  24.0 0.5 %collective-permute-done.7.other = bf16[2,256,256]{2,1,0:T(8,128)(2,1)S(1)} collective-permute-done((bf16[2,256,256]{2,1,0:T(8,128)(2,1)S(1)}, bf16[2,256,256]{2,1,0:T(8,128)(2,1)S(1)}, u32[]{:S(2)}, u32[]{:S(2)}) %collective-permute-start.7) | collective-permute-done | bytes 262176 | tf_op jit(solution)/shard_map/ppermute | solution.py:353
  24.5 1.5 %shard_map.127 = (f32[256,256]{1,0:T(8,128)S(1)}, f32[256,256]{1,0:T(8,128)S(1)}, f32[256,256]{1,0:T(8,128)S(1)}, f32[256,256]{1,0:T(8,128)S(1)}, bf16[256,256]{1,0:T(8,128)(2,1)S(1)}) custom-call(f32[2,256,256]{2,1,0:T(8,128)S(1)} %shard_map.125.own, bf16[2,256,256]{2,1,0:T(8,128)(2,1)S(1)} %collective-permute-done.7.other, ...), custom_call_target="tpu_custom_call" | custom-call | flops 13107200 | bytes 1966080 | tf_op jit(solution)/shard_map/pallas_call | solution.py:254
  26.0 1.9 %collective-permute-start.9 = (bf16[256,256]{1,0:T(8,128)(2,1)S(1)}, bf16[256,256]{1,0:T(8,128)(2,1)S(1)}, u32[]{:S(2)}, u32[]{:S(2)}) collective-permute-start(bf16[256,256]{1,0:T(8,128)(2,1)S(1)} %get-tuple-element.17.refs_0_), channel_id=1, source_target_pairs={{0,8},{2,10},{4,12},{6,14},{8,0},{10,2},{12,4},{14,6},{1,9},{3,11}... | collective-permute-start | bytes 393224 | tf_op jit(solution)/shard_map/ppermute | solution.py:31
  27.9 1.7 %collective-permute-start.14 = (bf16[256,256]{1,0:T(8,128)(2,1)S(1)}, bf16[256,256]{1,0:T(8,128)(2,1)S(1)}, u32[]{:S(2)}, u32[]{:S(2)}) collective-permute-start(bf16[256,256]{1,0:T(8,128)(2,1)S(1)} %get-tuple-element.17.refs_0_), channel_id=1, source_target_pairs={{0,4},{2,6},{4,0},{6,2},{8,12},{10,14},{12,8},{14,10},{1,5},{3,7},... | collective-permute-start | bytes 393224 | tf_op jit(solution)/shard_map/ppermute | solution.py:31
  29.7 1.7 %collective-permute-start.13 = (bf16[256,256]{1,0:T(8,128)(2,1)S(1)}, bf16[256,256]{1,0:T(8,128)(2,1)S(1)}, u32[]{:S(2)}, u32[]{:S(2)}) collective-permute-start(bf16[256,256]{1,0:T(8,128)(2,1)S(1)} %get-tuple-element.17.refs_0_), channel_id=1, source_target_pairs={{0,2},{2,0},{4,6},{6,4},{8,10},{10,8},{12,14},{14,12},{1,3},{3,1},... | collective-permute-start | bytes 393224 | tf_op jit(solution)/shard_map/ppermute | solution.py:31
  31.3 0.1 collective-permute-start.8
  31.4 4.0 %collective-permute-done.9.refs_2_ = bf16[256,256]{1,0:T(8,128)(2,1)S(1)} collective-permute-done((bf16[256,256]{1,0:T(8,128)(2,1)S(1)}, bf16[256,256]{1,0:T(8,128)(2,1)S(1)}, u32[]{:S(2)}, u32[]{:S(2)}) %collective-permute-start.9) | collective-permute-done | bytes 131104 | tf_op jit(solution)/shard_map/ppermute | solution.py:31
  35.4 0.0 collective-permute-start.12
  35.4 2.1 %collective-permute-start.11 = (bf16[256,256]{1,0:T(8,128)(2,1)S(1)}, bf16[256,256]{1,0:T(8,128)(2,1)S(1)}, u32[]{:S(2)}, u32[]{:S(2)}) collective-permute-start(bf16[256,256]{1,0:T(8,128)(2,1)S(1)} %collective-permute-done.9.refs_2_), channel_id=1, source_target_pairs={{0,4},{2,6},{4,0},{6,2},{8,12},{10,14},{12,8},{14,10},{1,5},{3,7},... | collective-permute-start | bytes 393224 | tf_op jit(solution)/shard_map/ppermute | solution.py:31
  37.5 0.0 collective-permute-done.14.refs_3_
  37.5 1.4 %collective-permute-start.10 = (bf16[256,256]{1,0:T(8,128)(2,1)S(1)}, bf16[256,256]{1,0:T(8,128)(2,1)S(1)}, u32[]{:S(2)}, u32[]{:S(2)}) collective-permute-start(bf16[256,256]{1,0:T(8,128)(2,1)S(1)} %collective-permute-done.9.refs_2_), channel_id=1, source_target_pairs={{0,2},{2,0},{4,6},{6,4},{8,10},{10,8},{12,14},{14,12},{1,3},{3,1},... | collective-permute-start | bytes 393224 | tf_op jit(solution)/shard_map/ppermute | solution.py:31
  38.9 0.0 collective-permute-done.13.refs_1_
  38.9 2.0 %shard_map.128.refs_4_ = f32[2,2,256,256]{3,2,1,0:T(8,128)S(1)} custom-call(s32[1]{0:T(128)} %bitcast.row_ref, s32[1]{0:T(128)} %bitcast.1.col_ref, s32[2,2]{1,0:T(2,128)S(1)} %copy-done.3, bf16[8,2,32,256]{3,2,1,0:T(8,128)(2,1)S(1)} %get-tuple-element.12.v_ref, bf16[2,512,256]{2,1,0:T(8,128)(2,1)S(1)} %get-tuple-element.13.u_ref, ...), custom_call_target="tpu_custom_call" | custom-call | flops 100663296 | bytes 2359296 | tf_op jit(solution)/shard_map/pallas_call | solution.py:254
  40.9 0.0 collective-permute-done.8.refs_0_
  40.9 1.6 %collective-permute-done.12.refs_3_ = bf16[256,256]{1,0:T(8,128)(2,1)S(1)} collective-permute-done((bf16[256,256]{1,0:T(8,128)(2,1)S(1)}, bf16[256,256]{1,0:T(8,128)(2,1)S(1)}, u32[]{:S(2)}, u32[]{:S(2)}) %collective-permute-start.12) | collective-permute-done | bytes 131104 | tf_op jit(solution)/shard_map/ppermute | solution.py:31
  42.6 1.2 %collective-permute-done.11.refs_2_ = bf16[256,256]{1,0:T(8,128)(2,1)S(1)} collective-permute-done((bf16[256,256]{1,0:T(8,128)(2,1)S(1)}, bf16[256,256]{1,0:T(8,128)(2,1)S(1)}, u32[]{:S(2)}, u32[]{:S(2)}) %collective-permute-start.11) | collective-permute-done | bytes 131104 | tf_op jit(solution)/shard_map/ppermute | solution.py:31
  43.7 0.2 collective-permute-done.10.refs_1_
  44.0 1.0 %shard_map.130 = bf16[2,256,256]{2,1,0:T(8,128)(2,1)S(1)} custom-call(s32[1]{0:T(128)} %bitcast.row_ref, s32[1]{0:T(128)} %bitcast.1.col_ref, s32[2,2]{1,0:T(2,128)S(1)} %copy-done.3, bf16[8,2,32,256]{3,2,1,0:T(8,128)(2,1)S(1)} %get-tuple-element.12.v_ref, bf16[2,512,256]{2,1,0:T(8,128)(2,1)S(1)} %get-tuple-element.13.u_ref, ...), custom_call_target="tpu_custom_call" | custom-call | flops 50331648 | bytes 3407872 | tf_op jit(solution)/shard_map/pallas_call | solution.py:254
  45.0 0.0 copy-start.2
  45.0 0.1 collective-permute-start.15
  45.1 1.0 %shard_map.129.own = f32[2,256,256]{2,1,0:T(8,128)S(1)} custom-call(s32[1]{0:T(128)} %bitcast.row_ref, s32[1]{0:T(128)} %bitcast.1.col_ref, s32[2,2]{1,0:T(2,128)S(1)} %copy-done.3, bf16[8,2,32,256]{3,2,1,0:T(8,128)(2,1)S(1)} %get-tuple-element.12.v_ref, bf16[2,512,256]{2,1,0:T(8,128)(2,1)S(1)} %get-tuple-element.13.u_ref, ...), custom_call_target="tpu_custom_call" | custom-call | flops 50331648 | bytes 3407872 | tf_op jit(solution)/shard_map/pallas_call | solution.py:254
  46.1 0.5 %collective-permute-done.15.other = bf16[2,256,256]{2,1,0:T(8,128)(2,1)S(1)} collective-permute-done((bf16[2,256,256]{2,1,0:T(8,128)(2,1)S(1)}, bf16[2,256,256]{2,1,0:T(8,128)(2,1)S(1)}, u32[]{:S(2)}, u32[]{:S(2)}) %collective-permute-start.15) | collective-permute-done | bytes 262176 | tf_op jit(solution)/shard_map/ppermute | solution.py:353
  46.6 0.0 copy-done.2
  46.6 2.6 %shard_map.131 = (f32[256,256]{1,0:T(8,128)}, f32[256,256]{1,0:T(8,128)}) custom-call(f32[2,256,256]{2,1,0:T(8,128)S(1)} %shard_map.129.own, bf16[2,256,256]{2,1,0:T(8,128)(2,1)S(1)} %collective-permute-done.15.other, f32[256,256]{1,0:T(8,128)S(1)} %copy-done.2, f32[256,256]{1,0:T(8,128)S(1)} %copy-done.1, f32[3,256,128]{2,1,0:T(8,128)S(1)} %get-tuple-element.16.coef, ...), custom_call_target="tpu_custom_call" | custom-call | flops 13107200 | bytes 2752512 | tf_op jit(solution)/shard_map/pallas_call | solution.py:254
  (2 shorter events, 0.0 us)
Async XLA Ops:
  0.6 16.8 %copy-start = (bf16[2,2,2,256,256]{4,3,2,1,0:T(8,128)(2,1)S(1)}, bf16[2,2,2,256,256]{4,3,2,1,0:T(8,128)(2,1)}, u32[]{:S(2)}) copy-start(bf16[2,2,2,256,256]{4,3,2,1,0:T(8,128)(2,1)} %d_ref.11) | copy-start | bytes 3145732
  1.7 10.5 %collective-permute-start.1 = (bf16[256,256]{1,0:T(8,128)(2,1)S(1)}, bf16[256,256]{1,0:T(8,128)(2,1)S(1)}, u32[]{:S(2)}, u32[]{:S(2)}) collective-permute-start(bf16[256,256]{1,0:T(8,128)(2,1)S(1)} %shard_map.123.refs_0_), channel_id=1, source_target_pairs={{0,8},{2,10},{4,12},{6,14},{8,0},{10,2},{12,4},{14,6},{1,9},{3,11}... | collective-permute-start | bytes 393224 | tf_op jit(solution)/shard_map/ppermute | solution.py:31
  5.8 9.4 %collective-permute-start.6 = (bf16[256,256]{1,0:T(8,128)(2,1)S(1)}, bf16[256,256]{1,0:T(8,128)(2,1)S(1)}, u32[]{:S(2)}, u32[]{:S(2)}) collective-permute-start(bf16[256,256]{1,0:T(8,128)(2,1)S(1)} %shard_map.123.refs_0_), channel_id=1, source_target_pairs={{0,4},{2,6},{4,0},{6,2},{8,12},{10,14},{12,8},{14,10},{1,5},{3,7},... | collective-permute-start | bytes 393224 | tf_op jit(solution)/shard_map/ppermute | solution.py:31
  7.4 10.0 %collective-permute-start.5 = (bf16[256,256]{1,0:T(8,128)(2,1)S(1)}, bf16[256,256]{1,0:T(8,128)(2,1)S(1)}, u32[]{:S(2)}, u32[]{:S(2)}) collective-permute-start(bf16[256,256]{1,0:T(8,128)(2,1)S(1)} %shard_map.123.refs_0_), channel_id=1, source_target_pairs={{0,2},{2,0},{4,6},{6,4},{8,10},{10,8},{12,14},{14,12},{1,3},{3,1},... | collective-permute-start | bytes 393224 | tf_op jit(solution)/shard_map/ppermute | solution.py:31
  8.9 11.2 %collective-permute-start = (bf16[256,256]{1,0:T(8,128)(2,1)S(1)}, bf16[256,256]{1,0:T(8,128)(2,1)S(1)}, u32[]{:S(2)}, u32[]{:S(2)}) collective-permute-start(bf16[256,256]{1,0:T(8,128)(2,1)S(1)} %shard_map.123.refs_0_), channel_id=1, source_target_pairs={{0,6},{2,4},{4,2},{6,0},{8,14},{10,12},{12,10},{14,8},{1,7},{3,5},... | collective-permute-start | bytes 393224 | tf_op jit(solution)/shard_map/ppermute | solution.py:31
  12.2 7.9 %collective-permute-start.4 = (bf16[256,256]{1,0:T(8,128)(2,1)S(1)}, bf16[256,256]{1,0:T(8,128)(2,1)S(1)}, u32[]{:S(2)}, u32[]{:S(2)}) collective-permute-start(bf16[256,256]{1,0:T(8,128)(2,1)S(1)} %collective-permute-done.1.refs_2_), channel_id=1, source_target_pairs={{0,6},{2,4},{4,2},{6,0},{8,14},{10,12},{12,10},{14,8},{1,7},{3,5},... | collective-permute-start | bytes 393224 | tf_op jit(solution)/shard_map/ppermute | solution.py:31
  13.8 7.0 %collective-permute-start.3 = (bf16[256,256]{1,0:T(8,128)(2,1)S(1)}, bf16[256,256]{1,0:T(8,128)(2,1)S(1)}, u32[]{:S(2)}, u32[]{:S(2)}) collective-permute-start(bf16[256,256]{1,0:T(8,128)(2,1)S(1)} %collective-permute-done.1.refs_2_), channel_id=1, source_target_pairs={{0,4},{2,6},{4,0},{6,2},{8,12},{10,14},{12,8},{14,10},{1,5},{3,7},... | collective-permute-start | bytes 393224 | tf_op jit(solution)/shard_map/ppermute | solution.py:31
  15.3 6.6 %collective-permute-start.2 = (bf16[256,256]{1,0:T(8,128)(2,1)S(1)}, bf16[256,256]{1,0:T(8,128)(2,1)S(1)}, u32[]{:S(2)}, u32[]{:S(2)}) collective-permute-start(bf16[256,256]{1,0:T(8,128)(2,1)S(1)} %collective-permute-done.1.refs_2_), channel_id=1, source_target_pairs={{0,2},{2,0},{4,6},{6,4},{8,10},{10,8},{12,14},{14,12},{1,3},{3,1},... | collective-permute-start | bytes 393224 | tf_op jit(solution)/shard_map/ppermute | solution.py:31
  17.4 0.7 %copy-start.3 = (s32[2,2]{1,0:T(2,128)S(1)}, s32[2,2]{1,0:T(2,128)}, u32[]{:S(2)}) copy-start(s32[2,2]{1,0:T(2,128)} %near_ref.11) | copy-start | bytes 52
  22.9 1.6 %copy-start.1 = (f32[256,256]{1,0:T(8,128)S(1)}, f32[256,256]{1,0:T(8,128)}, u32[]{:S(2)}) copy-start(f32[256,256]{1,0:T(8,128)} %tau.3) | copy-start | bytes 786436
  22.9 1.6 %collective-permute-start.7 = (bf16[2,256,256]{2,1,0:T(8,128)(2,1)S(1)}, bf16[2,256,256]{2,1,0:T(8,128)(2,1)S(1)}, u32[]{:S(2)}, u32[]{:S(2)}) collective-permute-start(bf16[2,256,256]{2,1,0:T(8,128)(2,1)S(1)} %shard_map.126), channel_id=1, source_target_pairs={{0,1},{1,0},{2,3},{3,2},{4,5},{5,4},{6,7},{7,6},{8,9},{9,8},{10,11... | collective-permute-start | bytes 786440 | tf_op jit(solution)/shard_map/ppermute | solution.py:353
  26.0 9.4 %collective-permute-start.9 = (bf16[256,256]{1,0:T(8,128)(2,1)S(1)}, bf16[256,256]{1,0:T(8,128)(2,1)S(1)}, u32[]{:S(2)}, u32[]{:S(2)}) collective-permute-start(bf16[256,256]{1,0:T(8,128)(2,1)S(1)} %get-tuple-element.17.refs_0_), channel_id=1, source_target_pairs={{0,8},{2,10},{4,12},{6,14},{8,0},{10,2},{12,4},{14,6},{1,9},{3,11}... | collective-permute-start | bytes 393224 | tf_op jit(solution)/shard_map/ppermute | solution.py:31
  27.9 9.6 %collective-permute-start.14 = (bf16[256,256]{1,0:T(8,128)(2,1)S(1)}, bf16[256,256]{1,0:T(8,128)(2,1)S(1)}, u32[]{:S(2)}, u32[]{:S(2)}) collective-permute-start(bf16[256,256]{1,0:T(8,128)(2,1)S(1)} %get-tuple-element.17.refs_0_), channel_id=1, source_target_pairs={{0,4},{2,6},{4,0},{6,2},{8,12},{10,14},{12,8},{14,10},{1,5},{3,7},... | collective-permute-start | bytes 393224 | tf_op jit(solution)/shard_map/ppermute | solution.py:31
  29.7 9.2 %collective-permute-start.13 = (bf16[256,256]{1,0:T(8,128)(2,1)S(1)}, bf16[256,256]{1,0:T(8,128)(2,1)S(1)}, u32[]{:S(2)}, u32[]{:S(2)}) collective-permute-start(bf16[256,256]{1,0:T(8,128)(2,1)S(1)} %get-tuple-element.17.refs_0_), channel_id=1, source_target_pairs={{0,2},{2,0},{4,6},{6,4},{8,10},{10,8},{12,14},{14,12},{1,3},{3,1},... | collective-permute-start | bytes 393224 | tf_op jit(solution)/shard_map/ppermute | solution.py:31
  31.3 9.6 %collective-permute-start.8 = (bf16[256,256]{1,0:T(8,128)(2,1)S(1)}, bf16[256,256]{1,0:T(8,128)(2,1)S(1)}, u32[]{:S(2)}, u32[]{:S(2)}) collective-permute-start(bf16[256,256]{1,0:T(8,128)(2,1)S(1)} %get-tuple-element.17.refs_0_), channel_id=1, source_target_pairs={{0,6},{2,4},{4,2},{6,0},{8,14},{10,12},{12,10},{14,8},{1,7},{3,5},... | collective-permute-start | bytes 393224 | tf_op jit(solution)/shard_map/ppermute | solution.py:31
  35.4 7.2 %collective-permute-start.12 = (bf16[256,256]{1,0:T(8,128)(2,1)S(1)}, bf16[256,256]{1,0:T(8,128)(2,1)S(1)}, u32[]{:S(2)}, u32[]{:S(2)}) collective-permute-start(bf16[256,256]{1,0:T(8,128)(2,1)S(1)} %collective-permute-done.9.refs_2_), channel_id=1, source_target_pairs={{0,6},{2,4},{4,2},{6,0},{8,14},{10,12},{12,10},{14,8},{1,7},{3,5},... | collective-permute-start | bytes 393224 | tf_op jit(solution)/shard_map/ppermute | solution.py:31
  35.4 8.3 %collective-permute-start.11 = (bf16[256,256]{1,0:T(8,128)(2,1)S(1)}, bf16[256,256]{1,0:T(8,128)(2,1)S(1)}, u32[]{:S(2)}, u32[]{:S(2)}) collective-permute-start(bf16[256,256]{1,0:T(8,128)(2,1)S(1)} %collective-permute-done.9.refs_2_), channel_id=1, source_target_pairs={{0,4},{2,6},{4,0},{6,2},{8,12},{10,14},{12,8},{14,10},{1,5},{3,7},... | collective-permute-start | bytes 393224 | tf_op jit(solution)/shard_map/ppermute | solution.py:31
  37.5 6.5 %collective-permute-start.10 = (bf16[256,256]{1,0:T(8,128)(2,1)S(1)}, bf16[256,256]{1,0:T(8,128)(2,1)S(1)}, u32[]{:S(2)}, u32[]{:S(2)}) collective-permute-start(bf16[256,256]{1,0:T(8,128)(2,1)S(1)} %collective-permute-done.9.refs_2_), channel_id=1, source_target_pairs={{0,2},{2,0},{4,6},{6,4},{8,10},{10,8},{12,14},{14,12},{1,3},{3,1},... | collective-permute-start | bytes 393224 | tf_op jit(solution)/shard_map/ppermute | solution.py:31
  45.0 1.6 %copy-start.2 = (f32[256,256]{1,0:T(8,128)S(1)}, f32[256,256]{1,0:T(8,128)}, u32[]{:S(2)}) copy-start(f32[256,256]{1,0:T(8,128)} %state.1) | copy-start | bytes 786436
  45.0 1.6 %collective-permute-start.15 = (bf16[2,256,256]{2,1,0:T(8,128)(2,1)S(1)}, bf16[2,256,256]{2,1,0:T(8,128)(2,1)S(1)}, u32[]{:S(2)}, u32[]{:S(2)}) collective-permute-start(bf16[2,256,256]{2,1,0:T(8,128)(2,1)S(1)} %shard_map.130), channel_id=1, source_target_pairs={{0,1},{1,0},{2,3},{3,2},{4,5},{5,4},{6,7},{7,6},{8,9},{9,8},{10,11... | collective-permute-start | bytes 786440 | tf_op jit(solution)/shard_map/ppermute | solution.py:353

commit v8 on v7

--- a/solution.py
+++ b/solution.py
@@ -59,7 +59,7 @@
         narrow_ref[part, :] = held[part, :].astype(narrow_ref.dtype)
 
 
-def prepare_kernel(spots, direct, row_ref, *refs):
+def prepare_kernel(spots, direct, *refs):
     far, (v_out, u_out, coef_out, weight_out, decay_out), near, sem = refs[:7], refs[7:12], refs[12:19], refs[19]
     copies = [
         pltpu.make_async_copy(source, held, sem.at[at])
@@ -71,7 +71,7 @@
         copy.wait()
     rank_ref, v_ref, u_ref, sigma_ref, a_ref, b_ref, state_ref = near
     kinds, rows, count, rank_count, size = u_ref.shape
-    row = row_ref[0]
+    row = lax.axis_index("row")
     met = [row_met(spot, row, direct) for spot in spots]
     for at, q in enumerate(met):
         for p in range(rows):
@@ -86,28 +86,30 @@
                     turned.astype(u_out.dtype)
                 )
     lanes = coef_out.shape[2]
-    for at, ref in enumerate((sigma_ref, a_ref, b_ref)):
-        coef_out[at] = jnp.broadcast_to(ref[...], (lanes, size)).T
+    for at, values in enumerate((sigma_ref[...], a_ref[...], b_ref[...], 1.0 / a_ref[...], 1.0 / b_ref[...])):
+        coef_out[at] = jnp.broadcast_to(values, (lanes, size)).T
     for first in range(0, state_ref.shape[1], lanes):
         part = slice(first, first + lanes)
         state = state_ref[:, part]
-        weight_out[:, part] = jnp.exp(-state / coef_out[1])
-        decay_out[:, part] = jnp.exp(-state / coef_out[2])
-
-
-def sums_kernel(spots, direct, first, pick, before, row_ref, col_ref, near_ref, v_ref, u_ref, d_ref, *refs):
+        weight_out[:, part] = jnp.exp(-state * coef_out[3])
+        decay_out[:, part] = jnp.exp(-state * coef_out[4])
+
+
+def sums_kernel(spots, direct, first, pick, before, near_any, v_ref, u_ref, d_ref, *refs):
     blocks = refs[: len(spots)]
     refs = refs[len(spots) :]
     if before:
         sums_ref, refs = refs[0], refs[1:]
-    out_ref, x_all, proj, total = refs
+    out_ref, x_all, proj, near_ref, near_sem = refs[:5]
+    total = refs[5] if pick == 1 else out_ref
     count, rows, rank_count, size = v_ref.shape
     kinds, slots = d_ref.shape[0], near_ref.shape[1]
-    row, col = row_ref[0], col_ref[0]
+    near_copy = pltpu.make_async_copy(near_any, near_ref, near_sem)
+    near_copy.start()
+    row, col = lax.axis_index("row"), lax.axis_index("col")
     met = [row_met(spot, row, direct) for spot in spots]
     chosen = list(range(rows)) if pick is None else [col if pick == 0 else 1 - col]
-    for at, block in enumerate(blocks):
-        x_all[at] = block[...]
+    places = [(place,) for place in range(rows)] if pick is None else [()]
     for at, block in enumerate(blocks):
         if pick is None:
             weights = v_ref[first + at].reshape(rows * rank_count, size)
@@ -118,12 +120,15 @@
             proj[place, at * rank_count : (at + 1) * rank_count, :] = part[
                 place * rank_count : (place + 1) * rank_count
             ]
+    for at, block in enumerate(blocks):
+        x_all[at] = block[...]
     lanes = slice(first * rank_count, (first + len(blocks)) * rank_count)
     for place, p in enumerate(chosen):
         gained = jnp.dot(u_ref[p, :, lanes], proj[place], preferred_element_type=jnp.float32)
         for kind in range(kinds):
             piece = gained[kind * size : (kind + 1) * size]
-            total[place, kind] = sums_ref[p, kind] + piece if before else piece
+            total[*places[place], kind] = sums_ref[p, kind] + piece if before else piece
+    near_copy.wait()
     for place, p in enumerate(chosen):
         for s in range(slots):
             near = near_ref[p, s] - col * count
@@ -134,53 +139,46 @@
             def _():
                 block = x_all[at]
                 for kind in range(kinds):
-                    total[place, kind] += jnp.dot(
+                    total[*places[place], kind] += jnp.dot(
                         d_ref[kind, p, s], block, preferred_element_type=jnp.float32
                     )
-    for place in range(len(chosen)):
-        for kind in range(kinds):
-            if pick is None:
-                out_ref[place, kind] = total[place, kind]
-            else:
-                out_ref[kind] = total[place, kind].astype(out_ref.dtype)
-
-
-def inverse_sinh(value):
-    magnitude = jnp.abs(value)
-    result = jnp.log(magnitude + jnp.sqrt(magnitude * magnitude + 1.0))
-    return jnp.where(value < 0.0, -result, result)
+    if pick == 1:
+        out_ref[...] = total[...].astype(out_ref.dtype)
+
+
+def inverse(value):
+    rough = pl.reciprocal(value, approx=True)
+    return rough * (2.0 - value * rough)
 
 
 def sinh_cosh(value):
     grown = jnp.exp(value)
-    shrunk = jnp.exp(-value)
+    shrunk = inverse(grown)
     square = value * value
-    small = value * (
-        1.0 + square * (1 / 6 + square * (1 / 120 + square * (1 / 5040 + square * (1 / 362880))))
-    )
-    sinh = jnp.where(square < 1.0, small, 0.5 * (grown - shrunk))
+    small = value * (1.0 + square * (1 / 6 + square * (1 / 120)))
+    sinh = jnp.where(square < 0.25, small, 0.5 * (grown - shrunk))
     return sinh, 0.5 * (grown + shrunk)
 
 
 def friction(shear, normal, weight, decay, tau_load, sigma_base, a_wide, b_wide):
     tau = tau_load + shear
-    sigma = jnp.maximum(sigma_base + normal, sigma_floor)
-    stiff = sigma * a_wide
-    first = tau / stiff
-    second = inverse_sinh(tau / (2.0 * damping * weight))
-    slope = jnp.where(jnp.abs(first) < jnp.abs(second), first, second)
+    size = jnp.abs(tau)
+    stiff = jnp.maximum(sigma_base + normal, sigma_floor) * a_wide
+    double = 2.0 * damping * weight
+    drive = size * inverse(double)
+    square = drive * drive + 1.0
+    slope = jnp.minimum(size * inverse(stiff), jnp.log(drive + square * lax.rsqrt(square)))
     for newton_step in range(NEWTON):
         sinh, cosh = sinh_cosh(slope)
-        excess = stiff * slope + 2.0 * damping * weight * sinh - tau
-        deriv = stiff + 2.0 * damping * weight * cosh
-        slope = slope - excess / deriv
+        excess = stiff * slope + double * sinh - size
+        slope = slope - excess * inverse(stiff + double * cosh)
     rate = 2.0 * weight * sinh_cosh(slope)[0]
     change = b_wide * (decay - jnp.abs(rate))
-    return (rate, change)
+    return (jnp.where(tau < 0.0, -rate, rate), change)
 
 
 def over_pieces(begin, tall, members, lanes, work):
-    step = min(tall, 16)
+    step = min(tall, 32)
 
     @pl.loop(0, tall // step)
     def _(index):
@@ -227,8 +225,8 @@
         first, second = friction(
             stress[rows, part] + section_step * shear,
             normal[rows, part] + section_step * press,
-            jnp.exp(-later / a_wide),
-            jnp.exp(-later / b_wide),
+            jnp.exp(-later * coef[3, rows, :]),
+            jnp.exp(-later * coef[4, rows, :]),
             tau[rows, part],
             sigma,
             a_wide,
@@ -247,21 +245,20 @@
         copy.wait()
 
 
-def on_core(kernel, outs, scalars, arrays, scratch=(), flops=0, room=16, far=(), out_far=False):
-    smem, vmem = pl.BlockSpec(memory_space=pltpu.SMEM), pl.BlockSpec(memory_space=pltpu.VMEM)
-    hbm = pl.BlockSpec(memory_space=pl.ANY)
+def on_core(kernel, outs, arrays, scratch=(), flops=0, room=16, far=(), out_far=False):
+    vmem, hbm = pl.BlockSpec(memory_space=pltpu.VMEM), pl.BlockSpec(memory_space=pl.ANY)
     arrays = (*(pltpu.with_memory_space_constraint(a, pltpu.HBM) for a in far), *arrays)
     return pl.pallas_call(
         kernel,
         out_shape=outs,
-        in_specs=[smem] * len(scalars) + [hbm] * len(far) + [vmem] * (len(arrays) - len(far)),
+        in_specs=[hbm] * len(far) + [vmem] * (len(arrays) - len(far)),
         out_specs=jax.tree.map(lambda _: hbm if out_far else vmem, outs),
         scratch_shapes=list(scratch),
         compiler_params=pltpu.CompilerParams(vmem_limit_bytes=room * 1024 * 1024),
         cost_estimate=pl.CostEstimate(
             flops=flops, bytes_accessed=sum(a.size * a.dtype.itemsize for a in arrays), transcendentals=0
         ),
-    )(*scalars, *arrays)
+    )(*arrays)
 
 
 def body(
@@ -286,7 +283,6 @@
     room = 16 if direct else 40
     lanes = min(members, 128)
     narrow, wide = jnp.bfloat16, jnp.float32
-    row, col = lax.axis_index("row").reshape(1), lax.axis_index("col").reshape(1)
     swap = [(0, 1), (1, 0)]
 
     def shaped(*shape, kind=wide):
@@ -298,11 +294,10 @@
         (
             shaped(count, rows, rank_count, size, kind=narrow),
             shaped(rows, kinds * size, count * rank_count, kind=narrow),
-            shaped(3, size, lanes),
+            shaped(5, size, lanes),
             full,
             full,
         ),
-        (row,),
         (),
         (
             pltpu.SMEM(block_ranks.shape, jnp.int32),
@@ -332,15 +327,17 @@
                 sums_kernel, spots[first : first + len(blocks)], direct, first, pick, before is not None
             ),
             shaped(*lead, size, members, kind=kind),
-            (row, col, near_index),
             (v_met, u_met, dense_blocks, *blocks, *(() if before is None else (before,))),
             (
                 pltpu.VMEM((len(blocks), size, members), narrow),
                 pltpu.VMEM((held, len(blocks) * rank_count, members), narrow),
-                pltpu.VMEM((held, kinds, size, members), wide),
+                pltpu.SMEM(near_index.shape, jnp.int32),
+                pltpu.SemaphoreType.DMA(()),
+                *([pltpu.VMEM((kinds, size, members), wide)] if pick == 1 else []),
             ),
             2 * held * size * members * rank_count * len(blocks) * 3,
             room,
+            far=(near_index,),
         )
 
     def lattice(field_half):
@@ -357,7 +354,6 @@
         narrow_kernel,
         shaped(size, members, kind=narrow),
         (),
-        (),
         (pltpu.VMEM((size, members), wide), pltpu.SemaphoreType.DMA((PIECES,))),
         far=(slip_deficit,),
     )
@@ -365,7 +361,6 @@
     stress, normal, rate, change, rate_half = on_core(
         section_one_kernel,
         (full, full, full, full, shaped(size, members, kind=narrow)),
-        (),
         (own, other, weight, decay, tau_load, coef),
         flops=200 * size * members,
     )
@@ -373,7 +368,6 @@
     return on_core(
         section_two_kernel,
         (full, full),
-        (),
         (own, other, state_var, tau_load, coef, stress, normal, rate, change),
         (
             pltpu.VMEM((size, members), wide),

time: 49.7 us -> 49 us (0.986)
  waiting for transfers between devices: 12.7 us -> 15.9 us
  Pallas kernels: 14.9 us -> 12.6 us
  local copies, waits for them, and re-layouts: 0.68 us -> 0.02 us
    ppermute x14, waiting for transfers between devices: 11.7 us -> 14.3 us  [swapped(): lax.ppermute(data, 'row', [(row, row ^ mask) for row in range(count)])]
    pallas_call x10, Pallas kernels: 14.9 us -> 12.6 us  [on_core(): pl.pallas_call(kernel, out_shape=outs, in_specs=[hbm] * len(far) + [vmem]...]
    unnamed x8 -> x6, local copies, waits for them, and re-layouts: 0.68 us -> 0.02 us
    ppermute x2, waiting for transfers between devices: 1.01 us -> 1.55 us  [lattice(): lax.ppermute(add(blocks[early:], early, 1, sums, narrow), 'col', swap)]
  transfers between devices with their start and end apart: 16 -> 16, of which waited for: 9 -> 10; matrix products, arithmetic and copies ran while one was open for 0% -> 0% of each run, Pallas kernels for 16% -> 11%
where the time goes in v8:
time: 49 us; the launch traced here: 48.9 us
  starting transfers between devices  19.7 us (40%)
  waiting for transfers between devices  15.9 us (32%)
  Pallas kernels  12.6 us (26%)
  between operations  0.78 us (2%)
    ppermute x14, starting transfers between devices, swapped(): lax.ppermute(data, 'row', [(row, row ^ mask) for row in range(count)])  19.5 us
    ppermute x14, waiting for transfers between devices, swapped(): lax.ppermute(data, 'row', [(row, row ^ mask) for row in range(count)])  14.3 us
    pallas_call x10, Pallas kernels, on_core(): pl.pallas_call(kernel, out_shape=outs, in_specs=[hbm] * len(far) + [vmem]...  12.6 us
    ppermute x2, waiting for transfers between devices, lattice(): lax.ppermute(add(blocks[early:], early, 1, sums, narrow), 'col', swap)  1.55 us
  transfers between devices with their start and end apart: 16, of which 10 were waited for; matrix products, arithmetic and copies ran while one was open for 0% of the time, Pallas kernels for 11%

profile of v8, /device:TPU:0, one launch (start us, length us, event | category | flops | bytes accessed | tf_op | source)
XLA Modules:
  0.0 48.9 jit_solution(795110655333134821)
XLA Ops:
  0.6 0.0 copy-start
  0.6 1.1 %shard_map.123.refs_0_ = bf16[256,256]{1,0:T(8,128)(2,1)S(1)} custom-call(f32[256,256]{1,0:T(8,128)} %wide_ref.1), custom_call_target="tpu_custom_call" | custom-call | bytes 262144 | tf_op jit(solution)/shard_map/pallas_call | solution.py:251
  1.7 4.1 %collective-permute-start.1 = (bf16[256,256]{1,0:T(8,128)(2,1)S(1)}, bf16[256,256]{1,0:T(8,128)(2,1)S(1)}, u32[]{:S(2)}, u32[]{:S(2)}) collective-permute-start(bf16[256,256]{1,0:T(8,128)(2,1)S(1)} %shard_map.123.refs_0_), channel_id=1, source_target_pairs={{0,8},{2,10},{4,12},{6,14},{8,0},{10,2},{12,4},{14,6},{1,9},{3,11}... | collective-permute-start | bytes 393224 | tf_op jit(solution)/shard_map/ppermute | solution.py:31
  5.8 1.6 %collective-permute-start.6 = (bf16[256,256]{1,0:T(8,128)(2,1)S(1)}, bf16[256,256]{1,0:T(8,128)(2,1)S(1)}, u32[]{:S(2)}, u32[]{:S(2)}) collective-permute-start(bf16[256,256]{1,0:T(8,128)(2,1)S(1)} %shard_map.123.refs_0_), channel_id=1, source_target_pairs={{0,4},{2,6},{4,0},{6,2},{8,12},{10,14},{12,8},{14,10},{1,5},{3,7},... | collective-permute-start | bytes 393224 | tf_op jit(solution)/shard_map/ppermute | solution.py:31
  7.4 1.5 %collective-permute-start.5 = (bf16[256,256]{1,0:T(8,128)(2,1)S(1)}, bf16[256,256]{1,0:T(8,128)(2,1)S(1)}, u32[]{:S(2)}, u32[]{:S(2)}) collective-permute-start(bf16[256,256]{1,0:T(8,128)(2,1)S(1)} %shard_map.123.refs_0_), channel_id=1, source_target_pairs={{0,2},{2,0},{4,6},{6,4},{8,10},{10,8},{12,14},{14,12},{1,3},{3,1},... | collective-permute-start | bytes 393224 | tf_op jit(solution)/shard_map/ppermute | solution.py:31
  8.9 0.4 collective-permute-start
  9.3 2.9 %collective-permute-done.1.refs_2_ = bf16[256,256]{1,0:T(8,128)(2,1)S(1)} collective-permute-done((bf16[256,256]{1,0:T(8,128)(2,1)S(1)}, bf16[256,256]{1,0:T(8,128)(2,1)S(1)}, u32[]{:S(2)}, u32[]{:S(2)}) %collective-permute-start.1) | collective-permute-done | bytes 131104 | tf_op jit(solution)/shard_map/ppermute | solution.py:31
  12.2 1.6 %collective-permute-start.4 = (bf16[256,256]{1,0:T(8,128)(2,1)S(1)}, bf16[256,256]{1,0:T(8,128)(2,1)S(1)}, u32[]{:S(2)}, u32[]{:S(2)}) collective-permute-start(bf16[256,256]{1,0:T(8,128)(2,1)S(1)} %collective-permute-done.1.refs_2_), channel_id=1, source_target_pairs={{0,6},{2,4},{4,2},{6,0},{8,14},{10,12},{12,10},{14,8},{1,7},{3,5},... | collective-permute-start | bytes 393224 | tf_op jit(solution)/shard_map/ppermute | solution.py:31
  13.8 1.4 %collective-permute-start.3 = (bf16[256,256]{1,0:T(8,128)(2,1)S(1)}, bf16[256,256]{1,0:T(8,128)(2,1)S(1)}, u32[]{:S(2)}, u32[]{:S(2)}) collective-permute-start(bf16[256,256]{1,0:T(8,128)(2,1)S(1)} %collective-permute-done.1.refs_2_), channel_id=1, source_target_pairs={{0,4},{2,6},{4,0},{6,2},{8,12},{10,14},{12,8},{14,10},{1,5},{3,7},... | collective-permute-start | bytes 393224 | tf_op jit(solution)/shard_map/ppermute | solution.py:31
  15.2 0.0 collective-permute-done.6.refs_3_
  15.3 0.5 collective-permute-start.2
  15.7 1.7 %shard_map.122 = (bf16[8,2,32,256]{3,2,1,0:T(8,128)(2,1)S(1)}, bf16[2,512,256]{2,1,0:T(8,128)(2,1)S(1)}, f32[5,256,128]{2,1,0:T(8,128)S(1)}, f32[256,256]{1,0:T(8,128)S(1)}, f32[256,256]{1,0:T(8,128)S(1)}) custom-call(s32[2,8]{1,0:T(2,128)} %refs_0_.1, bf16[2,8,32,256]{3,2,1,0:T(8,128)(2,1)} %refs_1_.1, bf16[2,2,8,32,256]{4,3,2,1,0:T(8,128)(2,1)} %refs_2_.1, ...), custom_call_target="tpu_custom_call" | custom-call | bytes 1051712 | tf_op jit(solution)/shard_map/pallas_call | solution.py:251
  17.4 0.0 collective-permute-done.5.refs_1_
  17.4 0.0 copy-done
  17.5 1.2 %shard_map.124.refs_4_ = f32[2,2,256,256]{3,2,1,0:T(8,128)S(1)} custom-call(s32[2,2]{1,0:T(2,128)} %near_any.11, bf16[8,2,32,256]{3,2,1,0:T(8,128)(2,1)S(1)} %get-tuple-element.12.v_ref, bf16[2,512,256]{2,1,0:T(8,128)(2,1)S(1)} %get-tuple-element.13.u_ref, bf16[2,2,2,256,256]{4,3,2,1,0:T(8,128)(2,1)S(1)} %copy-done, ...), custom_call_target="tpu_custom_call" | custom-call | flops 100663296 | bytes 2359312 | tf_op jit(solution)/shard_map/pallas_call | solution.py:251
  18.7 0.0 collective-permute-done.refs_0_
  18.7 1.3 %collective-permute-done.4.refs_3_ = bf16[256,256]{1,0:T(8,128)(2,1)S(1)} collective-permute-done((bf16[256,256]{1,0:T(8,128)(2,1)S(1)}, bf16[256,256]{1,0:T(8,128)(2,1)S(1)}, u32[]{:S(2)}, u32[]{:S(2)}) %collective-permute-start.4) | collective-permute-done | bytes 131104 | tf_op jit(solution)/shard_map/ppermute | solution.py:31
  19.9 0.9 %collective-permute-done.3.refs_2_ = bf16[256,256]{1,0:T(8,128)(2,1)S(1)} collective-permute-done((bf16[256,256]{1,0:T(8,128)(2,1)S(1)}, bf16[256,256]{1,0:T(8,128)(2,1)S(1)}, u32[]{:S(2)}, u32[]{:S(2)}) %collective-permute-start.3) | collective-permute-done | bytes 131104 | tf_op jit(solution)/shard_map/ppermute | solution.py:31
  20.9 1.0 %collective-permute-done.2.refs_1_ = bf16[256,256]{1,0:T(8,128)(2,1)S(1)} collective-permute-done((bf16[256,256]{1,0:T(8,128)(2,1)S(1)}, bf16[256,256]{1,0:T(8,128)(2,1)S(1)}, u32[]{:S(2)}, u32[]{:S(2)}) %collective-permute-start.2) | collective-permute-done | bytes 131104 | tf_op jit(solution)/shard_map/ppermute | solution.py:31
  21.9 1.2 %shard_map.126 = bf16[2,256,256]{2,1,0:T(8,128)(2,1)S(1)} custom-call(s32[2,2]{1,0:T(2,128)} %near_any.11, bf16[8,2,32,256]{3,2,1,0:T(8,128)(2,1)S(1)} %get-tuple-element.12.v_ref, bf16[2,512,256]{2,1,0:T(8,128)(2,1)S(1)} %get-tuple-element.13.u_ref, bf16[2,2,2,256,256]{4,3,2,1,0:T(8,128)(2,1)S(1)} %copy-done, ...), custom_call_target="tpu_custom_call" | custom-call | flops 50331648 | bytes 3407888 | tf_op jit(solution)/shard_map/pallas_call | solution.py:251
  23.1 0.0 copy-start.1
  23.1 0.1 collective-permute-start.7
  23.2 0.7 %shard_map.125.own = f32[2,256,256]{2,1,0:T(8,128)S(1)} custom-call(s32[2,2]{1,0:T(2,128)} %near_any.11, bf16[8,2,32,256]{3,2,1,0:T(8,128)(2,1)S(1)} %get-tuple-element.12.v_ref, bf16[2,512,256]{2,1,0:T(8,128)(2,1)S(1)} %get-tuple-element.13.u_ref, bf16[2,2,2,256,256]{4,3,2,1,0:T(8,128)(2,1)S(1)} %copy-done, ...), custom_call_target="tpu_custom_call" | custom-call | flops 50331648 | bytes 3407888 | tf_op jit(solution)/shard_map/pallas_call | solution.py:251
  23.9 0.8 %collective-permute-done.7.other = bf16[2,256,256]{2,1,0:T(8,128)(2,1)S(1)} collective-permute-done((bf16[2,256,256]{2,1,0:T(8,128)(2,1)S(1)}, bf16[2,256,256]{2,1,0:T(8,128)(2,1)S(1)}, u32[]{:S(2)}, u32[]{:S(2)}) %collective-permute-start.7) | collective-permute-done | bytes 262176 | tf_op jit(solution)/shard_map/ppermute | solution.py:350
  24.7 0.0 copy-done.1
  24.7 1.3 %shard_map.127 = (f32[256,256]{1,0:T(8,128)S(1)}, f32[256,256]{1,0:T(8,128)S(1)}, f32[256,256]{1,0:T(8,128)S(1)}, f32[256,256]{1,0:T(8,128)S(1)}, bf16[256,256]{1,0:T(8,128)(2,1)S(1)}) custom-call(f32[2,256,256]{2,1,0:T(8,128)S(1)} %shard_map.125.own, bf16[2,256,256]{2,1,0:T(8,128)(2,1)S(1)} %collective-permute-done.7.other, ...), custom_call_target="tpu_custom_call" | custom-call | flops 13107200 | bytes 2228224 | tf_op jit(solution)/shard_map/pallas_call | solution.py:251
  26.0 1.5 %collective-permute-start.9 = (bf16[256,256]{1,0:T(8,128)(2,1)S(1)}, bf16[256,256]{1,0:T(8,128)(2,1)S(1)}, u32[]{:S(2)}, u32[]{:S(2)}) collective-permute-start(bf16[256,256]{1,0:T(8,128)(2,1)S(1)} %get-tuple-element.17.refs_0_), channel_id=1, source_target_pairs={{0,8},{2,10},{4,12},{6,14},{8,0},{10,2},{12,4},{14,6},{1,9},{3,11}... | collective-permute-start | bytes 393224 | tf_op jit(solution)/shard_map/ppermute | solution.py:31
  27.5 2.0 %collective-permute-start.14 = (bf16[256,256]{1,0:T(8,128)(2,1)S(1)}, bf16[256,256]{1,0:T(8,128)(2,1)S(1)}, u32[]{:S(2)}, u32[]{:S(2)}) collective-permute-start(bf16[256,256]{1,0:T(8,128)(2,1)S(1)} %get-tuple-element.17.refs_0_), channel_id=1, source_target_pairs={{0,4},{2,6},{4,0},{6,2},{8,12},{10,14},{12,8},{14,10},{1,5},{3,7},... | collective-permute-start | bytes 393224 | tf_op jit(solution)/shard_map/ppermute | solution.py:31
  29.4 1.5 %collective-permute-start.13 = (bf16[256,256]{1,0:T(8,128)(2,1)S(1)}, bf16[256,256]{1,0:T(8,128)(2,1)S(1)}, u32[]{:S(2)}, u32[]{:S(2)}) collective-permute-start(bf16[256,256]{1,0:T(8,128)(2,1)S(1)} %get-tuple-element.17.refs_0_), channel_id=1, source_target_pairs={{0,2},{2,0},{4,6},{6,4},{8,10},{10,8},{12,14},{14,12},{1,3},{3,1},... | collective-permute-start | bytes 393224 | tf_op jit(solution)/shard_map/ppermute | solution.py:31
  30.9 0.1 collective-permute-start.8
  30.9 4.5 %collective-permute-done.9.refs_2_ = bf16[256,256]{1,0:T(8,128)(2,1)S(1)} collective-permute-done((bf16[256,256]{1,0:T(8,128)(2,1)S(1)}, bf16[256,256]{1,0:T(8,128)(2,1)S(1)}, u32[]{:S(2)}, u32[]{:S(2)}) %collective-permute-start.9) | collective-permute-done | bytes 131104 | tf_op jit(solution)/shard_map/ppermute | solution.py:31
  35.4 0.0 collective-permute-start.12
  35.4 1.9 %collective-permute-start.11 = (bf16[256,256]{1,0:T(8,128)(2,1)S(1)}, bf16[256,256]{1,0:T(8,128)(2,1)S(1)}, u32[]{:S(2)}, u32[]{:S(2)}) collective-permute-start(bf16[256,256]{1,0:T(8,128)(2,1)S(1)} %collective-permute-done.9.refs_2_), channel_id=1, source_target_pairs={{0,4},{2,6},{4,0},{6,2},{8,12},{10,14},{12,8},{14,10},{1,5},{3,7},... | collective-permute-start | bytes 393224 | tf_op jit(solution)/shard_map/ppermute | solution.py:31
  37.3 0.0 collective-permute-done.14.refs_3_
  37.3 1.6 %collective-permute-start.10 = (bf16[256,256]{1,0:T(8,128)(2,1)S(1)}, bf16[256,256]{1,0:T(8,128)(2,1)S(1)}, u32[]{:S(2)}, u32[]{:S(2)}) collective-permute-start(bf16[256,256]{1,0:T(8,128)(2,1)S(1)} %collective-permute-done.9.refs_2_), channel_id=1, source_target_pairs={{0,2},{2,0},{4,6},{6,4},{8,10},{10,8},{12,14},{14,12},{1,3},{3,1},... | collective-permute-start | bytes 393224 | tf_op jit(solution)/shard_map/ppermute | solution.py:31
  38.9 0.0 collective-permute-done.13.refs_1_
  38.9 1.2 %shard_map.128.refs_4_ = f32[2,2,256,256]{3,2,1,0:T(8,128)S(1)} custom-call(s32[2,2]{1,0:T(2,128)} %near_any.11, bf16[8,2,32,256]{3,2,1,0:T(8,128)(2,1)S(1)} %get-tuple-element.12.v_ref, bf16[2,512,256]{2,1,0:T(8,128)(2,1)S(1)} %get-tuple-element.13.u_ref, bf16[2,2,2,256,256]{4,3,2,1,0:T(8,128)(2,1)S(1)} %copy-done, ...), custom_call_target="tpu_custom_call" | custom-call | flops 100663296 | bytes 2359312 | tf_op jit(solution)/shard_map/pallas_call | solution.py:251
  40.1 0.0 collective-permute-done.8.refs_0_
  40.1 2.4 %collective-permute-done.12.refs_3_ = bf16[256,256]{1,0:T(8,128)(2,1)S(1)} collective-permute-done((bf16[256,256]{1,0:T(8,128)(2,1)S(1)}, bf16[256,256]{1,0:T(8,128)(2,1)S(1)}, u32[]{:S(2)}, u32[]{:S(2)}) %collective-permute-start.12) | collective-permute-done | bytes 131104 | tf_op jit(solution)/shard_map/ppermute | solution.py:31
  42.5 1.3 %collective-permute-done.11.refs_2_ = bf16[256,256]{1,0:T(8,128)(2,1)S(1)} collective-permute-done((bf16[256,256]{1,0:T(8,128)(2,1)S(1)}, bf16[256,256]{1,0:T(8,128)(2,1)S(1)}, u32[]{:S(2)}, u32[]{:S(2)}) %collective-permute-start.11) | collective-permute-done | bytes 131104 | tf_op jit(solution)/shard_map/ppermute | solution.py:31
  43.7 0.1 collective-permute-done.10.refs_1_
  43.9 1.2 %shard_map.130 = bf16[2,256,256]{2,1,0:T(8,128)(2,1)S(1)} custom-call(s32[2,2]{1,0:T(2,128)} %near_any.11, bf16[8,2,32,256]{3,2,1,0:T(8,128)(2,1)S(1)} %get-tuple-element.12.v_ref, bf16[2,512,256]{2,1,0:T(8,128)(2,1)S(1)} %get-tuple-element.13.u_ref, bf16[2,2,2,256,256]{4,3,2,1,0:T(8,128)(2,1)S(1)} %copy-done, ...), custom_call_target="tpu_custom_call" | custom-call | flops 50331648 | bytes 3407888 | tf_op jit(solution)/shard_map/pallas_call | solution.py:251
  45.1 0.0 copy-start.2
  45.1 0.1 collective-permute-start.15
  45.2 0.7 %shard_map.129.own = f32[2,256,256]{2,1,0:T(8,128)S(1)} custom-call(s32[2,2]{1,0:T(2,128)} %near_any.11, bf16[8,2,32,256]{3,2,1,0:T(8,128)(2,1)S(1)} %get-tuple-element.12.v_ref, bf16[2,512,256]{2,1,0:T(8,128)(2,1)S(1)} %get-tuple-element.13.u_ref, bf16[2,2,2,256,256]{4,3,2,1,0:T(8,128)(2,1)S(1)} %copy-done, ...), custom_call_target="tpu_custom_call" | custom-call | flops 50331648 | bytes 3407888 | tf_op jit(solution)/shard_map/pallas_call | solution.py:251
  45.9 0.8 %collective-permute-done.15.other = bf16[2,256,256]{2,1,0:T(8,128)(2,1)S(1)} collective-permute-done((bf16[2,256,256]{2,1,0:T(8,128)(2,1)S(1)}, bf16[2,256,256]{2,1,0:T(8,128)(2,1)S(1)}, u32[]{:S(2)}, u32[]{:S(2)}) %collective-permute-start.15) | collective-permute-done | bytes 262176 | tf_op jit(solution)/shard_map/ppermute | solution.py:350
  46.7 0.0 copy-done.2
  46.7 2.3 %shard_map.131 = (f32[256,256]{1,0:T(8,128)}, f32[256,256]{1,0:T(8,128)}) custom-call(f32[2,256,256]{2,1,0:T(8,128)S(1)} %shard_map.129.own, bf16[2,256,256]{2,1,0:T(8,128)(2,1)S(1)} %collective-permute-done.15.other, f32[256,256]{1,0:T(8,128)S(1)} %copy-done.2, f32[256,256]{1,0:T(8,128)S(1)} %copy-done.1, f32[5,256,128]{2,1,0:T(8,128)S(1)} %get-tuple-element.16.coef, ...), custom_call_target="tpu_custom_call" | custom-call | flops 13107200 | bytes 3014656 | tf_op jit(solution)/shard_map/pallas_call | solution.py:251
Async XLA Ops:
  0.6 16.8 %copy-start = (bf16[2,2,2,256,256]{4,3,2,1,0:T(8,128)(2,1)S(1)}, bf16[2,2,2,256,256]{4,3,2,1,0:T(8,128)(2,1)}, u32[]{:S(2)}) copy-start(bf16[2,2,2,256,256]{4,3,2,1,0:T(8,128)(2,1)} %d_ref.11) | copy-start | bytes 3145732
  1.7 10.5 %collective-permute-start.1 = (bf16[256,256]{1,0:T(8,128)(2,1)S(1)}, bf16[256,256]{1,0:T(8,128)(2,1)S(1)}, u32[]{:S(2)}, u32[]{:S(2)}) collective-permute-start(bf16[256,256]{1,0:T(8,128)(2,1)S(1)} %shard_map.123.refs_0_), channel_id=1, source_target_pairs={{0,8},{2,10},{4,12},{6,14},{8,0},{10,2},{12,4},{14,6},{1,9},{3,11}... | collective-permute-start | bytes 393224 | tf_op jit(solution)/shard_map/ppermute | solution.py:31
  5.8 9.4 %collective-permute-start.6 = (bf16[256,256]{1,0:T(8,128)(2,1)S(1)}, bf16[256,256]{1,0:T(8,128)(2,1)S(1)}, u32[]{:S(2)}, u32[]{:S(2)}) collective-permute-start(bf16[256,256]{1,0:T(8,128)(2,1)S(1)} %shard_map.123.refs_0_), channel_id=1, source_target_pairs={{0,4},{2,6},{4,0},{6,2},{8,12},{10,14},{12,8},{14,10},{1,5},{3,7},... | collective-permute-start | bytes 393224 | tf_op jit(solution)/shard_map/ppermute | solution.py:31
  7.4 10.1 %collective-permute-start.5 = (bf16[256,256]{1,0:T(8,128)(2,1)S(1)}, bf16[256,256]{1,0:T(8,128)(2,1)S(1)}, u32[]{:S(2)}, u32[]{:S(2)}) collective-permute-start(bf16[256,256]{1,0:T(8,128)(2,1)S(1)} %shard_map.123.refs_0_), channel_id=1, source_target_pairs={{0,2},{2,0},{4,6},{6,4},{8,10},{10,8},{12,14},{14,12},{1,3},{3,1},... | collective-permute-start | bytes 393224 | tf_op jit(solution)/shard_map/ppermute | solution.py:31
  8.9 9.8 %collective-permute-start = (bf16[256,256]{1,0:T(8,128)(2,1)S(1)}, bf16[256,256]{1,0:T(8,128)(2,1)S(1)}, u32[]{:S(2)}, u32[]{:S(2)}) collective-permute-start(bf16[256,256]{1,0:T(8,128)(2,1)S(1)} %shard_map.123.refs_0_), channel_id=1, source_target_pairs={{0,6},{2,4},{4,2},{6,0},{8,14},{10,12},{12,10},{14,8},{1,7},{3,5},... | collective-permute-start | bytes 393224 | tf_op jit(solution)/shard_map/ppermute | solution.py:31
  12.2 7.7 %collective-permute-start.4 = (bf16[256,256]{1,0:T(8,128)(2,1)S(1)}, bf16[256,256]{1,0:T(8,128)(2,1)S(1)}, u32[]{:S(2)}, u32[]{:S(2)}) collective-permute-start(bf16[256,256]{1,0:T(8,128)(2,1)S(1)} %collective-permute-done.1.refs_2_), channel_id=1, source_target_pairs={{0,6},{2,4},{4,2},{6,0},{8,14},{10,12},{12,10},{14,8},{1,7},{3,5},... | collective-permute-start | bytes 393224 | tf_op jit(solution)/shard_map/ppermute | solution.py:31
  13.8 7.0 %collective-permute-start.3 = (bf16[256,256]{1,0:T(8,128)(2,1)S(1)}, bf16[256,256]{1,0:T(8,128)(2,1)S(1)}, u32[]{:S(2)}, u32[]{:S(2)}) collective-permute-start(bf16[256,256]{1,0:T(8,128)(2,1)S(1)} %collective-permute-done.1.refs_2_), channel_id=1, source_target_pairs={{0,4},{2,6},{4,0},{6,2},{8,12},{10,14},{12,8},{14,10},{1,5},{3,7},... | collective-permute-start | bytes 393224 | tf_op jit(solution)/shard_map/ppermute | solution.py:31
  15.3 6.6 %collective-permute-start.2 = (bf16[256,256]{1,0:T(8,128)(2,1)S(1)}, bf16[256,256]{1,0:T(8,128)(2,1)S(1)}, u32[]{:S(2)}, u32[]{:S(2)}) collective-permute-start(bf16[256,256]{1,0:T(8,128)(2,1)S(1)} %collective-permute-done.1.refs_2_), channel_id=1, source_target_pairs={{0,2},{2,0},{4,6},{6,4},{8,10},{10,8},{12,14},{14,12},{1,3},{3,1},... | collective-permute-start | bytes 393224 | tf_op jit(solution)/shard_map/ppermute | solution.py:31
  23.1 1.6 %copy-start.1 = (f32[256,256]{1,0:T(8,128)S(1)}, f32[256,256]{1,0:T(8,128)}, u32[]{:S(2)}) copy-start(f32[256,256]{1,0:T(8,128)} %tau.3) | copy-start | bytes 786436
  23.1 1.6 %collective-permute-start.7 = (bf16[2,256,256]{2,1,0:T(8,128)(2,1)S(1)}, bf16[2,256,256]{2,1,0:T(8,128)(2,1)S(1)}, u32[]{:S(2)}, u32[]{:S(2)}) collective-permute-start(bf16[2,256,256]{2,1,0:T(8,128)(2,1)S(1)} %shard_map.126), channel_id=1, source_target_pairs={{0,1},{1,0},{2,3},{3,2},{4,5},{5,4},{6,7},{7,6},{8,9},{9,8},{10,11... | collective-permute-start | bytes 786440 | tf_op jit(solution)/shard_map/ppermute | solution.py:350
  26.0 9.4 %collective-permute-start.9 = (bf16[256,256]{1,0:T(8,128)(2,1)S(1)}, bf16[256,256]{1,0:T(8,128)(2,1)S(1)}, u32[]{:S(2)}, u32[]{:S(2)}) collective-permute-start(bf16[256,256]{1,0:T(8,128)(2,1)S(1)} %get-tuple-element.17.refs_0_), channel_id=1, source_target_pairs={{0,8},{2,10},{4,12},{6,14},{8,0},{10,2},{12,4},{14,6},{1,9},{3,11}... | collective-permute-start | bytes 393224 | tf_op jit(solution)/shard_map/ppermute | solution.py:31
  27.5 9.8 %collective-permute-start.14 = (bf16[256,256]{1,0:T(8,128)(2,1)S(1)}, bf16[256,256]{1,0:T(8,128)(2,1)S(1)}, u32[]{:S(2)}, u32[]{:S(2)}) collective-permute-start(bf16[256,256]{1,0:T(8,128)(2,1)S(1)} %get-tuple-element.17.refs_0_), channel_id=1, source_target_pairs={{0,4},{2,6},{4,0},{6,2},{8,12},{10,14},{12,8},{14,10},{1,5},{3,7},... | collective-permute-start | bytes 393224 | tf_op jit(solution)/shard_map/ppermute | solution.py:31
  29.4 9.5 %collective-permute-start.13 = (bf16[256,256]{1,0:T(8,128)(2,1)S(1)}, bf16[256,256]{1,0:T(8,128)(2,1)S(1)}, u32[]{:S(2)}, u32[]{:S(2)}) collective-permute-start(bf16[256,256]{1,0:T(8,128)(2,1)S(1)} %get-tuple-element.17.refs_0_), channel_id=1, source_target_pairs={{0,2},{2,0},{4,6},{6,4},{8,10},{10,8},{12,14},{14,12},{1,3},{3,1},... | collective-permute-start | bytes 393224 | tf_op jit(solution)/shard_map/ppermute | solution.py:31
  30.9 9.2 %collective-permute-start.8 = (bf16[256,256]{1,0:T(8,128)(2,1)S(1)}, bf16[256,256]{1,0:T(8,128)(2,1)S(1)}, u32[]{:S(2)}, u32[]{:S(2)}) collective-permute-start(bf16[256,256]{1,0:T(8,128)(2,1)S(1)} %get-tuple-element.17.refs_0_), channel_id=1, source_target_pairs={{0,6},{2,4},{4,2},{6,0},{8,14},{10,12},{12,10},{14,8},{1,7},{3,5},... | collective-permute-start | bytes 393224 | tf_op jit(solution)/shard_map/ppermute | solution.py:31
  35.4 7.1 %collective-permute-start.12 = (bf16[256,256]{1,0:T(8,128)(2,1)S(1)}, bf16[256,256]{1,0:T(8,128)(2,1)S(1)}, u32[]{:S(2)}, u32[]{:S(2)}) collective-permute-start(bf16[256,256]{1,0:T(8,128)(2,1)S(1)} %collective-permute-done.9.refs_2_), channel_id=1, source_target_pairs={{0,6},{2,4},{4,2},{6,0},{8,14},{10,12},{12,10},{14,8},{1,7},{3,5},... | collective-permute-start | bytes 393224 | tf_op jit(solution)/shard_map/ppermute | solution.py:31
  35.4 8.3 %collective-permute-start.11 = (bf16[256,256]{1,0:T(8,128)(2,1)S(1)}, bf16[256,256]{1,0:T(8,128)(2,1)S(1)}, u32[]{:S(2)}, u32[]{:S(2)}) collective-permute-start(bf16[256,256]{1,0:T(8,128)(2,1)S(1)} %collective-permute-done.9.refs_2_), channel_id=1, source_target_pairs={{0,4},{2,6},{4,0},{6,2},{8,12},{10,14},{12,8},{14,10},{1,5},{3,7},... | collective-permute-start | bytes 393224 | tf_op jit(solution)/shard_map/ppermute | solution.py:31
  37.3 6.6 %collective-permute-start.10 = (bf16[256,256]{1,0:T(8,128)(2,1)S(1)}, bf16[256,256]{1,0:T(8,128)(2,1)S(1)}, u32[]{:S(2)}, u32[]{:S(2)}) collective-permute-start(bf16[256,256]{1,0:T(8,128)(2,1)S(1)} %collective-permute-done.9.refs_2_), channel_id=1, source_target_pairs={{0,2},{2,0},{4,6},{6,4},{8,10},{10,8},{12,14},{14,12},{1,3},{3,1},... | collective-permute-start | bytes 393224 | tf_op jit(solution)/shard_map/ppermute | solution.py:31
  45.1 1.6 %copy-start.2 = (f32[256,256]{1,0:T(8,128)S(1)}, f32[256,256]{1,0:T(8,128)}, u32[]{:S(2)}) copy-start(f32[256,256]{1,0:T(8,128)} %state.1) | copy-start | bytes 786436
  45.1 1.6 %collective-permute-start.15 = (bf16[2,256,256]{2,1,0:T(8,128)(2,1)S(1)}, bf16[2,256,256]{2,1,0:T(8,128)(2,1)S(1)}, u32[]{:S(2)}, u32[]{:S(2)}) collective-permute-start(bf16[2,256,256]{2,1,0:T(8,128)(2,1)S(1)} %shard_map.130), channel_id=1, source_target_pairs={{0,1},{1,0},{2,3},{3,2},{4,5},{5,4},{6,7},{7,6},{8,9},{9,8},{10,11... | collective-permute-start | bytes 786440 | tf_op jit(solution)/shard_map/ppermute | solution.py:350

commit v9 on v8

--- a/solution.py
+++ b/solution.py
@@ -19,7 +19,7 @@
 def arrivals(count, direct):
     if not direct:
         return list(range(count))
-    return [0, 1, 4, 2, 3, 5, 6, 7] if count == 8 else [0, 1, 2, 3]
+    return [0, 1, 2, 4, 3, 7, 5, 6] if count == 8 else [0, 1, 2, 3]
 
 
 def row_met(spot, row, direct):
@@ -31,10 +31,10 @@
         return lax.ppermute(data, "row", [(row, row ^ mask) for row in range(count)])
 
     found = {0: block}
-    for mask in (4, 1, 2, 3) if count == 8 else (1, 2, 3):
+    for mask in (4, 1, 2, 3, 7) if count == 8 else (1, 2, 3):
         found[mask] = swapped(mask, block)
     if count == 8:
-        for mask in (1, 2, 3):
+        for mask in (1, 2):
             found[4 + mask] = swapped(mask, found[4])
     return [found[mask] for mask in arrivals(count, True)]
 

time: 49 us -> 51.1 us (1.043)
  waiting for transfers between devices: 15.9 us -> 18.8 us
  starting transfers between devices: 19.7 us -> 18.6 us
    ppermute x14, waiting for transfers between devices: 14.3 us -> 17.5 us  [swapped(): lax.ppermute(data, 'row', [(row, row ^ mask) for row in range(count)])]
    ppermute x14, starting transfers between devices: 19.5 us -> 18.3 us  [swapped(): lax.ppermute(data, 'row', [(row, row ^ mask) for row in range(count)])]
  transfers between devices with their start and end apart: 16 -> 16, of which waited for: 10 -> 11; matrix products, arithmetic and copies ran while one was open for 0% -> 0% of each run, Pallas kernels for 11% -> 12%
where the time goes in v9:
time: 51.1 us; the launch traced here: 50.9 us
  waiting for transfers between devices  18.8 us (37%)
  starting transfers between devices  18.6 us (36%)
  Pallas kernels  12.6 us (25%)
  between operations  0.78 us (2%)
    ppermute x14, starting transfers between devices, swapped(): lax.ppermute(data, 'row', [(row, row ^ mask) for row in range(count)])  18.3 us
    ppermute x14, waiting for transfers between devices, swapped(): lax.ppermute(data, 'row', [(row, row ^ mask) for row in range(count)])  17.5 us
    pallas_call x10, Pallas kernels, on_core(): pl.pallas_call(kernel, out_shape=outs, in_specs=[hbm] * len(far) + [vmem]...  12.6 us
    ppermute x2, waiting for transfers between devices, lattice(): lax.ppermute(add(blocks[early:], early, 1, sums, narrow), 'col', swap)  1.33 us
  transfers between devices with their start and end apart: 16, of which 11 were waited for; matrix products, arithmetic and copies ran while one was open for 0% of the time, Pallas kernels for 12%

profile of v9, /device:TPU:0, one launch (start us, length us, event | category | flops | bytes accessed | tf_op | source)
XLA Modules:
  0.0 50.9 jit_solution(3629728946318709368)
XLA Ops:
  0.6 0.0 copy-start
  0.6 1.1 %shard_map.123.refs_0_ = bf16[256,256]{1,0:T(8,128)(2,1)S(1)} custom-call(f32[256,256]{1,0:T(8,128)} %wide_ref.1), custom_call_target="tpu_custom_call" | custom-call | bytes 262144 | tf_op jit(solution)/shard_map/pallas_call | solution.py:251
  1.7 4.1 %collective-permute-start.2 = (bf16[256,256]{1,0:T(8,128)(2,1)S(1)}, bf16[256,256]{1,0:T(8,128)(2,1)S(1)}, u32[]{:S(2)}, u32[]{:S(2)}) collective-permute-start(bf16[256,256]{1,0:T(8,128)(2,1)S(1)} %shard_map.123.refs_0_), channel_id=1, source_target_pairs={{0,8},{2,10},{4,12},{6,14},{8,0},{10,2},{12,4},{14,6},{1,9},{3,11}... | collective-permute-start | bytes 393224 | tf_op jit(solution)/shard_map/ppermute | solution.py:31
  5.8 1.6 %collective-permute-start.6 = (bf16[256,256]{1,0:T(8,128)(2,1)S(1)}, bf16[256,256]{1,0:T(8,128)(2,1)S(1)}, u32[]{:S(2)}, u32[]{:S(2)}) collective-permute-start(bf16[256,256]{1,0:T(8,128)(2,1)S(1)} %shard_map.123.refs_0_), channel_id=1, source_target_pairs={{0,4},{2,6},{4,0},{6,2},{8,12},{10,14},{12,8},{14,10},{1,5},{3,7},... | collective-permute-start | bytes 393224 | tf_op jit(solution)/shard_map/ppermute | solution.py:31
  7.4 1.5 %collective-permute-start.5 = (bf16[256,256]{1,0:T(8,128)(2,1)S(1)}, bf16[256,256]{1,0:T(8,128)(2,1)S(1)}, u32[]{:S(2)}, u32[]{:S(2)}) collective-permute-start(bf16[256,256]{1,0:T(8,128)(2,1)S(1)} %shard_map.123.refs_0_), channel_id=1, source_target_pairs={{0,2},{2,0},{4,6},{6,4},{8,10},{10,8},{12,14},{14,12},{1,3},{3,1},... | collective-permute-start | bytes 393224 | tf_op jit(solution)/shard_map/ppermute | solution.py:31
  8.9 0.0 collective-permute-start.1
  8.9 1.8 %collective-permute-start = (bf16[256,256]{1,0:T(8,128)(2,1)S(1)}, bf16[256,256]{1,0:T(8,128)(2,1)S(1)}, u32[]{:S(2)}, u32[]{:S(2)}) collective-permute-start(bf16[256,256]{1,0:T(8,128)(2,1)S(1)} %shard_map.123.refs_0_), channel_id=1, source_target_pairs={{0,6},{2,4},{4,2},{6,0},{8,14},{10,12},{12,10},{14,8},{1,7},{3,5},... | collective-permute-start | bytes 393224 | tf_op jit(solution)/shard_map/ppermute | solution.py:31
  10.7 2.9 %collective-permute-done.2.refs_3_ = bf16[256,256]{1,0:T(8,128)(2,1)S(1)} collective-permute-done((bf16[256,256]{1,0:T(8,128)(2,1)S(1)}, bf16[256,256]{1,0:T(8,128)(2,1)S(1)}, u32[]{:S(2)}, u32[]{:S(2)}) %collective-permute-start.2) | collective-permute-done | bytes 131104 | tf_op jit(solution)/shard_map/ppermute | solution.py:31
  13.6 0.3 collective-permute-start.4
  13.8 0.0 collective-permute-done.6.refs_2_
  13.8 1.9 %collective-permute-start.3 = (bf16[256,256]{1,0:T(8,128)(2,1)S(1)}, bf16[256,256]{1,0:T(8,128)(2,1)S(1)}, u32[]{:S(2)}, u32[]{:S(2)}) collective-permute-start(bf16[256,256]{1,0:T(8,128)(2,1)S(1)} %collective-permute-done.2.refs_3_), channel_id=1, source_target_pairs={{0,2},{2,0},{4,6},{6,4},{8,10},{10,8},{12,14},{14,12},{1,3},{3,1},... | collective-permute-start | bytes 393224 | tf_op jit(solution)/shard_map/ppermute | solution.py:31
  15.8 1.7 %shard_map.122 = (bf16[8,2,32,256]{3,2,1,0:T(8,128)(2,1)S(1)}, bf16[2,512,256]{2,1,0:T(8,128)(2,1)S(1)}, f32[5,256,128]{2,1,0:T(8,128)S(1)}, f32[256,256]{1,0:T(8,128)S(1)}, f32[256,256]{1,0:T(8,128)S(1)}) custom-call(s32[2,8]{1,0:T(2,128)} %refs_0_.1, bf16[2,8,32,256]{3,2,1,0:T(8,128)(2,1)} %refs_1_.1, bf16[2,2,8,32,256]{4,3,2,1,0:T(8,128)(2,1)} %refs_2_.1, ...), custom_call_target="tpu_custom_call" | custom-call | bytes 1051712 | tf_op jit(solution)/shard_map/pallas_call | solution.py:251
  17.5 0.0 collective-permute-done.5.refs_1_
  17.5 0.0 copy-done
  17.5 1.4 %shard_map.124.refs_4_ = f32[2,2,256,256]{3,2,1,0:T(8,128)S(1)} custom-call(s32[2,2]{1,0:T(2,128)} %near_any.11, bf16[8,2,32,256]{3,2,1,0:T(8,128)(2,1)S(1)} %get-tuple-element.12.v_ref, bf16[2,512,256]{2,1,0:T(8,128)(2,1)S(1)} %get-tuple-element.13.u_ref, bf16[2,2,2,256,256]{4,3,2,1,0:T(8,128)(2,1)S(1)} %copy-done, ...), custom_call_target="tpu_custom_call" | custom-call | flops 100663296 | bytes 2359312 | tf_op jit(solution)/shard_map/pallas_call | solution.py:251
  18.9 0.0 collective-permute-done.1.refs_1_
  18.9 1.0 %collective-permute-done.refs_0_ = bf16[256,256]{1,0:T(8,128)(2,1)S(1)} collective-permute-done((bf16[256,256]{1,0:T(8,128)(2,1)S(1)}, bf16[256,256]{1,0:T(8,128)(2,1)S(1)}, u32[]{:S(2)}, u32[]{:S(2)}) %collective-permute-start) | collective-permute-done | bytes 131104 | tf_op jit(solution)/shard_map/ppermute | solution.py:31
  19.9 0.9 %collective-permute-done.4.refs_3_ = bf16[256,256]{1,0:T(8,128)(2,1)S(1)} collective-permute-done((bf16[256,256]{1,0:T(8,128)(2,1)S(1)}, bf16[256,256]{1,0:T(8,128)(2,1)S(1)}, u32[]{:S(2)}, u32[]{:S(2)}) %collective-permute-start.4) | collective-permute-done | bytes 131104 | tf_op jit(solution)/shard_map/ppermute | solution.py:31
  20.9 1.0 %collective-permute-done.3.refs_2_ = bf16[256,256]{1,0:T(8,128)(2,1)S(1)} collective-permute-done((bf16[256,256]{1,0:T(8,128)(2,1)S(1)}, bf16[256,256]{1,0:T(8,128)(2,1)S(1)}, u32[]{:S(2)}, u32[]{:S(2)}) %collective-permute-start.3) | collective-permute-done | bytes 131104 | tf_op jit(solution)/shard_map/ppermute | solution.py:31
  21.9 1.0 %shard_map.126 = bf16[2,256,256]{2,1,0:T(8,128)(2,1)S(1)} custom-call(s32[2,2]{1,0:T(2,128)} %near_any.11, bf16[8,2,32,256]{3,2,1,0:T(8,128)(2,1)S(1)} %get-tuple-element.12.v_ref, bf16[2,512,256]{2,1,0:T(8,128)(2,1)S(1)} %get-tuple-element.13.u_ref, bf16[2,2,2,256,256]{4,3,2,1,0:T(8,128)(2,1)S(1)} %copy-done, ...), custom_call_target="tpu_custom_call" | custom-call | flops 50331648 | bytes 3407888 | tf_op jit(solution)/shard_map/pallas_call | solution.py:251
  22.9 0.0 copy-start.1
  22.9 0.3 collective-permute-start.7
  23.2 0.7 %shard_map.125.own = f32[2,256,256]{2,1,0:T(8,128)S(1)} custom-call(s32[2,2]{1,0:T(2,128)} %near_any.11, bf16[8,2,32,256]{3,2,1,0:T(8,128)(2,1)S(1)} %get-tuple-element.12.v_ref, bf16[2,512,256]{2,1,0:T(8,128)(2,1)S(1)} %get-tuple-element.13.u_ref, bf16[2,2,2,256,256]{4,3,2,1,0:T(8,128)(2,1)S(1)} %copy-done, ...), custom_call_target="tpu_custom_call" | custom-call | flops 50331648 | bytes 3407888 | tf_op jit(solution)/shard_map/pallas_call | solution.py:251
  23.9 0.6 %collective-permute-done.7.other = bf16[2,256,256]{2,1,0:T(8,128)(2,1)S(1)} collective-permute-done((bf16[2,256,256]{2,1,0:T(8,128)(2,1)S(1)}, bf16[2,256,256]{2,1,0:T(8,128)(2,1)S(1)}, u32[]{:S(2)}, u32[]{:S(2)}) %collective-permute-start.7) | collective-permute-done | bytes 262176 | tf_op jit(solution)/shard_map/ppermute | solution.py:350
  24.5 0.0 copy-done.1
  24.5 1.3 %shard_map.127 = (f32[256,256]{1,0:T(8,128)S(1)}, f32[256,256]{1,0:T(8,128)S(1)}, f32[256,256]{1,0:T(8,128)S(1)}, f32[256,256]{1,0:T(8,128)S(1)}, bf16[256,256]{1,0:T(8,128)(2,1)S(1)}) custom-call(f32[2,256,256]{2,1,0:T(8,128)S(1)} %shard_map.125.own, bf16[2,256,256]{2,1,0:T(8,128)(2,1)S(1)} %collective-permute-done.7.other, ...), custom_call_target="tpu_custom_call" | custom-call | flops 13107200 | bytes 2228224 | tf_op jit(solution)/shard_map/pallas_call | solution.py:251
  25.8 3.6 %collective-permute-start.10 = (bf16[256,256]{1,0:T(8,128)(2,1)S(1)}, bf16[256,256]{1,0:T(8,128)(2,1)S(1)}, u32[]{:S(2)}, u32[]{:S(2)}) collective-permute-start(bf16[256,256]{1,0:T(8,128)(2,1)S(1)} %get-tuple-element.17.refs_0_), channel_id=1, source_target_pairs={{0,8},{2,10},{4,12},{6,14},{8,0},{10,2},{12,4},{14,6},{1,9},{3,11}... | collective-permute-start | bytes 393224 | tf_op jit(solution)/shard_map/ppermute | solution.py:31
  29.4 0.0 collective-permute-start.14
  29.4 0.8 %collective-permute-start.13 = (bf16[256,256]{1,0:T(8,128)(2,1)S(1)}, bf16[256,256]{1,0:T(8,128)(2,1)S(1)}, u32[]{:S(2)}, u32[]{:S(2)}) collective-permute-start(bf16[256,256]{1,0:T(8,128)(2,1)S(1)} %get-tuple-element.17.refs_0_), channel_id=1, source_target_pairs={{0,2},{2,0},{4,6},{6,4},{8,10},{10,8},{12,14},{14,12},{1,3},{3,1},... | collective-permute-start | bytes 393224 | tf_op jit(solution)/shard_map/ppermute | solution.py:31
  30.2 2.2 %collective-permute-start.9 = (bf16[256,256]{1,0:T(8,128)(2,1)S(1)}, bf16[256,256]{1,0:T(8,128)(2,1)S(1)}, u32[]{:S(2)}, u32[]{:S(2)}) collective-permute-start(bf16[256,256]{1,0:T(8,128)(2,1)S(1)} %get-tuple-element.17.refs_0_), channel_id=1, source_target_pairs={{0,14},{2,12},{4,10},{6,8},{8,6},{10,4},{12,2},{14,0},{1,15},{3,13... | collective-permute-start | bytes 393224 | tf_op jit(solution)/shard_map/ppermute | solution.py:31
  32.4 0.5 collective-permute-start.8
  32.9 4.0 %collective-permute-done.10.refs_3_ = bf16[256,256]{1,0:T(8,128)(2,1)S(1)} collective-permute-done((bf16[256,256]{1,0:T(8,128)(2,1)S(1)}, bf16[256,256]{1,0:T(8,128)(2,1)S(1)}, u32[]{:S(2)}, u32[]{:S(2)}) %collective-permute-start.10) | collective-permute-done | bytes 131104 | tf_op jit(solution)/shard_map/ppermute | solution.py:31
  36.9 0.0 collective-permute-start.12
  36.9 4.2 %collective-permute-done.14.refs_2_ = bf16[256,256]{1,0:T(8,128)(2,1)S(1)} collective-permute-done((bf16[256,256]{1,0:T(8,128)(2,1)S(1)}, bf16[256,256]{1,0:T(8,128)(2,1)S(1)}, u32[]{:S(2)}, u32[]{:S(2)}) %collective-permute-start.14) | collective-permute-done | bytes 131104 | tf_op jit(solution)/shard_map/ppermute | solution.py:31
  41.0 0.0 collective-permute-start.11
  41.0 0.0 collective-permute-done.13.refs_1_
  41.1 1.4 %shard_map.128.refs_4_ = f32[2,2,256,256]{3,2,1,0:T(8,128)S(1)} custom-call(s32[2,2]{1,0:T(2,128)} %near_any.11, bf16[8,2,32,256]{3,2,1,0:T(8,128)(2,1)S(1)} %get-tuple-element.12.v_ref, bf16[2,512,256]{2,1,0:T(8,128)(2,1)S(1)} %get-tuple-element.13.u_ref, bf16[2,2,2,256,256]{4,3,2,1,0:T(8,128)(2,1)S(1)} %copy-done, ...), custom_call_target="tpu_custom_call" | custom-call | flops 100663296 | bytes 2359312 | tf_op jit(solution)/shard_map/pallas_call | solution.py:251
  42.5 0.0 collective-permute-done.9.refs_1_
  42.5 0.6 %collective-permute-done.8.refs_0_ = bf16[256,256]{1,0:T(8,128)(2,1)S(1)} collective-permute-done((bf16[256,256]{1,0:T(8,128)(2,1)S(1)}, bf16[256,256]{1,0:T(8,128)(2,1)S(1)}, u32[]{:S(2)}, u32[]{:S(2)}) %collective-permute-start.8) | collective-permute-done | bytes 131104 | tf_op jit(solution)/shard_map/ppermute | solution.py:31
  43.1 2.7 %collective-permute-done.12.refs_3_ = bf16[256,256]{1,0:T(8,128)(2,1)S(1)} collective-permute-done((bf16[256,256]{1,0:T(8,128)(2,1)S(1)}, bf16[256,256]{1,0:T(8,128)(2,1)S(1)}, u32[]{:S(2)}, u32[]{:S(2)}) %collective-permute-start.12) | collective-permute-done | bytes 131104 | tf_op jit(solution)/shard_map/ppermute | solution.py:31
  45.8 0.2 collective-permute-done.11.refs_2_
  46.0 1.0 %shard_map.130 = bf16[2,256,256]{2,1,0:T(8,128)(2,1)S(1)} custom-call(s32[2,2]{1,0:T(2,128)} %near_any.11, bf16[8,2,32,256]{3,2,1,0:T(8,128)(2,1)S(1)} %get-tuple-element.12.v_ref, bf16[2,512,256]{2,1,0:T(8,128)(2,1)S(1)} %get-tuple-element.13.u_ref, bf16[2,2,2,256,256]{4,3,2,1,0:T(8,128)(2,1)S(1)} %copy-done, ...), custom_call_target="tpu_custom_call" | custom-call | flops 50331648 | bytes 3407888 | tf_op jit(solution)/shard_map/pallas_call | solution.py:251
  47.0 0.0 copy-start.2
  47.0 0.1 collective-permute-start.15
  47.1 0.7 %shard_map.129.own = f32[2,256,256]{2,1,0:T(8,128)S(1)} custom-call(s32[2,2]{1,0:T(2,128)} %near_any.11, bf16[8,2,32,256]{3,2,1,0:T(8,128)(2,1)S(1)} %get-tuple-element.12.v_ref, bf16[2,512,256]{2,1,0:T(8,128)(2,1)S(1)} %get-tuple-element.13.u_ref, bf16[2,2,2,256,256]{4,3,2,1,0:T(8,128)(2,1)S(1)} %copy-done, ...), custom_call_target="tpu_custom_call" | custom-call | flops 50331648 | bytes 3407888 | tf_op jit(solution)/shard_map/pallas_call | solution.py:251
  47.8 0.8 %collective-permute-done.15.other = bf16[2,256,256]{2,1,0:T(8,128)(2,1)S(1)} collective-permute-done((bf16[2,256,256]{2,1,0:T(8,128)(2,1)S(1)}, bf16[2,256,256]{2,1,0:T(8,128)(2,1)S(1)}, u32[]{:S(2)}, u32[]{:S(2)}) %collective-permute-start.15) | collective-permute-done | bytes 262176 | tf_op jit(solution)/shard_map/ppermute | solution.py:350
  48.6 0.0 copy-done.2
  48.6 2.3 %shard_map.131 = (f32[256,256]{1,0:T(8,128)}, f32[256,256]{1,0:T(8,128)}) custom-call(f32[2,256,256]{2,1,0:T(8,128)S(1)} %shard_map.129.own, bf16[2,256,256]{2,1,0:T(8,128)(2,1)S(1)} %collective-permute-done.15.other, f32[256,256]{1,0:T(8,128)S(1)} %copy-done.2, f32[256,256]{1,0:T(8,128)S(1)} %copy-done.1, f32[5,256,128]{2,1,0:T(8,128)S(1)} %get-tuple-element.16.coef, ...), custom_call_target="tpu_custom_call" | custom-call | flops 13107200 | bytes 3014656 | tf_op jit(solution)/shard_map/pallas_call | solution.py:251
Async XLA Ops:
  0.6 16.9 %copy-start = (bf16[2,2,2,256,256]{4,3,2,1,0:T(8,128)(2,1)S(1)}, bf16[2,2,2,256,256]{4,3,2,1,0:T(8,128)(2,1)}, u32[]{:S(2)}) copy-start(bf16[2,2,2,256,256]{4,3,2,1,0:T(8,128)(2,1)} %d_ref.11) | copy-start | bytes 3145732
  1.7 11.9 %collective-permute-start.2 = (bf16[256,256]{1,0:T(8,128)(2,1)S(1)}, bf16[256,256]{1,0:T(8,128)(2,1)S(1)}, u32[]{:S(2)}, u32[]{:S(2)}) collective-permute-start(bf16[256,256]{1,0:T(8,128)(2,1)S(1)} %shard_map.123.refs_0_), channel_id=1, source_target_pairs={{0,8},{2,10},{4,12},{6,14},{8,0},{10,2},{12,4},{14,6},{1,9},{3,11}... | collective-permute-start | bytes 393224 | tf_op jit(solution)/shard_map/ppermute | solution.py:31
  5.8 8.0 %collective-permute-start.6 = (bf16[256,256]{1,0:T(8,128)(2,1)S(1)}, bf16[256,256]{1,0:T(8,128)(2,1)S(1)}, u32[]{:S(2)}, u32[]{:S(2)}) collective-permute-start(bf16[256,256]{1,0:T(8,128)(2,1)S(1)} %shard_map.123.refs_0_), channel_id=1, source_target_pairs={{0,4},{2,6},{4,0},{6,2},{8,12},{10,14},{12,8},{14,10},{1,5},{3,7},... | collective-permute-start | bytes 393224 | tf_op jit(solution)/shard_map/ppermute | solution.py:31
  7.4 10.1 %collective-permute-start.5 = (bf16[256,256]{1,0:T(8,128)(2,1)S(1)}, bf16[256,256]{1,0:T(8,128)(2,1)S(1)}, u32[]{:S(2)}, u32[]{:S(2)}) collective-permute-start(bf16[256,256]{1,0:T(8,128)(2,1)S(1)} %shard_map.123.refs_0_), channel_id=1, source_target_pairs={{0,2},{2,0},{4,6},{6,4},{8,10},{10,8},{12,14},{14,12},{1,3},{3,1},... | collective-permute-start | bytes 393224 | tf_op jit(solution)/shard_map/ppermute | solution.py:31
  8.9 10.0 %collective-permute-start.1 = (bf16[256,256]{1,0:T(8,128)(2,1)S(1)}, bf16[256,256]{1,0:T(8,128)(2,1)S(1)}, u32[]{:S(2)}, u32[]{:S(2)}) collective-permute-start(bf16[256,256]{1,0:T(8,128)(2,1)S(1)} %shard_map.123.refs_0_), channel_id=1, source_target_pairs={{0,14},{2,12},{4,10},{6,8},{8,6},{10,4},{12,2},{14,0},{1,15},{3,13... | collective-permute-start | bytes 393224 | tf_op jit(solution)/shard_map/ppermute | solution.py:31
  8.9 11.0 %collective-permute-start = (bf16[256,256]{1,0:T(8,128)(2,1)S(1)}, bf16[256,256]{1,0:T(8,128)(2,1)S(1)}, u32[]{:S(2)}, u32[]{:S(2)}) collective-permute-start(bf16[256,256]{1,0:T(8,128)(2,1)S(1)} %shard_map.123.refs_0_), channel_id=1, source_target_pairs={{0,6},{2,4},{4,2},{6,0},{8,14},{10,12},{12,10},{14,8},{1,7},{3,5},... | collective-permute-start | bytes 393224 | tf_op jit(solution)/shard_map/ppermute | solution.py:31
  13.6 7.3 %collective-permute-start.4 = (bf16[256,256]{1,0:T(8,128)(2,1)S(1)}, bf16[256,256]{1,0:T(8,128)(2,1)S(1)}, u32[]{:S(2)}, u32[]{:S(2)}) collective-permute-start(bf16[256,256]{1,0:T(8,128)(2,1)S(1)} %collective-permute-done.2.refs_3_), channel_id=1, source_target_pairs={{0,4},{2,6},{4,0},{6,2},{8,12},{10,14},{12,8},{14,10},{1,5},{3,7},... | collective-permute-start | bytes 393224 | tf_op jit(solution)/shard_map/ppermute | solution.py:31
  13.8 8.0 %collective-permute-start.3 = (bf16[256,256]{1,0:T(8,128)(2,1)S(1)}, bf16[256,256]{1,0:T(8,128)(2,1)S(1)}, u32[]{:S(2)}, u32[]{:S(2)}) collective-permute-start(bf16[256,256]{1,0:T(8,128)(2,1)S(1)} %collective-permute-done.2.refs_3_), channel_id=1, source_target_pairs={{0,2},{2,0},{4,6},{6,4},{8,10},{10,8},{12,14},{14,12},{1,3},{3,1},... | collective-permute-start | bytes 393224 | tf_op jit(solution)/shard_map/ppermute | solution.py:31
  22.9 1.6 %copy-start.1 = (f32[256,256]{1,0:T(8,128)S(1)}, f32[256,256]{1,0:T(8,128)}, u32[]{:S(2)}) copy-start(f32[256,256]{1,0:T(8,128)} %tau.3) | copy-start | bytes 786436
  22.9 1.6 %collective-permute-start.7 = (bf16[2,256,256]{2,1,0:T(8,128)(2,1)S(1)}, bf16[2,256,256]{2,1,0:T(8,128)(2,1)S(1)}, u32[]{:S(2)}, u32[]{:S(2)}) collective-permute-start(bf16[2,256,256]{2,1,0:T(8,128)(2,1)S(1)} %shard_map.126), channel_id=1, source_target_pairs={{0,1},{1,0},{2,3},{3,2},{4,5},{5,4},{6,7},{7,6},{8,9},{9,8},{10,11... | collective-permute-start | bytes 786440 | tf_op jit(solution)/shard_map/ppermute | solution.py:350
  25.8 11.1 %collective-permute-start.10 = (bf16[256,256]{1,0:T(8,128)(2,1)S(1)}, bf16[256,256]{1,0:T(8,128)(2,1)S(1)}, u32[]{:S(2)}, u32[]{:S(2)}) collective-permute-start(bf16[256,256]{1,0:T(8,128)(2,1)S(1)} %get-tuple-element.17.refs_0_), channel_id=1, source_target_pairs={{0,8},{2,10},{4,12},{6,14},{8,0},{10,2},{12,4},{14,6},{1,9},{3,11}... | collective-permute-start | bytes 393224 | tf_op jit(solution)/shard_map/ppermute | solution.py:31
  29.4 11.7 %collective-permute-start.14 = (bf16[256,256]{1,0:T(8,128)(2,1)S(1)}, bf16[256,256]{1,0:T(8,128)(2,1)S(1)}, u32[]{:S(2)}, u32[]{:S(2)}) collective-permute-start(bf16[256,256]{1,0:T(8,128)(2,1)S(1)} %get-tuple-element.17.refs_0_), channel_id=1, source_target_pairs={{0,4},{2,6},{4,0},{6,2},{8,12},{10,14},{12,8},{14,10},{1,5},{3,7},... | collective-permute-start | bytes 393224 | tf_op jit(solution)/shard_map/ppermute | solution.py:31
  29.4 11.7 %collective-permute-start.13 = (bf16[256,256]{1,0:T(8,128)(2,1)S(1)}, bf16[256,256]{1,0:T(8,128)(2,1)S(1)}, u32[]{:S(2)}, u32[]{:S(2)}) collective-permute-start(bf16[256,256]{1,0:T(8,128)(2,1)S(1)} %get-tuple-element.17.refs_0_), channel_id=1, source_target_pairs={{0,2},{2,0},{4,6},{6,4},{8,10},{10,8},{12,14},{14,12},{1,3},{3,1},... | collective-permute-start | bytes 393224 | tf_op jit(solution)/shard_map/ppermute | solution.py:31
  30.2 12.3 %collective-permute-start.9 = (bf16[256,256]{1,0:T(8,128)(2,1)S(1)}, bf16[256,256]{1,0:T(8,128)(2,1)S(1)}, u32[]{:S(2)}, u32[]{:S(2)}) collective-permute-start(bf16[256,256]{1,0:T(8,128)(2,1)S(1)} %get-tuple-element.17.refs_0_), channel_id=1, source_target_pairs={{0,14},{2,12},{4,10},{6,8},{8,6},{10,4},{12,2},{14,0},{1,15},{3,13... | collective-permute-start | bytes 393224 | tf_op jit(solution)/shard_map/ppermute | solution.py:31
  32.4 10.7 %collective-permute-start.8 = (bf16[256,256]{1,0:T(8,128)(2,1)S(1)}, bf16[256,256]{1,0:T(8,128)(2,1)S(1)}, u32[]{:S(2)}, u32[]{:S(2)}) collective-permute-start(bf16[256,256]{1,0:T(8,128)(2,1)S(1)} %get-tuple-element.17.refs_0_), channel_id=1, source_target_pairs={{0,6},{2,4},{4,2},{6,0},{8,14},{10,12},{12,10},{14,8},{1,7},{3,5},... | collective-permute-start | bytes 393224 | tf_op jit(solution)/shard_map/ppermute | solution.py:31
  36.9 9.0 %collective-permute-start.12 = (bf16[256,256]{1,0:T(8,128)(2,1)S(1)}, bf16[256,256]{1,0:T(8,128)(2,1)S(1)}, u32[]{:S(2)}, u32[]{:S(2)}) collective-permute-start(bf16[256,256]{1,0:T(8,128)(2,1)S(1)} %collective-permute-done.10.refs_3_), channel_id=1, source_target_pairs={{0,4},{2,6},{4,0},{6,2},{8,12},{10,14},{12,8},{14,10},{1,5},{3,7},... | collective-permute-start | bytes 393224 | tf_op jit(solution)/shard_map/ppermute | solution.py:31
  41.0 5.0 %collective-permute-start.11 = (bf16[256,256]{1,0:T(8,128)(2,1)S(1)}, bf16[256,256]{1,0:T(8,128)(2,1)S(1)}, u32[]{:S(2)}, u32[]{:S(2)}) collective-permute-start(bf16[256,256]{1,0:T(8,128)(2,1)S(1)} %collective-permute-done.10.refs_3_), channel_id=1, source_target_pairs={{0,2},{2,0},{4,6},{6,4},{8,10},{10,8},{12,14},{14,12},{1,3},{3,1},... | collective-permute-start | bytes 393224 | tf_op jit(solution)/shard_map/ppermute | solution.py:31
  47.0 1.6 %copy-start.2 = (f32[256,256]{1,0:T(8,128)S(1)}, f32[256,256]{1,0:T(8,128)}, u32[]{:S(2)}) copy-start(f32[256,256]{1,0:T(8,128)} %state.1) | copy-start | bytes 786436
  47.0 1.6 %collective-permute-start.15 = (bf16[2,256,256]{2,1,0:T(8,128)(2,1)S(1)}, bf16[2,256,256]{2,1,0:T(8,128)(2,1)S(1)}, u32[]{:S(2)}, u32[]{:S(2)}) collective-permute-start(bf16[2,256,256]{2,1,0:T(8,128)(2,1)S(1)} %shard_map.130), channel_id=1, source_target_pairs={{0,1},{1,0},{2,3},{3,2},{4,5},{5,4},{6,7},{7,6},{8,9},{9,8},{10,11... | collective-permute-start | bytes 786440 | tf_op jit(solution)/shard_map/ppermute | solution.py:350

commit v10 on v9

--- a/solution.py
+++ b/solution.py
@@ -9,7 +9,7 @@
 
 NEWTON = 2
 DIRECT_COUNTS = (4, 8)
-LATE = 4
+TILE = 128
 
 damping = 0.5
 sigma_floor = 0.5
@@ -18,8 +18,9 @@
 
 def arrivals(count, direct):
     if not direct:
-        return list(range(count))
-    return [0, 1, 2, 4, 3, 7, 5, 6] if count == 8 else [0, 1, 2, 3]
+        cuts = [0, max(count - 4, 0), count]
+        return [list(range(first, last)) for first, last in zip(cuts, cuts[1:]) if last > first]
+    return [[0, 1, 4], [2, 3], [7, 5, 6]] if count == 8 else [[0, 1], [2, 3]]
 
 
 def row_met(spot, row, direct):
@@ -36,7 +37,7 @@
     if count == 8:
         for mask in (1, 2):
             found[4 + mask] = swapped(mask, found[4])
-    return [found[mask] for mask in arrivals(count, True)]
+    return [[found[mask] for mask in group] for group in arrivals(count, True)]
 
 
 PIECES = 4
@@ -59,7 +60,7 @@
         narrow_ref[part, :] = held[part, :].astype(narrow_ref.dtype)
 
 
-def prepare_kernel(spots, direct, *refs):
+def prepare_kernel(groups, direct, *refs):
     far, (v_out, u_out, coef_out, weight_out, decay_out), near, sem = refs[:7], refs[7:12], refs[12:19], refs[19]
     copies = [
         pltpu.make_async_copy(source, held, sem.at[at])
@@ -72,19 +73,23 @@
     rank_ref, v_ref, u_ref, sigma_ref, a_ref, b_ref, state_ref = near
     kinds, rows, count, rank_count, size = u_ref.shape
     row = lax.axis_index("row")
-    met = [row_met(spot, row, direct) for spot in spots]
+    met = [row_met(spot, row, direct) for group in groups for spot in group]
     for at, q in enumerate(met):
         for p in range(rows):
             inside = lax.broadcasted_iota(jnp.int32, (rank_count, size), 0) < rank_ref[p, q]
             v_out[at, p] = jnp.where(inside, v_ref[p, q].astype(jnp.float32), 0.0).astype(v_out.dtype)
     for p in range(rows):
         for kind in range(kinds):
-            for first in range(0, count, 4):
-                group = [u_ref[kind, p, q] for q in met[first : first + 4]]
+            first = start = 0
+            for spots in groups:
+                group = [u_ref[kind, p, q] for q in met[first : first + len(spots)]]
+                spare = -len(group) * rank_count % TILE
+                if spare:
+                    group.append(jnp.zeros((spare, size), u_ref.dtype))
                 turned = jnp.concatenate(group, axis=0).astype(jnp.float32).T
-                u_out[p, kind * size : (kind + 1) * size, first * rank_count : (first + len(group)) * rank_count] = (
-                    turned.astype(u_out.dtype)
-                )
+                stop = start + turned.shape[1]
+                u_out[p, kind * size : (kind + 1) * size, start:stop] = turned.astype(u_out.dtype)
+                first, start = first + len(spots), stop
     lanes = coef_out.shape[2]
     for at, values in enumerate((sigma_ref[...], a_ref[...], b_ref[...], 1.0 / a_ref[...], 1.0 / b_ref[...])):
         coef_out[at] = jnp.broadcast_to(values, (lanes, size)).T
@@ -95,7 +100,7 @@
         decay_out[:, part] = jnp.exp(-state * coef_out[4])
 
 
-def sums_kernel(spots, direct, first, pick, before, near_any, v_ref, u_ref, d_ref, *refs):
+def sums_kernel(spots, direct, first, start, pick, before, near_any, v_ref, u_ref, d_ref, *refs):
     blocks = refs[: len(spots)]
     refs = refs[len(spots) :]
     if before:
@@ -122,7 +127,7 @@
             ]
     for at, block in enumerate(blocks):
         x_all[at] = block[...]
-    lanes = slice(first * rank_count, (first + len(blocks)) * rank_count)
+    lanes = slice(start, start + len(blocks) * rank_count)
     for place, p in enumerate(chosen):
         gained = jnp.dot(u_ref[p, :, lanes], proj[place], preferred_element_type=jnp.float32)
         for kind in range(kinds):
@@ -278,8 +283,10 @@
     size, members = slip_deficit.shape
     kinds, rows, _, rank_count, _ = u_basis.shape
     direct = count in DIRECT_COUNTS
-    spots = arrivals(count, direct)
-    early = max(count - LATE, 0)
+    groups = arrivals(count, direct)
+    firsts = [sum(len(group) for group in groups[:at]) for at in range(len(groups))]
+    tiles = [-(-len(group) * rank_count // TILE) * TILE for group in groups]
+    starts = [sum(tiles[:at]) for at in range(len(groups))]
     room = 16 if direct else 40
     lanes = min(members, 128)
     narrow, wide = jnp.bfloat16, jnp.float32
@@ -290,10 +297,10 @@
 
     full = shaped(size, members)
     v_met, u_met, coef, weight, decay = on_core(
-        functools.partial(prepare_kernel, spots, direct),
+        functools.partial(prepare_kernel, groups, direct),
         (
             shaped(count, rows, rank_count, size, kind=narrow),
-            shaped(rows, kinds * size, count * rank_count, kind=narrow),
+            shaped(rows, kinds * size, sum(tiles), kind=narrow),
             shaped(5, size, lanes),
             full,
             full,
@@ -319,12 +326,12 @@
         ),
     )
 
-    def add(blocks, first, pick, before, kind):
+    def add(blocks, at, pick, before, kind):
         held = rows if pick is None else 1
         lead = (rows, kinds) if pick is None else (kinds,)
         return on_core(
             functools.partial(
-                sums_kernel, spots[first : first + len(blocks)], direct, first, pick, before is not None
+                sums_kernel, groups[at], direct, firsts[at], starts[at], pick, before is not None
             ),
             shaped(*lead, size, members, kind=kind),
             (v_met, u_met, dense_blocks, *blocks, *(() if before is None else (before,))),
@@ -342,13 +349,15 @@
 
     def lattice(field_half):
         if direct:
-            blocks = gather_direct(field_half, count)
+            found = gather_direct(field_half, count)
         else:
             whole = lax.all_gather(field_half, "row", axis=0)
-            blocks = [whole[r] for r in range(count)]
-        sums = add(blocks[:early], 0, None, None, wide) if early else None
-        other = lax.ppermute(add(blocks[early:], early, 1, sums, narrow), "col", swap)
-        return add(blocks[early:], early, 0, sums, wide), other
+            found = [[whole[r] for r in group] for group in groups]
+        sums, end = None, len(groups) - 1
+        for at in range(end):
+            sums = add(found[at], at, None, sums, wide)
+        other = lax.ppermute(add(found[end], end, 1, sums, narrow), "col", swap)
+        return add(found[end], end, 0, sums, wide), other
 
     slip_half = on_core(
         narrow_kernel,

time: 51.1 us -> 50.1 us (0.980)
  waiting for transfers between devices: 18.8 us -> 13.9 us
  starting transfers between devices: 18.6 us -> 21.2 us
  Pallas kernels: 12.6 us -> 14.2 us
    ppermute x14, waiting for transfers between devices: 17.5 us -> 12.8 us  [swapped(): lax.ppermute(data, 'row', [(row, row ^ mask) for row in range(count)])]
    ppermute x14, starting transfers between devices: 18.3 us -> 21.1 us  [swapped(): lax.ppermute(data, 'row', [(row, row ^ mask) for row in range(count)])]
    pallas_call x10 -> x12, Pallas kernels: 12.6 us -> 14.2 us  [on_core(): pl.pallas_call(kernel, out_shape=outs, in_specs=[hbm] * len(far) + [vmem]...]
  transfers between devices with their start and end apart: 16 -> 16, of which waited for: 11 -> 12; matrix products, arithmetic and copies ran while one was open for 0% -> 0% of each run, Pallas kernels for 12% -> 15%
where the time goes in v10:
time: 50.1 us
  starting transfers between devices  21.2 us (42%)
  Pallas kernels  14.2 us (28%)
  waiting for transfers between devices  13.9 us (28%)
  between operations  0.79 us (2%)
    ppermute x14, starting transfers between devices, swapped(): lax.ppermute(data, 'row', [(row, row ^ mask) for row in range(count)])  21.1 us
    pallas_call x12, Pallas kernels, on_core(): pl.pallas_call(kernel, out_shape=outs, in_specs=[hbm] * len(far) + [vmem]...  14.2 us
    ppermute x14, waiting for transfers between devices, swapped(): lax.ppermute(data, 'row', [(row, row ^ mask) for row in range(count)])  12.8 us
    ppermute x2, waiting for transfers between devices, lattice(): other = lax.ppermute(add(found[end], end, 1, sums, narrow), 'col', swap)  1.12 us
  transfers between devices with their start and end apart: 16, of which 12 were waited for; matrix products, arithmetic and copies ran while one was open for 0% of the time, Pallas kernels for 15%

profile of v10, /device:TPU:0, one launch (start us, length us, event | category | flops | bytes accessed | tf_op | source)
XLA Modules:
  0.0 50.1 jit_solution(3671081725624511077)
XLA Ops:
  0.6 0.0 copy-start
  0.6 1.1 %shard_map.123.refs_0_ = bf16[256,256]{1,0:T(8,128)(2,1)S(1)} custom-call(f32[256,256]{1,0:T(8,128)} %wide_ref.1), custom_call_target="tpu_custom_call" | custom-call | bytes 262144 | tf_op jit(solution)/shard_map/pallas_call | solution.py:256
  1.7 4.1 %collective-permute-start.1 = (bf16[256,256]{1,0:T(8,128)(2,1)S(1)}, bf16[256,256]{1,0:T(8,128)(2,1)S(1)}, u32[]{:S(2)}, u32[]{:S(2)}) collective-permute-start(bf16[256,256]{1,0:T(8,128)(2,1)S(1)} %shard_map.123.refs_0_), channel_id=1, source_target_pairs={{0,8},{2,10},{4,12},{6,14},{8,0},{10,2},{12,4},{14,6},{1,9},{3,11}... | collective-permute-start | bytes 393224 | tf_op jit(solution)/shard_map/ppermute | solution.py:32
  5.8 1.5 %collective-permute-start.6 = (bf16[256,256]{1,0:T(8,128)(2,1)S(1)}, bf16[256,256]{1,0:T(8,128)(2,1)S(1)}, u32[]{:S(2)}, u32[]{:S(2)}) collective-permute-start(bf16[256,256]{1,0:T(8,128)(2,1)S(1)} %shard_map.123.refs_0_), channel_id=1, source_target_pairs={{0,2},{2,0},{4,6},{6,4},{8,10},{10,8},{12,14},{14,12},{1,3},{3,1},... | collective-permute-start | bytes 393224 | tf_op jit(solution)/shard_map/ppermute | solution.py:32
  7.3 1.6 %collective-permute-start.4 = (bf16[256,256]{1,0:T(8,128)(2,1)S(1)}, bf16[256,256]{1,0:T(8,128)(2,1)S(1)}, u32[]{:S(2)}, u32[]{:S(2)}) collective-permute-start(bf16[256,256]{1,0:T(8,128)(2,1)S(1)} %shard_map.123.refs_0_), channel_id=1, source_target_pairs={{0,4},{2,6},{4,0},{6,2},{8,12},{10,14},{12,8},{14,10},{1,5},{3,7},... | collective-permute-start | bytes 393224 | tf_op jit(solution)/shard_map/ppermute | solution.py:32
  8.9 0.4 collective-permute-start.5
  9.3 2.3 %collective-permute-start = (bf16[256,256]{1,0:T(8,128)(2,1)S(1)}, bf16[256,256]{1,0:T(8,128)(2,1)S(1)}, u32[]{:S(2)}, u32[]{:S(2)}) collective-permute-start(bf16[256,256]{1,0:T(8,128)(2,1)S(1)} %shard_map.123.refs_0_), channel_id=1, source_target_pairs={{0,14},{2,12},{4,10},{6,8},{8,6},{10,4},{12,2},{14,0},{1,15},{3,13... | collective-permute-start | bytes 393224 | tf_op jit(solution)/shard_map/ppermute | solution.py:32
  11.6 0.6 %collective-permute-done.1.refs_2_ = bf16[256,256]{1,0:T(8,128)(2,1)S(1)} collective-permute-done((bf16[256,256]{1,0:T(8,128)(2,1)S(1)}, bf16[256,256]{1,0:T(8,128)(2,1)S(1)}, u32[]{:S(2)}, u32[]{:S(2)}) %collective-permute-start.1) | collective-permute-done | bytes 131104 | tf_op jit(solution)/shard_map/ppermute | solution.py:32
  12.2 2.0 %collective-permute-start.2 = (bf16[256,256]{1,0:T(8,128)(2,1)S(1)}, bf16[256,256]{1,0:T(8,128)(2,1)S(1)}, u32[]{:S(2)}, u32[]{:S(2)}) collective-permute-start(bf16[256,256]{1,0:T(8,128)(2,1)S(1)} %collective-permute-done.1.refs_2_), channel_id=1, source_target_pairs={{0,2},{2,0},{4,6},{6,4},{8,10},{10,8},{12,14},{14,12},{1,3},{3,1},... | collective-permute-start | bytes 393224 | tf_op jit(solution)/shard_map/ppermute | solution.py:32
  14.2 0.0 collective-permute-done.6.refs_1_
  14.2 0.3 collective-permute-start.3
  14.5 1.8 %shard_map.122 = (bf16[8,2,32,256]{3,2,1,0:T(8,128)(2,1)S(1)}, bf16[2,512,384]{2,1,0:T(8,128)(2,1)S(1)}, f32[5,256,128]{2,1,0:T(8,128)S(1)}, f32[256,256]{1,0:T(8,128)S(1)}, f32[256,256]{1,0:T(8,128)S(1)}) custom-call(s32[2,8]{1,0:T(2,128)} %refs_0_.1, bf16[2,8,32,256]{3,2,1,0:T(8,128)(2,1)} %refs_1_.1, bf16[2,2,8,32,256]{4,3,2,1,0:T(8,128)(2,1)} %refs_2_.1, ...), custom_call_target="tpu_custom_call" | custom-call | bytes 1051712 | tf_op jit(solution)/shard_map/pallas_call | solution.py:256
  16.3 1.2 %shard_map.124.refs_2_ = f32[2,2,256,256]{3,2,1,0:T(8,128)S(1)} custom-call(s32[2,2]{1,0:T(2,128)} %near_any.15, bf16[8,2,32,256]{3,2,1,0:T(8,128)(2,1)S(1)} %get-tuple-element.12.v_ref, bf16[2,512,384]{2,1,0:T(8,128)(2,1)S(1)} %get-tuple-element.13.u_ref, bf16[2,2,2,256,256]{4,3,2,1,0:T(8,128)(2,1)S(1)} %copy-done, ...), custom_call_target="tpu_custom_call" | custom-call | flops 75497472 | bytes 2490384 | tf_op jit(solution)/shard_map/pallas_call | solution.py:256
  17.5 0.0 collective-permute-done.4.refs_0_
  17.5 2.5 %collective-permute-done.5.refs_1_ = bf16[256,256]{1,0:T(8,128)(2,1)S(1)} collective-permute-done((bf16[256,256]{1,0:T(8,128)(2,1)S(1)}, bf16[256,256]{1,0:T(8,128)(2,1)S(1)}, u32[]{:S(2)}, u32[]{:S(2)}) %collective-permute-start.5) | collective-permute-done | bytes 131104 | tf_op jit(solution)/shard_map/ppermute | solution.py:32
  20.0 0.8 %shard_map.125.refs_3_ = f32[2,2,256,256]{3,2,1,0:T(8,128)S(1)} custom-call(s32[2,2]{1,0:T(2,128)} %near_any.15, bf16[8,2,32,256]{3,2,1,0:T(8,128)(2,1)S(1)} %get-tuple-element.12.v_ref, bf16[2,512,384]{2,1,0:T(8,128)(2,1)S(1)} %get-tuple-element.13.u_ref, bf16[2,2,2,256,256]{4,3,2,1,0:T(8,128)(2,1)S(1)} %copy-done, ...), custom_call_target="tpu_custom_call" | custom-call | flops 50331648 | bytes 3407888 | tf_op jit(solution)/shard_map/pallas_call | solution.py:256
  20.7 0.2 collective-permute-done.refs_0_
  20.9 0.7 %collective-permute-done.2.refs_1_ = bf16[256,256]{1,0:T(8,128)(2,1)S(1)} collective-permute-done((bf16[256,256]{1,0:T(8,128)(2,1)S(1)}, bf16[256,256]{1,0:T(8,128)(2,1)S(1)}, u32[]{:S(2)}, u32[]{:S(2)}) %collective-permute-start.2) | collective-permute-done | bytes 131104 | tf_op jit(solution)/shard_map/ppermute | solution.py:32
  21.6 0.5 %collective-permute-done.3.refs_2_ = bf16[256,256]{1,0:T(8,128)(2,1)S(1)} collective-permute-done((bf16[256,256]{1,0:T(8,128)(2,1)S(1)}, bf16[256,256]{1,0:T(8,128)(2,1)S(1)}, u32[]{:S(2)}, u32[]{:S(2)}) %collective-permute-start.3) | collective-permute-done | bytes 131104 | tf_op jit(solution)/shard_map/ppermute | solution.py:32
  22.1 1.0 %shard_map.127 = bf16[2,256,256]{2,1,0:T(8,128)(2,1)S(1)} custom-call(s32[2,2]{1,0:T(2,128)} %near_any.15, bf16[8,2,32,256]{3,2,1,0:T(8,128)(2,1)S(1)} %get-tuple-element.12.v_ref, bf16[2,512,384]{2,1,0:T(8,128)(2,1)S(1)} %get-tuple-element.13.u_ref, bf16[2,2,2,256,256]{4,3,2,1,0:T(8,128)(2,1)S(1)} %copy-done, ...), custom_call_target="tpu_custom_call" | custom-call | flops 37748736 | bytes 3538960 | tf_op jit(solution)/shard_map/pallas_call | solution.py:256
  23.1 0.0 copy-start.1
  23.1 0.1 collective-permute-start.7
  23.2 1.0 %shard_map.126.own = f32[2,256,256]{2,1,0:T(8,128)S(1)} custom-call(s32[2,2]{1,0:T(2,128)} %near_any.15, bf16[8,2,32,256]{3,2,1,0:T(8,128)(2,1)S(1)} %get-tuple-element.12.v_ref, bf16[2,512,384]{2,1,0:T(8,128)(2,1)S(1)} %get-tuple-element.13.u_ref, bf16[2,2,2,256,256]{4,3,2,1,0:T(8,128)(2,1)S(1)} %copy-done, ...), custom_call_target="tpu_custom_call" | custom-call | flops 37748736 | bytes 3538960 | tf_op jit(solution)/shard_map/pallas_call | solution.py:256
  24.2 0.6 %collective-permute-done.7.other = bf16[2,256,256]{2,1,0:T(8,128)(2,1)S(1)} collective-permute-done((bf16[2,256,256]{2,1,0:T(8,128)(2,1)S(1)}, bf16[2,256,256]{2,1,0:T(8,128)(2,1)S(1)}, u32[]{:S(2)}, u32[]{:S(2)}) %collective-permute-start.7) | collective-permute-done | bytes 262176 | tf_op jit(solution)/shard_map/ppermute | solution.py:359
  24.8 1.3 %shard_map.128 = (f32[256,256]{1,0:T(8,128)S(1)}, f32[256,256]{1,0:T(8,128)S(1)}, f32[256,256]{1,0:T(8,128)S(1)}, f32[256,256]{1,0:T(8,128)S(1)}, bf16[256,256]{1,0:T(8,128)(2,1)S(1)}) custom-call(f32[2,256,256]{2,1,0:T(8,128)S(1)} %shard_map.126.own, bf16[2,256,256]{2,1,0:T(8,128)(2,1)S(1)} %collective-permute-done.7.other, ...), custom_call_target="tpu_custom_call" | custom-call | flops 13107200 | bytes 2228224 | tf_op jit(solution)/shard_map/pallas_call | solution.py:256
  26.1 0.6 %collective-permute-start.9 = (bf16[256,256]{1,0:T(8,128)(2,1)S(1)}, bf16[256,256]{1,0:T(8,128)(2,1)S(1)}, u32[]{:S(2)}, u32[]{:S(2)}) collective-permute-start(bf16[256,256]{1,0:T(8,128)(2,1)S(1)} %get-tuple-element.17.refs_0_), channel_id=1, source_target_pairs={{0,8},{2,10},{4,12},{6,14},{8,0},{10,2},{12,4},{14,6},{1,9},{3,11}... | collective-permute-start | bytes 393224 | tf_op jit(solution)/shard_map/ppermute | solution.py:32
  26.7 1.1 %collective-permute-start.14 = (bf16[256,256]{1,0:T(8,128)(2,1)S(1)}, bf16[256,256]{1,0:T(8,128)(2,1)S(1)}, u32[]{:S(2)}, u32[]{:S(2)}) collective-permute-start(bf16[256,256]{1,0:T(8,128)(2,1)S(1)} %get-tuple-element.17.refs_0_), channel_id=1, source_target_pairs={{0,2},{2,0},{4,6},{6,4},{8,10},{10,8},{12,14},{14,12},{1,3},{3,1},... | collective-permute-start | bytes 393224 | tf_op jit(solution)/shard_map/ppermute | solution.py:32
  27.7 3.1 %collective-permute-start.12 = (bf16[256,256]{1,0:T(8,128)(2,1)S(1)}, bf16[256,256]{1,0:T(8,128)(2,1)S(1)}, u32[]{:S(2)}, u32[]{:S(2)}) collective-permute-start(bf16[256,256]{1,0:T(8,128)(2,1)S(1)} %get-tuple-element.17.refs_0_), channel_id=1, source_target_pairs={{0,4},{2,6},{4,0},{6,2},{8,12},{10,14},{12,8},{14,10},{1,5},{3,7},... | collective-permute-start | bytes 393224 | tf_op jit(solution)/shard_map/ppermute | solution.py:32
  30.8 0.0 collective-permute-start.13
  30.8 2.5 %collective-permute-start.8 = (bf16[256,256]{1,0:T(8,128)(2,1)S(1)}, bf16[256,256]{1,0:T(8,128)(2,1)S(1)}, u32[]{:S(2)}, u32[]{:S(2)}) collective-permute-start(bf16[256,256]{1,0:T(8,128)(2,1)S(1)} %get-tuple-element.17.refs_0_), channel_id=1, source_target_pairs={{0,14},{2,12},{4,10},{6,8},{8,6},{10,4},{12,2},{14,0},{1,15},{3,13... | collective-permute-start | bytes 393224 | tf_op jit(solution)/shard_map/ppermute | solution.py:32
  33.3 2.0 %collective-permute-done.9.refs_2_ = bf16[256,256]{1,0:T(8,128)(2,1)S(1)} collective-permute-done((bf16[256,256]{1,0:T(8,128)(2,1)S(1)}, bf16[256,256]{1,0:T(8,128)(2,1)S(1)}, u32[]{:S(2)}, u32[]{:S(2)}) %collective-permute-start.9) | collective-permute-done | bytes 131104 | tf_op jit(solution)/shard_map/ppermute | solution.py:32
  35.3 1.7 %collective-permute-start.10 = (bf16[256,256]{1,0:T(8,128)(2,1)S(1)}, bf16[256,256]{1,0:T(8,128)(2,1)S(1)}, u32[]{:S(2)}, u32[]{:S(2)}) collective-permute-start(bf16[256,256]{1,0:T(8,128)(2,1)S(1)} %collective-permute-done.9.refs_2_), channel_id=1, source_target_pairs={{0,2},{2,0},{4,6},{6,4},{8,10},{10,8},{12,14},{14,12},{1,3},{3,1},... | collective-permute-start | bytes 393224 | tf_op jit(solution)/shard_map/ppermute | solution.py:32
  37.0 0.0 collective-permute-done.14.refs_1_
  37.0 0.0 collective-permute-start.11
  37.0 1.2 %shard_map.129.refs_2_ = f32[2,2,256,256]{3,2,1,0:T(8,128)S(1)} custom-call(s32[2,2]{1,0:T(2,128)} %near_any.15, bf16[8,2,32,256]{3,2,1,0:T(8,128)(2,1)S(1)} %get-tuple-element.12.v_ref, bf16[2,512,384]{2,1,0:T(8,128)(2,1)S(1)} %get-tuple-element.13.u_ref, bf16[2,2,2,256,256]{4,3,2,1,0:T(8,128)(2,1)S(1)} %copy-done, ...), custom_call_target="tpu_custom_call" | custom-call | flops 75497472 | bytes 2490384 | tf_op jit(solution)/shard_map/pallas_call | solution.py:256
  38.2 0.0 collective-permute-done.12.refs_0_
  38.2 0.7 %collective-permute-done.13.refs_1_ = bf16[256,256]{1,0:T(8,128)(2,1)S(1)} collective-permute-done((bf16[256,256]{1,0:T(8,128)(2,1)S(1)}, bf16[256,256]{1,0:T(8,128)(2,1)S(1)}, u32[]{:S(2)}, u32[]{:S(2)}) %collective-permute-start.13) | collective-permute-done | bytes 131104 | tf_op jit(solution)/shard_map/ppermute | solution.py:32
  38.9 0.8 %shard_map.130.refs_3_ = f32[2,2,256,256]{3,2,1,0:T(8,128)S(1)} custom-call(s32[2,2]{1,0:T(2,128)} %near_any.15, bf16[8,2,32,256]{3,2,1,0:T(8,128)(2,1)S(1)} %get-tuple-element.12.v_ref, bf16[2,512,384]{2,1,0:T(8,128)(2,1)S(1)} %get-tuple-element.13.u_ref, bf16[2,2,2,256,256]{4,3,2,1,0:T(8,128)(2,1)S(1)} %copy-done, ...), custom_call_target="tpu_custom_call" | custom-call | flops 50331648 | bytes 3407888 | tf_op jit(solution)/shard_map/pallas_call | solution.py:256
  39.7 3.9 %collective-permute-done.8.refs_0_ = bf16[256,256]{1,0:T(8,128)(2,1)S(1)} collective-permute-done((bf16[256,256]{1,0:T(8,128)(2,1)S(1)}, bf16[256,256]{1,0:T(8,128)(2,1)S(1)}, u32[]{:S(2)}, u32[]{:S(2)}) %collective-permute-start.8) | collective-permute-done | bytes 131104 | tf_op jit(solution)/shard_map/ppermute | solution.py:32
  43.6 0.8 %collective-permute-done.10.refs_1_ = bf16[256,256]{1,0:T(8,128)(2,1)S(1)} collective-permute-done((bf16[256,256]{1,0:T(8,128)(2,1)S(1)}, bf16[256,256]{1,0:T(8,128)(2,1)S(1)}, u32[]{:S(2)}, u32[]{:S(2)}) %collective-permute-start.10) | collective-permute-done | bytes 131104 | tf_op jit(solution)/shard_map/ppermute | solution.py:32
  44.4 0.8 %collective-permute-done.11.refs_2_ = bf16[256,256]{1,0:T(8,128)(2,1)S(1)} collective-permute-done((bf16[256,256]{1,0:T(8,128)(2,1)S(1)}, bf16[256,256]{1,0:T(8,128)(2,1)S(1)}, u32[]{:S(2)}, u32[]{:S(2)}) %collective-permute-start.11) | collective-permute-done | bytes 131104 | tf_op jit(solution)/shard_map/ppermute | solution.py:32
  45.2 1.0 %shard_map.132 = bf16[2,256,256]{2,1,0:T(8,128)(2,1)S(1)} custom-call(s32[2,2]{1,0:T(2,128)} %near_any.15, bf16[8,2,32,256]{3,2,1,0:T(8,128)(2,1)S(1)} %get-tuple-element.12.v_ref, bf16[2,512,384]{2,1,0:T(8,128)(2,1)S(1)} %get-tuple-element.13.u_ref, bf16[2,2,2,256,256]{4,3,2,1,0:T(8,128)(2,1)S(1)} %copy-done, ...), custom_call_target="tpu_custom_call" | custom-call | flops 37748736 | bytes 3538960 | tf_op jit(solution)/shard_map/pallas_call | solution.py:256
  46.2 0.0 copy-start.2
  46.3 0.1 collective-permute-start.15
  46.3 1.0 %shard_map.131.own = f32[2,256,256]{2,1,0:T(8,128)S(1)} custom-call(s32[2,2]{1,0:T(2,128)} %near_any.15, bf16[8,2,32,256]{3,2,1,0:T(8,128)(2,1)S(1)} %get-tuple-element.12.v_ref, bf16[2,512,384]{2,1,0:T(8,128)(2,1)S(1)} %get-tuple-element.13.u_ref, bf16[2,2,2,256,256]{4,3,2,1,0:T(8,128)(2,1)S(1)} %copy-done, ...), custom_call_target="tpu_custom_call" | custom-call | flops 37748736 | bytes 3538960 | tf_op jit(solution)/shard_map/pallas_call | solution.py:256
  47.3 0.6 %collective-permute-done.15.other = bf16[2,256,256]{2,1,0:T(8,128)(2,1)S(1)} collective-permute-done((bf16[2,256,256]{2,1,0:T(8,128)(2,1)S(1)}, bf16[2,256,256]{2,1,0:T(8,128)(2,1)S(1)}, u32[]{:S(2)}, u32[]{:S(2)}) %collective-permute-start.15) | collective-permute-done | bytes 262176 | tf_op jit(solution)/shard_map/ppermute | solution.py:359
  47.9 0.0 copy-done.2
  47.9 2.3 %shard_map.133 = (f32[256,256]{1,0:T(8,128)}, f32[256,256]{1,0:T(8,128)}) custom-call(f32[2,256,256]{2,1,0:T(8,128)S(1)} %shard_map.131.own, bf16[2,256,256]{2,1,0:T(8,128)(2,1)S(1)} %collective-permute-done.15.other, f32[256,256]{1,0:T(8,128)S(1)} %copy-done.2, f32[256,256]{1,0:T(8,128)S(1)} %copy-done.1, f32[5,256,128]{2,1,0:T(8,128)S(1)} %get-tuple-element.16.coef, ...), custom_call_target="tpu_custom_call" | custom-call | flops 13107200 | bytes 3014656 | tf_op jit(solution)/shard_map/pallas_call | solution.py:256
  (2 shorter events, 0.0 us)
Async XLA Ops:
  0.6 15.7 %copy-start = (bf16[2,2,2,256,256]{4,3,2,1,0:T(8,128)(2,1)S(1)}, bf16[2,2,2,256,256]{4,3,2,1,0:T(8,128)(2,1)}, u32[]{:S(2)}) copy-start(bf16[2,2,2,256,256]{4,3,2,1,0:T(8,128)(2,1)} %d_ref.15) | copy-start | bytes 3145732
  1.7 10.5 %collective-permute-start.1 = (bf16[256,256]{1,0:T(8,128)(2,1)S(1)}, bf16[256,256]{1,0:T(8,128)(2,1)S(1)}, u32[]{:S(2)}, u32[]{:S(2)}) collective-permute-start(bf16[256,256]{1,0:T(8,128)(2,1)S(1)} %shard_map.123.refs_0_), channel_id=1, source_target_pairs={{0,8},{2,10},{4,12},{6,14},{8,0},{10,2},{12,4},{14,6},{1,9},{3,11}... | collective-permute-start | bytes 393224 | tf_op jit(solution)/shard_map/ppermute | solution.py:32
  5.8 8.4 %collective-permute-start.6 = (bf16[256,256]{1,0:T(8,128)(2,1)S(1)}, bf16[256,256]{1,0:T(8,128)(2,1)S(1)}, u32[]{:S(2)}, u32[]{:S(2)}) collective-permute-start(bf16[256,256]{1,0:T(8,128)(2,1)S(1)} %shard_map.123.refs_0_), channel_id=1, source_target_pairs={{0,2},{2,0},{4,6},{6,4},{8,10},{10,8},{12,14},{14,12},{1,3},{3,1},... | collective-permute-start | bytes 393224 | tf_op jit(solution)/shard_map/ppermute | solution.py:32
  7.3 10.2 %collective-permute-start.4 = (bf16[256,256]{1,0:T(8,128)(2,1)S(1)}, bf16[256,256]{1,0:T(8,128)(2,1)S(1)}, u32[]{:S(2)}, u32[]{:S(2)}) collective-permute-start(bf16[256,256]{1,0:T(8,128)(2,1)S(1)} %shard_map.123.refs_0_), channel_id=1, source_target_pairs={{0,4},{2,6},{4,0},{6,2},{8,12},{10,14},{12,8},{14,10},{1,5},{3,7},... | collective-permute-start | bytes 393224 | tf_op jit(solution)/shard_map/ppermute | solution.py:32
  8.9 11.1 %collective-permute-start.5 = (bf16[256,256]{1,0:T(8,128)(2,1)S(1)}, bf16[256,256]{1,0:T(8,128)(2,1)S(1)}, u32[]{:S(2)}, u32[]{:S(2)}) collective-permute-start(bf16[256,256]{1,0:T(8,128)(2,1)S(1)} %shard_map.123.refs_0_), channel_id=1, source_target_pairs={{0,6},{2,4},{4,2},{6,0},{8,14},{10,12},{12,10},{14,8},{1,7},{3,5},... | collective-permute-start | bytes 393224 | tf_op jit(solution)/shard_map/ppermute | solution.py:32
  9.3 11.6 %collective-permute-start = (bf16[256,256]{1,0:T(8,128)(2,1)S(1)}, bf16[256,256]{1,0:T(8,128)(2,1)S(1)}, u32[]{:S(2)}, u32[]{:S(2)}) collective-permute-start(bf16[256,256]{1,0:T(8,128)(2,1)S(1)} %shard_map.123.refs_0_), channel_id=1, source_target_pairs={{0,14},{2,12},{4,10},{6,8},{8,6},{10,4},{12,2},{14,0},{1,15},{3,13... | collective-permute-start | bytes 393224 | tf_op jit(solution)/shard_map/ppermute | solution.py:32
  12.2 9.4 %collective-permute-start.2 = (bf16[256,256]{1,0:T(8,128)(2,1)S(1)}, bf16[256,256]{1,0:T(8,128)(2,1)S(1)}, u32[]{:S(2)}, u32[]{:S(2)}) collective-permute-start(bf16[256,256]{1,0:T(8,128)(2,1)S(1)} %collective-permute-done.1.refs_2_), channel_id=1, source_target_pairs={{0,2},{2,0},{4,6},{6,4},{8,10},{10,8},{12,14},{14,12},{1,3},{3,1},... | collective-permute-start | bytes 393224 | tf_op jit(solution)/shard_map/ppermute | solution.py:32
  14.2 7.9 %collective-permute-start.3 = (bf16[256,256]{1,0:T(8,128)(2,1)S(1)}, bf16[256,256]{1,0:T(8,128)(2,1)S(1)}, u32[]{:S(2)}, u32[]{:S(2)}) collective-permute-start(bf16[256,256]{1,0:T(8,128)(2,1)S(1)} %collective-permute-done.1.refs_2_), channel_id=1, source_target_pairs={{0,4},{2,6},{4,0},{6,2},{8,12},{10,14},{12,8},{14,10},{1,5},{3,7},... | collective-permute-start | bytes 393224 | tf_op jit(solution)/shard_map/ppermute | solution.py:32
  23.1 1.6 %copy-start.1 = (f32[256,256]{1,0:T(8,128)S(1)}, f32[256,256]{1,0:T(8,128)}, u32[]{:S(2)}) copy-start(f32[256,256]{1,0:T(8,128)} %tau.3) | copy-start | bytes 786436
  23.1 1.6 %collective-permute-start.7 = (bf16[2,256,256]{2,1,0:T(8,128)(2,1)S(1)}, bf16[2,256,256]{2,1,0:T(8,128)(2,1)S(1)}, u32[]{:S(2)}, u32[]{:S(2)}) collective-permute-start(bf16[2,256,256]{2,1,0:T(8,128)(2,1)S(1)} %shard_map.127), channel_id=1, source_target_pairs={{0,1},{1,0},{2,3},{3,2},{4,5},{5,4},{6,7},{7,6},{8,9},{9,8},{10,11... | collective-permute-start | bytes 786440 | tf_op jit(solution)/shard_map/ppermute | solution.py:359
  26.1 9.2 %collective-permute-start.9 = (bf16[256,256]{1,0:T(8,128)(2,1)S(1)}, bf16[256,256]{1,0:T(8,128)(2,1)S(1)}, u32[]{:S(2)}, u32[]{:S(2)}) collective-permute-start(bf16[256,256]{1,0:T(8,128)(2,1)S(1)} %get-tuple-element.17.refs_0_), channel_id=1, source_target_pairs={{0,8},{2,10},{4,12},{6,14},{8,0},{10,2},{12,4},{14,6},{1,9},{3,11}... | collective-permute-start | bytes 393224 | tf_op jit(solution)/shard_map/ppermute | solution.py:32
  26.7 10.3 %collective-permute-start.14 = (bf16[256,256]{1,0:T(8,128)(2,1)S(1)}, bf16[256,256]{1,0:T(8,128)(2,1)S(1)}, u32[]{:S(2)}, u32[]{:S(2)}) collective-permute-start(bf16[256,256]{1,0:T(8,128)(2,1)S(1)} %get-tuple-element.17.refs_0_), channel_id=1, source_target_pairs={{0,2},{2,0},{4,6},{6,4},{8,10},{10,8},{12,14},{14,12},{1,3},{3,1},... | collective-permute-start | bytes 393224 | tf_op jit(solution)/shard_map/ppermute | solution.py:32
  27.7 10.5 %collective-permute-start.12 = (bf16[256,256]{1,0:T(8,128)(2,1)S(1)}, bf16[256,256]{1,0:T(8,128)(2,1)S(1)}, u32[]{:S(2)}, u32[]{:S(2)}) collective-permute-start(bf16[256,256]{1,0:T(8,128)(2,1)S(1)} %get-tuple-element.17.refs_0_), channel_id=1, source_target_pairs={{0,4},{2,6},{4,0},{6,2},{8,12},{10,14},{12,8},{14,10},{1,5},{3,7},... | collective-permute-start | bytes 393224 | tf_op jit(solution)/shard_map/ppermute | solution.py:32
  30.8 8.1 %collective-permute-start.13 = (bf16[256,256]{1,0:T(8,128)(2,1)S(1)}, bf16[256,256]{1,0:T(8,128)(2,1)S(1)}, u32[]{:S(2)}, u32[]{:S(2)}) collective-permute-start(bf16[256,256]{1,0:T(8,128)(2,1)S(1)} %get-tuple-element.17.refs_0_), channel_id=1, source_target_pairs={{0,6},{2,4},{4,2},{6,0},{8,14},{10,12},{12,10},{14,8},{1,7},{3,5},... | collective-permute-start | bytes 393224 | tf_op jit(solution)/shard_map/ppermute | solution.py:32
  30.8 12.8 %collective-permute-start.8 = (bf16[256,256]{1,0:T(8,128)(2,1)S(1)}, bf16[256,256]{1,0:T(8,128)(2,1)S(1)}, u32[]{:S(2)}, u32[]{:S(2)}) collective-permute-start(bf16[256,256]{1,0:T(8,128)(2,1)S(1)} %get-tuple-element.17.refs_0_), channel_id=1, source_target_pairs={{0,14},{2,12},{4,10},{6,8},{8,6},{10,4},{12,2},{14,0},{1,15},{3,13... | collective-permute-start | bytes 393224 | tf_op jit(solution)/shard_map/ppermute | solution.py:32
  35.3 9.1 %collective-permute-start.10 = (bf16[256,256]{1,0:T(8,128)(2,1)S(1)}, bf16[256,256]{1,0:T(8,128)(2,1)S(1)}, u32[]{:S(2)}, u32[]{:S(2)}) collective-permute-start(bf16[256,256]{1,0:T(8,128)(2,1)S(1)} %collective-permute-done.9.refs_2_), channel_id=1, source_target_pairs={{0,2},{2,0},{4,6},{6,4},{8,10},{10,8},{12,14},{14,12},{1,3},{3,1},... | collective-permute-start | bytes 393224 | tf_op jit(solution)/shard_map/ppermute | solution.py:32
  37.0 8.3 %collective-permute-start.11 = (bf16[256,256]{1,0:T(8,128)(2,1)S(1)}, bf16[256,256]{1,0:T(8,128)(2,1)S(1)}, u32[]{:S(2)}, u32[]{:S(2)}) collective-permute-start(bf16[256,256]{1,0:T(8,128)(2,1)S(1)} %collective-permute-done.9.refs_2_), channel_id=1, source_target_pairs={{0,4},{2,6},{4,0},{6,2},{8,12},{10,14},{12,8},{14,10},{1,5},{3,7},... | collective-permute-start | bytes 393224 | tf_op jit(solution)/shard_map/ppermute | solution.py:32
  46.2 1.6 %copy-start.2 = (f32[256,256]{1,0:T(8,128)S(1)}, f32[256,256]{1,0:T(8,128)}, u32[]{:S(2)}) copy-start(f32[256,256]{1,0:T(8,128)} %state.1) | copy-start | bytes 786436
  46.3 1.6 %collective-permute-start.15 = (bf16[2,256,256]{2,1,0:T(8,128)(2,1)S(1)}, bf16[2,256,256]{2,1,0:T(8,128)(2,1)S(1)}, u32[]{:S(2)}, u32[]{:S(2)}) collective-permute-start(bf16[2,256,256]{2,1,0:T(8,128)(2,1)S(1)} %shard_map.132), channel_id=1, source_target_pairs={{0,1},{1,0},{2,3},{3,2},{4,5},{5,4},{6,7},{7,6},{8,9},{9,8},{10,11... | collective-permute-start | bytes 786440 | tf_op jit(solution)/shard_map/ppermute | solution.py:359

commit v11 on v10

--- a/solution.py
+++ b/solution.py
@@ -20,7 +20,7 @@
     if not direct:
         cuts = [0, max(count - 4, 0), count]
         return [list(range(first, last)) for first, last in zip(cuts, cuts[1:]) if last > first]
-    return [[0, 1, 4], [2, 3], [7, 5, 6]] if count == 8 else [[0, 1], [2, 3]]
+    return [[0, 1, 4, 2], [7, 3, 5, 6]] if count == 8 else [[0, 1], [2, 3]]
 
 
 def row_met(spot, row, direct):
@@ -32,11 +32,12 @@
         return lax.ppermute(data, "row", [(row, row ^ mask) for row in range(count)])
 
     found = {0: block}
-    for mask in (4, 1, 2, 3, 7) if count == 8 else (1, 2, 3):
+    for mask in (4, 2, 1, 7) if count == 8 else (2, 1):
         found[mask] = swapped(mask, block)
     if count == 8:
         for mask in (1, 2):
             found[4 + mask] = swapped(mask, found[4])
+    found[3] = swapped(1, found[2])
     return [[found[mask] for mask in group] for group in arrivals(count, True)]
 
 

time: 50.1 us -> 51.9 us (1.036)
  waiting for transfers between devices: 13.9 us -> 18.1 us
  Pallas kernels: 14.2 us -> 12.6 us
  starting transfers between devices: 21.2 us -> 20.1 us
    ppermute x14, waiting for transfers between devices: 12.8 us -> 17 us  [swapped(): lax.ppermute(data, 'row', [(row, row ^ mask) for row in range(count)])]
    pallas_call x12 -> x10, Pallas kernels: 14.2 us -> 12.6 us  [on_core(): pl.pallas_call(kernel, out_shape=outs, in_specs=[hbm] * len(far) + [vmem]...]
    ppermute x14, starting transfers between devices: 21.1 us -> 19.9 us  [swapped(): lax.ppermute(data, 'row', [(row, row ^ mask) for row in range(count)])]
  transfers between devices with their start and end apart: 16 -> 16, of which waited for: 12 -> 9; matrix products, arithmetic and copies ran while one was open for 0% -> 0% of each run, Pallas kernels for 15% -> 13%
where the time goes in v11:
time: 51.9 us; the launch traced here: 51.6 us
  starting transfers between devices  20.1 us (39%)
  waiting for transfers between devices  18.1 us (35%)
  Pallas kernels  12.6 us (24%)
  between operations  0.78 us (2%)
    ppermute x14, starting transfers between devices, swapped(): lax.ppermute(data, 'row', [(row, row ^ mask) for row in range(count)])  19.9 us
    ppermute x14, waiting for transfers between devices, swapped(): lax.ppermute(data, 'row', [(row, row ^ mask) for row in range(count)])  17 us
    pallas_call x10, Pallas kernels, on_core(): pl.pallas_call(kernel, out_shape=outs, in_specs=[hbm] * len(far) + [vmem]...  12.6 us
    ppermute x2, waiting for transfers between devices, lattice(): other = lax.ppermute(add(found[end], end, 1, sums, narrow), 'col', swap)  1.04 us
  transfers between devices with their start and end apart: 16, of which 9 were waited for; matrix products, arithmetic and copies ran while one was open for 0% of the time, Pallas kernels for 13%

profile of v11, /device:TPU:0, one launch (start us, length us, event | category | flops | bytes accessed | tf_op | source)
XLA Modules:
  0.0 51.6 jit_solution(10520866032607445038)
XLA Ops:
  0.6 0.0 copy-start
  0.6 1.1 %shard_map.123.refs_0_ = bf16[256,256]{1,0:T(8,128)(2,1)S(1)} custom-call(f32[256,256]{1,0:T(8,128)} %wide_ref.1), custom_call_target="tpu_custom_call" | custom-call | bytes 262144 | tf_op jit(solution)/shard_map/pallas_call | solution.py:257
  1.7 4.1 %collective-permute-start.3 = (bf16[256,256]{1,0:T(8,128)(2,1)S(1)}, bf16[256,256]{1,0:T(8,128)(2,1)S(1)}, u32[]{:S(2)}, u32[]{:S(2)}) collective-permute-start(bf16[256,256]{1,0:T(8,128)(2,1)S(1)} %shard_map.123.refs_0_), channel_id=1, source_target_pairs={{0,8},{2,10},{4,12},{6,14},{8,0},{10,2},{12,4},{14,6},{1,9},{3,11}... | collective-permute-start | bytes 393224 | tf_op jit(solution)/shard_map/ppermute | solution.py:32
  5.8 1.6 %collective-permute-start.1 = (bf16[256,256]{1,0:T(8,128)(2,1)S(1)}, bf16[256,256]{1,0:T(8,128)(2,1)S(1)}, u32[]{:S(2)}, u32[]{:S(2)}) collective-permute-start(bf16[256,256]{1,0:T(8,128)(2,1)S(1)} %shard_map.123.refs_0_), channel_id=1, source_target_pairs={{0,4},{2,6},{4,0},{6,2},{8,12},{10,14},{12,8},{14,10},{1,5},{3,7},... | collective-permute-start | bytes 393224 | tf_op jit(solution)/shard_map/ppermute | solution.py:32
  7.4 1.5 %collective-permute-start.6 = (bf16[256,256]{1,0:T(8,128)(2,1)S(1)}, bf16[256,256]{1,0:T(8,128)(2,1)S(1)}, u32[]{:S(2)}, u32[]{:S(2)}) collective-permute-start(bf16[256,256]{1,0:T(8,128)(2,1)S(1)} %shard_map.123.refs_0_), channel_id=1, source_target_pairs={{0,2},{2,0},{4,6},{6,4},{8,10},{10,8},{12,14},{14,12},{1,3},{3,1},... | collective-permute-start | bytes 393224 | tf_op jit(solution)/shard_map/ppermute | solution.py:32
  8.9 0.0 collective-permute-start
  8.9 4.7 %collective-permute-done.3.refs_2_ = bf16[256,256]{1,0:T(8,128)(2,1)S(1)} collective-permute-done((bf16[256,256]{1,0:T(8,128)(2,1)S(1)}, bf16[256,256]{1,0:T(8,128)(2,1)S(1)}, u32[]{:S(2)}, u32[]{:S(2)}) %collective-permute-start.3) | collective-permute-done | bytes 131104 | tf_op jit(solution)/shard_map/ppermute | solution.py:32
  13.6 0.3 collective-permute-start.5
  13.8 1.9 %collective-permute-start.4 = (bf16[256,256]{1,0:T(8,128)(2,1)S(1)}, bf16[256,256]{1,0:T(8,128)(2,1)S(1)}, u32[]{:S(2)}, u32[]{:S(2)}) collective-permute-start(bf16[256,256]{1,0:T(8,128)(2,1)S(1)} %collective-permute-done.3.refs_2_), channel_id=1, source_target_pairs={{0,2},{2,0},{4,6},{6,4},{8,10},{10,8},{12,14},{14,12},{1,3},{3,1},... | collective-permute-start | bytes 393224 | tf_op jit(solution)/shard_map/ppermute | solution.py:32
  15.7 0.0 collective-permute-done.1.refs_3_
  15.7 0.1 collective-permute-start.2
  15.9 1.7 %shard_map.122 = (bf16[8,2,32,256]{3,2,1,0:T(8,128)(2,1)S(1)}, bf16[2,512,256]{2,1,0:T(8,128)(2,1)S(1)}, f32[5,256,128]{2,1,0:T(8,128)S(1)}, f32[256,256]{1,0:T(8,128)S(1)}, f32[256,256]{1,0:T(8,128)S(1)}) custom-call(s32[2,8]{1,0:T(2,128)} %refs_0_.1, bf16[2,8,32,256]{3,2,1,0:T(8,128)(2,1)} %refs_1_.1, bf16[2,2,8,32,256]{4,3,2,1,0:T(8,128)(2,1)} %refs_2_.1, ...), custom_call_target="tpu_custom_call" | custom-call | bytes 1051712 | tf_op jit(solution)/shard_map/pallas_call | solution.py:257
  17.6 0.0 collective-permute-done.6.refs_1_
  17.6 0.0 copy-done
  17.6 1.4 %shard_map.124.refs_4_ = f32[2,2,256,256]{3,2,1,0:T(8,128)S(1)} custom-call(s32[2,2]{1,0:T(2,128)} %near_any.11, bf16[8,2,32,256]{3,2,1,0:T(8,128)(2,1)S(1)} %get-tuple-element.12.v_ref, bf16[2,512,256]{2,1,0:T(8,128)(2,1)S(1)} %get-tuple-element.13.u_ref, bf16[2,2,2,256,256]{4,3,2,1,0:T(8,128)(2,1)S(1)} %copy-done, ...), custom_call_target="tpu_custom_call" | custom-call | flops 100663296 | bytes 2359312 | tf_op jit(solution)/shard_map/pallas_call | solution.py:257
  19.0 0.0 collective-permute-done.refs_0_
  19.0 0.0 collective-permute-done.5.refs_3_
  19.1 1.1 %collective-permute-done.4.refs_2_ = bf16[256,256]{1,0:T(8,128)(2,1)S(1)} collective-permute-done((bf16[256,256]{1,0:T(8,128)(2,1)S(1)}, bf16[256,256]{1,0:T(8,128)(2,1)S(1)}, u32[]{:S(2)}, u32[]{:S(2)}) %collective-permute-start.4) | collective-permute-done | bytes 131104 | tf_op jit(solution)/shard_map/ppermute | solution.py:32
  20.2 2.6 %collective-permute-done.2.refs_1_ = bf16[256,256]{1,0:T(8,128)(2,1)S(1)} collective-permute-done((bf16[256,256]{1,0:T(8,128)(2,1)S(1)}, bf16[256,256]{1,0:T(8,128)(2,1)S(1)}, u32[]{:S(2)}, u32[]{:S(2)}) %collective-permute-start.2) | collective-permute-done | bytes 131104 | tf_op jit(solution)/shard_map/ppermute | solution.py:32
  22.8 0.8 %shard_map.126 = bf16[2,256,256]{2,1,0:T(8,128)(2,1)S(1)} custom-call(s32[2,2]{1,0:T(2,128)} %near_any.11, bf16[8,2,32,256]{3,2,1,0:T(8,128)(2,1)S(1)} %get-tuple-element.12.v_ref, bf16[2,512,256]{2,1,0:T(8,128)(2,1)S(1)} %get-tuple-element.13.u_ref, bf16[2,2,2,256,256]{4,3,2,1,0:T(8,128)(2,1)S(1)} %copy-done, ...), custom_call_target="tpu_custom_call" | custom-call | flops 50331648 | bytes 3407888 | tf_op jit(solution)/shard_map/pallas_call | solution.py:257
  23.5 0.0 copy-start.1
  23.5 0.1 collective-permute-start.7
  23.7 1.0 %shard_map.125.own = f32[2,256,256]{2,1,0:T(8,128)S(1)} custom-call(s32[2,2]{1,0:T(2,128)} %near_any.11, bf16[8,2,32,256]{3,2,1,0:T(8,128)(2,1)S(1)} %get-tuple-element.12.v_ref, bf16[2,512,256]{2,1,0:T(8,128)(2,1)S(1)} %get-tuple-element.13.u_ref, bf16[2,2,2,256,256]{4,3,2,1,0:T(8,128)(2,1)S(1)} %copy-done, ...), custom_call_target="tpu_custom_call" | custom-call | flops 50331648 | bytes 3407888 | tf_op jit(solution)/shard_map/pallas_call | solution.py:257
  24.6 0.5 collective-permute-done.7.other
  25.1 0.0 copy-done.1
  25.1 1.3 %shard_map.127 = (f32[256,256]{1,0:T(8,128)S(1)}, f32[256,256]{1,0:T(8,128)S(1)}, f32[256,256]{1,0:T(8,128)S(1)}, f32[256,256]{1,0:T(8,128)S(1)}, bf16[256,256]{1,0:T(8,128)(2,1)S(1)}) custom-call(f32[2,256,256]{2,1,0:T(8,128)S(1)} %shard_map.125.own, bf16[2,256,256]{2,1,0:T(8,128)(2,1)S(1)} %collective-permute-done.7.other, ...), custom_call_target="tpu_custom_call" | custom-call | flops 13107200 | bytes 2228224 | tf_op jit(solution)/shard_map/pallas_call | solution.py:257
  26.4 4.3 %collective-permute-start.11 = (bf16[256,256]{1,0:T(8,128)(2,1)S(1)}, bf16[256,256]{1,0:T(8,128)(2,1)S(1)}, u32[]{:S(2)}, u32[]{:S(2)}) collective-permute-start(bf16[256,256]{1,0:T(8,128)(2,1)S(1)} %get-tuple-element.17.refs_0_), channel_id=1, source_target_pairs={{0,8},{2,10},{4,12},{6,14},{8,0},{10,2},{12,4},{14,6},{1,9},{3,11}... | collective-permute-start | bytes 393224 | tf_op jit(solution)/shard_map/ppermute | solution.py:32
  30.7 0.0 collective-permute-start.9
  30.7 0.7 %collective-permute-start.14 = (bf16[256,256]{1,0:T(8,128)(2,1)S(1)}, bf16[256,256]{1,0:T(8,128)(2,1)S(1)}, u32[]{:S(2)}, u32[]{:S(2)}) collective-permute-start(bf16[256,256]{1,0:T(8,128)(2,1)S(1)} %get-tuple-element.17.refs_0_), channel_id=1, source_target_pairs={{0,2},{2,0},{4,6},{6,4},{8,10},{10,8},{12,14},{14,12},{1,3},{3,1},... | collective-permute-start | bytes 393224 | tf_op jit(solution)/shard_map/ppermute | solution.py:32
  31.4 2.3 %collective-permute-start.8 = (bf16[256,256]{1,0:T(8,128)(2,1)S(1)}, bf16[256,256]{1,0:T(8,128)(2,1)S(1)}, u32[]{:S(2)}, u32[]{:S(2)}) collective-permute-start(bf16[256,256]{1,0:T(8,128)(2,1)S(1)} %get-tuple-element.17.refs_0_), channel_id=1, source_target_pairs={{0,14},{2,12},{4,10},{6,8},{8,6},{10,4},{12,2},{14,0},{1,15},{3,13... | collective-permute-start | bytes 393224 | tf_op jit(solution)/shard_map/ppermute | solution.py:32
  33.7 2.3 %collective-permute-done.11.refs_2_ = bf16[256,256]{1,0:T(8,128)(2,1)S(1)} collective-permute-done((bf16[256,256]{1,0:T(8,128)(2,1)S(1)}, bf16[256,256]{1,0:T(8,128)(2,1)S(1)}, u32[]{:S(2)}, u32[]{:S(2)}) %collective-permute-start.11) | collective-permute-done | bytes 131104 | tf_op jit(solution)/shard_map/ppermute | solution.py:32
  36.0 0.0 collective-permute-start.13
  36.0 2.0 %collective-permute-start.12 = (bf16[256,256]{1,0:T(8,128)(2,1)S(1)}, bf16[256,256]{1,0:T(8,128)(2,1)S(1)}, u32[]{:S(2)}, u32[]{:S(2)}) collective-permute-start(bf16[256,256]{1,0:T(8,128)(2,1)S(1)} %collective-permute-done.11.refs_2_), channel_id=1, source_target_pairs={{0,2},{2,0},{4,6},{6,4},{8,10},{10,8},{12,14},{14,12},{1,3},{3,1},... | collective-permute-start | bytes 393224 | tf_op jit(solution)/shard_map/ppermute | solution.py:32
  38.0 3.6 %collective-permute-done.9.refs_3_ = bf16[256,256]{1,0:T(8,128)(2,1)S(1)} collective-permute-done((bf16[256,256]{1,0:T(8,128)(2,1)S(1)}, bf16[256,256]{1,0:T(8,128)(2,1)S(1)}, u32[]{:S(2)}, u32[]{:S(2)}) %collective-permute-start.9) | collective-permute-done | bytes 131104 | tf_op jit(solution)/shard_map/ppermute | solution.py:32
  41.6 1.2 %collective-permute-start.10 = (bf16[256,256]{1,0:T(8,128)(2,1)S(1)}, bf16[256,256]{1,0:T(8,128)(2,1)S(1)}, u32[]{:S(2)}, u32[]{:S(2)}) collective-permute-start(bf16[256,256]{1,0:T(8,128)(2,1)S(1)} %collective-permute-done.9.refs_3_), channel_id=1, source_target_pairs={{0,2},{2,0},{4,6},{6,4},{8,10},{10,8},{12,14},{14,12},{1,3},{3,1},... | collective-permute-start | bytes 393224 | tf_op jit(solution)/shard_map/ppermute | solution.py:32
  42.8 0.0 collective-permute-done.14.refs_1_
  42.8 1.4 %shard_map.128.refs_4_ = f32[2,2,256,256]{3,2,1,0:T(8,128)S(1)} custom-call(s32[2,2]{1,0:T(2,128)} %near_any.11, bf16[8,2,32,256]{3,2,1,0:T(8,128)(2,1)S(1)} %get-tuple-element.12.v_ref, bf16[2,512,256]{2,1,0:T(8,128)(2,1)S(1)} %get-tuple-element.13.u_ref, bf16[2,2,2,256,256]{4,3,2,1,0:T(8,128)(2,1)S(1)} %copy-done, ...), custom_call_target="tpu_custom_call" | custom-call | flops 100663296 | bytes 2359312 | tf_op jit(solution)/shard_map/pallas_call | solution.py:257
  44.3 0.0 collective-permute-done.8.refs_0_
  44.3 0.1 collective-permute-done.13.refs_3_
  44.4 0.0 collective-permute-done.12.refs_2_
  44.4 2.6 %collective-permute-done.10.refs_1_ = bf16[256,256]{1,0:T(8,128)(2,1)S(1)} collective-permute-done((bf16[256,256]{1,0:T(8,128)(2,1)S(1)}, bf16[256,256]{1,0:T(8,128)(2,1)S(1)}, u32[]{:S(2)}, u32[]{:S(2)}) %collective-permute-start.10) | collective-permute-done | bytes 131104 | tf_op jit(solution)/shard_map/ppermute | solution.py:32
  47.0 0.8 %shard_map.130 = bf16[2,256,256]{2,1,0:T(8,128)(2,1)S(1)} custom-call(s32[2,2]{1,0:T(2,128)} %near_any.11, bf16[8,2,32,256]{3,2,1,0:T(8,128)(2,1)S(1)} %get-tuple-element.12.v_ref, bf16[2,512,256]{2,1,0:T(8,128)(2,1)S(1)} %get-tuple-element.13.u_ref, bf16[2,2,2,256,256]{4,3,2,1,0:T(8,128)(2,1)S(1)} %copy-done, ...), custom_call_target="tpu_custom_call" | custom-call | flops 50331648 | bytes 3407888 | tf_op jit(solution)/shard_map/pallas_call | solution.py:257
  47.7 0.0 copy-start.2
  47.7 0.1 collective-permute-start.15
  47.8 1.0 %shard_map.129.own = f32[2,256,256]{2,1,0:T(8,128)S(1)} custom-call(s32[2,2]{1,0:T(2,128)} %near_any.11, bf16[8,2,32,256]{3,2,1,0:T(8,128)(2,1)S(1)} %get-tuple-element.12.v_ref, bf16[2,512,256]{2,1,0:T(8,128)(2,1)S(1)} %get-tuple-element.13.u_ref, bf16[2,2,2,256,256]{4,3,2,1,0:T(8,128)(2,1)S(1)} %copy-done, ...), custom_call_target="tpu_custom_call" | custom-call | flops 50331648 | bytes 3407888 | tf_op jit(solution)/shard_map/pallas_call | solution.py:257
  48.8 0.6 %collective-permute-done.15.other = bf16[2,256,256]{2,1,0:T(8,128)(2,1)S(1)} collective-permute-done((bf16[2,256,256]{2,1,0:T(8,128)(2,1)S(1)}, bf16[2,256,256]{2,1,0:T(8,128)(2,1)S(1)}, u32[]{:S(2)}, u32[]{:S(2)}) %collective-permute-start.15) | collective-permute-done | bytes 262176 | tf_op jit(solution)/shard_map/ppermute | solution.py:360
  49.3 0.0 copy-done.2
  49.4 2.3 %shard_map.131 = (f32[256,256]{1,0:T(8,128)}, f32[256,256]{1,0:T(8,128)}) custom-call(f32[2,256,256]{2,1,0:T(8,128)S(1)} %shard_map.129.own, bf16[2,256,256]{2,1,0:T(8,128)(2,1)S(1)} %collective-permute-done.15.other, f32[256,256]{1,0:T(8,128)S(1)} %copy-done.2, f32[256,256]{1,0:T(8,128)S(1)} %copy-done.1, f32[5,256,128]{2,1,0:T(8,128)S(1)} %get-tuple-element.16.coef, ...), custom_call_target="tpu_custom_call" | custom-call | flops 13107200 | bytes 3014656 | tf_op jit(solution)/shard_map/pallas_call | solution.py:257
Async XLA Ops:
  0.6 17.0 %copy-start = (bf16[2,2,2,256,256]{4,3,2,1,0:T(8,128)(2,1)S(1)}, bf16[2,2,2,256,256]{4,3,2,1,0:T(8,128)(2,1)}, u32[]{:S(2)}) copy-start(bf16[2,2,2,256,256]{4,3,2,1,0:T(8,128)(2,1)} %d_ref.11) | copy-start | bytes 3145732
  1.7 11.9 %collective-permute-start.3 = (bf16[256,256]{1,0:T(8,128)(2,1)S(1)}, bf16[256,256]{1,0:T(8,128)(2,1)S(1)}, u32[]{:S(2)}, u32[]{:S(2)}) collective-permute-start(bf16[256,256]{1,0:T(8,128)(2,1)S(1)} %shard_map.123.refs_0_), channel_id=1, source_target_pairs={{0,8},{2,10},{4,12},{6,14},{8,0},{10,2},{12,4},{14,6},{1,9},{3,11}... | collective-permute-start | bytes 393224 | tf_op jit(solution)/shard_map/ppermute | solution.py:32
  5.8 9.9 %collective-permute-start.1 = (bf16[256,256]{1,0:T(8,128)(2,1)S(1)}, bf16[256,256]{1,0:T(8,128)(2,1)S(1)}, u32[]{:S(2)}, u32[]{:S(2)}) collective-permute-start(bf16[256,256]{1,0:T(8,128)(2,1)S(1)} %shard_map.123.refs_0_), channel_id=1, source_target_pairs={{0,4},{2,6},{4,0},{6,2},{8,12},{10,14},{12,8},{14,10},{1,5},{3,7},... | collective-permute-start | bytes 393224 | tf_op jit(solution)/shard_map/ppermute | solution.py:32
  7.4 10.2 %collective-permute-start.6 = (bf16[256,256]{1,0:T(8,128)(2,1)S(1)}, bf16[256,256]{1,0:T(8,128)(2,1)S(1)}, u32[]{:S(2)}, u32[]{:S(2)}) collective-permute-start(bf16[256,256]{1,0:T(8,128)(2,1)S(1)} %shard_map.123.refs_0_), channel_id=1, source_target_pairs={{0,2},{2,0},{4,6},{6,4},{8,10},{10,8},{12,14},{14,12},{1,3},{3,1},... | collective-permute-start | bytes 393224 | tf_op jit(solution)/shard_map/ppermute | solution.py:32
  8.9 10.1 %collective-permute-start = (bf16[256,256]{1,0:T(8,128)(2,1)S(1)}, bf16[256,256]{1,0:T(8,128)(2,1)S(1)}, u32[]{:S(2)}, u32[]{:S(2)}) collective-permute-start(bf16[256,256]{1,0:T(8,128)(2,1)S(1)} %shard_map.123.refs_0_), channel_id=1, source_target_pairs={{0,14},{2,12},{4,10},{6,8},{8,6},{10,4},{12,2},{14,0},{1,15},{3,13... | collective-permute-start | bytes 393224 | tf_op jit(solution)/shard_map/ppermute | solution.py:32
  13.6 5.5 %collective-permute-start.5 = (bf16[256,256]{1,0:T(8,128)(2,1)S(1)}, bf16[256,256]{1,0:T(8,128)(2,1)S(1)}, u32[]{:S(2)}, u32[]{:S(2)}) collective-permute-start(bf16[256,256]{1,0:T(8,128)(2,1)S(1)} %collective-permute-done.3.refs_2_), channel_id=1, source_target_pairs={{0,4},{2,6},{4,0},{6,2},{8,12},{10,14},{12,8},{14,10},{1,5},{3,7},... | collective-permute-start | bytes 393224 | tf_op jit(solution)/shard_map/ppermute | solution.py:32
  13.8 6.4 %collective-permute-start.4 = (bf16[256,256]{1,0:T(8,128)(2,1)S(1)}, bf16[256,256]{1,0:T(8,128)(2,1)S(1)}, u32[]{:S(2)}, u32[]{:S(2)}) collective-permute-start(bf16[256,256]{1,0:T(8,128)(2,1)S(1)} %collective-permute-done.3.refs_2_), channel_id=1, source_target_pairs={{0,2},{2,0},{4,6},{6,4},{8,10},{10,8},{12,14},{14,12},{1,3},{3,1},... | collective-permute-start | bytes 393224 | tf_op jit(solution)/shard_map/ppermute | solution.py:32
  15.7 7.0 %collective-permute-start.2 = (bf16[256,256]{1,0:T(8,128)(2,1)S(1)}, bf16[256,256]{1,0:T(8,128)(2,1)S(1)}, u32[]{:S(2)}, u32[]{:S(2)}) collective-permute-start(bf16[256,256]{1,0:T(8,128)(2,1)S(1)} %collective-permute-done.1.refs_3_), channel_id=1, source_target_pairs={{0,2},{2,0},{4,6},{6,4},{8,10},{10,8},{12,14},{14,12},{1,3},{3,1},... | collective-permute-start | bytes 393224 | tf_op jit(solution)/shard_map/ppermute | solution.py:32
  23.5 1.6 %copy-start.1 = (f32[256,256]{1,0:T(8,128)S(1)}, f32[256,256]{1,0:T(8,128)}, u32[]{:S(2)}) copy-start(f32[256,256]{1,0:T(8,128)} %tau.3) | copy-start | bytes 786436
  23.5 1.6 %collective-permute-start.7 = (bf16[2,256,256]{2,1,0:T(8,128)(2,1)S(1)}, bf16[2,256,256]{2,1,0:T(8,128)(2,1)S(1)}, u32[]{:S(2)}, u32[]{:S(2)}) collective-permute-start(bf16[2,256,256]{2,1,0:T(8,128)(2,1)S(1)} %shard_map.126), channel_id=1, source_target_pairs={{0,1},{1,0},{2,3},{3,2},{4,5},{5,4},{6,7},{7,6},{8,9},{9,8},{10,11... | collective-permute-start | bytes 786440 | tf_op jit(solution)/shard_map/ppermute | solution.py:360
  26.4 9.6 %collective-permute-start.11 = (bf16[256,256]{1,0:T(8,128)(2,1)S(1)}, bf16[256,256]{1,0:T(8,128)(2,1)S(1)}, u32[]{:S(2)}, u32[]{:S(2)}) collective-permute-start(bf16[256,256]{1,0:T(8,128)(2,1)S(1)} %get-tuple-element.17.refs_0_), channel_id=1, source_target_pairs={{0,8},{2,10},{4,12},{6,14},{8,0},{10,2},{12,4},{14,6},{1,9},{3,11}... | collective-permute-start | bytes 393224 | tf_op jit(solution)/shard_map/ppermute | solution.py:32
  30.7 10.9 %collective-permute-start.9 = (bf16[256,256]{1,0:T(8,128)(2,1)S(1)}, bf16[256,256]{1,0:T(8,128)(2,1)S(1)}, u32[]{:S(2)}, u32[]{:S(2)}) collective-permute-start(bf16[256,256]{1,0:T(8,128)(2,1)S(1)} %get-tuple-element.17.refs_0_), channel_id=1, source_target_pairs={{0,4},{2,6},{4,0},{6,2},{8,12},{10,14},{12,8},{14,10},{1,5},{3,7},... | collective-permute-start | bytes 393224 | tf_op jit(solution)/shard_map/ppermute | solution.py:32
  30.7 12.1 %collective-permute-start.14 = (bf16[256,256]{1,0:T(8,128)(2,1)S(1)}, bf16[256,256]{1,0:T(8,128)(2,1)S(1)}, u32[]{:S(2)}, u32[]{:S(2)}) collective-permute-start(bf16[256,256]{1,0:T(8,128)(2,1)S(1)} %get-tuple-element.17.refs_0_), channel_id=1, source_target_pairs={{0,2},{2,0},{4,6},{6,4},{8,10},{10,8},{12,14},{14,12},{1,3},{3,1},... | collective-permute-start | bytes 393224 | tf_op jit(solution)/shard_map/ppermute | solution.py:32
  31.4 12.8 %collective-permute-start.8 = (bf16[256,256]{1,0:T(8,128)(2,1)S(1)}, bf16[256,256]{1,0:T(8,128)(2,1)S(1)}, u32[]{:S(2)}, u32[]{:S(2)}) collective-permute-start(bf16[256,256]{1,0:T(8,128)(2,1)S(1)} %get-tuple-element.17.refs_0_), channel_id=1, source_target_pairs={{0,14},{2,12},{4,10},{6,8},{8,6},{10,4},{12,2},{14,0},{1,15},{3,13... | collective-permute-start | bytes 393224 | tf_op jit(solution)/shard_map/ppermute | solution.py:32
  36.0 8.3 %collective-permute-start.13 = (bf16[256,256]{1,0:T(8,128)(2,1)S(1)}, bf16[256,256]{1,0:T(8,128)(2,1)S(1)}, u32[]{:S(2)}, u32[]{:S(2)}) collective-permute-start(bf16[256,256]{1,0:T(8,128)(2,1)S(1)} %collective-permute-done.11.refs_2_), channel_id=1, source_target_pairs={{0,4},{2,6},{4,0},{6,2},{8,12},{10,14},{12,8},{14,10},{1,5},{3,7},... | collective-permute-start | bytes 393224 | tf_op jit(solution)/shard_map/ppermute | solution.py:32
  36.0 8.3 %collective-permute-start.12 = (bf16[256,256]{1,0:T(8,128)(2,1)S(1)}, bf16[256,256]{1,0:T(8,128)(2,1)S(1)}, u32[]{:S(2)}, u32[]{:S(2)}) collective-permute-start(bf16[256,256]{1,0:T(8,128)(2,1)S(1)} %collective-permute-done.11.refs_2_), channel_id=1, source_target_pairs={{0,2},{2,0},{4,6},{6,4},{8,10},{10,8},{12,14},{14,12},{1,3},{3,1},... | collective-permute-start | bytes 393224 | tf_op jit(solution)/shard_map/ppermute | solution.py:32
  41.6 5.3 %collective-permute-start.10 = (bf16[256,256]{1,0:T(8,128)(2,1)S(1)}, bf16[256,256]{1,0:T(8,128)(2,1)S(1)}, u32[]{:S(2)}, u32[]{:S(2)}) collective-permute-start(bf16[256,256]{1,0:T(8,128)(2,1)S(1)} %collective-permute-done.9.refs_3_), channel_id=1, source_target_pairs={{0,2},{2,0},{4,6},{6,4},{8,10},{10,8},{12,14},{14,12},{1,3},{3,1},... | collective-permute-start | bytes 393224 | tf_op jit(solution)/shard_map/ppermute | solution.py:32
  47.7 1.6 %copy-start.2 = (f32[256,256]{1,0:T(8,128)S(1)}, f32[256,256]{1,0:T(8,128)}, u32[]{:S(2)}) copy-start(f32[256,256]{1,0:T(8,128)} %state.1) | copy-start | bytes 786436
  47.7 1.6 %collective-permute-start.15 = (bf16[2,256,256]{2,1,0:T(8,128)(2,1)S(1)}, bf16[2,256,256]{2,1,0:T(8,128)(2,1)S(1)}, u32[]{:S(2)}, u32[]{:S(2)}) collective-permute-start(bf16[2,256,256]{2,1,0:T(8,128)(2,1)S(1)} %shard_map.130), channel_id=1, source_target_pairs={{0,1},{1,0},{2,3},{3,2},{4,5},{5,4},{6,7},{7,6},{8,9},{9,8},{10,11... | collective-permute-start | bytes 786440 | tf_op jit(solution)/shard_map/ppermute | solution.py:360

commit v12 on v8

--- a/solution.py
+++ b/solution.py
@@ -39,7 +39,7 @@
     return [found[mask] for mask in arrivals(count, True)]
 
 
-PIECES = 4
+PIECES = 8
 
 
 def row_pieces(size):
@@ -59,8 +59,21 @@
         narrow_ref[part, :] = held[part, :].astype(narrow_ref.dtype)
 
 
+def store_powers(outs, part, state, coef):
+    outs[0][:, part] = jnp.exp(-state * coef[3])
+    outs[1][:, part] = jnp.exp(state * coef[3])
+    outs[2][:, part] = jnp.exp(-state * coef[4])
+
+
+def later_kernel(state, change, coef, *outs):
+    lanes = coef.shape[2]
+    for first in range(0, state.shape[1], lanes):
+        part = slice(first, first + lanes)
+        store_powers(outs, part, state[:, part] + section_step * change[:, part], coef)
+
+
 def prepare_kernel(spots, direct, *refs):
-    far, (v_out, u_out, coef_out, weight_out, decay_out), near, sem = refs[:7], refs[7:12], refs[12:19], refs[19]
+    far, (v_out, u_out, coef_out, *powers), near, sem = refs[:7], refs[7:13], refs[13:20], refs[20]
     copies = [
         pltpu.make_async_copy(source, held, sem.at[at])
         for at, (source, held) in enumerate(zip(far, near))
@@ -90,9 +103,7 @@
         coef_out[at] = jnp.broadcast_to(values, (lanes, size)).T
     for first in range(0, state_ref.shape[1], lanes):
         part = slice(first, first + lanes)
-        state = state_ref[:, part]
-        weight_out[:, part] = jnp.exp(-state * coef_out[3])
-        decay_out[:, part] = jnp.exp(-state * coef_out[4])
+        store_powers(powers, part, state_ref[:, part], coef_out)
 
 
 def sums_kernel(spots, direct, first, pick, before, near_any, v_ref, u_ref, d_ref, *refs):
@@ -100,8 +111,7 @@
     refs = refs[len(spots) :]
     if before:
         sums_ref, refs = refs[0], refs[1:]
-    out_ref, x_all, proj, near_ref, near_sem = refs[:5]
-    total = refs[5] if pick == 1 else out_ref
+    out_ref, x_all, proj, near_ref, near_sem = refs
     count, rows, rank_count, size = v_ref.shape
     kinds, slots = d_ref.shape[0], near_ref.shape[1]
     near_copy = pltpu.make_async_copy(near_any, near_ref, near_sem)
@@ -122,28 +132,21 @@
             ]
     for at, block in enumerate(blocks):
         x_all[at] = block[...]
+    x_all[len(blocks)] = jnp.zeros_like(x_all[0])
     lanes = slice(first * rank_count, (first + len(blocks)) * rank_count)
-    for place, p in enumerate(chosen):
-        gained = jnp.dot(u_ref[p, :, lanes], proj[place], preferred_element_type=jnp.float32)
-        for kind in range(kinds):
-            piece = gained[kind * size : (kind + 1) * size]
-            total[*places[place], kind] = sums_ref[p, kind] + piece if before else piece
     near_copy.wait()
     for place, p in enumerate(chosen):
+        total = jnp.dot(u_ref[p, :, lanes], proj[place], preferred_element_type=jnp.float32)
         for s in range(slots):
             near = near_ref[p, s] - col * count
-            at = sum(jnp.where(near == q, i, 0) for i, q in enumerate(met))
-            hit = sum(jnp.where(near == q, 1, 0) for q in met)
-
-            @pl.when(hit > 0)
-            def _():
-                block = x_all[at]
-                for kind in range(kinds):
-                    total[*places[place], kind] += jnp.dot(
-                        d_ref[kind, p, s], block, preferred_element_type=jnp.float32
-                    )
-    if pick == 1:
-        out_ref[...] = total[...].astype(out_ref.dtype)
+            at = len(blocks) - sum(jnp.where(near == q, len(blocks) - i, 0) for i, q in enumerate(met))
+            weights = jnp.concatenate([d_ref[kind, p, s] for kind in range(kinds)], axis=0)
+            total += jnp.dot(weights, x_all[at], preferred_element_type=jnp.float32)
+        for kind in range(kinds):
+            piece = total[kind * size : (kind + 1) * size]
+            if before:
+                piece += sums_ref[p, kind]
+            out_ref[*places[place], kind] = piece.astype(out_ref.dtype)
 
 
 def inverse(value):
@@ -160,12 +163,12 @@
     return sinh, 0.5 * (grown + shrunk)
 
 
-def friction(shear, normal, weight, decay, tau_load, sigma_base, a_wide, b_wide):
+def friction(shear, normal, weight, unweight, decay, tau_load, sigma_base, a_wide, b_wide):
     tau = tau_load + shear
     size = jnp.abs(tau)
     stiff = jnp.maximum(sigma_base + normal, sigma_floor) * a_wide
     double = 2.0 * damping * weight
-    drive = size * inverse(double)
+    drive = size * unweight * (0.5 / damping)
     square = drive * drive + 1.0
     slope = jnp.minimum(size * inverse(stiff), jnp.log(drive + square * lax.rsqrt(square)))
     for newton_step in range(NEWTON):
@@ -187,7 +190,7 @@
             work(rows, slice(first, first + lanes))
 
 
-def section_one_kernel(own, other, weight, decay, tau, coef, stress, normal, rate, change, rate_half):
+def section_one_kernel(own, other, weight, unweight, decay, tau, coef, stress, normal, rate, change, rate_half):
     size, members = tau.shape
 
     def work(rows, part):
@@ -199,6 +202,7 @@
             shear,
             press,
             weight[rows, part],
+            unweight[rows, part],
             decay[rows, part],
             tau[rows, part],
             coef[0, rows, :],
@@ -213,24 +217,23 @@
 
 
 def section_two_kernel(
-    own, other, state, tau, coef, stress, normal, rate, change, rate_out, change_out, mean_rate, mean_change, sem
+    own, other, weight, unweight, decay, tau, coef, stress, normal, rate, change, rate_out, change_out, mean_rate, mean_change, sem
 ):
     size, members = tau.shape
 
     def work(rows, part):
         shear = own[0, rows, part] + other[0, rows, part].astype(jnp.float32)
         press = own[1, rows, part] + other[1, rows, part].astype(jnp.float32)
-        sigma, a_wide, b_wide = coef[0, rows, :], coef[1, rows, :], coef[2, rows, :]
-        later = state[rows, part] + section_step * change[rows, part]
         first, second = friction(
             stress[rows, part] + section_step * shear,
             normal[rows, part] + section_step * press,
-            jnp.exp(-later * coef[3, rows, :]),
-            jnp.exp(-later * coef[4, rows, :]),
+            weight[rows, part],
+            unweight[rows, part],
+            decay[rows, part],
             tau[rows, part],
-            sigma,
-            a_wide,
-            b_wide,
+            coef[0, rows, :],
+            coef[1, rows, :],
+            coef[2, rows, :],
         )
         mean_rate[rows, part] = (rate[rows, part] + first) * 0.5
         mean_change[rows, part] = (change[rows, part] + second) * 0.5
@@ -289,12 +292,13 @@
         return jax.ShapeDtypeStruct(shape, kind)
 
     full = shaped(size, members)
-    v_met, u_met, coef, weight, decay = on_core(
+    v_met, u_met, coef, *powers = on_core(
         functools.partial(prepare_kernel, spots, direct),
         (
             shaped(count, rows, rank_count, size, kind=narrow),
             shaped(rows, kinds * size, count * rank_count, kind=narrow),
             shaped(5, size, lanes),
+            full,
             full,
             full,
         ),
@@ -329,26 +333,26 @@
             shaped(*lead, size, members, kind=kind),
             (v_met, u_met, dense_blocks, *blocks, *(() if before is None else (before,))),
             (
-                pltpu.VMEM((len(blocks), size, members), narrow),
+                pltpu.VMEM((len(blocks) + 1, size, members), narrow),
                 pltpu.VMEM((held, len(blocks) * rank_count, members), narrow),
                 pltpu.SMEM(near_index.shape, jnp.int32),
                 pltpu.SemaphoreType.DMA(()),
-                *([pltpu.VMEM((kinds, size, members), wide)] if pick == 1 else []),
             ),
             2 * held * size * members * rank_count * len(blocks) * 3,
             room,
             far=(near_index,),
         )
 
-    def lattice(field_half):
+    def lattice(field_half, beside):
         if direct:
             blocks = gather_direct(field_half, count)
         else:
             whole = lax.all_gather(field_half, "row", axis=0)
             blocks = [whole[r] for r in range(count)]
+        blocks[0], beside = lax.optimization_barrier((blocks[0], beside))
         sums = add(blocks[:early], 0, None, None, wide) if early else None
         other = lax.ppermute(add(blocks[early:], early, 1, sums, narrow), "col", swap)
-        return add(blocks[early:], early, 0, sums, wide), other
+        return add(blocks[early:], early, 0, sums, wide), other, beside
 
     slip_half = on_core(
         narrow_kernel,
@@ -357,18 +361,19 @@
         (pltpu.VMEM((size, members), wide), pltpu.SemaphoreType.DMA((PIECES,))),
         far=(slip_deficit,),
     )
-    own, other = lattice(slip_half)
+    own, other, powers = lattice(slip_half, powers)
     stress, normal, rate, change, rate_half = on_core(
         section_one_kernel,
         (full, full, full, full, shaped(size, members, kind=narrow)),
-        (own, other, weight, decay, tau_load, coef),
+        (own, other, *powers, tau_load, coef),
         flops=200 * size * members,
     )
-    own, other = lattice(rate_half)
+    powers = on_core(later_kernel, (full, full, full), (state_var, change, coef))
+    own, other, powers = lattice(rate_half, powers)
     return on_core(
         section_two_kernel,
         (full, full),
-        (own, other, state_var, tau_load, coef, stress, normal, rate, change),
+        (own, other, *powers, tau_load, coef, stress, normal, rate, change),
         (
             pltpu.VMEM((size, members), wide),
             pltpu.VMEM((size, members), wide),

time: 49 us -> 48.5 us (0.990)
  waiting for transfers between devices: 15.9 us -> 14.4 us
    ppermute x2, waiting for transfers between devices: 1.55 us -> 0.83 us  [lattice(): lax.ppermute(add(blocks[early:], early, 1, sums, narrow), 'col', swap)]
    ppermute x14, waiting for transfers between devices: 14.3 us -> 13.6 us  [swapped(): lax.ppermute(data, 'row', [(row, row ^ mask) for row in range(count)])]
    pallas_call x10 -> x11, Pallas kernels: 12.6 us -> 12.9 us  [on_core(): pl.pallas_call(kernel, out_shape=outs, in_specs=[hbm] * len(far) + [vmem]...]
  transfers between devices with their start and end apart: 16 -> 16, of which waited for: 10 -> 10; matrix products, arithmetic and copies ran while one was open for 0% -> 0% of each run, Pallas kernels for 11% -> 14%
where the time goes in v12:
time: 48.5 us; the launch traced here: 48.2 us
  starting transfers between devices  20.1 us (41%)
  waiting for transfers between devices  14.4 us (30%)
  Pallas kernels  12.9 us (27%)
  between operations  0.79 us (2%)
    ppermute x14, starting transfers between devices, swapped(): lax.ppermute(data, 'row', [(row, row ^ mask) for row in range(count)])  20 us
    ppermute x14, waiting for transfers between devices, swapped(): lax.ppermute(data, 'row', [(row, row ^ mask) for row in range(count)])  13.6 us
    pallas_call x11, Pallas kernels, on_core(): pl.pallas_call(kernel, out_shape=outs, in_specs=[hbm] * len(far) + [vmem]...  12.9 us
  transfers between devices with their start and end apart: 16, of which 10 were waited for; matrix products, arithmetic and copies ran while one was open for 0% of the time, Pallas kernels for 14%

profile of v12, /device:TPU:0, one launch (start us, length us, event | category | flops | bytes accessed | tf_op | source)
XLA Modules:
  0.0 48.2 jit_solution(11672086210960346547)
XLA Ops:
  0.6 0.0 copy-start
  0.6 1.0 %shard_map.123.refs_0_ = bf16[256,256]{1,0:T(8,128)(2,1)S(1)} custom-call(f32[256,256]{1,0:T(8,128)} %wide_ref.1), custom_call_target="tpu_custom_call" | custom-call | bytes 262144 | tf_op jit(solution)/shard_map/pallas_call | solution.py:254
  1.7 4.1 %collective-permute-start.1 = (bf16[256,256]{1,0:T(8,128)(2,1)S(1)}, bf16[256,256]{1,0:T(8,128)(2,1)S(1)}, u32[]{:S(2)}, u32[]{:S(2)}) collective-permute-start(bf16[256,256]{1,0:T(8,128)(2,1)S(1)} %shard_map.123.refs_0_), channel_id=1, source_target_pairs={{0,8},{2,10},{4,12},{6,14},{8,0},{10,2},{12,4},{14,6},{1,9},{3,11}... | collective-permute-start | bytes 393224 | tf_op jit(solution)/shard_map/ppermute | solution.py:31
  5.8 1.6 %collective-permute-start.6 = (bf16[256,256]{1,0:T(8,128)(2,1)S(1)}, bf16[256,256]{1,0:T(8,128)(2,1)S(1)}, u32[]{:S(2)}, u32[]{:S(2)}) collective-permute-start(bf16[256,256]{1,0:T(8,128)(2,1)S(1)} %shard_map.123.refs_0_), channel_id=1, source_target_pairs={{0,4},{2,6},{4,0},{6,2},{8,12},{10,14},{12,8},{14,10},{1,5},{3,7},... | collective-permute-start | bytes 393224 | tf_op jit(solution)/shard_map/ppermute | solution.py:31
  7.4 1.5 %collective-permute-start.5 = (bf16[256,256]{1,0:T(8,128)(2,1)S(1)}, bf16[256,256]{1,0:T(8,128)(2,1)S(1)}, u32[]{:S(2)}, u32[]{:S(2)}) collective-permute-start(bf16[256,256]{1,0:T(8,128)(2,1)S(1)} %shard_map.123.refs_0_), channel_id=1, source_target_pairs={{0,2},{2,0},{4,6},{6,4},{8,10},{10,8},{12,14},{14,12},{1,3},{3,1},... | collective-permute-start | bytes 393224 | tf_op jit(solution)/shard_map/ppermute | solution.py:31
  8.9 0.4 collective-permute-start
  9.3 2.9 %collective-permute-done.1.refs_2_ = bf16[256,256]{1,0:T(8,128)(2,1)S(1)} collective-permute-done((bf16[256,256]{1,0:T(8,128)(2,1)S(1)}, bf16[256,256]{1,0:T(8,128)(2,1)S(1)}, u32[]{:S(2)}, u32[]{:S(2)}) %collective-permute-start.1) | collective-permute-done | bytes 131104 | tf_op jit(solution)/shard_map/ppermute | solution.py:31
  12.2 1.6 %collective-permute-start.4 = (bf16[256,256]{1,0:T(8,128)(2,1)S(1)}, bf16[256,256]{1,0:T(8,128)(2,1)S(1)}, u32[]{:S(2)}, u32[]{:S(2)}) collective-permute-start(bf16[256,256]{1,0:T(8,128)(2,1)S(1)} %collective-permute-done.1.refs_2_), channel_id=1, source_target_pairs={{0,6},{2,4},{4,2},{6,0},{8,14},{10,12},{12,10},{14,8},{1,7},{3,5},... | collective-permute-start | bytes 393224 | tf_op jit(solution)/shard_map/ppermute | solution.py:31
  13.8 1.4 %collective-permute-start.3 = (bf16[256,256]{1,0:T(8,128)(2,1)S(1)}, bf16[256,256]{1,0:T(8,128)(2,1)S(1)}, u32[]{:S(2)}, u32[]{:S(2)}) collective-permute-start(bf16[256,256]{1,0:T(8,128)(2,1)S(1)} %collective-permute-done.1.refs_2_), channel_id=1, source_target_pairs={{0,4},{2,6},{4,0},{6,2},{8,12},{10,14},{12,8},{14,10},{1,5},{3,7},... | collective-permute-start | bytes 393224 | tf_op jit(solution)/shard_map/ppermute | solution.py:31
  15.2 0.0 collective-permute-done.6.refs_3_
  15.2 0.5 collective-permute-start.2
  15.7 1.8 %shard_map.122 = (bf16[8,2,32,256]{3,2,1,0:T(8,128)(2,1)S(1)}, bf16[2,512,256]{2,1,0:T(8,128)(2,1)S(1)}, f32[5,256,128]{2,1,0:T(8,128)S(1)}, f32[256,256]{1,0:T(...) custom-call(s32[2,8]{1,0:T(2,128)} %refs_0_.1, bf16[2,8,32,256]{3,2,1,0:T(8,128)(2,1)} %refs_1_.1, ...), custom_call_target="tpu_custom_call" | custom-call | bytes 1051712 | tf_op jit(solution)/shard_map/pallas_call | solution.py:254
  17.4 0.0 collective-permute-done.5.refs_1_
  17.5 0.0 copy-done
  17.5 1.3 %shard_map.124.refs_4_ = f32[2,2,256,256]{3,2,1,0:T(8,128)S(1)} custom-call(s32[2,2]{1,0:T(2,128)} %near_any.11, bf16[8,2,32,256]{3,2,1,0:T(8,128)(2,1)S(1)} %get-tuple-element.24.v_ref, bf16[2,512,256]{2,1,0:T(8,128)(2,1)S(1)} %get-tuple-element.25.u_ref, bf16[2,2,2,256,256]{4,3,2,1,0:T(8,128)(2,1)S(1)} %copy-done, ...), custom_call_target="tpu_custom_call" | custom-call | flops 100663296 | bytes 2359312 | tf_op jit(solution)/shard_map/pallas_call | solution.py:254
  18.8 0.0 collective-permute-done.refs_0_
  18.8 1.1 %collective-permute-done.4.refs_3_ = bf16[256,256]{1,0:T(8,128)(2,1)S(1)} collective-permute-done((bf16[256,256]{1,0:T(8,128)(2,1)S(1)}, bf16[256,256]{1,0:T(8,128)(2,1)S(1)}, u32[]{:S(2)}, u32[]{:S(2)}) %collective-permute-start.4) | collective-permute-done | bytes 131104 | tf_op jit(solution)/shard_map/ppermute | solution.py:31
  19.9 0.9 %collective-permute-done.3.refs_2_ = bf16[256,256]{1,0:T(8,128)(2,1)S(1)} collective-permute-done((bf16[256,256]{1,0:T(8,128)(2,1)S(1)}, bf16[256,256]{1,0:T(8,128)(2,1)S(1)}, u32[]{:S(2)}, u32[]{:S(2)}) %collective-permute-start.3) | collective-permute-done | bytes 131104 | tf_op jit(solution)/shard_map/ppermute | solution.py:31
  20.8 1.0 %collective-permute-done.2.refs_1_ = bf16[256,256]{1,0:T(8,128)(2,1)S(1)} collective-permute-done((bf16[256,256]{1,0:T(8,128)(2,1)S(1)}, bf16[256,256]{1,0:T(8,128)(2,1)S(1)}, u32[]{:S(2)}, u32[]{:S(2)}) %collective-permute-start.2) | collective-permute-done | bytes 131104 | tf_op jit(solution)/shard_map/ppermute | solution.py:31
  21.8 1.1 %shard_map.126 = bf16[2,256,256]{2,1,0:T(8,128)(2,1)S(1)} custom-call(s32[2,2]{1,0:T(2,128)} %near_any.11, bf16[8,2,32,256]{3,2,1,0:T(8,128)(2,1)S(1)} %get-tuple-element.24.v_ref, bf16[2,512,256]{2,1,0:T(8,128)(2,1)S(1)} %get-tuple-element.25.u_ref, bf16[2,2,2,256,256]{4,3,2,1,0:T(8,128)(2,1)S(1)} %copy-done, ...), custom_call_target="tpu_custom_call" | custom-call | flops 50331648 | bytes 3407888 | tf_op jit(solution)/shard_map/pallas_call | solution.py:254
  22.9 0.0 copy-start.1
  22.9 0.1 collective-permute-start.7
  23.0 1.1 %shard_map.125.own = f32[2,256,256]{2,1,0:T(8,128)S(1)} custom-call(s32[2,2]{1,0:T(2,128)} %near_any.11, bf16[8,2,32,256]{3,2,1,0:T(8,128)(2,1)S(1)} %get-tuple-element.24.v_ref, bf16[2,512,256]{2,1,0:T(8,128)(2,1)S(1)} %get-tuple-element.25.u_ref, bf16[2,2,2,256,256]{4,3,2,1,0:T(8,128)(2,1)S(1)} %copy-done, ...), custom_call_target="tpu_custom_call" | custom-call | flops 50331648 | bytes 3407888 | tf_op jit(solution)/shard_map/pallas_call | solution.py:254
  24.1 0.4 collective-permute-done.7.other
  24.5 0.0 copy-done.1
  24.5 1.2 %shard_map.127 = (f32[256,256]{1,0:T(8,128)S(1)}, f32[256,256]{1,0:T(8,128)S(1)}, f32[256,256]{1,0:T(8,128)S(1)}, f32[256,256]{1,0:T(8,128)S(1)}, bf16[256,256]{1,0:T(8,128)(2,1)S(1)}) custom-call(f32[2,256,256]{2,1,0:T(8,128)S(1)} %shard_map.125.own, bf16[2,256,256]{2,1,0:T(8,128)(2,1)S(1)} %collective-permute-done.7.other, ...), custom_call_target="tpu_custom_call" | custom-call | flops 13107200 | bytes 2490368 | tf_op jit(solution)/shard_map/pallas_call | solution.py:254
  25.8 1.9 %collective-permute-start.9 = (bf16[256,256]{1,0:T(8,128)(2,1)S(1)}, bf16[256,256]{1,0:T(8,128)(2,1)S(1)}, u32[]{:S(2)}, u32[]{:S(2)}) collective-permute-start(bf16[256,256]{1,0:T(8,128)(2,1)S(1)} %get-tuple-element.39.refs_0_), channel_id=1, source_target_pairs={{0,8},{2,10},{4,12},{6,14},{8,0},{10,2},{12,4},{14,6},{1,9},{3,11}... | collective-permute-start | bytes 393224 | tf_op jit(solution)/shard_map/ppermute | solution.py:31
  27.7 1.7 %collective-permute-start.14 = (bf16[256,256]{1,0:T(8,128)(2,1)S(1)}, bf16[256,256]{1,0:T(8,128)(2,1)S(1)}, u32[]{:S(2)}, u32[]{:S(2)}) collective-permute-start(bf16[256,256]{1,0:T(8,128)(2,1)S(1)} %get-tuple-element.39.refs_0_), channel_id=1, source_target_pairs={{0,4},{2,6},{4,0},{6,2},{8,12},{10,14},{12,8},{14,10},{1,5},{3,7},... | collective-permute-start | bytes 393224 | tf_op jit(solution)/shard_map/ppermute | solution.py:31
  29.4 1.5 %collective-permute-start.13 = (bf16[256,256]{1,0:T(8,128)(2,1)S(1)}, bf16[256,256]{1,0:T(8,128)(2,1)S(1)}, u32[]{:S(2)}, u32[]{:S(2)}) collective-permute-start(bf16[256,256]{1,0:T(8,128)(2,1)S(1)} %get-tuple-element.39.refs_0_), channel_id=1, source_target_pairs={{0,2},{2,0},{4,6},{6,4},{8,10},{10,8},{12,14},{14,12},{1,3},{3,1},... | collective-permute-start | bytes 393224 | tf_op jit(solution)/shard_map/ppermute | solution.py:31
  30.9 0.3 collective-permute-start.8
  31.2 4.0 %collective-permute-done.9.refs_2_ = bf16[256,256]{1,0:T(8,128)(2,1)S(1)} collective-permute-done((bf16[256,256]{1,0:T(8,128)(2,1)S(1)}, bf16[256,256]{1,0:T(8,128)(2,1)S(1)}, u32[]{:S(2)}, u32[]{:S(2)}) %collective-permute-start.9) | collective-permute-done | bytes 131104 | tf_op jit(solution)/shard_map/ppermute | solution.py:31
  35.2 0.0 collective-permute-start.12
  35.2 2.1 %collective-permute-start.11 = (bf16[256,256]{1,0:T(8,128)(2,1)S(1)}, bf16[256,256]{1,0:T(8,128)(2,1)S(1)}, u32[]{:S(2)}, u32[]{:S(2)}) collective-permute-start(bf16[256,256]{1,0:T(8,128)(2,1)S(1)} %collective-permute-done.9.refs_2_), channel_id=1, source_target_pairs={{0,4},{2,6},{4,0},{6,2},{8,12},{10,14},{12,8},{14,10},{1,5},{3,7},... | collective-permute-start | bytes 393224 | tf_op jit(solution)/shard_map/ppermute | solution.py:31
  37.2 0.0 collective-permute-done.14.refs_3_
  37.3 1.4 %collective-permute-start.10 = (bf16[256,256]{1,0:T(8,128)(2,1)S(1)}, bf16[256,256]{1,0:T(8,128)(2,1)S(1)}, u32[]{:S(2)}, u32[]{:S(2)}) collective-permute-start(bf16[256,256]{1,0:T(8,128)(2,1)S(1)} %collective-permute-done.9.refs_2_), channel_id=1, source_target_pairs={{0,2},{2,0},{4,6},{6,4},{8,10},{10,8},{12,14},{14,12},{1,3},{3,1},... | collective-permute-start | bytes 393224 | tf_op jit(solution)/shard_map/ppermute | solution.py:31
  38.7 0.0 copy-done.2
  38.7 0.1 shard_map.128
  38.8 0.0 collective-permute-done.13.refs_1_
  38.8 1.3 %shard_map.129.refs_4_ = f32[2,2,256,256]{3,2,1,0:T(8,128)S(1)} custom-call(s32[2,2]{1,0:T(2,128)} %near_any.11, bf16[8,2,32,256]{3,2,1,0:T(8,128)(2,1)S(1)} %get-tuple-element.24.v_ref, bf16[2,512,256]{2,1,0:T(8,128)(2,1)S(1)} %get-tuple-element.25.u_ref, bf16[2,2,2,256,256]{4,3,2,1,0:T(8,128)(2,1)S(1)} %copy-done, ...), custom_call_target="tpu_custom_call" | custom-call | flops 100663296 | bytes 2359312 | tf_op jit(solution)/shard_map/pallas_call | solution.py:254
  40.1 0.0 collective-permute-done.8.refs_0_
  40.1 2.2 %collective-permute-done.12.refs_3_ = bf16[256,256]{1,0:T(8,128)(2,1)S(1)} collective-permute-done((bf16[256,256]{1,0:T(8,128)(2,1)S(1)}, bf16[256,256]{1,0:T(8,128)(2,1)S(1)}, u32[]{:S(2)}, u32[]{:S(2)}) %collective-permute-start.12) | collective-permute-done | bytes 131104 | tf_op jit(solution)/shard_map/ppermute | solution.py:31
  42.3 1.2 %collective-permute-done.11.refs_2_ = bf16[256,256]{1,0:T(8,128)(2,1)S(1)} collective-permute-done((bf16[256,256]{1,0:T(8,128)(2,1)S(1)}, bf16[256,256]{1,0:T(8,128)(2,1)S(1)}, u32[]{:S(2)}, u32[]{:S(2)}) %collective-permute-start.11) | collective-permute-done | bytes 131104 | tf_op jit(solution)/shard_map/ppermute | solution.py:31
  43.5 0.2 collective-permute-done.10.refs_1_
  43.7 1.1 %shard_map.131 = bf16[2,256,256]{2,1,0:T(8,128)(2,1)S(1)} custom-call(s32[2,2]{1,0:T(2,128)} %near_any.11, bf16[8,2,32,256]{3,2,1,0:T(8,128)(2,1)S(1)} %get-tuple-element.24.v_ref, bf16[2,512,256]{2,1,0:T(8,128)(2,1)S(1)} %get-tuple-element.25.u_ref, bf16[2,2,2,256,256]{4,3,2,1,0:T(8,128)(2,1)S(1)} %copy-done, ...), custom_call_target="tpu_custom_call" | custom-call | flops 50331648 | bytes 3407888 | tf_op jit(solution)/shard_map/pallas_call | solution.py:254
  44.8 0.1 collective-permute-start.15
  44.9 1.1 %shard_map.130.own = f32[2,256,256]{2,1,0:T(8,128)S(1)} custom-call(s32[2,2]{1,0:T(2,128)} %near_any.11, bf16[8,2,32,256]{3,2,1,0:T(8,128)(2,1)S(1)} %get-tuple-element.24.v_ref, bf16[2,512,256]{2,1,0:T(8,128)(2,1)S(1)} %get-tuple-element.25.u_ref, bf16[2,2,2,256,256]{4,3,2,1,0:T(8,128)(2,1)S(1)} %copy-done, ...), custom_call_target="tpu_custom_call" | custom-call | flops 50331648 | bytes 3407888 | tf_op jit(solution)/shard_map/pallas_call | solution.py:254
  46.0 0.4 collective-permute-done.15.other
  46.4 1.8 %shard_map.132 = (f32[256,256]{1,0:T(8,128)}, f32[256,256]{1,0:T(8,128)}) custom-call(f32[2,256,256]{2,1,0:T(8,128)S(1)} %shard_map.130.own, bf16[2,256,256]{2,1,0:T(8,128)(2,1)S(1)} %collective-permute-done.15.other, f32[256,256]{1,0:T(8,128)S(1)} %get-tuple-element.40.weight, f32[256,256]{1,0:T(8,128)S(1)} %get-tuple-element.41.unweight, ...), custom_call_target="tpu_custom_call" | custom-call | flops 13107200 | bytes 3538944 | tf_op jit(solution)/shard_map/pallas_call | solution.py:254
  (1 shorter events, 0.0 us)
Async XLA Ops:
  0.6 16.8 %copy-start = (bf16[2,2,2,256,256]{4,3,2,1,0:T(8,128)(2,1)S(1)}, bf16[2,2,2,256,256]{4,3,2,1,0:T(8,128)(2,1)}, u32[]{:S(2)}) copy-start(bf16[2,2,2,256,256]{4,3,2,1,0:T(8,128)(2,1)} %d_ref.11) | copy-start | bytes 3145732
  1.7 10.5 %collective-permute-start.1 = (bf16[256,256]{1,0:T(8,128)(2,1)S(1)}, bf16[256,256]{1,0:T(8,128)(2,1)S(1)}, u32[]{:S(2)}, u32[]{:S(2)}) collective-permute-start(bf16[256,256]{1,0:T(8,128)(2,1)S(1)} %shard_map.123.refs_0_), channel_id=1, source_target_pairs={{0,8},{2,10},{4,12},{6,14},{8,0},{10,2},{12,4},{14,6},{1,9},{3,11}... | collective-permute-start | bytes 393224 | tf_op jit(solution)/shard_map/ppermute | solution.py:31
  5.8 9.4 %collective-permute-start.6 = (bf16[256,256]{1,0:T(8,128)(2,1)S(1)}, bf16[256,256]{1,0:T(8,128)(2,1)S(1)}, u32[]{:S(2)}, u32[]{:S(2)}) collective-permute-start(bf16[256,256]{1,0:T(8,128)(2,1)S(1)} %shard_map.123.refs_0_), channel_id=1, source_target_pairs={{0,4},{2,6},{4,0},{6,2},{8,12},{10,14},{12,8},{14,10},{1,5},{3,7},... | collective-permute-start | bytes 393224 | tf_op jit(solution)/shard_map/ppermute | solution.py:31
  7.4 10.1 %collective-permute-start.5 = (bf16[256,256]{1,0:T(8,128)(2,1)S(1)}, bf16[256,256]{1,0:T(8,128)(2,1)S(1)}, u32[]{:S(2)}, u32[]{:S(2)}) collective-permute-start(bf16[256,256]{1,0:T(8,128)(2,1)S(1)} %shard_map.123.refs_0_), channel_id=1, source_target_pairs={{0,2},{2,0},{4,6},{6,4},{8,10},{10,8},{12,14},{14,12},{1,3},{3,1},... | collective-permute-start | bytes 393224 | tf_op jit(solution)/shard_map/ppermute | solution.py:31
  8.9 9.9 %collective-permute-start = (bf16[256,256]{1,0:T(8,128)(2,1)S(1)}, bf16[256,256]{1,0:T(8,128)(2,1)S(1)}, u32[]{:S(2)}, u32[]{:S(2)}) collective-permute-start(bf16[256,256]{1,0:T(8,128)(2,1)S(1)} %shard_map.123.refs_0_), channel_id=1, source_target_pairs={{0,6},{2,4},{4,2},{6,0},{8,14},{10,12},{12,10},{14,8},{1,7},{3,5},... | collective-permute-start | bytes 393224 | tf_op jit(solution)/shard_map/ppermute | solution.py:31
  12.2 7.7 %collective-permute-start.4 = (bf16[256,256]{1,0:T(8,128)(2,1)S(1)}, bf16[256,256]{1,0:T(8,128)(2,1)S(1)}, u32[]{:S(2)}, u32[]{:S(2)}) collective-permute-start(bf16[256,256]{1,0:T(8,128)(2,1)S(1)} %collective-permute-done.1.refs_2_), channel_id=1, source_target_pairs={{0,6},{2,4},{4,2},{6,0},{8,14},{10,12},{12,10},{14,8},{1,7},{3,5},... | collective-permute-start | bytes 393224 | tf_op jit(solution)/shard_map/ppermute | solution.py:31
  13.8 7.0 %collective-permute-start.3 = (bf16[256,256]{1,0:T(8,128)(2,1)S(1)}, bf16[256,256]{1,0:T(8,128)(2,1)S(1)}, u32[]{:S(2)}, u32[]{:S(2)}) collective-permute-start(bf16[256,256]{1,0:T(8,128)(2,1)S(1)} %collective-permute-done.1.refs_2_), channel_id=1, source_target_pairs={{0,4},{2,6},{4,0},{6,2},{8,12},{10,14},{12,8},{14,10},{1,5},{3,7},... | collective-permute-start | bytes 393224 | tf_op jit(solution)/shard_map/ppermute | solution.py:31
  15.2 6.6 %collective-permute-start.2 = (bf16[256,256]{1,0:T(8,128)(2,1)S(1)}, bf16[256,256]{1,0:T(8,128)(2,1)S(1)}, u32[]{:S(2)}, u32[]{:S(2)}) collective-permute-start(bf16[256,256]{1,0:T(8,128)(2,1)S(1)} %collective-permute-done.1.refs_2_), channel_id=1, source_target_pairs={{0,2},{2,0},{4,6},{6,4},{8,10},{10,8},{12,14},{14,12},{1,3},{3,1},... | collective-permute-start | bytes 393224 | tf_op jit(solution)/shard_map/ppermute | solution.py:31
  22.9 1.6 %copy-start.1 = (f32[256,256]{1,0:T(8,128)S(1)}, f32[256,256]{1,0:T(8,128)}, u32[]{:S(2)}) copy-start(f32[256,256]{1,0:T(8,128)} %tau.3) | copy-start | bytes 786436
  22.9 1.6 %collective-permute-start.7 = (bf16[2,256,256]{2,1,0:T(8,128)(2,1)S(1)}, bf16[2,256,256]{2,1,0:T(8,128)(2,1)S(1)}, u32[]{:S(2)}, u32[]{:S(2)}) collective-permute-start(bf16[2,256,256]{2,1,0:T(8,128)(2,1)S(1)} %shard_map.126), channel_id=1, source_target_pairs={{0,1},{1,0},{2,3},{3,2},{4,5},{5,4},{6,7},{7,6},{8,9},{9,8},{10,11... | collective-permute-start | bytes 786440 | tf_op jit(solution)/shard_map/ppermute | solution.py:354
  24.5 14.1 %copy-start.2 = (f32[256,256]{1,0:T(8,128)S(1)}, f32[256,256]{1,0:T(8,128)}, u32[]{:S(2)}) copy-start(f32[256,256]{1,0:T(8,128)} %state.1) | copy-start | bytes 786436
  25.8 9.4 %collective-permute-start.9 = (bf16[256,256]{1,0:T(8,128)(2,1)S(1)}, bf16[256,256]{1,0:T(8,128)(2,1)S(1)}, u32[]{:S(2)}, u32[]{:S(2)}) collective-permute-start(bf16[256,256]{1,0:T(8,128)(2,1)S(1)} %get-tuple-element.39.refs_0_), channel_id=1, source_target_pairs={{0,8},{2,10},{4,12},{6,14},{8,0},{10,2},{12,4},{14,6},{1,9},{3,11}... | collective-permute-start | bytes 393224 | tf_op jit(solution)/shard_map/ppermute | solution.py:31
  27.7 9.6 %collective-permute-start.14 = (bf16[256,256]{1,0:T(8,128)(2,1)S(1)}, bf16[256,256]{1,0:T(8,128)(2,1)S(1)}, u32[]{:S(2)}, u32[]{:S(2)}) collective-permute-start(bf16[256,256]{1,0:T(8,128)(2,1)S(1)} %get-tuple-element.39.refs_0_), channel_id=1, source_target_pairs={{0,4},{2,6},{4,0},{6,2},{8,12},{10,14},{12,8},{14,10},{1,5},{3,7},... | collective-permute-start | bytes 393224 | tf_op jit(solution)/shard_map/ppermute | solution.py:31
  29.4 9.4 %collective-permute-start.13 = (bf16[256,256]{1,0:T(8,128)(2,1)S(1)}, bf16[256,256]{1,0:T(8,128)(2,1)S(1)}, u32[]{:S(2)}, u32[]{:S(2)}) collective-permute-start(bf16[256,256]{1,0:T(8,128)(2,1)S(1)} %get-tuple-element.39.refs_0_), channel_id=1, source_target_pairs={{0,2},{2,0},{4,6},{6,4},{8,10},{10,8},{12,14},{14,12},{1,3},{3,1},... | collective-permute-start | bytes 393224 | tf_op jit(solution)/shard_map/ppermute | solution.py:31
  30.9 9.2 %collective-permute-start.8 = (bf16[256,256]{1,0:T(8,128)(2,1)S(1)}, bf16[256,256]{1,0:T(8,128)(2,1)S(1)}, u32[]{:S(2)}, u32[]{:S(2)}) collective-permute-start(bf16[256,256]{1,0:T(8,128)(2,1)S(1)} %get-tuple-element.39.refs_0_), channel_id=1, source_target_pairs={{0,6},{2,4},{4,2},{6,0},{8,14},{10,12},{12,10},{14,8},{1,7},{3,5},... | collective-permute-start | bytes 393224 | tf_op jit(solution)/shard_map/ppermute | solution.py:31
  35.2 7.2 %collective-permute-start.12 = (bf16[256,256]{1,0:T(8,128)(2,1)S(1)}, bf16[256,256]{1,0:T(8,128)(2,1)S(1)}, u32[]{:S(2)}, u32[]{:S(2)}) collective-permute-start(bf16[256,256]{1,0:T(8,128)(2,1)S(1)} %collective-permute-done.9.refs_2_), channel_id=1, source_target_pairs={{0,6},{2,4},{4,2},{6,0},{8,14},{10,12},{12,10},{14,8},{1,7},{3,5},... | collective-permute-start | bytes 393224 | tf_op jit(solution)/shard_map/ppermute | solution.py:31
  35.2 8.3 %collective-permute-start.11 = (bf16[256,256]{1,0:T(8,128)(2,1)S(1)}, bf16[256,256]{1,0:T(8,128)(2,1)S(1)}, u32[]{:S(2)}, u32[]{:S(2)}) collective-permute-start(bf16[256,256]{1,0:T(8,128)(2,1)S(1)} %collective-permute-done.9.refs_2_), channel_id=1, source_target_pairs={{0,4},{2,6},{4,0},{6,2},{8,12},{10,14},{12,8},{14,10},{1,5},{3,7},... | collective-permute-start | bytes 393224 | tf_op jit(solution)/shard_map/ppermute | solution.py:31
  37.3 6.5 %collective-permute-start.10 = (bf16[256,256]{1,0:T(8,128)(2,1)S(1)}, bf16[256,256]{1,0:T(8,128)(2,1)S(1)}, u32[]{:S(2)}, u32[]{:S(2)}) collective-permute-start(bf16[256,256]{1,0:T(8,128)(2,1)S(1)} %collective-permute-done.9.refs_2_), channel_id=1, source_target_pairs={{0,2},{2,0},{4,6},{6,4},{8,10},{10,8},{12,14},{14,12},{1,3},{3,1},... | collective-permute-start | bytes 393224 | tf_op jit(solution)/shard_map/ppermute | solution.py:31
  44.8 1.6 %collective-permute-start.15 = (bf16[2,256,256]{2,1,0:T(8,128)(2,1)S(1)}, bf16[2,256,256]{2,1,0:T(8,128)(2,1)S(1)}, u32[]{:S(2)}, u32[]{:S(2)}) collective-permute-start(bf16[2,256,256]{2,1,0:T(8,128)(2,1)S(1)} %shard_map.131), channel_id=1, source_target_pairs={{0,1},{1,0},{2,3},{3,2},{4,5},{5,4},{6,7},{7,6},{8,9},{9,8},{10,11... | collective-permute-start | bytes 786440 | tf_op jit(solution)/shard_map/ppermute | solution.py:354

commit v13 on v12

--- a/solution.py
+++ b/solution.py
@@ -39,22 +39,23 @@
     return [found[mask] for mask in arrivals(count, True)]
 
 
-PIECES = 8
-
-
-def row_pieces(size):
-    tall = size // PIECES
-    return [pl.ds(at * tall, tall) for at in range(PIECES)]
+IN_PIECES = 8
+OUT_PIECES = 4
+
+
+def row_pieces(size, pieces):
+    tall = size // pieces
+    return [pl.ds(at * tall, tall) for at in range(pieces)]
 
 
 def narrow_kernel(wide_ref, narrow_ref, held, sem):
     copies = [
         pltpu.make_async_copy(wide_ref.at[part], held.at[part], sem.at[at])
-        for at, part in enumerate(row_pieces(held.shape[0]))
+        for at, part in enumerate(row_pieces(held.shape[0], IN_PIECES))
     ]
     for copy in copies:
         copy.start()
-    for copy, part in zip(copies, row_pieces(held.shape[0])):
+    for copy, part in zip(copies, row_pieces(held.shape[0], IN_PIECES)):
         copy.wait()
         narrow_ref[part, :] = held[part, :].astype(narrow_ref.dtype)
 
@@ -136,12 +137,17 @@
     lanes = slice(first * rank_count, (first + len(blocks)) * rank_count)
     near_copy.wait()
     for place, p in enumerate(chosen):
-        total = jnp.dot(u_ref[p, :, lanes], proj[place], preferred_element_type=jnp.float32)
+        weights, fields = [u_ref[p, :, lanes]], [proj[place]]
         for s in range(slots):
             near = near_ref[p, s] - col * count
             at = len(blocks) - sum(jnp.where(near == q, len(blocks) - i, 0) for i, q in enumerate(met))
-            weights = jnp.concatenate([d_ref[kind, p, s] for kind in range(kinds)], axis=0)
-            total += jnp.dot(weights, x_all[at], preferred_element_type=jnp.float32)
+            weights.append(jnp.concatenate([d_ref[kind, p, s] for kind in range(kinds)], axis=0))
+            fields.append(x_all[at])
+        total = jnp.dot(
+            jnp.concatenate(weights, axis=1),
+            jnp.concatenate(fields, axis=0),
+            preferred_element_type=jnp.float32,
+        )
         for kind in range(kinds):
             piece = total[kind * size : (kind + 1) * size]
             if before:
@@ -181,7 +187,7 @@
 
 
 def over_pieces(begin, tall, members, lanes, work):
-    step = min(tall, 32)
+    step = min(tall, 64)
 
     @pl.loop(0, tall // step)
     def _(index):
@@ -239,7 +245,7 @@
         mean_change[rows, part] = (change[rows, part] + second) * 0.5
 
     copies = []
-    for at, part in enumerate(row_pieces(size)):
+    for at, part in enumerate(row_pieces(size, OUT_PIECES)):
         over_pieces(part.start, part.size, members, coef.shape[2], work)
         for kind, (held, out) in enumerate(((mean_rate, rate_out), (mean_change, change_out))):
             copies.append(pltpu.make_async_copy(held.at[part], out.at[part], sem.at[kind, at]))
@@ -358,7 +364,7 @@
         narrow_kernel,
         shaped(size, members, kind=narrow),
         (),
-        (pltpu.VMEM((size, members), wide), pltpu.SemaphoreType.DMA((PIECES,))),
+        (pltpu.VMEM((size, members), wide), pltpu.SemaphoreType.DMA((IN_PIECES,))),
         far=(slip_deficit,),
     )
     own, other, powers = lattice(slip_half, powers)
@@ -377,7 +383,7 @@
         (
             pltpu.VMEM((size, members), wide),
             pltpu.VMEM((size, members), wide),
-            pltpu.SemaphoreType.DMA((2, PIECES)),
+            pltpu.SemaphoreType.DMA((2, OUT_PIECES)),
         ),
         flops=200 * size * members,
         out_far=True,

time: 48.5 us -> 48.3 us (level)
  no operation moved by 1% of the time
where the time goes in v13:
time: 48.3 us; the launch traced here: 48 us
  starting transfers between devices  20.1 us (42%)
  waiting for transfers between devices  14.4 us (30%)
  Pallas kernels  12.7 us (26%)
  between operations  0.78 us (2%)
    ppermute x14, starting transfers between devices, swapped(): lax.ppermute(data, 'row', [(row, row ^ mask) for row in range(count)])  20 us
    ppermute x14, waiting for transfers between devices, swapped(): lax.ppermute(data, 'row', [(row, row ^ mask) for row in range(count)])  13.6 us
    pallas_call x11, Pallas kernels, on_core(): pl.pallas_call(kernel, out_shape=outs, in_specs=[hbm] * len(far) + [vmem]...  12.7 us
  transfers between devices with their start and end apart: 16, of which 10 were waited for; matrix products, arithmetic and copies ran while one was open for 0% of the time, Pallas kernels for 14%

profile of v13, /device:TPU:0, one launch (start us, length us, event | category | flops | bytes accessed | tf_op | source)
XLA Modules:
  0.0 48.0 jit_solution(10763461516916499613)
XLA Ops:
  0.6 0.0 copy-start
  0.6 1.0 %shard_map.123.refs_0_ = bf16[256,256]{1,0:T(8,128)(2,1)S(1)} custom-call(f32[256,256]{1,0:T(8,128)} %wide_ref.1), custom_call_target="tpu_custom_call" | custom-call | bytes 262144 | tf_op jit(solution)/shard_map/pallas_call | solution.py:260
  1.7 4.1 %collective-permute-start.1 = (bf16[256,256]{1,0:T(8,128)(2,1)S(1)}, bf16[256,256]{1,0:T(8,128)(2,1)S(1)}, u32[]{:S(2)}, u32[]{:S(2)}) collective-permute-start(bf16[256,256]{1,0:T(8,128)(2,1)S(1)} %shard_map.123.refs_0_), channel_id=1, source_target_pairs={{0,8},{2,10},{4,12},{6,14},{8,0},{10,2},{12,4},{14,6},{1,9},{3,11}... | collective-permute-start | bytes 393224 | tf_op jit(solution)/shard_map/ppermute | solution.py:31
  5.8 1.6 %collective-permute-start.6 = (bf16[256,256]{1,0:T(8,128)(2,1)S(1)}, bf16[256,256]{1,0:T(8,128)(2,1)S(1)}, u32[]{:S(2)}, u32[]{:S(2)}) collective-permute-start(bf16[256,256]{1,0:T(8,128)(2,1)S(1)} %shard_map.123.refs_0_), channel_id=1, source_target_pairs={{0,4},{2,6},{4,0},{6,2},{8,12},{10,14},{12,8},{14,10},{1,5},{3,7},... | collective-permute-start | bytes 393224 | tf_op jit(solution)/shard_map/ppermute | solution.py:31
  7.4 1.5 %collective-permute-start.5 = (bf16[256,256]{1,0:T(8,128)(2,1)S(1)}, bf16[256,256]{1,0:T(8,128)(2,1)S(1)}, u32[]{:S(2)}, u32[]{:S(2)}) collective-permute-start(bf16[256,256]{1,0:T(8,128)(2,1)S(1)} %shard_map.123.refs_0_), channel_id=1, source_target_pairs={{0,2},{2,0},{4,6},{6,4},{8,10},{10,8},{12,14},{14,12},{1,3},{3,1},... | collective-permute-start | bytes 393224 | tf_op jit(solution)/shard_map/ppermute | solution.py:31
  8.9 0.4 collective-permute-start
  9.3 2.9 %collective-permute-done.1.refs_2_ = bf16[256,256]{1,0:T(8,128)(2,1)S(1)} collective-permute-done((bf16[256,256]{1,0:T(8,128)(2,1)S(1)}, bf16[256,256]{1,0:T(8,128)(2,1)S(1)}, u32[]{:S(2)}, u32[]{:S(2)}) %collective-permute-start.1) | collective-permute-done | bytes 131104 | tf_op jit(solution)/shard_map/ppermute | solution.py:31
  12.2 1.6 %collective-permute-start.4 = (bf16[256,256]{1,0:T(8,128)(2,1)S(1)}, bf16[256,256]{1,0:T(8,128)(2,1)S(1)}, u32[]{:S(2)}, u32[]{:S(2)}) collective-permute-start(bf16[256,256]{1,0:T(8,128)(2,1)S(1)} %collective-permute-done.1.refs_2_), channel_id=1, source_target_pairs={{0,6},{2,4},{4,2},{6,0},{8,14},{10,12},{12,10},{14,8},{1,7},{3,5},... | collective-permute-start | bytes 393224 | tf_op jit(solution)/shard_map/ppermute | solution.py:31
  13.8 1.4 %collective-permute-start.3 = (bf16[256,256]{1,0:T(8,128)(2,1)S(1)}, bf16[256,256]{1,0:T(8,128)(2,1)S(1)}, u32[]{:S(2)}, u32[]{:S(2)}) collective-permute-start(bf16[256,256]{1,0:T(8,128)(2,1)S(1)} %collective-permute-done.1.refs_2_), channel_id=1, source_target_pairs={{0,4},{2,6},{4,0},{6,2},{8,12},{10,14},{12,8},{14,10},{1,5},{3,7},... | collective-permute-start | bytes 393224 | tf_op jit(solution)/shard_map/ppermute | solution.py:31
  15.2 0.0 collective-permute-done.6.refs_3_
  15.2 0.5 collective-permute-start.2
  15.7 1.8 %shard_map.122 = (bf16[8,2,32,256]{3,2,1,0:T(8,128)(2,1)S(1)}, bf16[2,512,256]{2,1,0:T(8,128)(2,1)S(1)}, f32[5,256,128]{2,1,0:T(8,128)S(1)}, f32[256,256]{1,0:T(...) custom-call(s32[2,8]{1,0:T(2,128)} %refs_0_.1, bf16[2,8,32,256]{3,2,1,0:T(8,128)(2,1)} %refs_1_.1, ...), custom_call_target="tpu_custom_call" | custom-call | bytes 1051712 | tf_op jit(solution)/shard_map/pallas_call | solution.py:260
  17.4 0.0 collective-permute-done.5.refs_1_
  17.5 0.0 copy-done
  17.5 1.3 %shard_map.124.refs_4_ = f32[2,2,256,256]{3,2,1,0:T(8,128)S(1)} custom-call(s32[2,2]{1,0:T(2,128)} %near_any.11, bf16[8,2,32,256]{3,2,1,0:T(8,128)(2,1)S(1)} %get-tuple-element.24.v_ref, bf16[2,512,256]{2,1,0:T(8,128)(2,1)S(1)} %get-tuple-element.25.u_ref, bf16[2,2,2,256,256]{4,3,2,1,0:T(8,128)(2,1)S(1)} %copy-done, ...), custom_call_target="tpu_custom_call" | custom-call | flops 100663296 | bytes 2359312 | tf_op jit(solution)/shard_map/pallas_call | solution.py:260
  18.8 0.0 collective-permute-done.refs_0_
  18.8 1.1 %collective-permute-done.4.refs_3_ = bf16[256,256]{1,0:T(8,128)(2,1)S(1)} collective-permute-done((bf16[256,256]{1,0:T(8,128)(2,1)S(1)}, bf16[256,256]{1,0:T(8,128)(2,1)S(1)}, u32[]{:S(2)}, u32[]{:S(2)}) %collective-permute-start.4) | collective-permute-done | bytes 131104 | tf_op jit(solution)/shard_map/ppermute | solution.py:31
  19.9 0.9 %collective-permute-done.3.refs_2_ = bf16[256,256]{1,0:T(8,128)(2,1)S(1)} collective-permute-done((bf16[256,256]{1,0:T(8,128)(2,1)S(1)}, bf16[256,256]{1,0:T(8,128)(2,1)S(1)}, u32[]{:S(2)}, u32[]{:S(2)}) %collective-permute-start.3) | collective-permute-done | bytes 131104 | tf_op jit(solution)/shard_map/ppermute | solution.py:31
  20.8 1.0 %collective-permute-done.2.refs_1_ = bf16[256,256]{1,0:T(8,128)(2,1)S(1)} collective-permute-done((bf16[256,256]{1,0:T(8,128)(2,1)S(1)}, bf16[256,256]{1,0:T(8,128)(2,1)S(1)}, u32[]{:S(2)}, u32[]{:S(2)}) %collective-permute-start.2) | collective-permute-done | bytes 131104 | tf_op jit(solution)/shard_map/ppermute | solution.py:31
  21.8 1.1 %shard_map.126 = bf16[2,256,256]{2,1,0:T(8,128)(2,1)S(1)} custom-call(s32[2,2]{1,0:T(2,128)} %near_any.11, bf16[8,2,32,256]{3,2,1,0:T(8,128)(2,1)S(1)} %get-tuple-element.24.v_ref, bf16[2,512,256]{2,1,0:T(8,128)(2,1)S(1)} %get-tuple-element.25.u_ref, bf16[2,2,2,256,256]{4,3,2,1,0:T(8,128)(2,1)S(1)} %copy-done, ...), custom_call_target="tpu_custom_call" | custom-call | flops 50331648 | bytes 3407888 | tf_op jit(solution)/shard_map/pallas_call | solution.py:260
  22.9 0.0 copy-start.1
  23.0 0.1 collective-permute-start.7
  23.0 1.1 %shard_map.125.own = f32[2,256,256]{2,1,0:T(8,128)S(1)} custom-call(s32[2,2]{1,0:T(2,128)} %near_any.11, bf16[8,2,32,256]{3,2,1,0:T(8,128)(2,1)S(1)} %get-tuple-element.24.v_ref, bf16[2,512,256]{2,1,0:T(8,128)(2,1)S(1)} %get-tuple-element.25.u_ref, bf16[2,2,2,256,256]{4,3,2,1,0:T(8,128)(2,1)S(1)} %copy-done, ...), custom_call_target="tpu_custom_call" | custom-call | flops 50331648 | bytes 3407888 | tf_op jit(solution)/shard_map/pallas_call | solution.py:260
  24.2 0.4 collective-permute-done.7.other
  24.6 0.0 copy-done.1
  24.6 1.0 %shard_map.127 = (f32[256,256]{1,0:T(8,128)S(1)}, f32[256,256]{1,0:T(8,128)S(1)}, f32[256,256]{1,0:T(8,128)S(1)}, f32[256,256]{1,0:T(8,128)S(1)}, bf16[256,256]{1,0:T(8,128)(2,1)S(1)}) custom-call(f32[2,256,256]{2,1,0:T(8,128)S(1)} %shard_map.125.own, bf16[2,256,256]{2,1,0:T(8,128)(2,1)S(1)} %collective-permute-done.7.other, ...), custom_call_target="tpu_custom_call" | custom-call | flops 13107200 | bytes 2490368 | tf_op jit(solution)/shard_map/pallas_call | solution.py:260
  25.6 1.9 %collective-permute-start.9 = (bf16[256,256]{1,0:T(8,128)(2,1)S(1)}, bf16[256,256]{1,0:T(8,128)(2,1)S(1)}, u32[]{:S(2)}, u32[]{:S(2)}) collective-permute-start(bf16[256,256]{1,0:T(8,128)(2,1)S(1)} %get-tuple-element.39.refs_0_), channel_id=1, source_target_pairs={{0,8},{2,10},{4,12},{6,14},{8,0},{10,2},{12,4},{14,6},{1,9},{3,11}... | collective-permute-start | bytes 393224 | tf_op jit(solution)/shard_map/ppermute | solution.py:31
  27.5 1.7 %collective-permute-start.14 = (bf16[256,256]{1,0:T(8,128)(2,1)S(1)}, bf16[256,256]{1,0:T(8,128)(2,1)S(1)}, u32[]{:S(2)}, u32[]{:S(2)}) collective-permute-start(bf16[256,256]{1,0:T(8,128)(2,1)S(1)} %get-tuple-element.39.refs_0_), channel_id=1, source_target_pairs={{0,4},{2,6},{4,0},{6,2},{8,12},{10,14},{12,8},{14,10},{1,5},{3,7},... | collective-permute-start | bytes 393224 | tf_op jit(solution)/shard_map/ppermute | solution.py:31
  29.3 1.5 %collective-permute-start.13 = (bf16[256,256]{1,0:T(8,128)(2,1)S(1)}, bf16[256,256]{1,0:T(8,128)(2,1)S(1)}, u32[]{:S(2)}, u32[]{:S(2)}) collective-permute-start(bf16[256,256]{1,0:T(8,128)(2,1)S(1)} %get-tuple-element.39.refs_0_), channel_id=1, source_target_pairs={{0,2},{2,0},{4,6},{6,4},{8,10},{10,8},{12,14},{14,12},{1,3},{3,1},... | collective-permute-start | bytes 393224 | tf_op jit(solution)/shard_map/ppermute | solution.py:31
  30.7 0.3 collective-permute-start.8
  31.0 4.0 %collective-permute-done.9.refs_2_ = bf16[256,256]{1,0:T(8,128)(2,1)S(1)} collective-permute-done((bf16[256,256]{1,0:T(8,128)(2,1)S(1)}, bf16[256,256]{1,0:T(8,128)(2,1)S(1)}, u32[]{:S(2)}, u32[]{:S(2)}) %collective-permute-start.9) | collective-permute-done | bytes 131104 | tf_op jit(solution)/shard_map/ppermute | solution.py:31
  35.0 0.0 collective-permute-start.12
  35.0 2.1 %collective-permute-start.11 = (bf16[256,256]{1,0:T(8,128)(2,1)S(1)}, bf16[256,256]{1,0:T(8,128)(2,1)S(1)}, u32[]{:S(2)}, u32[]{:S(2)}) collective-permute-start(bf16[256,256]{1,0:T(8,128)(2,1)S(1)} %collective-permute-done.9.refs_2_), channel_id=1, source_target_pairs={{0,4},{2,6},{4,0},{6,2},{8,12},{10,14},{12,8},{14,10},{1,5},{3,7},... | collective-permute-start | bytes 393224 | tf_op jit(solution)/shard_map/ppermute | solution.py:31
  37.1 0.0 collective-permute-done.14.refs_3_
  37.1 1.4 %collective-permute-start.10 = (bf16[256,256]{1,0:T(8,128)(2,1)S(1)}, bf16[256,256]{1,0:T(8,128)(2,1)S(1)}, u32[]{:S(2)}, u32[]{:S(2)}) collective-permute-start(bf16[256,256]{1,0:T(8,128)(2,1)S(1)} %collective-permute-done.9.refs_2_), channel_id=1, source_target_pairs={{0,2},{2,0},{4,6},{6,4},{8,10},{10,8},{12,14},{14,12},{1,3},{3,1},... | collective-permute-start | bytes 393224 | tf_op jit(solution)/shard_map/ppermute | solution.py:31
  38.5 0.0 copy-done.2
  38.5 0.1 shard_map.128
  38.6 0.0 collective-permute-done.13.refs_1_
  38.6 1.3 %shard_map.129.refs_4_ = f32[2,2,256,256]{3,2,1,0:T(8,128)S(1)} custom-call(s32[2,2]{1,0:T(2,128)} %near_any.11, bf16[8,2,32,256]{3,2,1,0:T(8,128)(2,1)S(1)} %get-tuple-element.24.v_ref, bf16[2,512,256]{2,1,0:T(8,128)(2,1)S(1)} %get-tuple-element.25.u_ref, bf16[2,2,2,256,256]{4,3,2,1,0:T(8,128)(2,1)S(1)} %copy-done, ...), custom_call_target="tpu_custom_call" | custom-call | flops 100663296 | bytes 2359312 | tf_op jit(solution)/shard_map/pallas_call | solution.py:260
  39.9 0.0 collective-permute-done.8.refs_0_
  39.9 2.2 %collective-permute-done.12.refs_3_ = bf16[256,256]{1,0:T(8,128)(2,1)S(1)} collective-permute-done((bf16[256,256]{1,0:T(8,128)(2,1)S(1)}, bf16[256,256]{1,0:T(8,128)(2,1)S(1)}, u32[]{:S(2)}, u32[]{:S(2)}) %collective-permute-start.12) | collective-permute-done | bytes 131104 | tf_op jit(solution)/shard_map/ppermute | solution.py:31
  42.2 1.2 %collective-permute-done.11.refs_2_ = bf16[256,256]{1,0:T(8,128)(2,1)S(1)} collective-permute-done((bf16[256,256]{1,0:T(8,128)(2,1)S(1)}, bf16[256,256]{1,0:T(8,128)(2,1)S(1)}, u32[]{:S(2)}, u32[]{:S(2)}) %collective-permute-start.11) | collective-permute-done | bytes 131104 | tf_op jit(solution)/shard_map/ppermute | solution.py:31
  43.3 0.2 collective-permute-done.10.refs_1_
  43.6 1.1 %shard_map.131 = bf16[2,256,256]{2,1,0:T(8,128)(2,1)S(1)} custom-call(s32[2,2]{1,0:T(2,128)} %near_any.11, bf16[8,2,32,256]{3,2,1,0:T(8,128)(2,1)S(1)} %get-tuple-element.24.v_ref, bf16[2,512,256]{2,1,0:T(8,128)(2,1)S(1)} %get-tuple-element.25.u_ref, bf16[2,2,2,256,256]{4,3,2,1,0:T(8,128)(2,1)S(1)} %copy-done, ...), custom_call_target="tpu_custom_call" | custom-call | flops 50331648 | bytes 3407888 | tf_op jit(solution)/shard_map/pallas_call | solution.py:260
  44.7 0.1 collective-permute-start.15
  44.8 1.1 %shard_map.130.own = f32[2,256,256]{2,1,0:T(8,128)S(1)} custom-call(s32[2,2]{1,0:T(2,128)} %near_any.11, bf16[8,2,32,256]{3,2,1,0:T(8,128)(2,1)S(1)} %get-tuple-element.24.v_ref, bf16[2,512,256]{2,1,0:T(8,128)(2,1)S(1)} %get-tuple-element.25.u_ref, bf16[2,2,2,256,256]{4,3,2,1,0:T(8,128)(2,1)S(1)} %copy-done, ...), custom_call_target="tpu_custom_call" | custom-call | flops 50331648 | bytes 3407888 | tf_op jit(solution)/shard_map/pallas_call | solution.py:260
  45.9 0.4 collective-permute-done.15.other
  46.3 1.7 %shard_map.132 = (f32[256,256]{1,0:T(8,128)}, f32[256,256]{1,0:T(8,128)}) custom-call(f32[2,256,256]{2,1,0:T(8,128)S(1)} %shard_map.130.own, bf16[2,256,256]{2,1,0:T(8,128)(2,1)S(1)} %collective-permute-done.15.other, f32[256,256]{1,0:T(8,128)S(1)} %get-tuple-element.40.weight, f32[256,256]{1,0:T(8,128)S(1)} %get-tuple-element.41.unweight, ...), custom_call_target="tpu_custom_call" | custom-call | flops 13107200 | bytes 3538944 | tf_op jit(solution)/shard_map/pallas_call | solution.py:260
  (1 shorter events, 0.0 us)
Async XLA Ops:
  0.6 16.8 %copy-start = (bf16[2,2,2,256,256]{4,3,2,1,0:T(8,128)(2,1)S(1)}, bf16[2,2,2,256,256]{4,3,2,1,0:T(8,128)(2,1)}, u32[]{:S(2)}) copy-start(bf16[2,2,2,256,256]{4,3,2,1,0:T(8,128)(2,1)} %d_ref.11) | copy-start | bytes 3145732
  1.7 10.5 %collective-permute-start.1 = (bf16[256,256]{1,0:T(8,128)(2,1)S(1)}, bf16[256,256]{1,0:T(8,128)(2,1)S(1)}, u32[]{:S(2)}, u32[]{:S(2)}) collective-permute-start(bf16[256,256]{1,0:T(8,128)(2,1)S(1)} %shard_map.123.refs_0_), channel_id=1, source_target_pairs={{0,8},{2,10},{4,12},{6,14},{8,0},{10,2},{12,4},{14,6},{1,9},{3,11}... | collective-permute-start | bytes 393224 | tf_op jit(solution)/shard_map/ppermute | solution.py:31
  5.8 9.4 %collective-permute-start.6 = (bf16[256,256]{1,0:T(8,128)(2,1)S(1)}, bf16[256,256]{1,0:T(8,128)(2,1)S(1)}, u32[]{:S(2)}, u32[]{:S(2)}) collective-permute-start(bf16[256,256]{1,0:T(8,128)(2,1)S(1)} %shard_map.123.refs_0_), channel_id=1, source_target_pairs={{0,4},{2,6},{4,0},{6,2},{8,12},{10,14},{12,8},{14,10},{1,5},{3,7},... | collective-permute-start | bytes 393224 | tf_op jit(solution)/shard_map/ppermute | solution.py:31
  7.4 10.1 %collective-permute-start.5 = (bf16[256,256]{1,0:T(8,128)(2,1)S(1)}, bf16[256,256]{1,0:T(8,128)(2,1)S(1)}, u32[]{:S(2)}, u32[]{:S(2)}) collective-permute-start(bf16[256,256]{1,0:T(8,128)(2,1)S(1)} %shard_map.123.refs_0_), channel_id=1, source_target_pairs={{0,2},{2,0},{4,6},{6,4},{8,10},{10,8},{12,14},{14,12},{1,3},{3,1},... | collective-permute-start | bytes 393224 | tf_op jit(solution)/shard_map/ppermute | solution.py:31
  8.9 9.9 %collective-permute-start = (bf16[256,256]{1,0:T(8,128)(2,1)S(1)}, bf16[256,256]{1,0:T(8,128)(2,1)S(1)}, u32[]{:S(2)}, u32[]{:S(2)}) collective-permute-start(bf16[256,256]{1,0:T(8,128)(2,1)S(1)} %shard_map.123.refs_0_), channel_id=1, source_target_pairs={{0,6},{2,4},{4,2},{6,0},{8,14},{10,12},{12,10},{14,8},{1,7},{3,5},... | collective-permute-start | bytes 393224 | tf_op jit(solution)/shard_map/ppermute | solution.py:31
  12.2 7.7 %collective-permute-start.4 = (bf16[256,256]{1,0:T(8,128)(2,1)S(1)}, bf16[256,256]{1,0:T(8,128)(2,1)S(1)}, u32[]{:S(2)}, u32[]{:S(2)}) collective-permute-start(bf16[256,256]{1,0:T(8,128)(2,1)S(1)} %collective-permute-done.1.refs_2_), channel_id=1, source_target_pairs={{0,6},{2,4},{4,2},{6,0},{8,14},{10,12},{12,10},{14,8},{1,7},{3,5},... | collective-permute-start | bytes 393224 | tf_op jit(solution)/shard_map/ppermute | solution.py:31
  13.8 7.0 %collective-permute-start.3 = (bf16[256,256]{1,0:T(8,128)(2,1)S(1)}, bf16[256,256]{1,0:T(8,128)(2,1)S(1)}, u32[]{:S(2)}, u32[]{:S(2)}) collective-permute-start(bf16[256,256]{1,0:T(8,128)(2,1)S(1)} %collective-permute-done.1.refs_2_), channel_id=1, source_target_pairs={{0,4},{2,6},{4,0},{6,2},{8,12},{10,14},{12,8},{14,10},{1,5},{3,7},... | collective-permute-start | bytes 393224 | tf_op jit(solution)/shard_map/ppermute | solution.py:31
  15.2 6.6 %collective-permute-start.2 = (bf16[256,256]{1,0:T(8,128)(2,1)S(1)}, bf16[256,256]{1,0:T(8,128)(2,1)S(1)}, u32[]{:S(2)}, u32[]{:S(2)}) collective-permute-start(bf16[256,256]{1,0:T(8,128)(2,1)S(1)} %collective-permute-done.1.refs_2_), channel_id=1, source_target_pairs={{0,2},{2,0},{4,6},{6,4},{8,10},{10,8},{12,14},{14,12},{1,3},{3,1},... | collective-permute-start | bytes 393224 | tf_op jit(solution)/shard_map/ppermute | solution.py:31
  22.9 1.6 %copy-start.1 = (f32[256,256]{1,0:T(8,128)S(1)}, f32[256,256]{1,0:T(8,128)}, u32[]{:S(2)}) copy-start(f32[256,256]{1,0:T(8,128)} %tau.3) | copy-start | bytes 786436
  23.0 1.6 %collective-permute-start.7 = (bf16[2,256,256]{2,1,0:T(8,128)(2,1)S(1)}, bf16[2,256,256]{2,1,0:T(8,128)(2,1)S(1)}, u32[]{:S(2)}, u32[]{:S(2)}) collective-permute-start(bf16[2,256,256]{2,1,0:T(8,128)(2,1)S(1)} %shard_map.126), channel_id=1, source_target_pairs={{0,1},{1,0},{2,3},{3,2},{4,5},{5,4},{6,7},{7,6},{8,9},{9,8},{10,11... | collective-permute-start | bytes 786440 | tf_op jit(solution)/shard_map/ppermute | solution.py:360
  24.6 13.9 %copy-start.2 = (f32[256,256]{1,0:T(8,128)S(1)}, f32[256,256]{1,0:T(8,128)}, u32[]{:S(2)}) copy-start(f32[256,256]{1,0:T(8,128)} %state.1) | copy-start | bytes 786436
  25.6 9.4 %collective-permute-start.9 = (bf16[256,256]{1,0:T(8,128)(2,1)S(1)}, bf16[256,256]{1,0:T(8,128)(2,1)S(1)}, u32[]{:S(2)}, u32[]{:S(2)}) collective-permute-start(bf16[256,256]{1,0:T(8,128)(2,1)S(1)} %get-tuple-element.39.refs_0_), channel_id=1, source_target_pairs={{0,8},{2,10},{4,12},{6,14},{8,0},{10,2},{12,4},{14,6},{1,9},{3,11}... | collective-permute-start | bytes 393224 | tf_op jit(solution)/shard_map/ppermute | solution.py:31
  27.5 9.6 %collective-permute-start.14 = (bf16[256,256]{1,0:T(8,128)(2,1)S(1)}, bf16[256,256]{1,0:T(8,128)(2,1)S(1)}, u32[]{:S(2)}, u32[]{:S(2)}) collective-permute-start(bf16[256,256]{1,0:T(8,128)(2,1)S(1)} %get-tuple-element.39.refs_0_), channel_id=1, source_target_pairs={{0,4},{2,6},{4,0},{6,2},{8,12},{10,14},{12,8},{14,10},{1,5},{3,7},... | collective-permute-start | bytes 393224 | tf_op jit(solution)/shard_map/ppermute | solution.py:31
  29.3 9.4 %collective-permute-start.13 = (bf16[256,256]{1,0:T(8,128)(2,1)S(1)}, bf16[256,256]{1,0:T(8,128)(2,1)S(1)}, u32[]{:S(2)}, u32[]{:S(2)}) collective-permute-start(bf16[256,256]{1,0:T(8,128)(2,1)S(1)} %get-tuple-element.39.refs_0_), channel_id=1, source_target_pairs={{0,2},{2,0},{4,6},{6,4},{8,10},{10,8},{12,14},{14,12},{1,3},{3,1},... | collective-permute-start | bytes 393224 | tf_op jit(solution)/shard_map/ppermute | solution.py:31
  30.7 9.2 %collective-permute-start.8 = (bf16[256,256]{1,0:T(8,128)(2,1)S(1)}, bf16[256,256]{1,0:T(8,128)(2,1)S(1)}, u32[]{:S(2)}, u32[]{:S(2)}) collective-permute-start(bf16[256,256]{1,0:T(8,128)(2,1)S(1)} %get-tuple-element.39.refs_0_), channel_id=1, source_target_pairs={{0,6},{2,4},{4,2},{6,0},{8,14},{10,12},{12,10},{14,8},{1,7},{3,5},... | collective-permute-start | bytes 393224 | tf_op jit(solution)/shard_map/ppermute | solution.py:31
  35.0 7.2 %collective-permute-start.12 = (bf16[256,256]{1,0:T(8,128)(2,1)S(1)}, bf16[256,256]{1,0:T(8,128)(2,1)S(1)}, u32[]{:S(2)}, u32[]{:S(2)}) collective-permute-start(bf16[256,256]{1,0:T(8,128)(2,1)S(1)} %collective-permute-done.9.refs_2_), channel_id=1, source_target_pairs={{0,6},{2,4},{4,2},{6,0},{8,14},{10,12},{12,10},{14,8},{1,7},{3,5},... | collective-permute-start | bytes 393224 | tf_op jit(solution)/shard_map/ppermute | solution.py:31
  35.0 8.3 %collective-permute-start.11 = (bf16[256,256]{1,0:T(8,128)(2,1)S(1)}, bf16[256,256]{1,0:T(8,128)(2,1)S(1)}, u32[]{:S(2)}, u32[]{:S(2)}) collective-permute-start(bf16[256,256]{1,0:T(8,128)(2,1)S(1)} %collective-permute-done.9.refs_2_), channel_id=1, source_target_pairs={{0,4},{2,6},{4,0},{6,2},{8,12},{10,14},{12,8},{14,10},{1,5},{3,7},... | collective-permute-start | bytes 393224 | tf_op jit(solution)/shard_map/ppermute | solution.py:31
  37.1 6.5 %collective-permute-start.10 = (bf16[256,256]{1,0:T(8,128)(2,1)S(1)}, bf16[256,256]{1,0:T(8,128)(2,1)S(1)}, u32[]{:S(2)}, u32[]{:S(2)}) collective-permute-start(bf16[256,256]{1,0:T(8,128)(2,1)S(1)} %collective-permute-done.9.refs_2_), channel_id=1, source_target_pairs={{0,2},{2,0},{4,6},{6,4},{8,10},{10,8},{12,14},{14,12},{1,3},{3,1},... | collective-permute-start | bytes 393224 | tf_op jit(solution)/shard_map/ppermute | solution.py:31
  44.7 1.6 %collective-permute-start.15 = (bf16[2,256,256]{2,1,0:T(8,128)(2,1)S(1)}, bf16[2,256,256]{2,1,0:T(8,128)(2,1)S(1)}, u32[]{:S(2)}, u32[]{:S(2)}) collective-permute-start(bf16[2,256,256]{2,1,0:T(8,128)(2,1)S(1)} %shard_map.131), channel_id=1, source_target_pairs={{0,1},{1,0},{2,3},{3,2},{4,5},{5,4},{6,7},{7,6},{8,9},{9,8},{10,11... | collective-permute-start | bytes 786440 | tf_op jit(solution)/shard_map/ppermute | solution.py:360

commit v14 on v13

--- a/solution.py
+++ b/solution.py
@@ -107,16 +107,14 @@
         store_powers(powers, part, state_ref[:, part], coef_out)
 
 
-def sums_kernel(spots, direct, first, pick, before, near_any, v_ref, u_ref, d_ref, *refs):
+def sums_kernel(spots, direct, first, pick, before, near_ref, v_ref, u_ref, d_ref, *refs):
     blocks = refs[: len(spots)]
     refs = refs[len(spots) :]
     if before:
         sums_ref, refs = refs[0], refs[1:]
-    out_ref, x_all, proj, near_ref, near_sem = refs
+    out_ref, proj = refs
     count, rows, rank_count, size = v_ref.shape
     kinds, slots = d_ref.shape[0], near_ref.shape[1]
-    near_copy = pltpu.make_async_copy(near_any, near_ref, near_sem)
-    near_copy.start()
     row, col = lax.axis_index("row"), lax.axis_index("col")
     met = [row_met(spot, row, direct) for spot in spots]
     chosen = list(range(rows)) if pick is None else [col if pick == 0 else 1 - col]
@@ -131,18 +129,18 @@
             proj[place, at * rank_count : (at + 1) * rank_count, :] = part[
                 place * rank_count : (place + 1) * rank_count
             ]
-    for at, block in enumerate(blocks):
-        x_all[at] = block[...]
-    x_all[len(blocks)] = jnp.zeros_like(x_all[0])
     lanes = slice(first * rank_count, (first + len(blocks)) * rank_count)
-    near_copy.wait()
     for place, p in enumerate(chosen):
         weights, fields = [u_ref[p, :, lanes]], [proj[place]]
         for s in range(slots):
-            near = near_ref[p, s] - col * count
-            at = len(blocks) - sum(jnp.where(near == q, len(blocks) - i, 0) for i, q in enumerate(met))
+            near = near_ref[pl.ds(p, 1), s : s + 1] - col * count
+            field = None
+            for q, block in zip(met, blocks):
+                mask = jnp.where(near == q, 1.0, 0.0).astype(block.dtype)
+                part = block[...] * mask
+                field = part if field is None else field + part
             weights.append(jnp.concatenate([d_ref[kind, p, s] for kind in range(kinds)], axis=0))
-            fields.append(x_all[at])
+            fields.append(field)
         total = jnp.dot(
             jnp.concatenate(weights, axis=1),
             jnp.concatenate(fields, axis=0),
@@ -337,16 +335,12 @@
                 sums_kernel, spots[first : first + len(blocks)], direct, first, pick, before is not None
             ),
             shaped(*lead, size, members, kind=kind),
-            (v_met, u_met, dense_blocks, *blocks, *(() if before is None else (before,))),
+            (near_index, v_met, u_met, dense_blocks, *blocks, *(() if before is None else (before,))),
             (
-                pltpu.VMEM((len(blocks) + 1, size, members), narrow),
                 pltpu.VMEM((held, len(blocks) * rank_count, members), narrow),
-                pltpu.SMEM(near_index.shape, jnp.int32),
-                pltpu.SemaphoreType.DMA(()),
             ),
             2 * held * size * members * rank_count * len(blocks) * 3,
             room,
-            far=(near_index,),
         )
 
     def lattice(field_half, beside):

time: 48.3 us -> 47.2 us (0.977)
  Pallas kernels: 12.7 us -> 9.59 us
  waiting for transfers between devices: 14.4 us -> 15.8 us
  local copies, waits for them, and re-layouts: 0.01 us -> 0.68 us
    pallas_call x11, Pallas kernels: 12.7 us -> 9.59 us  [on_core(): pl.pallas_call(kernel, out_shape=outs, in_specs=[hbm] * len(far) + [vmem]...]
    ppermute x2, waiting for transfers between devices: 0.8 us -> 1.89 us  [lattice(): lax.ppermute(add(blocks[early:], early, 1, sums, narrow), 'col', swap)]
    unnamed x6 -> x8, local copies, waits for them, and re-layouts: 0.01 us -> 0.68 us
  transfers between devices with their start and end apart: 16 -> 16, of which waited for: 10 -> 10; matrix products, arithmetic and copies ran while one was open for 0% -> 0% of each run, Pallas kernels for 14% -> 10%
where the time goes in v14:
time: 47.2 us; the launch traced here: 47 us
  starting transfers between devices  20.1 us (43%)
  waiting for transfers between devices  15.8 us (33%)
  Pallas kernels  9.59 us (20%)
  between operations  0.78 us (2%)
  local copies, waits for them, and re-layouts  0.68 us (1%)
    ppermute x14, starting transfers between devices, swapped(): lax.ppermute(data, 'row', [(row, row ^ mask) for row in range(count)])  20 us
    ppermute x14, waiting for transfers between devices, swapped(): lax.ppermute(data, 'row', [(row, row ^ mask) for row in range(count)])  13.9 us
    pallas_call x11, Pallas kernels, on_core(): pl.pallas_call(kernel, out_shape=outs, in_specs=[hbm] * len(far) + [vmem]...  9.59 us
    ppermute x2, waiting for transfers between devices, lattice(): lax.ppermute(add(blocks[early:], early, 1, sums, narrow), 'col', swap)  1.89 us
  transfers between devices with their start and end apart: 16, of which 10 were waited for; matrix products, arithmetic and copies ran while one was open for 0% of the time, Pallas kernels for 10%

profile of v14, /device:TPU:0, one launch (start us, length us, event | category | flops | bytes accessed | tf_op | source)
XLA Modules:
  0.0 47.0 jit_solution(4097445976876686779)
XLA Ops:
  0.6 0.0 copy-start
  0.6 1.0 %shard_map.123.refs_0_ = bf16[256,256]{1,0:T(8,128)(2,1)S(1)} custom-call(f32[256,256]{1,0:T(8,128)} %wide_ref.1), custom_call_target="tpu_custom_call" | custom-call | bytes 262144 | tf_op jit(solution)/shard_map/pallas_call | solution.py:258
  1.7 4.1 %collective-permute-start.1 = (bf16[256,256]{1,0:T(8,128)(2,1)S(1)}, bf16[256,256]{1,0:T(8,128)(2,1)S(1)}, u32[]{:S(2)}, u32[]{:S(2)}) collective-permute-start(bf16[256,256]{1,0:T(8,128)(2,1)S(1)} %shard_map.123.refs_0_), channel_id=1, source_target_pairs={{0,8},{2,10},{4,12},{6,14},{8,0},{10,2},{12,4},{14,6},{1,9},{3,11}... | collective-permute-start | bytes 393224 | tf_op jit(solution)/shard_map/ppermute | solution.py:31
  5.8 1.6 %collective-permute-start.6 = (bf16[256,256]{1,0:T(8,128)(2,1)S(1)}, bf16[256,256]{1,0:T(8,128)(2,1)S(1)}, u32[]{:S(2)}, u32[]{:S(2)}) collective-permute-start(bf16[256,256]{1,0:T(8,128)(2,1)S(1)} %shard_map.123.refs_0_), channel_id=1, source_target_pairs={{0,4},{2,6},{4,0},{6,2},{8,12},{10,14},{12,8},{14,10},{1,5},{3,7},... | collective-permute-start | bytes 393224 | tf_op jit(solution)/shard_map/ppermute | solution.py:31
  7.4 1.5 %collective-permute-start.5 = (bf16[256,256]{1,0:T(8,128)(2,1)S(1)}, bf16[256,256]{1,0:T(8,128)(2,1)S(1)}, u32[]{:S(2)}, u32[]{:S(2)}) collective-permute-start(bf16[256,256]{1,0:T(8,128)(2,1)S(1)} %shard_map.123.refs_0_), channel_id=1, source_target_pairs={{0,2},{2,0},{4,6},{6,4},{8,10},{10,8},{12,14},{14,12},{1,3},{3,1},... | collective-permute-start | bytes 393224 | tf_op jit(solution)/shard_map/ppermute | solution.py:31
  8.9 0.4 collective-permute-start
  9.3 2.9 %collective-permute-done.1.refs_2_ = bf16[256,256]{1,0:T(8,128)(2,1)S(1)} collective-permute-done((bf16[256,256]{1,0:T(8,128)(2,1)S(1)}, bf16[256,256]{1,0:T(8,128)(2,1)S(1)}, u32[]{:S(2)}, u32[]{:S(2)}) %collective-permute-start.1) | collective-permute-done | bytes 131104 | tf_op jit(solution)/shard_map/ppermute | solution.py:31
  12.2 1.6 %collective-permute-start.4 = (bf16[256,256]{1,0:T(8,128)(2,1)S(1)}, bf16[256,256]{1,0:T(8,128)(2,1)S(1)}, u32[]{:S(2)}, u32[]{:S(2)}) collective-permute-start(bf16[256,256]{1,0:T(8,128)(2,1)S(1)} %collective-permute-done.1.refs_2_), channel_id=1, source_target_pairs={{0,6},{2,4},{4,2},{6,0},{8,14},{10,12},{12,10},{14,8},{1,7},{3,5},... | collective-permute-start | bytes 393224 | tf_op jit(solution)/shard_map/ppermute | solution.py:31
  13.8 1.4 %collective-permute-start.3 = (bf16[256,256]{1,0:T(8,128)(2,1)S(1)}, bf16[256,256]{1,0:T(8,128)(2,1)S(1)}, u32[]{:S(2)}, u32[]{:S(2)}) collective-permute-start(bf16[256,256]{1,0:T(8,128)(2,1)S(1)} %collective-permute-done.1.refs_2_), channel_id=1, source_target_pairs={{0,4},{2,6},{4,0},{6,2},{8,12},{10,14},{12,8},{14,10},{1,5},{3,7},... | collective-permute-start | bytes 393224 | tf_op jit(solution)/shard_map/ppermute | solution.py:31
  15.2 0.0 collective-permute-done.6.refs_3_
  15.2 0.5 collective-permute-start.2
  15.7 1.8 %shard_map.122 = (bf16[8,2,32,256]{3,2,1,0:T(8,128)(2,1)S(1)}, bf16[2,512,256]{2,1,0:T(8,128)(2,1)S(1)}, f32[5,256,128]{2,1,0:T(8,128)S(1)}, f32[256,256]{1,0:T(...) custom-call(s32[2,8]{1,0:T(2,128)} %refs_0_.1, bf16[2,8,32,256]{3,2,1,0:T(8,128)(2,1)} %refs_1_.1, ...), custom_call_target="tpu_custom_call" | custom-call | bytes 1051712 | tf_op jit(solution)/shard_map/pallas_call | solution.py:258
  17.4 0.0 collective-permute-done.5.refs_1_
  17.5 0.0 copy-start.3
  17.5 0.7 %copy-done.3 = s32[2,2]{1,0:T(2,128)S(1)} copy-done((s32[2,2]{1,0:T(2,128)S(1)}, s32[2,2]{1,0:T(2,128)}, u32[]{:S(2)}) %copy-start.3) | copy-done | bytes 40
  18.1 0.8 %shard_map.124.refs_4_ = f32[2,2,256,256]{3,2,1,0:T(8,128)S(1)} custom-call(s32[2,2]{1,0:T(2,128)S(1)} %copy-done.3, bf16[8,2,32,256]{3,2,1,0:T(8,128)(2,1)S(1)} %get-tuple-element.24.v_ref, bf16[2,512,256]{2,1,0:T(8,128)(2,1)S(1)} %get-tuple-element.25.u_ref, bf16[2,2,2,256,256]{4,3,2,1,0:T(8,128)(2,1)S(1)} %copy-done, ...), custom_call_target="tpu_custom_call" | custom-call | flops 100663296 | bytes 2359312 | tf_op jit(solution)/shard_map/pallas_call | solution.py:258
  18.9 0.0 collective-permute-done.refs_0_
  18.9 1.0 %collective-permute-done.4.refs_3_ = bf16[256,256]{1,0:T(8,128)(2,1)S(1)} collective-permute-done((bf16[256,256]{1,0:T(8,128)(2,1)S(1)}, bf16[256,256]{1,0:T(8,128)(2,1)S(1)}, u32[]{:S(2)}, u32[]{:S(2)}) %collective-permute-start.4) | collective-permute-done | bytes 131104 | tf_op jit(solution)/shard_map/ppermute | solution.py:31
  19.9 0.9 %collective-permute-done.3.refs_2_ = bf16[256,256]{1,0:T(8,128)(2,1)S(1)} collective-permute-done((bf16[256,256]{1,0:T(8,128)(2,1)S(1)}, bf16[256,256]{1,0:T(8,128)(2,1)S(1)}, u32[]{:S(2)}, u32[]{:S(2)}) %collective-permute-start.3) | collective-permute-done | bytes 131104 | tf_op jit(solution)/shard_map/ppermute | solution.py:31
  20.8 1.0 %collective-permute-done.2.refs_1_ = bf16[256,256]{1,0:T(8,128)(2,1)S(1)} collective-permute-done((bf16[256,256]{1,0:T(8,128)(2,1)S(1)}, bf16[256,256]{1,0:T(8,128)(2,1)S(1)}, u32[]{:S(2)}, u32[]{:S(2)}) %collective-permute-start.2) | collective-permute-done | bytes 131104 | tf_op jit(solution)/shard_map/ppermute | solution.py:31
  21.8 0.6 %shard_map.126 = bf16[2,256,256]{2,1,0:T(8,128)(2,1)S(1)} custom-call(s32[2,2]{1,0:T(2,128)S(1)} %copy-done.3, bf16[8,2,32,256]{3,2,1,0:T(8,128)(2,1)S(1)} %get-tuple-element.24.v_ref, bf16[2,512,256]{2,1,0:T(8,128)(2,1)S(1)} %get-tuple-element.25.u_ref, bf16[2,2,2,256,256]{4,3,2,1,0:T(8,128)(2,1)S(1)} %copy-done, ...), custom_call_target="tpu_custom_call" | custom-call | flops 50331648 | bytes 3407888 | tf_op jit(solution)/shard_map/pallas_call | solution.py:258
  22.4 0.0 copy-start.1
  22.4 0.1 collective-permute-start.7
  22.5 0.6 %shard_map.125.own = f32[2,256,256]{2,1,0:T(8,128)S(1)} custom-call(s32[2,2]{1,0:T(2,128)S(1)} %copy-done.3, bf16[8,2,32,256]{3,2,1,0:T(8,128)(2,1)S(1)} %get-tuple-element.24.v_ref, bf16[2,512,256]{2,1,0:T(8,128)(2,1)S(1)} %get-tuple-element.25.u_ref, bf16[2,2,2,256,256]{4,3,2,1,0:T(8,128)(2,1)S(1)} %copy-done, ...), custom_call_target="tpu_custom_call" | custom-call | flops 50331648 | bytes 3407888 | tf_op jit(solution)/shard_map/pallas_call | solution.py:258
  23.1 0.9 %collective-permute-done.7.other = bf16[2,256,256]{2,1,0:T(8,128)(2,1)S(1)} collective-permute-done((bf16[2,256,256]{2,1,0:T(8,128)(2,1)S(1)}, bf16[2,256,256]{2,1,0:T(8,128)(2,1)S(1)}, u32[]{:S(2)}, u32[]{:S(2)}) %collective-permute-start.7) | collective-permute-done | bytes 262176 | tf_op jit(solution)/shard_map/ppermute | solution.py:354
  24.0 1.0 %shard_map.127 = (f32[256,256]{1,0:T(8,128)S(1)}, f32[256,256]{1,0:T(8,128)S(1)}, f32[256,256]{1,0:T(8,128)S(1)}, f32[256,256]{1,0:T(8,128)S(1)}, bf16[256,256]{1,0:T(8,128)(2,1)S(1)}) custom-call(f32[2,256,256]{2,1,0:T(8,128)S(1)} %shard_map.125.own, bf16[2,256,256]{2,1,0:T(8,128)(2,1)S(1)} %collective-permute-done.7.other, ...), custom_call_target="tpu_custom_call" | custom-call | flops 13107200 | bytes 2490368 | tf_op jit(solution)/shard_map/pallas_call | solution.py:258
  25.1 1.9 %collective-permute-start.9 = (bf16[256,256]{1,0:T(8,128)(2,1)S(1)}, bf16[256,256]{1,0:T(8,128)(2,1)S(1)}, u32[]{:S(2)}, u32[]{:S(2)}) collective-permute-start(bf16[256,256]{1,0:T(8,128)(2,1)S(1)} %get-tuple-element.39.refs_0_), channel_id=1, source_target_pairs={{0,8},{2,10},{4,12},{6,14},{8,0},{10,2},{12,4},{14,6},{1,9},{3,11}... | collective-permute-start | bytes 393224 | tf_op jit(solution)/shard_map/ppermute | solution.py:31
  27.0 1.7 %collective-permute-start.14 = (bf16[256,256]{1,0:T(8,128)(2,1)S(1)}, bf16[256,256]{1,0:T(8,128)(2,1)S(1)}, u32[]{:S(2)}, u32[]{:S(2)}) collective-permute-start(bf16[256,256]{1,0:T(8,128)(2,1)S(1)} %get-tuple-element.39.refs_0_), channel_id=1, source_target_pairs={{0,4},{2,6},{4,0},{6,2},{8,12},{10,14},{12,8},{14,10},{1,5},{3,7},... | collective-permute-start | bytes 393224 | tf_op jit(solution)/shard_map/ppermute | solution.py:31
  28.7 1.5 %collective-permute-start.13 = (bf16[256,256]{1,0:T(8,128)(2,1)S(1)}, bf16[256,256]{1,0:T(8,128)(2,1)S(1)}, u32[]{:S(2)}, u32[]{:S(2)}) collective-permute-start(bf16[256,256]{1,0:T(8,128)(2,1)S(1)} %get-tuple-element.39.refs_0_), channel_id=1, source_target_pairs={{0,2},{2,0},{4,6},{6,4},{8,10},{10,8},{12,14},{14,12},{1,3},{3,1},... | collective-permute-start | bytes 393224 | tf_op jit(solution)/shard_map/ppermute | solution.py:31
  30.2 0.3 collective-permute-start.8
  30.5 4.0 %collective-permute-done.9.refs_2_ = bf16[256,256]{1,0:T(8,128)(2,1)S(1)} collective-permute-done((bf16[256,256]{1,0:T(8,128)(2,1)S(1)}, bf16[256,256]{1,0:T(8,128)(2,1)S(1)}, u32[]{:S(2)}, u32[]{:S(2)}) %collective-permute-start.9) | collective-permute-done | bytes 131104 | tf_op jit(solution)/shard_map/ppermute | solution.py:31
  34.5 0.0 collective-permute-start.12
  34.5 2.1 %collective-permute-start.11 = (bf16[256,256]{1,0:T(8,128)(2,1)S(1)}, bf16[256,256]{1,0:T(8,128)(2,1)S(1)}, u32[]{:S(2)}, u32[]{:S(2)}) collective-permute-start(bf16[256,256]{1,0:T(8,128)(2,1)S(1)} %collective-permute-done.9.refs_2_), channel_id=1, source_target_pairs={{0,4},{2,6},{4,0},{6,2},{8,12},{10,14},{12,8},{14,10},{1,5},{3,7},... | collective-permute-start | bytes 393224 | tf_op jit(solution)/shard_map/ppermute | solution.py:31
  36.6 0.0 collective-permute-done.14.refs_3_
  36.6 1.4 %collective-permute-start.10 = (bf16[256,256]{1,0:T(8,128)(2,1)S(1)}, bf16[256,256]{1,0:T(8,128)(2,1)S(1)}, u32[]{:S(2)}, u32[]{:S(2)}) collective-permute-start(bf16[256,256]{1,0:T(8,128)(2,1)S(1)} %collective-permute-done.9.refs_2_), channel_id=1, source_target_pairs={{0,2},{2,0},{4,6},{6,4},{8,10},{10,8},{12,14},{14,12},{1,3},{3,1},... | collective-permute-start | bytes 393224 | tf_op jit(solution)/shard_map/ppermute | solution.py:31
  38.0 0.0 copy-done.2
  38.0 0.1 shard_map.128
  38.1 0.0 collective-permute-done.13.refs_1_
  38.1 0.8 %shard_map.129.refs_4_ = f32[2,2,256,256]{3,2,1,0:T(8,128)S(1)} custom-call(s32[2,2]{1,0:T(2,128)S(1)} %copy-done.3, bf16[8,2,32,256]{3,2,1,0:T(8,128)(2,1)S(1)} %get-tuple-element.24.v_ref, bf16[2,512,256]{2,1,0:T(8,128)(2,1)S(1)} %get-tuple-element.25.u_ref, bf16[2,2,2,256,256]{4,3,2,1,0:T(8,128)(2,1)S(1)} %copy-done, ...), custom_call_target="tpu_custom_call" | custom-call | flops 100663296 | bytes 2359312 | tf_op jit(solution)/shard_map/pallas_call | solution.py:258
  38.9 0.0 collective-permute-done.8.refs_0_
  38.9 2.7 %collective-permute-done.12.refs_3_ = bf16[256,256]{1,0:T(8,128)(2,1)S(1)} collective-permute-done((bf16[256,256]{1,0:T(8,128)(2,1)S(1)}, bf16[256,256]{1,0:T(8,128)(2,1)S(1)}, u32[]{:S(2)}, u32[]{:S(2)}) %collective-permute-start.12) | collective-permute-done | bytes 131104 | tf_op jit(solution)/shard_map/ppermute | solution.py:31
  41.6 1.2 %collective-permute-done.11.refs_2_ = bf16[256,256]{1,0:T(8,128)(2,1)S(1)} collective-permute-done((bf16[256,256]{1,0:T(8,128)(2,1)S(1)}, bf16[256,256]{1,0:T(8,128)(2,1)S(1)}, u32[]{:S(2)}, u32[]{:S(2)}) %collective-permute-start.11) | collective-permute-done | bytes 131104 | tf_op jit(solution)/shard_map/ppermute | solution.py:31
  42.8 0.2 collective-permute-done.10.refs_1_
  43.0 0.6 %shard_map.131 = bf16[2,256,256]{2,1,0:T(8,128)(2,1)S(1)} custom-call(s32[2,2]{1,0:T(2,128)S(1)} %copy-done.3, bf16[8,2,32,256]{3,2,1,0:T(8,128)(2,1)S(1)} %get-tuple-element.24.v_ref, bf16[2,512,256]{2,1,0:T(8,128)(2,1)S(1)} %get-tuple-element.25.u_ref, bf16[2,2,2,256,256]{4,3,2,1,0:T(8,128)(2,1)S(1)} %copy-done, ...), custom_call_target="tpu_custom_call" | custom-call | flops 50331648 | bytes 3407888 | tf_op jit(solution)/shard_map/pallas_call | solution.py:258
  43.6 0.1 collective-permute-start.15
  43.7 0.6 %shard_map.130.own = f32[2,256,256]{2,1,0:T(8,128)S(1)} custom-call(s32[2,2]{1,0:T(2,128)S(1)} %copy-done.3, bf16[8,2,32,256]{3,2,1,0:T(8,128)(2,1)S(1)} %get-tuple-element.24.v_ref, bf16[2,512,256]{2,1,0:T(8,128)(2,1)S(1)} %get-tuple-element.25.u_ref, bf16[2,2,2,256,256]{4,3,2,1,0:T(8,128)(2,1)S(1)} %copy-done, ...), custom_call_target="tpu_custom_call" | custom-call | flops 50331648 | bytes 3407888 | tf_op jit(solution)/shard_map/pallas_call | solution.py:258
  44.3 0.9 %collective-permute-done.15.other = bf16[2,256,256]{2,1,0:T(8,128)(2,1)S(1)} collective-permute-done((bf16[2,256,256]{2,1,0:T(8,128)(2,1)S(1)}, bf16[2,256,256]{2,1,0:T(8,128)(2,1)S(1)}, u32[]{:S(2)}, u32[]{:S(2)}) %collective-permute-start.15) | collective-permute-done | bytes 262176 | tf_op jit(solution)/shard_map/ppermute | solution.py:354
  45.2 1.8 %shard_map.132 = (f32[256,256]{1,0:T(8,128)}, f32[256,256]{1,0:T(8,128)}) custom-call(f32[2,256,256]{2,1,0:T(8,128)S(1)} %shard_map.130.own, bf16[2,256,256]{2,1,0:T(8,128)(2,1)S(1)} %collective-permute-done.15.other, f32[256,256]{1,0:T(8,128)S(1)} %get-tuple-element.40.weight, f32[256,256]{1,0:T(8,128)S(1)} %get-tuple-element.41.unweight, ...), custom_call_target="tpu_custom_call" | custom-call | flops 13107200 | bytes 3538944 | tf_op jit(solution)/shard_map/pallas_call | solution.py:258
  (3 shorter events, 0.0 us)
Async XLA Ops:
  0.6 16.8 %copy-start = (bf16[2,2,2,256,256]{4,3,2,1,0:T(8,128)(2,1)S(1)}, bf16[2,2,2,256,256]{4,3,2,1,0:T(8,128)(2,1)}, u32[]{:S(2)}) copy-start(bf16[2,2,2,256,256]{4,3,2,1,0:T(8,128)(2,1)} %d_ref.11) | copy-start | bytes 3145732
  1.7 10.5 %collective-permute-start.1 = (bf16[256,256]{1,0:T(8,128)(2,1)S(1)}, bf16[256,256]{1,0:T(8,128)(2,1)S(1)}, u32[]{:S(2)}, u32[]{:S(2)}) collective-permute-start(bf16[256,256]{1,0:T(8,128)(2,1)S(1)} %shard_map.123.refs_0_), channel_id=1, source_target_pairs={{0,8},{2,10},{4,12},{6,14},{8,0},{10,2},{12,4},{14,6},{1,9},{3,11}... | collective-permute-start | bytes 393224 | tf_op jit(solution)/shard_map/ppermute | solution.py:31
  5.8 9.4 %collective-permute-start.6 = (bf16[256,256]{1,0:T(8,128)(2,1)S(1)}, bf16[256,256]{1,0:T(8,128)(2,1)S(1)}, u32[]{:S(2)}, u32[]{:S(2)}) collective-permute-start(bf16[256,256]{1,0:T(8,128)(2,1)S(1)} %shard_map.123.refs_0_), channel_id=1, source_target_pairs={{0,4},{2,6},{4,0},{6,2},{8,12},{10,14},{12,8},{14,10},{1,5},{3,7},... | collective-permute-start | bytes 393224 | tf_op jit(solution)/shard_map/ppermute | solution.py:31
  7.4 10.1 %collective-permute-start.5 = (bf16[256,256]{1,0:T(8,128)(2,1)S(1)}, bf16[256,256]{1,0:T(8,128)(2,1)S(1)}, u32[]{:S(2)}, u32[]{:S(2)}) collective-permute-start(bf16[256,256]{1,0:T(8,128)(2,1)S(1)} %shard_map.123.refs_0_), channel_id=1, source_target_pairs={{0,2},{2,0},{4,6},{6,4},{8,10},{10,8},{12,14},{14,12},{1,3},{3,1},... | collective-permute-start | bytes 393224 | tf_op jit(solution)/shard_map/ppermute | solution.py:31
  8.9 10.0 %collective-permute-start = (bf16[256,256]{1,0:T(8,128)(2,1)S(1)}, bf16[256,256]{1,0:T(8,128)(2,1)S(1)}, u32[]{:S(2)}, u32[]{:S(2)}) collective-permute-start(bf16[256,256]{1,0:T(8,128)(2,1)S(1)} %shard_map.123.refs_0_), channel_id=1, source_target_pairs={{0,6},{2,4},{4,2},{6,0},{8,14},{10,12},{12,10},{14,8},{1,7},{3,5},... | collective-permute-start | bytes 393224 | tf_op jit(solution)/shard_map/ppermute | solution.py:31
  12.2 7.7 %collective-permute-start.4 = (bf16[256,256]{1,0:T(8,128)(2,1)S(1)}, bf16[256,256]{1,0:T(8,128)(2,1)S(1)}, u32[]{:S(2)}, u32[]{:S(2)}) collective-permute-start(bf16[256,256]{1,0:T(8,128)(2,1)S(1)} %collective-permute-done.1.refs_2_), channel_id=1, source_target_pairs={{0,6},{2,4},{4,2},{6,0},{8,14},{10,12},{12,10},{14,8},{1,7},{3,5},... | collective-permute-start | bytes 393224 | tf_op jit(solution)/shard_map/ppermute | solution.py:31
  13.8 7.0 %collective-permute-start.3 = (bf16[256,256]{1,0:T(8,128)(2,1)S(1)}, bf16[256,256]{1,0:T(8,128)(2,1)S(1)}, u32[]{:S(2)}, u32[]{:S(2)}) collective-permute-start(bf16[256,256]{1,0:T(8,128)(2,1)S(1)} %collective-permute-done.1.refs_2_), channel_id=1, source_target_pairs={{0,4},{2,6},{4,0},{6,2},{8,12},{10,14},{12,8},{14,10},{1,5},{3,7},... | collective-permute-start | bytes 393224 | tf_op jit(solution)/shard_map/ppermute | solution.py:31
  15.2 6.6 %collective-permute-start.2 = (bf16[256,256]{1,0:T(8,128)(2,1)S(1)}, bf16[256,256]{1,0:T(8,128)(2,1)S(1)}, u32[]{:S(2)}, u32[]{:S(2)}) collective-permute-start(bf16[256,256]{1,0:T(8,128)(2,1)S(1)} %collective-permute-done.1.refs_2_), channel_id=1, source_target_pairs={{0,2},{2,0},{4,6},{6,4},{8,10},{10,8},{12,14},{14,12},{1,3},{3,1},... | collective-permute-start | bytes 393224 | tf_op jit(solution)/shard_map/ppermute | solution.py:31
  17.5 0.7 %copy-start.3 = (s32[2,2]{1,0:T(2,128)S(1)}, s32[2,2]{1,0:T(2,128)}, u32[]{:S(2)}) copy-start(s32[2,2]{1,0:T(2,128)} %near_ref.11) | copy-start | bytes 52
  22.4 1.6 %copy-start.1 = (f32[256,256]{1,0:T(8,128)S(1)}, f32[256,256]{1,0:T(8,128)}, u32[]{:S(2)}) copy-start(f32[256,256]{1,0:T(8,128)} %tau.3) | copy-start | bytes 786436
  22.4 1.6 %collective-permute-start.7 = (bf16[2,256,256]{2,1,0:T(8,128)(2,1)S(1)}, bf16[2,256,256]{2,1,0:T(8,128)(2,1)S(1)}, u32[]{:S(2)}, u32[]{:S(2)}) collective-permute-start(bf16[2,256,256]{2,1,0:T(8,128)(2,1)S(1)} %shard_map.126), channel_id=1, source_target_pairs={{0,1},{1,0},{2,3},{3,2},{4,5},{5,4},{6,7},{7,6},{8,9},{9,8},{10,11... | collective-permute-start | bytes 786440 | tf_op jit(solution)/shard_map/ppermute | solution.py:354
  24.0 14.0 %copy-start.2 = (f32[256,256]{1,0:T(8,128)S(1)}, f32[256,256]{1,0:T(8,128)}, u32[]{:S(2)}) copy-start(f32[256,256]{1,0:T(8,128)} %state.1) | copy-start | bytes 786436
  25.1 9.4 %collective-permute-start.9 = (bf16[256,256]{1,0:T(8,128)(2,1)S(1)}, bf16[256,256]{1,0:T(8,128)(2,1)S(1)}, u32[]{:S(2)}, u32[]{:S(2)}) collective-permute-start(bf16[256,256]{1,0:T(8,128)(2,1)S(1)} %get-tuple-element.39.refs_0_), channel_id=1, source_target_pairs={{0,8},{2,10},{4,12},{6,14},{8,0},{10,2},{12,4},{14,6},{1,9},{3,11}... | collective-permute-start | bytes 393224 | tf_op jit(solution)/shard_map/ppermute | solution.py:31
  27.0 9.6 %collective-permute-start.14 = (bf16[256,256]{1,0:T(8,128)(2,1)S(1)}, bf16[256,256]{1,0:T(8,128)(2,1)S(1)}, u32[]{:S(2)}, u32[]{:S(2)}) collective-permute-start(bf16[256,256]{1,0:T(8,128)(2,1)S(1)} %get-tuple-element.39.refs_0_), channel_id=1, source_target_pairs={{0,4},{2,6},{4,0},{6,2},{8,12},{10,14},{12,8},{14,10},{1,5},{3,7},... | collective-permute-start | bytes 393224 | tf_op jit(solution)/shard_map/ppermute | solution.py:31
  28.7 9.4 %collective-permute-start.13 = (bf16[256,256]{1,0:T(8,128)(2,1)S(1)}, bf16[256,256]{1,0:T(8,128)(2,1)S(1)}, u32[]{:S(2)}, u32[]{:S(2)}) collective-permute-start(bf16[256,256]{1,0:T(8,128)(2,1)S(1)} %get-tuple-element.39.refs_0_), channel_id=1, source_target_pairs={{0,2},{2,0},{4,6},{6,4},{8,10},{10,8},{12,14},{14,12},{1,3},{3,1},... | collective-permute-start | bytes 393224 | tf_op jit(solution)/shard_map/ppermute | solution.py:31
  30.2 8.7 %collective-permute-start.8 = (bf16[256,256]{1,0:T(8,128)(2,1)S(1)}, bf16[256,256]{1,0:T(8,128)(2,1)S(1)}, u32[]{:S(2)}, u32[]{:S(2)}) collective-permute-start(bf16[256,256]{1,0:T(8,128)(2,1)S(1)} %get-tuple-element.39.refs_0_), channel_id=1, source_target_pairs={{0,6},{2,4},{4,2},{6,0},{8,14},{10,12},{12,10},{14,8},{1,7},{3,5},... | collective-permute-start | bytes 393224 | tf_op jit(solution)/shard_map/ppermute | solution.py:31
  34.5 7.2 %collective-permute-start.12 = (bf16[256,256]{1,0:T(8,128)(2,1)S(1)}, bf16[256,256]{1,0:T(8,128)(2,1)S(1)}, u32[]{:S(2)}, u32[]{:S(2)}) collective-permute-start(bf16[256,256]{1,0:T(8,128)(2,1)S(1)} %collective-permute-done.9.refs_2_), channel_id=1, source_target_pairs={{0,6},{2,4},{4,2},{6,0},{8,14},{10,12},{12,10},{14,8},{1,7},{3,5},... | collective-permute-start | bytes 393224 | tf_op jit(solution)/shard_map/ppermute | solution.py:31
  34.5 8.3 %collective-permute-start.11 = (bf16[256,256]{1,0:T(8,128)(2,1)S(1)}, bf16[256,256]{1,0:T(8,128)(2,1)S(1)}, u32[]{:S(2)}, u32[]{:S(2)}) collective-permute-start(bf16[256,256]{1,0:T(8,128)(2,1)S(1)} %collective-permute-done.9.refs_2_), channel_id=1, source_target_pairs={{0,4},{2,6},{4,0},{6,2},{8,12},{10,14},{12,8},{14,10},{1,5},{3,7},... | collective-permute-start | bytes 393224 | tf_op jit(solution)/shard_map/ppermute | solution.py:31
  36.6 6.5 %collective-permute-start.10 = (bf16[256,256]{1,0:T(8,128)(2,1)S(1)}, bf16[256,256]{1,0:T(8,128)(2,1)S(1)}, u32[]{:S(2)}, u32[]{:S(2)}) collective-permute-start(bf16[256,256]{1,0:T(8,128)(2,1)S(1)} %collective-permute-done.9.refs_2_), channel_id=1, source_target_pairs={{0,2},{2,0},{4,6},{6,4},{8,10},{10,8},{12,14},{14,12},{1,3},{3,1},... | collective-permute-start | bytes 393224 | tf_op jit(solution)/shard_map/ppermute | solution.py:31
  43.6 1.6 %collective-permute-start.15 = (bf16[2,256,256]{2,1,0:T(8,128)(2,1)S(1)}, bf16[2,256,256]{2,1,0:T(8,128)(2,1)S(1)}, u32[]{:S(2)}, u32[]{:S(2)}) collective-permute-start(bf16[2,256,256]{2,1,0:T(8,128)(2,1)S(1)} %shard_map.131), channel_id=1, source_target_pairs={{0,1},{1,0},{2,3},{3,2},{4,5},{5,4},{6,7},{7,6},{8,9},{9,8},{10,11... | collective-permute-start | bytes 786440 | tf_op jit(solution)/shard_map/ppermute | solution.py:354

commit v15 on v14

--- a/solution.py
+++ b/solution.py
@@ -8,35 +8,23 @@
 from jax.sharding import PartitionSpec as P
 
 NEWTON = 2
-DIRECT_COUNTS = (4, 8)
-LATE = 4
+SQUARE = 4
 
 damping = 0.5
 sigma_floor = 0.5
 section_step = 0.1
 
 
-def arrivals(count, direct):
-    if not direct:
-        return list(range(count))
-    return [0, 1, 4, 2, 3, 5, 6, 7] if count == 8 else [0, 1, 2, 3]
-
-
-def row_met(spot, row, direct):
-    return jnp.bitwise_xor(row, spot) if direct else spot
-
-
-def gather_direct(block, count):
-    def swapped(mask, data):
-        return lax.ppermute(data, "row", [(row, row ^ mask) for row in range(count)])
-
-    found = {0: block}
-    for mask in (4, 1, 2, 3) if count == 8 else (1, 2, 3):
-        found[mask] = swapped(mask, block)
-    if count == 8:
-        for mask in (1, 2, 3):
-            found[4 + mask] = swapped(mask, found[4])
-    return [found[mask] for mask in arrivals(count, True)]
+def rows_met(first, last, row, count):
+    if count != 2 * SQUARE:
+        return list(range(first, last))
+    base = row - lax.rem(row, SQUARE)
+    return [(base if at < SQUARE else SQUARE - base) + at % SQUARE for at in range(first, last)]
+
+
+def copies_kernel(block_ref, out_ref):
+    for at in range(SQUARE):
+        out_ref[at] = block_ref[...]
 
 
 IN_PIECES = 8
@@ -48,7 +36,7 @@
     return [pl.ds(at * tall, tall) for at in range(pieces)]
 
 
-def narrow_kernel(wide_ref, narrow_ref, held, sem):
+def narrow_kernel(wide_ref, narrow_ref, copies_ref, held, sem):
     copies = [
         pltpu.make_async_copy(wide_ref.at[part], held.at[part], sem.at[at])
         for at, part in enumerate(row_pieces(held.shape[0], IN_PIECES))
@@ -57,7 +45,10 @@
         copy.start()
     for copy, part in zip(copies, row_pieces(held.shape[0], IN_PIECES)):
         copy.wait()
-        narrow_ref[part, :] = held[part, :].astype(narrow_ref.dtype)
+        value = held[part, :].astype(narrow_ref.dtype)
+        narrow_ref[part, :] = value
+        for at in range(copies_ref.shape[0]):
+            copies_ref[at, part, :] = value
 
 
 def store_powers(outs, part, state, coef):
@@ -73,7 +64,7 @@
         store_powers(outs, part, state[:, part] + section_step * change[:, part], coef)
 
 
-def prepare_kernel(spots, direct, *refs):
+def prepare_kernel(*refs):
     far, (v_out, u_out, coef_out, *powers), near, sem = refs[:7], refs[7:13], refs[13:20], refs[20]
     copies = [
         pltpu.make_async_copy(source, held, sem.at[at])
@@ -85,8 +76,7 @@
         copy.wait()
     rank_ref, v_ref, u_ref, sigma_ref, a_ref, b_ref, state_ref = near
     kinds, rows, count, rank_count, size = u_ref.shape
-    row = lax.axis_index("row")
-    met = [row_met(spot, row, direct) for spot in spots]
+    met = rows_met(0, count, lax.axis_index("row"), count)
     for at, q in enumerate(met):
         for p in range(rows):
             inside = lax.broadcasted_iota(jnp.int32, (rank_count, size), 0) < rank_ref[p, q]
@@ -107,16 +97,15 @@
         store_powers(powers, part, state_ref[:, part], coef_out)
 
 
-def sums_kernel(spots, direct, first, pick, before, near_ref, v_ref, u_ref, d_ref, *refs):
-    blocks = refs[: len(spots)]
-    refs = refs[len(spots) :]
+def sums_kernel(first, pick, before, near_ref, v_ref, u_ref, d_ref, field_ref, *refs):
     if before:
         sums_ref, refs = refs[0], refs[1:]
     out_ref, proj = refs
+    blocks = [field_ref.at[at] for at in range(field_ref.shape[0])]
     count, rows, rank_count, size = v_ref.shape
     kinds, slots = d_ref.shape[0], near_ref.shape[1]
     row, col = lax.axis_index("row"), lax.axis_index("col")
-    met = [row_met(spot, row, direct) for spot in spots]
+    met = rows_met(first, first + len(blocks), row, count)
     chosen = list(range(rows)) if pick is None else [col if pick == 0 else 1 - col]
     places = [(place,) for place in range(rows)] if pick is None else [()]
     for at, block in enumerate(blocks):
@@ -194,7 +183,7 @@
             work(rows, slice(first, first + lanes))
 
 
-def section_one_kernel(own, other, weight, unweight, decay, tau, coef, stress, normal, rate, change, rate_half):
+def section_one_kernel(own, other, weight, unweight, decay, tau, coef, stress, normal, rate, change, rate_half, rate_copies):
     size, members = tau.shape
 
     def work(rows, part):
@@ -215,7 +204,10 @@
         )
         rate[rows, part] = first
         change[rows, part] = second
-        rate_half[rows, part] = first.astype(rate_half.dtype)
+        half = first.astype(rate_half.dtype)
+        rate_half[rows, part] = half
+        for at in range(rate_copies.shape[0]):
+            rate_copies[at, rows, part] = half
 
     over_pieces(0, size, members, coef.shape[2], work)
 
@@ -284,9 +276,8 @@
     count = lax.axis_size("row")
     size, members = slip_deficit.shape
     kinds, rows, _, rank_count, _ = u_basis.shape
-    direct = count in DIRECT_COUNTS
-    spots = arrivals(count, direct)
-    early = max(count - LATE, 0)
+    direct = count == 2 * SQUARE
+    early = max(count - SQUARE, 0)
     room = 16 if direct else 40
     lanes = min(members, 128)
     narrow, wide = jnp.bfloat16, jnp.float32
@@ -297,7 +288,7 @@
 
     full = shaped(size, members)
     v_met, u_met, coef, *powers = on_core(
-        functools.partial(prepare_kernel, spots, direct),
+        prepare_kernel,
         (
             shaped(count, rows, rank_count, size, kind=narrow),
             shaped(rows, kinds * size, count * rank_count, kind=narrow),
@@ -327,49 +318,57 @@
         ),
     )
 
-    def add(blocks, first, pick, before, kind):
+    def add(field, first, pick, before, kind):
         held = rows if pick is None else 1
         lead = (rows, kinds) if pick is None else (kinds,)
+        blocks = field.shape[0]
         return on_core(
-            functools.partial(
-                sums_kernel, spots[first : first + len(blocks)], direct, first, pick, before is not None
-            ),
+            functools.partial(sums_kernel, first, pick, before is not None),
             shaped(*lead, size, members, kind=kind),
-            (near_index, v_met, u_met, dense_blocks, *blocks, *(() if before is None else (before,))),
-            (
-                pltpu.VMEM((held, len(blocks) * rank_count, members), narrow),
-            ),
-            2 * held * size * members * rank_count * len(blocks) * 3,
+            (near_index, v_met, u_met, dense_blocks, field, *(() if before is None else (before,))),
+            (pltpu.VMEM((held, blocks * rank_count, members), narrow),),
+            2 * held * size * members * rank_count * blocks * 3,
             room,
         )
 
-    def lattice(field_half, beside):
+    def gather(block, copies):
+        squares = [list(range(first, first + SQUARE)) for first in range(0, count, SQUARE)]
+
+        def within(data):
+            return lax.all_to_all(data, "row", 0, 0, axis_index_groups=squares)
+
+        across = lax.ppermute(block, "row", [(row, (row + SQUARE) % count) for row in range(count)])
+        near = within(copies)
+        return near, within(on_core(copies_kernel, shaped(*copies.shape, kind=narrow), (across,)))
+
+    def lattice(block, copies, beside):
         if direct:
-            blocks = gather_direct(field_half, count)
+            near, last = gather(block, copies)
         else:
-            whole = lax.all_gather(field_half, "row", axis=0)
-            blocks = [whole[r] for r in range(count)]
-        blocks[0], beside = lax.optimization_barrier((blocks[0], beside))
-        sums = add(blocks[:early], 0, None, None, wide) if early else None
-        other = lax.ppermute(add(blocks[early:], early, 1, sums, narrow), "col", swap)
-        return add(blocks[early:], early, 0, sums, wide), other, beside
-
+            whole = lax.all_gather(block, "row", axis=0)
+            near, last = whole[:early], whole[early:]
+        near, beside = lax.optimization_barrier((near, beside))
+        sums = add(near, 0, None, None, wide) if early else None
+        other = lax.ppermute(add(last, early, 1, sums, narrow), "col", swap)
+        return add(last, early, 0, sums, wide), other, beside
+
+    sent = (shaped(size, members, kind=narrow), shaped(SQUARE if direct else 1, size, members, kind=narrow))
     slip_half = on_core(
         narrow_kernel,
-        shaped(size, members, kind=narrow),
+        sent,
         (),
         (pltpu.VMEM((size, members), wide), pltpu.SemaphoreType.DMA((IN_PIECES,))),
         far=(slip_deficit,),
     )
-    own, other, powers = lattice(slip_half, powers)
-    stress, normal, rate, change, rate_half = on_core(
+    own, other, powers = lattice(*slip_half, powers)
+    stress, normal, rate, change, *rate_half = on_core(
         section_one_kernel,
-        (full, full, full, full, shaped(size, members, kind=narrow)),
+        (full, full, full, full, *sent),
         (own, other, *powers, tau_load, coef),
         flops=200 * size * members,
     )
     powers = on_core(later_kernel, (full, full, full), (state_var, change, coef))
-    own, other, powers = lattice(rate_half, powers)
+    own, other, powers = lattice(*rate_half, powers)
     return on_core(
         section_two_kernel,
         (full, full),

time: 47.2 us -> 73.7 us (1.56)
  local copies, waits for them, and re-layouts: 0.68 us -> 9.47 us
  waiting for transfers between devices: 15.8 us -> 24.1 us
  Pallas kernels: 9.59 us -> 16.3 us
  starting transfers between devices: 20.1 us -> 22.2 us
    all_to_all x0 -> x4, starting transfers between devices: none -> 18.5 us  [within(): return lax.all_to_all(data, 'row', 0, 0, axis_index_groups=squares)]
    ppermute x16 -> x4, starting transfers between devices: 20.1 us -> 3.69 us  [the longest x2 3.55 us: gather(): lax.ppermute(block, 'row', [(row, (row + SQUARE) % count) for row in rang...]
    all_to_all x0 -> x4, waiting for transfers between devices: none -> 9.59 us  [within(): return lax.all_to_all(data, 'row', 0, 0, axis_index_groups=squares)]
    unnamed x8 -> x60, local copies, waits for them, and re-layouts: 0.68 us -> 9.47 us
    pallas_call x11 -> x13, Pallas kernels: 9.59 us -> 16.3 us  [on_core(): pl.pallas_call(kernel, out_shape=outs, in_specs=[hbm] * len(far) + [vmem]...]
    ppermute x16 -> x4, waiting for transfers between devices: 15.8 us -> 14.5 us  [the longest x2 14.5 us: gather(): lax.ppermute(block, 'row', [(row, (row + SQUARE) % count) for row in rang...]
  transfers between devices with their start and end apart: 16 -> 8, of which waited for: 10 -> 6; matrix products, arithmetic and copies ran while one was open for 0% -> 0% of each run, Pallas kernels for 10% -> 12%
where the time goes in v15:
time: 73.7 us; the launch traced here: 73.1 us
  waiting for transfers between devices  24.1 us (33%)
  starting transfers between devices  22.2 us (30%)
  Pallas kernels  16.3 us (22%)
  local copies, waits for them, and re-layouts  9.47 us (13%)
  between operations  1 us (1%)
    all_to_all x4, starting transfers between devices, within(): return lax.all_to_all(data, 'row', 0, 0, axis_index_groups=squares)  18.5 us
    pallas_call x13, Pallas kernels, on_core(): pl.pallas_call(kernel, out_shape=outs, in_specs=[hbm] * len(far) + [vmem]...  16.3 us
    ppermute x2, waiting for transfers between devices, gather(): lax.ppermute(block, 'row', [(row, (row + SQUARE) % count) for row in rang...  14.5 us
    all_to_all x4, waiting for transfers between devices, within(): return lax.all_to_all(data, 'row', 0, 0, axis_index_groups=squares)  9.59 us
    unnamed x60, local copies, waits for them, and re-layouts  9.47 us
    ppermute x2, starting transfers between devices, gather(): lax.ppermute(block, 'row', [(row, (row + SQUARE) % count) for row in rang...  3.55 us
  transfers between devices with their start and end apart: 8, of which 6 were waited for; matrix products, arithmetic and copies ran while one was open for 0% of the time, Pallas kernels for 12%

profile of v15, /device:TPU:0, one launch (start us, length us, event | category | flops | bytes accessed | tf_op | source)
XLA Modules:
  0.0 73.1 jit_solution(18235834519671415892)
XLA Ops:
  0.6 1.8 %shard_map.123 = (bf16[256,256]{1,0:T(8,128)(2,1)S(1)}, bf16[4,256,256]{2,1,0:T(8,128)(2,1)}) custom-call(f32[256,256]{1,0:T(8,128)} %wide_ref.1), custom_call_target="tpu_custom_call" | custom-call | bytes 262144 | tf_op jit(solution)/shard_map/pallas_call | solution.py:250
  2.4 5.3 %all-to-all-start.1 = ((bf16[4,256,256]{2,1,0:T(8,128)(2,1)}), bf16[4,256,256]{2,1,0:T(8,128)(2,1)S(1)}, u32[]{:S(2)}, u32[]{:S(2)}) async-start(bf16[4,256,256]{2,1,0:T(8,128)(2,1)} %get-tuple-element.30), calls=%async_computation.1 | async-start | bytes 1048576 | tf_op jit(solution)/shard_map/all_to_all | solution.py:338
  7.7 2.6 %collective-permute-start = (bf16[256,256]{1,0:T(8,128)(2,1)S(1)}, bf16[256,256]{1,0:T(8,128)(2,1)S(1)}, u32[]{:S(2)}, u32[]{:S(2)}) collective-permute-start(bf16[256,256]{1,0:T(8,128)(2,1)S(1)} %get-tuple-element.29), channel_id=1, source_target_pairs={{0,8},{2,10},{4,12},{6,14},{8,0},{10,2},{12,4},{14,6},{1,9},{3,11}... | collective-permute-start | bytes 393224 | tf_op jit(solution)/shard_map/ppermute | solution.py:340
  10.3 6.0 %collective-permute-done.block_ref = bf16[256,256]{1,0:T(8,128)(2,1)S(1)} collective-permute-done((bf16[256,256]{1,0:T(8,128)(2,1)S(1)}, bf16[256,256]{1,0:T(8,128)(2,1)S(1)}, u32[]{:S(2)}, u32[]{:S(2)}) %collective-permute-start) | collective-permute-done | bytes 131104 | tf_op jit(solution)/shard_map/ppermute | solution.py:340
  16.3 0.8 %shard_map.124 = bf16[4,256,256]{2,1,0:T(8,128)(2,1)} custom-call(bf16[256,256]{1,0:T(8,128)(2,1)S(1)} %collective-permute-done.block_ref), custom_call_target="tpu_custom_call" | custom-call | bytes 131072 | tf_op jit(solution)/shard_map/pallas_call | solution.py:250
  17.1 1.4 %all-to-all-done.1.field_ref = bf16[4,256,256]{2,1,0:T(8,128)(2,1)S(1)} async-done(((bf16[4,256,256]{2,1,0:T(8,128)(2,1)}), bf16[4,256,256]{2,1,0:T(8,128)(2,1)S(1)}, u32[]{:S(2)}, u32[]{:S(2)}) %all-to-all-start.1) | async-done | bytes 524320 | tf_op jit(solution)/shard_map/all_to_all | solution.py:338
  18.5 0.8 %copy-done.1 = bf16[4,256,256]{2,1,0:T(8,128)(2,1)} copy-done((bf16[4,256,256]{2,1,0:T(8,128)(2,1)}, bf16[4,256,256]{2,1,0:T(8,128)(2,1)S(1)}, u32[]{:S(2)}) %copy-start.1) | copy-done | bytes 524312
  19.3 5.6 %all-to-all-start = ((bf16[4,256,256]{2,1,0:T(8,128)(2,1)}), bf16[4,256,256]{2,1,0:T(8,128)(2,1)}, u32[]{:S(2)}, u32[]{:S(2)}) async-start(bf16[4,256,256]{2,1,0:T(8,128)(2,1)} %shard_map.124), calls=%async_computation | async-start | bytes 1048576 | tf_op jit(solution)/shard_map/all_to_all | solution.py:338
  24.9 1.8 %shard_map.122 = (bf16[8,2,32,256]{3,2,1,0:T(8,128)(2,1)S(1)}, bf16[2,512,256]{2,1,0:T(8,128)(2,1)S(1)}, f32[5,256,128]{2,1,0:T(8,128)S(1)}, f32[256,256]{1,0:T(...) custom-call(s32[2,8]{1,0:T(2,128)} %refs_0_.1, bf16[2,8,32,256]{3,2,1,0:T(8,128)(2,1)} %refs_1_.1, ...), custom_call_target="tpu_custom_call" | custom-call | bytes 1051712 | tf_op jit(solution)/shard_map/pallas_call | solution.py:250
  26.7 0.0 copy-start.23
  26.7 0.7 copy-done.23
  27.4 0.7 copy-done.25
  28.1 0.7 copy-done.27
  28.8 0.7 copy-done.29
  29.5 0.8 %shard_map.125.refs_0_ = f32[2,2,256,256]{3,2,1,0:T(8,128)S(1)} custom-call(s32[2,2]{1,0:T(2,128)S(1)} %copy-done.29, bf16[8,2,32,256]{3,2,1,0:T(8,128)(2,1)S(1)} %get-tuple-element.27.v_ref, bf16[2,512,256]{2,1,0:T(8,128)(2,1)S(1)} %get-tuple-element.28.u_ref, bf16[2,2,2,256,256]{4,3,2,1,0:T(8,128)(2,1)S(1)} %copy-done, bf16[4,256,256]{2,1,0:T(8,128)(2,1)S(1)} %copy-done.2), custom_call_target="tpu_custom_call" | custom-call | flops 100663296 | bytes 2359312 | tf_op jit(solution)/shard_map/pallas_call | solution.py:250
  30.3 1.7 %all-to-all-done.field_ref = bf16[4,256,256]{2,1,0:T(8,128)(2,1)} async-done(((bf16[4,256,256]{2,1,0:T(8,128)(2,1)}), bf16[4,256,256]{2,1,0:T(8,128)(2,1)}, u32[]{:S(2)}, u32[]{:S(2)}) %all-to-all-start) | async-done | bytes 524320 | tf_op jit(solution)/shard_map/all_to_all | solution.py:338
  32.0 1.6 %shard_map.127 = bf16[2,256,256]{2,1,0:T(8,128)(2,1)S(1)} custom-call(s32[2,2]{1,0:T(2,128)S(1)} %copy-done.29, bf16[8,2,32,256]{3,2,1,0:T(8,128)(2,1)S(1)} %get-tuple-element.27.v_ref, bf16[2,512,256]{2,1,0:T(8,128)(2,1)S(1)} %get-tuple-element.28.u_ref, bf16[2,2,2,256,256]{4,3,2,1,0:T(8,128)(2,1)S(1)} %copy-done, ...), custom_call_target="tpu_custom_call" | custom-call | flops 50331648 | bytes 3407888 | tf_op jit(solution)/shard_map/pallas_call | solution.py:250
  33.6 0.0 copy-start.5
  33.6 0.0 copy-start.24
  33.6 0.0 copy-start.26
  33.7 0.1 collective-permute-start.1
  33.7 1.7 %shard_map.126.own = f32[2,256,256]{2,1,0:T(8,128)S(1)} custom-call(s32[2,2]{1,0:T(2,128)S(1)} %copy-done.29, bf16[8,2,32,256]{3,2,1,0:T(8,128)(2,1)S(1)} %get-tuple-element.27.v_ref, bf16[2,512,256]{2,1,0:T(8,128)(2,1)S(1)} %get-tuple-element.28.u_ref, bf16[2,2,2,256,256]{4,3,2,1,0:T(8,128)(2,1)S(1)} %copy-done, ...), custom_call_target="tpu_custom_call" | custom-call | flops 50331648 | bytes 3407888 | tf_op jit(solution)/shard_map/pallas_call | solution.py:250
  35.5 1.1 %shard_map.128 = (f32[256,256]{1,0:T(8,128)S(1)}, f32[256,256]{1,0:T(8,128)S(1)}, f32[256,256]{1,0:T(8,128)S(1)}, f32[256,256]{1,0:T(8,128)S(1)}, bf16[256,256]{...) custom-call(f32[2,256,256]{2,1,0:T(8,128)S(1)} %shard_map.126.own, ...), custom_call_target="tpu_custom_call" | custom-call | flops 13107200 | bytes 2490368 | tf_op jit(solution)/shard_map/pallas_call | solution.py:250
  36.5 0.8 %copy-done.10 = bf16[4,256,256]{2,1,0:T(8,128)(2,1)} copy-done((bf16[4,256,256]{2,1,0:T(8,128)(2,1)}, bf16[4,256,256]{2,1,0:T(8,128)(2,1)S(1)}, u32[]{:S(2)}) %copy-start.10) | copy-done | bytes 524312
  37.4 0.7 copy-done.11
  38.1 0.7 copy-done.13
  38.8 0.7 copy-done.15
  39.5 3.5 %all-to-all-start.3 = ((bf16[4,256,256]{2,1,0:T(8,128)(2,1)}), bf16[4,256,256]{2,1,0:T(8,128)(2,1)S(1)}, u32[]{:S(2)}, u32[]{:S(2)}) async-start(bf16[4,256,256]{2,1,0:T(8,128)(2,1)} %copy-done.10), calls=%async_computation.3 | async-start | bytes 1048576 | tf_op jit(solution)/shard_map/all_to_all | solution.py:338
  42.9 1.0 %collective-permute-start.2 = (bf16[256,256]{1,0:T(8,128)(2,1)S(1)}, bf16[256,256]{1,0:T(8,128)(2,1)S(1)}, u32[]{:S(2)}, u32[]{:S(2)}) collective-permute-start(bf16[256,256]{1,0:T(8,128)(2,1)S(1)} %get-tuple-element.39), channel_id=1, source_target_pairs={{0,8},{2,10},{4,12},{6,14},{8,0},{10,2},{12,4},{14,6},{1,9},{3,11}... | collective-permute-start | bytes 393224 | tf_op jit(solution)/shard_map/ppermute | solution.py:340
  43.9 8.5 %collective-permute-done.2.block_ref = bf16[256,256]{1,0:T(8,128)(2,1)S(1)} collective-permute-done((bf16[256,256]{1,0:T(8,128)(2,1)S(1)}, bf16[256,256]{1,0:T(8,128)(2,1)S(1)}, u32[]{:S(2)}, u32[]{:S(2)}) %collective-permute-start.2) | collective-permute-done | bytes 131104 | tf_op jit(solution)/shard_map/ppermute | solution.py:340
  52.4 0.8 %shard_map.129 = bf16[4,256,256]{2,1,0:T(8,128)(2,1)} custom-call(bf16[256,256]{1,0:T(8,128)(2,1)S(1)} %collective-permute-done.2.block_ref), custom_call_target="tpu_custom_call" | custom-call | bytes 131072 | tf_op jit(solution)/shard_map/pallas_call | solution.py:250
  53.3 1.3 %all-to-all-done.3.field_ref = bf16[4,256,256]{2,1,0:T(8,128)(2,1)S(1)} async-done(((bf16[4,256,256]{2,1,0:T(8,128)(2,1)}), bf16[4,256,256]{2,1,0:T(8,128)(2,1)S(1)}, u32[]{:S(2)}, u32[]{:S(2)}) %all-to-all-start.3) | async-done | bytes 524320 | tf_op jit(solution)/shard_map/all_to_all | solution.py:338
  54.6 0.8 %copy-done.3 = bf16[4,256,256]{2,1,0:T(8,128)(2,1)} copy-done((bf16[4,256,256]{2,1,0:T(8,128)(2,1)}, bf16[4,256,256]{2,1,0:T(8,128)(2,1)S(1)}, u32[]{:S(2)}) %copy-start.3) | copy-done | bytes 524312
  55.4 4.1 %all-to-all-start.2 = ((bf16[4,256,256]{2,1,0:T(8,128)(2,1)}), bf16[4,256,256]{2,1,0:T(8,128)(2,1)}, u32[]{:S(2)}, u32[]{:S(2)}) async-start(bf16[4,256,256]{2,1,0:T(8,128)(2,1)} %shard_map.129), calls=%async_computation.2 | async-start | bytes 1048576 | tf_op jit(solution)/shard_map/all_to_all | solution.py:338
  59.5 0.1 shard_map.130
  59.7 0.0 copy-start.17
  59.7 0.7 copy-done.17
  60.4 0.7 copy-done.19
  61.1 0.7 copy-done.21
  61.8 0.8 %shard_map.131.refs_0_ = f32[2,2,256,256]{3,2,1,0:T(8,128)S(1)} custom-call(s32[2,2]{1,0:T(2,128)S(1)} %copy-done.29, bf16[8,2,32,256]{3,2,1,0:T(8,128)(2,1)S(1)} %get-tuple-element.27.v_ref, bf16[2,512,256]{2,1,0:T(8,128)(2,1)S(1)} %get-tuple-element.28.u_ref, bf16[2,2,2,256,256]{4,3,2,1,0:T(8,128)(2,1)S(1)} %copy-done, bf16[4,256,256]{2,1,0:T(8,128)(2,1)S(1)} %copy-done.4), custom_call_target="tpu_custom_call" | custom-call | flops 100663296 | bytes 2359312 | tf_op jit(solution)/shard_map/pallas_call | solution.py:250
  62.6 5.2 %all-to-all-done.2.field_ref = bf16[4,256,256]{2,1,0:T(8,128)(2,1)} async-done(((bf16[4,256,256]{2,1,0:T(8,128)(2,1)}), bf16[4,256,256]{2,1,0:T(8,128)(2,1)}, u32[]{:S(2)}, u32[]{:S(2)}) %all-to-all-start.2) | async-done | bytes 524320 | tf_op jit(solution)/shard_map/all_to_all | solution.py:338
  67.7 1.6 %shard_map.133 = bf16[2,256,256]{2,1,0:T(8,128)(2,1)S(1)} custom-call(s32[2,2]{1,0:T(2,128)S(1)} %copy-done.29, bf16[8,2,32,256]{3,2,1,0:T(8,128)(2,1)S(1)} %get-tuple-element.27.v_ref, bf16[2,512,256]{2,1,0:T(8,128)(2,1)S(1)} %get-tuple-element.28.u_ref, bf16[2,2,2,256,256]{4,3,2,1,0:T(8,128)(2,1)S(1)} %copy-done, ...), custom_call_target="tpu_custom_call" | custom-call | flops 50331648 | bytes 3407888 | tf_op jit(solution)/shard_map/pallas_call | solution.py:250
  69.3 0.0 copy-start.6
  69.4 0.0 copy-start.18
  69.4 0.0 copy-start.20
  69.4 0.1 collective-permute-start.3
  69.5 1.7 %shard_map.132.own = f32[2,256,256]{2,1,0:T(8,128)S(1)} custom-call(s32[2,2]{1,0:T(2,128)S(1)} %copy-done.29, bf16[8,2,32,256]{3,2,1,0:T(8,128)(2,1)S(1)} %get-tuple-element.27.v_ref, bf16[2,512,256]{2,1,0:T(8,128)(2,1)S(1)} %get-tuple-element.28.u_ref, bf16[2,2,2,256,256]{4,3,2,1,0:T(8,128)(2,1)S(1)} %copy-done, ...), custom_call_target="tpu_custom_call" | custom-call | flops 50331648 | bytes 3407888 | tf_op jit(solution)/shard_map/pallas_call | solution.py:250
  71.3 1.8 %shard_map.134 = (f32[256,256]{1,0:T(8,128)}, f32[256,256]{1,0:T(8,128)}) custom-call(f32[2,256,256]{2,1,0:T(8,128)S(1)} %shard_map.132.own, bf16[2,256,256]{2,1,0:T(8,128)(2,1)S(1)} %collective-permute-done.3.other, f32[256,256]{1,0:T(8,128)S(1)} %copy-done.18, f32[256,256]{1,0:T(8,128)S(1)} %copy-done.20, f32[256,256]{1,0:T(8,128)S(1)} %copy-done.22, ...), custom_call_target="tpu_custom_call" | custom-call | flops 13107200 | bytes 3538944 | tf_op jit(solution)/shard_map/pallas_call | solution.py:250
  (41 shorter events, 0.1 us)
Async XLA Ops:
  2.4 16.0 %all-to-all-start.1 = ((bf16[4,256,256]{2,1,0:T(8,128)(2,1)}), bf16[4,256,256]{2,1,0:T(8,128)(2,1)S(1)}, u32[]{:S(2)}, u32[]{:S(2)}) async-start(bf16[4,256,256]{2,1,0:T(8,128)(2,1)} %get-tuple-element.30), calls=%async_computation.1 | async-start | bytes 1048576 | tf_op jit(solution)/shard_map/all_to_all | solution.py:338
  7.7 8.6 %collective-permute-start = (bf16[256,256]{1,0:T(8,128)(2,1)S(1)}, bf16[256,256]{1,0:T(8,128)(2,1)S(1)}, u32[]{:S(2)}, u32[]{:S(2)}) collective-permute-start(bf16[256,256]{1,0:T(8,128)(2,1)S(1)} %get-tuple-element.29), channel_id=1, source_target_pairs={{0,8},{2,10},{4,12},{6,14},{8,0},{10,2},{12,4},{14,6},{1,9},{3,11}... | collective-permute-start | bytes 393224 | tf_op jit(solution)/shard_map/ppermute | solution.py:340
  17.1 11.7 %copy-start = (bf16[2,2,2,256,256]{4,3,2,1,0:T(8,128)(2,1)S(1)}, bf16[2,2,2,256,256]{4,3,2,1,0:T(8,128)(2,1)}, u32[]{:S(2)}) copy-start(bf16[2,2,2,256,256]{4,3,2,1,0:T(8,128)(2,1)} %d_ref.11) | copy-start | bytes 3145732
  18.5 0.8 %copy-start.1 = (bf16[4,256,256]{2,1,0:T(8,128)(2,1)}, bf16[4,256,256]{2,1,0:T(8,128)(2,1)S(1)}, u32[]{:S(2)}) copy-start(bf16[4,256,256]{2,1,0:T(8,128)(2,1)S(1)} %all-to-all-done.1.field_ref) | copy-start | bytes 1572868
  19.3 12.7 %all-to-all-start = ((bf16[4,256,256]{2,1,0:T(8,128)(2,1)}), bf16[4,256,256]{2,1,0:T(8,128)(2,1)}, u32[]{:S(2)}, u32[]{:S(2)}) async-start(bf16[4,256,256]{2,1,0:T(8,128)(2,1)} %shard_map.124), calls=%async_computation | async-start | bytes 1048576 | tf_op jit(solution)/shard_map/all_to_all | solution.py:338
  24.9 3.9 %copy-start.2 = (bf16[4,256,256]{2,1,0:T(8,128)(2,1)S(1)}, bf16[4,256,256]{2,1,0:T(8,128)(2,1)}, u32[]{:S(2)}) copy-start(bf16[4,256,256]{2,1,0:T(8,128)(2,1)} %copy-done.1) | copy-start | bytes 1572868
  26.7 0.7 copy-start.23
  27.4 0.7 copy-start.25
  28.1 0.7 copy-start.27
  28.8 0.7 copy-start.29
  33.6 1.8 %copy-start.5 = (f32[256,256]{1,0:T(8,128)S(1)}, f32[256,256]{1,0:T(8,128)}, u32[]{:S(2)}) copy-start(f32[256,256]{1,0:T(8,128)} %tau.3) | copy-start | bytes 786436
  33.6 1.8 %copy-start.24 = (f32[256,256]{1,0:T(8,128)S(1)}, f32[256,256]{1,0:T(8,128)}, u32[]{:S(2)}) copy-start(f32[256,256]{1,0:T(8,128)} %copy-done.23) | copy-start | bytes 786436
  33.6 1.8 %copy-start.26 = (f32[256,256]{1,0:T(8,128)S(1)}, f32[256,256]{1,0:T(8,128)}, u32[]{:S(2)}) copy-start(f32[256,256]{1,0:T(8,128)} %copy-done.25) | copy-start | bytes 786436
  33.7 1.8 %copy-start.28 = (f32[256,256]{1,0:T(8,128)S(1)}, f32[256,256]{1,0:T(8,128)}, u32[]{:S(2)}) copy-start(f32[256,256]{1,0:T(8,128)} %copy-done.27) | copy-start | bytes 786436
  33.7 1.8 %collective-permute-start.1 = (bf16[2,256,256]{2,1,0:T(8,128)(2,1)S(1)}, bf16[2,256,256]{2,1,0:T(8,128)(2,1)S(1)}, u32[]{:S(2)}, u32[]{:S(2)}) collective-permute-start(bf16[2,256,256]{2,1,0:T(8,128)(2,1)S(1)} %shard_map.127), channel_id=1, source_target_pairs={{0,1},{1,0},{2,3},{3,2},{4,5},{5,4},{6,7},{7,6},{8,9},{9,8},{10,11... | collective-permute-start | bytes 786440 | tf_op jit(solution)/shard_map/ppermute | solution.py:352
  36.5 0.8 %copy-start.10 = (bf16[4,256,256]{2,1,0:T(8,128)(2,1)}, bf16[4,256,256]{2,1,0:T(8,128)(2,1)S(1)}, u32[]{:S(2)}) copy-start(bf16[4,256,256]{2,1,0:T(8,128)(2,1)S(1)} %get-tuple-element.40) | copy-start | bytes 1572868
  37.4 0.7 copy-start.11
  38.1 0.7 copy-start.13
  38.8 0.7 copy-start.15
  39.5 20.1 %copy-start.7 = (f32[256,256]{1,0:T(8,128)}, f32[256,256]{1,0:T(8,128)S(1)}, u32[]{:S(2)}) copy-start(f32[256,256]{1,0:T(8,128)S(1)} %get-tuple-element.41.change) | copy-start | bytes 786436
  39.5 15.1 %all-to-all-start.3 = ((bf16[4,256,256]{2,1,0:T(8,128)(2,1)}), bf16[4,256,256]{2,1,0:T(8,128)(2,1)S(1)}, u32[]{:S(2)}, u32[]{:S(2)}) async-start(bf16[4,256,256]{2,1,0:T(8,128)(2,1)} %copy-done.10), calls=%async_computation.3 | async-start | bytes 1048576 | tf_op jit(solution)/shard_map/all_to_all | solution.py:338
  42.9 9.5 %collective-permute-start.2 = (bf16[256,256]{1,0:T(8,128)(2,1)S(1)}, bf16[256,256]{1,0:T(8,128)(2,1)S(1)}, u32[]{:S(2)}, u32[]{:S(2)}) collective-permute-start(bf16[256,256]{1,0:T(8,128)(2,1)S(1)} %get-tuple-element.39), channel_id=1, source_target_pairs={{0,8},{2,10},{4,12},{6,14},{8,0},{10,2},{12,4},{14,6},{1,9},{3,11}... | collective-permute-start | bytes 393224 | tf_op jit(solution)/shard_map/ppermute | solution.py:340
  53.2 6.3 %copy-start.9 = (f32[256,256]{1,0:T(8,128)S(1)}, f32[256,256]{1,0:T(8,128)}, u32[]{:S(2)}) copy-start(f32[256,256]{1,0:T(8,128)} %state.1) | copy-start | bytes 786436
  54.6 0.8 %copy-start.3 = (bf16[4,256,256]{2,1,0:T(8,128)(2,1)}, bf16[4,256,256]{2,1,0:T(8,128)(2,1)S(1)}, u32[]{:S(2)}) copy-start(bf16[4,256,256]{2,1,0:T(8,128)(2,1)S(1)} %all-to-all-done.3.field_ref) | copy-start | bytes 1572868
  55.4 12.4 %all-to-all-start.2 = ((bf16[4,256,256]{2,1,0:T(8,128)(2,1)}), bf16[4,256,256]{2,1,0:T(8,128)(2,1)}, u32[]{:S(2)}, u32[]{:S(2)}) async-start(bf16[4,256,256]{2,1,0:T(8,128)(2,1)} %shard_map.129), calls=%async_computation.2 | async-start | bytes 1048576 | tf_op jit(solution)/shard_map/all_to_all | solution.py:338
  59.5 2.3 %copy-start.4 = (bf16[4,256,256]{2,1,0:T(8,128)(2,1)S(1)}, bf16[4,256,256]{2,1,0:T(8,128)(2,1)}, u32[]{:S(2)}) copy-start(bf16[4,256,256]{2,1,0:T(8,128)(2,1)} %copy-done.3) | copy-start | bytes 1572868
  59.7 0.7 copy-start.17
  60.4 0.7 copy-start.19
  61.1 0.7 copy-start.21
  69.3 1.9 %copy-start.6 = (f32[256,256]{1,0:T(8,128)S(1)}, f32[256,256]{1,0:T(8,128)}, u32[]{:S(2)}) copy-start(f32[256,256]{1,0:T(8,128)} %tau.3) | copy-start | bytes 786436
  69.4 1.9 %copy-start.8 = (f32[256,256]{1,0:T(8,128)S(1)}, f32[256,256]{1,0:T(8,128)}, u32[]{:S(2)}) copy-start(f32[256,256]{1,0:T(8,128)} %copy-done.7) | copy-start | bytes 786436
  69.4 1.9 %copy-start.12 = (f32[256,256]{1,0:T(8,128)S(1)}, f32[256,256]{1,0:T(8,128)}, u32[]{:S(2)}) copy-start(f32[256,256]{1,0:T(8,128)} %copy-done.11) | copy-start | bytes 786436
  69.4 1.9 %copy-start.14 = (f32[256,256]{1,0:T(8,128)S(1)}, f32[256,256]{1,0:T(8,128)}, u32[]{:S(2)}) copy-start(f32[256,256]{1,0:T(8,128)} %copy-done.13) | copy-start | bytes 786436
  69.4 1.9 %copy-start.16 = (f32[256,256]{1,0:T(8,128)S(1)}, f32[256,256]{1,0:T(8,128)}, u32[]{:S(2)}) copy-start(f32[256,256]{1,0:T(8,128)} %copy-done.15) | copy-start | bytes 786436
  69.4 1.9 %copy-start.18 = (f32[256,256]{1,0:T(8,128)S(1)}, f32[256,256]{1,0:T(8,128)}, u32[]{:S(2)}) copy-start(f32[256,256]{1,0:T(8,128)} %copy-done.17) | copy-start | bytes 786436
  69.4 1.9 %copy-start.20 = (f32[256,256]{1,0:T(8,128)S(1)}, f32[256,256]{1,0:T(8,128)}, u32[]{:S(2)}) copy-start(f32[256,256]{1,0:T(8,128)} %copy-done.19) | copy-start | bytes 786436
  69.4 1.9 %copy-start.22 = (f32[256,256]{1,0:T(8,128)S(1)}, f32[256,256]{1,0:T(8,128)}, u32[]{:S(2)}) copy-start(f32[256,256]{1,0:T(8,128)} %copy-done.21) | copy-start | bytes 786436
  69.4 1.8 %collective-permute-start.3 = (bf16[2,256,256]{2,1,0:T(8,128)(2,1)S(1)}, bf16[2,256,256]{2,1,0:T(8,128)(2,1)S(1)}, u32[]{:S(2)}, u32[]{:S(2)}) collective-permute-start(bf16[2,256,256]{2,1,0:T(8,128)(2,1)S(1)} %shard_map.133), channel_id=1, source_target_pairs={{0,1},{1,0},{2,3},{3,2},{4,5},{5,4},{6,7},{7,6},{8,9},{9,8},{10,11... | collective-permute-start | bytes 786440 | tf_op jit(solution)/shard_map/ppermute | solution.py:352

commit v16 on v14

--- a/solution.py
+++ b/solution.py
@@ -9,7 +9,7 @@
 
 NEWTON = 2
 DIRECT_COUNTS = (4, 8)
-LATE = 4
+TILE = 128
 
 damping = 0.5
 sigma_floor = 0.5
@@ -18,8 +18,9 @@
 
 def arrivals(count, direct):
     if not direct:
-        return list(range(count))
-    return [0, 1, 4, 2, 3, 5, 6, 7] if count == 8 else [0, 1, 2, 3]
+        cuts = [0, max(count - 4, 0), count]
+        return [list(range(first, last)) for first, last in zip(cuts, cuts[1:]) if last > first]
+    return [[0, 1, 4, 2, 3], [6, 5, 7]] if count == 8 else [[0, 1], [2, 3]]
 
 
 def row_met(spot, row, direct):
@@ -31,12 +32,13 @@
         return lax.ppermute(data, "row", [(row, row ^ mask) for row in range(count)])
 
     found = {0: block}
-    for mask in (4, 1, 2, 3) if count == 8 else (1, 2, 3):
+    for mask in (4, 1, 2) if count == 8 else (1, 2):
         found[mask] = swapped(mask, block)
+    found[3] = swapped(2, found[1])
     if count == 8:
         for mask in (1, 2, 3):
             found[4 + mask] = swapped(mask, found[4])
-    return [found[mask] for mask in arrivals(count, True)]
+    return [[found[mask] for mask in group] for group in arrivals(count, True)]
 
 
 IN_PIECES = 8
@@ -73,7 +75,7 @@
         store_powers(outs, part, state[:, part] + section_step * change[:, part], coef)
 
 
-def prepare_kernel(spots, direct, *refs):
+def prepare_kernel(groups, direct, *refs):
     far, (v_out, u_out, coef_out, *powers), near, sem = refs[:7], refs[7:13], refs[13:20], refs[20]
     copies = [
         pltpu.make_async_copy(source, held, sem.at[at])
@@ -86,19 +88,23 @@
     rank_ref, v_ref, u_ref, sigma_ref, a_ref, b_ref, state_ref = near
     kinds, rows, count, rank_count, size = u_ref.shape
     row = lax.axis_index("row")
-    met = [row_met(spot, row, direct) for spot in spots]
+    met = [row_met(spot, row, direct) for group in groups for spot in group]
     for at, q in enumerate(met):
         for p in range(rows):
             inside = lax.broadcasted_iota(jnp.int32, (rank_count, size), 0) < rank_ref[p, q]
             v_out[at, p] = jnp.where(inside, v_ref[p, q].astype(jnp.float32), 0.0).astype(v_out.dtype)
     for p in range(rows):
         for kind in range(kinds):
-            for first in range(0, count, 4):
-                group = [u_ref[kind, p, q] for q in met[first : first + 4]]
+            first = start = 0
+            for spots in groups:
+                group = [u_ref[kind, p, q] for q in met[first : first + len(spots)]]
+                spare = -len(group) * rank_count % TILE
+                if spare:
+                    group.append(jnp.zeros((spare, size), u_ref.dtype))
                 turned = jnp.concatenate(group, axis=0).astype(jnp.float32).T
-                u_out[p, kind * size : (kind + 1) * size, first * rank_count : (first + len(group)) * rank_count] = (
-                    turned.astype(u_out.dtype)
-                )
+                stop = start + turned.shape[1]
+                u_out[p, kind * size : (kind + 1) * size, start:stop] = turned.astype(u_out.dtype)
+                first, start = first + len(spots), stop
     lanes = coef_out.shape[2]
     for at, values in enumerate((sigma_ref[...], a_ref[...], b_ref[...], 1.0 / a_ref[...], 1.0 / b_ref[...])):
         coef_out[at] = jnp.broadcast_to(values, (lanes, size)).T
@@ -107,7 +113,7 @@
         store_powers(powers, part, state_ref[:, part], coef_out)
 
 
-def sums_kernel(spots, direct, first, pick, before, near_ref, v_ref, u_ref, d_ref, *refs):
+def sums_kernel(spots, direct, first, start, pick, before, near_ref, v_ref, u_ref, d_ref, *refs):
     blocks = refs[: len(spots)]
     refs = refs[len(spots) :]
     if before:
@@ -129,7 +135,13 @@
             proj[place, at * rank_count : (at + 1) * rank_count, :] = part[
                 place * rank_count : (place + 1) * rank_count
             ]
-    lanes = slice(first * rank_count, (first + len(blocks)) * rank_count)
+    width = proj.shape[1]
+    lanes = slice(start, start + width)
+    if width > len(blocks) * rank_count:
+        for place in range(len(chosen)):
+            proj[place, len(blocks) * rank_count :, :] = jnp.zeros(
+                (width - len(blocks) * rank_count, proj.shape[2]), proj.dtype
+            )
     for place, p in enumerate(chosen):
         weights, fields = [u_ref[p, :, lanes]], [proj[place]]
         for s in range(slots):
@@ -285,8 +297,10 @@
     size, members = slip_deficit.shape
     kinds, rows, _, rank_count, _ = u_basis.shape
     direct = count in DIRECT_COUNTS
-    spots = arrivals(count, direct)
-    early = max(count - LATE, 0)
+    groups = arrivals(count, direct)
+    firsts = [sum(len(group) for group in groups[:at]) for at in range(len(groups))]
+    tiles = [-(-len(group) * rank_count // TILE) * TILE for group in groups]
+    starts = [sum(tiles[:at]) for at in range(len(groups))]
     room = 16 if direct else 40
     lanes = min(members, 128)
     narrow, wide = jnp.bfloat16, jnp.float32
@@ -297,10 +311,10 @@
 
     full = shaped(size, members)
     v_met, u_met, coef, *powers = on_core(
-        functools.partial(prepare_kernel, spots, direct),
+        functools.partial(prepare_kernel, groups, direct),
         (
             shaped(count, rows, rank_count, size, kind=narrow),
-            shaped(rows, kinds * size, count * rank_count, kind=narrow),
+            shaped(rows, kinds * size, sum(tiles), kind=narrow),
             shaped(5, size, lanes),
             full,
             full,
@@ -327,17 +341,17 @@
         ),
     )
 
-    def add(blocks, first, pick, before, kind):
+    def add(blocks, at, pick, before, kind):
         held = rows if pick is None else 1
         lead = (rows, kinds) if pick is None else (kinds,)
         return on_core(
             functools.partial(
-                sums_kernel, spots[first : first + len(blocks)], direct, first, pick, before is not None
+                sums_kernel, groups[at], direct, firsts[at], starts[at], pick, before is not None
             ),
             shaped(*lead, size, members, kind=kind),
             (near_index, v_met, u_met, dense_blocks, *blocks, *(() if before is None else (before,))),
             (
-                pltpu.VMEM((held, len(blocks) * rank_count, members), narrow),
+                pltpu.VMEM((held, tiles[at], members), narrow),
             ),
             2 * held * size * members * rank_count * len(blocks) * 3,
             room,
@@ -345,14 +359,16 @@
 
     def lattice(field_half, beside):
         if direct:
-            blocks = gather_direct(field_half, count)
+            found = gather_direct(field_half, count)
         else:
             whole = lax.all_gather(field_half, "row", axis=0)
-            blocks = [whole[r] for r in range(count)]
-        blocks[0], beside = lax.optimization_barrier((blocks[0], beside))
-        sums = add(blocks[:early], 0, None, None, wide) if early else None
-        other = lax.ppermute(add(blocks[early:], early, 1, sums, narrow), "col", swap)
-        return add(blocks[early:], early, 0, sums, wide), other, beside
+            found = [[whole[r] for r in group] for group in groups]
+        found[0][0], beside = lax.optimization_barrier((found[0][0], beside))
+        sums, end = None, len(groups) - 1
+        for at in range(end):
+            sums = add(found[at], at, None, sums, wide)
+        other = lax.ppermute(add(found[end], end, 1, sums, narrow), "col", swap)
+        return add(found[end], end, 0, sums, wide), other, beside
 
     slip_half = on_core(
         narrow_kernel,

time: 47.2 us -> 47.7 us (1.011)
  starting transfers between devices: 20.1 us -> 22 us
  waiting for transfers between devices: 15.8 us -> 14.5 us
    ppermute x14, starting transfers between devices: 20 us -> 21.9 us  [swapped(): lax.ppermute(data, 'row', [(row, row ^ mask) for row in range(count)])]
    ppermute x14, waiting for transfers between devices: 13.9 us -> 12.5 us  [swapped(): lax.ppermute(data, 'row', [(row, row ^ mask) for row in range(count)])]
  transfers between devices with their start and end apart: 16 -> 16, of which waited for: 10 -> 11; matrix products, arithmetic and copies ran while one was open for 0% -> 0% of each run, Pallas kernels for 10% -> 10%
where the time goes in v16:
time: 47.7 us; the launch traced here: 47.5 us
  starting transfers between devices  22 us (46%)
  waiting for transfers between devices  14.5 us (30%)
  Pallas kernels  9.6 us (20%)
  between operations  0.78 us (2%)
  local copies, waits for them, and re-layouts  0.68 us (1%)
    ppermute x14, starting transfers between devices, swapped(): lax.ppermute(data, 'row', [(row, row ^ mask) for row in range(count)])  21.9 us
    ppermute x14, waiting for transfers between devices, swapped(): lax.ppermute(data, 'row', [(row, row ^ mask) for row in range(count)])  12.5 us
    pallas_call x11, Pallas kernels, on_core(): pl.pallas_call(kernel, out_shape=outs, in_specs=[hbm] * len(far) + [vmem]...  9.6 us
    ppermute x2, waiting for transfers between devices, lattice(): other = lax.ppermute(add(found[end], end, 1, sums, narrow), 'col', swap)  1.97 us
  transfers between devices with their start and end apart: 16, of which 11 were waited for; matrix products, arithmetic and copies ran while one was open for 0% of the time, Pallas kernels for 10%

profile of v16, /device:TPU:0, one launch (start us, length us, event | category | flops | bytes accessed | tf_op | source)
XLA Modules:
  0.0 47.5 jit_solution(16686231686753855840)
XLA Ops:
  0.6 1.0 %shard_map.123.refs_0_ = bf16[256,256]{1,0:T(8,128)(2,1)S(1)} custom-call(f32[256,256]{1,0:T(8,128)} %wide_ref.1), custom_call_target="tpu_custom_call" | custom-call | bytes 262144 | tf_op jit(solution)/shard_map/pallas_call | solution.py:270
  1.7 3.0 %collective-permute-start.4 = (bf16[256,256]{1,0:T(8,128)(2,1)S(1)}, bf16[256,256]{1,0:T(8,128)(2,1)S(1)}, u32[]{:S(2)}, u32[]{:S(2)}) collective-permute-start(bf16[256,256]{1,0:T(8,128)(2,1)S(1)} %shard_map.123.refs_0_), channel_id=1, source_target_pairs={{0,2},{2,0},{4,6},{6,4},{8,10},{10,8},{12,14},{14,12},{1,3},{3,1},... | collective-permute-start | bytes 393224 | tf_op jit(solution)/shard_map/ppermute | solution.py:32
  4.7 2.6 %collective-permute-start = (bf16[256,256]{1,0:T(8,128)(2,1)S(1)}, bf16[256,256]{1,0:T(8,128)(2,1)S(1)}, u32[]{:S(2)}, u32[]{:S(2)}) collective-permute-start(bf16[256,256]{1,0:T(8,128)(2,1)S(1)} %shard_map.123.refs_0_), channel_id=1, source_target_pairs={{0,8},{2,10},{4,12},{6,14},{8,0},{10,2},{12,4},{14,6},{1,9},{3,11}... | collective-permute-start | bytes 393224 | tf_op jit(solution)/shard_map/ppermute | solution.py:32
  7.3 1.6 %collective-permute-start.5 = (bf16[256,256]{1,0:T(8,128)(2,1)S(1)}, bf16[256,256]{1,0:T(8,128)(2,1)S(1)}, u32[]{:S(2)}, u32[]{:S(2)}) collective-permute-start(bf16[256,256]{1,0:T(8,128)(2,1)S(1)} %shard_map.123.refs_0_), channel_id=1, source_target_pairs={{0,4},{2,6},{4,0},{6,2},{8,12},{10,14},{12,8},{14,10},{1,5},{3,7},... | collective-permute-start | bytes 393224 | tf_op jit(solution)/shard_map/ppermute | solution.py:32
  8.9 0.0 collective-permute-done.4.refs_1_
  8.9 1.1 %collective-permute-start.6 = (bf16[256,256]{1,0:T(8,128)(2,1)S(1)}, bf16[256,256]{1,0:T(8,128)(2,1)S(1)}, u32[]{:S(2)}, u32[]{:S(2)}) collective-permute-start(bf16[256,256]{1,0:T(8,128)(2,1)S(1)} %collective-permute-done.4.refs_1_), channel_id=1, source_target_pairs={{0,4},{2,6},{4,0},{6,2},{8,12},{10,14},{12,8},{14,10},{1,5},{3,7},... | collective-permute-start | bytes 393224 | tf_op jit(solution)/shard_map/ppermute | solution.py:32
  10.0 3.5 %collective-permute-done.refs_2_ = bf16[256,256]{1,0:T(8,128)(2,1)S(1)} collective-permute-done((bf16[256,256]{1,0:T(8,128)(2,1)S(1)}, bf16[256,256]{1,0:T(8,128)(2,1)S(1)}, u32[]{:S(2)}, u32[]{:S(2)}) %collective-permute-start) | collective-permute-done | bytes 131104 | tf_op jit(solution)/shard_map/ppermute | solution.py:32
  13.5 0.6 %collective-permute-start.3 = (bf16[256,256]{1,0:T(8,128)(2,1)S(1)}, bf16[256,256]{1,0:T(8,128)(2,1)S(1)}, u32[]{:S(2)}, u32[]{:S(2)}) collective-permute-start(bf16[256,256]{1,0:T(8,128)(2,1)S(1)} %collective-permute-done.refs_2_), channel_id=1, source_target_pairs={{0,6},{2,4},{4,2},{6,0},{8,14},{10,12},{12,10},{14,8},{1,7},{3,5},... | collective-permute-start | bytes 393224 | tf_op jit(solution)/shard_map/ppermute | solution.py:32
  14.0 1.5 %collective-permute-start.2 = (bf16[256,256]{1,0:T(8,128)(2,1)S(1)}, bf16[256,256]{1,0:T(8,128)(2,1)S(1)}, u32[]{:S(2)}, u32[]{:S(2)}) collective-permute-start(bf16[256,256]{1,0:T(8,128)(2,1)S(1)} %collective-permute-done.refs_2_), channel_id=1, source_target_pairs={{0,2},{2,0},{4,6},{6,4},{8,10},{10,8},{12,14},{14,12},{1,3},{3,1},... | collective-permute-start | bytes 393224 | tf_op jit(solution)/shard_map/ppermute | solution.py:32
  15.6 1.4 %collective-permute-start.1 = (bf16[256,256]{1,0:T(8,128)(2,1)S(1)}, bf16[256,256]{1,0:T(8,128)(2,1)S(1)}, u32[]{:S(2)}, u32[]{:S(2)}) collective-permute-start(bf16[256,256]{1,0:T(8,128)(2,1)S(1)} %collective-permute-done.refs_2_), channel_id=1, source_target_pairs={{0,4},{2,6},{4,0},{6,2},{8,12},{10,14},{12,8},{14,10},{1,5},{3,7},... | collective-permute-start | bytes 393224 | tf_op jit(solution)/shard_map/ppermute | solution.py:32
  17.0 1.8 %shard_map.122 = (bf16[8,2,32,256]{3,2,1,0:T(8,128)(2,1)S(1)}, bf16[2,512,384]{2,1,0:T(8,128)(2,1)S(1)}, f32[5,256,128]{2,1,0:T(8,128)S(1)}, f32[256,256]{1,0:T(...) custom-call(s32[2,8]{1,0:T(2,128)} %refs_0_.1, bf16[2,8,32,256]{3,2,1,0:T(8,128)(2,1)} %refs_1_.1, ...), custom_call_target="tpu_custom_call" | custom-call | bytes 1051712 | tf_op jit(solution)/shard_map/pallas_call | solution.py:270
  18.8 0.0 collective-permute-done.5.refs_3_
  18.8 0.0 collective-permute-done.6.refs_4_
  18.8 0.0 copy-start.3
  18.8 0.7 %copy-done.3 = s32[2,2]{1,0:T(2,128)S(1)} copy-done((s32[2,2]{1,0:T(2,128)S(1)}, s32[2,2]{1,0:T(2,128)}, u32[]{:S(2)}) %copy-start.3) | copy-done | bytes 40
  19.5 0.9 %shard_map.124.refs_3_ = f32[2,2,256,256]{3,2,1,0:T(8,128)S(1)} custom-call(s32[2,2]{1,0:T(2,128)S(1)} %copy-done.3, bf16[8,2,32,256]{3,2,1,0:T(8,128)(2,1)S(1)} %get-tuple-element.24.v_ref, bf16[2,512,384]{2,1,0:T(8,128)(2,1)S(1)} %get-tuple-element.25.u_ref, bf16[2,2,2,256,256]{4,3,2,1,0:T(8,128)(2,1)S(1)} %copy-done, ...), custom_call_target="tpu_custom_call" | custom-call | flops 125829120 | bytes 2752528 | tf_op jit(solution)/shard_map/pallas_call | solution.py:270
  20.3 0.3 collective-permute-done.3.refs_2_
  20.6 0.7 %collective-permute-done.2.refs_1_ = bf16[256,256]{1,0:T(8,128)(2,1)S(1)} collective-permute-done((bf16[256,256]{1,0:T(8,128)(2,1)S(1)}, bf16[256,256]{1,0:T(8,128)(2,1)S(1)}, u32[]{:S(2)}, u32[]{:S(2)}) %collective-permute-start.2) | collective-permute-done | bytes 131104 | tf_op jit(solution)/shard_map/ppermute | solution.py:32
  21.3 0.8 %collective-permute-done.1.refs_0_ = bf16[256,256]{1,0:T(8,128)(2,1)S(1)} collective-permute-done((bf16[256,256]{1,0:T(8,128)(2,1)S(1)}, bf16[256,256]{1,0:T(8,128)(2,1)S(1)}, u32[]{:S(2)}, u32[]{:S(2)}) %collective-permute-start.1) | collective-permute-done | bytes 131104 | tf_op jit(solution)/shard_map/ppermute | solution.py:32
  22.1 0.5 %shard_map.126 = bf16[2,256,256]{2,1,0:T(8,128)(2,1)S(1)} custom-call(s32[2,2]{1,0:T(2,128)S(1)} %copy-done.3, bf16[8,2,32,256]{3,2,1,0:T(8,128)(2,1)S(1)} %get-tuple-element.24.v_ref, bf16[2,512,384]{2,1,0:T(8,128)(2,1)S(1)} %get-tuple-element.25.u_ref, bf16[2,2,2,256,256]{4,3,2,1,0:T(8,128)(2,1)S(1)} %copy-done, ...), custom_call_target="tpu_custom_call" | custom-call | flops 37748736 | bytes 3538960 | tf_op jit(solution)/shard_map/pallas_call | solution.py:270
  22.6 0.0 copy-start.1
  22.6 0.1 collective-permute-start.7
  22.7 0.5 %shard_map.125.own = f32[2,256,256]{2,1,0:T(8,128)S(1)} custom-call(s32[2,2]{1,0:T(2,128)S(1)} %copy-done.3, bf16[8,2,32,256]{3,2,1,0:T(8,128)(2,1)S(1)} %get-tuple-element.24.v_ref, bf16[2,512,384]{2,1,0:T(8,128)(2,1)S(1)} %get-tuple-element.25.u_ref, bf16[2,2,2,256,256]{4,3,2,1,0:T(8,128)(2,1)S(1)} %copy-done, ...), custom_call_target="tpu_custom_call" | custom-call | flops 37748736 | bytes 3538960 | tf_op jit(solution)/shard_map/pallas_call | solution.py:270
  23.3 1.0 %collective-permute-done.7.other = bf16[2,256,256]{2,1,0:T(8,128)(2,1)S(1)} collective-permute-done((bf16[2,256,256]{2,1,0:T(8,128)(2,1)S(1)}, bf16[2,256,256]{2,1,0:T(8,128)(2,1)S(1)}, u32[]{:S(2)}, u32[]{:S(2)}) %collective-permute-start.7) | collective-permute-done | bytes 262176 | tf_op jit(solution)/shard_map/ppermute | solution.py:370
  24.2 0.0 copy-done.1
  24.3 1.0 %shard_map.127 = (f32[256,256]{1,0:T(8,128)S(1)}, f32[256,256]{1,0:T(8,128)S(1)}, f32[256,256]{1,0:T(8,128)S(1)}, f32[256,256]{1,0:T(8,128)S(1)}, bf16[256,256]{1,0:T(8,128)(2,1)S(1)}) custom-call(f32[2,256,256]{2,1,0:T(8,128)S(1)} %shard_map.125.own, bf16[2,256,256]{2,1,0:T(8,128)(2,1)S(1)} %collective-permute-done.7.other, ...), custom_call_target="tpu_custom_call" | custom-call | flops 13107200 | bytes 2490368 | tf_op jit(solution)/shard_map/pallas_call | solution.py:270
  25.3 0.8 %collective-permute-start.12 = (bf16[256,256]{1,0:T(8,128)(2,1)S(1)}, bf16[256,256]{1,0:T(8,128)(2,1)S(1)}, u32[]{:S(2)}, u32[]{:S(2)}) collective-permute-start(bf16[256,256]{1,0:T(8,128)(2,1)S(1)} %get-tuple-element.39.refs_0_), channel_id=1, source_target_pairs={{0,2},{2,0},{4,6},{6,4},{8,10},{10,8},{12,14},{14,12},{1,3},{3,1},... | collective-permute-start | bytes 393224 | tf_op jit(solution)/shard_map/ppermute | solution.py:32
  26.1 2.6 %collective-permute-start.8 = (bf16[256,256]{1,0:T(8,128)(2,1)S(1)}, bf16[256,256]{1,0:T(8,128)(2,1)S(1)}, u32[]{:S(2)}, u32[]{:S(2)}) collective-permute-start(bf16[256,256]{1,0:T(8,128)(2,1)S(1)} %get-tuple-element.39.refs_0_), channel_id=1, source_target_pairs={{0,8},{2,10},{4,12},{6,14},{8,0},{10,2},{12,4},{14,6},{1,9},{3,11}... | collective-permute-start | bytes 393224 | tf_op jit(solution)/shard_map/ppermute | solution.py:32
  28.7 1.8 %collective-permute-start.13 = (bf16[256,256]{1,0:T(8,128)(2,1)S(1)}, bf16[256,256]{1,0:T(8,128)(2,1)S(1)}, u32[]{:S(2)}, u32[]{:S(2)}) collective-permute-start(bf16[256,256]{1,0:T(8,128)(2,1)S(1)} %get-tuple-element.39.refs_0_), channel_id=1, source_target_pairs={{0,4},{2,6},{4,0},{6,2},{8,12},{10,14},{12,8},{14,10},{1,5},{3,7},... | collective-permute-start | bytes 393224 | tf_op jit(solution)/shard_map/ppermute | solution.py:32
  30.5 0.4 collective-permute-done.12.refs_1_
  30.9 1.4 %collective-permute-start.14 = (bf16[256,256]{1,0:T(8,128)(2,1)S(1)}, bf16[256,256]{1,0:T(8,128)(2,1)S(1)}, u32[]{:S(2)}, u32[]{:S(2)}) collective-permute-start(bf16[256,256]{1,0:T(8,128)(2,1)S(1)} %collective-permute-done.12.refs_1_), channel_id=1, source_target_pairs={{0,4},{2,6},{4,0},{6,2},{8,12},{10,14},{12,8},{14,10},{1,5},{3,7},... | collective-permute-start | bytes 393224 | tf_op jit(solution)/shard_map/ppermute | solution.py:32
  32.3 2.8 %collective-permute-done.8.refs_2_ = bf16[256,256]{1,0:T(8,128)(2,1)S(1)} collective-permute-done((bf16[256,256]{1,0:T(8,128)(2,1)S(1)}, bf16[256,256]{1,0:T(8,128)(2,1)S(1)}, u32[]{:S(2)}, u32[]{:S(2)}) %collective-permute-start.8) | collective-permute-done | bytes 131104 | tf_op jit(solution)/shard_map/ppermute | solution.py:32
  35.1 0.7 %collective-permute-start.11 = (bf16[256,256]{1,0:T(8,128)(2,1)S(1)}, bf16[256,256]{1,0:T(8,128)(2,1)S(1)}, u32[]{:S(2)}, u32[]{:S(2)}) collective-permute-start(bf16[256,256]{1,0:T(8,128)(2,1)S(1)} %collective-permute-done.8.refs_2_), channel_id=1, source_target_pairs={{0,6},{2,4},{4,2},{6,0},{8,14},{10,12},{12,10},{14,8},{1,7},{3,5},... | collective-permute-start | bytes 393224 | tf_op jit(solution)/shard_map/ppermute | solution.py:32
  35.8 1.5 %collective-permute-start.10 = (bf16[256,256]{1,0:T(8,128)(2,1)S(1)}, bf16[256,256]{1,0:T(8,128)(2,1)S(1)}, u32[]{:S(2)}, u32[]{:S(2)}) collective-permute-start(bf16[256,256]{1,0:T(8,128)(2,1)S(1)} %collective-permute-done.8.refs_2_), channel_id=1, source_target_pairs={{0,2},{2,0},{4,6},{6,4},{8,10},{10,8},{12,14},{14,12},{1,3},{3,1},... | collective-permute-start | bytes 393224 | tf_op jit(solution)/shard_map/ppermute | solution.py:32
  37.3 1.4 %collective-permute-start.9 = (bf16[256,256]{1,0:T(8,128)(2,1)S(1)}, bf16[256,256]{1,0:T(8,128)(2,1)S(1)}, u32[]{:S(2)}, u32[]{:S(2)}) collective-permute-start(bf16[256,256]{1,0:T(8,128)(2,1)S(1)} %collective-permute-done.8.refs_2_), channel_id=1, source_target_pairs={{0,4},{2,6},{4,0},{6,2},{8,12},{10,14},{12,8},{14,10},{1,5},{3,7},... | collective-permute-start | bytes 393224 | tf_op jit(solution)/shard_map/ppermute | solution.py:32
  38.6 0.0 copy-done.2
  38.6 0.1 shard_map.128
  38.8 0.0 collective-permute-done.13.refs_3_
  38.8 0.0 collective-permute-done.14.refs_4_
  38.8 0.8 %shard_map.129.refs_3_ = f32[2,2,256,256]{3,2,1,0:T(8,128)S(1)} custom-call(s32[2,2]{1,0:T(2,128)S(1)} %copy-done.3, bf16[8,2,32,256]{3,2,1,0:T(8,128)(2,1)S(1)} %get-tuple-element.24.v_ref, bf16[2,512,384]{2,1,0:T(8,128)(2,1)S(1)} %get-tuple-element.25.u_ref, bf16[2,2,2,256,256]{4,3,2,1,0:T(8,128)(2,1)S(1)} %copy-done, ...), custom_call_target="tpu_custom_call" | custom-call | flops 125829120 | bytes 2752528 | tf_op jit(solution)/shard_map/pallas_call | solution.py:270
  39.6 2.8 %collective-permute-done.11.refs_2_ = bf16[256,256]{1,0:T(8,128)(2,1)S(1)} collective-permute-done((bf16[256,256]{1,0:T(8,128)(2,1)S(1)}, bf16[256,256]{1,0:T(8,128)(2,1)S(1)}, u32[]{:S(2)}, u32[]{:S(2)}) %collective-permute-start.11) | collective-permute-done | bytes 131104 | tf_op jit(solution)/shard_map/ppermute | solution.py:32
  42.5 1.0 %collective-permute-done.10.refs_1_ = bf16[256,256]{1,0:T(8,128)(2,1)S(1)} collective-permute-done((bf16[256,256]{1,0:T(8,128)(2,1)S(1)}, bf16[256,256]{1,0:T(8,128)(2,1)S(1)}, u32[]{:S(2)}, u32[]{:S(2)}) %collective-permute-start.10) | collective-permute-done | bytes 131104 | tf_op jit(solution)/shard_map/ppermute | solution.py:32
  43.5 0.2 collective-permute-done.9.refs_0_
  43.6 0.5 %shard_map.131 = bf16[2,256,256]{2,1,0:T(8,128)(2,1)S(1)} custom-call(s32[2,2]{1,0:T(2,128)S(1)} %copy-done.3, bf16[8,2,32,256]{3,2,1,0:T(8,128)(2,1)S(1)} %get-tuple-element.24.v_ref, bf16[2,512,384]{2,1,0:T(8,128)(2,1)S(1)} %get-tuple-element.25.u_ref, bf16[2,2,2,256,256]{4,3,2,1,0:T(8,128)(2,1)S(1)} %copy-done, ...), custom_call_target="tpu_custom_call" | custom-call | flops 37748736 | bytes 3538960 | tf_op jit(solution)/shard_map/pallas_call | solution.py:270
  44.2 0.1 collective-permute-start.15
  44.2 0.5 %shard_map.130.own = f32[2,256,256]{2,1,0:T(8,128)S(1)} custom-call(s32[2,2]{1,0:T(2,128)S(1)} %copy-done.3, bf16[8,2,32,256]{3,2,1,0:T(8,128)(2,1)S(1)} %get-tuple-element.24.v_ref, bf16[2,512,384]{2,1,0:T(8,128)(2,1)S(1)} %get-tuple-element.25.u_ref, bf16[2,2,2,256,256]{4,3,2,1,0:T(8,128)(2,1)S(1)} %copy-done, ...), custom_call_target="tpu_custom_call" | custom-call | flops 37748736 | bytes 3538960 | tf_op jit(solution)/shard_map/pallas_call | solution.py:270
  44.8 1.0 %collective-permute-done.15.other = bf16[2,256,256]{2,1,0:T(8,128)(2,1)S(1)} collective-permute-done((bf16[2,256,256]{2,1,0:T(8,128)(2,1)S(1)}, bf16[2,256,256]{2,1,0:T(8,128)(2,1)S(1)}, u32[]{:S(2)}, u32[]{:S(2)}) %collective-permute-start.15) | collective-permute-done | bytes 262176 | tf_op jit(solution)/shard_map/ppermute | solution.py:370
  45.8 1.8 %shard_map.132 = (f32[256,256]{1,0:T(8,128)}, f32[256,256]{1,0:T(8,128)}) custom-call(f32[2,256,256]{2,1,0:T(8,128)S(1)} %shard_map.130.own, bf16[2,256,256]{2,1,0:T(8,128)(2,1)S(1)} %collective-permute-done.15.other, f32[256,256]{1,0:T(8,128)S(1)} %get-tuple-element.40.weight, f32[256,256]{1,0:T(8,128)S(1)} %get-tuple-element.41.unweight, ...), custom_call_target="tpu_custom_call" | custom-call | flops 13107200 | bytes 3538944 | tf_op jit(solution)/shard_map/pallas_call | solution.py:270
  (3 shorter events, 0.0 us)
Async XLA Ops:
  0.6 18.2 %copy-start = (bf16[2,2,2,256,256]{4,3,2,1,0:T(8,128)(2,1)S(1)}, bf16[2,2,2,256,256]{4,3,2,1,0:T(8,128)(2,1)}, u32[]{:S(2)}) copy-start(bf16[2,2,2,256,256]{4,3,2,1,0:T(8,128)(2,1)} %d_ref.11) | copy-start | bytes 3145732
  1.7 7.2 %collective-permute-start.4 = (bf16[256,256]{1,0:T(8,128)(2,1)S(1)}, bf16[256,256]{1,0:T(8,128)(2,1)S(1)}, u32[]{:S(2)}, u32[]{:S(2)}) collective-permute-start(bf16[256,256]{1,0:T(8,128)(2,1)S(1)} %shard_map.123.refs_0_), channel_id=1, source_target_pairs={{0,2},{2,0},{4,6},{6,4},{8,10},{10,8},{12,14},{14,12},{1,3},{3,1},... | collective-permute-start | bytes 393224 | tf_op jit(solution)/shard_map/ppermute | solution.py:32
  4.7 8.8 %collective-permute-start = (bf16[256,256]{1,0:T(8,128)(2,1)S(1)}, bf16[256,256]{1,0:T(8,128)(2,1)S(1)}, u32[]{:S(2)}, u32[]{:S(2)}) collective-permute-start(bf16[256,256]{1,0:T(8,128)(2,1)S(1)} %shard_map.123.refs_0_), channel_id=1, source_target_pairs={{0,8},{2,10},{4,12},{6,14},{8,0},{10,2},{12,4},{14,6},{1,9},{3,11}... | collective-permute-start | bytes 393224 | tf_op jit(solution)/shard_map/ppermute | solution.py:32
  7.3 11.5 %collective-permute-start.5 = (bf16[256,256]{1,0:T(8,128)(2,1)S(1)}, bf16[256,256]{1,0:T(8,128)(2,1)S(1)}, u32[]{:S(2)}, u32[]{:S(2)}) collective-permute-start(bf16[256,256]{1,0:T(8,128)(2,1)S(1)} %shard_map.123.refs_0_), channel_id=1, source_target_pairs={{0,4},{2,6},{4,0},{6,2},{8,12},{10,14},{12,8},{14,10},{1,5},{3,7},... | collective-permute-start | bytes 393224 | tf_op jit(solution)/shard_map/ppermute | solution.py:32
  8.9 9.9 %collective-permute-start.6 = (bf16[256,256]{1,0:T(8,128)(2,1)S(1)}, bf16[256,256]{1,0:T(8,128)(2,1)S(1)}, u32[]{:S(2)}, u32[]{:S(2)}) collective-permute-start(bf16[256,256]{1,0:T(8,128)(2,1)S(1)} %collective-permute-done.4.refs_1_), channel_id=1, source_target_pairs={{0,4},{2,6},{4,0},{6,2},{8,12},{10,14},{12,8},{14,10},{1,5},{3,7},... | collective-permute-start | bytes 393224 | tf_op jit(solution)/shard_map/ppermute | solution.py:32
  13.5 7.1 %collective-permute-start.3 = (bf16[256,256]{1,0:T(8,128)(2,1)S(1)}, bf16[256,256]{1,0:T(8,128)(2,1)S(1)}, u32[]{:S(2)}, u32[]{:S(2)}) collective-permute-start(bf16[256,256]{1,0:T(8,128)(2,1)S(1)} %collective-permute-done.refs_2_), channel_id=1, source_target_pairs={{0,6},{2,4},{4,2},{6,0},{8,14},{10,12},{12,10},{14,8},{1,7},{3,5},... | collective-permute-start | bytes 393224 | tf_op jit(solution)/shard_map/ppermute | solution.py:32
  14.0 7.3 %collective-permute-start.2 = (bf16[256,256]{1,0:T(8,128)(2,1)S(1)}, bf16[256,256]{1,0:T(8,128)(2,1)S(1)}, u32[]{:S(2)}, u32[]{:S(2)}) collective-permute-start(bf16[256,256]{1,0:T(8,128)(2,1)S(1)} %collective-permute-done.refs_2_), channel_id=1, source_target_pairs={{0,2},{2,0},{4,6},{6,4},{8,10},{10,8},{12,14},{14,12},{1,3},{3,1},... | collective-permute-start | bytes 393224 | tf_op jit(solution)/shard_map/ppermute | solution.py:32
  15.6 6.5 %collective-permute-start.1 = (bf16[256,256]{1,0:T(8,128)(2,1)S(1)}, bf16[256,256]{1,0:T(8,128)(2,1)S(1)}, u32[]{:S(2)}, u32[]{:S(2)}) collective-permute-start(bf16[256,256]{1,0:T(8,128)(2,1)S(1)} %collective-permute-done.refs_2_), channel_id=1, source_target_pairs={{0,4},{2,6},{4,0},{6,2},{8,12},{10,14},{12,8},{14,10},{1,5},{3,7},... | collective-permute-start | bytes 393224 | tf_op jit(solution)/shard_map/ppermute | solution.py:32
  18.8 0.7 %copy-start.3 = (s32[2,2]{1,0:T(2,128)S(1)}, s32[2,2]{1,0:T(2,128)}, u32[]{:S(2)}) copy-start(s32[2,2]{1,0:T(2,128)} %near_ref.11) | copy-start | bytes 52
  22.6 1.6 %copy-start.1 = (f32[256,256]{1,0:T(8,128)S(1)}, f32[256,256]{1,0:T(8,128)}, u32[]{:S(2)}) copy-start(f32[256,256]{1,0:T(8,128)} %tau.3) | copy-start | bytes 786436
  22.6 1.6 %collective-permute-start.7 = (bf16[2,256,256]{2,1,0:T(8,128)(2,1)S(1)}, bf16[2,256,256]{2,1,0:T(8,128)(2,1)S(1)}, u32[]{:S(2)}, u32[]{:S(2)}) collective-permute-start(bf16[2,256,256]{2,1,0:T(8,128)(2,1)S(1)} %shard_map.126), channel_id=1, source_target_pairs={{0,1},{1,0},{2,3},{3,2},{4,5},{5,4},{6,7},{7,6},{8,9},{9,8},{10,11... | collective-permute-start | bytes 786440 | tf_op jit(solution)/shard_map/ppermute | solution.py:370
  24.3 14.4 %copy-start.2 = (f32[256,256]{1,0:T(8,128)S(1)}, f32[256,256]{1,0:T(8,128)}, u32[]{:S(2)}) copy-start(f32[256,256]{1,0:T(8,128)} %state.1) | copy-start | bytes 786436
  25.3 5.6 %collective-permute-start.12 = (bf16[256,256]{1,0:T(8,128)(2,1)S(1)}, bf16[256,256]{1,0:T(8,128)(2,1)S(1)}, u32[]{:S(2)}, u32[]{:S(2)}) collective-permute-start(bf16[256,256]{1,0:T(8,128)(2,1)S(1)} %get-tuple-element.39.refs_0_), channel_id=1, source_target_pairs={{0,2},{2,0},{4,6},{6,4},{8,10},{10,8},{12,14},{14,12},{1,3},{3,1},... | collective-permute-start | bytes 393224 | tf_op jit(solution)/shard_map/ppermute | solution.py:32
  26.1 9.1 %collective-permute-start.8 = (bf16[256,256]{1,0:T(8,128)(2,1)S(1)}, bf16[256,256]{1,0:T(8,128)(2,1)S(1)}, u32[]{:S(2)}, u32[]{:S(2)}) collective-permute-start(bf16[256,256]{1,0:T(8,128)(2,1)S(1)} %get-tuple-element.39.refs_0_), channel_id=1, source_target_pairs={{0,8},{2,10},{4,12},{6,14},{8,0},{10,2},{12,4},{14,6},{1,9},{3,11}... | collective-permute-start | bytes 393224 | tf_op jit(solution)/shard_map/ppermute | solution.py:32
  28.7 10.1 %collective-permute-start.13 = (bf16[256,256]{1,0:T(8,128)(2,1)S(1)}, bf16[256,256]{1,0:T(8,128)(2,1)S(1)}, u32[]{:S(2)}, u32[]{:S(2)}) collective-permute-start(bf16[256,256]{1,0:T(8,128)(2,1)S(1)} %get-tuple-element.39.refs_0_), channel_id=1, source_target_pairs={{0,4},{2,6},{4,0},{6,2},{8,12},{10,14},{12,8},{14,10},{1,5},{3,7},... | collective-permute-start | bytes 393224 | tf_op jit(solution)/shard_map/ppermute | solution.py:32
  30.9 7.9 %collective-permute-start.14 = (bf16[256,256]{1,0:T(8,128)(2,1)S(1)}, bf16[256,256]{1,0:T(8,128)(2,1)S(1)}, u32[]{:S(2)}, u32[]{:S(2)}) collective-permute-start(bf16[256,256]{1,0:T(8,128)(2,1)S(1)} %collective-permute-done.12.refs_1_), channel_id=1, source_target_pairs={{0,4},{2,6},{4,0},{6,2},{8,12},{10,14},{12,8},{14,10},{1,5},{3,7},... | collective-permute-start | bytes 393224 | tf_op jit(solution)/shard_map/ppermute | solution.py:32
  35.1 7.3 %collective-permute-start.11 = (bf16[256,256]{1,0:T(8,128)(2,1)S(1)}, bf16[256,256]{1,0:T(8,128)(2,1)S(1)}, u32[]{:S(2)}, u32[]{:S(2)}) collective-permute-start(bf16[256,256]{1,0:T(8,128)(2,1)S(1)} %collective-permute-done.8.refs_2_), channel_id=1, source_target_pairs={{0,6},{2,4},{4,2},{6,0},{8,14},{10,12},{12,10},{14,8},{1,7},{3,5},... | collective-permute-start | bytes 393224 | tf_op jit(solution)/shard_map/ppermute | solution.py:32
  35.8 7.7 %collective-permute-start.10 = (bf16[256,256]{1,0:T(8,128)(2,1)S(1)}, bf16[256,256]{1,0:T(8,128)(2,1)S(1)}, u32[]{:S(2)}, u32[]{:S(2)}) collective-permute-start(bf16[256,256]{1,0:T(8,128)(2,1)S(1)} %collective-permute-done.8.refs_2_), channel_id=1, source_target_pairs={{0,2},{2,0},{4,6},{6,4},{8,10},{10,8},{12,14},{14,12},{1,3},{3,1},... | collective-permute-start | bytes 393224 | tf_op jit(solution)/shard_map/ppermute | solution.py:32
  37.3 6.4 %collective-permute-start.9 = (bf16[256,256]{1,0:T(8,128)(2,1)S(1)}, bf16[256,256]{1,0:T(8,128)(2,1)S(1)}, u32[]{:S(2)}, u32[]{:S(2)}) collective-permute-start(bf16[256,256]{1,0:T(8,128)(2,1)S(1)} %collective-permute-done.8.refs_2_), channel_id=1, source_target_pairs={{0,4},{2,6},{4,0},{6,2},{8,12},{10,14},{12,8},{14,10},{1,5},{3,7},... | collective-permute-start | bytes 393224 | tf_op jit(solution)/shard_map/ppermute | solution.py:32
  44.2 1.6 %collective-permute-start.15 = (bf16[2,256,256]{2,1,0:T(8,128)(2,1)S(1)}, bf16[2,256,256]{2,1,0:T(8,128)(2,1)S(1)}, u32[]{:S(2)}, u32[]{:S(2)}) collective-permute-start(bf16[2,256,256]{2,1,0:T(8,128)(2,1)S(1)} %shard_map.131), channel_id=1, source_target_pairs={{0,1},{1,0},{2,3},{3,2},{4,5},{5,4},{6,7},{7,6},{8,9},{9,8},{10,11... | collective-permute-start | bytes 786440 | tf_op jit(solution)/shard_map/ppermute | solution.py:370

commit v17 on v14

--- a/solution.py
+++ b/solution.py
@@ -19,7 +19,7 @@
 def arrivals(count, direct):
     if not direct:
         return list(range(count))
-    return [0, 1, 4, 2, 3, 5, 6, 7] if count == 8 else [0, 1, 2, 3]
+    return [0, 4, 2, 1, 3, 6, 7, 5] if count == 8 else [0, 1, 2, 3]
 
 
 def row_met(spot, row, direct):

time: 47.2 us -> 48.7 us (1.032)
  waiting for transfers between devices: 15.8 us -> 17.3 us
    ppermute x14, waiting for transfers between devices: 13.9 us -> 15.4 us  [swapped(): lax.ppermute(data, 'row', [(row, row ^ mask) for row in range(count)])]
  transfers between devices with their start and end apart: 16 -> 16, of which waited for: 10 -> 8; matrix products, arithmetic and copies ran while one was open for 0% -> 0% of each run, Pallas kernels for 10% -> 10%
where the time goes in v17:
time: 48.7 us; the launch traced here: 48.5 us
  starting transfers between devices  20.2 us (41%)
  waiting for transfers between devices  17.3 us (36%)
  Pallas kernels  9.61 us (20%)
  between operations  0.78 us (2%)
  local copies, waits for them, and re-layouts  0.68 us (1%)
    ppermute x14, starting transfers between devices, swapped(): lax.ppermute(data, 'row', [(row, row ^ mask) for row in range(count)])  20 us
    ppermute x14, waiting for transfers between devices, swapped(): lax.ppermute(data, 'row', [(row, row ^ mask) for row in range(count)])  15.4 us
    pallas_call x11, Pallas kernels, on_core(): pl.pallas_call(kernel, out_shape=outs, in_specs=[hbm] * len(far) + [vmem]...  9.61 us
    ppermute x2, waiting for transfers between devices, lattice(): lax.ppermute(add(blocks[early:], early, 1, sums, narrow), 'col', swap)  1.89 us
  transfers between devices with their start and end apart: 16, of which 8 were waited for; matrix products, arithmetic and copies ran while one was open for 0% of the time, Pallas kernels for 10%

profile of v17, /device:TPU:0, one launch (start us, length us, event | category | flops | bytes accessed | tf_op | source)
XLA Modules:
  0.0 48.5 jit_solution(15253168896162787651)
XLA Ops:
  0.6 0.0 copy-start
  0.6 1.0 %shard_map.123.refs_0_ = bf16[256,256]{1,0:T(8,128)(2,1)S(1)} custom-call(f32[256,256]{1,0:T(8,128)} %wide_ref.1), custom_call_target="tpu_custom_call" | custom-call | bytes 262144 | tf_op jit(solution)/shard_map/pallas_call | solution.py:258
  1.7 4.1 %collective-permute-start.1 = (bf16[256,256]{1,0:T(8,128)(2,1)S(1)}, bf16[256,256]{1,0:T(8,128)(2,1)S(1)}, u32[]{:S(2)}, u32[]{:S(2)}) collective-permute-start(bf16[256,256]{1,0:T(8,128)(2,1)S(1)} %shard_map.123.refs_0_), channel_id=1, source_target_pairs={{0,8},{2,10},{4,12},{6,14},{8,0},{10,2},{12,4},{14,6},{1,9},{3,11}... | collective-permute-start | bytes 393224 | tf_op jit(solution)/shard_map/ppermute | solution.py:31
  5.8 1.5 %collective-permute-start.6 = (bf16[256,256]{1,0:T(8,128)(2,1)S(1)}, bf16[256,256]{1,0:T(8,128)(2,1)S(1)}, u32[]{:S(2)}, u32[]{:S(2)}) collective-permute-start(bf16[256,256]{1,0:T(8,128)(2,1)S(1)} %shard_map.123.refs_0_), channel_id=1, source_target_pairs={{0,2},{2,0},{4,6},{6,4},{8,10},{10,8},{12,14},{14,12},{1,3},{3,1},... | collective-permute-start | bytes 393224 | tf_op jit(solution)/shard_map/ppermute | solution.py:31
  7.3 1.6 %collective-permute-start.5 = (bf16[256,256]{1,0:T(8,128)(2,1)S(1)}, bf16[256,256]{1,0:T(8,128)(2,1)S(1)}, u32[]{:S(2)}, u32[]{:S(2)}) collective-permute-start(bf16[256,256]{1,0:T(8,128)(2,1)S(1)} %shard_map.123.refs_0_), channel_id=1, source_target_pairs={{0,4},{2,6},{4,0},{6,2},{8,12},{10,14},{12,8},{14,10},{1,5},{3,7},... | collective-permute-start | bytes 393224 | tf_op jit(solution)/shard_map/ppermute | solution.py:31
  8.9 0.4 collective-permute-start
  9.3 2.9 %collective-permute-done.1.refs_1_ = bf16[256,256]{1,0:T(8,128)(2,1)S(1)} collective-permute-done((bf16[256,256]{1,0:T(8,128)(2,1)S(1)}, bf16[256,256]{1,0:T(8,128)(2,1)S(1)}, u32[]{:S(2)}, u32[]{:S(2)}) %collective-permute-start.1) | collective-permute-done | bytes 131104 | tf_op jit(solution)/shard_map/ppermute | solution.py:31
  12.2 1.6 %collective-permute-start.4 = (bf16[256,256]{1,0:T(8,128)(2,1)S(1)}, bf16[256,256]{1,0:T(8,128)(2,1)S(1)}, u32[]{:S(2)}, u32[]{:S(2)}) collective-permute-start(bf16[256,256]{1,0:T(8,128)(2,1)S(1)} %collective-permute-done.1.refs_1_), channel_id=1, source_target_pairs={{0,2},{2,0},{4,6},{6,4},{8,10},{10,8},{12,14},{14,12},{1,3},{3,1},... | collective-permute-start | bytes 393224 | tf_op jit(solution)/shard_map/ppermute | solution.py:31
  13.8 0.6 %collective-permute-start.3 = (bf16[256,256]{1,0:T(8,128)(2,1)S(1)}, bf16[256,256]{1,0:T(8,128)(2,1)S(1)}, u32[]{:S(2)}, u32[]{:S(2)}) collective-permute-start(bf16[256,256]{1,0:T(8,128)(2,1)S(1)} %collective-permute-done.1.refs_1_), channel_id=1, source_target_pairs={{0,6},{2,4},{4,2},{6,0},{8,14},{10,12},{12,10},{14,8},{1,7},{3,5},... | collective-permute-start | bytes 393224 | tf_op jit(solution)/shard_map/ppermute | solution.py:31
  14.3 0.0 collective-permute-done.6.refs_3_
  14.3 1.4 %collective-permute-start.2 = (bf16[256,256]{1,0:T(8,128)(2,1)S(1)}, bf16[256,256]{1,0:T(8,128)(2,1)S(1)}, u32[]{:S(2)}, u32[]{:S(2)}) collective-permute-start(bf16[256,256]{1,0:T(8,128)(2,1)S(1)} %collective-permute-done.1.refs_1_), channel_id=1, source_target_pairs={{0,4},{2,6},{4,0},{6,2},{8,12},{10,14},{12,8},{14,10},{1,5},{3,7},... | collective-permute-start | bytes 393224 | tf_op jit(solution)/shard_map/ppermute | solution.py:31
  15.7 1.8 %shard_map.122 = (bf16[8,2,32,256]{3,2,1,0:T(8,128)(2,1)S(1)}, bf16[2,512,256]{2,1,0:T(8,128)(2,1)S(1)}, f32[5,256,128]{2,1,0:T(8,128)S(1)}, f32[256,256]{1,0:T(...) custom-call(s32[2,8]{1,0:T(2,128)} %refs_0_.1, bf16[2,8,32,256]{3,2,1,0:T(8,128)(2,1)} %refs_1_.1, ...), custom_call_target="tpu_custom_call" | custom-call | bytes 1051712 | tf_op jit(solution)/shard_map/pallas_call | solution.py:258
  17.4 0.0 collective-permute-done.5.refs_2_
  17.5 0.0 copy-start.3
  17.5 0.7 %copy-done.3 = s32[2,2]{1,0:T(2,128)S(1)} copy-done((s32[2,2]{1,0:T(2,128)S(1)}, s32[2,2]{1,0:T(2,128)}, u32[]{:S(2)}) %copy-start.3) | copy-done | bytes 40
  18.1 0.8 %shard_map.124.refs_4_ = f32[2,2,256,256]{3,2,1,0:T(8,128)S(1)} custom-call(s32[2,2]{1,0:T(2,128)S(1)} %copy-done.3, bf16[8,2,32,256]{3,2,1,0:T(8,128)(2,1)S(1)} %get-tuple-element.24.v_ref, bf16[2,512,256]{2,1,0:T(8,128)(2,1)S(1)} %get-tuple-element.25.u_ref, bf16[2,2,2,256,256]{4,3,2,1,0:T(8,128)(2,1)S(1)} %copy-done, ...), custom_call_target="tpu_custom_call" | custom-call | flops 100663296 | bytes 2359312 | tf_op jit(solution)/shard_map/pallas_call | solution.py:258
  18.9 0.0 collective-permute-done.refs_0_
  18.9 2.6 %collective-permute-done.4.refs_3_ = bf16[256,256]{1,0:T(8,128)(2,1)S(1)} collective-permute-done((bf16[256,256]{1,0:T(8,128)(2,1)S(1)}, bf16[256,256]{1,0:T(8,128)(2,1)S(1)}, u32[]{:S(2)}, u32[]{:S(2)}) %collective-permute-start.4) | collective-permute-done | bytes 131104 | tf_op jit(solution)/shard_map/ppermute | solution.py:31
  21.6 0.0 collective-permute-done.3.refs_2_
  21.6 0.5 %collective-permute-done.2.refs_1_ = bf16[256,256]{1,0:T(8,128)(2,1)S(1)} collective-permute-done((bf16[256,256]{1,0:T(8,128)(2,1)S(1)}, bf16[256,256]{1,0:T(8,128)(2,1)S(1)}, u32[]{:S(2)}, u32[]{:S(2)}) %collective-permute-start.2) | collective-permute-done | bytes 131104 | tf_op jit(solution)/shard_map/ppermute | solution.py:31
  22.1 0.6 %shard_map.126 = bf16[2,256,256]{2,1,0:T(8,128)(2,1)S(1)} custom-call(s32[2,2]{1,0:T(2,128)S(1)} %copy-done.3, bf16[8,2,32,256]{3,2,1,0:T(8,128)(2,1)S(1)} %get-tuple-element.24.v_ref, bf16[2,512,256]{2,1,0:T(8,128)(2,1)S(1)} %get-tuple-element.25.u_ref, bf16[2,2,2,256,256]{4,3,2,1,0:T(8,128)(2,1)S(1)} %copy-done, ...), custom_call_target="tpu_custom_call" | custom-call | flops 50331648 | bytes 3407888 | tf_op jit(solution)/shard_map/pallas_call | solution.py:258
  22.7 0.0 copy-start.1
  22.7 0.1 collective-permute-start.7
  22.8 0.6 %shard_map.125.own = f32[2,256,256]{2,1,0:T(8,128)S(1)} custom-call(s32[2,2]{1,0:T(2,128)S(1)} %copy-done.3, bf16[8,2,32,256]{3,2,1,0:T(8,128)(2,1)S(1)} %get-tuple-element.24.v_ref, bf16[2,512,256]{2,1,0:T(8,128)(2,1)S(1)} %get-tuple-element.25.u_ref, bf16[2,2,2,256,256]{4,3,2,1,0:T(8,128)(2,1)S(1)} %copy-done, ...), custom_call_target="tpu_custom_call" | custom-call | flops 50331648 | bytes 3407888 | tf_op jit(solution)/shard_map/pallas_call | solution.py:258
  23.3 0.9 %collective-permute-done.7.other = bf16[2,256,256]{2,1,0:T(8,128)(2,1)S(1)} collective-permute-done((bf16[2,256,256]{2,1,0:T(8,128)(2,1)S(1)}, bf16[2,256,256]{2,1,0:T(8,128)(2,1)S(1)}, u32[]{:S(2)}, u32[]{:S(2)}) %collective-permute-start.7) | collective-permute-done | bytes 262176 | tf_op jit(solution)/shard_map/ppermute | solution.py:354
  24.3 1.0 %shard_map.127 = (f32[256,256]{1,0:T(8,128)S(1)}, f32[256,256]{1,0:T(8,128)S(1)}, f32[256,256]{1,0:T(8,128)S(1)}, f32[256,256]{1,0:T(8,128)S(1)}, bf16[256,256]{1,0:T(8,128)(2,1)S(1)}) custom-call(f32[2,256,256]{2,1,0:T(8,128)S(1)} %shard_map.125.own, bf16[2,256,256]{2,1,0:T(8,128)(2,1)S(1)} %collective-permute-done.7.other, ...), custom_call_target="tpu_custom_call" | custom-call | flops 13107200 | bytes 2490368 | tf_op jit(solution)/shard_map/pallas_call | solution.py:258
  25.3 2.0 %collective-permute-start.9 = (bf16[256,256]{1,0:T(8,128)(2,1)S(1)}, bf16[256,256]{1,0:T(8,128)(2,1)S(1)}, u32[]{:S(2)}, u32[]{:S(2)}) collective-permute-start(bf16[256,256]{1,0:T(8,128)(2,1)S(1)} %get-tuple-element.39.refs_0_), channel_id=1, source_target_pairs={{0,8},{2,10},{4,12},{6,14},{8,0},{10,2},{12,4},{14,6},{1,9},{3,11}... | collective-permute-start | bytes 393224 | tf_op jit(solution)/shard_map/ppermute | solution.py:31
  27.3 0.7 %collective-permute-start.14 = (bf16[256,256]{1,0:T(8,128)(2,1)S(1)}, bf16[256,256]{1,0:T(8,128)(2,1)S(1)}, u32[]{:S(2)}, u32[]{:S(2)}) collective-permute-start(bf16[256,256]{1,0:T(8,128)(2,1)S(1)} %get-tuple-element.39.refs_0_), channel_id=1, source_target_pairs={{0,2},{2,0},{4,6},{6,4},{8,10},{10,8},{12,14},{14,12},{1,3},{3,1},... | collective-permute-start | bytes 393224 | tf_op jit(solution)/shard_map/ppermute | solution.py:31
  28.0 2.5 %collective-permute-start.13 = (bf16[256,256]{1,0:T(8,128)(2,1)S(1)}, bf16[256,256]{1,0:T(8,128)(2,1)S(1)}, u32[]{:S(2)}, u32[]{:S(2)}) collective-permute-start(bf16[256,256]{1,0:T(8,128)(2,1)S(1)} %get-tuple-element.39.refs_0_), channel_id=1, source_target_pairs={{0,4},{2,6},{4,0},{6,2},{8,12},{10,14},{12,8},{14,10},{1,5},{3,7},... | collective-permute-start | bytes 393224 | tf_op jit(solution)/shard_map/ppermute | solution.py:31
  30.5 0.3 collective-permute-start.8
  30.8 4.0 %collective-permute-done.9.refs_1_ = bf16[256,256]{1,0:T(8,128)(2,1)S(1)} collective-permute-done((bf16[256,256]{1,0:T(8,128)(2,1)S(1)}, bf16[256,256]{1,0:T(8,128)(2,1)S(1)}, u32[]{:S(2)}, u32[]{:S(2)}) %collective-permute-start.9) | collective-permute-done | bytes 131104 | tf_op jit(solution)/shard_map/ppermute | solution.py:31
  34.8 0.7 %collective-permute-start.12 = (bf16[256,256]{1,0:T(8,128)(2,1)S(1)}, bf16[256,256]{1,0:T(8,128)(2,1)S(1)}, u32[]{:S(2)}, u32[]{:S(2)}) collective-permute-start(bf16[256,256]{1,0:T(8,128)(2,1)S(1)} %collective-permute-done.9.refs_1_), channel_id=1, source_target_pairs={{0,2},{2,0},{4,6},{6,4},{8,10},{10,8},{12,14},{14,12},{1,3},{3,1},... | collective-permute-start | bytes 393224 | tf_op jit(solution)/shard_map/ppermute | solution.py:31
  35.5 0.7 %collective-permute-start.11 = (bf16[256,256]{1,0:T(8,128)(2,1)S(1)}, bf16[256,256]{1,0:T(8,128)(2,1)S(1)}, u32[]{:S(2)}, u32[]{:S(2)}) collective-permute-start(bf16[256,256]{1,0:T(8,128)(2,1)S(1)} %collective-permute-done.9.refs_1_), channel_id=1, source_target_pairs={{0,6},{2,4},{4,2},{6,0},{8,14},{10,12},{12,10},{14,8},{1,7},{3,5},... | collective-permute-start | bytes 393224 | tf_op jit(solution)/shard_map/ppermute | solution.py:31
  36.1 0.0 collective-permute-done.14.refs_3_
  36.1 2.1 %collective-permute-start.10 = (bf16[256,256]{1,0:T(8,128)(2,1)S(1)}, bf16[256,256]{1,0:T(8,128)(2,1)S(1)}, u32[]{:S(2)}, u32[]{:S(2)}) collective-permute-start(bf16[256,256]{1,0:T(8,128)(2,1)S(1)} %collective-permute-done.9.refs_1_), channel_id=1, source_target_pairs={{0,4},{2,6},{4,0},{6,2},{8,12},{10,14},{12,8},{14,10},{1,5},{3,7},... | collective-permute-start | bytes 393224 | tf_op jit(solution)/shard_map/ppermute | solution.py:31
  38.2 0.0 copy-done.2
  38.2 0.1 shard_map.128
  38.4 0.0 collective-permute-done.13.refs_2_
  38.4 0.8 %shard_map.129.refs_4_ = f32[2,2,256,256]{3,2,1,0:T(8,128)S(1)} custom-call(s32[2,2]{1,0:T(2,128)S(1)} %copy-done.3, bf16[8,2,32,256]{3,2,1,0:T(8,128)(2,1)S(1)} %get-tuple-element.24.v_ref, bf16[2,512,256]{2,1,0:T(8,128)(2,1)S(1)} %get-tuple-element.25.u_ref, bf16[2,2,2,256,256]{4,3,2,1,0:T(8,128)(2,1)S(1)} %copy-done, ...), custom_call_target="tpu_custom_call" | custom-call | flops 100663296 | bytes 2359312 | tf_op jit(solution)/shard_map/pallas_call | solution.py:258
  39.2 0.0 collective-permute-done.8.refs_0_
  39.2 4.5 %collective-permute-done.12.refs_3_ = bf16[256,256]{1,0:T(8,128)(2,1)S(1)} collective-permute-done((bf16[256,256]{1,0:T(8,128)(2,1)S(1)}, bf16[256,256]{1,0:T(8,128)(2,1)S(1)}, u32[]{:S(2)}, u32[]{:S(2)}) %collective-permute-start.12) | collective-permute-done | bytes 131104 | tf_op jit(solution)/shard_map/ppermute | solution.py:31
  43.7 0.0 collective-permute-done.11.refs_2_
  43.7 0.8 %collective-permute-done.10.refs_1_ = bf16[256,256]{1,0:T(8,128)(2,1)S(1)} collective-permute-done((bf16[256,256]{1,0:T(8,128)(2,1)S(1)}, bf16[256,256]{1,0:T(8,128)(2,1)S(1)}, u32[]{:S(2)}, u32[]{:S(2)}) %collective-permute-start.10) | collective-permute-done | bytes 131104 | tf_op jit(solution)/shard_map/ppermute | solution.py:31
  44.5 0.6 %shard_map.131 = bf16[2,256,256]{2,1,0:T(8,128)(2,1)S(1)} custom-call(s32[2,2]{1,0:T(2,128)S(1)} %copy-done.3, bf16[8,2,32,256]{3,2,1,0:T(8,128)(2,1)S(1)} %get-tuple-element.24.v_ref, bf16[2,512,256]{2,1,0:T(8,128)(2,1)S(1)} %get-tuple-element.25.u_ref, bf16[2,2,2,256,256]{4,3,2,1,0:T(8,128)(2,1)S(1)} %copy-done, ...), custom_call_target="tpu_custom_call" | custom-call | flops 50331648 | bytes 3407888 | tf_op jit(solution)/shard_map/pallas_call | solution.py:258
  45.1 0.1 collective-permute-start.15
  45.2 0.6 %shard_map.130.own = f32[2,256,256]{2,1,0:T(8,128)S(1)} custom-call(s32[2,2]{1,0:T(2,128)S(1)} %copy-done.3, bf16[8,2,32,256]{3,2,1,0:T(8,128)(2,1)S(1)} %get-tuple-element.24.v_ref, bf16[2,512,256]{2,1,0:T(8,128)(2,1)S(1)} %get-tuple-element.25.u_ref, bf16[2,2,2,256,256]{4,3,2,1,0:T(8,128)(2,1)S(1)} %copy-done, ...), custom_call_target="tpu_custom_call" | custom-call | flops 50331648 | bytes 3407888 | tf_op jit(solution)/shard_map/pallas_call | solution.py:258
  45.8 0.9 %collective-permute-done.15.other = bf16[2,256,256]{2,1,0:T(8,128)(2,1)S(1)} collective-permute-done((bf16[2,256,256]{2,1,0:T(8,128)(2,1)S(1)}, bf16[2,256,256]{2,1,0:T(8,128)(2,1)S(1)}, u32[]{:S(2)}, u32[]{:S(2)}) %collective-permute-start.15) | collective-permute-done | bytes 262176 | tf_op jit(solution)/shard_map/ppermute | solution.py:354
  46.7 1.8 %shard_map.132 = (f32[256,256]{1,0:T(8,128)}, f32[256,256]{1,0:T(8,128)}) custom-call(f32[2,256,256]{2,1,0:T(8,128)S(1)} %shard_map.130.own, bf16[2,256,256]{2,1,0:T(8,128)(2,1)S(1)} %collective-permute-done.15.other, f32[256,256]{1,0:T(8,128)S(1)} %get-tuple-element.40.weight, f32[256,256]{1,0:T(8,128)S(1)} %get-tuple-element.41.unweight, ...), custom_call_target="tpu_custom_call" | custom-call | flops 13107200 | bytes 3538944 | tf_op jit(solution)/shard_map/pallas_call | solution.py:258
  (3 shorter events, 0.0 us)
Async XLA Ops:
  0.6 16.8 %copy-start = (bf16[2,2,2,256,256]{4,3,2,1,0:T(8,128)(2,1)S(1)}, bf16[2,2,2,256,256]{4,3,2,1,0:T(8,128)(2,1)}, u32[]{:S(2)}) copy-start(bf16[2,2,2,256,256]{4,3,2,1,0:T(8,128)(2,1)} %d_ref.11) | copy-start | bytes 3145732
  1.7 10.5 %collective-permute-start.1 = (bf16[256,256]{1,0:T(8,128)(2,1)S(1)}, bf16[256,256]{1,0:T(8,128)(2,1)S(1)}, u32[]{:S(2)}, u32[]{:S(2)}) collective-permute-start(bf16[256,256]{1,0:T(8,128)(2,1)S(1)} %shard_map.123.refs_0_), channel_id=1, source_target_pairs={{0,8},{2,10},{4,12},{6,14},{8,0},{10,2},{12,4},{14,6},{1,9},{3,11}... | collective-permute-start | bytes 393224 | tf_op jit(solution)/shard_map/ppermute | solution.py:31
  5.8 8.5 %collective-permute-start.6 = (bf16[256,256]{1,0:T(8,128)(2,1)S(1)}, bf16[256,256]{1,0:T(8,128)(2,1)S(1)}, u32[]{:S(2)}, u32[]{:S(2)}) collective-permute-start(bf16[256,256]{1,0:T(8,128)(2,1)S(1)} %shard_map.123.refs_0_), channel_id=1, source_target_pairs={{0,2},{2,0},{4,6},{6,4},{8,10},{10,8},{12,14},{14,12},{1,3},{3,1},... | collective-permute-start | bytes 393224 | tf_op jit(solution)/shard_map/ppermute | solution.py:31
  7.3 10.1 %collective-permute-start.5 = (bf16[256,256]{1,0:T(8,128)(2,1)S(1)}, bf16[256,256]{1,0:T(8,128)(2,1)S(1)}, u32[]{:S(2)}, u32[]{:S(2)}) collective-permute-start(bf16[256,256]{1,0:T(8,128)(2,1)S(1)} %shard_map.123.refs_0_), channel_id=1, source_target_pairs={{0,4},{2,6},{4,0},{6,2},{8,12},{10,14},{12,8},{14,10},{1,5},{3,7},... | collective-permute-start | bytes 393224 | tf_op jit(solution)/shard_map/ppermute | solution.py:31
  8.9 10.1 %collective-permute-start = (bf16[256,256]{1,0:T(8,128)(2,1)S(1)}, bf16[256,256]{1,0:T(8,128)(2,1)S(1)}, u32[]{:S(2)}, u32[]{:S(2)}) collective-permute-start(bf16[256,256]{1,0:T(8,128)(2,1)S(1)} %shard_map.123.refs_0_), channel_id=1, source_target_pairs={{0,6},{2,4},{4,2},{6,0},{8,14},{10,12},{12,10},{14,8},{1,7},{3,5},... | collective-permute-start | bytes 393224 | tf_op jit(solution)/shard_map/ppermute | solution.py:31
  12.2 9.4 %collective-permute-start.4 = (bf16[256,256]{1,0:T(8,128)(2,1)S(1)}, bf16[256,256]{1,0:T(8,128)(2,1)S(1)}, u32[]{:S(2)}, u32[]{:S(2)}) collective-permute-start(bf16[256,256]{1,0:T(8,128)(2,1)S(1)} %collective-permute-done.1.refs_1_), channel_id=1, source_target_pairs={{0,2},{2,0},{4,6},{6,4},{8,10},{10,8},{12,14},{14,12},{1,3},{3,1},... | collective-permute-start | bytes 393224 | tf_op jit(solution)/shard_map/ppermute | solution.py:31
  13.8 7.8 %collective-permute-start.3 = (bf16[256,256]{1,0:T(8,128)(2,1)S(1)}, bf16[256,256]{1,0:T(8,128)(2,1)S(1)}, u32[]{:S(2)}, u32[]{:S(2)}) collective-permute-start(bf16[256,256]{1,0:T(8,128)(2,1)S(1)} %collective-permute-done.1.refs_1_), channel_id=1, source_target_pairs={{0,6},{2,4},{4,2},{6,0},{8,14},{10,12},{12,10},{14,8},{1,7},{3,5},... | collective-permute-start | bytes 393224 | tf_op jit(solution)/shard_map/ppermute | solution.py:31
  14.3 7.8 %collective-permute-start.2 = (bf16[256,256]{1,0:T(8,128)(2,1)S(1)}, bf16[256,256]{1,0:T(8,128)(2,1)S(1)}, u32[]{:S(2)}, u32[]{:S(2)}) collective-permute-start(bf16[256,256]{1,0:T(8,128)(2,1)S(1)} %collective-permute-done.1.refs_1_), channel_id=1, source_target_pairs={{0,4},{2,6},{4,0},{6,2},{8,12},{10,14},{12,8},{14,10},{1,5},{3,7},... | collective-permute-start | bytes 393224 | tf_op jit(solution)/shard_map/ppermute | solution.py:31
  17.5 0.7 %copy-start.3 = (s32[2,2]{1,0:T(2,128)S(1)}, s32[2,2]{1,0:T(2,128)}, u32[]{:S(2)}) copy-start(s32[2,2]{1,0:T(2,128)} %near_ref.11) | copy-start | bytes 52
  22.7 1.6 %copy-start.1 = (f32[256,256]{1,0:T(8,128)S(1)}, f32[256,256]{1,0:T(8,128)}, u32[]{:S(2)}) copy-start(f32[256,256]{1,0:T(8,128)} %tau.3) | copy-start | bytes 786436
  22.7 1.6 %collective-permute-start.7 = (bf16[2,256,256]{2,1,0:T(8,128)(2,1)S(1)}, bf16[2,256,256]{2,1,0:T(8,128)(2,1)S(1)}, u32[]{:S(2)}, u32[]{:S(2)}) collective-permute-start(bf16[2,256,256]{2,1,0:T(8,128)(2,1)S(1)} %shard_map.126), channel_id=1, source_target_pairs={{0,1},{1,0},{2,3},{3,2},{4,5},{5,4},{6,7},{7,6},{8,9},{9,8},{10,11... | collective-permute-start | bytes 786440 | tf_op jit(solution)/shard_map/ppermute | solution.py:354
  24.3 14.0 %copy-start.2 = (f32[256,256]{1,0:T(8,128)S(1)}, f32[256,256]{1,0:T(8,128)}, u32[]{:S(2)}) copy-start(f32[256,256]{1,0:T(8,128)} %state.1) | copy-start | bytes 786436
  25.3 9.4 %collective-permute-start.9 = (bf16[256,256]{1,0:T(8,128)(2,1)S(1)}, bf16[256,256]{1,0:T(8,128)(2,1)S(1)}, u32[]{:S(2)}, u32[]{:S(2)}) collective-permute-start(bf16[256,256]{1,0:T(8,128)(2,1)S(1)} %get-tuple-element.39.refs_0_), channel_id=1, source_target_pairs={{0,8},{2,10},{4,12},{6,14},{8,0},{10,2},{12,4},{14,6},{1,9},{3,11}... | collective-permute-start | bytes 393224 | tf_op jit(solution)/shard_map/ppermute | solution.py:31
  27.3 8.8 %collective-permute-start.14 = (bf16[256,256]{1,0:T(8,128)(2,1)S(1)}, bf16[256,256]{1,0:T(8,128)(2,1)S(1)}, u32[]{:S(2)}, u32[]{:S(2)}) collective-permute-start(bf16[256,256]{1,0:T(8,128)(2,1)S(1)} %get-tuple-element.39.refs_0_), channel_id=1, source_target_pairs={{0,2},{2,0},{4,6},{6,4},{8,10},{10,8},{12,14},{14,12},{1,3},{3,1},... | collective-permute-start | bytes 393224 | tf_op jit(solution)/shard_map/ppermute | solution.py:31
  28.0 10.4 %collective-permute-start.13 = (bf16[256,256]{1,0:T(8,128)(2,1)S(1)}, bf16[256,256]{1,0:T(8,128)(2,1)S(1)}, u32[]{:S(2)}, u32[]{:S(2)}) collective-permute-start(bf16[256,256]{1,0:T(8,128)(2,1)S(1)} %get-tuple-element.39.refs_0_), channel_id=1, source_target_pairs={{0,4},{2,6},{4,0},{6,2},{8,12},{10,14},{12,8},{14,10},{1,5},{3,7},... | collective-permute-start | bytes 393224 | tf_op jit(solution)/shard_map/ppermute | solution.py:31
  30.5 8.7 %collective-permute-start.8 = (bf16[256,256]{1,0:T(8,128)(2,1)S(1)}, bf16[256,256]{1,0:T(8,128)(2,1)S(1)}, u32[]{:S(2)}, u32[]{:S(2)}) collective-permute-start(bf16[256,256]{1,0:T(8,128)(2,1)S(1)} %get-tuple-element.39.refs_0_), channel_id=1, source_target_pairs={{0,6},{2,4},{4,2},{6,0},{8,14},{10,12},{12,10},{14,8},{1,7},{3,5},... | collective-permute-start | bytes 393224 | tf_op jit(solution)/shard_map/ppermute | solution.py:31
  34.8 9.0 %collective-permute-start.12 = (bf16[256,256]{1,0:T(8,128)(2,1)S(1)}, bf16[256,256]{1,0:T(8,128)(2,1)S(1)}, u32[]{:S(2)}, u32[]{:S(2)}) collective-permute-start(bf16[256,256]{1,0:T(8,128)(2,1)S(1)} %collective-permute-done.9.refs_1_), channel_id=1, source_target_pairs={{0,2},{2,0},{4,6},{6,4},{8,10},{10,8},{12,14},{14,12},{1,3},{3,1},... | collective-permute-start | bytes 393224 | tf_op jit(solution)/shard_map/ppermute | solution.py:31
  35.5 8.2 %collective-permute-start.11 = (bf16[256,256]{1,0:T(8,128)(2,1)S(1)}, bf16[256,256]{1,0:T(8,128)(2,1)S(1)}, u32[]{:S(2)}, u32[]{:S(2)}) collective-permute-start(bf16[256,256]{1,0:T(8,128)(2,1)S(1)} %collective-permute-done.9.refs_1_), channel_id=1, source_target_pairs={{0,6},{2,4},{4,2},{6,0},{8,14},{10,12},{12,10},{14,8},{1,7},{3,5},... | collective-permute-start | bytes 393224 | tf_op jit(solution)/shard_map/ppermute | solution.py:31
  36.1 8.4 %collective-permute-start.10 = (bf16[256,256]{1,0:T(8,128)(2,1)S(1)}, bf16[256,256]{1,0:T(8,128)(2,1)S(1)}, u32[]{:S(2)}, u32[]{:S(2)}) collective-permute-start(bf16[256,256]{1,0:T(8,128)(2,1)S(1)} %collective-permute-done.9.refs_1_), channel_id=1, source_target_pairs={{0,4},{2,6},{4,0},{6,2},{8,12},{10,14},{12,8},{14,10},{1,5},{3,7},... | collective-permute-start | bytes 393224 | tf_op jit(solution)/shard_map/ppermute | solution.py:31
  45.1 1.6 %collective-permute-start.15 = (bf16[2,256,256]{2,1,0:T(8,128)(2,1)S(1)}, bf16[2,256,256]{2,1,0:T(8,128)(2,1)S(1)}, u32[]{:S(2)}, u32[]{:S(2)}) collective-permute-start(bf16[2,256,256]{2,1,0:T(8,128)(2,1)S(1)} %shard_map.131), channel_id=1, source_target_pairs={{0,1},{1,0},{2,3},{3,2},{4,5},{5,4},{6,7},{7,6},{8,9},{9,8},{10,11... | collective-permute-start | bytes 786440 | tf_op jit(solution)/shard_map/ppermute | solution.py:354

commit v18 on v17

--- a/solution.py
+++ b/solution.py
@@ -19,7 +19,7 @@
 def arrivals(count, direct):
     if not direct:
         return list(range(count))
-    return [0, 4, 2, 1, 3, 6, 7, 5] if count == 8 else [0, 1, 2, 3]
+    return [0, 1, 4, 2, 7, 6, 3, 5] if count == 8 else [0, 1, 2, 3]
 
 
 def row_met(spot, row, direct):
@@ -31,11 +31,12 @@
         return lax.ppermute(data, "row", [(row, row ^ mask) for row in range(count)])
 
     found = {0: block}
-    for mask in (4, 1, 2, 3) if count == 8 else (1, 2, 3):
+    for mask in (4, 2, 1, 7) if count == 8 else (2, 1):
         found[mask] = swapped(mask, block)
     if count == 8:
-        for mask in (1, 2, 3):
+        for mask in (1, 2):
             found[4 + mask] = swapped(mask, found[4])
+    found[3] = swapped(1, found[2])
     return [found[mask] for mask in arrivals(count, True)]
 
 

time: 48.7 us -> 49.8 us (1.023)
  waiting for transfers between devices: 17.3 us -> 21 us
  starting transfers between devices: 20.2 us -> 17.6 us
    ppermute x14, waiting for transfers between devices: 15.4 us -> 19.1 us  [swapped(): lax.ppermute(data, 'row', [(row, row ^ mask) for row in range(count)])]
    ppermute x14, starting transfers between devices: 20 us -> 17.5 us  [swapped(): lax.ppermute(data, 'row', [(row, row ^ mask) for row in range(count)])]
  transfers between devices with their start and end apart: 16 -> 16, of which waited for: 8 -> 11; matrix products, arithmetic and copies ran while one was open for 0% -> 0% of each run, Pallas kernels for 10% -> 9%
where the time goes in v18:
time: 49.8 us; the launch traced here: 49.6 us
  waiting for transfers between devices  21 us (42%)
  starting transfers between devices  17.6 us (35%)
  Pallas kernels  9.58 us (19%)
  between operations  0.79 us (2%)
  local copies, waits for them, and re-layouts  0.68 us (1%)
    ppermute x14, waiting for transfers between devices, swapped(): lax.ppermute(data, 'row', [(row, row ^ mask) for row in range(count)])  19.1 us
    ppermute x14, starting transfers between devices, swapped(): lax.ppermute(data, 'row', [(row, row ^ mask) for row in range(count)])  17.5 us
    pallas_call x11, Pallas kernels, on_core(): pl.pallas_call(kernel, out_shape=outs, in_specs=[hbm] * len(far) + [vmem]...  9.58 us
    ppermute x2, waiting for transfers between devices, lattice(): lax.ppermute(add(blocks[early:], early, 1, sums, narrow), 'col', swap)  1.89 us
  transfers between devices with their start and end apart: 16, of which 11 were waited for; matrix products, arithmetic and copies ran while one was open for 0% of the time, Pallas kernels for 9%

profile of v18, /device:TPU:0, one launch (start us, length us, event | category | flops | bytes accessed | tf_op | source)
XLA Modules:
  0.0 49.6 jit_solution(5922589408328852520)
XLA Ops:
  0.6 0.0 copy-start
  0.6 1.0 %shard_map.123.refs_0_ = bf16[256,256]{1,0:T(8,128)(2,1)S(1)} custom-call(f32[256,256]{1,0:T(8,128)} %wide_ref.1), custom_call_target="tpu_custom_call" | custom-call | bytes 262144 | tf_op jit(solution)/shard_map/pallas_call | solution.py:259
  1.7 3.1 %collective-permute-start.3 = (bf16[256,256]{1,0:T(8,128)(2,1)S(1)}, bf16[256,256]{1,0:T(8,128)(2,1)S(1)}, u32[]{:S(2)}, u32[]{:S(2)}) collective-permute-start(bf16[256,256]{1,0:T(8,128)(2,1)S(1)} %shard_map.123.refs_0_), channel_id=1, source_target_pairs={{0,4},{2,6},{4,0},{6,2},{8,12},{10,14},{12,8},{14,10},{1,5},{3,7},... | collective-permute-start | bytes 393224 | tf_op jit(solution)/shard_map/ppermute | solution.py:31
  4.8 2.6 %collective-permute-start.1 = (bf16[256,256]{1,0:T(8,128)(2,1)S(1)}, bf16[256,256]{1,0:T(8,128)(2,1)S(1)}, u32[]{:S(2)}, u32[]{:S(2)}) collective-permute-start(bf16[256,256]{1,0:T(8,128)(2,1)S(1)} %shard_map.123.refs_0_), channel_id=1, source_target_pairs={{0,8},{2,10},{4,12},{6,14},{8,0},{10,2},{12,4},{14,6},{1,9},{3,11}... | collective-permute-start | bytes 393224 | tf_op jit(solution)/shard_map/ppermute | solution.py:31
  7.4 1.5 %collective-permute-start.6 = (bf16[256,256]{1,0:T(8,128)(2,1)S(1)}, bf16[256,256]{1,0:T(8,128)(2,1)S(1)}, u32[]{:S(2)}, u32[]{:S(2)}) collective-permute-start(bf16[256,256]{1,0:T(8,128)(2,1)S(1)} %shard_map.123.refs_0_), channel_id=1, source_target_pairs={{0,2},{2,0},{4,6},{6,4},{8,10},{10,8},{12,14},{14,12},{1,3},{3,1},... | collective-permute-start | bytes 393224 | tf_op jit(solution)/shard_map/ppermute | solution.py:31
  8.9 0.0 collective-permute-start
  8.9 1.2 %collective-permute-done.3.refs_3_ = bf16[256,256]{1,0:T(8,128)(2,1)S(1)} collective-permute-done((bf16[256,256]{1,0:T(8,128)(2,1)S(1)}, bf16[256,256]{1,0:T(8,128)(2,1)S(1)}, u32[]{:S(2)}, u32[]{:S(2)}) %collective-permute-start.3) | collective-permute-done | bytes 131104 | tf_op jit(solution)/shard_map/ppermute | solution.py:31
  10.1 1.8 %collective-permute-start.4 = (bf16[256,256]{1,0:T(8,128)(2,1)S(1)}, bf16[256,256]{1,0:T(8,128)(2,1)S(1)}, u32[]{:S(2)}, u32[]{:S(2)}) collective-permute-start(bf16[256,256]{1,0:T(8,128)(2,1)S(1)} %collective-permute-done.3.refs_3_), channel_id=1, source_target_pairs={{0,2},{2,0},{4,6},{6,4},{8,10},{10,8},{12,14},{14,12},{1,3},{3,1},... | collective-permute-start | bytes 393224 | tf_op jit(solution)/shard_map/ppermute | solution.py:31
  11.9 5.2 %collective-permute-done.1.refs_2_ = bf16[256,256]{1,0:T(8,128)(2,1)S(1)} collective-permute-done((bf16[256,256]{1,0:T(8,128)(2,1)S(1)}, bf16[256,256]{1,0:T(8,128)(2,1)S(1)}, u32[]{:S(2)}, u32[]{:S(2)}) %collective-permute-start.1) | collective-permute-done | bytes 131104 | tf_op jit(solution)/shard_map/ppermute | solution.py:31
  17.2 1.6 %collective-permute-start.5 = (bf16[256,256]{1,0:T(8,128)(2,1)S(1)}, bf16[256,256]{1,0:T(8,128)(2,1)S(1)}, u32[]{:S(2)}, u32[]{:S(2)}) collective-permute-start(bf16[256,256]{1,0:T(8,128)(2,1)S(1)} %collective-permute-done.1.refs_2_), channel_id=1, source_target_pairs={{0,2},{2,0},{4,6},{6,4},{8,10},{10,8},{12,14},{14,12},{1,3},{3,1},... | collective-permute-start | bytes 393224 | tf_op jit(solution)/shard_map/ppermute | solution.py:31
  18.7 0.0 collective-permute-start.2
  18.7 1.8 %shard_map.122 = (bf16[8,2,32,256]{3,2,1,0:T(8,128)(2,1)S(1)}, bf16[2,512,256]{2,1,0:T(8,128)(2,1)S(1)}, f32[5,256,128]{2,1,0:T(8,128)S(1)}, f32[256,256]{1,0:T(...) custom-call(s32[2,8]{1,0:T(2,128)} %refs_0_.1, bf16[2,8,32,256]{3,2,1,0:T(8,128)(2,1)} %refs_1_.1, ...), custom_call_target="tpu_custom_call" | custom-call | bytes 1051712 | tf_op jit(solution)/shard_map/pallas_call | solution.py:259
  20.5 0.0 collective-permute-done.6.refs_1_
  20.5 0.0 copy-start.3
  20.5 0.7 %copy-done.3 = s32[2,2]{1,0:T(2,128)S(1)} copy-done((s32[2,2]{1,0:T(2,128)S(1)}, s32[2,2]{1,0:T(2,128)}, u32[]{:S(2)}) %copy-start.3) | copy-done | bytes 40
  21.2 0.8 %shard_map.124.refs_4_ = f32[2,2,256,256]{3,2,1,0:T(8,128)S(1)} custom-call(s32[2,2]{1,0:T(2,128)S(1)} %copy-done.3, bf16[8,2,32,256]{3,2,1,0:T(8,128)(2,1)S(1)} %get-tuple-element.24.v_ref, bf16[2,512,256]{2,1,0:T(8,128)(2,1)S(1)} %get-tuple-element.25.u_ref, bf16[2,2,2,256,256]{4,3,2,1,0:T(8,128)(2,1)S(1)} %copy-done, ...), custom_call_target="tpu_custom_call" | custom-call | flops 100663296 | bytes 2359312 | tf_op jit(solution)/shard_map/pallas_call | solution.py:259
  22.0 0.0 collective-permute-done.refs_0_
  22.0 0.0 collective-permute-done.4.refs_2_
  22.0 0.1 collective-permute-done.5.refs_3_
  22.1 1.6 %collective-permute-done.2.refs_1_ = bf16[256,256]{1,0:T(8,128)(2,1)S(1)} collective-permute-done((bf16[256,256]{1,0:T(8,128)(2,1)S(1)}, bf16[256,256]{1,0:T(8,128)(2,1)S(1)}, u32[]{:S(2)}, u32[]{:S(2)}) %collective-permute-start.2) | collective-permute-done | bytes 131104 | tf_op jit(solution)/shard_map/ppermute | solution.py:31
  23.7 0.6 %shard_map.126 = bf16[2,256,256]{2,1,0:T(8,128)(2,1)S(1)} custom-call(s32[2,2]{1,0:T(2,128)S(1)} %copy-done.3, bf16[8,2,32,256]{3,2,1,0:T(8,128)(2,1)S(1)} %get-tuple-element.24.v_ref, bf16[2,512,256]{2,1,0:T(8,128)(2,1)S(1)} %get-tuple-element.25.u_ref, bf16[2,2,2,256,256]{4,3,2,1,0:T(8,128)(2,1)S(1)} %copy-done, ...), custom_call_target="tpu_custom_call" | custom-call | flops 50331648 | bytes 3407888 | tf_op jit(solution)/shard_map/pallas_call | solution.py:259
  24.2 0.0 copy-start.1
  24.3 0.1 collective-permute-start.7
  24.3 0.6 %shard_map.125.own = f32[2,256,256]{2,1,0:T(8,128)S(1)} custom-call(s32[2,2]{1,0:T(2,128)S(1)} %copy-done.3, bf16[8,2,32,256]{3,2,1,0:T(8,128)(2,1)S(1)} %get-tuple-element.24.v_ref, bf16[2,512,256]{2,1,0:T(8,128)(2,1)S(1)} %get-tuple-element.25.u_ref, bf16[2,2,2,256,256]{4,3,2,1,0:T(8,128)(2,1)S(1)} %copy-done, ...), custom_call_target="tpu_custom_call" | custom-call | flops 50331648 | bytes 3407888 | tf_op jit(solution)/shard_map/pallas_call | solution.py:259
  24.9 1.0 %collective-permute-done.7.other = bf16[2,256,256]{2,1,0:T(8,128)(2,1)S(1)} collective-permute-done((bf16[2,256,256]{2,1,0:T(8,128)(2,1)S(1)}, bf16[2,256,256]{2,1,0:T(8,128)(2,1)S(1)}, u32[]{:S(2)}, u32[]{:S(2)}) %collective-permute-start.7) | collective-permute-done | bytes 262176 | tf_op jit(solution)/shard_map/ppermute | solution.py:355
  25.9 0.0 copy-done.1
  25.9 1.0 %shard_map.127 = (f32[256,256]{1,0:T(8,128)S(1)}, f32[256,256]{1,0:T(8,128)S(1)}, f32[256,256]{1,0:T(8,128)S(1)}, f32[256,256]{1,0:T(8,128)S(1)}, bf16[256,256]{1,0:T(8,128)(2,1)S(1)}) custom-call(f32[2,256,256]{2,1,0:T(8,128)S(1)} %shard_map.125.own, bf16[2,256,256]{2,1,0:T(8,128)(2,1)S(1)} %collective-permute-done.7.other, ...), custom_call_target="tpu_custom_call" | custom-call | flops 13107200 | bytes 2490368 | tf_op jit(solution)/shard_map/pallas_call | solution.py:259
  26.9 0.4 collective-permute-start.11
  27.3 3.0 %collective-permute-start.9 = (bf16[256,256]{1,0:T(8,128)(2,1)S(1)}, bf16[256,256]{1,0:T(8,128)(2,1)S(1)}, u32[]{:S(2)}, u32[]{:S(2)}) collective-permute-start(bf16[256,256]{1,0:T(8,128)(2,1)S(1)} %get-tuple-element.39.refs_0_), channel_id=1, source_target_pairs={{0,8},{2,10},{4,12},{6,14},{8,0},{10,2},{12,4},{14,6},{1,9},{3,11}... | collective-permute-start | bytes 393224 | tf_op jit(solution)/shard_map/ppermute | solution.py:31
  30.3 0.5 %collective-permute-start.14 = (bf16[256,256]{1,0:T(8,128)(2,1)S(1)}, bf16[256,256]{1,0:T(8,128)(2,1)S(1)}, u32[]{:S(2)}, u32[]{:S(2)}) collective-permute-start(bf16[256,256]{1,0:T(8,128)(2,1)S(1)} %get-tuple-element.39.refs_0_), channel_id=1, source_target_pairs={{0,2},{2,0},{4,6},{6,4},{8,10},{10,8},{12,14},{14,12},{1,3},{3,1},... | collective-permute-start | bytes 393224 | tf_op jit(solution)/shard_map/ppermute | solution.py:31
  30.9 2.0 %collective-permute-start.8 = (bf16[256,256]{1,0:T(8,128)(2,1)S(1)}, bf16[256,256]{1,0:T(8,128)(2,1)S(1)}, u32[]{:S(2)}, u32[]{:S(2)}) collective-permute-start(bf16[256,256]{1,0:T(8,128)(2,1)S(1)} %get-tuple-element.39.refs_0_), channel_id=1, source_target_pairs={{0,14},{2,12},{4,10},{6,8},{8,6},{10,4},{12,2},{14,0},{1,15},{3,13... | collective-permute-start | bytes 393224 | tf_op jit(solution)/shard_map/ppermute | solution.py:31
  32.8 2.1 %collective-permute-done.11.refs_3_ = bf16[256,256]{1,0:T(8,128)(2,1)S(1)} collective-permute-done((bf16[256,256]{1,0:T(8,128)(2,1)S(1)}, bf16[256,256]{1,0:T(8,128)(2,1)S(1)}, u32[]{:S(2)}, u32[]{:S(2)}) %collective-permute-start.11) | collective-permute-done | bytes 131104 | tf_op jit(solution)/shard_map/ppermute | solution.py:31
  34.9 0.5 collective-permute-start.12
  35.4 4.8 %collective-permute-done.9.refs_2_ = bf16[256,256]{1,0:T(8,128)(2,1)S(1)} collective-permute-done((bf16[256,256]{1,0:T(8,128)(2,1)S(1)}, bf16[256,256]{1,0:T(8,128)(2,1)S(1)}, u32[]{:S(2)}, u32[]{:S(2)}) %collective-permute-start.9) | collective-permute-done | bytes 131104 | tf_op jit(solution)/shard_map/ppermute | solution.py:31
  40.2 0.5 %collective-permute-start.13 = (bf16[256,256]{1,0:T(8,128)(2,1)S(1)}, bf16[256,256]{1,0:T(8,128)(2,1)S(1)}, u32[]{:S(2)}, u32[]{:S(2)}) collective-permute-start(bf16[256,256]{1,0:T(8,128)(2,1)S(1)} %collective-permute-done.9.refs_2_), channel_id=1, source_target_pairs={{0,2},{2,0},{4,6},{6,4},{8,10},{10,8},{12,14},{14,12},{1,3},{3,1},... | collective-permute-start | bytes 393224 | tf_op jit(solution)/shard_map/ppermute | solution.py:31
  40.7 0.0 collective-permute-start.10
  40.7 0.1 shard_map.128
  40.9 0.0 collective-permute-done.14.refs_1_
  40.9 0.8 %shard_map.129.refs_4_ = f32[2,2,256,256]{3,2,1,0:T(8,128)S(1)} custom-call(s32[2,2]{1,0:T(2,128)S(1)} %copy-done.3, bf16[8,2,32,256]{3,2,1,0:T(8,128)(2,1)S(1)} %get-tuple-element.24.v_ref, bf16[2,512,256]{2,1,0:T(8,128)(2,1)S(1)} %get-tuple-element.25.u_ref, bf16[2,2,2,256,256]{4,3,2,1,0:T(8,128)(2,1)S(1)} %copy-done, ...), custom_call_target="tpu_custom_call" | custom-call | flops 100663296 | bytes 2359312 | tf_op jit(solution)/shard_map/pallas_call | solution.py:259
  41.7 0.0 collective-permute-done.8.refs_0_
  41.7 0.6 %collective-permute-done.12.refs_2_ = bf16[256,256]{1,0:T(8,128)(2,1)S(1)} collective-permute-done((bf16[256,256]{1,0:T(8,128)(2,1)S(1)}, bf16[256,256]{1,0:T(8,128)(2,1)S(1)}, u32[]{:S(2)}, u32[]{:S(2)}) %collective-permute-start.12) | collective-permute-done | bytes 131104 | tf_op jit(solution)/shard_map/ppermute | solution.py:31
  42.3 2.9 %collective-permute-done.13.refs_3_ = bf16[256,256]{1,0:T(8,128)(2,1)S(1)} collective-permute-done((bf16[256,256]{1,0:T(8,128)(2,1)S(1)}, bf16[256,256]{1,0:T(8,128)(2,1)S(1)}, u32[]{:S(2)}, u32[]{:S(2)}) %collective-permute-start.13) | collective-permute-done | bytes 131104 | tf_op jit(solution)/shard_map/ppermute | solution.py:31
  45.2 0.5 %collective-permute-done.10.refs_1_ = bf16[256,256]{1,0:T(8,128)(2,1)S(1)} collective-permute-done((bf16[256,256]{1,0:T(8,128)(2,1)S(1)}, bf16[256,256]{1,0:T(8,128)(2,1)S(1)}, u32[]{:S(2)}, u32[]{:S(2)}) %collective-permute-start.10) | collective-permute-done | bytes 131104 | tf_op jit(solution)/shard_map/ppermute | solution.py:31
  45.7 0.6 %shard_map.131 = bf16[2,256,256]{2,1,0:T(8,128)(2,1)S(1)} custom-call(s32[2,2]{1,0:T(2,128)S(1)} %copy-done.3, bf16[8,2,32,256]{3,2,1,0:T(8,128)(2,1)S(1)} %get-tuple-element.24.v_ref, bf16[2,512,256]{2,1,0:T(8,128)(2,1)S(1)} %get-tuple-element.25.u_ref, bf16[2,2,2,256,256]{4,3,2,1,0:T(8,128)(2,1)S(1)} %copy-done, ...), custom_call_target="tpu_custom_call" | custom-call | flops 50331648 | bytes 3407888 | tf_op jit(solution)/shard_map/pallas_call | solution.py:259
  46.3 0.1 collective-permute-start.15
  46.3 0.6 %shard_map.130.own = f32[2,256,256]{2,1,0:T(8,128)S(1)} custom-call(s32[2,2]{1,0:T(2,128)S(1)} %copy-done.3, bf16[8,2,32,256]{3,2,1,0:T(8,128)(2,1)S(1)} %get-tuple-element.24.v_ref, bf16[2,512,256]{2,1,0:T(8,128)(2,1)S(1)} %get-tuple-element.25.u_ref, bf16[2,2,2,256,256]{4,3,2,1,0:T(8,128)(2,1)S(1)} %copy-done, ...), custom_call_target="tpu_custom_call" | custom-call | flops 50331648 | bytes 3407888 | tf_op jit(solution)/shard_map/pallas_call | solution.py:259
  46.9 0.9 %collective-permute-done.15.other = bf16[2,256,256]{2,1,0:T(8,128)(2,1)S(1)} collective-permute-done((bf16[2,256,256]{2,1,0:T(8,128)(2,1)S(1)}, bf16[2,256,256]{2,1,0:T(8,128)(2,1)S(1)}, u32[]{:S(2)}, u32[]{:S(2)}) %collective-permute-start.15) | collective-permute-done | bytes 262176 | tf_op jit(solution)/shard_map/ppermute | solution.py:355
  47.9 1.8 %shard_map.132 = (f32[256,256]{1,0:T(8,128)}, f32[256,256]{1,0:T(8,128)}) custom-call(f32[2,256,256]{2,1,0:T(8,128)S(1)} %shard_map.130.own, bf16[2,256,256]{2,1,0:T(8,128)(2,1)S(1)} %collective-permute-done.15.other, f32[256,256]{1,0:T(8,128)S(1)} %get-tuple-element.40.weight, f32[256,256]{1,0:T(8,128)S(1)} %get-tuple-element.41.unweight, ...), custom_call_target="tpu_custom_call" | custom-call | flops 13107200 | bytes 3538944 | tf_op jit(solution)/shard_map/pallas_call | solution.py:259
  (3 shorter events, 0.0 us)
Async XLA Ops:
  0.6 19.9 %copy-start = (bf16[2,2,2,256,256]{4,3,2,1,0:T(8,128)(2,1)S(1)}, bf16[2,2,2,256,256]{4,3,2,1,0:T(8,128)(2,1)}, u32[]{:S(2)}) copy-start(bf16[2,2,2,256,256]{4,3,2,1,0:T(8,128)(2,1)} %d_ref.11) | copy-start | bytes 3145732
  1.7 8.4 %collective-permute-start.3 = (bf16[256,256]{1,0:T(8,128)(2,1)S(1)}, bf16[256,256]{1,0:T(8,128)(2,1)S(1)}, u32[]{:S(2)}, u32[]{:S(2)}) collective-permute-start(bf16[256,256]{1,0:T(8,128)(2,1)S(1)} %shard_map.123.refs_0_), channel_id=1, source_target_pairs={{0,4},{2,6},{4,0},{6,2},{8,12},{10,14},{12,8},{14,10},{1,5},{3,7},... | collective-permute-start | bytes 393224 | tf_op jit(solution)/shard_map/ppermute | solution.py:31
  4.8 12.4 %collective-permute-start.1 = (bf16[256,256]{1,0:T(8,128)(2,1)S(1)}, bf16[256,256]{1,0:T(8,128)(2,1)S(1)}, u32[]{:S(2)}, u32[]{:S(2)}) collective-permute-start(bf16[256,256]{1,0:T(8,128)(2,1)S(1)} %shard_map.123.refs_0_), channel_id=1, source_target_pairs={{0,8},{2,10},{4,12},{6,14},{8,0},{10,2},{12,4},{14,6},{1,9},{3,11}... | collective-permute-start | bytes 393224 | tf_op jit(solution)/shard_map/ppermute | solution.py:31
  7.4 13.1 %collective-permute-start.6 = (bf16[256,256]{1,0:T(8,128)(2,1)S(1)}, bf16[256,256]{1,0:T(8,128)(2,1)S(1)}, u32[]{:S(2)}, u32[]{:S(2)}) collective-permute-start(bf16[256,256]{1,0:T(8,128)(2,1)S(1)} %shard_map.123.refs_0_), channel_id=1, source_target_pairs={{0,2},{2,0},{4,6},{6,4},{8,10},{10,8},{12,14},{14,12},{1,3},{3,1},... | collective-permute-start | bytes 393224 | tf_op jit(solution)/shard_map/ppermute | solution.py:31
  8.9 13.1 %collective-permute-start = (bf16[256,256]{1,0:T(8,128)(2,1)S(1)}, bf16[256,256]{1,0:T(8,128)(2,1)S(1)}, u32[]{:S(2)}, u32[]{:S(2)}) collective-permute-start(bf16[256,256]{1,0:T(8,128)(2,1)S(1)} %shard_map.123.refs_0_), channel_id=1, source_target_pairs={{0,14},{2,12},{4,10},{6,8},{8,6},{10,4},{12,2},{14,0},{1,15},{3,13... | collective-permute-start | bytes 393224 | tf_op jit(solution)/shard_map/ppermute | solution.py:31
  10.1 11.9 %collective-permute-start.4 = (bf16[256,256]{1,0:T(8,128)(2,1)S(1)}, bf16[256,256]{1,0:T(8,128)(2,1)S(1)}, u32[]{:S(2)}, u32[]{:S(2)}) collective-permute-start(bf16[256,256]{1,0:T(8,128)(2,1)S(1)} %collective-permute-done.3.refs_3_), channel_id=1, source_target_pairs={{0,2},{2,0},{4,6},{6,4},{8,10},{10,8},{12,14},{14,12},{1,3},{3,1},... | collective-permute-start | bytes 393224 | tf_op jit(solution)/shard_map/ppermute | solution.py:31
  17.2 5.0 %collective-permute-start.5 = (bf16[256,256]{1,0:T(8,128)(2,1)S(1)}, bf16[256,256]{1,0:T(8,128)(2,1)S(1)}, u32[]{:S(2)}, u32[]{:S(2)}) collective-permute-start(bf16[256,256]{1,0:T(8,128)(2,1)S(1)} %collective-permute-done.1.refs_2_), channel_id=1, source_target_pairs={{0,2},{2,0},{4,6},{6,4},{8,10},{10,8},{12,14},{14,12},{1,3},{3,1},... | collective-permute-start | bytes 393224 | tf_op jit(solution)/shard_map/ppermute | solution.py:31
  18.7 5.0 %collective-permute-start.2 = (bf16[256,256]{1,0:T(8,128)(2,1)S(1)}, bf16[256,256]{1,0:T(8,128)(2,1)S(1)}, u32[]{:S(2)}, u32[]{:S(2)}) collective-permute-start(bf16[256,256]{1,0:T(8,128)(2,1)S(1)} %collective-permute-done.1.refs_2_), channel_id=1, source_target_pairs={{0,4},{2,6},{4,0},{6,2},{8,12},{10,14},{12,8},{14,10},{1,5},{3,7},... | collective-permute-start | bytes 393224 | tf_op jit(solution)/shard_map/ppermute | solution.py:31
  20.5 0.7 %copy-start.3 = (s32[2,2]{1,0:T(2,128)S(1)}, s32[2,2]{1,0:T(2,128)}, u32[]{:S(2)}) copy-start(s32[2,2]{1,0:T(2,128)} %near_ref.11) | copy-start | bytes 52
  24.2 1.6 %copy-start.1 = (f32[256,256]{1,0:T(8,128)S(1)}, f32[256,256]{1,0:T(8,128)}, u32[]{:S(2)}) copy-start(f32[256,256]{1,0:T(8,128)} %tau.3) | copy-start | bytes 786436
  24.3 1.6 %collective-permute-start.7 = (bf16[2,256,256]{2,1,0:T(8,128)(2,1)S(1)}, bf16[2,256,256]{2,1,0:T(8,128)(2,1)S(1)}, u32[]{:S(2)}, u32[]{:S(2)}) collective-permute-start(bf16[2,256,256]{2,1,0:T(8,128)(2,1)S(1)} %shard_map.126), channel_id=1, source_target_pairs={{0,1},{1,0},{2,3},{3,2},{4,5},{5,4},{6,7},{7,6},{8,9},{9,8},{10,11... | collective-permute-start | bytes 786440 | tf_op jit(solution)/shard_map/ppermute | solution.py:355
  25.9 14.8 %copy-start.2 = (f32[256,256]{1,0:T(8,128)S(1)}, f32[256,256]{1,0:T(8,128)}, u32[]{:S(2)}) copy-start(f32[256,256]{1,0:T(8,128)} %state.1) | copy-start | bytes 786436
  26.9 8.0 %collective-permute-start.11 = (bf16[256,256]{1,0:T(8,128)(2,1)S(1)}, bf16[256,256]{1,0:T(8,128)(2,1)S(1)}, u32[]{:S(2)}, u32[]{:S(2)}) collective-permute-start(bf16[256,256]{1,0:T(8,128)(2,1)S(1)} %get-tuple-element.39.refs_0_), channel_id=1, source_target_pairs={{0,4},{2,6},{4,0},{6,2},{8,12},{10,14},{12,8},{14,10},{1,5},{3,7},... | collective-permute-start | bytes 393224 | tf_op jit(solution)/shard_map/ppermute | solution.py:31
  27.3 12.9 %collective-permute-start.9 = (bf16[256,256]{1,0:T(8,128)(2,1)S(1)}, bf16[256,256]{1,0:T(8,128)(2,1)S(1)}, u32[]{:S(2)}, u32[]{:S(2)}) collective-permute-start(bf16[256,256]{1,0:T(8,128)(2,1)S(1)} %get-tuple-element.39.refs_0_), channel_id=1, source_target_pairs={{0,8},{2,10},{4,12},{6,14},{8,0},{10,2},{12,4},{14,6},{1,9},{3,11}... | collective-permute-start | bytes 393224 | tf_op jit(solution)/shard_map/ppermute | solution.py:31
  30.3 10.5 %collective-permute-start.14 = (bf16[256,256]{1,0:T(8,128)(2,1)S(1)}, bf16[256,256]{1,0:T(8,128)(2,1)S(1)}, u32[]{:S(2)}, u32[]{:S(2)}) collective-permute-start(bf16[256,256]{1,0:T(8,128)(2,1)S(1)} %get-tuple-element.39.refs_0_), channel_id=1, source_target_pairs={{0,2},{2,0},{4,6},{6,4},{8,10},{10,8},{12,14},{14,12},{1,3},{3,1},... | collective-permute-start | bytes 393224 | tf_op jit(solution)/shard_map/ppermute | solution.py:31
  30.9 10.8 %collective-permute-start.8 = (bf16[256,256]{1,0:T(8,128)(2,1)S(1)}, bf16[256,256]{1,0:T(8,128)(2,1)S(1)}, u32[]{:S(2)}, u32[]{:S(2)}) collective-permute-start(bf16[256,256]{1,0:T(8,128)(2,1)S(1)} %get-tuple-element.39.refs_0_), channel_id=1, source_target_pairs={{0,14},{2,12},{4,10},{6,8},{8,6},{10,4},{12,2},{14,0},{1,15},{3,13... | collective-permute-start | bytes 393224 | tf_op jit(solution)/shard_map/ppermute | solution.py:31
  34.9 7.4 %collective-permute-start.12 = (bf16[256,256]{1,0:T(8,128)(2,1)S(1)}, bf16[256,256]{1,0:T(8,128)(2,1)S(1)}, u32[]{:S(2)}, u32[]{:S(2)}) collective-permute-start(bf16[256,256]{1,0:T(8,128)(2,1)S(1)} %collective-permute-done.11.refs_3_), channel_id=1, source_target_pairs={{0,2},{2,0},{4,6},{6,4},{8,10},{10,8},{12,14},{14,12},{1,3},{3,1},... | collective-permute-start | bytes 393224 | tf_op jit(solution)/shard_map/ppermute | solution.py:31
  40.2 5.0 %collective-permute-start.13 = (bf16[256,256]{1,0:T(8,128)(2,1)S(1)}, bf16[256,256]{1,0:T(8,128)(2,1)S(1)}, u32[]{:S(2)}, u32[]{:S(2)}) collective-permute-start(bf16[256,256]{1,0:T(8,128)(2,1)S(1)} %collective-permute-done.9.refs_2_), channel_id=1, source_target_pairs={{0,2},{2,0},{4,6},{6,4},{8,10},{10,8},{12,14},{14,12},{1,3},{3,1},... | collective-permute-start | bytes 393224 | tf_op jit(solution)/shard_map/ppermute | solution.py:31
  40.7 5.0 %collective-permute-start.10 = (bf16[256,256]{1,0:T(8,128)(2,1)S(1)}, bf16[256,256]{1,0:T(8,128)(2,1)S(1)}, u32[]{:S(2)}, u32[]{:S(2)}) collective-permute-start(bf16[256,256]{1,0:T(8,128)(2,1)S(1)} %collective-permute-done.9.refs_2_), channel_id=1, source_target_pairs={{0,4},{2,6},{4,0},{6,2},{8,12},{10,14},{12,8},{14,10},{1,5},{3,7},... | collective-permute-start | bytes 393224 | tf_op jit(solution)/shard_map/ppermute | solution.py:31
  46.3 1.6 %collective-permute-start.15 = (bf16[2,256,256]{2,1,0:T(8,128)(2,1)S(1)}, bf16[2,256,256]{2,1,0:T(8,128)(2,1)S(1)}, u32[]{:S(2)}, u32[]{:S(2)}) collective-permute-start(bf16[2,256,256]{2,1,0:T(8,128)(2,1)S(1)} %shard_map.131), channel_id=1, source_target_pairs={{0,1},{1,0},{2,3},{3,2},{4,5},{5,4},{6,7},{7,6},{8,9},{9,8},{10,11... | collective-permute-start | bytes 786440 | tf_op jit(solution)/shard_map/ppermute | solution.py:355

commit v19 on v17

--- a/solution.py
+++ b/solution.py
@@ -19,7 +19,7 @@
 def arrivals(count, direct):
     if not direct:
         return list(range(count))
-    return [0, 4, 2, 1, 3, 6, 7, 5] if count == 8 else [0, 1, 2, 3]
+    return [0, 1, 4, 2, 3, 6, 5, 7] if count == 8 else [0, 1, 2, 3]
 
 
 def row_met(spot, row, direct):
@@ -66,11 +66,15 @@
     outs[2][:, part] = jnp.exp(-state * coef[4])
 
 
-def later_kernel(state, change, coef, *outs):
+def later_kernel(own, other, state, decay, rate, coef, stress, normal, change, *outs):
+    stress[...] = own[0] + other[0].astype(jnp.float32)
+    normal[...] = own[1] + other[1].astype(jnp.float32)
     lanes = coef.shape[2]
     for first in range(0, state.shape[1], lanes):
         part = slice(first, first + lanes)
-        store_powers(outs, part, state[:, part] + section_step * change[:, part], coef)
+        step = state_change(rate[:, part], decay[:, part], coef[2])
+        change[:, part] = step
+        store_powers(outs, part, state[:, part] + section_step * step, coef)
 
 
 def prepare_kernel(spots, direct, *refs):
@@ -167,7 +171,7 @@
     return sinh, 0.5 * (grown + shrunk)
 
 
-def friction(shear, normal, weight, unweight, decay, tau_load, sigma_base, a_wide, b_wide):
+def friction(shear, normal, weight, unweight, tau_load, sigma_base, a_wide):
     tau = tau_load + shear
     size = jnp.abs(tau)
     stiff = jnp.maximum(sigma_base + normal, sigma_floor) * a_wide
@@ -180,8 +184,11 @@
         excess = stiff * slope + double * sinh - size
         slope = slope - excess * inverse(stiff + double * cosh)
     rate = 2.0 * weight * sinh_cosh(slope)[0]
-    change = b_wide * (decay - jnp.abs(rate))
-    return (jnp.where(tau < 0.0, -rate, rate), change)
+    return jnp.where(tau < 0.0, -rate, rate)
+
+
+def state_change(rate, decay, b_wide):
+    return b_wide * (decay - jnp.abs(rate))
 
 
 def over_pieces(begin, tall, members, lanes, work):
@@ -194,27 +201,20 @@
             work(rows, slice(first, first + lanes))
 
 
-def section_one_kernel(own, other, weight, unweight, decay, tau, coef, stress, normal, rate, change, rate_half):
+def section_one_kernel(own, other, weight, unweight, tau, coef, rate, rate_half):
     size, members = tau.shape
 
     def work(rows, part):
-        shear = own[0, rows, part] + other[0, rows, part].astype(jnp.float32)
-        press = own[1, rows, part] + other[1, rows, part].astype(jnp.float32)
-        stress[rows, part] = shear
-        normal[rows, part] = press
-        first, second = friction(
-            shear,
-            press,
+        first = friction(
+            own[0, rows, part] + other[0, rows, part].astype(jnp.float32),
+            own[1, rows, part] + other[1, rows, part].astype(jnp.float32),
             weight[rows, part],
             unweight[rows, part],
-            decay[rows, part],
             tau[rows, part],
             coef[0, rows, :],
             coef[1, rows, :],
-            coef[2, rows, :],
         )
         rate[rows, part] = first
-        change[rows, part] = second
         rate_half[rows, part] = first.astype(rate_half.dtype)
 
     over_pieces(0, size, members, coef.shape[2], work)
@@ -228,18 +228,17 @@
     def work(rows, part):
         shear = own[0, rows, part] + other[0, rows, part].astype(jnp.float32)
         press = own[1, rows, part] + other[1, rows, part].astype(jnp.float32)
-        first, second = friction(
+        later = friction(
             stress[rows, part] + section_step * shear,
             normal[rows, part] + section_step * press,
             weight[rows, part],
             unweight[rows, part],
-            decay[rows, part],
             tau[rows, part],
             coef[0, rows, :],
             coef[1, rows, :],
-            coef[2, rows, :],
         )
-        mean_rate[rows, part] = (rate[rows, part] + first) * 0.5
+        second = state_change(later, decay[rows, part], coef[2, rows, :])
+        mean_rate[rows, part] = (rate[rows, part] + later) * 0.5
         mean_change[rows, part] = (change[rows, part] + second) * 0.5
 
     copies = []
@@ -362,14 +361,14 @@
         far=(slip_deficit,),
     )
     own, other, powers = lattice(slip_half, powers)
-    stress, normal, rate, change, rate_half = on_core(
+    rate, rate_half = on_core(
         section_one_kernel,
-        (full, full, full, full, shaped(size, members, kind=narrow)),
-        (own, other, *powers, tau_load, coef),
+        (full, shaped(size, members, kind=narrow)),
+        (own, other, *powers[:2], tau_load, coef),
         flops=200 * size * members,
     )
-    powers = on_core(later_kernel, (full, full, full), (state_var, change, coef))
-    own, other, powers = lattice(rate_half, powers)
+    beside = on_core(later_kernel, (full,) * 6, (own, other, state_var, powers[2], rate, coef))
+    own, other, (stress, normal, change, *powers) = lattice(rate_half, beside)
     return on_core(
         section_two_kernel,
         (full, full),

time: 48.7 us -> 47 us (0.965)
  waiting for transfers between devices: 17.3 us -> 15.5 us
    ppermute x14, waiting for transfers between devices: 15.4 us -> 13.6 us  [swapped(): lax.ppermute(data, 'row', [(row, row ^ mask) for row in range(count)])]
where the time goes in v19:
time: 47 us; the launch traced here: 46.9 us
  starting transfers between devices  20.1 us (43%)
  waiting for transfers between devices  15.5 us (33%)
  Pallas kernels  9.76 us (21%)
  between operations  0.77 us (2%)
  local copies, waits for them, and re-layouts  0.68 us (1%)
    ppermute x14, starting transfers between devices, swapped(): lax.ppermute(data, 'row', [(row, row ^ mask) for row in range(count)])  20 us
    ppermute x14, waiting for transfers between devices, swapped(): lax.ppermute(data, 'row', [(row, row ^ mask) for row in range(count)])  13.6 us
    pallas_call x11, Pallas kernels, on_core(): pl.pallas_call(kernel, out_shape=outs, in_specs=[hbm] * len(far) + [vmem]...  9.76 us
    ppermute x2, waiting for transfers between devices, lattice(): lax.ppermute(add(blocks[early:], early, 1, sums, narrow), 'col', swap)  1.89 us
  transfers between devices with their start and end apart: 16, of which 8 were waited for; matrix products, arithmetic and copies ran while one was open for 0% of the time, Pallas kernels for 10%

profile of v19, /device:TPU:0, one launch (start us, length us, event | category | flops | bytes accessed | tf_op | source)
XLA Modules:
  0.0 46.9 jit_solution(9897965186433103550)
XLA Ops:
  0.6 0.0 copy-start
  0.6 1.0 %shard_map.123.refs_0_ = bf16[256,256]{1,0:T(8,128)(2,1)S(1)} custom-call(f32[256,256]{1,0:T(8,128)} %wide_ref.1), custom_call_target="tpu_custom_call" | custom-call | bytes 262144 | tf_op jit(solution)/shard_map/pallas_call | solution.py:257
  1.7 4.1 %collective-permute-start.1 = (bf16[256,256]{1,0:T(8,128)(2,1)S(1)}, bf16[256,256]{1,0:T(8,128)(2,1)S(1)}, u32[]{:S(2)}, u32[]{:S(2)}) collective-permute-start(bf16[256,256]{1,0:T(8,128)(2,1)S(1)} %shard_map.123.refs_0_), channel_id=1, source_target_pairs={{0,8},{2,10},{4,12},{6,14},{8,0},{10,2},{12,4},{14,6},{1,9},{3,11}... | collective-permute-start | bytes 393224 | tf_op jit(solution)/shard_map/ppermute | solution.py:31
  5.8 1.6 %collective-permute-start.6 = (bf16[256,256]{1,0:T(8,128)(2,1)S(1)}, bf16[256,256]{1,0:T(8,128)(2,1)S(1)}, u32[]{:S(2)}, u32[]{:S(2)}) collective-permute-start(bf16[256,256]{1,0:T(8,128)(2,1)S(1)} %shard_map.123.refs_0_), channel_id=1, source_target_pairs={{0,4},{2,6},{4,0},{6,2},{8,12},{10,14},{12,8},{14,10},{1,5},{3,7},... | collective-permute-start | bytes 393224 | tf_op jit(solution)/shard_map/ppermute | solution.py:31
  7.4 1.5 %collective-permute-start.5 = (bf16[256,256]{1,0:T(8,128)(2,1)S(1)}, bf16[256,256]{1,0:T(8,128)(2,1)S(1)}, u32[]{:S(2)}, u32[]{:S(2)}) collective-permute-start(bf16[256,256]{1,0:T(8,128)(2,1)S(1)} %shard_map.123.refs_0_), channel_id=1, source_target_pairs={{0,2},{2,0},{4,6},{6,4},{8,10},{10,8},{12,14},{14,12},{1,3},{3,1},... | collective-permute-start | bytes 393224 | tf_op jit(solution)/shard_map/ppermute | solution.py:31
  8.9 0.4 collective-permute-start
  9.3 2.9 %collective-permute-done.1.refs_2_ = bf16[256,256]{1,0:T(8,128)(2,1)S(1)} collective-permute-done((bf16[256,256]{1,0:T(8,128)(2,1)S(1)}, bf16[256,256]{1,0:T(8,128)(2,1)S(1)}, u32[]{:S(2)}, u32[]{:S(2)}) %collective-permute-start.1) | collective-permute-done | bytes 131104 | tf_op jit(solution)/shard_map/ppermute | solution.py:31
  12.2 1.6 %collective-permute-start.4 = (bf16[256,256]{1,0:T(8,128)(2,1)S(1)}, bf16[256,256]{1,0:T(8,128)(2,1)S(1)}, u32[]{:S(2)}, u32[]{:S(2)}) collective-permute-start(bf16[256,256]{1,0:T(8,128)(2,1)S(1)} %collective-permute-done.1.refs_2_), channel_id=1, source_target_pairs={{0,6},{2,4},{4,2},{6,0},{8,14},{10,12},{12,10},{14,8},{1,7},{3,5},... | collective-permute-start | bytes 393224 | tf_op jit(solution)/shard_map/ppermute | solution.py:31
  13.8 0.5 %collective-permute-start.3 = (bf16[256,256]{1,0:T(8,128)(2,1)S(1)}, bf16[256,256]{1,0:T(8,128)(2,1)S(1)}, u32[]{:S(2)}, u32[]{:S(2)}) collective-permute-start(bf16[256,256]{1,0:T(8,128)(2,1)S(1)} %collective-permute-done.1.refs_2_), channel_id=1, source_target_pairs={{0,2},{2,0},{4,6},{6,4},{8,10},{10,8},{12,14},{14,12},{1,3},{3,1},... | collective-permute-start | bytes 393224 | tf_op jit(solution)/shard_map/ppermute | solution.py:31
  14.3 0.0 collective-permute-done.6.refs_3_
  14.3 1.4 %collective-permute-start.2 = (bf16[256,256]{1,0:T(8,128)(2,1)S(1)}, bf16[256,256]{1,0:T(8,128)(2,1)S(1)}, u32[]{:S(2)}, u32[]{:S(2)}) collective-permute-start(bf16[256,256]{1,0:T(8,128)(2,1)S(1)} %collective-permute-done.1.refs_2_), channel_id=1, source_target_pairs={{0,4},{2,6},{4,0},{6,2},{8,12},{10,14},{12,8},{14,10},{1,5},{3,7},... | collective-permute-start | bytes 393224 | tf_op jit(solution)/shard_map/ppermute | solution.py:31
  15.7 1.8 %shard_map.122 = (bf16[8,2,32,256]{3,2,1,0:T(8,128)(2,1)S(1)}, bf16[2,512,256]{2,1,0:T(8,128)(2,1)S(1)}, f32[5,256,128]{2,1,0:T(8,128)S(1)}, f32[256,256]{1,0:T(...) custom-call(s32[2,8]{1,0:T(2,128)} %refs_0_.1, bf16[2,8,32,256]{3,2,1,0:T(8,128)(2,1)} %refs_1_.1, ...), custom_call_target="tpu_custom_call" | custom-call | bytes 1051712 | tf_op jit(solution)/shard_map/pallas_call | solution.py:257
  17.4 0.0 collective-permute-done.5.refs_1_
  17.5 0.0 copy-start.3
  17.5 0.0 copy-done
  17.5 0.7 %copy-done.3 = s32[2,2]{1,0:T(2,128)S(1)} copy-done((s32[2,2]{1,0:T(2,128)S(1)}, s32[2,2]{1,0:T(2,128)}, u32[]{:S(2)}) %copy-start.3) | copy-done | bytes 40
  18.1 0.8 %shard_map.124.refs_4_ = f32[2,2,256,256]{3,2,1,0:T(8,128)S(1)} custom-call(s32[2,2]{1,0:T(2,128)S(1)} %copy-done.3, bf16[8,2,32,256]{3,2,1,0:T(8,128)(2,1)S(1)} %get-tuple-element.27.v_ref, bf16[2,512,256]{2,1,0:T(8,128)(2,1)S(1)} %get-tuple-element.28.u_ref, bf16[2,2,2,256,256]{4,3,2,1,0:T(8,128)(2,1)S(1)} %copy-done, ...), custom_call_target="tpu_custom_call" | custom-call | flops 100663296 | bytes 2359312 | tf_op jit(solution)/shard_map/pallas_call | solution.py:257
  18.9 0.0 collective-permute-done.refs_0_
  18.9 1.0 %collective-permute-done.4.refs_3_ = bf16[256,256]{1,0:T(8,128)(2,1)S(1)} collective-permute-done((bf16[256,256]{1,0:T(8,128)(2,1)S(1)}, bf16[256,256]{1,0:T(8,128)(2,1)S(1)}, u32[]{:S(2)}, u32[]{:S(2)}) %collective-permute-start.4) | collective-permute-done | bytes 131104 | tf_op jit(solution)/shard_map/ppermute | solution.py:31
  19.9 1.9 %collective-permute-done.3.refs_2_ = bf16[256,256]{1,0:T(8,128)(2,1)S(1)} collective-permute-done((bf16[256,256]{1,0:T(8,128)(2,1)S(1)}, bf16[256,256]{1,0:T(8,128)(2,1)S(1)}, u32[]{:S(2)}, u32[]{:S(2)}) %collective-permute-start.3) | collective-permute-done | bytes 131104 | tf_op jit(solution)/shard_map/ppermute | solution.py:31
  21.8 0.0 collective-permute-done.2.refs_1_
  21.8 0.6 %shard_map.126 = bf16[2,256,256]{2,1,0:T(8,128)(2,1)S(1)} custom-call(s32[2,2]{1,0:T(2,128)S(1)} %copy-done.3, bf16[8,2,32,256]{3,2,1,0:T(8,128)(2,1)S(1)} %get-tuple-element.27.v_ref, bf16[2,512,256]{2,1,0:T(8,128)(2,1)S(1)} %get-tuple-element.28.u_ref, bf16[2,2,2,256,256]{4,3,2,1,0:T(8,128)(2,1)S(1)} %copy-done, ...), custom_call_target="tpu_custom_call" | custom-call | flops 50331648 | bytes 3407888 | tf_op jit(solution)/shard_map/pallas_call | solution.py:257
  22.4 0.0 copy-start.1
  22.4 0.1 collective-permute-start.7
  22.5 0.6 %shard_map.125.own = f32[2,256,256]{2,1,0:T(8,128)S(1)} custom-call(s32[2,2]{1,0:T(2,128)S(1)} %copy-done.3, bf16[8,2,32,256]{3,2,1,0:T(8,128)(2,1)S(1)} %get-tuple-element.27.v_ref, bf16[2,512,256]{2,1,0:T(8,128)(2,1)S(1)} %get-tuple-element.28.u_ref, bf16[2,2,2,256,256]{4,3,2,1,0:T(8,128)(2,1)S(1)} %copy-done, ...), custom_call_target="tpu_custom_call" | custom-call | flops 50331648 | bytes 3407888 | tf_op jit(solution)/shard_map/pallas_call | solution.py:257
  23.1 0.9 %collective-permute-done.7.other = bf16[2,256,256]{2,1,0:T(8,128)(2,1)S(1)} collective-permute-done((bf16[2,256,256]{2,1,0:T(8,128)(2,1)S(1)}, bf16[2,256,256]{2,1,0:T(8,128)(2,1)S(1)}, u32[]{:S(2)}, u32[]{:S(2)}) %collective-permute-start.7) | collective-permute-done | bytes 262176 | tf_op jit(solution)/shard_map/ppermute | solution.py:353
  24.0 1.1 %shard_map.127 = (f32[256,256]{1,0:T(8,128)S(1)}, bf16[256,256]{1,0:T(8,128)(2,1)S(1)}) custom-call(f32[2,256,256]{2,1,0:T(8,128)S(1)} %shard_map.125.own, bf16[2,256,256]{2,1,0:T(8,128)(2,1)S(1)} %collective-permute-done.7.other, f32[256,256]{1,0:T(8,128)S(1)} %get-tuple-element.33.weight, f32[256,256]{1,0:T(8,128)S(1)} %get-tuple-element.34.unweight, ...), custom_call_target="tpu_custom_call" | custom-call | flops 13107200 | bytes 2228224 | tf_op jit(solution)/shard_map/pallas_call | solution.py:257
  25.1 1.9 %collective-permute-start.9 = (bf16[256,256]{1,0:T(8,128)(2,1)S(1)}, bf16[256,256]{1,0:T(8,128)(2,1)S(1)}, u32[]{:S(2)}, u32[]{:S(2)}) collective-permute-start(bf16[256,256]{1,0:T(8,128)(2,1)S(1)} %get-tuple-element.45.refs_0_), channel_id=1, source_target_pairs={{0,8},{2,10},{4,12},{6,14},{8,0},{10,2},{12,4},{14,6},{1,9},{3,11}... | collective-permute-start | bytes 393224 | tf_op jit(solution)/shard_map/ppermute | solution.py:31
  27.0 1.8 %collective-permute-start.14 = (bf16[256,256]{1,0:T(8,128)(2,1)S(1)}, bf16[256,256]{1,0:T(8,128)(2,1)S(1)}, u32[]{:S(2)}, u32[]{:S(2)}) collective-permute-start(bf16[256,256]{1,0:T(8,128)(2,1)S(1)} %get-tuple-element.45.refs_0_), channel_id=1, source_target_pairs={{0,4},{2,6},{4,0},{6,2},{8,12},{10,14},{12,8},{14,10},{1,5},{3,7},... | collective-permute-start | bytes 393224 | tf_op jit(solution)/shard_map/ppermute | solution.py:31
  28.8 0.5 %collective-permute-start.13 = (bf16[256,256]{1,0:T(8,128)(2,1)S(1)}, bf16[256,256]{1,0:T(8,128)(2,1)S(1)}, u32[]{:S(2)}, u32[]{:S(2)}) collective-permute-start(bf16[256,256]{1,0:T(8,128)(2,1)S(1)} %get-tuple-element.45.refs_0_), channel_id=1, source_target_pairs={{0,2},{2,0},{4,6},{6,4},{8,10},{10,8},{12,14},{14,12},{1,3},{3,1},... | collective-permute-start | bytes 393224 | tf_op jit(solution)/shard_map/ppermute | solution.py:31
  29.4 1.2 %collective-permute-start.8 = (bf16[256,256]{1,0:T(8,128)(2,1)S(1)}, bf16[256,256]{1,0:T(8,128)(2,1)S(1)}, u32[]{:S(2)}, u32[]{:S(2)}) collective-permute-start(bf16[256,256]{1,0:T(8,128)(2,1)S(1)} %get-tuple-element.45.refs_0_), channel_id=1, source_target_pairs={{0,6},{2,4},{4,2},{6,0},{8,14},{10,12},{12,10},{14,8},{1,7},{3,5},... | collective-permute-start | bytes 393224 | tf_op jit(solution)/shard_map/ppermute | solution.py:31
  30.5 4.0 %collective-permute-done.9.refs_2_ = bf16[256,256]{1,0:T(8,128)(2,1)S(1)} collective-permute-done((bf16[256,256]{1,0:T(8,128)(2,1)S(1)}, bf16[256,256]{1,0:T(8,128)(2,1)S(1)}, u32[]{:S(2)}, u32[]{:S(2)}) %collective-permute-start.9) | collective-permute-done | bytes 131104 | tf_op jit(solution)/shard_map/ppermute | solution.py:31
  34.5 0.0 collective-permute-start.12
  34.5 1.3 %collective-permute-start.11 = (bf16[256,256]{1,0:T(8,128)(2,1)S(1)}, bf16[256,256]{1,0:T(8,128)(2,1)S(1)}, u32[]{:S(2)}, u32[]{:S(2)}) collective-permute-start(bf16[256,256]{1,0:T(8,128)(2,1)S(1)} %collective-permute-done.9.refs_2_), channel_id=1, source_target_pairs={{0,2},{2,0},{4,6},{6,4},{8,10},{10,8},{12,14},{14,12},{1,3},{3,1},... | collective-permute-start | bytes 393224 | tf_op jit(solution)/shard_map/ppermute | solution.py:31
  35.9 0.0 collective-permute-done.14.refs_3_
  35.9 2.1 %collective-permute-start.10 = (bf16[256,256]{1,0:T(8,128)(2,1)S(1)}, bf16[256,256]{1,0:T(8,128)(2,1)S(1)}, u32[]{:S(2)}, u32[]{:S(2)}) collective-permute-start(bf16[256,256]{1,0:T(8,128)(2,1)S(1)} %collective-permute-done.9.refs_2_), channel_id=1, source_target_pairs={{0,4},{2,6},{4,0},{6,2},{8,12},{10,14},{12,8},{14,10},{1,5},{3,7},... | collective-permute-start | bytes 393224 | tf_op jit(solution)/shard_map/ppermute | solution.py:31
  38.0 0.2 shard_map.128
  38.3 0.0 collective-permute-done.13.refs_1_
  38.3 0.8 %shard_map.129.refs_4_ = f32[2,2,256,256]{3,2,1,0:T(8,128)S(1)} custom-call(s32[2,2]{1,0:T(2,128)S(1)} %copy-done.3, bf16[8,2,32,256]{3,2,1,0:T(8,128)(2,1)S(1)} %get-tuple-element.27.v_ref, bf16[2,512,256]{2,1,0:T(8,128)(2,1)S(1)} %get-tuple-element.28.u_ref, bf16[2,2,2,256,256]{4,3,2,1,0:T(8,128)(2,1)S(1)} %copy-done, ...), custom_call_target="tpu_custom_call" | custom-call | flops 100663296 | bytes 2359312 | tf_op jit(solution)/shard_map/pallas_call | solution.py:257
  39.1 0.0 collective-permute-done.8.refs_0_
  39.1 2.5 %collective-permute-done.12.refs_3_ = bf16[256,256]{1,0:T(8,128)(2,1)S(1)} collective-permute-done((bf16[256,256]{1,0:T(8,128)(2,1)S(1)}, bf16[256,256]{1,0:T(8,128)(2,1)S(1)}, u32[]{:S(2)}, u32[]{:S(2)}) %collective-permute-start.12) | collective-permute-done | bytes 131104 | tf_op jit(solution)/shard_map/ppermute | solution.py:31
  41.6 1.3 %collective-permute-done.11.refs_2_ = bf16[256,256]{1,0:T(8,128)(2,1)S(1)} collective-permute-done((bf16[256,256]{1,0:T(8,128)(2,1)S(1)}, bf16[256,256]{1,0:T(8,128)(2,1)S(1)}, u32[]{:S(2)}, u32[]{:S(2)}) %collective-permute-start.11) | collective-permute-done | bytes 131104 | tf_op jit(solution)/shard_map/ppermute | solution.py:31
  42.9 0.0 collective-permute-done.10.refs_1_
  42.9 0.6 %shard_map.131 = bf16[2,256,256]{2,1,0:T(8,128)(2,1)S(1)} custom-call(s32[2,2]{1,0:T(2,128)S(1)} %copy-done.3, bf16[8,2,32,256]{3,2,1,0:T(8,128)(2,1)S(1)} %get-tuple-element.27.v_ref, bf16[2,512,256]{2,1,0:T(8,128)(2,1)S(1)} %get-tuple-element.28.u_ref, bf16[2,2,2,256,256]{4,3,2,1,0:T(8,128)(2,1)S(1)} %copy-done, ...), custom_call_target="tpu_custom_call" | custom-call | flops 50331648 | bytes 3407888 | tf_op jit(solution)/shard_map/pallas_call | solution.py:257
  43.5 0.1 collective-permute-start.15
  43.6 0.6 %shard_map.130.own = f32[2,256,256]{2,1,0:T(8,128)S(1)} custom-call(s32[2,2]{1,0:T(2,128)S(1)} %copy-done.3, bf16[8,2,32,256]{3,2,1,0:T(8,128)(2,1)S(1)} %get-tuple-element.27.v_ref, bf16[2,512,256]{2,1,0:T(8,128)(2,1)S(1)} %get-tuple-element.28.u_ref, bf16[2,2,2,256,256]{4,3,2,1,0:T(8,128)(2,1)S(1)} %copy-done, ...), custom_call_target="tpu_custom_call" | custom-call | flops 50331648 | bytes 3407888 | tf_op jit(solution)/shard_map/pallas_call | solution.py:257
  44.2 0.9 %collective-permute-done.15.other = bf16[2,256,256]{2,1,0:T(8,128)(2,1)S(1)} collective-permute-done((bf16[2,256,256]{2,1,0:T(8,128)(2,1)S(1)}, bf16[2,256,256]{2,1,0:T(8,128)(2,1)S(1)}, u32[]{:S(2)}, u32[]{:S(2)}) %collective-permute-start.15) | collective-permute-done | bytes 262176 | tf_op jit(solution)/shard_map/ppermute | solution.py:353
  45.1 1.8 %shard_map.132 = (f32[256,256]{1,0:T(8,128)}, f32[256,256]{1,0:T(8,128)}) custom-call(f32[2,256,256]{2,1,0:T(8,128)S(1)} %shard_map.130.own, bf16[2,256,256]{2,1,0:T(8,128)(2,1)S(1)} %collective-permute-done.15.other, f32[256,256]{1,0:T(8,128)S(1)} %get-tuple-element.46.weight, f32[256,256]{1,0:T(8,128)S(1)} %get-tuple-element.47.unweight, ...), custom_call_target="tpu_custom_call" | custom-call | flops 13107200 | bytes 3538944 | tf_op jit(solution)/shard_map/pallas_call | solution.py:257
  (3 shorter events, 0.0 us)
Async XLA Ops:
  0.6 16.8 %copy-start = (bf16[2,2,2,256,256]{4,3,2,1,0:T(8,128)(2,1)S(1)}, bf16[2,2,2,256,256]{4,3,2,1,0:T(8,128)(2,1)}, u32[]{:S(2)}) copy-start(bf16[2,2,2,256,256]{4,3,2,1,0:T(8,128)(2,1)} %d_ref.11) | copy-start | bytes 3145732
  1.7 10.5 %collective-permute-start.1 = (bf16[256,256]{1,0:T(8,128)(2,1)S(1)}, bf16[256,256]{1,0:T(8,128)(2,1)S(1)}, u32[]{:S(2)}, u32[]{:S(2)}) collective-permute-start(bf16[256,256]{1,0:T(8,128)(2,1)S(1)} %shard_map.123.refs_0_), channel_id=1, source_target_pairs={{0,8},{2,10},{4,12},{6,14},{8,0},{10,2},{12,4},{14,6},{1,9},{3,11}... | collective-permute-start | bytes 393224 | tf_op jit(solution)/shard_map/ppermute | solution.py:31
  5.8 8.5 %collective-permute-start.6 = (bf16[256,256]{1,0:T(8,128)(2,1)S(1)}, bf16[256,256]{1,0:T(8,128)(2,1)S(1)}, u32[]{:S(2)}, u32[]{:S(2)}) collective-permute-start(bf16[256,256]{1,0:T(8,128)(2,1)S(1)} %shard_map.123.refs_0_), channel_id=1, source_target_pairs={{0,4},{2,6},{4,0},{6,2},{8,12},{10,14},{12,8},{14,10},{1,5},{3,7},... | collective-permute-start | bytes 393224 | tf_op jit(solution)/shard_map/ppermute | solution.py:31
  7.4 10.1 %collective-permute-start.5 = (bf16[256,256]{1,0:T(8,128)(2,1)S(1)}, bf16[256,256]{1,0:T(8,128)(2,1)S(1)}, u32[]{:S(2)}, u32[]{:S(2)}) collective-permute-start(bf16[256,256]{1,0:T(8,128)(2,1)S(1)} %shard_map.123.refs_0_), channel_id=1, source_target_pairs={{0,2},{2,0},{4,6},{6,4},{8,10},{10,8},{12,14},{14,12},{1,3},{3,1},... | collective-permute-start | bytes 393224 | tf_op jit(solution)/shard_map/ppermute | solution.py:31
  8.9 10.1 %collective-permute-start = (bf16[256,256]{1,0:T(8,128)(2,1)S(1)}, bf16[256,256]{1,0:T(8,128)(2,1)S(1)}, u32[]{:S(2)}, u32[]{:S(2)}) collective-permute-start(bf16[256,256]{1,0:T(8,128)(2,1)S(1)} %shard_map.123.refs_0_), channel_id=1, source_target_pairs={{0,6},{2,4},{4,2},{6,0},{8,14},{10,12},{12,10},{14,8},{1,7},{3,5},... | collective-permute-start | bytes 393224 | tf_op jit(solution)/shard_map/ppermute | solution.py:31
  12.2 7.7 %collective-permute-start.4 = (bf16[256,256]{1,0:T(8,128)(2,1)S(1)}, bf16[256,256]{1,0:T(8,128)(2,1)S(1)}, u32[]{:S(2)}, u32[]{:S(2)}) collective-permute-start(bf16[256,256]{1,0:T(8,128)(2,1)S(1)} %collective-permute-done.1.refs_2_), channel_id=1, source_target_pairs={{0,6},{2,4},{4,2},{6,0},{8,14},{10,12},{12,10},{14,8},{1,7},{3,5},... | collective-permute-start | bytes 393224 | tf_op jit(solution)/shard_map/ppermute | solution.py:31
  13.8 8.0 %collective-permute-start.3 = (bf16[256,256]{1,0:T(8,128)(2,1)S(1)}, bf16[256,256]{1,0:T(8,128)(2,1)S(1)}, u32[]{:S(2)}, u32[]{:S(2)}) collective-permute-start(bf16[256,256]{1,0:T(8,128)(2,1)S(1)} %collective-permute-done.1.refs_2_), channel_id=1, source_target_pairs={{0,2},{2,0},{4,6},{6,4},{8,10},{10,8},{12,14},{14,12},{1,3},{3,1},... | collective-permute-start | bytes 393224 | tf_op jit(solution)/shard_map/ppermute | solution.py:31
  14.3 7.5 %collective-permute-start.2 = (bf16[256,256]{1,0:T(8,128)(2,1)S(1)}, bf16[256,256]{1,0:T(8,128)(2,1)S(1)}, u32[]{:S(2)}, u32[]{:S(2)}) collective-permute-start(bf16[256,256]{1,0:T(8,128)(2,1)S(1)} %collective-permute-done.1.refs_2_), channel_id=1, source_target_pairs={{0,4},{2,6},{4,0},{6,2},{8,12},{10,14},{12,8},{14,10},{1,5},{3,7},... | collective-permute-start | bytes 393224 | tf_op jit(solution)/shard_map/ppermute | solution.py:31
  17.5 0.7 %copy-start.3 = (s32[2,2]{1,0:T(2,128)S(1)}, s32[2,2]{1,0:T(2,128)}, u32[]{:S(2)}) copy-start(s32[2,2]{1,0:T(2,128)} %near_ref.11) | copy-start | bytes 52
  22.4 1.6 %copy-start.1 = (f32[256,256]{1,0:T(8,128)S(1)}, f32[256,256]{1,0:T(8,128)}, u32[]{:S(2)}) copy-start(f32[256,256]{1,0:T(8,128)} %tau.3) | copy-start | bytes 786436
  22.4 1.6 %collective-permute-start.7 = (bf16[2,256,256]{2,1,0:T(8,128)(2,1)S(1)}, bf16[2,256,256]{2,1,0:T(8,128)(2,1)S(1)}, u32[]{:S(2)}, u32[]{:S(2)}) collective-permute-start(bf16[2,256,256]{2,1,0:T(8,128)(2,1)S(1)} %shard_map.126), channel_id=1, source_target_pairs={{0,1},{1,0},{2,3},{3,2},{4,5},{5,4},{6,7},{7,6},{8,9},{9,8},{10,11... | collective-permute-start | bytes 786440 | tf_op jit(solution)/shard_map/ppermute | solution.py:353
  24.0 14.0 %copy-start.2 = (f32[256,256]{1,0:T(8,128)S(1)}, f32[256,256]{1,0:T(8,128)}, u32[]{:S(2)}) copy-start(f32[256,256]{1,0:T(8,128)} %state.1) | copy-start | bytes 786436
  25.1 9.4 %collective-permute-start.9 = (bf16[256,256]{1,0:T(8,128)(2,1)S(1)}, bf16[256,256]{1,0:T(8,128)(2,1)S(1)}, u32[]{:S(2)}, u32[]{:S(2)}) collective-permute-start(bf16[256,256]{1,0:T(8,128)(2,1)S(1)} %get-tuple-element.45.refs_0_), channel_id=1, source_target_pairs={{0,8},{2,10},{4,12},{6,14},{8,0},{10,2},{12,4},{14,6},{1,9},{3,11}... | collective-permute-start | bytes 393224 | tf_op jit(solution)/shard_map/ppermute | solution.py:31
  27.0 8.8 %collective-permute-start.14 = (bf16[256,256]{1,0:T(8,128)(2,1)S(1)}, bf16[256,256]{1,0:T(8,128)(2,1)S(1)}, u32[]{:S(2)}, u32[]{:S(2)}) collective-permute-start(bf16[256,256]{1,0:T(8,128)(2,1)S(1)} %get-tuple-element.45.refs_0_), channel_id=1, source_target_pairs={{0,4},{2,6},{4,0},{6,2},{8,12},{10,14},{12,8},{14,10},{1,5},{3,7},... | collective-permute-start | bytes 393224 | tf_op jit(solution)/shard_map/ppermute | solution.py:31
  28.8 9.4 %collective-permute-start.13 = (bf16[256,256]{1,0:T(8,128)(2,1)S(1)}, bf16[256,256]{1,0:T(8,128)(2,1)S(1)}, u32[]{:S(2)}, u32[]{:S(2)}) collective-permute-start(bf16[256,256]{1,0:T(8,128)(2,1)S(1)} %get-tuple-element.45.refs_0_), channel_id=1, source_target_pairs={{0,2},{2,0},{4,6},{6,4},{8,10},{10,8},{12,14},{14,12},{1,3},{3,1},... | collective-permute-start | bytes 393224 | tf_op jit(solution)/shard_map/ppermute | solution.py:31
  29.4 9.7 %collective-permute-start.8 = (bf16[256,256]{1,0:T(8,128)(2,1)S(1)}, bf16[256,256]{1,0:T(8,128)(2,1)S(1)}, u32[]{:S(2)}, u32[]{:S(2)}) collective-permute-start(bf16[256,256]{1,0:T(8,128)(2,1)S(1)} %get-tuple-element.45.refs_0_), channel_id=1, source_target_pairs={{0,6},{2,4},{4,2},{6,0},{8,14},{10,12},{12,10},{14,8},{1,7},{3,5},... | collective-permute-start | bytes 393224 | tf_op jit(solution)/shard_map/ppermute | solution.py:31
  34.5 7.0 %collective-permute-start.12 = (bf16[256,256]{1,0:T(8,128)(2,1)S(1)}, bf16[256,256]{1,0:T(8,128)(2,1)S(1)}, u32[]{:S(2)}, u32[]{:S(2)}) collective-permute-start(bf16[256,256]{1,0:T(8,128)(2,1)S(1)} %collective-permute-done.9.refs_2_), channel_id=1, source_target_pairs={{0,6},{2,4},{4,2},{6,0},{8,14},{10,12},{12,10},{14,8},{1,7},{3,5},... | collective-permute-start | bytes 393224 | tf_op jit(solution)/shard_map/ppermute | solution.py:31
  34.5 8.4 %collective-permute-start.11 = (bf16[256,256]{1,0:T(8,128)(2,1)S(1)}, bf16[256,256]{1,0:T(8,128)(2,1)S(1)}, u32[]{:S(2)}, u32[]{:S(2)}) collective-permute-start(bf16[256,256]{1,0:T(8,128)(2,1)S(1)} %collective-permute-done.9.refs_2_), channel_id=1, source_target_pairs={{0,2},{2,0},{4,6},{6,4},{8,10},{10,8},{12,14},{14,12},{1,3},{3,1},... | collective-permute-start | bytes 393224 | tf_op jit(solution)/shard_map/ppermute | solution.py:31
  35.9 7.0 %collective-permute-start.10 = (bf16[256,256]{1,0:T(8,128)(2,1)S(1)}, bf16[256,256]{1,0:T(8,128)(2,1)S(1)}, u32[]{:S(2)}, u32[]{:S(2)}) collective-permute-start(bf16[256,256]{1,0:T(8,128)(2,1)S(1)} %collective-permute-done.9.refs_2_), channel_id=1, source_target_pairs={{0,4},{2,6},{4,0},{6,2},{8,12},{10,14},{12,8},{14,10},{1,5},{3,7},... | collective-permute-start | bytes 393224 | tf_op jit(solution)/shard_map/ppermute | solution.py:31
  43.5 1.6 %collective-permute-start.15 = (bf16[2,256,256]{2,1,0:T(8,128)(2,1)S(1)}, bf16[2,256,256]{2,1,0:T(8,128)(2,1)S(1)}, u32[]{:S(2)}, u32[]{:S(2)}) collective-permute-start(bf16[2,256,256]{2,1,0:T(8,128)(2,1)S(1)} %shard_map.131), channel_id=1, source_target_pairs={{0,1},{1,0},{2,3},{3,2},{4,5},{5,4},{6,7},{7,6},{8,9},{9,8},{10,11... | collective-permute-start | bytes 786440 | tf_op jit(solution)/shard_map/ppermute | solution.py:353

commit v20 on v16

--- a/solution.py
+++ b/solution.py
@@ -20,7 +20,7 @@
     if not direct:
         cuts = [0, max(count - 4, 0), count]
         return [list(range(first, last)) for first, last in zip(cuts, cuts[1:]) if last > first]
-    return [[0, 1, 4, 2, 3], [6, 5, 7]] if count == 8 else [[0, 1], [2, 3]]
+    return [[0, 1, 4], [2, 3], [7, 6, 5]] if count == 8 else [[0, 1], [2, 3]]
 
 
 def row_met(spot, row, direct):
@@ -32,11 +32,10 @@
         return lax.ppermute(data, "row", [(row, row ^ mask) for row in range(count)])
 
     found = {0: block}
-    for mask in (4, 1, 2) if count == 8 else (1, 2):
+    for mask in (4, 1, 2, 3, 7) if count == 8 else (1, 2, 3):
         found[mask] = swapped(mask, block)
-    found[3] = swapped(2, found[1])
     if count == 8:
-        for mask in (1, 2, 3):
+        for mask in (1, 2):
             found[4 + mask] = swapped(mask, found[4])
     return [[found[mask] for mask in group] for group in arrivals(count, True)]
 

time: 47.7 us -> 48.4 us (1.015)
  Pallas kernels: 9.6 us -> 11 us
  starting transfers between devices: 22 us -> 21.1 us
    pallas_call x11 -> x13, Pallas kernels: 9.6 us -> 11 us  [on_core(): pl.pallas_call(kernel, out_shape=outs, in_specs=[hbm] * len(far) + [vmem]...]
    ppermute x14, starting transfers between devices: 21.9 us -> 21 us  [swapped(): lax.ppermute(data, 'row', [(row, row ^ mask) for row in range(count)])]
  transfers between devices with their start and end apart: 16 -> 16, of which waited for: 11 -> 13; matrix products, arithmetic and copies ran while one was open for 0% -> 0% of each run, Pallas kernels for 10% -> 13%
where the time goes in v20:
time: 48.4 us; the launch traced here: 48.2 us
  starting transfers between devices  21.1 us (44%)
  waiting for transfers between devices  14.6 us (30%)
  Pallas kernels  11 us (23%)
  between operations  0.77 us (2%)
  local copies, waits for them, and re-layouts  0.68 us (1%)
    ppermute x14, starting transfers between devices, swapped(): lax.ppermute(data, 'row', [(row, row ^ mask) for row in range(count)])  21 us
    ppermute x14, waiting for transfers between devices, swapped(): lax.ppermute(data, 'row', [(row, row ^ mask) for row in range(count)])  12.7 us
    pallas_call x13, Pallas kernels, on_core(): pl.pallas_call(kernel, out_shape=outs, in_specs=[hbm] * len(far) + [vmem]...  11 us
    ppermute x2, waiting for transfers between devices, lattice(): other = lax.ppermute(add(found[end], end, 1, sums, narrow), 'col', swap)  1.96 us
  transfers between devices with their start and end apart: 16, of which 13 were waited for; matrix products, arithmetic and copies ran while one was open for 0% of the time, Pallas kernels for 13%

profile of v20, /device:TPU:0, one launch (start us, length us, event | category | flops | bytes accessed | tf_op | source)
XLA Modules:
  0.0 48.2 jit_solution(5864210063557482044)
XLA Ops:
  0.6 1.0 %shard_map.123.refs_0_ = bf16[256,256]{1,0:T(8,128)(2,1)S(1)} custom-call(f32[256,256]{1,0:T(8,128)} %wide_ref.1), custom_call_target="tpu_custom_call" | custom-call | bytes 262144 | tf_op jit(solution)/shard_map/pallas_call | solution.py:269
  1.7 4.1 %collective-permute-start.1 = (bf16[256,256]{1,0:T(8,128)(2,1)S(1)}, bf16[256,256]{1,0:T(8,128)(2,1)S(1)}, u32[]{:S(2)}, u32[]{:S(2)}) collective-permute-start(bf16[256,256]{1,0:T(8,128)(2,1)S(1)} %shard_map.123.refs_0_), channel_id=1, source_target_pairs={{0,8},{2,10},{4,12},{6,14},{8,0},{10,2},{12,4},{14,6},{1,9},{3,11}... | collective-permute-start | bytes 393224 | tf_op jit(solution)/shard_map/ppermute | solution.py:32
  5.8 1.5 %collective-permute-start.6 = (bf16[256,256]{1,0:T(8,128)(2,1)S(1)}, bf16[256,256]{1,0:T(8,128)(2,1)S(1)}, u32[]{:S(2)}, u32[]{:S(2)}) collective-permute-start(bf16[256,256]{1,0:T(8,128)(2,1)S(1)} %shard_map.123.refs_0_), channel_id=1, source_target_pairs={{0,2},{2,0},{4,6},{6,4},{8,10},{10,8},{12,14},{14,12},{1,3},{3,1},... | collective-permute-start | bytes 393224 | tf_op jit(solution)/shard_map/ppermute | solution.py:32
  7.3 1.6 %collective-permute-start.4 = (bf16[256,256]{1,0:T(8,128)(2,1)S(1)}, bf16[256,256]{1,0:T(8,128)(2,1)S(1)}, u32[]{:S(2)}, u32[]{:S(2)}) collective-permute-start(bf16[256,256]{1,0:T(8,128)(2,1)S(1)} %shard_map.123.refs_0_), channel_id=1, source_target_pairs={{0,4},{2,6},{4,0},{6,2},{8,12},{10,14},{12,8},{14,10},{1,5},{3,7},... | collective-permute-start | bytes 393224 | tf_op jit(solution)/shard_map/ppermute | solution.py:32
  8.9 0.4 collective-permute-start.5
  9.3 2.3 %collective-permute-start = (bf16[256,256]{1,0:T(8,128)(2,1)S(1)}, bf16[256,256]{1,0:T(8,128)(2,1)S(1)}, u32[]{:S(2)}, u32[]{:S(2)}) collective-permute-start(bf16[256,256]{1,0:T(8,128)(2,1)S(1)} %shard_map.123.refs_0_), channel_id=1, source_target_pairs={{0,14},{2,12},{4,10},{6,8},{8,6},{10,4},{12,2},{14,0},{1,15},{3,13... | collective-permute-start | bytes 393224 | tf_op jit(solution)/shard_map/ppermute | solution.py:32
  11.6 0.6 %collective-permute-done.1.refs_2_ = bf16[256,256]{1,0:T(8,128)(2,1)S(1)} collective-permute-done((bf16[256,256]{1,0:T(8,128)(2,1)S(1)}, bf16[256,256]{1,0:T(8,128)(2,1)S(1)}, u32[]{:S(2)}, u32[]{:S(2)}) %collective-permute-start.1) | collective-permute-done | bytes 131104 | tf_op jit(solution)/shard_map/ppermute | solution.py:32
  12.2 0.8 %collective-permute-start.2 = (bf16[256,256]{1,0:T(8,128)(2,1)S(1)}, bf16[256,256]{1,0:T(8,128)(2,1)S(1)}, u32[]{:S(2)}, u32[]{:S(2)}) collective-permute-start(bf16[256,256]{1,0:T(8,128)(2,1)S(1)} %collective-permute-done.1.refs_2_), channel_id=1, source_target_pairs={{0,4},{2,6},{4,0},{6,2},{8,12},{10,14},{12,8},{14,10},{1,5},{3,7},... | collective-permute-start | bytes 393224 | tf_op jit(solution)/shard_map/ppermute | solution.py:32
  12.9 0.0 collective-permute-done.6.refs_1_
  12.9 1.5 %collective-permute-start.3 = (bf16[256,256]{1,0:T(8,128)(2,1)S(1)}, bf16[256,256]{1,0:T(8,128)(2,1)S(1)}, u32[]{:S(2)}, u32[]{:S(2)}) collective-permute-start(bf16[256,256]{1,0:T(8,128)(2,1)S(1)} %collective-permute-done.1.refs_2_), channel_id=1, source_target_pairs={{0,2},{2,0},{4,6},{6,4},{8,10},{10,8},{12,14},{14,12},{1,3},{3,1},... | collective-permute-start | bytes 393224 | tf_op jit(solution)/shard_map/ppermute | solution.py:32
  14.5 1.8 %shard_map.122 = (bf16[8,2,32,256]{3,2,1,0:T(8,128)(2,1)S(1)}, bf16[2,512,384]{2,1,0:T(8,128)(2,1)S(1)}, f32[5,256,128]{2,1,0:T(8,128)S(1)}, f32[256,256]{1,0:T(...) custom-call(s32[2,8]{1,0:T(2,128)} %refs_0_.1, bf16[2,8,32,256]{3,2,1,0:T(8,128)(2,1)} %refs_1_.1, ...), custom_call_target="tpu_custom_call" | custom-call | bytes 1051712 | tf_op jit(solution)/shard_map/pallas_call | solution.py:269
  16.3 0.0 copy-start.3
  16.3 0.7 %copy-done.3 = s32[2,2]{1,0:T(2,128)S(1)} copy-done((s32[2,2]{1,0:T(2,128)S(1)}, s32[2,2]{1,0:T(2,128)}, u32[]{:S(2)}) %copy-start.3) | copy-done | bytes 40
  17.0 0.8 %shard_map.124.refs_2_ = f32[2,2,256,256]{3,2,1,0:T(8,128)S(1)} custom-call(s32[2,2]{1,0:T(2,128)S(1)} %copy-done.3, bf16[8,2,32,256]{3,2,1,0:T(8,128)(2,1)S(1)} %get-tuple-element.24.v_ref, bf16[2,512,384]{2,1,0:T(8,128)(2,1)S(1)} %get-tuple-element.25.u_ref, bf16[2,2,2,256,256]{4,3,2,1,0:T(8,128)(2,1)S(1)} %copy-done, ...), custom_call_target="tpu_custom_call" | custom-call | flops 75497472 | bytes 2490384 | tf_op jit(solution)/shard_map/pallas_call | solution.py:269
  17.8 0.0 collective-permute-done.4.refs_0_
  17.8 2.2 %collective-permute-done.5.refs_1_ = bf16[256,256]{1,0:T(8,128)(2,1)S(1)} collective-permute-done((bf16[256,256]{1,0:T(8,128)(2,1)S(1)}, bf16[256,256]{1,0:T(8,128)(2,1)S(1)}, u32[]{:S(2)}, u32[]{:S(2)}) %collective-permute-start.5) | collective-permute-done | bytes 131104 | tf_op jit(solution)/shard_map/ppermute | solution.py:32
  20.0 0.7 %shard_map.125.refs_3_ = f32[2,2,256,256]{3,2,1,0:T(8,128)S(1)} custom-call(s32[2,2]{1,0:T(2,128)S(1)} %copy-done.3, bf16[8,2,32,256]{3,2,1,0:T(8,128)(2,1)S(1)} %get-tuple-element.24.v_ref, bf16[2,512,384]{2,1,0:T(8,128)(2,1)S(1)} %get-tuple-element.25.u_ref, bf16[2,2,2,256,256]{4,3,2,1,0:T(8,128)(2,1)S(1)} %copy-done, ...), custom_call_target="tpu_custom_call" | custom-call | flops 50331648 | bytes 3407888 | tf_op jit(solution)/shard_map/pallas_call | solution.py:269
  20.7 0.2 collective-permute-done.refs_0_
  20.9 1.2 %collective-permute-done.2.refs_1_ = bf16[256,256]{1,0:T(8,128)(2,1)S(1)} collective-permute-done((bf16[256,256]{1,0:T(8,128)(2,1)S(1)}, bf16[256,256]{1,0:T(8,128)(2,1)S(1)}, u32[]{:S(2)}, u32[]{:S(2)}) %collective-permute-start.2) | collective-permute-done | bytes 131104 | tf_op jit(solution)/shard_map/ppermute | solution.py:32
  22.1 0.1 collective-permute-done.3.refs_2_
  22.1 0.5 %shard_map.127 = bf16[2,256,256]{2,1,0:T(8,128)(2,1)S(1)} custom-call(s32[2,2]{1,0:T(2,128)S(1)} %copy-done.3, bf16[8,2,32,256]{3,2,1,0:T(8,128)(2,1)S(1)} %get-tuple-element.24.v_ref, bf16[2,512,384]{2,1,0:T(8,128)(2,1)S(1)} %get-tuple-element.25.u_ref, bf16[2,2,2,256,256]{4,3,2,1,0:T(8,128)(2,1)S(1)} %copy-done, ...), custom_call_target="tpu_custom_call" | custom-call | flops 37748736 | bytes 3538960 | tf_op jit(solution)/shard_map/pallas_call | solution.py:269
  22.6 0.0 copy-start.1
  22.6 0.1 collective-permute-start.7
  22.7 0.5 %shard_map.126.own = f32[2,256,256]{2,1,0:T(8,128)S(1)} custom-call(s32[2,2]{1,0:T(2,128)S(1)} %copy-done.3, bf16[8,2,32,256]{3,2,1,0:T(8,128)(2,1)S(1)} %get-tuple-element.24.v_ref, bf16[2,512,384]{2,1,0:T(8,128)(2,1)S(1)} %get-tuple-element.25.u_ref, bf16[2,2,2,256,256]{4,3,2,1,0:T(8,128)(2,1)S(1)} %copy-done, ...), custom_call_target="tpu_custom_call" | custom-call | flops 37748736 | bytes 3538960 | tf_op jit(solution)/shard_map/pallas_call | solution.py:269
  23.3 1.0 %collective-permute-done.7.other = bf16[2,256,256]{2,1,0:T(8,128)(2,1)S(1)} collective-permute-done((bf16[2,256,256]{2,1,0:T(8,128)(2,1)S(1)}, bf16[2,256,256]{2,1,0:T(8,128)(2,1)S(1)}, u32[]{:S(2)}, u32[]{:S(2)}) %collective-permute-start.7) | collective-permute-done | bytes 262176 | tf_op jit(solution)/shard_map/ppermute | solution.py:369
  24.3 1.0 %shard_map.128 = (f32[256,256]{1,0:T(8,128)S(1)}, f32[256,256]{1,0:T(8,128)S(1)}, f32[256,256]{1,0:T(8,128)S(1)}, f32[256,256]{1,0:T(8,128)S(1)}, bf16[256,256]{1,0:T(8,128)(2,1)S(1)}) custom-call(f32[2,256,256]{2,1,0:T(8,128)S(1)} %shard_map.126.own, bf16[2,256,256]{2,1,0:T(8,128)(2,1)S(1)} %collective-permute-done.7.other, ...), custom_call_target="tpu_custom_call" | custom-call | flops 13107200 | bytes 2490368 | tf_op jit(solution)/shard_map/pallas_call | solution.py:269
  25.3 1.0 %collective-permute-start.9 = (bf16[256,256]{1,0:T(8,128)(2,1)S(1)}, bf16[256,256]{1,0:T(8,128)(2,1)S(1)}, u32[]{:S(2)}, u32[]{:S(2)}) collective-permute-start(bf16[256,256]{1,0:T(8,128)(2,1)S(1)} %get-tuple-element.39.refs_0_), channel_id=1, source_target_pairs={{0,8},{2,10},{4,12},{6,14},{8,0},{10,2},{12,4},{14,6},{1,9},{3,11}... | collective-permute-start | bytes 393224 | tf_op jit(solution)/shard_map/ppermute | solution.py:32
  26.3 0.7 %collective-permute-start.14 = (bf16[256,256]{1,0:T(8,128)(2,1)S(1)}, bf16[256,256]{1,0:T(8,128)(2,1)S(1)}, u32[]{:S(2)}, u32[]{:S(2)}) collective-permute-start(bf16[256,256]{1,0:T(8,128)(2,1)S(1)} %get-tuple-element.39.refs_0_), channel_id=1, source_target_pairs={{0,2},{2,0},{4,6},{6,4},{8,10},{10,8},{12,14},{14,12},{1,3},{3,1},... | collective-permute-start | bytes 393224 | tf_op jit(solution)/shard_map/ppermute | solution.py:32
  27.0 2.9 %collective-permute-start.12 = (bf16[256,256]{1,0:T(8,128)(2,1)S(1)}, bf16[256,256]{1,0:T(8,128)(2,1)S(1)}, u32[]{:S(2)}, u32[]{:S(2)}) collective-permute-start(bf16[256,256]{1,0:T(8,128)(2,1)S(1)} %get-tuple-element.39.refs_0_), channel_id=1, source_target_pairs={{0,4},{2,6},{4,0},{6,2},{8,12},{10,14},{12,8},{14,10},{1,5},{3,7},... | collective-permute-start | bytes 393224 | tf_op jit(solution)/shard_map/ppermute | solution.py:32
  29.8 0.0 collective-permute-start.13
  29.8 2.7 %collective-permute-start.8 = (bf16[256,256]{1,0:T(8,128)(2,1)S(1)}, bf16[256,256]{1,0:T(8,128)(2,1)S(1)}, u32[]{:S(2)}, u32[]{:S(2)}) collective-permute-start(bf16[256,256]{1,0:T(8,128)(2,1)S(1)} %get-tuple-element.39.refs_0_), channel_id=1, source_target_pairs={{0,14},{2,12},{4,10},{6,8},{8,6},{10,4},{12,2},{14,0},{1,15},{3,13... | collective-permute-start | bytes 393224 | tf_op jit(solution)/shard_map/ppermute | solution.py:32
  32.6 2.0 %collective-permute-done.9.refs_2_ = bf16[256,256]{1,0:T(8,128)(2,1)S(1)} collective-permute-done((bf16[256,256]{1,0:T(8,128)(2,1)S(1)}, bf16[256,256]{1,0:T(8,128)(2,1)S(1)}, u32[]{:S(2)}, u32[]{:S(2)}) %collective-permute-start.9) | collective-permute-done | bytes 131104 | tf_op jit(solution)/shard_map/ppermute | solution.py:32
  34.5 0.0 collective-permute-start.10
  34.5 0.0 collective-permute-done.14.refs_1_
  34.6 1.5 %collective-permute-start.11 = (bf16[256,256]{1,0:T(8,128)(2,1)S(1)}, bf16[256,256]{1,0:T(8,128)(2,1)S(1)}, u32[]{:S(2)}, u32[]{:S(2)}) collective-permute-start(bf16[256,256]{1,0:T(8,128)(2,1)S(1)} %collective-permute-done.9.refs_2_), channel_id=1, source_target_pairs={{0,2},{2,0},{4,6},{6,4},{8,10},{10,8},{12,14},{14,12},{1,3},{3,1},... | collective-permute-start | bytes 393224 | tf_op jit(solution)/shard_map/ppermute | solution.py:32
  36.1 0.1 shard_map.129
  36.2 0.8 %shard_map.130.refs_2_ = f32[2,2,256,256]{3,2,1,0:T(8,128)S(1)} custom-call(s32[2,2]{1,0:T(2,128)S(1)} %copy-done.3, bf16[8,2,32,256]{3,2,1,0:T(8,128)(2,1)S(1)} %get-tuple-element.24.v_ref, bf16[2,512,384]{2,1,0:T(8,128)(2,1)S(1)} %get-tuple-element.25.u_ref, bf16[2,2,2,256,256]{4,3,2,1,0:T(8,128)(2,1)S(1)} %copy-done, ...), custom_call_target="tpu_custom_call" | custom-call | flops 75497472 | bytes 2490384 | tf_op jit(solution)/shard_map/pallas_call | solution.py:269
  37.0 0.6 %collective-permute-done.12.refs_0_ = bf16[256,256]{1,0:T(8,128)(2,1)S(1)} collective-permute-done((bf16[256,256]{1,0:T(8,128)(2,1)S(1)}, bf16[256,256]{1,0:T(8,128)(2,1)S(1)}, u32[]{:S(2)}, u32[]{:S(2)}) %collective-permute-start.12) | collective-permute-done | bytes 131104 | tf_op jit(solution)/shard_map/ppermute | solution.py:32
  37.6 3.9 %collective-permute-done.13.refs_1_ = bf16[256,256]{1,0:T(8,128)(2,1)S(1)} collective-permute-done((bf16[256,256]{1,0:T(8,128)(2,1)S(1)}, bf16[256,256]{1,0:T(8,128)(2,1)S(1)}, u32[]{:S(2)}, u32[]{:S(2)}) %collective-permute-start.13) | collective-permute-done | bytes 131104 | tf_op jit(solution)/shard_map/ppermute | solution.py:32
  41.5 0.7 %shard_map.131.refs_3_ = f32[2,2,256,256]{3,2,1,0:T(8,128)S(1)} custom-call(s32[2,2]{1,0:T(2,128)S(1)} %copy-done.3, bf16[8,2,32,256]{3,2,1,0:T(8,128)(2,1)S(1)} %get-tuple-element.24.v_ref, bf16[2,512,384]{2,1,0:T(8,128)(2,1)S(1)} %get-tuple-element.25.u_ref, bf16[2,2,2,256,256]{4,3,2,1,0:T(8,128)(2,1)S(1)} %copy-done, ...), custom_call_target="tpu_custom_call" | custom-call | flops 50331648 | bytes 3407888 | tf_op jit(solution)/shard_map/pallas_call | solution.py:269
  42.3 0.2 collective-permute-done.8.refs_0_
  42.5 1.7 %collective-permute-done.10.refs_1_ = bf16[256,256]{1,0:T(8,128)(2,1)S(1)} collective-permute-done((bf16[256,256]{1,0:T(8,128)(2,1)S(1)}, bf16[256,256]{1,0:T(8,128)(2,1)S(1)}, u32[]{:S(2)}, u32[]{:S(2)}) %collective-permute-start.10) | collective-permute-done | bytes 131104 | tf_op jit(solution)/shard_map/ppermute | solution.py:32
  44.2 0.1 collective-permute-done.11.refs_2_
  44.3 0.5 %shard_map.133 = bf16[2,256,256]{2,1,0:T(8,128)(2,1)S(1)} custom-call(s32[2,2]{1,0:T(2,128)S(1)} %copy-done.3, bf16[8,2,32,256]{3,2,1,0:T(8,128)(2,1)S(1)} %get-tuple-element.24.v_ref, bf16[2,512,384]{2,1,0:T(8,128)(2,1)S(1)} %get-tuple-element.25.u_ref, bf16[2,2,2,256,256]{4,3,2,1,0:T(8,128)(2,1)S(1)} %copy-done, ...), custom_call_target="tpu_custom_call" | custom-call | flops 37748736 | bytes 3538960 | tf_op jit(solution)/shard_map/pallas_call | solution.py:269
  44.8 0.1 collective-permute-start.15
  44.9 0.5 %shard_map.132.own = f32[2,256,256]{2,1,0:T(8,128)S(1)} custom-call(s32[2,2]{1,0:T(2,128)S(1)} %copy-done.3, bf16[8,2,32,256]{3,2,1,0:T(8,128)(2,1)S(1)} %get-tuple-element.24.v_ref, bf16[2,512,384]{2,1,0:T(8,128)(2,1)S(1)} %get-tuple-element.25.u_ref, bf16[2,2,2,256,256]{4,3,2,1,0:T(8,128)(2,1)S(1)} %copy-done, ...), custom_call_target="tpu_custom_call" | custom-call | flops 37748736 | bytes 3538960 | tf_op jit(solution)/shard_map/pallas_call | solution.py:269
  45.4 1.0 %collective-permute-done.15.other = bf16[2,256,256]{2,1,0:T(8,128)(2,1)S(1)} collective-permute-done((bf16[2,256,256]{2,1,0:T(8,128)(2,1)S(1)}, bf16[2,256,256]{2,1,0:T(8,128)(2,1)S(1)}, u32[]{:S(2)}, u32[]{:S(2)}) %collective-permute-start.15) | collective-permute-done | bytes 262176 | tf_op jit(solution)/shard_map/ppermute | solution.py:369
  46.4 1.8 %shard_map.134 = (f32[256,256]{1,0:T(8,128)}, f32[256,256]{1,0:T(8,128)}) custom-call(f32[2,256,256]{2,1,0:T(8,128)S(1)} %shard_map.132.own, bf16[2,256,256]{2,1,0:T(8,128)(2,1)S(1)} %collective-permute-done.15.other, f32[256,256]{1,0:T(8,128)S(1)} %get-tuple-element.40.weight, f32[256,256]{1,0:T(8,128)S(1)} %get-tuple-element.41.unweight, ...), custom_call_target="tpu_custom_call" | custom-call | flops 13107200 | bytes 3538944 | tf_op jit(solution)/shard_map/pallas_call | solution.py:269
  (5 shorter events, 0.0 us)
Async XLA Ops:
  0.6 15.7 %copy-start = (bf16[2,2,2,256,256]{4,3,2,1,0:T(8,128)(2,1)S(1)}, bf16[2,2,2,256,256]{4,3,2,1,0:T(8,128)(2,1)}, u32[]{:S(2)}) copy-start(bf16[2,2,2,256,256]{4,3,2,1,0:T(8,128)(2,1)} %d_ref.15) | copy-start | bytes 3145732
  1.7 10.5 %collective-permute-start.1 = (bf16[256,256]{1,0:T(8,128)(2,1)S(1)}, bf16[256,256]{1,0:T(8,128)(2,1)S(1)}, u32[]{:S(2)}, u32[]{:S(2)}) collective-permute-start(bf16[256,256]{1,0:T(8,128)(2,1)S(1)} %shard_map.123.refs_0_), channel_id=1, source_target_pairs={{0,8},{2,10},{4,12},{6,14},{8,0},{10,2},{12,4},{14,6},{1,9},{3,11}... | collective-permute-start | bytes 393224 | tf_op jit(solution)/shard_map/ppermute | solution.py:32
  5.8 7.2 %collective-permute-start.6 = (bf16[256,256]{1,0:T(8,128)(2,1)S(1)}, bf16[256,256]{1,0:T(8,128)(2,1)S(1)}, u32[]{:S(2)}, u32[]{:S(2)}) collective-permute-start(bf16[256,256]{1,0:T(8,128)(2,1)S(1)} %shard_map.123.refs_0_), channel_id=1, source_target_pairs={{0,2},{2,0},{4,6},{6,4},{8,10},{10,8},{12,14},{14,12},{1,3},{3,1},... | collective-permute-start | bytes 393224 | tf_op jit(solution)/shard_map/ppermute | solution.py:32
  7.3 10.5 %collective-permute-start.4 = (bf16[256,256]{1,0:T(8,128)(2,1)S(1)}, bf16[256,256]{1,0:T(8,128)(2,1)S(1)}, u32[]{:S(2)}, u32[]{:S(2)}) collective-permute-start(bf16[256,256]{1,0:T(8,128)(2,1)S(1)} %shard_map.123.refs_0_), channel_id=1, source_target_pairs={{0,4},{2,6},{4,0},{6,2},{8,12},{10,14},{12,8},{14,10},{1,5},{3,7},... | collective-permute-start | bytes 393224 | tf_op jit(solution)/shard_map/ppermute | solution.py:32
  8.9 11.1 %collective-permute-start.5 = (bf16[256,256]{1,0:T(8,128)(2,1)S(1)}, bf16[256,256]{1,0:T(8,128)(2,1)S(1)}, u32[]{:S(2)}, u32[]{:S(2)}) collective-permute-start(bf16[256,256]{1,0:T(8,128)(2,1)S(1)} %shard_map.123.refs_0_), channel_id=1, source_target_pairs={{0,6},{2,4},{4,2},{6,0},{8,14},{10,12},{12,10},{14,8},{1,7},{3,5},... | collective-permute-start | bytes 393224 | tf_op jit(solution)/shard_map/ppermute | solution.py:32
  9.3 11.6 %collective-permute-start = (bf16[256,256]{1,0:T(8,128)(2,1)S(1)}, bf16[256,256]{1,0:T(8,128)(2,1)S(1)}, u32[]{:S(2)}, u32[]{:S(2)}) collective-permute-start(bf16[256,256]{1,0:T(8,128)(2,1)S(1)} %shard_map.123.refs_0_), channel_id=1, source_target_pairs={{0,14},{2,12},{4,10},{6,8},{8,6},{10,4},{12,2},{14,0},{1,15},{3,13... | collective-permute-start | bytes 393224 | tf_op jit(solution)/shard_map/ppermute | solution.py:32
  12.2 9.9 %collective-permute-start.2 = (bf16[256,256]{1,0:T(8,128)(2,1)S(1)}, bf16[256,256]{1,0:T(8,128)(2,1)S(1)}, u32[]{:S(2)}, u32[]{:S(2)}) collective-permute-start(bf16[256,256]{1,0:T(8,128)(2,1)S(1)} %collective-permute-done.1.refs_2_), channel_id=1, source_target_pairs={{0,4},{2,6},{4,0},{6,2},{8,12},{10,14},{12,8},{14,10},{1,5},{3,7},... | collective-permute-start | bytes 393224 | tf_op jit(solution)/shard_map/ppermute | solution.py:32
  12.9 9.2 %collective-permute-start.3 = (bf16[256,256]{1,0:T(8,128)(2,1)S(1)}, bf16[256,256]{1,0:T(8,128)(2,1)S(1)}, u32[]{:S(2)}, u32[]{:S(2)}) collective-permute-start(bf16[256,256]{1,0:T(8,128)(2,1)S(1)} %collective-permute-done.1.refs_2_), channel_id=1, source_target_pairs={{0,2},{2,0},{4,6},{6,4},{8,10},{10,8},{12,14},{14,12},{1,3},{3,1},... | collective-permute-start | bytes 393224 | tf_op jit(solution)/shard_map/ppermute | solution.py:32
  16.3 0.7 %copy-start.3 = (s32[2,2]{1,0:T(2,128)S(1)}, s32[2,2]{1,0:T(2,128)}, u32[]{:S(2)}) copy-start(s32[2,2]{1,0:T(2,128)} %near_ref.15) | copy-start | bytes 52
  22.6 1.6 %copy-start.1 = (f32[256,256]{1,0:T(8,128)S(1)}, f32[256,256]{1,0:T(8,128)}, u32[]{:S(2)}) copy-start(f32[256,256]{1,0:T(8,128)} %tau.3) | copy-start | bytes 786436
  22.6 1.6 %collective-permute-start.7 = (bf16[2,256,256]{2,1,0:T(8,128)(2,1)S(1)}, bf16[2,256,256]{2,1,0:T(8,128)(2,1)S(1)}, u32[]{:S(2)}, u32[]{:S(2)}) collective-permute-start(bf16[2,256,256]{2,1,0:T(8,128)(2,1)S(1)} %shard_map.127), channel_id=1, source_target_pairs={{0,1},{1,0},{2,3},{3,2},{4,5},{5,4},{6,7},{7,6},{8,9},{9,8},{10,11... | collective-permute-start | bytes 786440 | tf_op jit(solution)/shard_map/ppermute | solution.py:369
  24.3 11.8 %copy-start.2 = (f32[256,256]{1,0:T(8,128)S(1)}, f32[256,256]{1,0:T(8,128)}, u32[]{:S(2)}) copy-start(f32[256,256]{1,0:T(8,128)} %state.1) | copy-start | bytes 786436
  25.3 9.2 %collective-permute-start.9 = (bf16[256,256]{1,0:T(8,128)(2,1)S(1)}, bf16[256,256]{1,0:T(8,128)(2,1)S(1)}, u32[]{:S(2)}, u32[]{:S(2)}) collective-permute-start(bf16[256,256]{1,0:T(8,128)(2,1)S(1)} %get-tuple-element.39.refs_0_), channel_id=1, source_target_pairs={{0,8},{2,10},{4,12},{6,14},{8,0},{10,2},{12,4},{14,6},{1,9},{3,11}... | collective-permute-start | bytes 393224 | tf_op jit(solution)/shard_map/ppermute | solution.py:32
  26.3 8.2 %collective-permute-start.14 = (bf16[256,256]{1,0:T(8,128)(2,1)S(1)}, bf16[256,256]{1,0:T(8,128)(2,1)S(1)}, u32[]{:S(2)}, u32[]{:S(2)}) collective-permute-start(bf16[256,256]{1,0:T(8,128)(2,1)S(1)} %get-tuple-element.39.refs_0_), channel_id=1, source_target_pairs={{0,2},{2,0},{4,6},{6,4},{8,10},{10,8},{12,14},{14,12},{1,3},{3,1},... | collective-permute-start | bytes 393224 | tf_op jit(solution)/shard_map/ppermute | solution.py:32
  27.0 10.7 %collective-permute-start.12 = (bf16[256,256]{1,0:T(8,128)(2,1)S(1)}, bf16[256,256]{1,0:T(8,128)(2,1)S(1)}, u32[]{:S(2)}, u32[]{:S(2)}) collective-permute-start(bf16[256,256]{1,0:T(8,128)(2,1)S(1)} %get-tuple-element.39.refs_0_), channel_id=1, source_target_pairs={{0,4},{2,6},{4,0},{6,2},{8,12},{10,14},{12,8},{14,10},{1,5},{3,7},... | collective-permute-start | bytes 393224 | tf_op jit(solution)/shard_map/ppermute | solution.py:32
  29.8 11.7 %collective-permute-start.13 = (bf16[256,256]{1,0:T(8,128)(2,1)S(1)}, bf16[256,256]{1,0:T(8,128)(2,1)S(1)}, u32[]{:S(2)}, u32[]{:S(2)}) collective-permute-start(bf16[256,256]{1,0:T(8,128)(2,1)S(1)} %get-tuple-element.39.refs_0_), channel_id=1, source_target_pairs={{0,6},{2,4},{4,2},{6,0},{8,14},{10,12},{12,10},{14,8},{1,7},{3,5},... | collective-permute-start | bytes 393224 | tf_op jit(solution)/shard_map/ppermute | solution.py:32
  29.8 12.6 %collective-permute-start.8 = (bf16[256,256]{1,0:T(8,128)(2,1)S(1)}, bf16[256,256]{1,0:T(8,128)(2,1)S(1)}, u32[]{:S(2)}, u32[]{:S(2)}) collective-permute-start(bf16[256,256]{1,0:T(8,128)(2,1)S(1)} %get-tuple-element.39.refs_0_), channel_id=1, source_target_pairs={{0,14},{2,12},{4,10},{6,8},{8,6},{10,4},{12,2},{14,0},{1,15},{3,13... | collective-permute-start | bytes 393224 | tf_op jit(solution)/shard_map/ppermute | solution.py:32
  34.5 9.7 %collective-permute-start.10 = (bf16[256,256]{1,0:T(8,128)(2,1)S(1)}, bf16[256,256]{1,0:T(8,128)(2,1)S(1)}, u32[]{:S(2)}, u32[]{:S(2)}) collective-permute-start(bf16[256,256]{1,0:T(8,128)(2,1)S(1)} %collective-permute-done.9.refs_2_), channel_id=1, source_target_pairs={{0,4},{2,6},{4,0},{6,2},{8,12},{10,14},{12,8},{14,10},{1,5},{3,7},... | collective-permute-start | bytes 393224 | tf_op jit(solution)/shard_map/ppermute | solution.py:32
  34.6 9.7 %collective-permute-start.11 = (bf16[256,256]{1,0:T(8,128)(2,1)S(1)}, bf16[256,256]{1,0:T(8,128)(2,1)S(1)}, u32[]{:S(2)}, u32[]{:S(2)}) collective-permute-start(bf16[256,256]{1,0:T(8,128)(2,1)S(1)} %collective-permute-done.9.refs_2_), channel_id=1, source_target_pairs={{0,2},{2,0},{4,6},{6,4},{8,10},{10,8},{12,14},{14,12},{1,3},{3,1},... | collective-permute-start | bytes 393224 | tf_op jit(solution)/shard_map/ppermute | solution.py:32
  44.8 1.6 %collective-permute-start.15 = (bf16[2,256,256]{2,1,0:T(8,128)(2,1)S(1)}, bf16[2,256,256]{2,1,0:T(8,128)(2,1)S(1)}, u32[]{:S(2)}, u32[]{:S(2)}) collective-permute-start(bf16[2,256,256]{2,1,0:T(8,128)(2,1)S(1)} %shard_map.133), channel_id=1, source_target_pairs={{0,1},{1,0},{2,3},{3,2},{4,5},{5,4},{6,7},{7,6},{8,9},{9,8},{10,11... | collective-permute-start | bytes 786440 | tf_op jit(solution)/shard_map/ppermute | solution.py:369

commit v21 on v19

--- a/solution.py
+++ b/solution.py
@@ -162,13 +162,17 @@
     return rough * (2.0 - value * rough)
 
 
-def sinh_cosh(value):
+def rough_inverse(value):
+    return pl.reciprocal(value, approx=True)
+
+
+def scaled_sinh_cosh(value, scale):
     grown = jnp.exp(value)
-    shrunk = inverse(grown)
+    half = 0.5 * scale
+    up, down = half * grown, half * inverse(grown)
     square = value * value
-    small = value * (1.0 + square * (1 / 6 + square * (1 / 120)))
-    sinh = jnp.where(square < 0.25, small, 0.5 * (grown - shrunk))
-    return sinh, 0.5 * (grown + shrunk)
+    small = scale * value * (1.0 + square * (1 / 6 + square * (1 / 120)))
+    return jnp.where(square < 0.25, small, up - down), up + down
 
 
 def friction(shear, normal, weight, unweight, tau_load, sigma_base, a_wide):
@@ -178,12 +182,11 @@
     double = 2.0 * damping * weight
     drive = size * unweight * (0.5 / damping)
     square = drive * drive + 1.0
-    slope = jnp.minimum(size * inverse(stiff), jnp.log(drive + square * lax.rsqrt(square)))
+    slope = jnp.minimum(size * rough_inverse(stiff), jnp.log(drive + square * lax.rsqrt(square)))
     for newton_step in range(NEWTON):
-        sinh, cosh = sinh_cosh(slope)
-        excess = stiff * slope + double * sinh - size
-        slope = slope - excess * inverse(stiff + double * cosh)
-    rate = 2.0 * weight * sinh_cosh(slope)[0]
+        sinh, cosh = scaled_sinh_cosh(slope, double)
+        slope = slope - (stiff * slope + sinh - size) * rough_inverse(stiff + cosh)
+    rate = scaled_sinh_cosh(slope, double)[0] * (1.0 / damping)
     return jnp.where(tau < 0.0, -rate, rate)
 
 

time: 47 us -> 46.9 us (level)
  no operation moved by 1% of the time
where the time goes in v21:
time: 46.9 us; the launch traced here: 46.8 us
  starting transfers between devices  20.1 us (43%)
  waiting for transfers between devices  15.5 us (33%)
  Pallas kernels  9.65 us (21%)
  between operations  0.77 us (2%)
  local copies, waits for them, and re-layouts  0.68 us (1%)
    ppermute x14, starting transfers between devices, swapped(): lax.ppermute(data, 'row', [(row, row ^ mask) for row in range(count)])  20 us
    ppermute x14, waiting for transfers between devices, swapped(): lax.ppermute(data, 'row', [(row, row ^ mask) for row in range(count)])  13.6 us
    pallas_call x11, Pallas kernels, on_core(): pl.pallas_call(kernel, out_shape=outs, in_specs=[hbm] * len(far) + [vmem]...  9.65 us
    ppermute x2, waiting for transfers between devices, lattice(): lax.ppermute(add(blocks[early:], early, 1, sums, narrow), 'col', swap)  1.89 us
  transfers between devices with their start and end apart: 16, of which 8 were waited for; matrix products, arithmetic and copies ran while one was open for 0% of the time, Pallas kernels for 10%

profile of v21, /device:TPU:0, one launch (start us, length us, event | category | flops | bytes accessed | tf_op | source)
XLA Modules:
  0.0 46.8 jit_solution(12997695636514902867)
XLA Ops:
  0.6 0.0 copy-start
  0.6 1.0 %shard_map.123.refs_0_ = bf16[256,256]{1,0:T(8,128)(2,1)S(1)} custom-call(f32[256,256]{1,0:T(8,128)} %wide_ref.1), custom_call_target="tpu_custom_call" | custom-call | bytes 262144 | tf_op jit(solution)/shard_map/pallas_call | solution.py:260
  1.7 4.1 %collective-permute-start.1 = (bf16[256,256]{1,0:T(8,128)(2,1)S(1)}, bf16[256,256]{1,0:T(8,128)(2,1)S(1)}, u32[]{:S(2)}, u32[]{:S(2)}) collective-permute-start(bf16[256,256]{1,0:T(8,128)(2,1)S(1)} %shard_map.123.refs_0_), channel_id=1, source_target_pairs={{0,8},{2,10},{4,12},{6,14},{8,0},{10,2},{12,4},{14,6},{1,9},{3,11}... | collective-permute-start | bytes 393224 | tf_op jit(solution)/shard_map/ppermute | solution.py:31
  5.8 1.6 %collective-permute-start.6 = (bf16[256,256]{1,0:T(8,128)(2,1)S(1)}, bf16[256,256]{1,0:T(8,128)(2,1)S(1)}, u32[]{:S(2)}, u32[]{:S(2)}) collective-permute-start(bf16[256,256]{1,0:T(8,128)(2,1)S(1)} %shard_map.123.refs_0_), channel_id=1, source_target_pairs={{0,4},{2,6},{4,0},{6,2},{8,12},{10,14},{12,8},{14,10},{1,5},{3,7},... | collective-permute-start | bytes 393224 | tf_op jit(solution)/shard_map/ppermute | solution.py:31
  7.4 1.5 %collective-permute-start.5 = (bf16[256,256]{1,0:T(8,128)(2,1)S(1)}, bf16[256,256]{1,0:T(8,128)(2,1)S(1)}, u32[]{:S(2)}, u32[]{:S(2)}) collective-permute-start(bf16[256,256]{1,0:T(8,128)(2,1)S(1)} %shard_map.123.refs_0_), channel_id=1, source_target_pairs={{0,2},{2,0},{4,6},{6,4},{8,10},{10,8},{12,14},{14,12},{1,3},{3,1},... | collective-permute-start | bytes 393224 | tf_op jit(solution)/shard_map/ppermute | solution.py:31
  8.9 0.4 collective-permute-start
  9.3 2.9 %collective-permute-done.1.refs_2_ = bf16[256,256]{1,0:T(8,128)(2,1)S(1)} collective-permute-done((bf16[256,256]{1,0:T(8,128)(2,1)S(1)}, bf16[256,256]{1,0:T(8,128)(2,1)S(1)}, u32[]{:S(2)}, u32[]{:S(2)}) %collective-permute-start.1) | collective-permute-done | bytes 131104 | tf_op jit(solution)/shard_map/ppermute | solution.py:31
  12.2 1.6 %collective-permute-start.4 = (bf16[256,256]{1,0:T(8,128)(2,1)S(1)}, bf16[256,256]{1,0:T(8,128)(2,1)S(1)}, u32[]{:S(2)}, u32[]{:S(2)}) collective-permute-start(bf16[256,256]{1,0:T(8,128)(2,1)S(1)} %collective-permute-done.1.refs_2_), channel_id=1, source_target_pairs={{0,6},{2,4},{4,2},{6,0},{8,14},{10,12},{12,10},{14,8},{1,7},{3,5},... | collective-permute-start | bytes 393224 | tf_op jit(solution)/shard_map/ppermute | solution.py:31
  13.8 0.5 %collective-permute-start.3 = (bf16[256,256]{1,0:T(8,128)(2,1)S(1)}, bf16[256,256]{1,0:T(8,128)(2,1)S(1)}, u32[]{:S(2)}, u32[]{:S(2)}) collective-permute-start(bf16[256,256]{1,0:T(8,128)(2,1)S(1)} %collective-permute-done.1.refs_2_), channel_id=1, source_target_pairs={{0,2},{2,0},{4,6},{6,4},{8,10},{10,8},{12,14},{14,12},{1,3},{3,1},... | collective-permute-start | bytes 393224 | tf_op jit(solution)/shard_map/ppermute | solution.py:31
  14.3 0.0 collective-permute-done.6.refs_3_
  14.3 1.4 %collective-permute-start.2 = (bf16[256,256]{1,0:T(8,128)(2,1)S(1)}, bf16[256,256]{1,0:T(8,128)(2,1)S(1)}, u32[]{:S(2)}, u32[]{:S(2)}) collective-permute-start(bf16[256,256]{1,0:T(8,128)(2,1)S(1)} %collective-permute-done.1.refs_2_), channel_id=1, source_target_pairs={{0,4},{2,6},{4,0},{6,2},{8,12},{10,14},{12,8},{14,10},{1,5},{3,7},... | collective-permute-start | bytes 393224 | tf_op jit(solution)/shard_map/ppermute | solution.py:31
  15.7 1.8 %shard_map.122 = (bf16[8,2,32,256]{3,2,1,0:T(8,128)(2,1)S(1)}, bf16[2,512,256]{2,1,0:T(8,128)(2,1)S(1)}, f32[5,256,128]{2,1,0:T(8,128)S(1)}, f32[256,256]{1,0:T(...) custom-call(s32[2,8]{1,0:T(2,128)} %refs_0_.1, bf16[2,8,32,256]{3,2,1,0:T(8,128)(2,1)} %refs_1_.1, ...), custom_call_target="tpu_custom_call" | custom-call | bytes 1051712 | tf_op jit(solution)/shard_map/pallas_call | solution.py:260
  17.4 0.0 collective-permute-done.5.refs_1_
  17.5 0.0 copy-start.3
  17.5 0.7 %copy-done.3 = s32[2,2]{1,0:T(2,128)S(1)} copy-done((s32[2,2]{1,0:T(2,128)S(1)}, s32[2,2]{1,0:T(2,128)}, u32[]{:S(2)}) %copy-start.3) | copy-done | bytes 40
  18.1 0.8 %shard_map.124.refs_4_ = f32[2,2,256,256]{3,2,1,0:T(8,128)S(1)} custom-call(s32[2,2]{1,0:T(2,128)S(1)} %copy-done.3, bf16[8,2,32,256]{3,2,1,0:T(8,128)(2,1)S(1)} %get-tuple-element.27.v_ref, bf16[2,512,256]{2,1,0:T(8,128)(2,1)S(1)} %get-tuple-element.28.u_ref, bf16[2,2,2,256,256]{4,3,2,1,0:T(8,128)(2,1)S(1)} %copy-done, ...), custom_call_target="tpu_custom_call" | custom-call | flops 100663296 | bytes 2359312 | tf_op jit(solution)/shard_map/pallas_call | solution.py:260
  18.9 0.0 collective-permute-done.refs_0_
  18.9 1.0 %collective-permute-done.4.refs_3_ = bf16[256,256]{1,0:T(8,128)(2,1)S(1)} collective-permute-done((bf16[256,256]{1,0:T(8,128)(2,1)S(1)}, bf16[256,256]{1,0:T(8,128)(2,1)S(1)}, u32[]{:S(2)}, u32[]{:S(2)}) %collective-permute-start.4) | collective-permute-done | bytes 131104 | tf_op jit(solution)/shard_map/ppermute | solution.py:31
  19.9 1.9 %collective-permute-done.3.refs_2_ = bf16[256,256]{1,0:T(8,128)(2,1)S(1)} collective-permute-done((bf16[256,256]{1,0:T(8,128)(2,1)S(1)}, bf16[256,256]{1,0:T(8,128)(2,1)S(1)}, u32[]{:S(2)}, u32[]{:S(2)}) %collective-permute-start.3) | collective-permute-done | bytes 131104 | tf_op jit(solution)/shard_map/ppermute | solution.py:31
  21.8 0.0 collective-permute-done.2.refs_1_
  21.8 0.6 %shard_map.126 = bf16[2,256,256]{2,1,0:T(8,128)(2,1)S(1)} custom-call(s32[2,2]{1,0:T(2,128)S(1)} %copy-done.3, bf16[8,2,32,256]{3,2,1,0:T(8,128)(2,1)S(1)} %get-tuple-element.27.v_ref, bf16[2,512,256]{2,1,0:T(8,128)(2,1)S(1)} %get-tuple-element.28.u_ref, bf16[2,2,2,256,256]{4,3,2,1,0:T(8,128)(2,1)S(1)} %copy-done, ...), custom_call_target="tpu_custom_call" | custom-call | flops 50331648 | bytes 3407888 | tf_op jit(solution)/shard_map/pallas_call | solution.py:260
  22.4 0.0 copy-start.1
  22.4 0.1 collective-permute-start.7
  22.5 0.6 %shard_map.125.own = f32[2,256,256]{2,1,0:T(8,128)S(1)} custom-call(s32[2,2]{1,0:T(2,128)S(1)} %copy-done.3, bf16[8,2,32,256]{3,2,1,0:T(8,128)(2,1)S(1)} %get-tuple-element.27.v_ref, bf16[2,512,256]{2,1,0:T(8,128)(2,1)S(1)} %get-tuple-element.28.u_ref, bf16[2,2,2,256,256]{4,3,2,1,0:T(8,128)(2,1)S(1)} %copy-done, ...), custom_call_target="tpu_custom_call" | custom-call | flops 50331648 | bytes 3407888 | tf_op jit(solution)/shard_map/pallas_call | solution.py:260
  23.1 0.9 %collective-permute-done.7.other = bf16[2,256,256]{2,1,0:T(8,128)(2,1)S(1)} collective-permute-done((bf16[2,256,256]{2,1,0:T(8,128)(2,1)S(1)}, bf16[2,256,256]{2,1,0:T(8,128)(2,1)S(1)}, u32[]{:S(2)}, u32[]{:S(2)}) %collective-permute-start.7) | collective-permute-done | bytes 262176 | tf_op jit(solution)/shard_map/ppermute | solution.py:356
  24.0 0.0 copy-done.1
  24.0 1.1 %shard_map.127 = (f32[256,256]{1,0:T(8,128)S(1)}, bf16[256,256]{1,0:T(8,128)(2,1)S(1)}) custom-call(f32[2,256,256]{2,1,0:T(8,128)S(1)} %shard_map.125.own, bf16[2,256,256]{2,1,0:T(8,128)(2,1)S(1)} %collective-permute-done.7.other, f32[256,256]{1,0:T(8,128)S(1)} %get-tuple-element.33.weight, f32[256,256]{1,0:T(8,128)S(1)} %get-tuple-element.34.unweight, ...), custom_call_target="tpu_custom_call" | custom-call | flops 13107200 | bytes 2228224 | tf_op jit(solution)/shard_map/pallas_call | solution.py:260
  25.1 1.9 %collective-permute-start.9 = (bf16[256,256]{1,0:T(8,128)(2,1)S(1)}, bf16[256,256]{1,0:T(8,128)(2,1)S(1)}, u32[]{:S(2)}, u32[]{:S(2)}) collective-permute-start(bf16[256,256]{1,0:T(8,128)(2,1)S(1)} %get-tuple-element.45.refs_0_), channel_id=1, source_target_pairs={{0,8},{2,10},{4,12},{6,14},{8,0},{10,2},{12,4},{14,6},{1,9},{3,11}... | collective-permute-start | bytes 393224 | tf_op jit(solution)/shard_map/ppermute | solution.py:31
  27.0 1.8 %collective-permute-start.14 = (bf16[256,256]{1,0:T(8,128)(2,1)S(1)}, bf16[256,256]{1,0:T(8,128)(2,1)S(1)}, u32[]{:S(2)}, u32[]{:S(2)}) collective-permute-start(bf16[256,256]{1,0:T(8,128)(2,1)S(1)} %get-tuple-element.45.refs_0_), channel_id=1, source_target_pairs={{0,4},{2,6},{4,0},{6,2},{8,12},{10,14},{12,8},{14,10},{1,5},{3,7},... | collective-permute-start | bytes 393224 | tf_op jit(solution)/shard_map/ppermute | solution.py:31
  28.8 0.5 %collective-permute-start.13 = (bf16[256,256]{1,0:T(8,128)(2,1)S(1)}, bf16[256,256]{1,0:T(8,128)(2,1)S(1)}, u32[]{:S(2)}, u32[]{:S(2)}) collective-permute-start(bf16[256,256]{1,0:T(8,128)(2,1)S(1)} %get-tuple-element.45.refs_0_), channel_id=1, source_target_pairs={{0,2},{2,0},{4,6},{6,4},{8,10},{10,8},{12,14},{14,12},{1,3},{3,1},... | collective-permute-start | bytes 393224 | tf_op jit(solution)/shard_map/ppermute | solution.py:31
  29.3 1.2 %collective-permute-start.8 = (bf16[256,256]{1,0:T(8,128)(2,1)S(1)}, bf16[256,256]{1,0:T(8,128)(2,1)S(1)}, u32[]{:S(2)}, u32[]{:S(2)}) collective-permute-start(bf16[256,256]{1,0:T(8,128)(2,1)S(1)} %get-tuple-element.45.refs_0_), channel_id=1, source_target_pairs={{0,6},{2,4},{4,2},{6,0},{8,14},{10,12},{12,10},{14,8},{1,7},{3,5},... | collective-permute-start | bytes 393224 | tf_op jit(solution)/shard_map/ppermute | solution.py:31
  30.5 4.0 %collective-permute-done.9.refs_2_ = bf16[256,256]{1,0:T(8,128)(2,1)S(1)} collective-permute-done((bf16[256,256]{1,0:T(8,128)(2,1)S(1)}, bf16[256,256]{1,0:T(8,128)(2,1)S(1)}, u32[]{:S(2)}, u32[]{:S(2)}) %collective-permute-start.9) | collective-permute-done | bytes 131104 | tf_op jit(solution)/shard_map/ppermute | solution.py:31
  34.5 0.0 collective-permute-start.12
  34.5 1.3 %collective-permute-start.11 = (bf16[256,256]{1,0:T(8,128)(2,1)S(1)}, bf16[256,256]{1,0:T(8,128)(2,1)S(1)}, u32[]{:S(2)}, u32[]{:S(2)}) collective-permute-start(bf16[256,256]{1,0:T(8,128)(2,1)S(1)} %collective-permute-done.9.refs_2_), channel_id=1, source_target_pairs={{0,2},{2,0},{4,6},{6,4},{8,10},{10,8},{12,14},{14,12},{1,3},{3,1},... | collective-permute-start | bytes 393224 | tf_op jit(solution)/shard_map/ppermute | solution.py:31
  35.8 0.0 collective-permute-done.14.refs_3_
  35.8 2.1 %collective-permute-start.10 = (bf16[256,256]{1,0:T(8,128)(2,1)S(1)}, bf16[256,256]{1,0:T(8,128)(2,1)S(1)}, u32[]{:S(2)}, u32[]{:S(2)}) collective-permute-start(bf16[256,256]{1,0:T(8,128)(2,1)S(1)} %collective-permute-done.9.refs_2_), channel_id=1, source_target_pairs={{0,4},{2,6},{4,0},{6,2},{8,12},{10,14},{12,8},{14,10},{1,5},{3,7},... | collective-permute-start | bytes 393224 | tf_op jit(solution)/shard_map/ppermute | solution.py:31
  38.0 0.2 shard_map.128
  38.2 0.0 collective-permute-done.13.refs_1_
  38.2 0.8 %shard_map.129.refs_4_ = f32[2,2,256,256]{3,2,1,0:T(8,128)S(1)} custom-call(s32[2,2]{1,0:T(2,128)S(1)} %copy-done.3, bf16[8,2,32,256]{3,2,1,0:T(8,128)(2,1)S(1)} %get-tuple-element.27.v_ref, bf16[2,512,256]{2,1,0:T(8,128)(2,1)S(1)} %get-tuple-element.28.u_ref, bf16[2,2,2,256,256]{4,3,2,1,0:T(8,128)(2,1)S(1)} %copy-done, ...), custom_call_target="tpu_custom_call" | custom-call | flops 100663296 | bytes 2359312 | tf_op jit(solution)/shard_map/pallas_call | solution.py:260
  39.0 0.0 collective-permute-done.8.refs_0_
  39.0 2.5 %collective-permute-done.12.refs_3_ = bf16[256,256]{1,0:T(8,128)(2,1)S(1)} collective-permute-done((bf16[256,256]{1,0:T(8,128)(2,1)S(1)}, bf16[256,256]{1,0:T(8,128)(2,1)S(1)}, u32[]{:S(2)}, u32[]{:S(2)}) %collective-permute-start.12) | collective-permute-done | bytes 131104 | tf_op jit(solution)/shard_map/ppermute | solution.py:31
  41.5 1.3 %collective-permute-done.11.refs_2_ = bf16[256,256]{1,0:T(8,128)(2,1)S(1)} collective-permute-done((bf16[256,256]{1,0:T(8,128)(2,1)S(1)}, bf16[256,256]{1,0:T(8,128)(2,1)S(1)}, u32[]{:S(2)}, u32[]{:S(2)}) %collective-permute-start.11) | collective-permute-done | bytes 131104 | tf_op jit(solution)/shard_map/ppermute | solution.py:31
  42.9 0.0 collective-permute-done.10.refs_1_
  42.9 0.6 %shard_map.131 = bf16[2,256,256]{2,1,0:T(8,128)(2,1)S(1)} custom-call(s32[2,2]{1,0:T(2,128)S(1)} %copy-done.3, bf16[8,2,32,256]{3,2,1,0:T(8,128)(2,1)S(1)} %get-tuple-element.27.v_ref, bf16[2,512,256]{2,1,0:T(8,128)(2,1)S(1)} %get-tuple-element.28.u_ref, bf16[2,2,2,256,256]{4,3,2,1,0:T(8,128)(2,1)S(1)} %copy-done, ...), custom_call_target="tpu_custom_call" | custom-call | flops 50331648 | bytes 3407888 | tf_op jit(solution)/shard_map/pallas_call | solution.py:260
  43.4 0.1 collective-permute-start.15
  43.5 0.6 %shard_map.130.own = f32[2,256,256]{2,1,0:T(8,128)S(1)} custom-call(s32[2,2]{1,0:T(2,128)S(1)} %copy-done.3, bf16[8,2,32,256]{3,2,1,0:T(8,128)(2,1)S(1)} %get-tuple-element.27.v_ref, bf16[2,512,256]{2,1,0:T(8,128)(2,1)S(1)} %get-tuple-element.28.u_ref, bf16[2,2,2,256,256]{4,3,2,1,0:T(8,128)(2,1)S(1)} %copy-done, ...), custom_call_target="tpu_custom_call" | custom-call | flops 50331648 | bytes 3407888 | tf_op jit(solution)/shard_map/pallas_call | solution.py:260
  44.1 0.9 %collective-permute-done.15.other = bf16[2,256,256]{2,1,0:T(8,128)(2,1)S(1)} collective-permute-done((bf16[2,256,256]{2,1,0:T(8,128)(2,1)S(1)}, bf16[2,256,256]{2,1,0:T(8,128)(2,1)S(1)}, u32[]{:S(2)}, u32[]{:S(2)}) %collective-permute-start.15) | collective-permute-done | bytes 262176 | tf_op jit(solution)/shard_map/ppermute | solution.py:356
  45.0 1.7 %shard_map.132 = (f32[256,256]{1,0:T(8,128)}, f32[256,256]{1,0:T(8,128)}) custom-call(f32[2,256,256]{2,1,0:T(8,128)S(1)} %shard_map.130.own, bf16[2,256,256]{2,1,0:T(8,128)(2,1)S(1)} %collective-permute-done.15.other, f32[256,256]{1,0:T(8,128)S(1)} %get-tuple-element.46.weight, f32[256,256]{1,0:T(8,128)S(1)} %get-tuple-element.47.unweight, ...), custom_call_target="tpu_custom_call" | custom-call | flops 13107200 | bytes 3538944 | tf_op jit(solution)/shard_map/pallas_call | solution.py:260
  (3 shorter events, 0.0 us)
Async XLA Ops:
  0.6 16.8 %copy-start = (bf16[2,2,2,256,256]{4,3,2,1,0:T(8,128)(2,1)S(1)}, bf16[2,2,2,256,256]{4,3,2,1,0:T(8,128)(2,1)}, u32[]{:S(2)}) copy-start(bf16[2,2,2,256,256]{4,3,2,1,0:T(8,128)(2,1)} %d_ref.11) | copy-start | bytes 3145732
  1.7 10.5 %collective-permute-start.1 = (bf16[256,256]{1,0:T(8,128)(2,1)S(1)}, bf16[256,256]{1,0:T(8,128)(2,1)S(1)}, u32[]{:S(2)}, u32[]{:S(2)}) collective-permute-start(bf16[256,256]{1,0:T(8,128)(2,1)S(1)} %shard_map.123.refs_0_), channel_id=1, source_target_pairs={{0,8},{2,10},{4,12},{6,14},{8,0},{10,2},{12,4},{14,6},{1,9},{3,11}... | collective-permute-start | bytes 393224 | tf_op jit(solution)/shard_map/ppermute | solution.py:31
  5.8 8.5 %collective-permute-start.6 = (bf16[256,256]{1,0:T(8,128)(2,1)S(1)}, bf16[256,256]{1,0:T(8,128)(2,1)S(1)}, u32[]{:S(2)}, u32[]{:S(2)}) collective-permute-start(bf16[256,256]{1,0:T(8,128)(2,1)S(1)} %shard_map.123.refs_0_), channel_id=1, source_target_pairs={{0,4},{2,6},{4,0},{6,2},{8,12},{10,14},{12,8},{14,10},{1,5},{3,7},... | collective-permute-start | bytes 393224 | tf_op jit(solution)/shard_map/ppermute | solution.py:31
  7.4 10.1 %collective-permute-start.5 = (bf16[256,256]{1,0:T(8,128)(2,1)S(1)}, bf16[256,256]{1,0:T(8,128)(2,1)S(1)}, u32[]{:S(2)}, u32[]{:S(2)}) collective-permute-start(bf16[256,256]{1,0:T(8,128)(2,1)S(1)} %shard_map.123.refs_0_), channel_id=1, source_target_pairs={{0,2},{2,0},{4,6},{6,4},{8,10},{10,8},{12,14},{14,12},{1,3},{3,1},... | collective-permute-start | bytes 393224 | tf_op jit(solution)/shard_map/ppermute | solution.py:31
  8.9 10.1 %collective-permute-start = (bf16[256,256]{1,0:T(8,128)(2,1)S(1)}, bf16[256,256]{1,0:T(8,128)(2,1)S(1)}, u32[]{:S(2)}, u32[]{:S(2)}) collective-permute-start(bf16[256,256]{1,0:T(8,128)(2,1)S(1)} %shard_map.123.refs_0_), channel_id=1, source_target_pairs={{0,6},{2,4},{4,2},{6,0},{8,14},{10,12},{12,10},{14,8},{1,7},{3,5},... | collective-permute-start | bytes 393224 | tf_op jit(solution)/shard_map/ppermute | solution.py:31
  12.2 7.7 %collective-permute-start.4 = (bf16[256,256]{1,0:T(8,128)(2,1)S(1)}, bf16[256,256]{1,0:T(8,128)(2,1)S(1)}, u32[]{:S(2)}, u32[]{:S(2)}) collective-permute-start(bf16[256,256]{1,0:T(8,128)(2,1)S(1)} %collective-permute-done.1.refs_2_), channel_id=1, source_target_pairs={{0,6},{2,4},{4,2},{6,0},{8,14},{10,12},{12,10},{14,8},{1,7},{3,5},... | collective-permute-start | bytes 393224 | tf_op jit(solution)/shard_map/ppermute | solution.py:31
  13.8 8.0 %collective-permute-start.3 = (bf16[256,256]{1,0:T(8,128)(2,1)S(1)}, bf16[256,256]{1,0:T(8,128)(2,1)S(1)}, u32[]{:S(2)}, u32[]{:S(2)}) collective-permute-start(bf16[256,256]{1,0:T(8,128)(2,1)S(1)} %collective-permute-done.1.refs_2_), channel_id=1, source_target_pairs={{0,2},{2,0},{4,6},{6,4},{8,10},{10,8},{12,14},{14,12},{1,3},{3,1},... | collective-permute-start | bytes 393224 | tf_op jit(solution)/shard_map/ppermute | solution.py:31
  14.3 7.5 %collective-permute-start.2 = (bf16[256,256]{1,0:T(8,128)(2,1)S(1)}, bf16[256,256]{1,0:T(8,128)(2,1)S(1)}, u32[]{:S(2)}, u32[]{:S(2)}) collective-permute-start(bf16[256,256]{1,0:T(8,128)(2,1)S(1)} %collective-permute-done.1.refs_2_), channel_id=1, source_target_pairs={{0,4},{2,6},{4,0},{6,2},{8,12},{10,14},{12,8},{14,10},{1,5},{3,7},... | collective-permute-start | bytes 393224 | tf_op jit(solution)/shard_map/ppermute | solution.py:31
  17.5 0.7 %copy-start.3 = (s32[2,2]{1,0:T(2,128)S(1)}, s32[2,2]{1,0:T(2,128)}, u32[]{:S(2)}) copy-start(s32[2,2]{1,0:T(2,128)} %near_ref.11) | copy-start | bytes 52
  22.4 1.6 %copy-start.1 = (f32[256,256]{1,0:T(8,128)S(1)}, f32[256,256]{1,0:T(8,128)}, u32[]{:S(2)}) copy-start(f32[256,256]{1,0:T(8,128)} %tau.3) | copy-start | bytes 786436
  22.4 1.6 %collective-permute-start.7 = (bf16[2,256,256]{2,1,0:T(8,128)(2,1)S(1)}, bf16[2,256,256]{2,1,0:T(8,128)(2,1)S(1)}, u32[]{:S(2)}, u32[]{:S(2)}) collective-permute-start(bf16[2,256,256]{2,1,0:T(8,128)(2,1)S(1)} %shard_map.126), channel_id=1, source_target_pairs={{0,1},{1,0},{2,3},{3,2},{4,5},{5,4},{6,7},{7,6},{8,9},{9,8},{10,11... | collective-permute-start | bytes 786440 | tf_op jit(solution)/shard_map/ppermute | solution.py:356
  24.0 14.0 %copy-start.2 = (f32[256,256]{1,0:T(8,128)S(1)}, f32[256,256]{1,0:T(8,128)}, u32[]{:S(2)}) copy-start(f32[256,256]{1,0:T(8,128)} %state.1) | copy-start | bytes 786436
  25.1 9.4 %collective-permute-start.9 = (bf16[256,256]{1,0:T(8,128)(2,1)S(1)}, bf16[256,256]{1,0:T(8,128)(2,1)S(1)}, u32[]{:S(2)}, u32[]{:S(2)}) collective-permute-start(bf16[256,256]{1,0:T(8,128)(2,1)S(1)} %get-tuple-element.45.refs_0_), channel_id=1, source_target_pairs={{0,8},{2,10},{4,12},{6,14},{8,0},{10,2},{12,4},{14,6},{1,9},{3,11}... | collective-permute-start | bytes 393224 | tf_op jit(solution)/shard_map/ppermute | solution.py:31
  27.0 8.8 %collective-permute-start.14 = (bf16[256,256]{1,0:T(8,128)(2,1)S(1)}, bf16[256,256]{1,0:T(8,128)(2,1)S(1)}, u32[]{:S(2)}, u32[]{:S(2)}) collective-permute-start(bf16[256,256]{1,0:T(8,128)(2,1)S(1)} %get-tuple-element.45.refs_0_), channel_id=1, source_target_pairs={{0,4},{2,6},{4,0},{6,2},{8,12},{10,14},{12,8},{14,10},{1,5},{3,7},... | collective-permute-start | bytes 393224 | tf_op jit(solution)/shard_map/ppermute | solution.py:31
  28.8 9.4 %collective-permute-start.13 = (bf16[256,256]{1,0:T(8,128)(2,1)S(1)}, bf16[256,256]{1,0:T(8,128)(2,1)S(1)}, u32[]{:S(2)}, u32[]{:S(2)}) collective-permute-start(bf16[256,256]{1,0:T(8,128)(2,1)S(1)} %get-tuple-element.45.refs_0_), channel_id=1, source_target_pairs={{0,2},{2,0},{4,6},{6,4},{8,10},{10,8},{12,14},{14,12},{1,3},{3,1},... | collective-permute-start | bytes 393224 | tf_op jit(solution)/shard_map/ppermute | solution.py:31
  29.3 9.7 %collective-permute-start.8 = (bf16[256,256]{1,0:T(8,128)(2,1)S(1)}, bf16[256,256]{1,0:T(8,128)(2,1)S(1)}, u32[]{:S(2)}, u32[]{:S(2)}) collective-permute-start(bf16[256,256]{1,0:T(8,128)(2,1)S(1)} %get-tuple-element.45.refs_0_), channel_id=1, source_target_pairs={{0,6},{2,4},{4,2},{6,0},{8,14},{10,12},{12,10},{14,8},{1,7},{3,5},... | collective-permute-start | bytes 393224 | tf_op jit(solution)/shard_map/ppermute | solution.py:31
  34.5 7.0 %collective-permute-start.12 = (bf16[256,256]{1,0:T(8,128)(2,1)S(1)}, bf16[256,256]{1,0:T(8,128)(2,1)S(1)}, u32[]{:S(2)}, u32[]{:S(2)}) collective-permute-start(bf16[256,256]{1,0:T(8,128)(2,1)S(1)} %collective-permute-done.9.refs_2_), channel_id=1, source_target_pairs={{0,6},{2,4},{4,2},{6,0},{8,14},{10,12},{12,10},{14,8},{1,7},{3,5},... | collective-permute-start | bytes 393224 | tf_op jit(solution)/shard_map/ppermute | solution.py:31
  34.5 8.4 %collective-permute-start.11 = (bf16[256,256]{1,0:T(8,128)(2,1)S(1)}, bf16[256,256]{1,0:T(8,128)(2,1)S(1)}, u32[]{:S(2)}, u32[]{:S(2)}) collective-permute-start(bf16[256,256]{1,0:T(8,128)(2,1)S(1)} %collective-permute-done.9.refs_2_), channel_id=1, source_target_pairs={{0,2},{2,0},{4,6},{6,4},{8,10},{10,8},{12,14},{14,12},{1,3},{3,1},... | collective-permute-start | bytes 393224 | tf_op jit(solution)/shard_map/ppermute | solution.py:31
  35.8 7.0 %collective-permute-start.10 = (bf16[256,256]{1,0:T(8,128)(2,1)S(1)}, bf16[256,256]{1,0:T(8,128)(2,1)S(1)}, u32[]{:S(2)}, u32[]{:S(2)}) collective-permute-start(bf16[256,256]{1,0:T(8,128)(2,1)S(1)} %collective-permute-done.9.refs_2_), channel_id=1, source_target_pairs={{0,4},{2,6},{4,0},{6,2},{8,12},{10,14},{12,8},{14,10},{1,5},{3,7},... | collective-permute-start | bytes 393224 | tf_op jit(solution)/shard_map/ppermute | solution.py:31
  43.4 1.6 %collective-permute-start.15 = (bf16[2,256,256]{2,1,0:T(8,128)(2,1)S(1)}, bf16[2,256,256]{2,1,0:T(8,128)(2,1)S(1)}, u32[]{:S(2)}, u32[]{:S(2)}) collective-permute-start(bf16[2,256,256]{2,1,0:T(8,128)(2,1)S(1)} %shard_map.131), channel_id=1, source_target_pairs={{0,1},{1,0},{2,3},{3,2},{4,5},{5,4},{6,7},{7,6},{8,9},{9,8},{10,11... | collective-permute-start | bytes 786440 | tf_op jit(solution)/shard_map/ppermute | solution.py:356

commit v22 on v21

--- a/solution.py
+++ b/solution.py
@@ -196,12 +196,9 @@
 
 def over_pieces(begin, tall, members, lanes, work):
     step = min(tall, 64)
-
-    @pl.loop(0, tall // step)
-    def _(index):
-        rows = pl.ds(pl.multiple_of(begin + index * step, step), step)
+    for at in range(begin, begin + tall, step):
         for first in range(0, members, lanes):
-            work(rows, slice(first, first + lanes))
+            work(pl.ds(at, step), slice(first, first + lanes))
 
 
 def section_one_kernel(own, other, weight, unweight, tau, coef, rate, rate_half):

time: 46.9 us -> 46.8 us (level)
  no operation moved by 1% of the time
where the time goes in v22:
time: 46.8 us; the launch traced here: 46.6 us
  starting transfers between devices  20.1 us (43%)
  waiting for transfers between devices  15.5 us (33%)
  Pallas kernels  9.5 us (20%)
  between operations  0.77 us (2%)
  local copies, waits for them, and re-layouts  0.68 us (1%)
    ppermute x14, starting transfers between devices, swapped(): lax.ppermute(data, 'row', [(row, row ^ mask) for row in range(count)])  20 us
    ppermute x14, waiting for transfers between devices, swapped(): lax.ppermute(data, 'row', [(row, row ^ mask) for row in range(count)])  13.6 us
    pallas_call x11, Pallas kernels, on_core(): pl.pallas_call(kernel, out_shape=outs, in_specs=[hbm] * len(far) + [vmem]...  9.5 us
    ppermute x2, waiting for transfers between devices, lattice(): lax.ppermute(add(blocks[early:], early, 1, sums, narrow), 'col', swap)  1.89 us
  transfers between devices with their start and end apart: 16, of which 8 were waited for; matrix products, arithmetic and copies ran while one was open for 0% of the time, Pallas kernels for 10%

profile of v22, /device:TPU:0, one launch (start us, length us, event | category | flops | bytes accessed | tf_op | source)
XLA Modules:
  0.0 46.6 jit_solution(3604812233622226260)
XLA Ops:
  0.6 0.0 copy-start
  0.6 1.0 %shard_map.123.refs_0_ = bf16[256,256]{1,0:T(8,128)(2,1)S(1)} custom-call(f32[256,256]{1,0:T(8,128)} %wide_ref.1), custom_call_target="tpu_custom_call" | custom-call | bytes 262144 | tf_op jit(solution)/shard_map/pallas_call | solution.py:257
  1.7 4.1 %collective-permute-start.1 = (bf16[256,256]{1,0:T(8,128)(2,1)S(1)}, bf16[256,256]{1,0:T(8,128)(2,1)S(1)}, u32[]{:S(2)}, u32[]{:S(2)}) collective-permute-start(bf16[256,256]{1,0:T(8,128)(2,1)S(1)} %shard_map.123.refs_0_), channel_id=1, source_target_pairs={{0,8},{2,10},{4,12},{6,14},{8,0},{10,2},{12,4},{14,6},{1,9},{3,11}... | collective-permute-start | bytes 393224 | tf_op jit(solution)/shard_map/ppermute | solution.py:31
  5.8 1.6 %collective-permute-start.6 = (bf16[256,256]{1,0:T(8,128)(2,1)S(1)}, bf16[256,256]{1,0:T(8,128)(2,1)S(1)}, u32[]{:S(2)}, u32[]{:S(2)}) collective-permute-start(bf16[256,256]{1,0:T(8,128)(2,1)S(1)} %shard_map.123.refs_0_), channel_id=1, source_target_pairs={{0,4},{2,6},{4,0},{6,2},{8,12},{10,14},{12,8},{14,10},{1,5},{3,7},... | collective-permute-start | bytes 393224 | tf_op jit(solution)/shard_map/ppermute | solution.py:31
  7.4 1.5 %collective-permute-start.5 = (bf16[256,256]{1,0:T(8,128)(2,1)S(1)}, bf16[256,256]{1,0:T(8,128)(2,1)S(1)}, u32[]{:S(2)}, u32[]{:S(2)}) collective-permute-start(bf16[256,256]{1,0:T(8,128)(2,1)S(1)} %shard_map.123.refs_0_), channel_id=1, source_target_pairs={{0,2},{2,0},{4,6},{6,4},{8,10},{10,8},{12,14},{14,12},{1,3},{3,1},... | collective-permute-start | bytes 393224 | tf_op jit(solution)/shard_map/ppermute | solution.py:31
  8.9 0.4 collective-permute-start
  9.3 2.9 %collective-permute-done.1.refs_2_ = bf16[256,256]{1,0:T(8,128)(2,1)S(1)} collective-permute-done((bf16[256,256]{1,0:T(8,128)(2,1)S(1)}, bf16[256,256]{1,0:T(8,128)(2,1)S(1)}, u32[]{:S(2)}, u32[]{:S(2)}) %collective-permute-start.1) | collective-permute-done | bytes 131104 | tf_op jit(solution)/shard_map/ppermute | solution.py:31
  12.2 1.6 %collective-permute-start.4 = (bf16[256,256]{1,0:T(8,128)(2,1)S(1)}, bf16[256,256]{1,0:T(8,128)(2,1)S(1)}, u32[]{:S(2)}, u32[]{:S(2)}) collective-permute-start(bf16[256,256]{1,0:T(8,128)(2,1)S(1)} %collective-permute-done.1.refs_2_), channel_id=1, source_target_pairs={{0,6},{2,4},{4,2},{6,0},{8,14},{10,12},{12,10},{14,8},{1,7},{3,5},... | collective-permute-start | bytes 393224 | tf_op jit(solution)/shard_map/ppermute | solution.py:31
  13.8 0.5 %collective-permute-start.3 = (bf16[256,256]{1,0:T(8,128)(2,1)S(1)}, bf16[256,256]{1,0:T(8,128)(2,1)S(1)}, u32[]{:S(2)}, u32[]{:S(2)}) collective-permute-start(bf16[256,256]{1,0:T(8,128)(2,1)S(1)} %collective-permute-done.1.refs_2_), channel_id=1, source_target_pairs={{0,2},{2,0},{4,6},{6,4},{8,10},{10,8},{12,14},{14,12},{1,3},{3,1},... | collective-permute-start | bytes 393224 | tf_op jit(solution)/shard_map/ppermute | solution.py:31
  14.3 0.0 collective-permute-done.6.refs_3_
  14.3 1.4 %collective-permute-start.2 = (bf16[256,256]{1,0:T(8,128)(2,1)S(1)}, bf16[256,256]{1,0:T(8,128)(2,1)S(1)}, u32[]{:S(2)}, u32[]{:S(2)}) collective-permute-start(bf16[256,256]{1,0:T(8,128)(2,1)S(1)} %collective-permute-done.1.refs_2_), channel_id=1, source_target_pairs={{0,4},{2,6},{4,0},{6,2},{8,12},{10,14},{12,8},{14,10},{1,5},{3,7},... | collective-permute-start | bytes 393224 | tf_op jit(solution)/shard_map/ppermute | solution.py:31
  15.7 1.8 %shard_map.122 = (bf16[8,2,32,256]{3,2,1,0:T(8,128)(2,1)S(1)}, bf16[2,512,256]{2,1,0:T(8,128)(2,1)S(1)}, f32[5,256,128]{2,1,0:T(8,128)S(1)}, f32[256,256]{1,0:T(...) custom-call(s32[2,8]{1,0:T(2,128)} %refs_0_.1, bf16[2,8,32,256]{3,2,1,0:T(8,128)(2,1)} %refs_1_.1, ...), custom_call_target="tpu_custom_call" | custom-call | bytes 1051712 | tf_op jit(solution)/shard_map/pallas_call | solution.py:257
  17.4 0.0 collective-permute-done.5.refs_1_
  17.5 0.0 copy-start.3
  17.5 0.7 %copy-done.3 = s32[2,2]{1,0:T(2,128)S(1)} copy-done((s32[2,2]{1,0:T(2,128)S(1)}, s32[2,2]{1,0:T(2,128)}, u32[]{:S(2)}) %copy-start.3) | copy-done | bytes 40
  18.1 0.8 %shard_map.124.refs_4_ = f32[2,2,256,256]{3,2,1,0:T(8,128)S(1)} custom-call(s32[2,2]{1,0:T(2,128)S(1)} %copy-done.3, bf16[8,2,32,256]{3,2,1,0:T(8,128)(2,1)S(1)} %get-tuple-element.27.v_ref, bf16[2,512,256]{2,1,0:T(8,128)(2,1)S(1)} %get-tuple-element.28.u_ref, bf16[2,2,2,256,256]{4,3,2,1,0:T(8,128)(2,1)S(1)} %copy-done, ...), custom_call_target="tpu_custom_call" | custom-call | flops 100663296 | bytes 2359312 | tf_op jit(solution)/shard_map/pallas_call | solution.py:257
  18.9 0.0 collective-permute-done.refs_0_
  18.9 1.0 %collective-permute-done.4.refs_3_ = bf16[256,256]{1,0:T(8,128)(2,1)S(1)} collective-permute-done((bf16[256,256]{1,0:T(8,128)(2,1)S(1)}, bf16[256,256]{1,0:T(8,128)(2,1)S(1)}, u32[]{:S(2)}, u32[]{:S(2)}) %collective-permute-start.4) | collective-permute-done | bytes 131104 | tf_op jit(solution)/shard_map/ppermute | solution.py:31
  19.9 1.9 %collective-permute-done.3.refs_2_ = bf16[256,256]{1,0:T(8,128)(2,1)S(1)} collective-permute-done((bf16[256,256]{1,0:T(8,128)(2,1)S(1)}, bf16[256,256]{1,0:T(8,128)(2,1)S(1)}, u32[]{:S(2)}, u32[]{:S(2)}) %collective-permute-start.3) | collective-permute-done | bytes 131104 | tf_op jit(solution)/shard_map/ppermute | solution.py:31
  21.8 0.0 collective-permute-done.2.refs_1_
  21.8 0.6 %shard_map.126 = bf16[2,256,256]{2,1,0:T(8,128)(2,1)S(1)} custom-call(s32[2,2]{1,0:T(2,128)S(1)} %copy-done.3, bf16[8,2,32,256]{3,2,1,0:T(8,128)(2,1)S(1)} %get-tuple-element.27.v_ref, bf16[2,512,256]{2,1,0:T(8,128)(2,1)S(1)} %get-tuple-element.28.u_ref, bf16[2,2,2,256,256]{4,3,2,1,0:T(8,128)(2,1)S(1)} %copy-done, ...), custom_call_target="tpu_custom_call" | custom-call | flops 50331648 | bytes 3407888 | tf_op jit(solution)/shard_map/pallas_call | solution.py:257
  22.4 0.0 copy-start.1
  22.4 0.1 collective-permute-start.7
  22.5 0.6 %shard_map.125.own = f32[2,256,256]{2,1,0:T(8,128)S(1)} custom-call(s32[2,2]{1,0:T(2,128)S(1)} %copy-done.3, bf16[8,2,32,256]{3,2,1,0:T(8,128)(2,1)S(1)} %get-tuple-element.27.v_ref, bf16[2,512,256]{2,1,0:T(8,128)(2,1)S(1)} %get-tuple-element.28.u_ref, bf16[2,2,2,256,256]{4,3,2,1,0:T(8,128)(2,1)S(1)} %copy-done, ...), custom_call_target="tpu_custom_call" | custom-call | flops 50331648 | bytes 3407888 | tf_op jit(solution)/shard_map/pallas_call | solution.py:257
  23.1 0.9 %collective-permute-done.7.other = bf16[2,256,256]{2,1,0:T(8,128)(2,1)S(1)} collective-permute-done((bf16[2,256,256]{2,1,0:T(8,128)(2,1)S(1)}, bf16[2,256,256]{2,1,0:T(8,128)(2,1)S(1)}, u32[]{:S(2)}, u32[]{:S(2)}) %collective-permute-start.7) | collective-permute-done | bytes 262176 | tf_op jit(solution)/shard_map/ppermute | solution.py:353
  24.0 0.0 copy-done.1
  24.0 0.9 %shard_map.127 = (f32[256,256]{1,0:T(8,128)S(1)}, bf16[256,256]{1,0:T(8,128)(2,1)S(1)}) custom-call(f32[2,256,256]{2,1,0:T(8,128)S(1)} %shard_map.125.own, bf16[2,256,256]{2,1,0:T(8,128)(2,1)S(1)} %collective-permute-done.7.other, f32[256,256]{1,0:T(8,128)S(1)} %get-tuple-element.33.weight, f32[256,256]{1,0:T(8,128)S(1)} %get-tuple-element.34.unweight, ...), custom_call_target="tpu_custom_call" | custom-call | flops 13107200 | bytes 2228224 | tf_op jit(solution)/shard_map/pallas_call | solution.py:257
  24.9 1.9 %collective-permute-start.9 = (bf16[256,256]{1,0:T(8,128)(2,1)S(1)}, bf16[256,256]{1,0:T(8,128)(2,1)S(1)}, u32[]{:S(2)}, u32[]{:S(2)}) collective-permute-start(bf16[256,256]{1,0:T(8,128)(2,1)S(1)} %get-tuple-element.45.refs_0_), channel_id=1, source_target_pairs={{0,8},{2,10},{4,12},{6,14},{8,0},{10,2},{12,4},{14,6},{1,9},{3,11}... | collective-permute-start | bytes 393224 | tf_op jit(solution)/shard_map/ppermute | solution.py:31
  26.8 1.8 %collective-permute-start.14 = (bf16[256,256]{1,0:T(8,128)(2,1)S(1)}, bf16[256,256]{1,0:T(8,128)(2,1)S(1)}, u32[]{:S(2)}, u32[]{:S(2)}) collective-permute-start(bf16[256,256]{1,0:T(8,128)(2,1)S(1)} %get-tuple-element.45.refs_0_), channel_id=1, source_target_pairs={{0,4},{2,6},{4,0},{6,2},{8,12},{10,14},{12,8},{14,10},{1,5},{3,7},... | collective-permute-start | bytes 393224 | tf_op jit(solution)/shard_map/ppermute | solution.py:31
  28.6 0.5 %collective-permute-start.13 = (bf16[256,256]{1,0:T(8,128)(2,1)S(1)}, bf16[256,256]{1,0:T(8,128)(2,1)S(1)}, u32[]{:S(2)}, u32[]{:S(2)}) collective-permute-start(bf16[256,256]{1,0:T(8,128)(2,1)S(1)} %get-tuple-element.45.refs_0_), channel_id=1, source_target_pairs={{0,2},{2,0},{4,6},{6,4},{8,10},{10,8},{12,14},{14,12},{1,3},{3,1},... | collective-permute-start | bytes 393224 | tf_op jit(solution)/shard_map/ppermute | solution.py:31
  29.1 1.2 %collective-permute-start.8 = (bf16[256,256]{1,0:T(8,128)(2,1)S(1)}, bf16[256,256]{1,0:T(8,128)(2,1)S(1)}, u32[]{:S(2)}, u32[]{:S(2)}) collective-permute-start(bf16[256,256]{1,0:T(8,128)(2,1)S(1)} %get-tuple-element.45.refs_0_), channel_id=1, source_target_pairs={{0,6},{2,4},{4,2},{6,0},{8,14},{10,12},{12,10},{14,8},{1,7},{3,5},... | collective-permute-start | bytes 393224 | tf_op jit(solution)/shard_map/ppermute | solution.py:31
  30.3 4.0 %collective-permute-done.9.refs_2_ = bf16[256,256]{1,0:T(8,128)(2,1)S(1)} collective-permute-done((bf16[256,256]{1,0:T(8,128)(2,1)S(1)}, bf16[256,256]{1,0:T(8,128)(2,1)S(1)}, u32[]{:S(2)}, u32[]{:S(2)}) %collective-permute-start.9) | collective-permute-done | bytes 131104 | tf_op jit(solution)/shard_map/ppermute | solution.py:31
  34.3 0.0 collective-permute-start.12
  34.3 1.3 %collective-permute-start.11 = (bf16[256,256]{1,0:T(8,128)(2,1)S(1)}, bf16[256,256]{1,0:T(8,128)(2,1)S(1)}, u32[]{:S(2)}, u32[]{:S(2)}) collective-permute-start(bf16[256,256]{1,0:T(8,128)(2,1)S(1)} %collective-permute-done.9.refs_2_), channel_id=1, source_target_pairs={{0,2},{2,0},{4,6},{6,4},{8,10},{10,8},{12,14},{14,12},{1,3},{3,1},... | collective-permute-start | bytes 393224 | tf_op jit(solution)/shard_map/ppermute | solution.py:31
  35.7 0.0 collective-permute-done.14.refs_3_
  35.7 2.1 %collective-permute-start.10 = (bf16[256,256]{1,0:T(8,128)(2,1)S(1)}, bf16[256,256]{1,0:T(8,128)(2,1)S(1)}, u32[]{:S(2)}, u32[]{:S(2)}) collective-permute-start(bf16[256,256]{1,0:T(8,128)(2,1)S(1)} %collective-permute-done.9.refs_2_), channel_id=1, source_target_pairs={{0,4},{2,6},{4,0},{6,2},{8,12},{10,14},{12,8},{14,10},{1,5},{3,7},... | collective-permute-start | bytes 393224 | tf_op jit(solution)/shard_map/ppermute | solution.py:31
  37.8 0.2 shard_map.128
  38.1 0.0 collective-permute-done.13.refs_1_
  38.1 0.8 %shard_map.129.refs_4_ = f32[2,2,256,256]{3,2,1,0:T(8,128)S(1)} custom-call(s32[2,2]{1,0:T(2,128)S(1)} %copy-done.3, bf16[8,2,32,256]{3,2,1,0:T(8,128)(2,1)S(1)} %get-tuple-element.27.v_ref, bf16[2,512,256]{2,1,0:T(8,128)(2,1)S(1)} %get-tuple-element.28.u_ref, bf16[2,2,2,256,256]{4,3,2,1,0:T(8,128)(2,1)S(1)} %copy-done, ...), custom_call_target="tpu_custom_call" | custom-call | flops 100663296 | bytes 2359312 | tf_op jit(solution)/shard_map/pallas_call | solution.py:257
  38.9 0.0 collective-permute-done.8.refs_0_
  38.9 2.5 %collective-permute-done.12.refs_3_ = bf16[256,256]{1,0:T(8,128)(2,1)S(1)} collective-permute-done((bf16[256,256]{1,0:T(8,128)(2,1)S(1)}, bf16[256,256]{1,0:T(8,128)(2,1)S(1)}, u32[]{:S(2)}, u32[]{:S(2)}) %collective-permute-start.12) | collective-permute-done | bytes 131104 | tf_op jit(solution)/shard_map/ppermute | solution.py:31
  41.4 1.3 %collective-permute-done.11.refs_2_ = bf16[256,256]{1,0:T(8,128)(2,1)S(1)} collective-permute-done((bf16[256,256]{1,0:T(8,128)(2,1)S(1)}, bf16[256,256]{1,0:T(8,128)(2,1)S(1)}, u32[]{:S(2)}, u32[]{:S(2)}) %collective-permute-start.11) | collective-permute-done | bytes 131104 | tf_op jit(solution)/shard_map/ppermute | solution.py:31
  42.7 0.0 collective-permute-done.10.refs_1_
  42.7 0.6 %shard_map.131 = bf16[2,256,256]{2,1,0:T(8,128)(2,1)S(1)} custom-call(s32[2,2]{1,0:T(2,128)S(1)} %copy-done.3, bf16[8,2,32,256]{3,2,1,0:T(8,128)(2,1)S(1)} %get-tuple-element.27.v_ref, bf16[2,512,256]{2,1,0:T(8,128)(2,1)S(1)} %get-tuple-element.28.u_ref, bf16[2,2,2,256,256]{4,3,2,1,0:T(8,128)(2,1)S(1)} %copy-done, ...), custom_call_target="tpu_custom_call" | custom-call | flops 50331648 | bytes 3407888 | tf_op jit(solution)/shard_map/pallas_call | solution.py:257
  43.3 0.1 collective-permute-start.15
  43.4 0.6 %shard_map.130.own = f32[2,256,256]{2,1,0:T(8,128)S(1)} custom-call(s32[2,2]{1,0:T(2,128)S(1)} %copy-done.3, bf16[8,2,32,256]{3,2,1,0:T(8,128)(2,1)S(1)} %get-tuple-element.27.v_ref, bf16[2,512,256]{2,1,0:T(8,128)(2,1)S(1)} %get-tuple-element.28.u_ref, bf16[2,2,2,256,256]{4,3,2,1,0:T(8,128)(2,1)S(1)} %copy-done, ...), custom_call_target="tpu_custom_call" | custom-call | flops 50331648 | bytes 3407888 | tf_op jit(solution)/shard_map/pallas_call | solution.py:257
  43.9 0.9 %collective-permute-done.15.other = bf16[2,256,256]{2,1,0:T(8,128)(2,1)S(1)} collective-permute-done((bf16[2,256,256]{2,1,0:T(8,128)(2,1)S(1)}, bf16[2,256,256]{2,1,0:T(8,128)(2,1)S(1)}, u32[]{:S(2)}, u32[]{:S(2)}) %collective-permute-start.15) | collective-permute-done | bytes 262176 | tf_op jit(solution)/shard_map/ppermute | solution.py:353
  44.9 1.7 %shard_map.132 = (f32[256,256]{1,0:T(8,128)}, f32[256,256]{1,0:T(8,128)}) custom-call(f32[2,256,256]{2,1,0:T(8,128)S(1)} %shard_map.130.own, bf16[2,256,256]{2,1,0:T(8,128)(2,1)S(1)} %collective-permute-done.15.other, f32[256,256]{1,0:T(8,128)S(1)} %get-tuple-element.46.weight, f32[256,256]{1,0:T(8,128)S(1)} %get-tuple-element.47.unweight, ...), custom_call_target="tpu_custom_call" | custom-call | flops 13107200 | bytes 3538944 | tf_op jit(solution)/shard_map/pallas_call | solution.py:257
  (3 shorter events, 0.0 us)
Async XLA Ops:
  0.6 16.8 %copy-start = (bf16[2,2,2,256,256]{4,3,2,1,0:T(8,128)(2,1)S(1)}, bf16[2,2,2,256,256]{4,3,2,1,0:T(8,128)(2,1)}, u32[]{:S(2)}) copy-start(bf16[2,2,2,256,256]{4,3,2,1,0:T(8,128)(2,1)} %d_ref.11) | copy-start | bytes 3145732
  1.7 10.5 %collective-permute-start.1 = (bf16[256,256]{1,0:T(8,128)(2,1)S(1)}, bf16[256,256]{1,0:T(8,128)(2,1)S(1)}, u32[]{:S(2)}, u32[]{:S(2)}) collective-permute-start(bf16[256,256]{1,0:T(8,128)(2,1)S(1)} %shard_map.123.refs_0_), channel_id=1, source_target_pairs={{0,8},{2,10},{4,12},{6,14},{8,0},{10,2},{12,4},{14,6},{1,9},{3,11}... | collective-permute-start | bytes 393224 | tf_op jit(solution)/shard_map/ppermute | solution.py:31
  5.8 8.5 %collective-permute-start.6 = (bf16[256,256]{1,0:T(8,128)(2,1)S(1)}, bf16[256,256]{1,0:T(8,128)(2,1)S(1)}, u32[]{:S(2)}, u32[]{:S(2)}) collective-permute-start(bf16[256,256]{1,0:T(8,128)(2,1)S(1)} %shard_map.123.refs_0_), channel_id=1, source_target_pairs={{0,4},{2,6},{4,0},{6,2},{8,12},{10,14},{12,8},{14,10},{1,5},{3,7},... | collective-permute-start | bytes 393224 | tf_op jit(solution)/shard_map/ppermute | solution.py:31
  7.4 10.1 %collective-permute-start.5 = (bf16[256,256]{1,0:T(8,128)(2,1)S(1)}, bf16[256,256]{1,0:T(8,128)(2,1)S(1)}, u32[]{:S(2)}, u32[]{:S(2)}) collective-permute-start(bf16[256,256]{1,0:T(8,128)(2,1)S(1)} %shard_map.123.refs_0_), channel_id=1, source_target_pairs={{0,2},{2,0},{4,6},{6,4},{8,10},{10,8},{12,14},{14,12},{1,3},{3,1},... | collective-permute-start | bytes 393224 | tf_op jit(solution)/shard_map/ppermute | solution.py:31
  8.9 10.1 %collective-permute-start = (bf16[256,256]{1,0:T(8,128)(2,1)S(1)}, bf16[256,256]{1,0:T(8,128)(2,1)S(1)}, u32[]{:S(2)}, u32[]{:S(2)}) collective-permute-start(bf16[256,256]{1,0:T(8,128)(2,1)S(1)} %shard_map.123.refs_0_), channel_id=1, source_target_pairs={{0,6},{2,4},{4,2},{6,0},{8,14},{10,12},{12,10},{14,8},{1,7},{3,5},... | collective-permute-start | bytes 393224 | tf_op jit(solution)/shard_map/ppermute | solution.py:31
  12.2 7.7 %collective-permute-start.4 = (bf16[256,256]{1,0:T(8,128)(2,1)S(1)}, bf16[256,256]{1,0:T(8,128)(2,1)S(1)}, u32[]{:S(2)}, u32[]{:S(2)}) collective-permute-start(bf16[256,256]{1,0:T(8,128)(2,1)S(1)} %collective-permute-done.1.refs_2_), channel_id=1, source_target_pairs={{0,6},{2,4},{4,2},{6,0},{8,14},{10,12},{12,10},{14,8},{1,7},{3,5},... | collective-permute-start | bytes 393224 | tf_op jit(solution)/shard_map/ppermute | solution.py:31
  13.8 8.0 %collective-permute-start.3 = (bf16[256,256]{1,0:T(8,128)(2,1)S(1)}, bf16[256,256]{1,0:T(8,128)(2,1)S(1)}, u32[]{:S(2)}, u32[]{:S(2)}) collective-permute-start(bf16[256,256]{1,0:T(8,128)(2,1)S(1)} %collective-permute-done.1.refs_2_), channel_id=1, source_target_pairs={{0,2},{2,0},{4,6},{6,4},{8,10},{10,8},{12,14},{14,12},{1,3},{3,1},... | collective-permute-start | bytes 393224 | tf_op jit(solution)/shard_map/ppermute | solution.py:31
  14.3 7.5 %collective-permute-start.2 = (bf16[256,256]{1,0:T(8,128)(2,1)S(1)}, bf16[256,256]{1,0:T(8,128)(2,1)S(1)}, u32[]{:S(2)}, u32[]{:S(2)}) collective-permute-start(bf16[256,256]{1,0:T(8,128)(2,1)S(1)} %collective-permute-done.1.refs_2_), channel_id=1, source_target_pairs={{0,4},{2,6},{4,0},{6,2},{8,12},{10,14},{12,8},{14,10},{1,5},{3,7},... | collective-permute-start | bytes 393224 | tf_op jit(solution)/shard_map/ppermute | solution.py:31
  17.5 0.7 %copy-start.3 = (s32[2,2]{1,0:T(2,128)S(1)}, s32[2,2]{1,0:T(2,128)}, u32[]{:S(2)}) copy-start(s32[2,2]{1,0:T(2,128)} %near_ref.11) | copy-start | bytes 52
  22.4 1.6 %copy-start.1 = (f32[256,256]{1,0:T(8,128)S(1)}, f32[256,256]{1,0:T(8,128)}, u32[]{:S(2)}) copy-start(f32[256,256]{1,0:T(8,128)} %tau.3) | copy-start | bytes 786436
  22.4 1.6 %collective-permute-start.7 = (bf16[2,256,256]{2,1,0:T(8,128)(2,1)S(1)}, bf16[2,256,256]{2,1,0:T(8,128)(2,1)S(1)}, u32[]{:S(2)}, u32[]{:S(2)}) collective-permute-start(bf16[2,256,256]{2,1,0:T(8,128)(2,1)S(1)} %shard_map.126), channel_id=1, source_target_pairs={{0,1},{1,0},{2,3},{3,2},{4,5},{5,4},{6,7},{7,6},{8,9},{9,8},{10,11... | collective-permute-start | bytes 786440 | tf_op jit(solution)/shard_map/ppermute | solution.py:353
  24.0 13.8 %copy-start.2 = (f32[256,256]{1,0:T(8,128)S(1)}, f32[256,256]{1,0:T(8,128)}, u32[]{:S(2)}) copy-start(f32[256,256]{1,0:T(8,128)} %state.1) | copy-start | bytes 786436
  24.9 9.4 %collective-permute-start.9 = (bf16[256,256]{1,0:T(8,128)(2,1)S(1)}, bf16[256,256]{1,0:T(8,128)(2,1)S(1)}, u32[]{:S(2)}, u32[]{:S(2)}) collective-permute-start(bf16[256,256]{1,0:T(8,128)(2,1)S(1)} %get-tuple-element.45.refs_0_), channel_id=1, source_target_pairs={{0,8},{2,10},{4,12},{6,14},{8,0},{10,2},{12,4},{14,6},{1,9},{3,11}... | collective-permute-start | bytes 393224 | tf_op jit(solution)/shard_map/ppermute | solution.py:31
  26.8 8.8 %collective-permute-start.14 = (bf16[256,256]{1,0:T(8,128)(2,1)S(1)}, bf16[256,256]{1,0:T(8,128)(2,1)S(1)}, u32[]{:S(2)}, u32[]{:S(2)}) collective-permute-start(bf16[256,256]{1,0:T(8,128)(2,1)S(1)} %get-tuple-element.45.refs_0_), channel_id=1, source_target_pairs={{0,4},{2,6},{4,0},{6,2},{8,12},{10,14},{12,8},{14,10},{1,5},{3,7},... | collective-permute-start | bytes 393224 | tf_op jit(solution)/shard_map/ppermute | solution.py:31
  28.6 9.4 %collective-permute-start.13 = (bf16[256,256]{1,0:T(8,128)(2,1)S(1)}, bf16[256,256]{1,0:T(8,128)(2,1)S(1)}, u32[]{:S(2)}, u32[]{:S(2)}) collective-permute-start(bf16[256,256]{1,0:T(8,128)(2,1)S(1)} %get-tuple-element.45.refs_0_), channel_id=1, source_target_pairs={{0,2},{2,0},{4,6},{6,4},{8,10},{10,8},{12,14},{14,12},{1,3},{3,1},... | collective-permute-start | bytes 393224 | tf_op jit(solution)/shard_map/ppermute | solution.py:31
  29.1 9.7 %collective-permute-start.8 = (bf16[256,256]{1,0:T(8,128)(2,1)S(1)}, bf16[256,256]{1,0:T(8,128)(2,1)S(1)}, u32[]{:S(2)}, u32[]{:S(2)}) collective-permute-start(bf16[256,256]{1,0:T(8,128)(2,1)S(1)} %get-tuple-element.45.refs_0_), channel_id=1, source_target_pairs={{0,6},{2,4},{4,2},{6,0},{8,14},{10,12},{12,10},{14,8},{1,7},{3,5},... | collective-permute-start | bytes 393224 | tf_op jit(solution)/shard_map/ppermute | solution.py:31
  34.3 7.0 %collective-permute-start.12 = (bf16[256,256]{1,0:T(8,128)(2,1)S(1)}, bf16[256,256]{1,0:T(8,128)(2,1)S(1)}, u32[]{:S(2)}, u32[]{:S(2)}) collective-permute-start(bf16[256,256]{1,0:T(8,128)(2,1)S(1)} %collective-permute-done.9.refs_2_), channel_id=1, source_target_pairs={{0,6},{2,4},{4,2},{6,0},{8,14},{10,12},{12,10},{14,8},{1,7},{3,5},... | collective-permute-start | bytes 393224 | tf_op jit(solution)/shard_map/ppermute | solution.py:31
  34.3 8.4 %collective-permute-start.11 = (bf16[256,256]{1,0:T(8,128)(2,1)S(1)}, bf16[256,256]{1,0:T(8,128)(2,1)S(1)}, u32[]{:S(2)}, u32[]{:S(2)}) collective-permute-start(bf16[256,256]{1,0:T(8,128)(2,1)S(1)} %collective-permute-done.9.refs_2_), channel_id=1, source_target_pairs={{0,2},{2,0},{4,6},{6,4},{8,10},{10,8},{12,14},{14,12},{1,3},{3,1},... | collective-permute-start | bytes 393224 | tf_op jit(solution)/shard_map/ppermute | solution.py:31
  35.7 7.0 %collective-permute-start.10 = (bf16[256,256]{1,0:T(8,128)(2,1)S(1)}, bf16[256,256]{1,0:T(8,128)(2,1)S(1)}, u32[]{:S(2)}, u32[]{:S(2)}) collective-permute-start(bf16[256,256]{1,0:T(8,128)(2,1)S(1)} %collective-permute-done.9.refs_2_), channel_id=1, source_target_pairs={{0,4},{2,6},{4,0},{6,2},{8,12},{10,14},{12,8},{14,10},{1,5},{3,7},... | collective-permute-start | bytes 393224 | tf_op jit(solution)/shard_map/ppermute | solution.py:31
  43.3 1.6 %collective-permute-start.15 = (bf16[2,256,256]{2,1,0:T(8,128)(2,1)S(1)}, bf16[2,256,256]{2,1,0:T(8,128)(2,1)S(1)}, u32[]{:S(2)}, u32[]{:S(2)}) collective-permute-start(bf16[2,256,256]{2,1,0:T(8,128)(2,1)S(1)} %shard_map.131), channel_id=1, source_target_pairs={{0,1},{1,0},{2,3},{3,2},{4,5},{5,4},{6,7},{7,6},{8,9},{9,8},{10,11... | collective-permute-start | bytes 786440 | tf_op jit(solution)/shard_map/ppermute | solution.py:353

commit v23 on v22

--- a/solution.py
+++ b/solution.py
@@ -19,7 +19,7 @@
 def arrivals(count, direct):
     if not direct:
         return list(range(count))
-    return [0, 1, 4, 2, 3, 6, 5, 7] if count == 8 else [0, 1, 2, 3]
+    return [0, 4, 2, 1, 3, 6, 5, 7] if count == 8 else [0, 1, 2, 3]
 
 
 def row_met(spot, row, direct):

time: 46.8 us -> 48.3 us (1.032)
  waiting for transfers between devices: 15.5 us -> 17.4 us
    ppermute x14, waiting for transfers between devices: 13.6 us -> 15.5 us  [swapped(): lax.ppermute(data, 'row', [(row, row ^ mask) for row in range(count)])]
  transfers between devices with their start and end apart: 16 -> 16, of which waited for: 8 -> 9; matrix products, arithmetic and copies ran while one was open for 0% -> 0% of each run, Pallas kernels for 10% -> 10%
where the time goes in v23:
time: 48.3 us; the launch traced here: 48.1 us
  starting transfers between devices  19.8 us (41%)
  waiting for transfers between devices  17.4 us (36%)
  Pallas kernels  9.5 us (20%)
  between operations  0.77 us (2%)
  local copies, waits for them, and re-layouts  0.68 us (1%)
    ppermute x14, starting transfers between devices, swapped(): lax.ppermute(data, 'row', [(row, row ^ mask) for row in range(count)])  19.7 us
    ppermute x14, waiting for transfers between devices, swapped(): lax.ppermute(data, 'row', [(row, row ^ mask) for row in range(count)])  15.5 us
    pallas_call x11, Pallas kernels, on_core(): pl.pallas_call(kernel, out_shape=outs, in_specs=[hbm] * len(far) + [vmem]...  9.5 us
    ppermute x2, waiting for transfers between devices, lattice(): lax.ppermute(add(blocks[early:], early, 1, sums, narrow), 'col', swap)  1.89 us
  transfers between devices with their start and end apart: 16, of which 9 were waited for; matrix products, arithmetic and copies ran while one was open for 0% of the time, Pallas kernels for 10%

profile of v23, /device:TPU:0, one launch (start us, length us, event | category | flops | bytes accessed | tf_op | source)
XLA Modules:
  0.0 48.1 jit_solution(10897626407513620205)
XLA Ops:
  0.6 1.0 %shard_map.123.refs_0_ = bf16[256,256]{1,0:T(8,128)(2,1)S(1)} custom-call(f32[256,256]{1,0:T(8,128)} %wide_ref.1), custom_call_target="tpu_custom_call" | custom-call | bytes 262144 | tf_op jit(solution)/shard_map/pallas_call | solution.py:257
  1.7 4.1 %collective-permute-start.1 = (bf16[256,256]{1,0:T(8,128)(2,1)S(1)}, bf16[256,256]{1,0:T(8,128)(2,1)S(1)}, u32[]{:S(2)}, u32[]{:S(2)}) collective-permute-start(bf16[256,256]{1,0:T(8,128)(2,1)S(1)} %shard_map.123.refs_0_), channel_id=1, source_target_pairs={{0,8},{2,10},{4,12},{6,14},{8,0},{10,2},{12,4},{14,6},{1,9},{3,11}... | collective-permute-start | bytes 393224 | tf_op jit(solution)/shard_map/ppermute | solution.py:31
  5.8 1.5 %collective-permute-start.6 = (bf16[256,256]{1,0:T(8,128)(2,1)S(1)}, bf16[256,256]{1,0:T(8,128)(2,1)S(1)}, u32[]{:S(2)}, u32[]{:S(2)}) collective-permute-start(bf16[256,256]{1,0:T(8,128)(2,1)S(1)} %shard_map.123.refs_0_), channel_id=1, source_target_pairs={{0,2},{2,0},{4,6},{6,4},{8,10},{10,8},{12,14},{14,12},{1,3},{3,1},... | collective-permute-start | bytes 393224 | tf_op jit(solution)/shard_map/ppermute | solution.py:31
  7.3 1.6 %collective-permute-start.5 = (bf16[256,256]{1,0:T(8,128)(2,1)S(1)}, bf16[256,256]{1,0:T(8,128)(2,1)S(1)}, u32[]{:S(2)}, u32[]{:S(2)}) collective-permute-start(bf16[256,256]{1,0:T(8,128)(2,1)S(1)} %shard_map.123.refs_0_), channel_id=1, source_target_pairs={{0,4},{2,6},{4,0},{6,2},{8,12},{10,14},{12,8},{14,10},{1,5},{3,7},... | collective-permute-start | bytes 393224 | tf_op jit(solution)/shard_map/ppermute | solution.py:31
  8.9 0.4 collective-permute-start
  9.3 2.9 %collective-permute-done.1.refs_1_ = bf16[256,256]{1,0:T(8,128)(2,1)S(1)} collective-permute-done((bf16[256,256]{1,0:T(8,128)(2,1)S(1)}, bf16[256,256]{1,0:T(8,128)(2,1)S(1)}, u32[]{:S(2)}, u32[]{:S(2)}) %collective-permute-start.1) | collective-permute-done | bytes 131104 | tf_op jit(solution)/shard_map/ppermute | solution.py:31
  12.2 1.6 %collective-permute-start.4 = (bf16[256,256]{1,0:T(8,128)(2,1)S(1)}, bf16[256,256]{1,0:T(8,128)(2,1)S(1)}, u32[]{:S(2)}, u32[]{:S(2)}) collective-permute-start(bf16[256,256]{1,0:T(8,128)(2,1)S(1)} %collective-permute-done.1.refs_1_), channel_id=1, source_target_pairs={{0,6},{2,4},{4,2},{6,0},{8,14},{10,12},{12,10},{14,8},{1,7},{3,5},... | collective-permute-start | bytes 393224 | tf_op jit(solution)/shard_map/ppermute | solution.py:31
  13.8 0.5 %collective-permute-start.3 = (bf16[256,256]{1,0:T(8,128)(2,1)S(1)}, bf16[256,256]{1,0:T(8,128)(2,1)S(1)}, u32[]{:S(2)}, u32[]{:S(2)}) collective-permute-start(bf16[256,256]{1,0:T(8,128)(2,1)S(1)} %collective-permute-done.1.refs_1_), channel_id=1, source_target_pairs={{0,2},{2,0},{4,6},{6,4},{8,10},{10,8},{12,14},{14,12},{1,3},{3,1},... | collective-permute-start | bytes 393224 | tf_op jit(solution)/shard_map/ppermute | solution.py:31
  14.3 0.0 collective-permute-done.6.refs_3_
  14.3 1.4 %collective-permute-start.2 = (bf16[256,256]{1,0:T(8,128)(2,1)S(1)}, bf16[256,256]{1,0:T(8,128)(2,1)S(1)}, u32[]{:S(2)}, u32[]{:S(2)}) collective-permute-start(bf16[256,256]{1,0:T(8,128)(2,1)S(1)} %collective-permute-done.1.refs_1_), channel_id=1, source_target_pairs={{0,4},{2,6},{4,0},{6,2},{8,12},{10,14},{12,8},{14,10},{1,5},{3,7},... | collective-permute-start | bytes 393224 | tf_op jit(solution)/shard_map/ppermute | solution.py:31
  15.7 1.8 %shard_map.122 = (bf16[8,2,32,256]{3,2,1,0:T(8,128)(2,1)S(1)}, bf16[2,512,256]{2,1,0:T(8,128)(2,1)S(1)}, f32[5,256,128]{2,1,0:T(8,128)S(1)}, f32[256,256]{1,0:T(...) custom-call(s32[2,8]{1,0:T(2,128)} %refs_0_.1, bf16[2,8,32,256]{3,2,1,0:T(8,128)(2,1)} %refs_1_.1, ...), custom_call_target="tpu_custom_call" | custom-call | bytes 1051712 | tf_op jit(solution)/shard_map/pallas_call | solution.py:257
  17.4 0.0 collective-permute-done.5.refs_2_
  17.5 0.0 copy-start.3
  17.5 0.0 copy-done
  17.5 0.7 %copy-done.3 = s32[2,2]{1,0:T(2,128)S(1)} copy-done((s32[2,2]{1,0:T(2,128)S(1)}, s32[2,2]{1,0:T(2,128)}, u32[]{:S(2)}) %copy-start.3) | copy-done | bytes 40
  18.1 0.8 %shard_map.124.refs_4_ = f32[2,2,256,256]{3,2,1,0:T(8,128)S(1)} custom-call(s32[2,2]{1,0:T(2,128)S(1)} %copy-done.3, bf16[8,2,32,256]{3,2,1,0:T(8,128)(2,1)S(1)} %get-tuple-element.27.v_ref, bf16[2,512,256]{2,1,0:T(8,128)(2,1)S(1)} %get-tuple-element.28.u_ref, bf16[2,2,2,256,256]{4,3,2,1,0:T(8,128)(2,1)S(1)} %copy-done, ...), custom_call_target="tpu_custom_call" | custom-call | flops 100663296 | bytes 2359312 | tf_op jit(solution)/shard_map/pallas_call | solution.py:257
  18.9 0.0 collective-permute-done.refs_0_
  19.0 1.5 %collective-permute-done.4.refs_3_ = bf16[256,256]{1,0:T(8,128)(2,1)S(1)} collective-permute-done((bf16[256,256]{1,0:T(8,128)(2,1)S(1)}, bf16[256,256]{1,0:T(8,128)(2,1)S(1)}, u32[]{:S(2)}, u32[]{:S(2)}) %collective-permute-start.4) | collective-permute-done | bytes 131104 | tf_op jit(solution)/shard_map/ppermute | solution.py:31
  20.5 1.6 %collective-permute-done.3.refs_2_ = bf16[256,256]{1,0:T(8,128)(2,1)S(1)} collective-permute-done((bf16[256,256]{1,0:T(8,128)(2,1)S(1)}, bf16[256,256]{1,0:T(8,128)(2,1)S(1)}, u32[]{:S(2)}, u32[]{:S(2)}) %collective-permute-start.3) | collective-permute-done | bytes 131104 | tf_op jit(solution)/shard_map/ppermute | solution.py:31
  22.1 0.0 collective-permute-done.2.refs_1_
  22.1 0.6 %shard_map.126 = bf16[2,256,256]{2,1,0:T(8,128)(2,1)S(1)} custom-call(s32[2,2]{1,0:T(2,128)S(1)} %copy-done.3, bf16[8,2,32,256]{3,2,1,0:T(8,128)(2,1)S(1)} %get-tuple-element.27.v_ref, bf16[2,512,256]{2,1,0:T(8,128)(2,1)S(1)} %get-tuple-element.28.u_ref, bf16[2,2,2,256,256]{4,3,2,1,0:T(8,128)(2,1)S(1)} %copy-done, ...), custom_call_target="tpu_custom_call" | custom-call | flops 50331648 | bytes 3407888 | tf_op jit(solution)/shard_map/pallas_call | solution.py:257
  22.7 0.0 copy-start.1
  22.7 0.1 collective-permute-start.7
  22.8 0.6 %shard_map.125.own = f32[2,256,256]{2,1,0:T(8,128)S(1)} custom-call(s32[2,2]{1,0:T(2,128)S(1)} %copy-done.3, bf16[8,2,32,256]{3,2,1,0:T(8,128)(2,1)S(1)} %get-tuple-element.27.v_ref, bf16[2,512,256]{2,1,0:T(8,128)(2,1)S(1)} %get-tuple-element.28.u_ref, bf16[2,2,2,256,256]{4,3,2,1,0:T(8,128)(2,1)S(1)} %copy-done, ...), custom_call_target="tpu_custom_call" | custom-call | flops 50331648 | bytes 3407888 | tf_op jit(solution)/shard_map/pallas_call | solution.py:257
  23.3 0.9 %collective-permute-done.7.other = bf16[2,256,256]{2,1,0:T(8,128)(2,1)S(1)} collective-permute-done((bf16[2,256,256]{2,1,0:T(8,128)(2,1)S(1)}, bf16[2,256,256]{2,1,0:T(8,128)(2,1)S(1)}, u32[]{:S(2)}, u32[]{:S(2)}) %collective-permute-start.7) | collective-permute-done | bytes 262176 | tf_op jit(solution)/shard_map/ppermute | solution.py:353
  24.3 0.0 copy-done.1
  24.3 0.9 %shard_map.127 = (f32[256,256]{1,0:T(8,128)S(1)}, bf16[256,256]{1,0:T(8,128)(2,1)S(1)}) custom-call(f32[2,256,256]{2,1,0:T(8,128)S(1)} %shard_map.125.own, bf16[2,256,256]{2,1,0:T(8,128)(2,1)S(1)} %collective-permute-done.7.other, f32[256,256]{1,0:T(8,128)S(1)} %get-tuple-element.33.weight, f32[256,256]{1,0:T(8,128)S(1)} %get-tuple-element.34.unweight, ...), custom_call_target="tpu_custom_call" | custom-call | flops 13107200 | bytes 2228224 | tf_op jit(solution)/shard_map/pallas_call | solution.py:257
  25.2 1.6 %collective-permute-start.9 = (bf16[256,256]{1,0:T(8,128)(2,1)S(1)}, bf16[256,256]{1,0:T(8,128)(2,1)S(1)}, u32[]{:S(2)}, u32[]{:S(2)}) collective-permute-start(bf16[256,256]{1,0:T(8,128)(2,1)S(1)} %get-tuple-element.45.refs_0_), channel_id=1, source_target_pairs={{0,8},{2,10},{4,12},{6,14},{8,0},{10,2},{12,4},{14,6},{1,9},{3,11}... | collective-permute-start | bytes 393224 | tf_op jit(solution)/shard_map/ppermute | solution.py:31
  26.8 0.6 %collective-permute-start.14 = (bf16[256,256]{1,0:T(8,128)(2,1)S(1)}, bf16[256,256]{1,0:T(8,128)(2,1)S(1)}, u32[]{:S(2)}, u32[]{:S(2)}) collective-permute-start(bf16[256,256]{1,0:T(8,128)(2,1)S(1)} %get-tuple-element.45.refs_0_), channel_id=1, source_target_pairs={{0,2},{2,0},{4,6},{6,4},{8,10},{10,8},{12,14},{14,12},{1,3},{3,1},... | collective-permute-start | bytes 393224 | tf_op jit(solution)/shard_map/ppermute | solution.py:31
  27.4 2.3 %collective-permute-start.13 = (bf16[256,256]{1,0:T(8,128)(2,1)S(1)}, bf16[256,256]{1,0:T(8,128)(2,1)S(1)}, u32[]{:S(2)}, u32[]{:S(2)}) collective-permute-start(bf16[256,256]{1,0:T(8,128)(2,1)S(1)} %get-tuple-element.45.refs_0_), channel_id=1, source_target_pairs={{0,4},{2,6},{4,0},{6,2},{8,12},{10,14},{12,8},{14,10},{1,5},{3,7},... | collective-permute-start | bytes 393224 | tf_op jit(solution)/shard_map/ppermute | solution.py:31
  29.7 0.6 %collective-permute-start.8 = (bf16[256,256]{1,0:T(8,128)(2,1)S(1)}, bf16[256,256]{1,0:T(8,128)(2,1)S(1)}, u32[]{:S(2)}, u32[]{:S(2)}) collective-permute-start(bf16[256,256]{1,0:T(8,128)(2,1)S(1)} %get-tuple-element.45.refs_0_), channel_id=1, source_target_pairs={{0,6},{2,4},{4,2},{6,0},{8,14},{10,12},{12,10},{14,8},{1,7},{3,5},... | collective-permute-start | bytes 393224 | tf_op jit(solution)/shard_map/ppermute | solution.py:31
  30.3 4.3 %collective-permute-done.9.refs_1_ = bf16[256,256]{1,0:T(8,128)(2,1)S(1)} collective-permute-done((bf16[256,256]{1,0:T(8,128)(2,1)S(1)}, bf16[256,256]{1,0:T(8,128)(2,1)S(1)}, u32[]{:S(2)}, u32[]{:S(2)}) %collective-permute-start.9) | collective-permute-done | bytes 131104 | tf_op jit(solution)/shard_map/ppermute | solution.py:31
  34.6 0.0 collective-permute-start.12
  34.6 1.3 %collective-permute-start.11 = (bf16[256,256]{1,0:T(8,128)(2,1)S(1)}, bf16[256,256]{1,0:T(8,128)(2,1)S(1)}, u32[]{:S(2)}, u32[]{:S(2)}) collective-permute-start(bf16[256,256]{1,0:T(8,128)(2,1)S(1)} %collective-permute-done.9.refs_1_), channel_id=1, source_target_pairs={{0,2},{2,0},{4,6},{6,4},{8,10},{10,8},{12,14},{14,12},{1,3},{3,1},... | collective-permute-start | bytes 393224 | tf_op jit(solution)/shard_map/ppermute | solution.py:31
  35.9 0.0 collective-permute-done.14.refs_3_
  35.9 2.2 %collective-permute-start.10 = (bf16[256,256]{1,0:T(8,128)(2,1)S(1)}, bf16[256,256]{1,0:T(8,128)(2,1)S(1)}, u32[]{:S(2)}, u32[]{:S(2)}) collective-permute-start(bf16[256,256]{1,0:T(8,128)(2,1)S(1)} %collective-permute-done.9.refs_1_), channel_id=1, source_target_pairs={{0,4},{2,6},{4,0},{6,2},{8,12},{10,14},{12,8},{14,10},{1,5},{3,7},... | collective-permute-start | bytes 393224 | tf_op jit(solution)/shard_map/ppermute | solution.py:31
  38.1 0.2 shard_map.128
  38.3 0.0 collective-permute-done.13.refs_2_
  38.3 0.8 %shard_map.129.refs_4_ = f32[2,2,256,256]{3,2,1,0:T(8,128)S(1)} custom-call(s32[2,2]{1,0:T(2,128)S(1)} %copy-done.3, bf16[8,2,32,256]{3,2,1,0:T(8,128)(2,1)S(1)} %get-tuple-element.27.v_ref, bf16[2,512,256]{2,1,0:T(8,128)(2,1)S(1)} %get-tuple-element.28.u_ref, bf16[2,2,2,256,256]{4,3,2,1,0:T(8,128)(2,1)S(1)} %copy-done, ...), custom_call_target="tpu_custom_call" | custom-call | flops 100663296 | bytes 2359312 | tf_op jit(solution)/shard_map/pallas_call | solution.py:257
  39.1 0.9 %collective-permute-done.8.refs_0_ = bf16[256,256]{1,0:T(8,128)(2,1)S(1)} collective-permute-done((bf16[256,256]{1,0:T(8,128)(2,1)S(1)}, bf16[256,256]{1,0:T(8,128)(2,1)S(1)}, u32[]{:S(2)}, u32[]{:S(2)}) %collective-permute-start.8) | collective-permute-done | bytes 131104 | tf_op jit(solution)/shard_map/ppermute | solution.py:31
  40.0 2.8 %collective-permute-done.12.refs_3_ = bf16[256,256]{1,0:T(8,128)(2,1)S(1)} collective-permute-done((bf16[256,256]{1,0:T(8,128)(2,1)S(1)}, bf16[256,256]{1,0:T(8,128)(2,1)S(1)}, u32[]{:S(2)}, u32[]{:S(2)}) %collective-permute-start.12) | collective-permute-done | bytes 131104 | tf_op jit(solution)/shard_map/ppermute | solution.py:31
  42.8 1.5 %collective-permute-done.11.refs_2_ = bf16[256,256]{1,0:T(8,128)(2,1)S(1)} collective-permute-done((bf16[256,256]{1,0:T(8,128)(2,1)S(1)}, bf16[256,256]{1,0:T(8,128)(2,1)S(1)}, u32[]{:S(2)}, u32[]{:S(2)}) %collective-permute-start.11) | collective-permute-done | bytes 131104 | tf_op jit(solution)/shard_map/ppermute | solution.py:31
  44.2 0.0 collective-permute-done.10.refs_1_
  44.2 0.6 %shard_map.131 = bf16[2,256,256]{2,1,0:T(8,128)(2,1)S(1)} custom-call(s32[2,2]{1,0:T(2,128)S(1)} %copy-done.3, bf16[8,2,32,256]{3,2,1,0:T(8,128)(2,1)S(1)} %get-tuple-element.27.v_ref, bf16[2,512,256]{2,1,0:T(8,128)(2,1)S(1)} %get-tuple-element.28.u_ref, bf16[2,2,2,256,256]{4,3,2,1,0:T(8,128)(2,1)S(1)} %copy-done, ...), custom_call_target="tpu_custom_call" | custom-call | flops 50331648 | bytes 3407888 | tf_op jit(solution)/shard_map/pallas_call | solution.py:257
  44.8 0.1 collective-permute-start.15
  44.9 0.6 %shard_map.130.own = f32[2,256,256]{2,1,0:T(8,128)S(1)} custom-call(s32[2,2]{1,0:T(2,128)S(1)} %copy-done.3, bf16[8,2,32,256]{3,2,1,0:T(8,128)(2,1)S(1)} %get-tuple-element.27.v_ref, bf16[2,512,256]{2,1,0:T(8,128)(2,1)S(1)} %get-tuple-element.28.u_ref, bf16[2,2,2,256,256]{4,3,2,1,0:T(8,128)(2,1)S(1)} %copy-done, ...), custom_call_target="tpu_custom_call" | custom-call | flops 50331648 | bytes 3407888 | tf_op jit(solution)/shard_map/pallas_call | solution.py:257
  45.5 0.9 %collective-permute-done.15.other = bf16[2,256,256]{2,1,0:T(8,128)(2,1)S(1)} collective-permute-done((bf16[2,256,256]{2,1,0:T(8,128)(2,1)S(1)}, bf16[2,256,256]{2,1,0:T(8,128)(2,1)S(1)}, u32[]{:S(2)}, u32[]{:S(2)}) %collective-permute-start.15) | collective-permute-done | bytes 262176 | tf_op jit(solution)/shard_map/ppermute | solution.py:353
  46.4 1.7 %shard_map.132 = (f32[256,256]{1,0:T(8,128)}, f32[256,256]{1,0:T(8,128)}) custom-call(f32[2,256,256]{2,1,0:T(8,128)S(1)} %shard_map.130.own, bf16[2,256,256]{2,1,0:T(8,128)(2,1)S(1)} %collective-permute-done.15.other, f32[256,256]{1,0:T(8,128)S(1)} %get-tuple-element.46.weight, f32[256,256]{1,0:T(8,128)S(1)} %get-tuple-element.47.unweight, ...), custom_call_target="tpu_custom_call" | custom-call | flops 13107200 | bytes 3538944 | tf_op jit(solution)/shard_map/pallas_call | solution.py:257
  (3 shorter events, 0.0 us)
Async XLA Ops:
  0.6 16.8 %copy-start = (bf16[2,2,2,256,256]{4,3,2,1,0:T(8,128)(2,1)S(1)}, bf16[2,2,2,256,256]{4,3,2,1,0:T(8,128)(2,1)}, u32[]{:S(2)}) copy-start(bf16[2,2,2,256,256]{4,3,2,1,0:T(8,128)(2,1)} %d_ref.11) | copy-start | bytes 3145732
  1.7 10.5 %collective-permute-start.1 = (bf16[256,256]{1,0:T(8,128)(2,1)S(1)}, bf16[256,256]{1,0:T(8,128)(2,1)S(1)}, u32[]{:S(2)}, u32[]{:S(2)}) collective-permute-start(bf16[256,256]{1,0:T(8,128)(2,1)S(1)} %shard_map.123.refs_0_), channel_id=1, source_target_pairs={{0,8},{2,10},{4,12},{6,14},{8,0},{10,2},{12,4},{14,6},{1,9},{3,11}... | collective-permute-start | bytes 393224 | tf_op jit(solution)/shard_map/ppermute | solution.py:31
  5.8 8.5 %collective-permute-start.6 = (bf16[256,256]{1,0:T(8,128)(2,1)S(1)}, bf16[256,256]{1,0:T(8,128)(2,1)S(1)}, u32[]{:S(2)}, u32[]{:S(2)}) collective-permute-start(bf16[256,256]{1,0:T(8,128)(2,1)S(1)} %shard_map.123.refs_0_), channel_id=1, source_target_pairs={{0,2},{2,0},{4,6},{6,4},{8,10},{10,8},{12,14},{14,12},{1,3},{3,1},... | collective-permute-start | bytes 393224 | tf_op jit(solution)/shard_map/ppermute | solution.py:31
  7.3 10.2 %collective-permute-start.5 = (bf16[256,256]{1,0:T(8,128)(2,1)S(1)}, bf16[256,256]{1,0:T(8,128)(2,1)S(1)}, u32[]{:S(2)}, u32[]{:S(2)}) collective-permute-start(bf16[256,256]{1,0:T(8,128)(2,1)S(1)} %shard_map.123.refs_0_), channel_id=1, source_target_pairs={{0,4},{2,6},{4,0},{6,2},{8,12},{10,14},{12,8},{14,10},{1,5},{3,7},... | collective-permute-start | bytes 393224 | tf_op jit(solution)/shard_map/ppermute | solution.py:31
  8.9 10.1 %collective-permute-start = (bf16[256,256]{1,0:T(8,128)(2,1)S(1)}, bf16[256,256]{1,0:T(8,128)(2,1)S(1)}, u32[]{:S(2)}, u32[]{:S(2)}) collective-permute-start(bf16[256,256]{1,0:T(8,128)(2,1)S(1)} %shard_map.123.refs_0_), channel_id=1, source_target_pairs={{0,6},{2,4},{4,2},{6,0},{8,14},{10,12},{12,10},{14,8},{1,7},{3,5},... | collective-permute-start | bytes 393224 | tf_op jit(solution)/shard_map/ppermute | solution.py:31
  12.2 8.3 %collective-permute-start.4 = (bf16[256,256]{1,0:T(8,128)(2,1)S(1)}, bf16[256,256]{1,0:T(8,128)(2,1)S(1)}, u32[]{:S(2)}, u32[]{:S(2)}) collective-permute-start(bf16[256,256]{1,0:T(8,128)(2,1)S(1)} %collective-permute-done.1.refs_1_), channel_id=1, source_target_pairs={{0,6},{2,4},{4,2},{6,0},{8,14},{10,12},{12,10},{14,8},{1,7},{3,5},... | collective-permute-start | bytes 393224 | tf_op jit(solution)/shard_map/ppermute | solution.py:31
  13.8 8.3 %collective-permute-start.3 = (bf16[256,256]{1,0:T(8,128)(2,1)S(1)}, bf16[256,256]{1,0:T(8,128)(2,1)S(1)}, u32[]{:S(2)}, u32[]{:S(2)}) collective-permute-start(bf16[256,256]{1,0:T(8,128)(2,1)S(1)} %collective-permute-done.1.refs_1_), channel_id=1, source_target_pairs={{0,2},{2,0},{4,6},{6,4},{8,10},{10,8},{12,14},{14,12},{1,3},{3,1},... | collective-permute-start | bytes 393224 | tf_op jit(solution)/shard_map/ppermute | solution.py:31
  14.3 7.8 %collective-permute-start.2 = (bf16[256,256]{1,0:T(8,128)(2,1)S(1)}, bf16[256,256]{1,0:T(8,128)(2,1)S(1)}, u32[]{:S(2)}, u32[]{:S(2)}) collective-permute-start(bf16[256,256]{1,0:T(8,128)(2,1)S(1)} %collective-permute-done.1.refs_1_), channel_id=1, source_target_pairs={{0,4},{2,6},{4,0},{6,2},{8,12},{10,14},{12,8},{14,10},{1,5},{3,7},... | collective-permute-start | bytes 393224 | tf_op jit(solution)/shard_map/ppermute | solution.py:31
  17.5 0.7 %copy-start.3 = (s32[2,2]{1,0:T(2,128)S(1)}, s32[2,2]{1,0:T(2,128)}, u32[]{:S(2)}) copy-start(s32[2,2]{1,0:T(2,128)} %near_ref.11) | copy-start | bytes 52
  22.7 1.6 %copy-start.1 = (f32[256,256]{1,0:T(8,128)S(1)}, f32[256,256]{1,0:T(8,128)}, u32[]{:S(2)}) copy-start(f32[256,256]{1,0:T(8,128)} %tau.3) | copy-start | bytes 786436
  22.7 1.6 %collective-permute-start.7 = (bf16[2,256,256]{2,1,0:T(8,128)(2,1)S(1)}, bf16[2,256,256]{2,1,0:T(8,128)(2,1)S(1)}, u32[]{:S(2)}, u32[]{:S(2)}) collective-permute-start(bf16[2,256,256]{2,1,0:T(8,128)(2,1)S(1)} %shard_map.126), channel_id=1, source_target_pairs={{0,1},{1,0},{2,3},{3,2},{4,5},{5,4},{6,7},{7,6},{8,9},{9,8},{10,11... | collective-permute-start | bytes 786440 | tf_op jit(solution)/shard_map/ppermute | solution.py:353
  24.3 13.8 %copy-start.2 = (f32[256,256]{1,0:T(8,128)S(1)}, f32[256,256]{1,0:T(8,128)}, u32[]{:S(2)}) copy-start(f32[256,256]{1,0:T(8,128)} %state.1) | copy-start | bytes 786436
  25.2 9.4 %collective-permute-start.9 = (bf16[256,256]{1,0:T(8,128)(2,1)S(1)}, bf16[256,256]{1,0:T(8,128)(2,1)S(1)}, u32[]{:S(2)}, u32[]{:S(2)}) collective-permute-start(bf16[256,256]{1,0:T(8,128)(2,1)S(1)} %get-tuple-element.45.refs_0_), channel_id=1, source_target_pairs={{0,8},{2,10},{4,12},{6,14},{8,0},{10,2},{12,4},{14,6},{1,9},{3,11}... | collective-permute-start | bytes 393224 | tf_op jit(solution)/shard_map/ppermute | solution.py:31
  26.8 9.0 %collective-permute-start.14 = (bf16[256,256]{1,0:T(8,128)(2,1)S(1)}, bf16[256,256]{1,0:T(8,128)(2,1)S(1)}, u32[]{:S(2)}, u32[]{:S(2)}) collective-permute-start(bf16[256,256]{1,0:T(8,128)(2,1)S(1)} %get-tuple-element.45.refs_0_), channel_id=1, source_target_pairs={{0,2},{2,0},{4,6},{6,4},{8,10},{10,8},{12,14},{14,12},{1,3},{3,1},... | collective-permute-start | bytes 393224 | tf_op jit(solution)/shard_map/ppermute | solution.py:31
  27.4 10.9 %collective-permute-start.13 = (bf16[256,256]{1,0:T(8,128)(2,1)S(1)}, bf16[256,256]{1,0:T(8,128)(2,1)S(1)}, u32[]{:S(2)}, u32[]{:S(2)}) collective-permute-start(bf16[256,256]{1,0:T(8,128)(2,1)S(1)} %get-tuple-element.45.refs_0_), channel_id=1, source_target_pairs={{0,4},{2,6},{4,0},{6,2},{8,12},{10,14},{12,8},{14,10},{1,5},{3,7},... | collective-permute-start | bytes 393224 | tf_op jit(solution)/shard_map/ppermute | solution.py:31
  29.7 10.3 %collective-permute-start.8 = (bf16[256,256]{1,0:T(8,128)(2,1)S(1)}, bf16[256,256]{1,0:T(8,128)(2,1)S(1)}, u32[]{:S(2)}, u32[]{:S(2)}) collective-permute-start(bf16[256,256]{1,0:T(8,128)(2,1)S(1)} %get-tuple-element.45.refs_0_), channel_id=1, source_target_pairs={{0,6},{2,4},{4,2},{6,0},{8,14},{10,12},{12,10},{14,8},{1,7},{3,5},... | collective-permute-start | bytes 393224 | tf_op jit(solution)/shard_map/ppermute | solution.py:31
  34.6 8.2 %collective-permute-start.12 = (bf16[256,256]{1,0:T(8,128)(2,1)S(1)}, bf16[256,256]{1,0:T(8,128)(2,1)S(1)}, u32[]{:S(2)}, u32[]{:S(2)}) collective-permute-start(bf16[256,256]{1,0:T(8,128)(2,1)S(1)} %collective-permute-done.9.refs_1_), channel_id=1, source_target_pairs={{0,6},{2,4},{4,2},{6,0},{8,14},{10,12},{12,10},{14,8},{1,7},{3,5},... | collective-permute-start | bytes 393224 | tf_op jit(solution)/shard_map/ppermute | solution.py:31
  34.6 9.6 %collective-permute-start.11 = (bf16[256,256]{1,0:T(8,128)(2,1)S(1)}, bf16[256,256]{1,0:T(8,128)(2,1)S(1)}, u32[]{:S(2)}, u32[]{:S(2)}) collective-permute-start(bf16[256,256]{1,0:T(8,128)(2,1)S(1)} %collective-permute-done.9.refs_1_), channel_id=1, source_target_pairs={{0,2},{2,0},{4,6},{6,4},{8,10},{10,8},{12,14},{14,12},{1,3},{3,1},... | collective-permute-start | bytes 393224 | tf_op jit(solution)/shard_map/ppermute | solution.py:31
  35.9 8.4 %collective-permute-start.10 = (bf16[256,256]{1,0:T(8,128)(2,1)S(1)}, bf16[256,256]{1,0:T(8,128)(2,1)S(1)}, u32[]{:S(2)}, u32[]{:S(2)}) collective-permute-start(bf16[256,256]{1,0:T(8,128)(2,1)S(1)} %collective-permute-done.9.refs_1_), channel_id=1, source_target_pairs={{0,4},{2,6},{4,0},{6,2},{8,12},{10,14},{12,8},{14,10},{1,5},{3,7},... | collective-permute-start | bytes 393224 | tf_op jit(solution)/shard_map/ppermute | solution.py:31
  44.8 1.6 %collective-permute-start.15 = (bf16[2,256,256]{2,1,0:T(8,128)(2,1)S(1)}, bf16[2,256,256]{2,1,0:T(8,128)(2,1)S(1)}, u32[]{:S(2)}, u32[]{:S(2)}) collective-permute-start(bf16[2,256,256]{2,1,0:T(8,128)(2,1)S(1)} %shard_map.131), channel_id=1, source_target_pairs={{0,1},{1,0},{2,3},{3,2},{4,5},{5,4},{6,7},{7,6},{8,9},{9,8},{10,11... | collective-permute-start | bytes 786440 | tf_op jit(solution)/shard_map/ppermute | solution.py:353

commit v24 on v23

--- a/solution.py
+++ b/solution.py
@@ -9,7 +9,7 @@
 
 NEWTON = 2
 DIRECT_COUNTS = (4, 8)
-LATE = 4
+TILE = 128
 
 damping = 0.5
 sigma_floor = 0.5
@@ -18,8 +18,9 @@
 
 def arrivals(count, direct):
     if not direct:
-        return list(range(count))
-    return [0, 4, 2, 1, 3, 6, 5, 7] if count == 8 else [0, 1, 2, 3]
+        cuts = [0, max(count - 4, 0), count]
+        return [list(range(first, last)) for first, last in zip(cuts, cuts[1:]) if last > first]
+    return [[0, 1, 4, 3, 2], [6, 5, 7]] if count == 8 else [[0, 1], [2, 3]]
 
 
 def row_met(spot, row, direct):
@@ -36,7 +37,7 @@
     if count == 8:
         for mask in (1, 2, 3):
             found[4 + mask] = swapped(mask, found[4])
-    return [found[mask] for mask in arrivals(count, True)]
+    return [[found[mask] for mask in group] for group in arrivals(count, True)]
 
 
 IN_PIECES = 8
@@ -77,7 +78,7 @@
         store_powers(outs, part, state[:, part] + section_step * step, coef)
 
 
-def prepare_kernel(spots, direct, *refs):
+def prepare_kernel(groups, direct, *refs):
     far, (v_out, u_out, coef_out, *powers), near, sem = refs[:7], refs[7:13], refs[13:20], refs[20]
     copies = [
         pltpu.make_async_copy(source, held, sem.at[at])
@@ -90,19 +91,23 @@
     rank_ref, v_ref, u_ref, sigma_ref, a_ref, b_ref, state_ref = near
     kinds, rows, count, rank_count, size = u_ref.shape
     row = lax.axis_index("row")
-    met = [row_met(spot, row, direct) for spot in spots]
+    met = [row_met(spot, row, direct) for group in groups for spot in group]
     for at, q in enumerate(met):
         for p in range(rows):
             inside = lax.broadcasted_iota(jnp.int32, (rank_count, size), 0) < rank_ref[p, q]
             v_out[at, p] = jnp.where(inside, v_ref[p, q].astype(jnp.float32), 0.0).astype(v_out.dtype)
     for p in range(rows):
         for kind in range(kinds):
-            for first in range(0, count, 4):
-                group = [u_ref[kind, p, q] for q in met[first : first + 4]]
+            first = start = 0
+            for spots in groups:
+                group = [u_ref[kind, p, q] for q in met[first : first + len(spots)]]
+                spare = -len(group) * rank_count % TILE
+                if spare:
+                    group.append(jnp.zeros((spare, size), u_ref.dtype))
                 turned = jnp.concatenate(group, axis=0).astype(jnp.float32).T
-                u_out[p, kind * size : (kind + 1) * size, first * rank_count : (first + len(group)) * rank_count] = (
-                    turned.astype(u_out.dtype)
-                )
+                stop = start + turned.shape[1]
+                u_out[p, kind * size : (kind + 1) * size, start:stop] = turned.astype(u_out.dtype)
+                first, start = first + len(spots), stop
     lanes = coef_out.shape[2]
     for at, values in enumerate((sigma_ref[...], a_ref[...], b_ref[...], 1.0 / a_ref[...], 1.0 / b_ref[...])):
         coef_out[at] = jnp.broadcast_to(values, (lanes, size)).T
@@ -111,7 +116,7 @@
         store_powers(powers, part, state_ref[:, part], coef_out)
 
 
-def sums_kernel(spots, direct, first, pick, before, near_ref, v_ref, u_ref, d_ref, *refs):
+def sums_kernel(spots, direct, first, start, pick, before, near_ref, v_ref, u_ref, d_ref, *refs):
     blocks = refs[: len(spots)]
     refs = refs[len(spots) :]
     if before:
@@ -133,7 +138,13 @@
             proj[place, at * rank_count : (at + 1) * rank_count, :] = part[
                 place * rank_count : (place + 1) * rank_count
             ]
-    lanes = slice(first * rank_count, (first + len(blocks)) * rank_count)
+    width = proj.shape[1]
+    lanes = slice(start, start + width)
+    if width > len(blocks) * rank_count:
+        for place in range(len(chosen)):
+            proj[place, len(blocks) * rank_count :, :] = jnp.zeros(
+                (width - len(blocks) * rank_count, proj.shape[2]), proj.dtype
+            )
     for place, p in enumerate(chosen):
         weights, fields = [u_ref[p, :, lanes]], [proj[place]]
         for s in range(slots):
@@ -284,8 +295,10 @@
     size, members = slip_deficit.shape
     kinds, rows, _, rank_count, _ = u_basis.shape
     direct = count in DIRECT_COUNTS
-    spots = arrivals(count, direct)
-    early = max(count - LATE, 0)
+    groups = arrivals(count, direct)
+    firsts = [sum(len(group) for group in groups[:at]) for at in range(len(groups))]
+    tiles = [-(-len(group) * rank_count // TILE) * TILE for group in groups]
+    starts = [sum(tiles[:at]) for at in range(len(groups))]
     room = 16 if direct else 40
     lanes = min(members, 128)
     narrow, wide = jnp.bfloat16, jnp.float32
@@ -296,10 +309,10 @@
 
     full = shaped(size, members)
     v_met, u_met, coef, *powers = on_core(
-        functools.partial(prepare_kernel, spots, direct),
+        functools.partial(prepare_kernel, groups, direct),
         (
             shaped(count, rows, rank_count, size, kind=narrow),
-            shaped(rows, kinds * size, count * rank_count, kind=narrow),
+            shaped(rows, kinds * size, sum(tiles), kind=narrow),
             shaped(5, size, lanes),
             full,
             full,
@@ -326,17 +339,17 @@
         ),
     )
 
-    def add(blocks, first, pick, before, kind):
+    def add(blocks, at, pick, before, kind):
         held = rows if pick is None else 1
         lead = (rows, kinds) if pick is None else (kinds,)
         return on_core(
             functools.partial(
-                sums_kernel, spots[first : first + len(blocks)], direct, first, pick, before is not None
+                sums_kernel, groups[at], direct, firsts[at], starts[at], pick, before is not None
             ),
             shaped(*lead, size, members, kind=kind),
             (near_index, v_met, u_met, dense_blocks, *blocks, *(() if before is None else (before,))),
             (
-                pltpu.VMEM((held, len(blocks) * rank_count, members), narrow),
+                pltpu.VMEM((held, tiles[at], members), narrow),
             ),
             2 * held * size * members * rank_count * len(blocks) * 3,
             room,
@@ -344,14 +357,16 @@
 
     def lattice(field_half, beside):
         if direct:
-            blocks = gather_direct(field_half, count)
+            found = gather_direct(field_half, count)
         else:
             whole = lax.all_gather(field_half, "row", axis=0)
-            blocks = [whole[r] for r in range(count)]
-        blocks[0], beside = lax.optimization_barrier((blocks[0], beside))
-        sums = add(blocks[:early], 0, None, None, wide) if early else None
-        other = lax.ppermute(add(blocks[early:], early, 1, sums, narrow), "col", swap)
-        return add(blocks[early:], early, 0, sums, wide), other, beside
+            found = [[whole[r] for r in group] for group in groups]
+        found[0][0], beside = lax.optimization_barrier((found[0][0], beside))
+        sums, end = None, len(groups) - 1
+        for at in range(end):
+            sums = add(found[at], at, None, sums, wide)
+        other = lax.ppermute(add(found[end], end, 1, sums, narrow), "col", swap)
+        return add(found[end], end, 0, sums, wide), other, beside
 
     slip_half = on_core(
         narrow_kernel,

time: 48.3 us -> 46.7 us (0.967)
  waiting for transfers between devices: 17.4 us -> 15.4 us
    ppermute x14, waiting for transfers between devices: 15.5 us -> 13.5 us  [swapped(): lax.ppermute(data, 'row', [(row, row ^ mask) for row in range(count)])]
where the time goes in v24:
time: 46.7 us; the launch traced here: 46.5 us
  starting transfers between devices  20.1 us (43%)
  waiting for transfers between devices  15.4 us (33%)
  Pallas kernels  9.49 us (20%)
  between operations  0.75 us (2%)
  local copies, waits for them, and re-layouts  0.69 us (1%)
    ppermute x14, starting transfers between devices, swapped(): lax.ppermute(data, 'row', [(row, row ^ mask) for row in range(count)])  20 us
    ppermute x14, waiting for transfers between devices, swapped(): lax.ppermute(data, 'row', [(row, row ^ mask) for row in range(count)])  13.5 us
    pallas_call x11, Pallas kernels, on_core(): pl.pallas_call(kernel, out_shape=outs, in_specs=[hbm] * len(far) + [vmem]...  9.49 us
    ppermute x2, waiting for transfers between devices, lattice(): other = lax.ppermute(add(found[end], end, 1, sums, narrow), 'col', swap)  1.96 us
  transfers between devices with their start and end apart: 16, of which 9 were waited for; matrix products, arithmetic and copies ran while one was open for 0% of the time, Pallas kernels for 10%

profile of v24, /device:TPU:0, one launch (start us, length us, event | category | flops | bytes accessed | tf_op | source)
XLA Modules:
  0.0 46.5 jit_solution(13248360441271623466)
XLA Ops:
  0.6 0.0 copy-start
  0.6 1.0 %shard_map.123.refs_0_ = bf16[256,256]{1,0:T(8,128)(2,1)S(1)} custom-call(f32[256,256]{1,0:T(8,128)} %wide_ref.1), custom_call_target="tpu_custom_call" | custom-call | bytes 262144 | tf_op jit(solution)/shard_map/pallas_call | solution.py:268
  1.7 4.1 %collective-permute-start = (bf16[256,256]{1,0:T(8,128)(2,1)S(1)}, bf16[256,256]{1,0:T(8,128)(2,1)S(1)}, u32[]{:S(2)}, u32[]{:S(2)}) collective-permute-start(bf16[256,256]{1,0:T(8,128)(2,1)S(1)} %shard_map.123.refs_0_), channel_id=1, source_target_pairs={{0,8},{2,10},{4,12},{6,14},{8,0},{10,2},{12,4},{14,6},{1,9},{3,11}... | collective-permute-start | bytes 393224 | tf_op jit(solution)/shard_map/ppermute | solution.py:32
  5.8 1.6 %collective-permute-start.6 = (bf16[256,256]{1,0:T(8,128)(2,1)S(1)}, bf16[256,256]{1,0:T(8,128)(2,1)S(1)}, u32[]{:S(2)}, u32[]{:S(2)}) collective-permute-start(bf16[256,256]{1,0:T(8,128)(2,1)S(1)} %shard_map.123.refs_0_), channel_id=1, source_target_pairs={{0,4},{2,6},{4,0},{6,2},{8,12},{10,14},{12,8},{14,10},{1,5},{3,7},... | collective-permute-start | bytes 393224 | tf_op jit(solution)/shard_map/ppermute | solution.py:32
  7.4 1.4 %collective-permute-start.5 = (bf16[256,256]{1,0:T(8,128)(2,1)S(1)}, bf16[256,256]{1,0:T(8,128)(2,1)S(1)}, u32[]{:S(2)}, u32[]{:S(2)}) collective-permute-start(bf16[256,256]{1,0:T(8,128)(2,1)S(1)} %shard_map.123.refs_0_), channel_id=1, source_target_pairs={{0,6},{2,4},{4,2},{6,0},{8,14},{10,12},{12,10},{14,8},{1,7},{3,5},... | collective-permute-start | bytes 393224 | tf_op jit(solution)/shard_map/ppermute | solution.py:32
  8.8 0.5 %collective-permute-start.4 = (bf16[256,256]{1,0:T(8,128)(2,1)S(1)}, bf16[256,256]{1,0:T(8,128)(2,1)S(1)}, u32[]{:S(2)}, u32[]{:S(2)}) collective-permute-start(bf16[256,256]{1,0:T(8,128)(2,1)S(1)} %shard_map.123.refs_0_), channel_id=1, source_target_pairs={{0,2},{2,0},{4,6},{6,4},{8,10},{10,8},{12,14},{14,12},{1,3},{3,1},... | collective-permute-start | bytes 393224 | tf_op jit(solution)/shard_map/ppermute | solution.py:32
  9.3 2.9 %collective-permute-done.refs_2_ = bf16[256,256]{1,0:T(8,128)(2,1)S(1)} collective-permute-done((bf16[256,256]{1,0:T(8,128)(2,1)S(1)}, bf16[256,256]{1,0:T(8,128)(2,1)S(1)}, u32[]{:S(2)}, u32[]{:S(2)}) %collective-permute-start) | collective-permute-done | bytes 131104 | tf_op jit(solution)/shard_map/ppermute | solution.py:32
  12.2 1.6 %collective-permute-start.3 = (bf16[256,256]{1,0:T(8,128)(2,1)S(1)}, bf16[256,256]{1,0:T(8,128)(2,1)S(1)}, u32[]{:S(2)}, u32[]{:S(2)}) collective-permute-start(bf16[256,256]{1,0:T(8,128)(2,1)S(1)} %collective-permute-done.refs_2_), channel_id=1, source_target_pairs={{0,6},{2,4},{4,2},{6,0},{8,14},{10,12},{12,10},{14,8},{1,7},{3,5},... | collective-permute-start | bytes 393224 | tf_op jit(solution)/shard_map/ppermute | solution.py:32
  13.8 0.5 %collective-permute-start.2 = (bf16[256,256]{1,0:T(8,128)(2,1)S(1)}, bf16[256,256]{1,0:T(8,128)(2,1)S(1)}, u32[]{:S(2)}, u32[]{:S(2)}) collective-permute-start(bf16[256,256]{1,0:T(8,128)(2,1)S(1)} %collective-permute-done.refs_2_), channel_id=1, source_target_pairs={{0,2},{2,0},{4,6},{6,4},{8,10},{10,8},{12,14},{14,12},{1,3},{3,1},... | collective-permute-start | bytes 393224 | tf_op jit(solution)/shard_map/ppermute | solution.py:32
  14.3 0.0 collective-permute-done.6.refs_4_
  14.3 1.4 %collective-permute-start.1 = (bf16[256,256]{1,0:T(8,128)(2,1)S(1)}, bf16[256,256]{1,0:T(8,128)(2,1)S(1)}, u32[]{:S(2)}, u32[]{:S(2)}) collective-permute-start(bf16[256,256]{1,0:T(8,128)(2,1)S(1)} %collective-permute-done.refs_2_), channel_id=1, source_target_pairs={{0,4},{2,6},{4,0},{6,2},{8,12},{10,14},{12,8},{14,10},{1,5},{3,7},... | collective-permute-start | bytes 393224 | tf_op jit(solution)/shard_map/ppermute | solution.py:32
  15.7 1.8 %shard_map.122 = (bf16[8,2,32,256]{3,2,1,0:T(8,128)(2,1)S(1)}, bf16[2,512,384]{2,1,0:T(8,128)(2,1)S(1)}, f32[5,256,128]{2,1,0:T(8,128)S(1)}, f32[256,256]{1,0:T(...) custom-call(s32[2,8]{1,0:T(2,128)} %refs_0_.1, bf16[2,8,32,256]{3,2,1,0:T(8,128)(2,1)} %refs_1_.1, ...), custom_call_target="tpu_custom_call" | custom-call | bytes 1051712 | tf_op jit(solution)/shard_map/pallas_call | solution.py:268
  17.5 0.2 collective-permute-done.5.refs_3_
  17.7 0.0 collective-permute-done.4.refs_1_
  17.7 0.0 copy-done
  17.7 0.7 %copy-done.3 = s32[2,2]{1,0:T(2,128)S(1)} copy-done((s32[2,2]{1,0:T(2,128)S(1)}, s32[2,2]{1,0:T(2,128)}, u32[]{:S(2)}) %copy-start.3) | copy-done | bytes 40
  18.4 0.9 %shard_map.124.refs_3_ = f32[2,2,256,256]{3,2,1,0:T(8,128)S(1)} custom-call(s32[2,2]{1,0:T(2,128)S(1)} %copy-done.3, bf16[8,2,32,256]{3,2,1,0:T(8,128)(2,1)S(1)} %get-tuple-element.27.v_ref, bf16[2,512,384]{2,1,0:T(8,128)(2,1)S(1)} %get-tuple-element.28.u_ref, bf16[2,2,2,256,256]{4,3,2,1,0:T(8,128)(2,1)S(1)} %copy-done, ...), custom_call_target="tpu_custom_call" | custom-call | flops 125829120 | bytes 2752528 | tf_op jit(solution)/shard_map/pallas_call | solution.py:268
  19.2 1.2 %collective-permute-done.3.refs_2_ = bf16[256,256]{1,0:T(8,128)(2,1)S(1)} collective-permute-done((bf16[256,256]{1,0:T(8,128)(2,1)S(1)}, bf16[256,256]{1,0:T(8,128)(2,1)S(1)}, u32[]{:S(2)}, u32[]{:S(2)}) %collective-permute-start.3) | collective-permute-done | bytes 131104 | tf_op jit(solution)/shard_map/ppermute | solution.py:32
  20.4 1.4 %collective-permute-done.2.refs_1_ = bf16[256,256]{1,0:T(8,128)(2,1)S(1)} collective-permute-done((bf16[256,256]{1,0:T(8,128)(2,1)S(1)}, bf16[256,256]{1,0:T(8,128)(2,1)S(1)}, u32[]{:S(2)}, u32[]{:S(2)}) %collective-permute-start.2) | collective-permute-done | bytes 131104 | tf_op jit(solution)/shard_map/ppermute | solution.py:32
  21.8 0.0 collective-permute-done.1.refs_0_
  21.8 0.5 %shard_map.126 = bf16[2,256,256]{2,1,0:T(8,128)(2,1)S(1)} custom-call(s32[2,2]{1,0:T(2,128)S(1)} %copy-done.3, bf16[8,2,32,256]{3,2,1,0:T(8,128)(2,1)S(1)} %get-tuple-element.27.v_ref, bf16[2,512,384]{2,1,0:T(8,128)(2,1)S(1)} %get-tuple-element.28.u_ref, bf16[2,2,2,256,256]{4,3,2,1,0:T(8,128)(2,1)S(1)} %copy-done, ...), custom_call_target="tpu_custom_call" | custom-call | flops 37748736 | bytes 3538960 | tf_op jit(solution)/shard_map/pallas_call | solution.py:268
  22.4 0.0 copy-start.1
  22.4 0.1 collective-permute-start.7
  22.4 0.5 %shard_map.125.own = f32[2,256,256]{2,1,0:T(8,128)S(1)} custom-call(s32[2,2]{1,0:T(2,128)S(1)} %copy-done.3, bf16[8,2,32,256]{3,2,1,0:T(8,128)(2,1)S(1)} %get-tuple-element.27.v_ref, bf16[2,512,384]{2,1,0:T(8,128)(2,1)S(1)} %get-tuple-element.28.u_ref, bf16[2,2,2,256,256]{4,3,2,1,0:T(8,128)(2,1)S(1)} %copy-done, ...), custom_call_target="tpu_custom_call" | custom-call | flops 37748736 | bytes 3538960 | tf_op jit(solution)/shard_map/pallas_call | solution.py:268
  23.0 1.0 %collective-permute-done.7.other = bf16[2,256,256]{2,1,0:T(8,128)(2,1)S(1)} collective-permute-done((bf16[2,256,256]{2,1,0:T(8,128)(2,1)S(1)}, bf16[2,256,256]{2,1,0:T(8,128)(2,1)S(1)}, u32[]{:S(2)}, u32[]{:S(2)}) %collective-permute-start.7) | collective-permute-done | bytes 262176 | tf_op jit(solution)/shard_map/ppermute | solution.py:368
  24.0 0.0 copy-done.1
  24.0 0.9 %shard_map.127 = (f32[256,256]{1,0:T(8,128)S(1)}, bf16[256,256]{1,0:T(8,128)(2,1)S(1)}) custom-call(f32[2,256,256]{2,1,0:T(8,128)S(1)} %shard_map.125.own, bf16[2,256,256]{2,1,0:T(8,128)(2,1)S(1)} %collective-permute-done.7.other, f32[256,256]{1,0:T(8,128)S(1)} %get-tuple-element.33.weight, f32[256,256]{1,0:T(8,128)S(1)} %get-tuple-element.34.unweight, ...), custom_call_target="tpu_custom_call" | custom-call | flops 13107200 | bytes 2228224 | tf_op jit(solution)/shard_map/pallas_call | solution.py:268
  24.9 1.9 %collective-permute-start.8 = (bf16[256,256]{1,0:T(8,128)(2,1)S(1)}, bf16[256,256]{1,0:T(8,128)(2,1)S(1)}, u32[]{:S(2)}, u32[]{:S(2)}) collective-permute-start(bf16[256,256]{1,0:T(8,128)(2,1)S(1)} %get-tuple-element.45.refs_0_), channel_id=1, source_target_pairs={{0,8},{2,10},{4,12},{6,14},{8,0},{10,2},{12,4},{14,6},{1,9},{3,11}... | collective-permute-start | bytes 393224 | tf_op jit(solution)/shard_map/ppermute | solution.py:32
  26.8 1.8 %collective-permute-start.14 = (bf16[256,256]{1,0:T(8,128)(2,1)S(1)}, bf16[256,256]{1,0:T(8,128)(2,1)S(1)}, u32[]{:S(2)}, u32[]{:S(2)}) collective-permute-start(bf16[256,256]{1,0:T(8,128)(2,1)S(1)} %get-tuple-element.45.refs_0_), channel_id=1, source_target_pairs={{0,4},{2,6},{4,0},{6,2},{8,12},{10,14},{12,8},{14,10},{1,5},{3,7},... | collective-permute-start | bytes 393224 | tf_op jit(solution)/shard_map/ppermute | solution.py:32
  28.6 0.2 collective-permute-start.13
  28.8 1.5 %collective-permute-start.12 = (bf16[256,256]{1,0:T(8,128)(2,1)S(1)}, bf16[256,256]{1,0:T(8,128)(2,1)S(1)}, u32[]{:S(2)}, u32[]{:S(2)}) collective-permute-start(bf16[256,256]{1,0:T(8,128)(2,1)S(1)} %get-tuple-element.45.refs_0_), channel_id=1, source_target_pairs={{0,2},{2,0},{4,6},{6,4},{8,10},{10,8},{12,14},{14,12},{1,3},{3,1},... | collective-permute-start | bytes 393224 | tf_op jit(solution)/shard_map/ppermute | solution.py:32
  30.3 4.0 %collective-permute-done.8.refs_2_ = bf16[256,256]{1,0:T(8,128)(2,1)S(1)} collective-permute-done((bf16[256,256]{1,0:T(8,128)(2,1)S(1)}, bf16[256,256]{1,0:T(8,128)(2,1)S(1)}, u32[]{:S(2)}, u32[]{:S(2)}) %collective-permute-start.8) | collective-permute-done | bytes 131104 | tf_op jit(solution)/shard_map/ppermute | solution.py:32
  34.3 0.0 collective-permute-start.11
  34.3 1.3 %collective-permute-start.10 = (bf16[256,256]{1,0:T(8,128)(2,1)S(1)}, bf16[256,256]{1,0:T(8,128)(2,1)S(1)}, u32[]{:S(2)}, u32[]{:S(2)}) collective-permute-start(bf16[256,256]{1,0:T(8,128)(2,1)S(1)} %collective-permute-done.8.refs_2_), channel_id=1, source_target_pairs={{0,2},{2,0},{4,6},{6,4},{8,10},{10,8},{12,14},{14,12},{1,3},{3,1},... | collective-permute-start | bytes 393224 | tf_op jit(solution)/shard_map/ppermute | solution.py:32
  35.6 0.0 collective-permute-done.14.refs_4_
  35.6 2.1 %collective-permute-start.9 = (bf16[256,256]{1,0:T(8,128)(2,1)S(1)}, bf16[256,256]{1,0:T(8,128)(2,1)S(1)}, u32[]{:S(2)}, u32[]{:S(2)}) collective-permute-start(bf16[256,256]{1,0:T(8,128)(2,1)S(1)} %collective-permute-done.8.refs_2_), channel_id=1, source_target_pairs={{0,4},{2,6},{4,0},{6,2},{8,12},{10,14},{12,8},{14,10},{1,5},{3,7},... | collective-permute-start | bytes 393224 | tf_op jit(solution)/shard_map/ppermute | solution.py:32
  37.8 0.2 shard_map.128
  38.0 0.0 collective-permute-done.13.refs_3_
  38.0 0.0 collective-permute-done.12.refs_1_
  38.0 0.8 %shard_map.129.refs_3_ = f32[2,2,256,256]{3,2,1,0:T(8,128)S(1)} custom-call(s32[2,2]{1,0:T(2,128)S(1)} %copy-done.3, bf16[8,2,32,256]{3,2,1,0:T(8,128)(2,1)S(1)} %get-tuple-element.27.v_ref, bf16[2,512,384]{2,1,0:T(8,128)(2,1)S(1)} %get-tuple-element.28.u_ref, bf16[2,2,2,256,256]{4,3,2,1,0:T(8,128)(2,1)S(1)} %copy-done, ...), custom_call_target="tpu_custom_call" | custom-call | flops 125829120 | bytes 2752528 | tf_op jit(solution)/shard_map/pallas_call | solution.py:268
  38.9 2.4 %collective-permute-done.11.refs_2_ = bf16[256,256]{1,0:T(8,128)(2,1)S(1)} collective-permute-done((bf16[256,256]{1,0:T(8,128)(2,1)S(1)}, bf16[256,256]{1,0:T(8,128)(2,1)S(1)}, u32[]{:S(2)}, u32[]{:S(2)}) %collective-permute-start.11) | collective-permute-done | bytes 131104 | tf_op jit(solution)/shard_map/ppermute | solution.py:32
  41.3 1.3 %collective-permute-done.10.refs_1_ = bf16[256,256]{1,0:T(8,128)(2,1)S(1)} collective-permute-done((bf16[256,256]{1,0:T(8,128)(2,1)S(1)}, bf16[256,256]{1,0:T(8,128)(2,1)S(1)}, u32[]{:S(2)}, u32[]{:S(2)}) %collective-permute-start.10) | collective-permute-done | bytes 131104 | tf_op jit(solution)/shard_map/ppermute | solution.py:32
  42.6 0.0 collective-permute-done.9.refs_0_
  42.7 0.5 %shard_map.131 = bf16[2,256,256]{2,1,0:T(8,128)(2,1)S(1)} custom-call(s32[2,2]{1,0:T(2,128)S(1)} %copy-done.3, bf16[8,2,32,256]{3,2,1,0:T(8,128)(2,1)S(1)} %get-tuple-element.27.v_ref, bf16[2,512,384]{2,1,0:T(8,128)(2,1)S(1)} %get-tuple-element.28.u_ref, bf16[2,2,2,256,256]{4,3,2,1,0:T(8,128)(2,1)S(1)} %copy-done, ...), custom_call_target="tpu_custom_call" | custom-call | flops 37748736 | bytes 3538960 | tf_op jit(solution)/shard_map/pallas_call | solution.py:268
  43.2 0.1 collective-permute-start.15
  43.3 0.5 %shard_map.130.own = f32[2,256,256]{2,1,0:T(8,128)S(1)} custom-call(s32[2,2]{1,0:T(2,128)S(1)} %copy-done.3, bf16[8,2,32,256]{3,2,1,0:T(8,128)(2,1)S(1)} %get-tuple-element.27.v_ref, bf16[2,512,384]{2,1,0:T(8,128)(2,1)S(1)} %get-tuple-element.28.u_ref, bf16[2,2,2,256,256]{4,3,2,1,0:T(8,128)(2,1)S(1)} %copy-done, ...), custom_call_target="tpu_custom_call" | custom-call | flops 37748736 | bytes 3538960 | tf_op jit(solution)/shard_map/pallas_call | solution.py:268
  43.8 1.0 %collective-permute-done.15.other = bf16[2,256,256]{2,1,0:T(8,128)(2,1)S(1)} collective-permute-done((bf16[2,256,256]{2,1,0:T(8,128)(2,1)S(1)}, bf16[2,256,256]{2,1,0:T(8,128)(2,1)S(1)}, u32[]{:S(2)}, u32[]{:S(2)}) %collective-permute-start.15) | collective-permute-done | bytes 262176 | tf_op jit(solution)/shard_map/ppermute | solution.py:368
  44.8 1.7 %shard_map.132 = (f32[256,256]{1,0:T(8,128)}, f32[256,256]{1,0:T(8,128)}) custom-call(f32[2,256,256]{2,1,0:T(8,128)S(1)} %shard_map.130.own, bf16[2,256,256]{2,1,0:T(8,128)(2,1)S(1)} %collective-permute-done.15.other, f32[256,256]{1,0:T(8,128)S(1)} %get-tuple-element.46.weight, f32[256,256]{1,0:T(8,128)S(1)} %get-tuple-element.47.unweight, ...), custom_call_target="tpu_custom_call" | custom-call | flops 13107200 | bytes 3538944 | tf_op jit(solution)/shard_map/pallas_call | solution.py:268
  (3 shorter events, 0.0 us)
Async XLA Ops:
  0.6 17.1 %copy-start = (bf16[2,2,2,256,256]{4,3,2,1,0:T(8,128)(2,1)S(1)}, bf16[2,2,2,256,256]{4,3,2,1,0:T(8,128)(2,1)}, u32[]{:S(2)}) copy-start(bf16[2,2,2,256,256]{4,3,2,1,0:T(8,128)(2,1)} %d_ref.11) | copy-start | bytes 3145732
  1.7 10.5 %collective-permute-start = (bf16[256,256]{1,0:T(8,128)(2,1)S(1)}, bf16[256,256]{1,0:T(8,128)(2,1)S(1)}, u32[]{:S(2)}, u32[]{:S(2)}) collective-permute-start(bf16[256,256]{1,0:T(8,128)(2,1)S(1)} %shard_map.123.refs_0_), channel_id=1, source_target_pairs={{0,8},{2,10},{4,12},{6,14},{8,0},{10,2},{12,4},{14,6},{1,9},{3,11}... | collective-permute-start | bytes 393224 | tf_op jit(solution)/shard_map/ppermute | solution.py:32
  5.8 8.5 %collective-permute-start.6 = (bf16[256,256]{1,0:T(8,128)(2,1)S(1)}, bf16[256,256]{1,0:T(8,128)(2,1)S(1)}, u32[]{:S(2)}, u32[]{:S(2)}) collective-permute-start(bf16[256,256]{1,0:T(8,128)(2,1)S(1)} %shard_map.123.refs_0_), channel_id=1, source_target_pairs={{0,4},{2,6},{4,0},{6,2},{8,12},{10,14},{12,8},{14,10},{1,5},{3,7},... | collective-permute-start | bytes 393224 | tf_op jit(solution)/shard_map/ppermute | solution.py:32
  7.4 10.3 %collective-permute-start.5 = (bf16[256,256]{1,0:T(8,128)(2,1)S(1)}, bf16[256,256]{1,0:T(8,128)(2,1)S(1)}, u32[]{:S(2)}, u32[]{:S(2)}) collective-permute-start(bf16[256,256]{1,0:T(8,128)(2,1)S(1)} %shard_map.123.refs_0_), channel_id=1, source_target_pairs={{0,6},{2,4},{4,2},{6,0},{8,14},{10,12},{12,10},{14,8},{1,7},{3,5},... | collective-permute-start | bytes 393224 | tf_op jit(solution)/shard_map/ppermute | solution.py:32
  8.8 8.9 %collective-permute-start.4 = (bf16[256,256]{1,0:T(8,128)(2,1)S(1)}, bf16[256,256]{1,0:T(8,128)(2,1)S(1)}, u32[]{:S(2)}, u32[]{:S(2)}) collective-permute-start(bf16[256,256]{1,0:T(8,128)(2,1)S(1)} %shard_map.123.refs_0_), channel_id=1, source_target_pairs={{0,2},{2,0},{4,6},{6,4},{8,10},{10,8},{12,14},{14,12},{1,3},{3,1},... | collective-permute-start | bytes 393224 | tf_op jit(solution)/shard_map/ppermute | solution.py:32
  12.2 8.2 %collective-permute-start.3 = (bf16[256,256]{1,0:T(8,128)(2,1)S(1)}, bf16[256,256]{1,0:T(8,128)(2,1)S(1)}, u32[]{:S(2)}, u32[]{:S(2)}) collective-permute-start(bf16[256,256]{1,0:T(8,128)(2,1)S(1)} %collective-permute-done.refs_2_), channel_id=1, source_target_pairs={{0,6},{2,4},{4,2},{6,0},{8,14},{10,12},{12,10},{14,8},{1,7},{3,5},... | collective-permute-start | bytes 393224 | tf_op jit(solution)/shard_map/ppermute | solution.py:32
  13.8 8.0 %collective-permute-start.2 = (bf16[256,256]{1,0:T(8,128)(2,1)S(1)}, bf16[256,256]{1,0:T(8,128)(2,1)S(1)}, u32[]{:S(2)}, u32[]{:S(2)}) collective-permute-start(bf16[256,256]{1,0:T(8,128)(2,1)S(1)} %collective-permute-done.refs_2_), channel_id=1, source_target_pairs={{0,2},{2,0},{4,6},{6,4},{8,10},{10,8},{12,14},{14,12},{1,3},{3,1},... | collective-permute-start | bytes 393224 | tf_op jit(solution)/shard_map/ppermute | solution.py:32
  14.3 7.5 %collective-permute-start.1 = (bf16[256,256]{1,0:T(8,128)(2,1)S(1)}, bf16[256,256]{1,0:T(8,128)(2,1)S(1)}, u32[]{:S(2)}, u32[]{:S(2)}) collective-permute-start(bf16[256,256]{1,0:T(8,128)(2,1)S(1)} %collective-permute-done.refs_2_), channel_id=1, source_target_pairs={{0,4},{2,6},{4,0},{6,2},{8,12},{10,14},{12,8},{14,10},{1,5},{3,7},... | collective-permute-start | bytes 393224 | tf_op jit(solution)/shard_map/ppermute | solution.py:32
  17.7 0.7 %copy-start.3 = (s32[2,2]{1,0:T(2,128)S(1)}, s32[2,2]{1,0:T(2,128)}, u32[]{:S(2)}) copy-start(s32[2,2]{1,0:T(2,128)} %near_ref.11) | copy-start | bytes 52
  22.4 1.6 %copy-start.1 = (f32[256,256]{1,0:T(8,128)S(1)}, f32[256,256]{1,0:T(8,128)}, u32[]{:S(2)}) copy-start(f32[256,256]{1,0:T(8,128)} %tau.3) | copy-start | bytes 786436
  22.4 1.6 %collective-permute-start.7 = (bf16[2,256,256]{2,1,0:T(8,128)(2,1)S(1)}, bf16[2,256,256]{2,1,0:T(8,128)(2,1)S(1)}, u32[]{:S(2)}, u32[]{:S(2)}) collective-permute-start(bf16[2,256,256]{2,1,0:T(8,128)(2,1)S(1)} %shard_map.126), channel_id=1, source_target_pairs={{0,1},{1,0},{2,3},{3,2},{4,5},{5,4},{6,7},{7,6},{8,9},{9,8},{10,11... | collective-permute-start | bytes 786440 | tf_op jit(solution)/shard_map/ppermute | solution.py:368
  24.0 13.8 %copy-start.2 = (f32[256,256]{1,0:T(8,128)S(1)}, f32[256,256]{1,0:T(8,128)}, u32[]{:S(2)}) copy-start(f32[256,256]{1,0:T(8,128)} %state.1) | copy-start | bytes 786436
  24.9 9.4 %collective-permute-start.8 = (bf16[256,256]{1,0:T(8,128)(2,1)S(1)}, bf16[256,256]{1,0:T(8,128)(2,1)S(1)}, u32[]{:S(2)}, u32[]{:S(2)}) collective-permute-start(bf16[256,256]{1,0:T(8,128)(2,1)S(1)} %get-tuple-element.45.refs_0_), channel_id=1, source_target_pairs={{0,8},{2,10},{4,12},{6,14},{8,0},{10,2},{12,4},{14,6},{1,9},{3,11}... | collective-permute-start | bytes 393224 | tf_op jit(solution)/shard_map/ppermute | solution.py:32
  26.8 8.8 %collective-permute-start.14 = (bf16[256,256]{1,0:T(8,128)(2,1)S(1)}, bf16[256,256]{1,0:T(8,128)(2,1)S(1)}, u32[]{:S(2)}, u32[]{:S(2)}) collective-permute-start(bf16[256,256]{1,0:T(8,128)(2,1)S(1)} %get-tuple-element.45.refs_0_), channel_id=1, source_target_pairs={{0,4},{2,6},{4,0},{6,2},{8,12},{10,14},{12,8},{14,10},{1,5},{3,7},... | collective-permute-start | bytes 393224 | tf_op jit(solution)/shard_map/ppermute | solution.py:32
  28.6 9.4 %collective-permute-start.13 = (bf16[256,256]{1,0:T(8,128)(2,1)S(1)}, bf16[256,256]{1,0:T(8,128)(2,1)S(1)}, u32[]{:S(2)}, u32[]{:S(2)}) collective-permute-start(bf16[256,256]{1,0:T(8,128)(2,1)S(1)} %get-tuple-element.45.refs_0_), channel_id=1, source_target_pairs={{0,6},{2,4},{4,2},{6,0},{8,14},{10,12},{12,10},{14,8},{1,7},{3,5},... | collective-permute-start | bytes 393224 | tf_op jit(solution)/shard_map/ppermute | solution.py:32
  28.8 9.2 %collective-permute-start.12 = (bf16[256,256]{1,0:T(8,128)(2,1)S(1)}, bf16[256,256]{1,0:T(8,128)(2,1)S(1)}, u32[]{:S(2)}, u32[]{:S(2)}) collective-permute-start(bf16[256,256]{1,0:T(8,128)(2,1)S(1)} %get-tuple-element.45.refs_0_), channel_id=1, source_target_pairs={{0,2},{2,0},{4,6},{6,4},{8,10},{10,8},{12,14},{14,12},{1,3},{3,1},... | collective-permute-start | bytes 393224 | tf_op jit(solution)/shard_map/ppermute | solution.py:32
  34.3 7.0 %collective-permute-start.11 = (bf16[256,256]{1,0:T(8,128)(2,1)S(1)}, bf16[256,256]{1,0:T(8,128)(2,1)S(1)}, u32[]{:S(2)}, u32[]{:S(2)}) collective-permute-start(bf16[256,256]{1,0:T(8,128)(2,1)S(1)} %collective-permute-done.8.refs_2_), channel_id=1, source_target_pairs={{0,6},{2,4},{4,2},{6,0},{8,14},{10,12},{12,10},{14,8},{1,7},{3,5},... | collective-permute-start | bytes 393224 | tf_op jit(solution)/shard_map/ppermute | solution.py:32
  34.3 8.3 %collective-permute-start.10 = (bf16[256,256]{1,0:T(8,128)(2,1)S(1)}, bf16[256,256]{1,0:T(8,128)(2,1)S(1)}, u32[]{:S(2)}, u32[]{:S(2)}) collective-permute-start(bf16[256,256]{1,0:T(8,128)(2,1)S(1)} %collective-permute-done.8.refs_2_), channel_id=1, source_target_pairs={{0,2},{2,0},{4,6},{6,4},{8,10},{10,8},{12,14},{14,12},{1,3},{3,1},... | collective-permute-start | bytes 393224 | tf_op jit(solution)/shard_map/ppermute | solution.py:32
  35.6 7.0 %collective-permute-start.9 = (bf16[256,256]{1,0:T(8,128)(2,1)S(1)}, bf16[256,256]{1,0:T(8,128)(2,1)S(1)}, u32[]{:S(2)}, u32[]{:S(2)}) collective-permute-start(bf16[256,256]{1,0:T(8,128)(2,1)S(1)} %collective-permute-done.8.refs_2_), channel_id=1, source_target_pairs={{0,4},{2,6},{4,0},{6,2},{8,12},{10,14},{12,8},{14,10},{1,5},{3,7},... | collective-permute-start | bytes 393224 | tf_op jit(solution)/shard_map/ppermute | solution.py:32
  43.2 1.6 %collective-permute-start.15 = (bf16[2,256,256]{2,1,0:T(8,128)(2,1)S(1)}, bf16[2,256,256]{2,1,0:T(8,128)(2,1)S(1)}, u32[]{:S(2)}, u32[]{:S(2)}) collective-permute-start(bf16[2,256,256]{2,1,0:T(8,128)(2,1)S(1)} %shard_map.131), channel_id=1, source_target_pairs={{0,1},{1,0},{2,3},{3,2},{4,5},{5,4},{6,7},{7,6},{8,9},{9,8},{10,11... | collective-permute-start | bytes 786440 | tf_op jit(solution)/shard_map/ppermute | solution.py:368

commit v25 on v24

--- a/solution.py
+++ b/solution.py
@@ -20,7 +20,7 @@
     if not direct:
         cuts = [0, max(count - 4, 0), count]
         return [list(range(first, last)) for first, last in zip(cuts, cuts[1:]) if last > first]
-    return [[0, 1, 4, 3, 2], [6, 5, 7]] if count == 8 else [[0, 1], [2, 3]]
+    return [[0, 1, 4, 2, 3], [6, 5, 7]] if count == 8 else [[0, 1], [2, 3]]
 
 
 def row_met(spot, row, direct):

time: 46.7 us -> 46.8 us (level)
  waiting for transfers between devices: 15.4 us -> 15.9 us
  transfers between devices with their start and end apart: 16 -> 16, of which waited for: 9 -> 13; matrix products, arithmetic and copies ran while one was open for 0% -> 0% of each run, Pallas kernels for 10% -> 10%
where the time goes in v25:
time: 46.8 us; the launch traced here: 46.6 us
  starting transfers between devices  19.8 us (42%)
  waiting for transfers between devices  15.9 us (34%)
  Pallas kernels  9.49 us (20%)
  between operations  0.77 us (2%)
  local copies, waits for them, and re-layouts  0.68 us (1%)
    ppermute x14, starting transfers between devices, swapped(): lax.ppermute(data, 'row', [(row, row ^ mask) for row in range(count)])  19.6 us
    ppermute x14, waiting for transfers between devices, swapped(): lax.ppermute(data, 'row', [(row, row ^ mask) for row in range(count)])  13.9 us
    pallas_call x11, Pallas kernels, on_core(): pl.pallas_call(kernel, out_shape=outs, in_specs=[hbm] * len(far) + [vmem]...  9.49 us
    ppermute x2, waiting for transfers between devices, lattice(): other = lax.ppermute(add(found[end], end, 1, sums, narrow), 'col', swap)  1.96 us
  transfers between devices with their start and end apart: 16, of which 13 were waited for; matrix products, arithmetic and copies ran while one was open for 0% of the time, Pallas kernels for 10%

profile of v25, /device:TPU:0, one launch (start us, length us, event | category | flops | bytes accessed | tf_op | source)
XLA Modules:
  0.0 46.6 jit_solution(4772192018230765459)
XLA Ops:
  0.6 0.0 copy-start
  0.6 1.0 %shard_map.123.refs_0_ = bf16[256,256]{1,0:T(8,128)(2,1)S(1)} custom-call(f32[256,256]{1,0:T(8,128)} %wide_ref.1), custom_call_target="tpu_custom_call" | custom-call | bytes 262144 | tf_op jit(solution)/shard_map/pallas_call | solution.py:268
  1.7 4.1 %collective-permute-start = (bf16[256,256]{1,0:T(8,128)(2,1)S(1)}, bf16[256,256]{1,0:T(8,128)(2,1)S(1)}, u32[]{:S(2)}, u32[]{:S(2)}) collective-permute-start(bf16[256,256]{1,0:T(8,128)(2,1)S(1)} %shard_map.123.refs_0_), channel_id=1, source_target_pairs={{0,8},{2,10},{4,12},{6,14},{8,0},{10,2},{12,4},{14,6},{1,9},{3,11}... | collective-permute-start | bytes 393224 | tf_op jit(solution)/shard_map/ppermute | solution.py:32
  5.8 2.5 %collective-permute-start.6 = (bf16[256,256]{1,0:T(8,128)(2,1)S(1)}, bf16[256,256]{1,0:T(8,128)(2,1)S(1)}, u32[]{:S(2)}, u32[]{:S(2)}) collective-permute-start(bf16[256,256]{1,0:T(8,128)(2,1)S(1)} %shard_map.123.refs_0_), channel_id=1, source_target_pairs={{0,6},{2,4},{4,2},{6,0},{8,14},{10,12},{12,10},{14,8},{1,7},{3,5},... | collective-permute-start | bytes 393224 | tf_op jit(solution)/shard_map/ppermute | solution.py:32
  8.3 0.4 collective-permute-start.5
  8.8 0.5 %collective-permute-start.4 = (bf16[256,256]{1,0:T(8,128)(2,1)S(1)}, bf16[256,256]{1,0:T(8,128)(2,1)S(1)}, u32[]{:S(2)}, u32[]{:S(2)}) collective-permute-start(bf16[256,256]{1,0:T(8,128)(2,1)S(1)} %shard_map.123.refs_0_), channel_id=1, source_target_pairs={{0,2},{2,0},{4,6},{6,4},{8,10},{10,8},{12,14},{14,12},{1,3},{3,1},... | collective-permute-start | bytes 393224 | tf_op jit(solution)/shard_map/ppermute | solution.py:32
  9.3 2.9 %collective-permute-done.refs_2_ = bf16[256,256]{1,0:T(8,128)(2,1)S(1)} collective-permute-done((bf16[256,256]{1,0:T(8,128)(2,1)S(1)}, bf16[256,256]{1,0:T(8,128)(2,1)S(1)}, u32[]{:S(2)}, u32[]{:S(2)}) %collective-permute-start) | collective-permute-done | bytes 131104 | tf_op jit(solution)/shard_map/ppermute | solution.py:32
  12.2 1.6 %collective-permute-start.3 = (bf16[256,256]{1,0:T(8,128)(2,1)S(1)}, bf16[256,256]{1,0:T(8,128)(2,1)S(1)}, u32[]{:S(2)}, u32[]{:S(2)}) collective-permute-start(bf16[256,256]{1,0:T(8,128)(2,1)S(1)} %collective-permute-done.refs_2_), channel_id=1, source_target_pairs={{0,6},{2,4},{4,2},{6,0},{8,14},{10,12},{12,10},{14,8},{1,7},{3,5},... | collective-permute-start | bytes 393224 | tf_op jit(solution)/shard_map/ppermute | solution.py:32
  13.8 0.5 %collective-permute-start.2 = (bf16[256,256]{1,0:T(8,128)(2,1)S(1)}, bf16[256,256]{1,0:T(8,128)(2,1)S(1)}, u32[]{:S(2)}, u32[]{:S(2)}) collective-permute-start(bf16[256,256]{1,0:T(8,128)(2,1)S(1)} %collective-permute-done.refs_2_), channel_id=1, source_target_pairs={{0,2},{2,0},{4,6},{6,4},{8,10},{10,8},{12,14},{14,12},{1,3},{3,1},... | collective-permute-start | bytes 393224 | tf_op jit(solution)/shard_map/ppermute | solution.py:32
  14.3 0.4 collective-permute-done.6.refs_4_
  14.7 1.2 %collective-permute-start.1 = (bf16[256,256]{1,0:T(8,128)(2,1)S(1)}, bf16[256,256]{1,0:T(8,128)(2,1)S(1)}, u32[]{:S(2)}, u32[]{:S(2)}) collective-permute-start(bf16[256,256]{1,0:T(8,128)(2,1)S(1)} %collective-permute-done.refs_2_), channel_id=1, source_target_pairs={{0,4},{2,6},{4,0},{6,2},{8,12},{10,14},{12,8},{14,10},{1,5},{3,7},... | collective-permute-start | bytes 393224 | tf_op jit(solution)/shard_map/ppermute | solution.py:32
  15.9 1.8 %shard_map.122 = (bf16[8,2,32,256]{3,2,1,0:T(8,128)(2,1)S(1)}, bf16[2,512,384]{2,1,0:T(8,128)(2,1)S(1)}, f32[5,256,128]{2,1,0:T(8,128)S(1)}, f32[256,256]{1,0:T(...) custom-call(s32[2,8]{1,0:T(2,128)} %refs_0_.1, bf16[2,8,32,256]{3,2,1,0:T(8,128)(2,1)} %refs_1_.1, ...), custom_call_target="tpu_custom_call" | custom-call | bytes 1051712 | tf_op jit(solution)/shard_map/pallas_call | solution.py:268
  17.7 0.0 collective-permute-done.5.refs_3_
  17.8 0.0 collective-permute-done.4.refs_1_
  17.8 0.0 copy-start.3
  17.8 0.0 copy-done
  17.8 0.7 %copy-done.3 = s32[2,2]{1,0:T(2,128)S(1)} copy-done((s32[2,2]{1,0:T(2,128)S(1)}, s32[2,2]{1,0:T(2,128)}, u32[]{:S(2)}) %copy-start.3) | copy-done | bytes 40
  18.4 0.9 %shard_map.124.refs_3_ = f32[2,2,256,256]{3,2,1,0:T(8,128)S(1)} custom-call(s32[2,2]{1,0:T(2,128)S(1)} %copy-done.3, bf16[8,2,32,256]{3,2,1,0:T(8,128)(2,1)S(1)} %get-tuple-element.27.v_ref, bf16[2,512,384]{2,1,0:T(8,128)(2,1)S(1)} %get-tuple-element.28.u_ref, bf16[2,2,2,256,256]{4,3,2,1,0:T(8,128)(2,1)S(1)} %copy-done, ...), custom_call_target="tpu_custom_call" | custom-call | flops 125829120 | bytes 2752528 | tf_op jit(solution)/shard_map/pallas_call | solution.py:268
  19.3 1.0 %collective-permute-done.3.refs_2_ = bf16[256,256]{1,0:T(8,128)(2,1)S(1)} collective-permute-done((bf16[256,256]{1,0:T(8,128)(2,1)S(1)}, bf16[256,256]{1,0:T(8,128)(2,1)S(1)}, u32[]{:S(2)}, u32[]{:S(2)}) %collective-permute-start.3) | collective-permute-done | bytes 131104 | tf_op jit(solution)/shard_map/ppermute | solution.py:32
  20.3 0.7 %collective-permute-done.2.refs_1_ = bf16[256,256]{1,0:T(8,128)(2,1)S(1)} collective-permute-done((bf16[256,256]{1,0:T(8,128)(2,1)S(1)}, bf16[256,256]{1,0:T(8,128)(2,1)S(1)}, u32[]{:S(2)}, u32[]{:S(2)}) %collective-permute-start.2) | collective-permute-done | bytes 131104 | tf_op jit(solution)/shard_map/ppermute | solution.py:32
  21.1 0.7 %collective-permute-done.1.refs_0_ = bf16[256,256]{1,0:T(8,128)(2,1)S(1)} collective-permute-done((bf16[256,256]{1,0:T(8,128)(2,1)S(1)}, bf16[256,256]{1,0:T(8,128)(2,1)S(1)}, u32[]{:S(2)}, u32[]{:S(2)}) %collective-permute-start.1) | collective-permute-done | bytes 131104 | tf_op jit(solution)/shard_map/ppermute | solution.py:32
  21.8 0.5 %shard_map.126 = bf16[2,256,256]{2,1,0:T(8,128)(2,1)S(1)} custom-call(s32[2,2]{1,0:T(2,128)S(1)} %copy-done.3, bf16[8,2,32,256]{3,2,1,0:T(8,128)(2,1)S(1)} %get-tuple-element.27.v_ref, bf16[2,512,384]{2,1,0:T(8,128)(2,1)S(1)} %get-tuple-element.28.u_ref, bf16[2,2,2,256,256]{4,3,2,1,0:T(8,128)(2,1)S(1)} %copy-done, ...), custom_call_target="tpu_custom_call" | custom-call | flops 37748736 | bytes 3538960 | tf_op jit(solution)/shard_map/pallas_call | solution.py:268
  22.3 0.0 copy-start.1
  22.3 0.1 collective-permute-start.7
  22.4 0.5 %shard_map.125.own = f32[2,256,256]{2,1,0:T(8,128)S(1)} custom-call(s32[2,2]{1,0:T(2,128)S(1)} %copy-done.3, bf16[8,2,32,256]{3,2,1,0:T(8,128)(2,1)S(1)} %get-tuple-element.27.v_ref, bf16[2,512,384]{2,1,0:T(8,128)(2,1)S(1)} %get-tuple-element.28.u_ref, bf16[2,2,2,256,256]{4,3,2,1,0:T(8,128)(2,1)S(1)} %copy-done, ...), custom_call_target="tpu_custom_call" | custom-call | flops 37748736 | bytes 3538960 | tf_op jit(solution)/shard_map/pallas_call | solution.py:268
  22.9 1.0 %collective-permute-done.7.other = bf16[2,256,256]{2,1,0:T(8,128)(2,1)S(1)} collective-permute-done((bf16[2,256,256]{2,1,0:T(8,128)(2,1)S(1)}, bf16[2,256,256]{2,1,0:T(8,128)(2,1)S(1)}, u32[]{:S(2)}, u32[]{:S(2)}) %collective-permute-start.7) | collective-permute-done | bytes 262176 | tf_op jit(solution)/shard_map/ppermute | solution.py:368
  23.9 0.9 %shard_map.127 = (f32[256,256]{1,0:T(8,128)S(1)}, bf16[256,256]{1,0:T(8,128)(2,1)S(1)}) custom-call(f32[2,256,256]{2,1,0:T(8,128)S(1)} %shard_map.125.own, bf16[2,256,256]{2,1,0:T(8,128)(2,1)S(1)} %collective-permute-done.7.other, f32[256,256]{1,0:T(8,128)S(1)} %get-tuple-element.33.weight, f32[256,256]{1,0:T(8,128)S(1)} %get-tuple-element.34.unweight, ...), custom_call_target="tpu_custom_call" | custom-call | flops 13107200 | bytes 2228224 | tf_op jit(solution)/shard_map/pallas_call | solution.py:268
  24.8 2.0 %collective-permute-start.8 = (bf16[256,256]{1,0:T(8,128)(2,1)S(1)}, bf16[256,256]{1,0:T(8,128)(2,1)S(1)}, u32[]{:S(2)}, u32[]{:S(2)}) collective-permute-start(bf16[256,256]{1,0:T(8,128)(2,1)S(1)} %get-tuple-element.45.refs_0_), channel_id=1, source_target_pairs={{0,8},{2,10},{4,12},{6,14},{8,0},{10,2},{12,4},{14,6},{1,9},{3,11}... | collective-permute-start | bytes 393224 | tf_op jit(solution)/shard_map/ppermute | solution.py:32
  26.8 1.7 %collective-permute-start.14 = (bf16[256,256]{1,0:T(8,128)(2,1)S(1)}, bf16[256,256]{1,0:T(8,128)(2,1)S(1)}, u32[]{:S(2)}, u32[]{:S(2)}) collective-permute-start(bf16[256,256]{1,0:T(8,128)(2,1)S(1)} %get-tuple-element.45.refs_0_), channel_id=1, source_target_pairs={{0,6},{2,4},{4,2},{6,0},{8,14},{10,12},{12,10},{14,8},{1,7},{3,5},... | collective-permute-start | bytes 393224 | tf_op jit(solution)/shard_map/ppermute | solution.py:32
  28.5 0.3 collective-permute-start.13
  28.8 1.5 %collective-permute-start.12 = (bf16[256,256]{1,0:T(8,128)(2,1)S(1)}, bf16[256,256]{1,0:T(8,128)(2,1)S(1)}, u32[]{:S(2)}, u32[]{:S(2)}) collective-permute-start(bf16[256,256]{1,0:T(8,128)(2,1)S(1)} %get-tuple-element.45.refs_0_), channel_id=1, source_target_pairs={{0,2},{2,0},{4,6},{6,4},{8,10},{10,8},{12,14},{14,12},{1,3},{3,1},... | collective-permute-start | bytes 393224 | tf_op jit(solution)/shard_map/ppermute | solution.py:32
  30.3 3.9 %collective-permute-done.8.refs_2_ = bf16[256,256]{1,0:T(8,128)(2,1)S(1)} collective-permute-done((bf16[256,256]{1,0:T(8,128)(2,1)S(1)}, bf16[256,256]{1,0:T(8,128)(2,1)S(1)}, u32[]{:S(2)}, u32[]{:S(2)}) %collective-permute-start.8) | collective-permute-done | bytes 131104 | tf_op jit(solution)/shard_map/ppermute | solution.py:32
  34.2 0.0 collective-permute-start.11
  34.2 1.4 %collective-permute-start.10 = (bf16[256,256]{1,0:T(8,128)(2,1)S(1)}, bf16[256,256]{1,0:T(8,128)(2,1)S(1)}, u32[]{:S(2)}, u32[]{:S(2)}) collective-permute-start(bf16[256,256]{1,0:T(8,128)(2,1)S(1)} %collective-permute-done.8.refs_2_), channel_id=1, source_target_pairs={{0,2},{2,0},{4,6},{6,4},{8,10},{10,8},{12,14},{14,12},{1,3},{3,1},... | collective-permute-start | bytes 393224 | tf_op jit(solution)/shard_map/ppermute | solution.py:32
  35.6 0.3 collective-permute-done.14.refs_4_
  35.9 1.8 %collective-permute-start.9 = (bf16[256,256]{1,0:T(8,128)(2,1)S(1)}, bf16[256,256]{1,0:T(8,128)(2,1)S(1)}, u32[]{:S(2)}, u32[]{:S(2)}) collective-permute-start(bf16[256,256]{1,0:T(8,128)(2,1)S(1)} %collective-permute-done.8.refs_2_), channel_id=1, source_target_pairs={{0,4},{2,6},{4,0},{6,2},{8,12},{10,14},{12,8},{14,10},{1,5},{3,7},... | collective-permute-start | bytes 393224 | tf_op jit(solution)/shard_map/ppermute | solution.py:32
  37.7 0.2 shard_map.128
  38.0 0.2 collective-permute-done.13.refs_3_
  38.2 0.0 collective-permute-done.12.refs_1_
  38.2 0.8 %shard_map.129.refs_3_ = f32[2,2,256,256]{3,2,1,0:T(8,128)S(1)} custom-call(s32[2,2]{1,0:T(2,128)S(1)} %copy-done.3, bf16[8,2,32,256]{3,2,1,0:T(8,128)(2,1)S(1)} %get-tuple-element.27.v_ref, bf16[2,512,384]{2,1,0:T(8,128)(2,1)S(1)} %get-tuple-element.28.u_ref, bf16[2,2,2,256,256]{4,3,2,1,0:T(8,128)(2,1)S(1)} %copy-done, ...), custom_call_target="tpu_custom_call" | custom-call | flops 125829120 | bytes 2752528 | tf_op jit(solution)/shard_map/pallas_call | solution.py:268
  39.0 2.6 %collective-permute-done.11.refs_2_ = bf16[256,256]{1,0:T(8,128)(2,1)S(1)} collective-permute-done((bf16[256,256]{1,0:T(8,128)(2,1)S(1)}, bf16[256,256]{1,0:T(8,128)(2,1)S(1)}, u32[]{:S(2)}, u32[]{:S(2)}) %collective-permute-start.11) | collective-permute-done | bytes 131104 | tf_op jit(solution)/shard_map/ppermute | solution.py:32
  41.6 0.5 %collective-permute-done.10.refs_1_ = bf16[256,256]{1,0:T(8,128)(2,1)S(1)} collective-permute-done((bf16[256,256]{1,0:T(8,128)(2,1)S(1)}, bf16[256,256]{1,0:T(8,128)(2,1)S(1)}, u32[]{:S(2)}, u32[]{:S(2)}) %collective-permute-start.10) | collective-permute-done | bytes 131104 | tf_op jit(solution)/shard_map/ppermute | solution.py:32
  42.1 0.6 %collective-permute-done.9.refs_0_ = bf16[256,256]{1,0:T(8,128)(2,1)S(1)} collective-permute-done((bf16[256,256]{1,0:T(8,128)(2,1)S(1)}, bf16[256,256]{1,0:T(8,128)(2,1)S(1)}, u32[]{:S(2)}, u32[]{:S(2)}) %collective-permute-start.9) | collective-permute-done | bytes 131104 | tf_op jit(solution)/shard_map/ppermute | solution.py:32
  42.7 0.5 %shard_map.131 = bf16[2,256,256]{2,1,0:T(8,128)(2,1)S(1)} custom-call(s32[2,2]{1,0:T(2,128)S(1)} %copy-done.3, bf16[8,2,32,256]{3,2,1,0:T(8,128)(2,1)S(1)} %get-tuple-element.27.v_ref, bf16[2,512,384]{2,1,0:T(8,128)(2,1)S(1)} %get-tuple-element.28.u_ref, bf16[2,2,2,256,256]{4,3,2,1,0:T(8,128)(2,1)S(1)} %copy-done, ...), custom_call_target="tpu_custom_call" | custom-call | flops 37748736 | bytes 3538960 | tf_op jit(solution)/shard_map/pallas_call | solution.py:268
  43.3 0.1 collective-permute-start.15
  43.4 0.5 %shard_map.130.own = f32[2,256,256]{2,1,0:T(8,128)S(1)} custom-call(s32[2,2]{1,0:T(2,128)S(1)} %copy-done.3, bf16[8,2,32,256]{3,2,1,0:T(8,128)(2,1)S(1)} %get-tuple-element.27.v_ref, bf16[2,512,384]{2,1,0:T(8,128)(2,1)S(1)} %get-tuple-element.28.u_ref, bf16[2,2,2,256,256]{4,3,2,1,0:T(8,128)(2,1)S(1)} %copy-done, ...), custom_call_target="tpu_custom_call" | custom-call | flops 37748736 | bytes 3538960 | tf_op jit(solution)/shard_map/pallas_call | solution.py:268
  43.9 1.0 %collective-permute-done.15.other = bf16[2,256,256]{2,1,0:T(8,128)(2,1)S(1)} collective-permute-done((bf16[2,256,256]{2,1,0:T(8,128)(2,1)S(1)}, bf16[2,256,256]{2,1,0:T(8,128)(2,1)S(1)}, u32[]{:S(2)}, u32[]{:S(2)}) %collective-permute-start.15) | collective-permute-done | bytes 262176 | tf_op jit(solution)/shard_map/ppermute | solution.py:368
  44.9 1.7 %shard_map.132 = (f32[256,256]{1,0:T(8,128)}, f32[256,256]{1,0:T(8,128)}) custom-call(f32[2,256,256]{2,1,0:T(8,128)S(1)} %shard_map.130.own, bf16[2,256,256]{2,1,0:T(8,128)(2,1)S(1)} %collective-permute-done.15.other, f32[256,256]{1,0:T(8,128)S(1)} %get-tuple-element.46.weight, f32[256,256]{1,0:T(8,128)S(1)} %get-tuple-element.47.unweight, ...), custom_call_target="tpu_custom_call" | custom-call | flops 13107200 | bytes 3538944 | tf_op jit(solution)/shard_map/pallas_call | solution.py:268
  (3 shorter events, 0.0 us)
Async XLA Ops:
  0.6 17.2 %copy-start = (bf16[2,2,2,256,256]{4,3,2,1,0:T(8,128)(2,1)S(1)}, bf16[2,2,2,256,256]{4,3,2,1,0:T(8,128)(2,1)}, u32[]{:S(2)}) copy-start(bf16[2,2,2,256,256]{4,3,2,1,0:T(8,128)(2,1)} %d_ref.11) | copy-start | bytes 3145732
  1.7 10.5 %collective-permute-start = (bf16[256,256]{1,0:T(8,128)(2,1)S(1)}, bf16[256,256]{1,0:T(8,128)(2,1)S(1)}, u32[]{:S(2)}, u32[]{:S(2)}) collective-permute-start(bf16[256,256]{1,0:T(8,128)(2,1)S(1)} %shard_map.123.refs_0_), channel_id=1, source_target_pairs={{0,8},{2,10},{4,12},{6,14},{8,0},{10,2},{12,4},{14,6},{1,9},{3,11}... | collective-permute-start | bytes 393224 | tf_op jit(solution)/shard_map/ppermute | solution.py:32
  5.8 9.0 %collective-permute-start.6 = (bf16[256,256]{1,0:T(8,128)(2,1)S(1)}, bf16[256,256]{1,0:T(8,128)(2,1)S(1)}, u32[]{:S(2)}, u32[]{:S(2)}) collective-permute-start(bf16[256,256]{1,0:T(8,128)(2,1)S(1)} %shard_map.123.refs_0_), channel_id=1, source_target_pairs={{0,6},{2,4},{4,2},{6,0},{8,14},{10,12},{12,10},{14,8},{1,7},{3,5},... | collective-permute-start | bytes 393224 | tf_op jit(solution)/shard_map/ppermute | solution.py:32
  8.3 9.4 %collective-permute-start.5 = (bf16[256,256]{1,0:T(8,128)(2,1)S(1)}, bf16[256,256]{1,0:T(8,128)(2,1)S(1)}, u32[]{:S(2)}, u32[]{:S(2)}) collective-permute-start(bf16[256,256]{1,0:T(8,128)(2,1)S(1)} %shard_map.123.refs_0_), channel_id=1, source_target_pairs={{0,4},{2,6},{4,0},{6,2},{8,12},{10,14},{12,8},{14,10},{1,5},{3,7},... | collective-permute-start | bytes 393224 | tf_op jit(solution)/shard_map/ppermute | solution.py:32
  8.8 9.0 %collective-permute-start.4 = (bf16[256,256]{1,0:T(8,128)(2,1)S(1)}, bf16[256,256]{1,0:T(8,128)(2,1)S(1)}, u32[]{:S(2)}, u32[]{:S(2)}) collective-permute-start(bf16[256,256]{1,0:T(8,128)(2,1)S(1)} %shard_map.123.refs_0_), channel_id=1, source_target_pairs={{0,2},{2,0},{4,6},{6,4},{8,10},{10,8},{12,14},{14,12},{1,3},{3,1},... | collective-permute-start | bytes 393224 | tf_op jit(solution)/shard_map/ppermute | solution.py:32
  12.2 8.2 %collective-permute-start.3 = (bf16[256,256]{1,0:T(8,128)(2,1)S(1)}, bf16[256,256]{1,0:T(8,128)(2,1)S(1)}, u32[]{:S(2)}, u32[]{:S(2)}) collective-permute-start(bf16[256,256]{1,0:T(8,128)(2,1)S(1)} %collective-permute-done.refs_2_), channel_id=1, source_target_pairs={{0,6},{2,4},{4,2},{6,0},{8,14},{10,12},{12,10},{14,8},{1,7},{3,5},... | collective-permute-start | bytes 393224 | tf_op jit(solution)/shard_map/ppermute | solution.py:32
  13.8 7.2 %collective-permute-start.2 = (bf16[256,256]{1,0:T(8,128)(2,1)S(1)}, bf16[256,256]{1,0:T(8,128)(2,1)S(1)}, u32[]{:S(2)}, u32[]{:S(2)}) collective-permute-start(bf16[256,256]{1,0:T(8,128)(2,1)S(1)} %collective-permute-done.refs_2_), channel_id=1, source_target_pairs={{0,2},{2,0},{4,6},{6,4},{8,10},{10,8},{12,14},{14,12},{1,3},{3,1},... | collective-permute-start | bytes 393224 | tf_op jit(solution)/shard_map/ppermute | solution.py:32
  14.7 7.0 %collective-permute-start.1 = (bf16[256,256]{1,0:T(8,128)(2,1)S(1)}, bf16[256,256]{1,0:T(8,128)(2,1)S(1)}, u32[]{:S(2)}, u32[]{:S(2)}) collective-permute-start(bf16[256,256]{1,0:T(8,128)(2,1)S(1)} %collective-permute-done.refs_2_), channel_id=1, source_target_pairs={{0,4},{2,6},{4,0},{6,2},{8,12},{10,14},{12,8},{14,10},{1,5},{3,7},... | collective-permute-start | bytes 393224 | tf_op jit(solution)/shard_map/ppermute | solution.py:32
  17.8 0.7 %copy-start.3 = (s32[2,2]{1,0:T(2,128)S(1)}, s32[2,2]{1,0:T(2,128)}, u32[]{:S(2)}) copy-start(s32[2,2]{1,0:T(2,128)} %near_ref.11) | copy-start | bytes 52
  22.3 1.6 %copy-start.1 = (f32[256,256]{1,0:T(8,128)S(1)}, f32[256,256]{1,0:T(8,128)}, u32[]{:S(2)}) copy-start(f32[256,256]{1,0:T(8,128)} %tau.3) | copy-start | bytes 786436
  22.3 1.6 %collective-permute-start.7 = (bf16[2,256,256]{2,1,0:T(8,128)(2,1)S(1)}, bf16[2,256,256]{2,1,0:T(8,128)(2,1)S(1)}, u32[]{:S(2)}, u32[]{:S(2)}) collective-permute-start(bf16[2,256,256]{2,1,0:T(8,128)(2,1)S(1)} %shard_map.126), channel_id=1, source_target_pairs={{0,1},{1,0},{2,3},{3,2},{4,5},{5,4},{6,7},{7,6},{8,9},{9,8},{10,11... | collective-permute-start | bytes 786440 | tf_op jit(solution)/shard_map/ppermute | solution.py:368
  23.9 13.8 %copy-start.2 = (f32[256,256]{1,0:T(8,128)S(1)}, f32[256,256]{1,0:T(8,128)}, u32[]{:S(2)}) copy-start(f32[256,256]{1,0:T(8,128)} %state.1) | copy-start | bytes 786436
  24.8 9.4 %collective-permute-start.8 = (bf16[256,256]{1,0:T(8,128)(2,1)S(1)}, bf16[256,256]{1,0:T(8,128)(2,1)S(1)}, u32[]{:S(2)}, u32[]{:S(2)}) collective-permute-start(bf16[256,256]{1,0:T(8,128)(2,1)S(1)} %get-tuple-element.45.refs_0_), channel_id=1, source_target_pairs={{0,8},{2,10},{4,12},{6,14},{8,0},{10,2},{12,4},{14,6},{1,9},{3,11}... | collective-permute-start | bytes 393224 | tf_op jit(solution)/shard_map/ppermute | solution.py:32
  26.8 9.1 %collective-permute-start.14 = (bf16[256,256]{1,0:T(8,128)(2,1)S(1)}, bf16[256,256]{1,0:T(8,128)(2,1)S(1)}, u32[]{:S(2)}, u32[]{:S(2)}) collective-permute-start(bf16[256,256]{1,0:T(8,128)(2,1)S(1)} %get-tuple-element.45.refs_0_), channel_id=1, source_target_pairs={{0,6},{2,4},{4,2},{6,0},{8,14},{10,12},{12,10},{14,8},{1,7},{3,5},... | collective-permute-start | bytes 393224 | tf_op jit(solution)/shard_map/ppermute | solution.py:32
  28.5 9.7 %collective-permute-start.13 = (bf16[256,256]{1,0:T(8,128)(2,1)S(1)}, bf16[256,256]{1,0:T(8,128)(2,1)S(1)}, u32[]{:S(2)}, u32[]{:S(2)}) collective-permute-start(bf16[256,256]{1,0:T(8,128)(2,1)S(1)} %get-tuple-element.45.refs_0_), channel_id=1, source_target_pairs={{0,4},{2,6},{4,0},{6,2},{8,12},{10,14},{12,8},{14,10},{1,5},{3,7},... | collective-permute-start | bytes 393224 | tf_op jit(solution)/shard_map/ppermute | solution.py:32
  28.8 9.4 %collective-permute-start.12 = (bf16[256,256]{1,0:T(8,128)(2,1)S(1)}, bf16[256,256]{1,0:T(8,128)(2,1)S(1)}, u32[]{:S(2)}, u32[]{:S(2)}) collective-permute-start(bf16[256,256]{1,0:T(8,128)(2,1)S(1)} %get-tuple-element.45.refs_0_), channel_id=1, source_target_pairs={{0,2},{2,0},{4,6},{6,4},{8,10},{10,8},{12,14},{14,12},{1,3},{3,1},... | collective-permute-start | bytes 393224 | tf_op jit(solution)/shard_map/ppermute | solution.py:32
  34.2 7.4 %collective-permute-start.11 = (bf16[256,256]{1,0:T(8,128)(2,1)S(1)}, bf16[256,256]{1,0:T(8,128)(2,1)S(1)}, u32[]{:S(2)}, u32[]{:S(2)}) collective-permute-start(bf16[256,256]{1,0:T(8,128)(2,1)S(1)} %collective-permute-done.8.refs_2_), channel_id=1, source_target_pairs={{0,6},{2,4},{4,2},{6,0},{8,14},{10,12},{12,10},{14,8},{1,7},{3,5},... | collective-permute-start | bytes 393224 | tf_op jit(solution)/shard_map/ppermute | solution.py:32
  34.2 7.9 %collective-permute-start.10 = (bf16[256,256]{1,0:T(8,128)(2,1)S(1)}, bf16[256,256]{1,0:T(8,128)(2,1)S(1)}, u32[]{:S(2)}, u32[]{:S(2)}) collective-permute-start(bf16[256,256]{1,0:T(8,128)(2,1)S(1)} %collective-permute-done.8.refs_2_), channel_id=1, source_target_pairs={{0,2},{2,0},{4,6},{6,4},{8,10},{10,8},{12,14},{14,12},{1,3},{3,1},... | collective-permute-start | bytes 393224 | tf_op jit(solution)/shard_map/ppermute | solution.py:32
  35.9 6.8 %collective-permute-start.9 = (bf16[256,256]{1,0:T(8,128)(2,1)S(1)}, bf16[256,256]{1,0:T(8,128)(2,1)S(1)}, u32[]{:S(2)}, u32[]{:S(2)}) collective-permute-start(bf16[256,256]{1,0:T(8,128)(2,1)S(1)} %collective-permute-done.8.refs_2_), channel_id=1, source_target_pairs={{0,4},{2,6},{4,0},{6,2},{8,12},{10,14},{12,8},{14,10},{1,5},{3,7},... | collective-permute-start | bytes 393224 | tf_op jit(solution)/shard_map/ppermute | solution.py:32
  43.3 1.6 %collective-permute-start.15 = (bf16[2,256,256]{2,1,0:T(8,128)(2,1)S(1)}, bf16[2,256,256]{2,1,0:T(8,128)(2,1)S(1)}, u32[]{:S(2)}, u32[]{:S(2)}) collective-permute-start(bf16[2,256,256]{2,1,0:T(8,128)(2,1)S(1)} %shard_map.131), channel_id=1, source_target_pairs={{0,1},{1,0},{2,3},{3,2},{4,5},{5,4},{6,7},{7,6},{8,9},{9,8},{10,11... | collective-permute-start | bytes 786440 | tf_op jit(solution)/shard_map/ppermute | solution.py:368

commit v26 on v25

--- a/solution.py
+++ b/solution.py
@@ -20,7 +20,7 @@
     if not direct:
         cuts = [0, max(count - 4, 0), count]
         return [list(range(first, last)) for first, last in zip(cuts, cuts[1:]) if last > first]
-    return [[0, 1, 4, 2, 3], [6, 5, 7]] if count == 8 else [[0, 1], [2, 3]]
+    return [[0, 1, 4, 2, 3], [5, 6, 7]] if count == 8 else [[0, 1], [2, 3]]
 
 
 def row_met(spot, row, direct):

time: 46.8 us -> 46.9 us (level)
  starting transfers between devices: 19.8 us -> 20.3 us
    ppermute x14, starting transfers between devices: 19.6 us -> 20.2 us  [swapped(): lax.ppermute(data, 'row', [(row, row ^ mask) for row in range(count)])]
  transfers between devices with their start and end apart: 16 -> 16, of which waited for: 13 -> 9; matrix products, arithmetic and copies ran while one was open for 0% -> 0% of each run, Pallas kernels for 10% -> 10%
where the time goes in v26:
time: 46.9 us; the launch traced here: 46.7 us
  starting transfers between devices  20.3 us (43%)
  waiting for transfers between devices  15.5 us (33%)
  Pallas kernels  9.5 us (20%)
  between operations  0.78 us (2%)
  local copies, waits for them, and re-layouts  0.68 us (1%)
    ppermute x14, starting transfers between devices, swapped(): lax.ppermute(data, 'row', [(row, row ^ mask) for row in range(count)])  20.2 us
    ppermute x14, waiting for transfers between devices, swapped(): lax.ppermute(data, 'row', [(row, row ^ mask) for row in range(count)])  13.5 us
    pallas_call x11, Pallas kernels, on_core(): pl.pallas_call(kernel, out_shape=outs, in_specs=[hbm] * len(far) + [vmem]...  9.5 us
    ppermute x2, waiting for transfers between devices, lattice(): other = lax.ppermute(add(found[end], end, 1, sums, narrow), 'col', swap)  1.97 us
  transfers between devices with their start and end apart: 16, of which 9 were waited for; matrix products, arithmetic and copies ran while one was open for 0% of the time, Pallas kernels for 10%

profile of v26, /device:TPU:0, one launch (start us, length us, event | category | flops | bytes accessed | tf_op | source)
XLA Modules:
  0.0 46.7 jit_solution(15333282879460356218)
XLA Ops:
  0.6 0.0 copy-start
  0.6 1.0 %shard_map.123.refs_0_ = bf16[256,256]{1,0:T(8,128)(2,1)S(1)} custom-call(f32[256,256]{1,0:T(8,128)} %wide_ref.1), custom_call_target="tpu_custom_call" | custom-call | bytes 262144 | tf_op jit(solution)/shard_map/pallas_call | solution.py:268
  1.7 4.1 %collective-permute-start = (bf16[256,256]{1,0:T(8,128)(2,1)S(1)}, bf16[256,256]{1,0:T(8,128)(2,1)S(1)}, u32[]{:S(2)}, u32[]{:S(2)}) collective-permute-start(bf16[256,256]{1,0:T(8,128)(2,1)S(1)} %shard_map.123.refs_0_), channel_id=1, source_target_pairs={{0,8},{2,10},{4,12},{6,14},{8,0},{10,2},{12,4},{14,6},{1,9},{3,11}... | collective-permute-start | bytes 393224 | tf_op jit(solution)/shard_map/ppermute | solution.py:32
  5.8 2.5 %collective-permute-start.6 = (bf16[256,256]{1,0:T(8,128)(2,1)S(1)}, bf16[256,256]{1,0:T(8,128)(2,1)S(1)}, u32[]{:S(2)}, u32[]{:S(2)}) collective-permute-start(bf16[256,256]{1,0:T(8,128)(2,1)S(1)} %shard_map.123.refs_0_), channel_id=1, source_target_pairs={{0,6},{2,4},{4,2},{6,0},{8,14},{10,12},{12,10},{14,8},{1,7},{3,5},... | collective-permute-start | bytes 393224 | tf_op jit(solution)/shard_map/ppermute | solution.py:32
  8.3 0.4 collective-permute-start.5
  8.8 0.5 %collective-permute-start.4 = (bf16[256,256]{1,0:T(8,128)(2,1)S(1)}, bf16[256,256]{1,0:T(8,128)(2,1)S(1)}, u32[]{:S(2)}, u32[]{:S(2)}) collective-permute-start(bf16[256,256]{1,0:T(8,128)(2,1)S(1)} %shard_map.123.refs_0_), channel_id=1, source_target_pairs={{0,2},{2,0},{4,6},{6,4},{8,10},{10,8},{12,14},{14,12},{1,3},{3,1},... | collective-permute-start | bytes 393224 | tf_op jit(solution)/shard_map/ppermute | solution.py:32
  9.3 2.9 %collective-permute-done.refs_2_ = bf16[256,256]{1,0:T(8,128)(2,1)S(1)} collective-permute-done((bf16[256,256]{1,0:T(8,128)(2,1)S(1)}, bf16[256,256]{1,0:T(8,128)(2,1)S(1)}, u32[]{:S(2)}, u32[]{:S(2)}) %collective-permute-start) | collective-permute-done | bytes 131104 | tf_op jit(solution)/shard_map/ppermute | solution.py:32
  12.2 1.6 %collective-permute-start.3 = (bf16[256,256]{1,0:T(8,128)(2,1)S(1)}, bf16[256,256]{1,0:T(8,128)(2,1)S(1)}, u32[]{:S(2)}, u32[]{:S(2)}) collective-permute-start(bf16[256,256]{1,0:T(8,128)(2,1)S(1)} %collective-permute-done.refs_2_), channel_id=1, source_target_pairs={{0,6},{2,4},{4,2},{6,0},{8,14},{10,12},{12,10},{14,8},{1,7},{3,5},... | collective-permute-start | bytes 393224 | tf_op jit(solution)/shard_map/ppermute | solution.py:32
  13.8 1.4 %collective-permute-start.2 = (bf16[256,256]{1,0:T(8,128)(2,1)S(1)}, bf16[256,256]{1,0:T(8,128)(2,1)S(1)}, u32[]{:S(2)}, u32[]{:S(2)}) collective-permute-start(bf16[256,256]{1,0:T(8,128)(2,1)S(1)} %collective-permute-done.refs_2_), channel_id=1, source_target_pairs={{0,4},{2,6},{4,0},{6,2},{8,12},{10,14},{12,8},{14,10},{1,5},{3,7},... | collective-permute-start | bytes 393224 | tf_op jit(solution)/shard_map/ppermute | solution.py:32
  15.2 0.0 collective-permute-done.6.refs_4_
  15.2 0.6 %collective-permute-start.1 = (bf16[256,256]{1,0:T(8,128)(2,1)S(1)}, bf16[256,256]{1,0:T(8,128)(2,1)S(1)}, u32[]{:S(2)}, u32[]{:S(2)}) collective-permute-start(bf16[256,256]{1,0:T(8,128)(2,1)S(1)} %collective-permute-done.refs_2_), channel_id=1, source_target_pairs={{0,2},{2,0},{4,6},{6,4},{8,10},{10,8},{12,14},{14,12},{1,3},{3,1},... | collective-permute-start | bytes 393224 | tf_op jit(solution)/shard_map/ppermute | solution.py:32
  15.8 1.8 %shard_map.122 = (bf16[8,2,32,256]{3,2,1,0:T(8,128)(2,1)S(1)}, bf16[2,512,384]{2,1,0:T(8,128)(2,1)S(1)}, f32[5,256,128]{2,1,0:T(8,128)S(1)}, f32[256,256]{1,0:T(...) custom-call(s32[2,8]{1,0:T(2,128)} %refs_0_.1, bf16[2,8,32,256]{3,2,1,0:T(8,128)(2,1)} %refs_1_.1, ...), custom_call_target="tpu_custom_call" | custom-call | bytes 1051712 | tf_op jit(solution)/shard_map/pallas_call | solution.py:268
  17.6 0.0 collective-permute-done.5.refs_3_
  17.6 0.0 collective-permute-done.4.refs_1_
  17.6 0.0 copy-start.3
  17.7 0.7 %copy-done.3 = s32[2,2]{1,0:T(2,128)S(1)} copy-done((s32[2,2]{1,0:T(2,128)S(1)}, s32[2,2]{1,0:T(2,128)}, u32[]{:S(2)}) %copy-start.3) | copy-done | bytes 40
  18.3 0.9 %shard_map.124.refs_3_ = f32[2,2,256,256]{3,2,1,0:T(8,128)S(1)} custom-call(s32[2,2]{1,0:T(2,128)S(1)} %copy-done.3, bf16[8,2,32,256]{3,2,1,0:T(8,128)(2,1)S(1)} %get-tuple-element.27.v_ref, bf16[2,512,384]{2,1,0:T(8,128)(2,1)S(1)} %get-tuple-element.28.u_ref, bf16[2,2,2,256,256]{4,3,2,1,0:T(8,128)(2,1)S(1)} %copy-done, ...), custom_call_target="tpu_custom_call" | custom-call | flops 125829120 | bytes 2752528 | tf_op jit(solution)/shard_map/pallas_call | solution.py:268
  19.2 1.2 %collective-permute-done.3.refs_2_ = bf16[256,256]{1,0:T(8,128)(2,1)S(1)} collective-permute-done((bf16[256,256]{1,0:T(8,128)(2,1)S(1)}, bf16[256,256]{1,0:T(8,128)(2,1)S(1)}, u32[]{:S(2)}, u32[]{:S(2)}) %collective-permute-start.3) | collective-permute-done | bytes 131104 | tf_op jit(solution)/shard_map/ppermute | solution.py:32
  20.3 1.4 %collective-permute-done.2.refs_1_ = bf16[256,256]{1,0:T(8,128)(2,1)S(1)} collective-permute-done((bf16[256,256]{1,0:T(8,128)(2,1)S(1)}, bf16[256,256]{1,0:T(8,128)(2,1)S(1)}, u32[]{:S(2)}, u32[]{:S(2)}) %collective-permute-start.2) | collective-permute-done | bytes 131104 | tf_op jit(solution)/shard_map/ppermute | solution.py:32
  21.8 0.0 collective-permute-done.1.refs_0_
  21.8 0.5 %shard_map.126 = bf16[2,256,256]{2,1,0:T(8,128)(2,1)S(1)} custom-call(s32[2,2]{1,0:T(2,128)S(1)} %copy-done.3, bf16[8,2,32,256]{3,2,1,0:T(8,128)(2,1)S(1)} %get-tuple-element.27.v_ref, bf16[2,512,384]{2,1,0:T(8,128)(2,1)S(1)} %get-tuple-element.28.u_ref, bf16[2,2,2,256,256]{4,3,2,1,0:T(8,128)(2,1)S(1)} %copy-done, ...), custom_call_target="tpu_custom_call" | custom-call | flops 37748736 | bytes 3538960 | tf_op jit(solution)/shard_map/pallas_call | solution.py:268
  22.3 0.0 copy-start.1
  22.3 0.1 collective-permute-start.7
  22.4 0.5 %shard_map.125.own = f32[2,256,256]{2,1,0:T(8,128)S(1)} custom-call(s32[2,2]{1,0:T(2,128)S(1)} %copy-done.3, bf16[8,2,32,256]{3,2,1,0:T(8,128)(2,1)S(1)} %get-tuple-element.27.v_ref, bf16[2,512,384]{2,1,0:T(8,128)(2,1)S(1)} %get-tuple-element.28.u_ref, bf16[2,2,2,256,256]{4,3,2,1,0:T(8,128)(2,1)S(1)} %copy-done, ...), custom_call_target="tpu_custom_call" | custom-call | flops 37748736 | bytes 3538960 | tf_op jit(solution)/shard_map/pallas_call | solution.py:268
  22.9 1.0 %collective-permute-done.7.other = bf16[2,256,256]{2,1,0:T(8,128)(2,1)S(1)} collective-permute-done((bf16[2,256,256]{2,1,0:T(8,128)(2,1)S(1)}, bf16[2,256,256]{2,1,0:T(8,128)(2,1)S(1)}, u32[]{:S(2)}, u32[]{:S(2)}) %collective-permute-start.7) | collective-permute-done | bytes 262176 | tf_op jit(solution)/shard_map/ppermute | solution.py:368
  23.9 0.0 copy-done.1
  23.9 0.9 %shard_map.127 = (f32[256,256]{1,0:T(8,128)S(1)}, bf16[256,256]{1,0:T(8,128)(2,1)S(1)}) custom-call(f32[2,256,256]{2,1,0:T(8,128)S(1)} %shard_map.125.own, bf16[2,256,256]{2,1,0:T(8,128)(2,1)S(1)} %collective-permute-done.7.other, f32[256,256]{1,0:T(8,128)S(1)} %get-tuple-element.33.weight, f32[256,256]{1,0:T(8,128)S(1)} %get-tuple-element.34.unweight, ...), custom_call_target="tpu_custom_call" | custom-call | flops 13107200 | bytes 2228224 | tf_op jit(solution)/shard_map/pallas_call | solution.py:268
  24.8 2.0 %collective-permute-start.8 = (bf16[256,256]{1,0:T(8,128)(2,1)S(1)}, bf16[256,256]{1,0:T(8,128)(2,1)S(1)}, u32[]{:S(2)}, u32[]{:S(2)}) collective-permute-start(bf16[256,256]{1,0:T(8,128)(2,1)S(1)} %get-tuple-element.45.refs_0_), channel_id=1, source_target_pairs={{0,8},{2,10},{4,12},{6,14},{8,0},{10,2},{12,4},{14,6},{1,9},{3,11}... | collective-permute-start | bytes 393224 | tf_op jit(solution)/shard_map/ppermute | solution.py:32
  26.8 2.6 %collective-permute-start.14 = (bf16[256,256]{1,0:T(8,128)(2,1)S(1)}, bf16[256,256]{1,0:T(8,128)(2,1)S(1)}, u32[]{:S(2)}, u32[]{:S(2)}) collective-permute-start(bf16[256,256]{1,0:T(8,128)(2,1)S(1)} %get-tuple-element.45.refs_0_), channel_id=1, source_target_pairs={{0,6},{2,4},{4,2},{6,0},{8,14},{10,12},{12,10},{14,8},{1,7},{3,5},... | collective-permute-start | bytes 393224 | tf_op jit(solution)/shard_map/ppermute | solution.py:32
  29.4 0.0 collective-permute-start.13
  29.4 0.8 %collective-permute-start.12 = (bf16[256,256]{1,0:T(8,128)(2,1)S(1)}, bf16[256,256]{1,0:T(8,128)(2,1)S(1)}, u32[]{:S(2)}, u32[]{:S(2)}) collective-permute-start(bf16[256,256]{1,0:T(8,128)(2,1)S(1)} %get-tuple-element.45.refs_0_), channel_id=1, source_target_pairs={{0,2},{2,0},{4,6},{6,4},{8,10},{10,8},{12,14},{14,12},{1,3},{3,1},... | collective-permute-start | bytes 393224 | tf_op jit(solution)/shard_map/ppermute | solution.py:32
  30.3 4.0 %collective-permute-done.8.refs_2_ = bf16[256,256]{1,0:T(8,128)(2,1)S(1)} collective-permute-done((bf16[256,256]{1,0:T(8,128)(2,1)S(1)}, bf16[256,256]{1,0:T(8,128)(2,1)S(1)}, u32[]{:S(2)}, u32[]{:S(2)}) %collective-permute-start.8) | collective-permute-done | bytes 131104 | tf_op jit(solution)/shard_map/ppermute | solution.py:32
  34.2 0.0 collective-permute-start.11
  34.2 2.0 %collective-permute-start.10 = (bf16[256,256]{1,0:T(8,128)(2,1)S(1)}, bf16[256,256]{1,0:T(8,128)(2,1)S(1)}, u32[]{:S(2)}, u32[]{:S(2)}) collective-permute-start(bf16[256,256]{1,0:T(8,128)(2,1)S(1)} %collective-permute-done.8.refs_2_), channel_id=1, source_target_pairs={{0,4},{2,6},{4,0},{6,2},{8,12},{10,14},{12,8},{14,10},{1,5},{3,7},... | collective-permute-start | bytes 393224 | tf_op jit(solution)/shard_map/ppermute | solution.py:32
  36.3 0.0 collective-permute-done.14.refs_4_
  36.3 1.5 %collective-permute-start.9 = (bf16[256,256]{1,0:T(8,128)(2,1)S(1)}, bf16[256,256]{1,0:T(8,128)(2,1)S(1)}, u32[]{:S(2)}, u32[]{:S(2)}) collective-permute-start(bf16[256,256]{1,0:T(8,128)(2,1)S(1)} %collective-permute-done.8.refs_2_), channel_id=1, source_target_pairs={{0,2},{2,0},{4,6},{6,4},{8,10},{10,8},{12,14},{14,12},{1,3},{3,1},... | collective-permute-start | bytes 393224 | tf_op jit(solution)/shard_map/ppermute | solution.py:32
  37.7 0.2 shard_map.128
  38.0 0.0 collective-permute-done.13.refs_3_
  38.0 0.0 collective-permute-done.12.refs_1_
  38.0 0.9 %shard_map.129.refs_3_ = f32[2,2,256,256]{3,2,1,0:T(8,128)S(1)} custom-call(s32[2,2]{1,0:T(2,128)S(1)} %copy-done.3, bf16[8,2,32,256]{3,2,1,0:T(8,128)(2,1)S(1)} %get-tuple-element.27.v_ref, bf16[2,512,384]{2,1,0:T(8,128)(2,1)S(1)} %get-tuple-element.28.u_ref, bf16[2,2,2,256,256]{4,3,2,1,0:T(8,128)(2,1)S(1)} %copy-done, ...), custom_call_target="tpu_custom_call" | custom-call | flops 125829120 | bytes 2752528 | tf_op jit(solution)/shard_map/pallas_call | solution.py:268
  38.8 2.6 %collective-permute-done.11.refs_2_ = bf16[256,256]{1,0:T(8,128)(2,1)S(1)} collective-permute-done((bf16[256,256]{1,0:T(8,128)(2,1)S(1)}, bf16[256,256]{1,0:T(8,128)(2,1)S(1)}, u32[]{:S(2)}, u32[]{:S(2)}) %collective-permute-start.11) | collective-permute-done | bytes 131104 | tf_op jit(solution)/shard_map/ppermute | solution.py:32
  41.5 1.3 %collective-permute-done.10.refs_1_ = bf16[256,256]{1,0:T(8,128)(2,1)S(1)} collective-permute-done((bf16[256,256]{1,0:T(8,128)(2,1)S(1)}, bf16[256,256]{1,0:T(8,128)(2,1)S(1)}, u32[]{:S(2)}, u32[]{:S(2)}) %collective-permute-start.10) | collective-permute-done | bytes 131104 | tf_op jit(solution)/shard_map/ppermute | solution.py:32
  42.7 0.1 collective-permute-done.9.refs_0_
  42.9 0.5 %shard_map.131 = bf16[2,256,256]{2,1,0:T(8,128)(2,1)S(1)} custom-call(s32[2,2]{1,0:T(2,128)S(1)} %copy-done.3, bf16[8,2,32,256]{3,2,1,0:T(8,128)(2,1)S(1)} %get-tuple-element.27.v_ref, bf16[2,512,384]{2,1,0:T(8,128)(2,1)S(1)} %get-tuple-element.28.u_ref, bf16[2,2,2,256,256]{4,3,2,1,0:T(8,128)(2,1)S(1)} %copy-done, ...), custom_call_target="tpu_custom_call" | custom-call | flops 37748736 | bytes 3538960 | tf_op jit(solution)/shard_map/pallas_call | solution.py:268
  43.4 0.1 collective-permute-start.15
  43.5 0.5 %shard_map.130.own = f32[2,256,256]{2,1,0:T(8,128)S(1)} custom-call(s32[2,2]{1,0:T(2,128)S(1)} %copy-done.3, bf16[8,2,32,256]{3,2,1,0:T(8,128)(2,1)S(1)} %get-tuple-element.27.v_ref, bf16[2,512,384]{2,1,0:T(8,128)(2,1)S(1)} %get-tuple-element.28.u_ref, bf16[2,2,2,256,256]{4,3,2,1,0:T(8,128)(2,1)S(1)} %copy-done, ...), custom_call_target="tpu_custom_call" | custom-call | flops 37748736 | bytes 3538960 | tf_op jit(solution)/shard_map/pallas_call | solution.py:268
  44.0 1.0 %collective-permute-done.15.other = bf16[2,256,256]{2,1,0:T(8,128)(2,1)S(1)} collective-permute-done((bf16[2,256,256]{2,1,0:T(8,128)(2,1)S(1)}, bf16[2,256,256]{2,1,0:T(8,128)(2,1)S(1)}, u32[]{:S(2)}, u32[]{:S(2)}) %collective-permute-start.15) | collective-permute-done | bytes 262176 | tf_op jit(solution)/shard_map/ppermute | solution.py:368
  45.0 1.7 %shard_map.132 = (f32[256,256]{1,0:T(8,128)}, f32[256,256]{1,0:T(8,128)}) custom-call(f32[2,256,256]{2,1,0:T(8,128)S(1)} %shard_map.130.own, bf16[2,256,256]{2,1,0:T(8,128)(2,1)S(1)} %collective-permute-done.15.other, f32[256,256]{1,0:T(8,128)S(1)} %get-tuple-element.46.weight, f32[256,256]{1,0:T(8,128)S(1)} %get-tuple-element.47.unweight, ...), custom_call_target="tpu_custom_call" | custom-call | flops 13107200 | bytes 3538944 | tf_op jit(solution)/shard_map/pallas_call | solution.py:268
  (3 shorter events, 0.0 us)
Async XLA Ops:
  0.6 17.0 %copy-start = (bf16[2,2,2,256,256]{4,3,2,1,0:T(8,128)(2,1)S(1)}, bf16[2,2,2,256,256]{4,3,2,1,0:T(8,128)(2,1)}, u32[]{:S(2)}) copy-start(bf16[2,2,2,256,256]{4,3,2,1,0:T(8,128)(2,1)} %d_ref.11) | copy-start | bytes 3145732
  1.7 10.5 %collective-permute-start = (bf16[256,256]{1,0:T(8,128)(2,1)S(1)}, bf16[256,256]{1,0:T(8,128)(2,1)S(1)}, u32[]{:S(2)}, u32[]{:S(2)}) collective-permute-start(bf16[256,256]{1,0:T(8,128)(2,1)S(1)} %shard_map.123.refs_0_), channel_id=1, source_target_pairs={{0,8},{2,10},{4,12},{6,14},{8,0},{10,2},{12,4},{14,6},{1,9},{3,11}... | collective-permute-start | bytes 393224 | tf_op jit(solution)/shard_map/ppermute | solution.py:32
  5.8 9.4 %collective-permute-start.6 = (bf16[256,256]{1,0:T(8,128)(2,1)S(1)}, bf16[256,256]{1,0:T(8,128)(2,1)S(1)}, u32[]{:S(2)}, u32[]{:S(2)}) collective-permute-start(bf16[256,256]{1,0:T(8,128)(2,1)S(1)} %shard_map.123.refs_0_), channel_id=1, source_target_pairs={{0,6},{2,4},{4,2},{6,0},{8,14},{10,12},{12,10},{14,8},{1,7},{3,5},... | collective-permute-start | bytes 393224 | tf_op jit(solution)/shard_map/ppermute | solution.py:32
  8.3 9.3 %collective-permute-start.5 = (bf16[256,256]{1,0:T(8,128)(2,1)S(1)}, bf16[256,256]{1,0:T(8,128)(2,1)S(1)}, u32[]{:S(2)}, u32[]{:S(2)}) collective-permute-start(bf16[256,256]{1,0:T(8,128)(2,1)S(1)} %shard_map.123.refs_0_), channel_id=1, source_target_pairs={{0,4},{2,6},{4,0},{6,2},{8,12},{10,14},{12,8},{14,10},{1,5},{3,7},... | collective-permute-start | bytes 393224 | tf_op jit(solution)/shard_map/ppermute | solution.py:32
  8.8 8.9 %collective-permute-start.4 = (bf16[256,256]{1,0:T(8,128)(2,1)S(1)}, bf16[256,256]{1,0:T(8,128)(2,1)S(1)}, u32[]{:S(2)}, u32[]{:S(2)}) collective-permute-start(bf16[256,256]{1,0:T(8,128)(2,1)S(1)} %shard_map.123.refs_0_), channel_id=1, source_target_pairs={{0,2},{2,0},{4,6},{6,4},{8,10},{10,8},{12,14},{14,12},{1,3},{3,1},... | collective-permute-start | bytes 393224 | tf_op jit(solution)/shard_map/ppermute | solution.py:32
  12.2 8.2 %collective-permute-start.3 = (bf16[256,256]{1,0:T(8,128)(2,1)S(1)}, bf16[256,256]{1,0:T(8,128)(2,1)S(1)}, u32[]{:S(2)}, u32[]{:S(2)}) collective-permute-start(bf16[256,256]{1,0:T(8,128)(2,1)S(1)} %collective-permute-done.refs_2_), channel_id=1, source_target_pairs={{0,6},{2,4},{4,2},{6,0},{8,14},{10,12},{12,10},{14,8},{1,7},{3,5},... | collective-permute-start | bytes 393224 | tf_op jit(solution)/shard_map/ppermute | solution.py:32
  13.8 8.0 %collective-permute-start.2 = (bf16[256,256]{1,0:T(8,128)(2,1)S(1)}, bf16[256,256]{1,0:T(8,128)(2,1)S(1)}, u32[]{:S(2)}, u32[]{:S(2)}) collective-permute-start(bf16[256,256]{1,0:T(8,128)(2,1)S(1)} %collective-permute-done.refs_2_), channel_id=1, source_target_pairs={{0,4},{2,6},{4,0},{6,2},{8,12},{10,14},{12,8},{14,10},{1,5},{3,7},... | collective-permute-start | bytes 393224 | tf_op jit(solution)/shard_map/ppermute | solution.py:32
  15.2 6.5 %collective-permute-start.1 = (bf16[256,256]{1,0:T(8,128)(2,1)S(1)}, bf16[256,256]{1,0:T(8,128)(2,1)S(1)}, u32[]{:S(2)}, u32[]{:S(2)}) collective-permute-start(bf16[256,256]{1,0:T(8,128)(2,1)S(1)} %collective-permute-done.refs_2_), channel_id=1, source_target_pairs={{0,2},{2,0},{4,6},{6,4},{8,10},{10,8},{12,14},{14,12},{1,3},{3,1},... | collective-permute-start | bytes 393224 | tf_op jit(solution)/shard_map/ppermute | solution.py:32
  17.6 0.7 %copy-start.3 = (s32[2,2]{1,0:T(2,128)S(1)}, s32[2,2]{1,0:T(2,128)}, u32[]{:S(2)}) copy-start(s32[2,2]{1,0:T(2,128)} %near_ref.11) | copy-start | bytes 52
  22.3 1.6 %copy-start.1 = (f32[256,256]{1,0:T(8,128)S(1)}, f32[256,256]{1,0:T(8,128)}, u32[]{:S(2)}) copy-start(f32[256,256]{1,0:T(8,128)} %tau.3) | copy-start | bytes 786436
  22.3 1.6 %collective-permute-start.7 = (bf16[2,256,256]{2,1,0:T(8,128)(2,1)S(1)}, bf16[2,256,256]{2,1,0:T(8,128)(2,1)S(1)}, u32[]{:S(2)}, u32[]{:S(2)}) collective-permute-start(bf16[2,256,256]{2,1,0:T(8,128)(2,1)S(1)} %shard_map.126), channel_id=1, source_target_pairs={{0,1},{1,0},{2,3},{3,2},{4,5},{5,4},{6,7},{7,6},{8,9},{9,8},{10,11... | collective-permute-start | bytes 786440 | tf_op jit(solution)/shard_map/ppermute | solution.py:368
  23.9 13.8 %copy-start.2 = (f32[256,256]{1,0:T(8,128)S(1)}, f32[256,256]{1,0:T(8,128)}, u32[]{:S(2)}) copy-start(f32[256,256]{1,0:T(8,128)} %state.1) | copy-start | bytes 786436
  24.8 9.4 %collective-permute-start.8 = (bf16[256,256]{1,0:T(8,128)(2,1)S(1)}, bf16[256,256]{1,0:T(8,128)(2,1)S(1)}, u32[]{:S(2)}, u32[]{:S(2)}) collective-permute-start(bf16[256,256]{1,0:T(8,128)(2,1)S(1)} %get-tuple-element.45.refs_0_), channel_id=1, source_target_pairs={{0,8},{2,10},{4,12},{6,14},{8,0},{10,2},{12,4},{14,6},{1,9},{3,11}... | collective-permute-start | bytes 393224 | tf_op jit(solution)/shard_map/ppermute | solution.py:32
  26.8 9.5 %collective-permute-start.14 = (bf16[256,256]{1,0:T(8,128)(2,1)S(1)}, bf16[256,256]{1,0:T(8,128)(2,1)S(1)}, u32[]{:S(2)}, u32[]{:S(2)}) collective-permute-start(bf16[256,256]{1,0:T(8,128)(2,1)S(1)} %get-tuple-element.45.refs_0_), channel_id=1, source_target_pairs={{0,6},{2,4},{4,2},{6,0},{8,14},{10,12},{12,10},{14,8},{1,7},{3,5},... | collective-permute-start | bytes 393224 | tf_op jit(solution)/shard_map/ppermute | solution.py:32
  29.4 8.5 %collective-permute-start.13 = (bf16[256,256]{1,0:T(8,128)(2,1)S(1)}, bf16[256,256]{1,0:T(8,128)(2,1)S(1)}, u32[]{:S(2)}, u32[]{:S(2)}) collective-permute-start(bf16[256,256]{1,0:T(8,128)(2,1)S(1)} %get-tuple-element.45.refs_0_), channel_id=1, source_target_pairs={{0,4},{2,6},{4,0},{6,2},{8,12},{10,14},{12,8},{14,10},{1,5},{3,7},... | collective-permute-start | bytes 393224 | tf_op jit(solution)/shard_map/ppermute | solution.py:32
  29.4 8.5 %collective-permute-start.12 = (bf16[256,256]{1,0:T(8,128)(2,1)S(1)}, bf16[256,256]{1,0:T(8,128)(2,1)S(1)}, u32[]{:S(2)}, u32[]{:S(2)}) collective-permute-start(bf16[256,256]{1,0:T(8,128)(2,1)S(1)} %get-tuple-element.45.refs_0_), channel_id=1, source_target_pairs={{0,2},{2,0},{4,6},{6,4},{8,10},{10,8},{12,14},{14,12},{1,3},{3,1},... | collective-permute-start | bytes 393224 | tf_op jit(solution)/shard_map/ppermute | solution.py:32
  34.2 7.2 %collective-permute-start.11 = (bf16[256,256]{1,0:T(8,128)(2,1)S(1)}, bf16[256,256]{1,0:T(8,128)(2,1)S(1)}, u32[]{:S(2)}, u32[]{:S(2)}) collective-permute-start(bf16[256,256]{1,0:T(8,128)(2,1)S(1)} %collective-permute-done.8.refs_2_), channel_id=1, source_target_pairs={{0,6},{2,4},{4,2},{6,0},{8,14},{10,12},{12,10},{14,8},{1,7},{3,5},... | collective-permute-start | bytes 393224 | tf_op jit(solution)/shard_map/ppermute | solution.py:32
  34.2 8.5 %collective-permute-start.10 = (bf16[256,256]{1,0:T(8,128)(2,1)S(1)}, bf16[256,256]{1,0:T(8,128)(2,1)S(1)}, u32[]{:S(2)}, u32[]{:S(2)}) collective-permute-start(bf16[256,256]{1,0:T(8,128)(2,1)S(1)} %collective-permute-done.8.refs_2_), channel_id=1, source_target_pairs={{0,4},{2,6},{4,0},{6,2},{8,12},{10,14},{12,8},{14,10},{1,5},{3,7},... | collective-permute-start | bytes 393224 | tf_op jit(solution)/shard_map/ppermute | solution.py:32
  36.3 6.6 %collective-permute-start.9 = (bf16[256,256]{1,0:T(8,128)(2,1)S(1)}, bf16[256,256]{1,0:T(8,128)(2,1)S(1)}, u32[]{:S(2)}, u32[]{:S(2)}) collective-permute-start(bf16[256,256]{1,0:T(8,128)(2,1)S(1)} %collective-permute-done.8.refs_2_), channel_id=1, source_target_pairs={{0,2},{2,0},{4,6},{6,4},{8,10},{10,8},{12,14},{14,12},{1,3},{3,1},... | collective-permute-start | bytes 393224 | tf_op jit(solution)/shard_map/ppermute | solution.py:32
  43.4 1.6 %collective-permute-start.15 = (bf16[2,256,256]{2,1,0:T(8,128)(2,1)S(1)}, bf16[2,256,256]{2,1,0:T(8,128)(2,1)S(1)}, u32[]{:S(2)}, u32[]{:S(2)}) collective-permute-start(bf16[2,256,256]{2,1,0:T(8,128)(2,1)S(1)} %shard_map.131), channel_id=1, source_target_pairs={{0,1},{1,0},{2,3},{3,2},{4,5},{5,4},{6,7},{7,6},{8,9},{9,8},{10,11... | collective-permute-start | bytes 786440 | tf_op jit(solution)/shard_map/ppermute | solution.py:368

commit v27 on v25

--- a/solution.py
+++ b/solution.py
@@ -41,12 +41,17 @@
 
 
 IN_PIECES = 8
-OUT_PIECES = 4
+OUT_SHARES = (2, 4, 8, 8)
 
 
 def row_pieces(size, pieces):
     tall = size // pieces
     return [pl.ds(at * tall, tall) for at in range(pieces)]
+
+
+def shrinking_pieces(size):
+    talls = [size // share for share in OUT_SHARES]
+    return [pl.ds(sum(talls[:at]), tall) for at, tall in enumerate(talls)]
 
 
 def narrow_kernel(wide_ref, narrow_ref, held, sem):
@@ -253,7 +258,7 @@
         mean_change[rows, part] = (change[rows, part] + second) * 0.5
 
     copies = []
-    for at, part in enumerate(row_pieces(size, OUT_PIECES)):
+    for at, part in enumerate(shrinking_pieces(size)):
         over_pieces(part.start, part.size, members, coef.shape[2], work)
         for kind, (held, out) in enumerate(((mean_rate, rate_out), (mean_change, change_out))):
             copies.append(pltpu.make_async_copy(held.at[part], out.at[part], sem.at[kind, at]))
@@ -391,7 +396,7 @@
         (
             pltpu.VMEM((size, members), wide),
             pltpu.VMEM((size, members), wide),
-            pltpu.SemaphoreType.DMA((2, OUT_PIECES)),
+            pltpu.SemaphoreType.DMA((2, len(OUT_SHARES))),
         ),
         flops=200 * size * members,
         out_far=True,

time: 46.8 us -> 46.7 us (level)
  no operation moved by 1% of the time
where the time goes in v27:
time: 46.7 us; the launch traced here: 46.6 us
  starting transfers between devices  19.8 us (42%)
  waiting for transfers between devices  15.9 us (34%)
  Pallas kernels  9.47 us (20%)
  between operations  0.77 us (2%)
  local copies, waits for them, and re-layouts  0.68 us (1%)
    ppermute x14, starting transfers between devices, swapped(): lax.ppermute(data, 'row', [(row, row ^ mask) for row in range(count)])  19.6 us
    ppermute x14, waiting for transfers between devices, swapped(): lax.ppermute(data, 'row', [(row, row ^ mask) for row in range(count)])  13.9 us
    pallas_call x11, Pallas kernels, on_core(): pl.pallas_call(kernel, out_shape=outs, in_specs=[hbm] * len(far) + [vmem]...  9.47 us
    ppermute x2, waiting for transfers between devices, lattice(): other = lax.ppermute(add(found[end], end, 1, sums, narrow), 'col', swap)  1.96 us
  transfers between devices with their start and end apart: 16, of which 13 were waited for; matrix products, arithmetic and copies ran while one was open for 0% of the time, Pallas kernels for 10%

profile of v27, /device:TPU:0, one launch (start us, length us, event | category | flops | bytes accessed | tf_op | source)
XLA Modules:
  0.0 46.6 jit_solution(16875360729213532321)
XLA Ops:
  0.6 0.0 copy-start
  0.6 1.0 %shard_map.123.refs_0_ = bf16[256,256]{1,0:T(8,128)(2,1)S(1)} custom-call(f32[256,256]{1,0:T(8,128)} %wide_ref.1), custom_call_target="tpu_custom_call" | custom-call | bytes 262144 | tf_op jit(solution)/shard_map/pallas_call | solution.py:273
  1.7 4.1 %collective-permute-start = (bf16[256,256]{1,0:T(8,128)(2,1)S(1)}, bf16[256,256]{1,0:T(8,128)(2,1)S(1)}, u32[]{:S(2)}, u32[]{:S(2)}) collective-permute-start(bf16[256,256]{1,0:T(8,128)(2,1)S(1)} %shard_map.123.refs_0_), channel_id=1, source_target_pairs={{0,8},{2,10},{4,12},{6,14},{8,0},{10,2},{12,4},{14,6},{1,9},{3,11}... | collective-permute-start | bytes 393224 | tf_op jit(solution)/shard_map/ppermute | solution.py:32
  5.8 2.5 %collective-permute-start.6 = (bf16[256,256]{1,0:T(8,128)(2,1)S(1)}, bf16[256,256]{1,0:T(8,128)(2,1)S(1)}, u32[]{:S(2)}, u32[]{:S(2)}) collective-permute-start(bf16[256,256]{1,0:T(8,128)(2,1)S(1)} %shard_map.123.refs_0_), channel_id=1, source_target_pairs={{0,6},{2,4},{4,2},{6,0},{8,14},{10,12},{12,10},{14,8},{1,7},{3,5},... | collective-permute-start | bytes 393224 | tf_op jit(solution)/shard_map/ppermute | solution.py:32
  8.3 0.4 collective-permute-start.5
  8.8 0.5 %collective-permute-start.4 = (bf16[256,256]{1,0:T(8,128)(2,1)S(1)}, bf16[256,256]{1,0:T(8,128)(2,1)S(1)}, u32[]{:S(2)}, u32[]{:S(2)}) collective-permute-start(bf16[256,256]{1,0:T(8,128)(2,1)S(1)} %shard_map.123.refs_0_), channel_id=1, source_target_pairs={{0,2},{2,0},{4,6},{6,4},{8,10},{10,8},{12,14},{14,12},{1,3},{3,1},... | collective-permute-start | bytes 393224 | tf_op jit(solution)/shard_map/ppermute | solution.py:32
  9.3 2.9 %collective-permute-done.refs_2_ = bf16[256,256]{1,0:T(8,128)(2,1)S(1)} collective-permute-done((bf16[256,256]{1,0:T(8,128)(2,1)S(1)}, bf16[256,256]{1,0:T(8,128)(2,1)S(1)}, u32[]{:S(2)}, u32[]{:S(2)}) %collective-permute-start) | collective-permute-done | bytes 131104 | tf_op jit(solution)/shard_map/ppermute | solution.py:32
  12.2 1.6 %collective-permute-start.3 = (bf16[256,256]{1,0:T(8,128)(2,1)S(1)}, bf16[256,256]{1,0:T(8,128)(2,1)S(1)}, u32[]{:S(2)}, u32[]{:S(2)}) collective-permute-start(bf16[256,256]{1,0:T(8,128)(2,1)S(1)} %collective-permute-done.refs_2_), channel_id=1, source_target_pairs={{0,6},{2,4},{4,2},{6,0},{8,14},{10,12},{12,10},{14,8},{1,7},{3,5},... | collective-permute-start | bytes 393224 | tf_op jit(solution)/shard_map/ppermute | solution.py:32
  13.8 0.5 %collective-permute-start.2 = (bf16[256,256]{1,0:T(8,128)(2,1)S(1)}, bf16[256,256]{1,0:T(8,128)(2,1)S(1)}, u32[]{:S(2)}, u32[]{:S(2)}) collective-permute-start(bf16[256,256]{1,0:T(8,128)(2,1)S(1)} %collective-permute-done.refs_2_), channel_id=1, source_target_pairs={{0,2},{2,0},{4,6},{6,4},{8,10},{10,8},{12,14},{14,12},{1,3},{3,1},... | collective-permute-start | bytes 393224 | tf_op jit(solution)/shard_map/ppermute | solution.py:32
  14.3 0.4 collective-permute-done.6.refs_4_
  14.7 1.2 %collective-permute-start.1 = (bf16[256,256]{1,0:T(8,128)(2,1)S(1)}, bf16[256,256]{1,0:T(8,128)(2,1)S(1)}, u32[]{:S(2)}, u32[]{:S(2)}) collective-permute-start(bf16[256,256]{1,0:T(8,128)(2,1)S(1)} %collective-permute-done.refs_2_), channel_id=1, source_target_pairs={{0,4},{2,6},{4,0},{6,2},{8,12},{10,14},{12,8},{14,10},{1,5},{3,7},... | collective-permute-start | bytes 393224 | tf_op jit(solution)/shard_map/ppermute | solution.py:32
  15.9 1.8 %shard_map.122 = (bf16[8,2,32,256]{3,2,1,0:T(8,128)(2,1)S(1)}, bf16[2,512,384]{2,1,0:T(8,128)(2,1)S(1)}, f32[5,256,128]{2,1,0:T(8,128)S(1)}, f32[256,256]{1,0:T(...) custom-call(s32[2,8]{1,0:T(2,128)} %refs_0_.1, bf16[2,8,32,256]{3,2,1,0:T(8,128)(2,1)} %refs_1_.1, ...), custom_call_target="tpu_custom_call" | custom-call | bytes 1051712 | tf_op jit(solution)/shard_map/pallas_call | solution.py:273
  17.7 0.0 collective-permute-done.5.refs_3_
  17.8 0.0 collective-permute-done.4.refs_1_
  17.8 0.0 copy-start.3
  17.8 0.0 copy-done
  17.8 0.7 %copy-done.3 = s32[2,2]{1,0:T(2,128)S(1)} copy-done((s32[2,2]{1,0:T(2,128)S(1)}, s32[2,2]{1,0:T(2,128)}, u32[]{:S(2)}) %copy-start.3) | copy-done | bytes 40
  18.4 0.9 %shard_map.124.refs_3_ = f32[2,2,256,256]{3,2,1,0:T(8,128)S(1)} custom-call(s32[2,2]{1,0:T(2,128)S(1)} %copy-done.3, bf16[8,2,32,256]{3,2,1,0:T(8,128)(2,1)S(1)} %get-tuple-element.27.v_ref, bf16[2,512,384]{2,1,0:T(8,128)(2,1)S(1)} %get-tuple-element.28.u_ref, bf16[2,2,2,256,256]{4,3,2,1,0:T(8,128)(2,1)S(1)} %copy-done, ...), custom_call_target="tpu_custom_call" | custom-call | flops 125829120 | bytes 2752528 | tf_op jit(solution)/shard_map/pallas_call | solution.py:273
  19.3 1.0 %collective-permute-done.3.refs_2_ = bf16[256,256]{1,0:T(8,128)(2,1)S(1)} collective-permute-done((bf16[256,256]{1,0:T(8,128)(2,1)S(1)}, bf16[256,256]{1,0:T(8,128)(2,1)S(1)}, u32[]{:S(2)}, u32[]{:S(2)}) %collective-permute-start.3) | collective-permute-done | bytes 131104 | tf_op jit(solution)/shard_map/ppermute | solution.py:32
  20.3 0.7 %collective-permute-done.2.refs_1_ = bf16[256,256]{1,0:T(8,128)(2,1)S(1)} collective-permute-done((bf16[256,256]{1,0:T(8,128)(2,1)S(1)}, bf16[256,256]{1,0:T(8,128)(2,1)S(1)}, u32[]{:S(2)}, u32[]{:S(2)}) %collective-permute-start.2) | collective-permute-done | bytes 131104 | tf_op jit(solution)/shard_map/ppermute | solution.py:32
  21.1 0.7 %collective-permute-done.1.refs_0_ = bf16[256,256]{1,0:T(8,128)(2,1)S(1)} collective-permute-done((bf16[256,256]{1,0:T(8,128)(2,1)S(1)}, bf16[256,256]{1,0:T(8,128)(2,1)S(1)}, u32[]{:S(2)}, u32[]{:S(2)}) %collective-permute-start.1) | collective-permute-done | bytes 131104 | tf_op jit(solution)/shard_map/ppermute | solution.py:32
  21.8 0.5 %shard_map.126 = bf16[2,256,256]{2,1,0:T(8,128)(2,1)S(1)} custom-call(s32[2,2]{1,0:T(2,128)S(1)} %copy-done.3, bf16[8,2,32,256]{3,2,1,0:T(8,128)(2,1)S(1)} %get-tuple-element.27.v_ref, bf16[2,512,384]{2,1,0:T(8,128)(2,1)S(1)} %get-tuple-element.28.u_ref, bf16[2,2,2,256,256]{4,3,2,1,0:T(8,128)(2,1)S(1)} %copy-done, ...), custom_call_target="tpu_custom_call" | custom-call | flops 37748736 | bytes 3538960 | tf_op jit(solution)/shard_map/pallas_call | solution.py:273
  22.3 0.0 copy-start.1
  22.3 0.1 collective-permute-start.7
  22.4 0.5 %shard_map.125.own = f32[2,256,256]{2,1,0:T(8,128)S(1)} custom-call(s32[2,2]{1,0:T(2,128)S(1)} %copy-done.3, bf16[8,2,32,256]{3,2,1,0:T(8,128)(2,1)S(1)} %get-tuple-element.27.v_ref, bf16[2,512,384]{2,1,0:T(8,128)(2,1)S(1)} %get-tuple-element.28.u_ref, bf16[2,2,2,256,256]{4,3,2,1,0:T(8,128)(2,1)S(1)} %copy-done, ...), custom_call_target="tpu_custom_call" | custom-call | flops 37748736 | bytes 3538960 | tf_op jit(solution)/shard_map/pallas_call | solution.py:273
  22.9 1.0 %collective-permute-done.7.other = bf16[2,256,256]{2,1,0:T(8,128)(2,1)S(1)} collective-permute-done((bf16[2,256,256]{2,1,0:T(8,128)(2,1)S(1)}, bf16[2,256,256]{2,1,0:T(8,128)(2,1)S(1)}, u32[]{:S(2)}, u32[]{:S(2)}) %collective-permute-start.7) | collective-permute-done | bytes 262176 | tf_op jit(solution)/shard_map/ppermute | solution.py:373
  23.9 0.9 %shard_map.127 = (f32[256,256]{1,0:T(8,128)S(1)}, bf16[256,256]{1,0:T(8,128)(2,1)S(1)}) custom-call(f32[2,256,256]{2,1,0:T(8,128)S(1)} %shard_map.125.own, bf16[2,256,256]{2,1,0:T(8,128)(2,1)S(1)} %collective-permute-done.7.other, f32[256,256]{1,0:T(8,128)S(1)} %get-tuple-element.33.weight, f32[256,256]{1,0:T(8,128)S(1)} %get-tuple-element.34.unweight, ...), custom_call_target="tpu_custom_call" | custom-call | flops 13107200 | bytes 2228224 | tf_op jit(solution)/shard_map/pallas_call | solution.py:273
  24.8 2.0 %collective-permute-start.8 = (bf16[256,256]{1,0:T(8,128)(2,1)S(1)}, bf16[256,256]{1,0:T(8,128)(2,1)S(1)}, u32[]{:S(2)}, u32[]{:S(2)}) collective-permute-start(bf16[256,256]{1,0:T(8,128)(2,1)S(1)} %get-tuple-element.45.refs_0_), channel_id=1, source_target_pairs={{0,8},{2,10},{4,12},{6,14},{8,0},{10,2},{12,4},{14,6},{1,9},{3,11}... | collective-permute-start | bytes 393224 | tf_op jit(solution)/shard_map/ppermute | solution.py:32
  26.8 1.7 %collective-permute-start.14 = (bf16[256,256]{1,0:T(8,128)(2,1)S(1)}, bf16[256,256]{1,0:T(8,128)(2,1)S(1)}, u32[]{:S(2)}, u32[]{:S(2)}) collective-permute-start(bf16[256,256]{1,0:T(8,128)(2,1)S(1)} %get-tuple-element.45.refs_0_), channel_id=1, source_target_pairs={{0,6},{2,4},{4,2},{6,0},{8,14},{10,12},{12,10},{14,8},{1,7},{3,5},... | collective-permute-start | bytes 393224 | tf_op jit(solution)/shard_map/ppermute | solution.py:32
  28.5 0.3 collective-permute-start.13
  28.8 1.5 %collective-permute-start.12 = (bf16[256,256]{1,0:T(8,128)(2,1)S(1)}, bf16[256,256]{1,0:T(8,128)(2,1)S(1)}, u32[]{:S(2)}, u32[]{:S(2)}) collective-permute-start(bf16[256,256]{1,0:T(8,128)(2,1)S(1)} %get-tuple-element.45.refs_0_), channel_id=1, source_target_pairs={{0,2},{2,0},{4,6},{6,4},{8,10},{10,8},{12,14},{14,12},{1,3},{3,1},... | collective-permute-start | bytes 393224 | tf_op jit(solution)/shard_map/ppermute | solution.py:32
  30.3 3.9 %collective-permute-done.8.refs_2_ = bf16[256,256]{1,0:T(8,128)(2,1)S(1)} collective-permute-done((bf16[256,256]{1,0:T(8,128)(2,1)S(1)}, bf16[256,256]{1,0:T(8,128)(2,1)S(1)}, u32[]{:S(2)}, u32[]{:S(2)}) %collective-permute-start.8) | collective-permute-done | bytes 131104 | tf_op jit(solution)/shard_map/ppermute | solution.py:32
  34.2 0.0 collective-permute-start.11
  34.2 1.4 %collective-permute-start.10 = (bf16[256,256]{1,0:T(8,128)(2,1)S(1)}, bf16[256,256]{1,0:T(8,128)(2,1)S(1)}, u32[]{:S(2)}, u32[]{:S(2)}) collective-permute-start(bf16[256,256]{1,0:T(8,128)(2,1)S(1)} %collective-permute-done.8.refs_2_), channel_id=1, source_target_pairs={{0,2},{2,0},{4,6},{6,4},{8,10},{10,8},{12,14},{14,12},{1,3},{3,1},... | collective-permute-start | bytes 393224 | tf_op jit(solution)/shard_map/ppermute | solution.py:32
  35.6 0.3 collective-permute-done.14.refs_4_
  35.9 1.8 %collective-permute-start.9 = (bf16[256,256]{1,0:T(8,128)(2,1)S(1)}, bf16[256,256]{1,0:T(8,128)(2,1)S(1)}, u32[]{:S(2)}, u32[]{:S(2)}) collective-permute-start(bf16[256,256]{1,0:T(8,128)(2,1)S(1)} %collective-permute-done.8.refs_2_), channel_id=1, source_target_pairs={{0,4},{2,6},{4,0},{6,2},{8,12},{10,14},{12,8},{14,10},{1,5},{3,7},... | collective-permute-start | bytes 393224 | tf_op jit(solution)/shard_map/ppermute | solution.py:32
  37.7 0.2 shard_map.128
  38.0 0.2 collective-permute-done.13.refs_3_
  38.2 0.0 collective-permute-done.12.refs_1_
  38.2 0.8 %shard_map.129.refs_3_ = f32[2,2,256,256]{3,2,1,0:T(8,128)S(1)} custom-call(s32[2,2]{1,0:T(2,128)S(1)} %copy-done.3, bf16[8,2,32,256]{3,2,1,0:T(8,128)(2,1)S(1)} %get-tuple-element.27.v_ref, bf16[2,512,384]{2,1,0:T(8,128)(2,1)S(1)} %get-tuple-element.28.u_ref, bf16[2,2,2,256,256]{4,3,2,1,0:T(8,128)(2,1)S(1)} %copy-done, ...), custom_call_target="tpu_custom_call" | custom-call | flops 125829120 | bytes 2752528 | tf_op jit(solution)/shard_map/pallas_call | solution.py:273
  39.0 2.6 %collective-permute-done.11.refs_2_ = bf16[256,256]{1,0:T(8,128)(2,1)S(1)} collective-permute-done((bf16[256,256]{1,0:T(8,128)(2,1)S(1)}, bf16[256,256]{1,0:T(8,128)(2,1)S(1)}, u32[]{:S(2)}, u32[]{:S(2)}) %collective-permute-start.11) | collective-permute-done | bytes 131104 | tf_op jit(solution)/shard_map/ppermute | solution.py:32
  41.6 0.5 %collective-permute-done.10.refs_1_ = bf16[256,256]{1,0:T(8,128)(2,1)S(1)} collective-permute-done((bf16[256,256]{1,0:T(8,128)(2,1)S(1)}, bf16[256,256]{1,0:T(8,128)(2,1)S(1)}, u32[]{:S(2)}, u32[]{:S(2)}) %collective-permute-start.10) | collective-permute-done | bytes 131104 | tf_op jit(solution)/shard_map/ppermute | solution.py:32
  42.1 0.6 %collective-permute-done.9.refs_0_ = bf16[256,256]{1,0:T(8,128)(2,1)S(1)} collective-permute-done((bf16[256,256]{1,0:T(8,128)(2,1)S(1)}, bf16[256,256]{1,0:T(8,128)(2,1)S(1)}, u32[]{:S(2)}, u32[]{:S(2)}) %collective-permute-start.9) | collective-permute-done | bytes 131104 | tf_op jit(solution)/shard_map/ppermute | solution.py:32
  42.7 0.5 %shard_map.131 = bf16[2,256,256]{2,1,0:T(8,128)(2,1)S(1)} custom-call(s32[2,2]{1,0:T(2,128)S(1)} %copy-done.3, bf16[8,2,32,256]{3,2,1,0:T(8,128)(2,1)S(1)} %get-tuple-element.27.v_ref, bf16[2,512,384]{2,1,0:T(8,128)(2,1)S(1)} %get-tuple-element.28.u_ref, bf16[2,2,2,256,256]{4,3,2,1,0:T(8,128)(2,1)S(1)} %copy-done, ...), custom_call_target="tpu_custom_call" | custom-call | flops 37748736 | bytes 3538960 | tf_op jit(solution)/shard_map/pallas_call | solution.py:273
  43.3 0.1 collective-permute-start.15
  43.4 0.5 %shard_map.130.own = f32[2,256,256]{2,1,0:T(8,128)S(1)} custom-call(s32[2,2]{1,0:T(2,128)S(1)} %copy-done.3, bf16[8,2,32,256]{3,2,1,0:T(8,128)(2,1)S(1)} %get-tuple-element.27.v_ref, bf16[2,512,384]{2,1,0:T(8,128)(2,1)S(1)} %get-tuple-element.28.u_ref, bf16[2,2,2,256,256]{4,3,2,1,0:T(8,128)(2,1)S(1)} %copy-done, ...), custom_call_target="tpu_custom_call" | custom-call | flops 37748736 | bytes 3538960 | tf_op jit(solution)/shard_map/pallas_call | solution.py:273
  43.9 1.0 %collective-permute-done.15.other = bf16[2,256,256]{2,1,0:T(8,128)(2,1)S(1)} collective-permute-done((bf16[2,256,256]{2,1,0:T(8,128)(2,1)S(1)}, bf16[2,256,256]{2,1,0:T(8,128)(2,1)S(1)}, u32[]{:S(2)}, u32[]{:S(2)}) %collective-permute-start.15) | collective-permute-done | bytes 262176 | tf_op jit(solution)/shard_map/ppermute | solution.py:373
  44.9 1.7 %shard_map.132 = (f32[256,256]{1,0:T(8,128)}, f32[256,256]{1,0:T(8,128)}) custom-call(f32[2,256,256]{2,1,0:T(8,128)S(1)} %shard_map.130.own, bf16[2,256,256]{2,1,0:T(8,128)(2,1)S(1)} %collective-permute-done.15.other, f32[256,256]{1,0:T(8,128)S(1)} %get-tuple-element.46.weight, f32[256,256]{1,0:T(8,128)S(1)} %get-tuple-element.47.unweight, ...), custom_call_target="tpu_custom_call" | custom-call | flops 13107200 | bytes 3538944 | tf_op jit(solution)/shard_map/pallas_call | solution.py:273
  (3 shorter events, 0.0 us)
Async XLA Ops:
  0.6 17.2 %copy-start = (bf16[2,2,2,256,256]{4,3,2,1,0:T(8,128)(2,1)S(1)}, bf16[2,2,2,256,256]{4,3,2,1,0:T(8,128)(2,1)}, u32[]{:S(2)}) copy-start(bf16[2,2,2,256,256]{4,3,2,1,0:T(8,128)(2,1)} %d_ref.11) | copy-start | bytes 3145732
  1.7 10.5 %collective-permute-start = (bf16[256,256]{1,0:T(8,128)(2,1)S(1)}, bf16[256,256]{1,0:T(8,128)(2,1)S(1)}, u32[]{:S(2)}, u32[]{:S(2)}) collective-permute-start(bf16[256,256]{1,0:T(8,128)(2,1)S(1)} %shard_map.123.refs_0_), channel_id=1, source_target_pairs={{0,8},{2,10},{4,12},{6,14},{8,0},{10,2},{12,4},{14,6},{1,9},{3,11}... | collective-permute-start | bytes 393224 | tf_op jit(solution)/shard_map/ppermute | solution.py:32
  5.8 9.0 %collective-permute-start.6 = (bf16[256,256]{1,0:T(8,128)(2,1)S(1)}, bf16[256,256]{1,0:T(8,128)(2,1)S(1)}, u32[]{:S(2)}, u32[]{:S(2)}) collective-permute-start(bf16[256,256]{1,0:T(8,128)(2,1)S(1)} %shard_map.123.refs_0_), channel_id=1, source_target_pairs={{0,6},{2,4},{4,2},{6,0},{8,14},{10,12},{12,10},{14,8},{1,7},{3,5},... | collective-permute-start | bytes 393224 | tf_op jit(solution)/shard_map/ppermute | solution.py:32
  8.3 9.4 %collective-permute-start.5 = (bf16[256,256]{1,0:T(8,128)(2,1)S(1)}, bf16[256,256]{1,0:T(8,128)(2,1)S(1)}, u32[]{:S(2)}, u32[]{:S(2)}) collective-permute-start(bf16[256,256]{1,0:T(8,128)(2,1)S(1)} %shard_map.123.refs_0_), channel_id=1, source_target_pairs={{0,4},{2,6},{4,0},{6,2},{8,12},{10,14},{12,8},{14,10},{1,5},{3,7},... | collective-permute-start | bytes 393224 | tf_op jit(solution)/shard_map/ppermute | solution.py:32
  8.8 9.0 %collective-permute-start.4 = (bf16[256,256]{1,0:T(8,128)(2,1)S(1)}, bf16[256,256]{1,0:T(8,128)(2,1)S(1)}, u32[]{:S(2)}, u32[]{:S(2)}) collective-permute-start(bf16[256,256]{1,0:T(8,128)(2,1)S(1)} %shard_map.123.refs_0_), channel_id=1, source_target_pairs={{0,2},{2,0},{4,6},{6,4},{8,10},{10,8},{12,14},{14,12},{1,3},{3,1},... | collective-permute-start | bytes 393224 | tf_op jit(solution)/shard_map/ppermute | solution.py:32
  12.2 8.2 %collective-permute-start.3 = (bf16[256,256]{1,0:T(8,128)(2,1)S(1)}, bf16[256,256]{1,0:T(8,128)(2,1)S(1)}, u32[]{:S(2)}, u32[]{:S(2)}) collective-permute-start(bf16[256,256]{1,0:T(8,128)(2,1)S(1)} %collective-permute-done.refs_2_), channel_id=1, source_target_pairs={{0,6},{2,4},{4,2},{6,0},{8,14},{10,12},{12,10},{14,8},{1,7},{3,5},... | collective-permute-start | bytes 393224 | tf_op jit(solution)/shard_map/ppermute | solution.py:32
  13.8 7.2 %collective-permute-start.2 = (bf16[256,256]{1,0:T(8,128)(2,1)S(1)}, bf16[256,256]{1,0:T(8,128)(2,1)S(1)}, u32[]{:S(2)}, u32[]{:S(2)}) collective-permute-start(bf16[256,256]{1,0:T(8,128)(2,1)S(1)} %collective-permute-done.refs_2_), channel_id=1, source_target_pairs={{0,2},{2,0},{4,6},{6,4},{8,10},{10,8},{12,14},{14,12},{1,3},{3,1},... | collective-permute-start | bytes 393224 | tf_op jit(solution)/shard_map/ppermute | solution.py:32
  14.7 7.0 %collective-permute-start.1 = (bf16[256,256]{1,0:T(8,128)(2,1)S(1)}, bf16[256,256]{1,0:T(8,128)(2,1)S(1)}, u32[]{:S(2)}, u32[]{:S(2)}) collective-permute-start(bf16[256,256]{1,0:T(8,128)(2,1)S(1)} %collective-permute-done.refs_2_), channel_id=1, source_target_pairs={{0,4},{2,6},{4,0},{6,2},{8,12},{10,14},{12,8},{14,10},{1,5},{3,7},... | collective-permute-start | bytes 393224 | tf_op jit(solution)/shard_map/ppermute | solution.py:32
  17.8 0.7 %copy-start.3 = (s32[2,2]{1,0:T(2,128)S(1)}, s32[2,2]{1,0:T(2,128)}, u32[]{:S(2)}) copy-start(s32[2,2]{1,0:T(2,128)} %near_ref.11) | copy-start | bytes 52
  22.3 1.6 %copy-start.1 = (f32[256,256]{1,0:T(8,128)S(1)}, f32[256,256]{1,0:T(8,128)}, u32[]{:S(2)}) copy-start(f32[256,256]{1,0:T(8,128)} %tau.3) | copy-start | bytes 786436
  22.3 1.6 %collective-permute-start.7 = (bf16[2,256,256]{2,1,0:T(8,128)(2,1)S(1)}, bf16[2,256,256]{2,1,0:T(8,128)(2,1)S(1)}, u32[]{:S(2)}, u32[]{:S(2)}) collective-permute-start(bf16[2,256,256]{2,1,0:T(8,128)(2,1)S(1)} %shard_map.126), channel_id=1, source_target_pairs={{0,1},{1,0},{2,3},{3,2},{4,5},{5,4},{6,7},{7,6},{8,9},{9,8},{10,11... | collective-permute-start | bytes 786440 | tf_op jit(solution)/shard_map/ppermute | solution.py:373
  23.9 13.8 %copy-start.2 = (f32[256,256]{1,0:T(8,128)S(1)}, f32[256,256]{1,0:T(8,128)}, u32[]{:S(2)}) copy-start(f32[256,256]{1,0:T(8,128)} %state.1) | copy-start | bytes 786436
  24.8 9.4 %collective-permute-start.8 = (bf16[256,256]{1,0:T(8,128)(2,1)S(1)}, bf16[256,256]{1,0:T(8,128)(2,1)S(1)}, u32[]{:S(2)}, u32[]{:S(2)}) collective-permute-start(bf16[256,256]{1,0:T(8,128)(2,1)S(1)} %get-tuple-element.45.refs_0_), channel_id=1, source_target_pairs={{0,8},{2,10},{4,12},{6,14},{8,0},{10,2},{12,4},{14,6},{1,9},{3,11}... | collective-permute-start | bytes 393224 | tf_op jit(solution)/shard_map/ppermute | solution.py:32
  26.8 9.1 %collective-permute-start.14 = (bf16[256,256]{1,0:T(8,128)(2,1)S(1)}, bf16[256,256]{1,0:T(8,128)(2,1)S(1)}, u32[]{:S(2)}, u32[]{:S(2)}) collective-permute-start(bf16[256,256]{1,0:T(8,128)(2,1)S(1)} %get-tuple-element.45.refs_0_), channel_id=1, source_target_pairs={{0,6},{2,4},{4,2},{6,0},{8,14},{10,12},{12,10},{14,8},{1,7},{3,5},... | collective-permute-start | bytes 393224 | tf_op jit(solution)/shard_map/ppermute | solution.py:32
  28.5 9.7 %collective-permute-start.13 = (bf16[256,256]{1,0:T(8,128)(2,1)S(1)}, bf16[256,256]{1,0:T(8,128)(2,1)S(1)}, u32[]{:S(2)}, u32[]{:S(2)}) collective-permute-start(bf16[256,256]{1,0:T(8,128)(2,1)S(1)} %get-tuple-element.45.refs_0_), channel_id=1, source_target_pairs={{0,4},{2,6},{4,0},{6,2},{8,12},{10,14},{12,8},{14,10},{1,5},{3,7},... | collective-permute-start | bytes 393224 | tf_op jit(solution)/shard_map/ppermute | solution.py:32
  28.8 9.4 %collective-permute-start.12 = (bf16[256,256]{1,0:T(8,128)(2,1)S(1)}, bf16[256,256]{1,0:T(8,128)(2,1)S(1)}, u32[]{:S(2)}, u32[]{:S(2)}) collective-permute-start(bf16[256,256]{1,0:T(8,128)(2,1)S(1)} %get-tuple-element.45.refs_0_), channel_id=1, source_target_pairs={{0,2},{2,0},{4,6},{6,4},{8,10},{10,8},{12,14},{14,12},{1,3},{3,1},... | collective-permute-start | bytes 393224 | tf_op jit(solution)/shard_map/ppermute | solution.py:32
  34.2 7.4 %collective-permute-start.11 = (bf16[256,256]{1,0:T(8,128)(2,1)S(1)}, bf16[256,256]{1,0:T(8,128)(2,1)S(1)}, u32[]{:S(2)}, u32[]{:S(2)}) collective-permute-start(bf16[256,256]{1,0:T(8,128)(2,1)S(1)} %collective-permute-done.8.refs_2_), channel_id=1, source_target_pairs={{0,6},{2,4},{4,2},{6,0},{8,14},{10,12},{12,10},{14,8},{1,7},{3,5},... | collective-permute-start | bytes 393224 | tf_op jit(solution)/shard_map/ppermute | solution.py:32
  34.2 7.9 %collective-permute-start.10 = (bf16[256,256]{1,0:T(8,128)(2,1)S(1)}, bf16[256,256]{1,0:T(8,128)(2,1)S(1)}, u32[]{:S(2)}, u32[]{:S(2)}) collective-permute-start(bf16[256,256]{1,0:T(8,128)(2,1)S(1)} %collective-permute-done.8.refs_2_), channel_id=1, source_target_pairs={{0,2},{2,0},{4,6},{6,4},{8,10},{10,8},{12,14},{14,12},{1,3},{3,1},... | collective-permute-start | bytes 393224 | tf_op jit(solution)/shard_map/ppermute | solution.py:32
  35.9 6.8 %collective-permute-start.9 = (bf16[256,256]{1,0:T(8,128)(2,1)S(1)}, bf16[256,256]{1,0:T(8,128)(2,1)S(1)}, u32[]{:S(2)}, u32[]{:S(2)}) collective-permute-start(bf16[256,256]{1,0:T(8,128)(2,1)S(1)} %collective-permute-done.8.refs_2_), channel_id=1, source_target_pairs={{0,4},{2,6},{4,0},{6,2},{8,12},{10,14},{12,8},{14,10},{1,5},{3,7},... | collective-permute-start | bytes 393224 | tf_op jit(solution)/shard_map/ppermute | solution.py:32
  43.3 1.6 %collective-permute-start.15 = (bf16[2,256,256]{2,1,0:T(8,128)(2,1)S(1)}, bf16[2,256,256]{2,1,0:T(8,128)(2,1)S(1)}, u32[]{:S(2)}, u32[]{:S(2)}) collective-permute-start(bf16[2,256,256]{2,1,0:T(8,128)(2,1)S(1)} %shard_map.131), channel_id=1, source_target_pairs={{0,1},{1,0},{2,3},{3,2},{4,5},{5,4},{6,7},{7,6},{8,9},{9,8},{10,11... | collective-permute-start | bytes 786440 | tf_op jit(solution)/shard_map/ppermute | solution.py:373

commit v28 on v25

--- a/solution.py
+++ b/solution.py
@@ -41,7 +41,7 @@
 
 
 IN_PIECES = 8
-OUT_PIECES = 4
+OUT_PIECES = 2
 
 
 def row_pieces(size, pieces):

time: 46.8 us -> 46.8 us (level)
  no operation moved by 1% of the time
where the time goes in v28:
time: 46.8 us; the launch traced here: 46.6 us
  starting transfers between devices  19.8 us (42%)
  waiting for transfers between devices  15.9 us (34%)
  Pallas kernels  9.5 us (20%)
  between operations  0.77 us (2%)
  local copies, waits for them, and re-layouts  0.68 us (1%)
    ppermute x14, starting transfers between devices, swapped(): lax.ppermute(data, 'row', [(row, row ^ mask) for row in range(count)])  19.6 us
    ppermute x14, waiting for transfers between devices, swapped(): lax.ppermute(data, 'row', [(row, row ^ mask) for row in range(count)])  13.9 us
    pallas_call x11, Pallas kernels, on_core(): pl.pallas_call(kernel, out_shape=outs, in_specs=[hbm] * len(far) + [vmem]...  9.5 us
    ppermute x2, waiting for transfers between devices, lattice(): other = lax.ppermute(add(found[end], end, 1, sums, narrow), 'col', swap)  1.96 us
  transfers between devices with their start and end apart: 16, of which 13 were waited for; matrix products, arithmetic and copies ran while one was open for 0% of the time, Pallas kernels for 10%

profile of v28, /device:TPU:0, one launch (start us, length us, event | category | flops | bytes accessed | tf_op | source)
XLA Modules:
  0.0 46.6 jit_solution(17181006209723909453)
XLA Ops:
  0.6 0.0 copy-start
  0.6 1.0 %shard_map.123.refs_0_ = bf16[256,256]{1,0:T(8,128)(2,1)S(1)} custom-call(f32[256,256]{1,0:T(8,128)} %wide_ref.1), custom_call_target="tpu_custom_call" | custom-call | bytes 262144 | tf_op jit(solution)/shard_map/pallas_call | solution.py:268
  1.7 4.1 %collective-permute-start = (bf16[256,256]{1,0:T(8,128)(2,1)S(1)}, bf16[256,256]{1,0:T(8,128)(2,1)S(1)}, u32[]{:S(2)}, u32[]{:S(2)}) collective-permute-start(bf16[256,256]{1,0:T(8,128)(2,1)S(1)} %shard_map.123.refs_0_), channel_id=1, source_target_pairs={{0,8},{2,10},{4,12},{6,14},{8,0},{10,2},{12,4},{14,6},{1,9},{3,11}... | collective-permute-start | bytes 393224 | tf_op jit(solution)/shard_map/ppermute | solution.py:32
  5.8 2.5 %collective-permute-start.6 = (bf16[256,256]{1,0:T(8,128)(2,1)S(1)}, bf16[256,256]{1,0:T(8,128)(2,1)S(1)}, u32[]{:S(2)}, u32[]{:S(2)}) collective-permute-start(bf16[256,256]{1,0:T(8,128)(2,1)S(1)} %shard_map.123.refs_0_), channel_id=1, source_target_pairs={{0,6},{2,4},{4,2},{6,0},{8,14},{10,12},{12,10},{14,8},{1,7},{3,5},... | collective-permute-start | bytes 393224 | tf_op jit(solution)/shard_map/ppermute | solution.py:32
  8.3 0.4 collective-permute-start.5
  8.8 0.5 %collective-permute-start.4 = (bf16[256,256]{1,0:T(8,128)(2,1)S(1)}, bf16[256,256]{1,0:T(8,128)(2,1)S(1)}, u32[]{:S(2)}, u32[]{:S(2)}) collective-permute-start(bf16[256,256]{1,0:T(8,128)(2,1)S(1)} %shard_map.123.refs_0_), channel_id=1, source_target_pairs={{0,2},{2,0},{4,6},{6,4},{8,10},{10,8},{12,14},{14,12},{1,3},{3,1},... | collective-permute-start | bytes 393224 | tf_op jit(solution)/shard_map/ppermute | solution.py:32
  9.3 2.9 %collective-permute-done.refs_2_ = bf16[256,256]{1,0:T(8,128)(2,1)S(1)} collective-permute-done((bf16[256,256]{1,0:T(8,128)(2,1)S(1)}, bf16[256,256]{1,0:T(8,128)(2,1)S(1)}, u32[]{:S(2)}, u32[]{:S(2)}) %collective-permute-start) | collective-permute-done | bytes 131104 | tf_op jit(solution)/shard_map/ppermute | solution.py:32
  12.2 1.6 %collective-permute-start.3 = (bf16[256,256]{1,0:T(8,128)(2,1)S(1)}, bf16[256,256]{1,0:T(8,128)(2,1)S(1)}, u32[]{:S(2)}, u32[]{:S(2)}) collective-permute-start(bf16[256,256]{1,0:T(8,128)(2,1)S(1)} %collective-permute-done.refs_2_), channel_id=1, source_target_pairs={{0,6},{2,4},{4,2},{6,0},{8,14},{10,12},{12,10},{14,8},{1,7},{3,5},... | collective-permute-start | bytes 393224 | tf_op jit(solution)/shard_map/ppermute | solution.py:32
  13.8 0.5 %collective-permute-start.2 = (bf16[256,256]{1,0:T(8,128)(2,1)S(1)}, bf16[256,256]{1,0:T(8,128)(2,1)S(1)}, u32[]{:S(2)}, u32[]{:S(2)}) collective-permute-start(bf16[256,256]{1,0:T(8,128)(2,1)S(1)} %collective-permute-done.refs_2_), channel_id=1, source_target_pairs={{0,2},{2,0},{4,6},{6,4},{8,10},{10,8},{12,14},{14,12},{1,3},{3,1},... | collective-permute-start | bytes 393224 | tf_op jit(solution)/shard_map/ppermute | solution.py:32
  14.3 0.4 collective-permute-done.6.refs_4_
  14.7 1.2 %collective-permute-start.1 = (bf16[256,256]{1,0:T(8,128)(2,1)S(1)}, bf16[256,256]{1,0:T(8,128)(2,1)S(1)}, u32[]{:S(2)}, u32[]{:S(2)}) collective-permute-start(bf16[256,256]{1,0:T(8,128)(2,1)S(1)} %collective-permute-done.refs_2_), channel_id=1, source_target_pairs={{0,4},{2,6},{4,0},{6,2},{8,12},{10,14},{12,8},{14,10},{1,5},{3,7},... | collective-permute-start | bytes 393224 | tf_op jit(solution)/shard_map/ppermute | solution.py:32
  15.9 1.8 %shard_map.122 = (bf16[8,2,32,256]{3,2,1,0:T(8,128)(2,1)S(1)}, bf16[2,512,384]{2,1,0:T(8,128)(2,1)S(1)}, f32[5,256,128]{2,1,0:T(8,128)S(1)}, f32[256,256]{1,0:T(...) custom-call(s32[2,8]{1,0:T(2,128)} %refs_0_.1, bf16[2,8,32,256]{3,2,1,0:T(8,128)(2,1)} %refs_1_.1, ...), custom_call_target="tpu_custom_call" | custom-call | bytes 1051712 | tf_op jit(solution)/shard_map/pallas_call | solution.py:268
  17.7 0.0 collective-permute-done.5.refs_3_
  17.8 0.0 collective-permute-done.4.refs_1_
  17.8 0.0 copy-start.3
  17.8 0.0 copy-done
  17.8 0.7 %copy-done.3 = s32[2,2]{1,0:T(2,128)S(1)} copy-done((s32[2,2]{1,0:T(2,128)S(1)}, s32[2,2]{1,0:T(2,128)}, u32[]{:S(2)}) %copy-start.3) | copy-done | bytes 40
  18.4 0.9 %shard_map.124.refs_3_ = f32[2,2,256,256]{3,2,1,0:T(8,128)S(1)} custom-call(s32[2,2]{1,0:T(2,128)S(1)} %copy-done.3, bf16[8,2,32,256]{3,2,1,0:T(8,128)(2,1)S(1)} %get-tuple-element.27.v_ref, bf16[2,512,384]{2,1,0:T(8,128)(2,1)S(1)} %get-tuple-element.28.u_ref, bf16[2,2,2,256,256]{4,3,2,1,0:T(8,128)(2,1)S(1)} %copy-done, ...), custom_call_target="tpu_custom_call" | custom-call | flops 125829120 | bytes 2752528 | tf_op jit(solution)/shard_map/pallas_call | solution.py:268
  19.3 1.0 %collective-permute-done.3.refs_2_ = bf16[256,256]{1,0:T(8,128)(2,1)S(1)} collective-permute-done((bf16[256,256]{1,0:T(8,128)(2,1)S(1)}, bf16[256,256]{1,0:T(8,128)(2,1)S(1)}, u32[]{:S(2)}, u32[]{:S(2)}) %collective-permute-start.3) | collective-permute-done | bytes 131104 | tf_op jit(solution)/shard_map/ppermute | solution.py:32
  20.3 0.7 %collective-permute-done.2.refs_1_ = bf16[256,256]{1,0:T(8,128)(2,1)S(1)} collective-permute-done((bf16[256,256]{1,0:T(8,128)(2,1)S(1)}, bf16[256,256]{1,0:T(8,128)(2,1)S(1)}, u32[]{:S(2)}, u32[]{:S(2)}) %collective-permute-start.2) | collective-permute-done | bytes 131104 | tf_op jit(solution)/shard_map/ppermute | solution.py:32
  21.1 0.7 %collective-permute-done.1.refs_0_ = bf16[256,256]{1,0:T(8,128)(2,1)S(1)} collective-permute-done((bf16[256,256]{1,0:T(8,128)(2,1)S(1)}, bf16[256,256]{1,0:T(8,128)(2,1)S(1)}, u32[]{:S(2)}, u32[]{:S(2)}) %collective-permute-start.1) | collective-permute-done | bytes 131104 | tf_op jit(solution)/shard_map/ppermute | solution.py:32
  21.8 0.5 %shard_map.126 = bf16[2,256,256]{2,1,0:T(8,128)(2,1)S(1)} custom-call(s32[2,2]{1,0:T(2,128)S(1)} %copy-done.3, bf16[8,2,32,256]{3,2,1,0:T(8,128)(2,1)S(1)} %get-tuple-element.27.v_ref, bf16[2,512,384]{2,1,0:T(8,128)(2,1)S(1)} %get-tuple-element.28.u_ref, bf16[2,2,2,256,256]{4,3,2,1,0:T(8,128)(2,1)S(1)} %copy-done, ...), custom_call_target="tpu_custom_call" | custom-call | flops 37748736 | bytes 3538960 | tf_op jit(solution)/shard_map/pallas_call | solution.py:268
  22.3 0.0 copy-start.1
  22.3 0.1 collective-permute-start.7
  22.4 0.5 %shard_map.125.own = f32[2,256,256]{2,1,0:T(8,128)S(1)} custom-call(s32[2,2]{1,0:T(2,128)S(1)} %copy-done.3, bf16[8,2,32,256]{3,2,1,0:T(8,128)(2,1)S(1)} %get-tuple-element.27.v_ref, bf16[2,512,384]{2,1,0:T(8,128)(2,1)S(1)} %get-tuple-element.28.u_ref, bf16[2,2,2,256,256]{4,3,2,1,0:T(8,128)(2,1)S(1)} %copy-done, ...), custom_call_target="tpu_custom_call" | custom-call | flops 37748736 | bytes 3538960 | tf_op jit(solution)/shard_map/pallas_call | solution.py:268
  22.9 1.0 %collective-permute-done.7.other = bf16[2,256,256]{2,1,0:T(8,128)(2,1)S(1)} collective-permute-done((bf16[2,256,256]{2,1,0:T(8,128)(2,1)S(1)}, bf16[2,256,256]{2,1,0:T(8,128)(2,1)S(1)}, u32[]{:S(2)}, u32[]{:S(2)}) %collective-permute-start.7) | collective-permute-done | bytes 262176 | tf_op jit(solution)/shard_map/ppermute | solution.py:368
  23.9 0.9 %shard_map.127 = (f32[256,256]{1,0:T(8,128)S(1)}, bf16[256,256]{1,0:T(8,128)(2,1)S(1)}) custom-call(f32[2,256,256]{2,1,0:T(8,128)S(1)} %shard_map.125.own, bf16[2,256,256]{2,1,0:T(8,128)(2,1)S(1)} %collective-permute-done.7.other, f32[256,256]{1,0:T(8,128)S(1)} %get-tuple-element.33.weight, f32[256,256]{1,0:T(8,128)S(1)} %get-tuple-element.34.unweight, ...), custom_call_target="tpu_custom_call" | custom-call | flops 13107200 | bytes 2228224 | tf_op jit(solution)/shard_map/pallas_call | solution.py:268
  24.8 2.0 %collective-permute-start.8 = (bf16[256,256]{1,0:T(8,128)(2,1)S(1)}, bf16[256,256]{1,0:T(8,128)(2,1)S(1)}, u32[]{:S(2)}, u32[]{:S(2)}) collective-permute-start(bf16[256,256]{1,0:T(8,128)(2,1)S(1)} %get-tuple-element.45.refs_0_), channel_id=1, source_target_pairs={{0,8},{2,10},{4,12},{6,14},{8,0},{10,2},{12,4},{14,6},{1,9},{3,11}... | collective-permute-start | bytes 393224 | tf_op jit(solution)/shard_map/ppermute | solution.py:32
  26.8 1.7 %collective-permute-start.14 = (bf16[256,256]{1,0:T(8,128)(2,1)S(1)}, bf16[256,256]{1,0:T(8,128)(2,1)S(1)}, u32[]{:S(2)}, u32[]{:S(2)}) collective-permute-start(bf16[256,256]{1,0:T(8,128)(2,1)S(1)} %get-tuple-element.45.refs_0_), channel_id=1, source_target_pairs={{0,6},{2,4},{4,2},{6,0},{8,14},{10,12},{12,10},{14,8},{1,7},{3,5},... | collective-permute-start | bytes 393224 | tf_op jit(solution)/shard_map/ppermute | solution.py:32
  28.5 0.3 collective-permute-start.13
  28.8 1.5 %collective-permute-start.12 = (bf16[256,256]{1,0:T(8,128)(2,1)S(1)}, bf16[256,256]{1,0:T(8,128)(2,1)S(1)}, u32[]{:S(2)}, u32[]{:S(2)}) collective-permute-start(bf16[256,256]{1,0:T(8,128)(2,1)S(1)} %get-tuple-element.45.refs_0_), channel_id=1, source_target_pairs={{0,2},{2,0},{4,6},{6,4},{8,10},{10,8},{12,14},{14,12},{1,3},{3,1},... | collective-permute-start | bytes 393224 | tf_op jit(solution)/shard_map/ppermute | solution.py:32
  30.3 3.9 %collective-permute-done.8.refs_2_ = bf16[256,256]{1,0:T(8,128)(2,1)S(1)} collective-permute-done((bf16[256,256]{1,0:T(8,128)(2,1)S(1)}, bf16[256,256]{1,0:T(8,128)(2,1)S(1)}, u32[]{:S(2)}, u32[]{:S(2)}) %collective-permute-start.8) | collective-permute-done | bytes 131104 | tf_op jit(solution)/shard_map/ppermute | solution.py:32
  34.2 0.0 collective-permute-start.11
  34.2 1.4 %collective-permute-start.10 = (bf16[256,256]{1,0:T(8,128)(2,1)S(1)}, bf16[256,256]{1,0:T(8,128)(2,1)S(1)}, u32[]{:S(2)}, u32[]{:S(2)}) collective-permute-start(bf16[256,256]{1,0:T(8,128)(2,1)S(1)} %collective-permute-done.8.refs_2_), channel_id=1, source_target_pairs={{0,2},{2,0},{4,6},{6,4},{8,10},{10,8},{12,14},{14,12},{1,3},{3,1},... | collective-permute-start | bytes 393224 | tf_op jit(solution)/shard_map/ppermute | solution.py:32
  35.6 0.3 collective-permute-done.14.refs_4_
  35.9 1.8 %collective-permute-start.9 = (bf16[256,256]{1,0:T(8,128)(2,1)S(1)}, bf16[256,256]{1,0:T(8,128)(2,1)S(1)}, u32[]{:S(2)}, u32[]{:S(2)}) collective-permute-start(bf16[256,256]{1,0:T(8,128)(2,1)S(1)} %collective-permute-done.8.refs_2_), channel_id=1, source_target_pairs={{0,4},{2,6},{4,0},{6,2},{8,12},{10,14},{12,8},{14,10},{1,5},{3,7},... | collective-permute-start | bytes 393224 | tf_op jit(solution)/shard_map/ppermute | solution.py:32
  37.7 0.2 shard_map.128
  38.0 0.2 collective-permute-done.13.refs_3_
  38.2 0.0 collective-permute-done.12.refs_1_
  38.2 0.8 %shard_map.129.refs_3_ = f32[2,2,256,256]{3,2,1,0:T(8,128)S(1)} custom-call(s32[2,2]{1,0:T(2,128)S(1)} %copy-done.3, bf16[8,2,32,256]{3,2,1,0:T(8,128)(2,1)S(1)} %get-tuple-element.27.v_ref, bf16[2,512,384]{2,1,0:T(8,128)(2,1)S(1)} %get-tuple-element.28.u_ref, bf16[2,2,2,256,256]{4,3,2,1,0:T(8,128)(2,1)S(1)} %copy-done, ...), custom_call_target="tpu_custom_call" | custom-call | flops 125829120 | bytes 2752528 | tf_op jit(solution)/shard_map/pallas_call | solution.py:268
  39.0 2.6 %collective-permute-done.11.refs_2_ = bf16[256,256]{1,0:T(8,128)(2,1)S(1)} collective-permute-done((bf16[256,256]{1,0:T(8,128)(2,1)S(1)}, bf16[256,256]{1,0:T(8,128)(2,1)S(1)}, u32[]{:S(2)}, u32[]{:S(2)}) %collective-permute-start.11) | collective-permute-done | bytes 131104 | tf_op jit(solution)/shard_map/ppermute | solution.py:32
  41.6 0.5 %collective-permute-done.10.refs_1_ = bf16[256,256]{1,0:T(8,128)(2,1)S(1)} collective-permute-done((bf16[256,256]{1,0:T(8,128)(2,1)S(1)}, bf16[256,256]{1,0:T(8,128)(2,1)S(1)}, u32[]{:S(2)}, u32[]{:S(2)}) %collective-permute-start.10) | collective-permute-done | bytes 131104 | tf_op jit(solution)/shard_map/ppermute | solution.py:32
  42.1 0.6 %collective-permute-done.9.refs_0_ = bf16[256,256]{1,0:T(8,128)(2,1)S(1)} collective-permute-done((bf16[256,256]{1,0:T(8,128)(2,1)S(1)}, bf16[256,256]{1,0:T(8,128)(2,1)S(1)}, u32[]{:S(2)}, u32[]{:S(2)}) %collective-permute-start.9) | collective-permute-done | bytes 131104 | tf_op jit(solution)/shard_map/ppermute | solution.py:32
  42.7 0.5 %shard_map.131 = bf16[2,256,256]{2,1,0:T(8,128)(2,1)S(1)} custom-call(s32[2,2]{1,0:T(2,128)S(1)} %copy-done.3, bf16[8,2,32,256]{3,2,1,0:T(8,128)(2,1)S(1)} %get-tuple-element.27.v_ref, bf16[2,512,384]{2,1,0:T(8,128)(2,1)S(1)} %get-tuple-element.28.u_ref, bf16[2,2,2,256,256]{4,3,2,1,0:T(8,128)(2,1)S(1)} %copy-done, ...), custom_call_target="tpu_custom_call" | custom-call | flops 37748736 | bytes 3538960 | tf_op jit(solution)/shard_map/pallas_call | solution.py:268
  43.3 0.1 collective-permute-start.15
  43.4 0.5 %shard_map.130.own = f32[2,256,256]{2,1,0:T(8,128)S(1)} custom-call(s32[2,2]{1,0:T(2,128)S(1)} %copy-done.3, bf16[8,2,32,256]{3,2,1,0:T(8,128)(2,1)S(1)} %get-tuple-element.27.v_ref, bf16[2,512,384]{2,1,0:T(8,128)(2,1)S(1)} %get-tuple-element.28.u_ref, bf16[2,2,2,256,256]{4,3,2,1,0:T(8,128)(2,1)S(1)} %copy-done, ...), custom_call_target="tpu_custom_call" | custom-call | flops 37748736 | bytes 3538960 | tf_op jit(solution)/shard_map/pallas_call | solution.py:268
  43.9 1.0 %collective-permute-done.15.other = bf16[2,256,256]{2,1,0:T(8,128)(2,1)S(1)} collective-permute-done((bf16[2,256,256]{2,1,0:T(8,128)(2,1)S(1)}, bf16[2,256,256]{2,1,0:T(8,128)(2,1)S(1)}, u32[]{:S(2)}, u32[]{:S(2)}) %collective-permute-start.15) | collective-permute-done | bytes 262176 | tf_op jit(solution)/shard_map/ppermute | solution.py:368
  44.9 1.7 %shard_map.132 = (f32[256,256]{1,0:T(8,128)}, f32[256,256]{1,0:T(8,128)}) custom-call(f32[2,256,256]{2,1,0:T(8,128)S(1)} %shard_map.130.own, bf16[2,256,256]{2,1,0:T(8,128)(2,1)S(1)} %collective-permute-done.15.other, f32[256,256]{1,0:T(8,128)S(1)} %get-tuple-element.46.weight, f32[256,256]{1,0:T(8,128)S(1)} %get-tuple-element.47.unweight, ...), custom_call_target="tpu_custom_call" | custom-call | flops 13107200 | bytes 3538944 | tf_op jit(solution)/shard_map/pallas_call | solution.py:268
  (3 shorter events, 0.0 us)
Async XLA Ops:
  0.6 17.2 %copy-start = (bf16[2,2,2,256,256]{4,3,2,1,0:T(8,128)(2,1)S(1)}, bf16[2,2,2,256,256]{4,3,2,1,0:T(8,128)(2,1)}, u32[]{:S(2)}) copy-start(bf16[2,2,2,256,256]{4,3,2,1,0:T(8,128)(2,1)} %d_ref.11) | copy-start | bytes 3145732
  1.7 10.5 %collective-permute-start = (bf16[256,256]{1,0:T(8,128)(2,1)S(1)}, bf16[256,256]{1,0:T(8,128)(2,1)S(1)}, u32[]{:S(2)}, u32[]{:S(2)}) collective-permute-start(bf16[256,256]{1,0:T(8,128)(2,1)S(1)} %shard_map.123.refs_0_), channel_id=1, source_target_pairs={{0,8},{2,10},{4,12},{6,14},{8,0},{10,2},{12,4},{14,6},{1,9},{3,11}... | collective-permute-start | bytes 393224 | tf_op jit(solution)/shard_map/ppermute | solution.py:32
  5.8 9.0 %collective-permute-start.6 = (bf16[256,256]{1,0:T(8,128)(2,1)S(1)}, bf16[256,256]{1,0:T(8,128)(2,1)S(1)}, u32[]{:S(2)}, u32[]{:S(2)}) collective-permute-start(bf16[256,256]{1,0:T(8,128)(2,1)S(1)} %shard_map.123.refs_0_), channel_id=1, source_target_pairs={{0,6},{2,4},{4,2},{6,0},{8,14},{10,12},{12,10},{14,8},{1,7},{3,5},... | collective-permute-start | bytes 393224 | tf_op jit(solution)/shard_map/ppermute | solution.py:32
  8.3 9.4 %collective-permute-start.5 = (bf16[256,256]{1,0:T(8,128)(2,1)S(1)}, bf16[256,256]{1,0:T(8,128)(2,1)S(1)}, u32[]{:S(2)}, u32[]{:S(2)}) collective-permute-start(bf16[256,256]{1,0:T(8,128)(2,1)S(1)} %shard_map.123.refs_0_), channel_id=1, source_target_pairs={{0,4},{2,6},{4,0},{6,2},{8,12},{10,14},{12,8},{14,10},{1,5},{3,7},... | collective-permute-start | bytes 393224 | tf_op jit(solution)/shard_map/ppermute | solution.py:32
  8.8 9.0 %collective-permute-start.4 = (bf16[256,256]{1,0:T(8,128)(2,1)S(1)}, bf16[256,256]{1,0:T(8,128)(2,1)S(1)}, u32[]{:S(2)}, u32[]{:S(2)}) collective-permute-start(bf16[256,256]{1,0:T(8,128)(2,1)S(1)} %shard_map.123.refs_0_), channel_id=1, source_target_pairs={{0,2},{2,0},{4,6},{6,4},{8,10},{10,8},{12,14},{14,12},{1,3},{3,1},... | collective-permute-start | bytes 393224 | tf_op jit(solution)/shard_map/ppermute | solution.py:32
  12.2 8.2 %collective-permute-start.3 = (bf16[256,256]{1,0:T(8,128)(2,1)S(1)}, bf16[256,256]{1,0:T(8,128)(2,1)S(1)}, u32[]{:S(2)}, u32[]{:S(2)}) collective-permute-start(bf16[256,256]{1,0:T(8,128)(2,1)S(1)} %collective-permute-done.refs_2_), channel_id=1, source_target_pairs={{0,6},{2,4},{4,2},{6,0},{8,14},{10,12},{12,10},{14,8},{1,7},{3,5},... | collective-permute-start | bytes 393224 | tf_op jit(solution)/shard_map/ppermute | solution.py:32
  13.8 7.2 %collective-permute-start.2 = (bf16[256,256]{1,0:T(8,128)(2,1)S(1)}, bf16[256,256]{1,0:T(8,128)(2,1)S(1)}, u32[]{:S(2)}, u32[]{:S(2)}) collective-permute-start(bf16[256,256]{1,0:T(8,128)(2,1)S(1)} %collective-permute-done.refs_2_), channel_id=1, source_target_pairs={{0,2},{2,0},{4,6},{6,4},{8,10},{10,8},{12,14},{14,12},{1,3},{3,1},... | collective-permute-start | bytes 393224 | tf_op jit(solution)/shard_map/ppermute | solution.py:32
  14.7 7.0 %collective-permute-start.1 = (bf16[256,256]{1,0:T(8,128)(2,1)S(1)}, bf16[256,256]{1,0:T(8,128)(2,1)S(1)}, u32[]{:S(2)}, u32[]{:S(2)}) collective-permute-start(bf16[256,256]{1,0:T(8,128)(2,1)S(1)} %collective-permute-done.refs_2_), channel_id=1, source_target_pairs={{0,4},{2,6},{4,0},{6,2},{8,12},{10,14},{12,8},{14,10},{1,5},{3,7},... | collective-permute-start | bytes 393224 | tf_op jit(solution)/shard_map/ppermute | solution.py:32
  17.8 0.7 %copy-start.3 = (s32[2,2]{1,0:T(2,128)S(1)}, s32[2,2]{1,0:T(2,128)}, u32[]{:S(2)}) copy-start(s32[2,2]{1,0:T(2,128)} %near_ref.11) | copy-start | bytes 52
  22.3 1.6 %copy-start.1 = (f32[256,256]{1,0:T(8,128)S(1)}, f32[256,256]{1,0:T(8,128)}, u32[]{:S(2)}) copy-start(f32[256,256]{1,0:T(8,128)} %tau.3) | copy-start | bytes 786436
  22.3 1.6 %collective-permute-start.7 = (bf16[2,256,256]{2,1,0:T(8,128)(2,1)S(1)}, bf16[2,256,256]{2,1,0:T(8,128)(2,1)S(1)}, u32[]{:S(2)}, u32[]{:S(2)}) collective-permute-start(bf16[2,256,256]{2,1,0:T(8,128)(2,1)S(1)} %shard_map.126), channel_id=1, source_target_pairs={{0,1},{1,0},{2,3},{3,2},{4,5},{5,4},{6,7},{7,6},{8,9},{9,8},{10,11... | collective-permute-start | bytes 786440 | tf_op jit(solution)/shard_map/ppermute | solution.py:368
  23.9 13.8 %copy-start.2 = (f32[256,256]{1,0:T(8,128)S(1)}, f32[256,256]{1,0:T(8,128)}, u32[]{:S(2)}) copy-start(f32[256,256]{1,0:T(8,128)} %state.1) | copy-start | bytes 786436
  24.8 9.4 %collective-permute-start.8 = (bf16[256,256]{1,0:T(8,128)(2,1)S(1)}, bf16[256,256]{1,0:T(8,128)(2,1)S(1)}, u32[]{:S(2)}, u32[]{:S(2)}) collective-permute-start(bf16[256,256]{1,0:T(8,128)(2,1)S(1)} %get-tuple-element.45.refs_0_), channel_id=1, source_target_pairs={{0,8},{2,10},{4,12},{6,14},{8,0},{10,2},{12,4},{14,6},{1,9},{3,11}... | collective-permute-start | bytes 393224 | tf_op jit(solution)/shard_map/ppermute | solution.py:32
  26.8 9.1 %collective-permute-start.14 = (bf16[256,256]{1,0:T(8,128)(2,1)S(1)}, bf16[256,256]{1,0:T(8,128)(2,1)S(1)}, u32[]{:S(2)}, u32[]{:S(2)}) collective-permute-start(bf16[256,256]{1,0:T(8,128)(2,1)S(1)} %get-tuple-element.45.refs_0_), channel_id=1, source_target_pairs={{0,6},{2,4},{4,2},{6,0},{8,14},{10,12},{12,10},{14,8},{1,7},{3,5},... | collective-permute-start | bytes 393224 | tf_op jit(solution)/shard_map/ppermute | solution.py:32
  28.5 9.7 %collective-permute-start.13 = (bf16[256,256]{1,0:T(8,128)(2,1)S(1)}, bf16[256,256]{1,0:T(8,128)(2,1)S(1)}, u32[]{:S(2)}, u32[]{:S(2)}) collective-permute-start(bf16[256,256]{1,0:T(8,128)(2,1)S(1)} %get-tuple-element.45.refs_0_), channel_id=1, source_target_pairs={{0,4},{2,6},{4,0},{6,2},{8,12},{10,14},{12,8},{14,10},{1,5},{3,7},... | collective-permute-start | bytes 393224 | tf_op jit(solution)/shard_map/ppermute | solution.py:32
  28.8 9.4 %collective-permute-start.12 = (bf16[256,256]{1,0:T(8,128)(2,1)S(1)}, bf16[256,256]{1,0:T(8,128)(2,1)S(1)}, u32[]{:S(2)}, u32[]{:S(2)}) collective-permute-start(bf16[256,256]{1,0:T(8,128)(2,1)S(1)} %get-tuple-element.45.refs_0_), channel_id=1, source_target_pairs={{0,2},{2,0},{4,6},{6,4},{8,10},{10,8},{12,14},{14,12},{1,3},{3,1},... | collective-permute-start | bytes 393224 | tf_op jit(solution)/shard_map/ppermute | solution.py:32
  34.2 7.4 %collective-permute-start.11 = (bf16[256,256]{1,0:T(8,128)(2,1)S(1)}, bf16[256,256]{1,0:T(8,128)(2,1)S(1)}, u32[]{:S(2)}, u32[]{:S(2)}) collective-permute-start(bf16[256,256]{1,0:T(8,128)(2,1)S(1)} %collective-permute-done.8.refs_2_), channel_id=1, source_target_pairs={{0,6},{2,4},{4,2},{6,0},{8,14},{10,12},{12,10},{14,8},{1,7},{3,5},... | collective-permute-start | bytes 393224 | tf_op jit(solution)/shard_map/ppermute | solution.py:32
  34.2 7.9 %collective-permute-start.10 = (bf16[256,256]{1,0:T(8,128)(2,1)S(1)}, bf16[256,256]{1,0:T(8,128)(2,1)S(1)}, u32[]{:S(2)}, u32[]{:S(2)}) collective-permute-start(bf16[256,256]{1,0:T(8,128)(2,1)S(1)} %collective-permute-done.8.refs_2_), channel_id=1, source_target_pairs={{0,2},{2,0},{4,6},{6,4},{8,10},{10,8},{12,14},{14,12},{1,3},{3,1},... | collective-permute-start | bytes 393224 | tf_op jit(solution)/shard_map/ppermute | solution.py:32
  35.9 6.8 %collective-permute-start.9 = (bf16[256,256]{1,0:T(8,128)(2,1)S(1)}, bf16[256,256]{1,0:T(8,128)(2,1)S(1)}, u32[]{:S(2)}, u32[]{:S(2)}) collective-permute-start(bf16[256,256]{1,0:T(8,128)(2,1)S(1)} %collective-permute-done.8.refs_2_), channel_id=1, source_target_pairs={{0,4},{2,6},{4,0},{6,2},{8,12},{10,14},{12,8},{14,10},{1,5},{3,7},... | collective-permute-start | bytes 393224 | tf_op jit(solution)/shard_map/ppermute | solution.py:32
  43.3 1.6 %collective-permute-start.15 = (bf16[2,256,256]{2,1,0:T(8,128)(2,1)S(1)}, bf16[2,256,256]{2,1,0:T(8,128)(2,1)S(1)}, u32[]{:S(2)}, u32[]{:S(2)}) collective-permute-start(bf16[2,256,256]{2,1,0:T(8,128)(2,1)S(1)} %shard_map.131), channel_id=1, source_target_pairs={{0,1},{1,0},{2,3},{3,2},{4,5},{5,4},{6,7},{7,6},{8,9},{9,8},{10,11... | collective-permute-start | bytes 786440 | tf_op jit(solution)/shard_map/ppermute | solution.py:368

commit v29 on v25

--- a/solution.py
+++ b/solution.py
@@ -206,7 +206,7 @@
 
 
 def over_pieces(begin, tall, members, lanes, work):
-    step = min(tall, 64)
+    step = min(tall, 128)
     for at in range(begin, begin + tall, step):
         for first in range(0, members, lanes):
             work(pl.ds(at, step), slice(first, first + lanes))

time: 46.8 us -> 46.8 us (level)
  no operation moved by 1% of the time
where the time goes in v29:
time: 46.8 us; the launch traced here: 46.6 us
  starting transfers between devices  19.8 us (42%)
  waiting for transfers between devices  15.9 us (34%)
  Pallas kernels  9.5 us (20%)
  between operations  0.77 us (2%)
  local copies, waits for them, and re-layouts  0.68 us (1%)
    ppermute x14, starting transfers between devices, swapped(): lax.ppermute(data, 'row', [(row, row ^ mask) for row in range(count)])  19.6 us
    ppermute x14, waiting for transfers between devices, swapped(): lax.ppermute(data, 'row', [(row, row ^ mask) for row in range(count)])  13.9 us
    pallas_call x11, Pallas kernels, on_core(): pl.pallas_call(kernel, out_shape=outs, in_specs=[hbm] * len(far) + [vmem]...  9.5 us
    ppermute x2, waiting for transfers between devices, lattice(): other = lax.ppermute(add(found[end], end, 1, sums, narrow), 'col', swap)  1.96 us
  transfers between devices with their start and end apart: 16, of which 13 were waited for; matrix products, arithmetic and copies ran while one was open for 0% of the time, Pallas kernels for 10%

profile of v29, /device:TPU:0, one launch (start us, length us, event | category | flops | bytes accessed | tf_op | source)
XLA Modules:
  0.0 46.6 jit_solution(14426987809598293315)
XLA Ops:
  0.6 0.0 copy-start
  0.6 1.0 %shard_map.123.refs_0_ = bf16[256,256]{1,0:T(8,128)(2,1)S(1)} custom-call(f32[256,256]{1,0:T(8,128)} %wide_ref.1), custom_call_target="tpu_custom_call" | custom-call | bytes 262144 | tf_op jit(solution)/shard_map/pallas_call | solution.py:268
  1.7 4.1 %collective-permute-start = (bf16[256,256]{1,0:T(8,128)(2,1)S(1)}, bf16[256,256]{1,0:T(8,128)(2,1)S(1)}, u32[]{:S(2)}, u32[]{:S(2)}) collective-permute-start(bf16[256,256]{1,0:T(8,128)(2,1)S(1)} %shard_map.123.refs_0_), channel_id=1, source_target_pairs={{0,8},{2,10},{4,12},{6,14},{8,0},{10,2},{12,4},{14,6},{1,9},{3,11}... | collective-permute-start | bytes 393224 | tf_op jit(solution)/shard_map/ppermute | solution.py:32
  5.8 2.5 %collective-permute-start.6 = (bf16[256,256]{1,0:T(8,128)(2,1)S(1)}, bf16[256,256]{1,0:T(8,128)(2,1)S(1)}, u32[]{:S(2)}, u32[]{:S(2)}) collective-permute-start(bf16[256,256]{1,0:T(8,128)(2,1)S(1)} %shard_map.123.refs_0_), channel_id=1, source_target_pairs={{0,6},{2,4},{4,2},{6,0},{8,14},{10,12},{12,10},{14,8},{1,7},{3,5},... | collective-permute-start | bytes 393224 | tf_op jit(solution)/shard_map/ppermute | solution.py:32
  8.3 0.4 collective-permute-start.5
  8.8 0.5 %collective-permute-start.4 = (bf16[256,256]{1,0:T(8,128)(2,1)S(1)}, bf16[256,256]{1,0:T(8,128)(2,1)S(1)}, u32[]{:S(2)}, u32[]{:S(2)}) collective-permute-start(bf16[256,256]{1,0:T(8,128)(2,1)S(1)} %shard_map.123.refs_0_), channel_id=1, source_target_pairs={{0,2},{2,0},{4,6},{6,4},{8,10},{10,8},{12,14},{14,12},{1,3},{3,1},... | collective-permute-start | bytes 393224 | tf_op jit(solution)/shard_map/ppermute | solution.py:32
  9.3 2.9 %collective-permute-done.refs_2_ = bf16[256,256]{1,0:T(8,128)(2,1)S(1)} collective-permute-done((bf16[256,256]{1,0:T(8,128)(2,1)S(1)}, bf16[256,256]{1,0:T(8,128)(2,1)S(1)}, u32[]{:S(2)}, u32[]{:S(2)}) %collective-permute-start) | collective-permute-done | bytes 131104 | tf_op jit(solution)/shard_map/ppermute | solution.py:32
  12.2 1.6 %collective-permute-start.3 = (bf16[256,256]{1,0:T(8,128)(2,1)S(1)}, bf16[256,256]{1,0:T(8,128)(2,1)S(1)}, u32[]{:S(2)}, u32[]{:S(2)}) collective-permute-start(bf16[256,256]{1,0:T(8,128)(2,1)S(1)} %collective-permute-done.refs_2_), channel_id=1, source_target_pairs={{0,6},{2,4},{4,2},{6,0},{8,14},{10,12},{12,10},{14,8},{1,7},{3,5},... | collective-permute-start | bytes 393224 | tf_op jit(solution)/shard_map/ppermute | solution.py:32
  13.8 0.5 %collective-permute-start.2 = (bf16[256,256]{1,0:T(8,128)(2,1)S(1)}, bf16[256,256]{1,0:T(8,128)(2,1)S(1)}, u32[]{:S(2)}, u32[]{:S(2)}) collective-permute-start(bf16[256,256]{1,0:T(8,128)(2,1)S(1)} %collective-permute-done.refs_2_), channel_id=1, source_target_pairs={{0,2},{2,0},{4,6},{6,4},{8,10},{10,8},{12,14},{14,12},{1,3},{3,1},... | collective-permute-start | bytes 393224 | tf_op jit(solution)/shard_map/ppermute | solution.py:32
  14.3 0.4 collective-permute-done.6.refs_4_
  14.7 1.2 %collective-permute-start.1 = (bf16[256,256]{1,0:T(8,128)(2,1)S(1)}, bf16[256,256]{1,0:T(8,128)(2,1)S(1)}, u32[]{:S(2)}, u32[]{:S(2)}) collective-permute-start(bf16[256,256]{1,0:T(8,128)(2,1)S(1)} %collective-permute-done.refs_2_), channel_id=1, source_target_pairs={{0,4},{2,6},{4,0},{6,2},{8,12},{10,14},{12,8},{14,10},{1,5},{3,7},... | collective-permute-start | bytes 393224 | tf_op jit(solution)/shard_map/ppermute | solution.py:32
  15.9 1.8 %shard_map.122 = (bf16[8,2,32,256]{3,2,1,0:T(8,128)(2,1)S(1)}, bf16[2,512,384]{2,1,0:T(8,128)(2,1)S(1)}, f32[5,256,128]{2,1,0:T(8,128)S(1)}, f32[256,256]{1,0:T(...) custom-call(s32[2,8]{1,0:T(2,128)} %refs_0_.1, bf16[2,8,32,256]{3,2,1,0:T(8,128)(2,1)} %refs_1_.1, ...), custom_call_target="tpu_custom_call" | custom-call | bytes 1051712 | tf_op jit(solution)/shard_map/pallas_call | solution.py:268
  17.7 0.0 collective-permute-done.5.refs_3_
  17.8 0.0 collective-permute-done.4.refs_1_
  17.8 0.0 copy-start.3
  17.8 0.7 %copy-done.3 = s32[2,2]{1,0:T(2,128)S(1)} copy-done((s32[2,2]{1,0:T(2,128)S(1)}, s32[2,2]{1,0:T(2,128)}, u32[]{:S(2)}) %copy-start.3) | copy-done | bytes 40
  18.4 0.9 %shard_map.124.refs_3_ = f32[2,2,256,256]{3,2,1,0:T(8,128)S(1)} custom-call(s32[2,2]{1,0:T(2,128)S(1)} %copy-done.3, bf16[8,2,32,256]{3,2,1,0:T(8,128)(2,1)S(1)} %get-tuple-element.27.v_ref, bf16[2,512,384]{2,1,0:T(8,128)(2,1)S(1)} %get-tuple-element.28.u_ref, bf16[2,2,2,256,256]{4,3,2,1,0:T(8,128)(2,1)S(1)} %copy-done, ...), custom_call_target="tpu_custom_call" | custom-call | flops 125829120 | bytes 2752528 | tf_op jit(solution)/shard_map/pallas_call | solution.py:268
  19.3 1.0 %collective-permute-done.3.refs_2_ = bf16[256,256]{1,0:T(8,128)(2,1)S(1)} collective-permute-done((bf16[256,256]{1,0:T(8,128)(2,1)S(1)}, bf16[256,256]{1,0:T(8,128)(2,1)S(1)}, u32[]{:S(2)}, u32[]{:S(2)}) %collective-permute-start.3) | collective-permute-done | bytes 131104 | tf_op jit(solution)/shard_map/ppermute | solution.py:32
  20.3 0.7 %collective-permute-done.2.refs_1_ = bf16[256,256]{1,0:T(8,128)(2,1)S(1)} collective-permute-done((bf16[256,256]{1,0:T(8,128)(2,1)S(1)}, bf16[256,256]{1,0:T(8,128)(2,1)S(1)}, u32[]{:S(2)}, u32[]{:S(2)}) %collective-permute-start.2) | collective-permute-done | bytes 131104 | tf_op jit(solution)/shard_map/ppermute | solution.py:32
  21.1 0.7 %collective-permute-done.1.refs_0_ = bf16[256,256]{1,0:T(8,128)(2,1)S(1)} collective-permute-done((bf16[256,256]{1,0:T(8,128)(2,1)S(1)}, bf16[256,256]{1,0:T(8,128)(2,1)S(1)}, u32[]{:S(2)}, u32[]{:S(2)}) %collective-permute-start.1) | collective-permute-done | bytes 131104 | tf_op jit(solution)/shard_map/ppermute | solution.py:32
  21.8 0.5 %shard_map.126 = bf16[2,256,256]{2,1,0:T(8,128)(2,1)S(1)} custom-call(s32[2,2]{1,0:T(2,128)S(1)} %copy-done.3, bf16[8,2,32,256]{3,2,1,0:T(8,128)(2,1)S(1)} %get-tuple-element.27.v_ref, bf16[2,512,384]{2,1,0:T(8,128)(2,1)S(1)} %get-tuple-element.28.u_ref, bf16[2,2,2,256,256]{4,3,2,1,0:T(8,128)(2,1)S(1)} %copy-done, ...), custom_call_target="tpu_custom_call" | custom-call | flops 37748736 | bytes 3538960 | tf_op jit(solution)/shard_map/pallas_call | solution.py:268
  22.3 0.0 copy-start.1
  22.3 0.1 collective-permute-start.7
  22.4 0.5 %shard_map.125.own = f32[2,256,256]{2,1,0:T(8,128)S(1)} custom-call(s32[2,2]{1,0:T(2,128)S(1)} %copy-done.3, bf16[8,2,32,256]{3,2,1,0:T(8,128)(2,1)S(1)} %get-tuple-element.27.v_ref, bf16[2,512,384]{2,1,0:T(8,128)(2,1)S(1)} %get-tuple-element.28.u_ref, bf16[2,2,2,256,256]{4,3,2,1,0:T(8,128)(2,1)S(1)} %copy-done, ...), custom_call_target="tpu_custom_call" | custom-call | flops 37748736 | bytes 3538960 | tf_op jit(solution)/shard_map/pallas_call | solution.py:268
  22.9 1.0 %collective-permute-done.7.other = bf16[2,256,256]{2,1,0:T(8,128)(2,1)S(1)} collective-permute-done((bf16[2,256,256]{2,1,0:T(8,128)(2,1)S(1)}, bf16[2,256,256]{2,1,0:T(8,128)(2,1)S(1)}, u32[]{:S(2)}, u32[]{:S(2)}) %collective-permute-start.7) | collective-permute-done | bytes 262176 | tf_op jit(solution)/shard_map/ppermute | solution.py:368
  23.9 0.0 copy-done.1
  23.9 0.9 %shard_map.127 = (f32[256,256]{1,0:T(8,128)S(1)}, bf16[256,256]{1,0:T(8,128)(2,1)S(1)}) custom-call(f32[2,256,256]{2,1,0:T(8,128)S(1)} %shard_map.125.own, bf16[2,256,256]{2,1,0:T(8,128)(2,1)S(1)} %collective-permute-done.7.other, f32[256,256]{1,0:T(8,128)S(1)} %get-tuple-element.33.weight, f32[256,256]{1,0:T(8,128)S(1)} %get-tuple-element.34.unweight, ...), custom_call_target="tpu_custom_call" | custom-call | flops 13107200 | bytes 2228224 | tf_op jit(solution)/shard_map/pallas_call | solution.py:268
  24.8 2.0 %collective-permute-start.8 = (bf16[256,256]{1,0:T(8,128)(2,1)S(1)}, bf16[256,256]{1,0:T(8,128)(2,1)S(1)}, u32[]{:S(2)}, u32[]{:S(2)}) collective-permute-start(bf16[256,256]{1,0:T(8,128)(2,1)S(1)} %get-tuple-element.45.refs_0_), channel_id=1, source_target_pairs={{0,8},{2,10},{4,12},{6,14},{8,0},{10,2},{12,4},{14,6},{1,9},{3,11}... | collective-permute-start | bytes 393224 | tf_op jit(solution)/shard_map/ppermute | solution.py:32
  26.8 1.7 %collective-permute-start.14 = (bf16[256,256]{1,0:T(8,128)(2,1)S(1)}, bf16[256,256]{1,0:T(8,128)(2,1)S(1)}, u32[]{:S(2)}, u32[]{:S(2)}) collective-permute-start(bf16[256,256]{1,0:T(8,128)(2,1)S(1)} %get-tuple-element.45.refs_0_), channel_id=1, source_target_pairs={{0,6},{2,4},{4,2},{6,0},{8,14},{10,12},{12,10},{14,8},{1,7},{3,5},... | collective-permute-start | bytes 393224 | tf_op jit(solution)/shard_map/ppermute | solution.py:32
  28.6 0.3 collective-permute-start.13
  28.8 1.5 %collective-permute-start.12 = (bf16[256,256]{1,0:T(8,128)(2,1)S(1)}, bf16[256,256]{1,0:T(8,128)(2,1)S(1)}, u32[]{:S(2)}, u32[]{:S(2)}) collective-permute-start(bf16[256,256]{1,0:T(8,128)(2,1)S(1)} %get-tuple-element.45.refs_0_), channel_id=1, source_target_pairs={{0,2},{2,0},{4,6},{6,4},{8,10},{10,8},{12,14},{14,12},{1,3},{3,1},... | collective-permute-start | bytes 393224 | tf_op jit(solution)/shard_map/ppermute | solution.py:32
  30.3 3.9 %collective-permute-done.8.refs_2_ = bf16[256,256]{1,0:T(8,128)(2,1)S(1)} collective-permute-done((bf16[256,256]{1,0:T(8,128)(2,1)S(1)}, bf16[256,256]{1,0:T(8,128)(2,1)S(1)}, u32[]{:S(2)}, u32[]{:S(2)}) %collective-permute-start.8) | collective-permute-done | bytes 131104 | tf_op jit(solution)/shard_map/ppermute | solution.py:32
  34.2 0.0 collective-permute-start.11
  34.2 1.4 %collective-permute-start.10 = (bf16[256,256]{1,0:T(8,128)(2,1)S(1)}, bf16[256,256]{1,0:T(8,128)(2,1)S(1)}, u32[]{:S(2)}, u32[]{:S(2)}) collective-permute-start(bf16[256,256]{1,0:T(8,128)(2,1)S(1)} %collective-permute-done.8.refs_2_), channel_id=1, source_target_pairs={{0,2},{2,0},{4,6},{6,4},{8,10},{10,8},{12,14},{14,12},{1,3},{3,1},... | collective-permute-start | bytes 393224 | tf_op jit(solution)/shard_map/ppermute | solution.py:32
  35.6 0.3 collective-permute-done.14.refs_4_
  35.9 1.8 %collective-permute-start.9 = (bf16[256,256]{1,0:T(8,128)(2,1)S(1)}, bf16[256,256]{1,0:T(8,128)(2,1)S(1)}, u32[]{:S(2)}, u32[]{:S(2)}) collective-permute-start(bf16[256,256]{1,0:T(8,128)(2,1)S(1)} %collective-permute-done.8.refs_2_), channel_id=1, source_target_pairs={{0,4},{2,6},{4,0},{6,2},{8,12},{10,14},{12,8},{14,10},{1,5},{3,7},... | collective-permute-start | bytes 393224 | tf_op jit(solution)/shard_map/ppermute | solution.py:32
  37.7 0.2 shard_map.128
  38.0 0.2 collective-permute-done.13.refs_3_
  38.2 0.0 collective-permute-done.12.refs_1_
  38.2 0.8 %shard_map.129.refs_3_ = f32[2,2,256,256]{3,2,1,0:T(8,128)S(1)} custom-call(s32[2,2]{1,0:T(2,128)S(1)} %copy-done.3, bf16[8,2,32,256]{3,2,1,0:T(8,128)(2,1)S(1)} %get-tuple-element.27.v_ref, bf16[2,512,384]{2,1,0:T(8,128)(2,1)S(1)} %get-tuple-element.28.u_ref, bf16[2,2,2,256,256]{4,3,2,1,0:T(8,128)(2,1)S(1)} %copy-done, ...), custom_call_target="tpu_custom_call" | custom-call | flops 125829120 | bytes 2752528 | tf_op jit(solution)/shard_map/pallas_call | solution.py:268
  39.1 2.6 %collective-permute-done.11.refs_2_ = bf16[256,256]{1,0:T(8,128)(2,1)S(1)} collective-permute-done((bf16[256,256]{1,0:T(8,128)(2,1)S(1)}, bf16[256,256]{1,0:T(8,128)(2,1)S(1)}, u32[]{:S(2)}, u32[]{:S(2)}) %collective-permute-start.11) | collective-permute-done | bytes 131104 | tf_op jit(solution)/shard_map/ppermute | solution.py:32
  41.6 0.5 %collective-permute-done.10.refs_1_ = bf16[256,256]{1,0:T(8,128)(2,1)S(1)} collective-permute-done((bf16[256,256]{1,0:T(8,128)(2,1)S(1)}, bf16[256,256]{1,0:T(8,128)(2,1)S(1)}, u32[]{:S(2)}, u32[]{:S(2)}) %collective-permute-start.10) | collective-permute-done | bytes 131104 | tf_op jit(solution)/shard_map/ppermute | solution.py:32
  42.1 0.6 %collective-permute-done.9.refs_0_ = bf16[256,256]{1,0:T(8,128)(2,1)S(1)} collective-permute-done((bf16[256,256]{1,0:T(8,128)(2,1)S(1)}, bf16[256,256]{1,0:T(8,128)(2,1)S(1)}, u32[]{:S(2)}, u32[]{:S(2)}) %collective-permute-start.9) | collective-permute-done | bytes 131104 | tf_op jit(solution)/shard_map/ppermute | solution.py:32
  42.7 0.5 %shard_map.131 = bf16[2,256,256]{2,1,0:T(8,128)(2,1)S(1)} custom-call(s32[2,2]{1,0:T(2,128)S(1)} %copy-done.3, bf16[8,2,32,256]{3,2,1,0:T(8,128)(2,1)S(1)} %get-tuple-element.27.v_ref, bf16[2,512,384]{2,1,0:T(8,128)(2,1)S(1)} %get-tuple-element.28.u_ref, bf16[2,2,2,256,256]{4,3,2,1,0:T(8,128)(2,1)S(1)} %copy-done, ...), custom_call_target="tpu_custom_call" | custom-call | flops 37748736 | bytes 3538960 | tf_op jit(solution)/shard_map/pallas_call | solution.py:268
  43.3 0.1 collective-permute-start.15
  43.4 0.5 %shard_map.130.own = f32[2,256,256]{2,1,0:T(8,128)S(1)} custom-call(s32[2,2]{1,0:T(2,128)S(1)} %copy-done.3, bf16[8,2,32,256]{3,2,1,0:T(8,128)(2,1)S(1)} %get-tuple-element.27.v_ref, bf16[2,512,384]{2,1,0:T(8,128)(2,1)S(1)} %get-tuple-element.28.u_ref, bf16[2,2,2,256,256]{4,3,2,1,0:T(8,128)(2,1)S(1)} %copy-done, ...), custom_call_target="tpu_custom_call" | custom-call | flops 37748736 | bytes 3538960 | tf_op jit(solution)/shard_map/pallas_call | solution.py:268
  43.9 1.0 %collective-permute-done.15.other = bf16[2,256,256]{2,1,0:T(8,128)(2,1)S(1)} collective-permute-done((bf16[2,256,256]{2,1,0:T(8,128)(2,1)S(1)}, bf16[2,256,256]{2,1,0:T(8,128)(2,1)S(1)}, u32[]{:S(2)}, u32[]{:S(2)}) %collective-permute-start.15) | collective-permute-done | bytes 262176 | tf_op jit(solution)/shard_map/ppermute | solution.py:368
  44.9 1.7 %shard_map.132 = (f32[256,256]{1,0:T(8,128)}, f32[256,256]{1,0:T(8,128)}) custom-call(f32[2,256,256]{2,1,0:T(8,128)S(1)} %shard_map.130.own, bf16[2,256,256]{2,1,0:T(8,128)(2,1)S(1)} %collective-permute-done.15.other, f32[256,256]{1,0:T(8,128)S(1)} %get-tuple-element.46.weight, f32[256,256]{1,0:T(8,128)S(1)} %get-tuple-element.47.unweight, ...), custom_call_target="tpu_custom_call" | custom-call | flops 13107200 | bytes 3538944 | tf_op jit(solution)/shard_map/pallas_call | solution.py:268
  (3 shorter events, 0.0 us)
Async XLA Ops:
  0.6 17.2 %copy-start = (bf16[2,2,2,256,256]{4,3,2,1,0:T(8,128)(2,1)S(1)}, bf16[2,2,2,256,256]{4,3,2,1,0:T(8,128)(2,1)}, u32[]{:S(2)}) copy-start(bf16[2,2,2,256,256]{4,3,2,1,0:T(8,128)(2,1)} %d_ref.11) | copy-start | bytes 3145732
  1.7 10.5 %collective-permute-start = (bf16[256,256]{1,0:T(8,128)(2,1)S(1)}, bf16[256,256]{1,0:T(8,128)(2,1)S(1)}, u32[]{:S(2)}, u32[]{:S(2)}) collective-permute-start(bf16[256,256]{1,0:T(8,128)(2,1)S(1)} %shard_map.123.refs_0_), channel_id=1, source_target_pairs={{0,8},{2,10},{4,12},{6,14},{8,0},{10,2},{12,4},{14,6},{1,9},{3,11}... | collective-permute-start | bytes 393224 | tf_op jit(solution)/shard_map/ppermute | solution.py:32
  5.8 9.0 %collective-permute-start.6 = (bf16[256,256]{1,0:T(8,128)(2,1)S(1)}, bf16[256,256]{1,0:T(8,128)(2,1)S(1)}, u32[]{:S(2)}, u32[]{:S(2)}) collective-permute-start(bf16[256,256]{1,0:T(8,128)(2,1)S(1)} %shard_map.123.refs_0_), channel_id=1, source_target_pairs={{0,6},{2,4},{4,2},{6,0},{8,14},{10,12},{12,10},{14,8},{1,7},{3,5},... | collective-permute-start | bytes 393224 | tf_op jit(solution)/shard_map/ppermute | solution.py:32
  8.3 9.4 %collective-permute-start.5 = (bf16[256,256]{1,0:T(8,128)(2,1)S(1)}, bf16[256,256]{1,0:T(8,128)(2,1)S(1)}, u32[]{:S(2)}, u32[]{:S(2)}) collective-permute-start(bf16[256,256]{1,0:T(8,128)(2,1)S(1)} %shard_map.123.refs_0_), channel_id=1, source_target_pairs={{0,4},{2,6},{4,0},{6,2},{8,12},{10,14},{12,8},{14,10},{1,5},{3,7},... | collective-permute-start | bytes 393224 | tf_op jit(solution)/shard_map/ppermute | solution.py:32
  8.8 9.0 %collective-permute-start.4 = (bf16[256,256]{1,0:T(8,128)(2,1)S(1)}, bf16[256,256]{1,0:T(8,128)(2,1)S(1)}, u32[]{:S(2)}, u32[]{:S(2)}) collective-permute-start(bf16[256,256]{1,0:T(8,128)(2,1)S(1)} %shard_map.123.refs_0_), channel_id=1, source_target_pairs={{0,2},{2,0},{4,6},{6,4},{8,10},{10,8},{12,14},{14,12},{1,3},{3,1},... | collective-permute-start | bytes 393224 | tf_op jit(solution)/shard_map/ppermute | solution.py:32
  12.2 8.2 %collective-permute-start.3 = (bf16[256,256]{1,0:T(8,128)(2,1)S(1)}, bf16[256,256]{1,0:T(8,128)(2,1)S(1)}, u32[]{:S(2)}, u32[]{:S(2)}) collective-permute-start(bf16[256,256]{1,0:T(8,128)(2,1)S(1)} %collective-permute-done.refs_2_), channel_id=1, source_target_pairs={{0,6},{2,4},{4,2},{6,0},{8,14},{10,12},{12,10},{14,8},{1,7},{3,5},... | collective-permute-start | bytes 393224 | tf_op jit(solution)/shard_map/ppermute | solution.py:32
  13.8 7.2 %collective-permute-start.2 = (bf16[256,256]{1,0:T(8,128)(2,1)S(1)}, bf16[256,256]{1,0:T(8,128)(2,1)S(1)}, u32[]{:S(2)}, u32[]{:S(2)}) collective-permute-start(bf16[256,256]{1,0:T(8,128)(2,1)S(1)} %collective-permute-done.refs_2_), channel_id=1, source_target_pairs={{0,2},{2,0},{4,6},{6,4},{8,10},{10,8},{12,14},{14,12},{1,3},{3,1},... | collective-permute-start | bytes 393224 | tf_op jit(solution)/shard_map/ppermute | solution.py:32
  14.7 7.0 %collective-permute-start.1 = (bf16[256,256]{1,0:T(8,128)(2,1)S(1)}, bf16[256,256]{1,0:T(8,128)(2,1)S(1)}, u32[]{:S(2)}, u32[]{:S(2)}) collective-permute-start(bf16[256,256]{1,0:T(8,128)(2,1)S(1)} %collective-permute-done.refs_2_), channel_id=1, source_target_pairs={{0,4},{2,6},{4,0},{6,2},{8,12},{10,14},{12,8},{14,10},{1,5},{3,7},... | collective-permute-start | bytes 393224 | tf_op jit(solution)/shard_map/ppermute | solution.py:32
  17.8 0.7 %copy-start.3 = (s32[2,2]{1,0:T(2,128)S(1)}, s32[2,2]{1,0:T(2,128)}, u32[]{:S(2)}) copy-start(s32[2,2]{1,0:T(2,128)} %near_ref.11) | copy-start | bytes 52
  22.3 1.6 %copy-start.1 = (f32[256,256]{1,0:T(8,128)S(1)}, f32[256,256]{1,0:T(8,128)}, u32[]{:S(2)}) copy-start(f32[256,256]{1,0:T(8,128)} %tau.3) | copy-start | bytes 786436
  22.3 1.6 %collective-permute-start.7 = (bf16[2,256,256]{2,1,0:T(8,128)(2,1)S(1)}, bf16[2,256,256]{2,1,0:T(8,128)(2,1)S(1)}, u32[]{:S(2)}, u32[]{:S(2)}) collective-permute-start(bf16[2,256,256]{2,1,0:T(8,128)(2,1)S(1)} %shard_map.126), channel_id=1, source_target_pairs={{0,1},{1,0},{2,3},{3,2},{4,5},{5,4},{6,7},{7,6},{8,9},{9,8},{10,11... | collective-permute-start | bytes 786440 | tf_op jit(solution)/shard_map/ppermute | solution.py:368
  23.9 13.8 %copy-start.2 = (f32[256,256]{1,0:T(8,128)S(1)}, f32[256,256]{1,0:T(8,128)}, u32[]{:S(2)}) copy-start(f32[256,256]{1,0:T(8,128)} %state.1) | copy-start | bytes 786436
  24.8 9.4 %collective-permute-start.8 = (bf16[256,256]{1,0:T(8,128)(2,1)S(1)}, bf16[256,256]{1,0:T(8,128)(2,1)S(1)}, u32[]{:S(2)}, u32[]{:S(2)}) collective-permute-start(bf16[256,256]{1,0:T(8,128)(2,1)S(1)} %get-tuple-element.45.refs_0_), channel_id=1, source_target_pairs={{0,8},{2,10},{4,12},{6,14},{8,0},{10,2},{12,4},{14,6},{1,9},{3,11}... | collective-permute-start | bytes 393224 | tf_op jit(solution)/shard_map/ppermute | solution.py:32
  26.8 9.1 %collective-permute-start.14 = (bf16[256,256]{1,0:T(8,128)(2,1)S(1)}, bf16[256,256]{1,0:T(8,128)(2,1)S(1)}, u32[]{:S(2)}, u32[]{:S(2)}) collective-permute-start(bf16[256,256]{1,0:T(8,128)(2,1)S(1)} %get-tuple-element.45.refs_0_), channel_id=1, source_target_pairs={{0,6},{2,4},{4,2},{6,0},{8,14},{10,12},{12,10},{14,8},{1,7},{3,5},... | collective-permute-start | bytes 393224 | tf_op jit(solution)/shard_map/ppermute | solution.py:32
  28.6 9.7 %collective-permute-start.13 = (bf16[256,256]{1,0:T(8,128)(2,1)S(1)}, bf16[256,256]{1,0:T(8,128)(2,1)S(1)}, u32[]{:S(2)}, u32[]{:S(2)}) collective-permute-start(bf16[256,256]{1,0:T(8,128)(2,1)S(1)} %get-tuple-element.45.refs_0_), channel_id=1, source_target_pairs={{0,4},{2,6},{4,0},{6,2},{8,12},{10,14},{12,8},{14,10},{1,5},{3,7},... | collective-permute-start | bytes 393224 | tf_op jit(solution)/shard_map/ppermute | solution.py:32
  28.8 9.4 %collective-permute-start.12 = (bf16[256,256]{1,0:T(8,128)(2,1)S(1)}, bf16[256,256]{1,0:T(8,128)(2,1)S(1)}, u32[]{:S(2)}, u32[]{:S(2)}) collective-permute-start(bf16[256,256]{1,0:T(8,128)(2,1)S(1)} %get-tuple-element.45.refs_0_), channel_id=1, source_target_pairs={{0,2},{2,0},{4,6},{6,4},{8,10},{10,8},{12,14},{14,12},{1,3},{3,1},... | collective-permute-start | bytes 393224 | tf_op jit(solution)/shard_map/ppermute | solution.py:32
  34.2 7.4 %collective-permute-start.11 = (bf16[256,256]{1,0:T(8,128)(2,1)S(1)}, bf16[256,256]{1,0:T(8,128)(2,1)S(1)}, u32[]{:S(2)}, u32[]{:S(2)}) collective-permute-start(bf16[256,256]{1,0:T(8,128)(2,1)S(1)} %collective-permute-done.8.refs_2_), channel_id=1, source_target_pairs={{0,6},{2,4},{4,2},{6,0},{8,14},{10,12},{12,10},{14,8},{1,7},{3,5},... | collective-permute-start | bytes 393224 | tf_op jit(solution)/shard_map/ppermute | solution.py:32
  34.2 7.9 %collective-permute-start.10 = (bf16[256,256]{1,0:T(8,128)(2,1)S(1)}, bf16[256,256]{1,0:T(8,128)(2,1)S(1)}, u32[]{:S(2)}, u32[]{:S(2)}) collective-permute-start(bf16[256,256]{1,0:T(8,128)(2,1)S(1)} %collective-permute-done.8.refs_2_), channel_id=1, source_target_pairs={{0,2},{2,0},{4,6},{6,4},{8,10},{10,8},{12,14},{14,12},{1,3},{3,1},... | collective-permute-start | bytes 393224 | tf_op jit(solution)/shard_map/ppermute | solution.py:32
  35.9 6.8 %collective-permute-start.9 = (bf16[256,256]{1,0:T(8,128)(2,1)S(1)}, bf16[256,256]{1,0:T(8,128)(2,1)S(1)}, u32[]{:S(2)}, u32[]{:S(2)}) collective-permute-start(bf16[256,256]{1,0:T(8,128)(2,1)S(1)} %collective-permute-done.8.refs_2_), channel_id=1, source_target_pairs={{0,4},{2,6},{4,0},{6,2},{8,12},{10,14},{12,8},{14,10},{1,5},{3,7},... | collective-permute-start | bytes 393224 | tf_op jit(solution)/shard_map/ppermute | solution.py:32
  43.3 1.6 %collective-permute-start.15 = (bf16[2,256,256]{2,1,0:T(8,128)(2,1)S(1)}, bf16[2,256,256]{2,1,0:T(8,128)(2,1)S(1)}, u32[]{:S(2)}, u32[]{:S(2)}) collective-permute-start(bf16[2,256,256]{2,1,0:T(8,128)(2,1)S(1)} %shard_map.131), channel_id=1, source_target_pairs={{0,1},{1,0},{2,3},{3,2},{4,5},{5,4},{6,7},{7,6},{8,9},{9,8},{10,11... | collective-permute-start | bytes 786440 | tf_op jit(solution)/shard_map/ppermute | solution.py:368
